TPU v7x, 32 devices: a whole 2x2x4 slice. The times are simulated.
32 devices in a mesh: groups: 2 (over y), tensor: 4 (over z), section: 2 (over core), replica: 2 (over x).
Axes of the slice: x: 2, y: 2, z: 4, core: 2. Of those that a mesh axis runs over, the one named last changes fastest.
Arguments:
- tokens: bfloat16 [768, 8192], P(('groups', 'replica'), 'tensor'), parts along dimension 0
- cotangent: bfloat16 [768, 8192], P(('groups', 'replica'), 'tensor'), parts along dimension 0, may hold values from -0.29882812 to 0.29882812
- gain: float32 [2, 8192], P('section', 'tensor'), may hold values from 0.5 to 1.5
- frozen_base_weight: bfloat16 [2, 8192, 8192], P('section', 'tensor'), may hold values from -0.0625 to 0.0625
- adapter_down_factors: bfloat16 [2, 8192, 256], P('section', 'tensor'), may hold values from -0.0625 to 0.0625
- adapter_up_factors: bfloat16 [2, 256, 8192], P('section', None, 'tensor'), may hold values from -0.375 to 0.375
- tenant_adapter_scale: float32 [4], replicated, may hold values from 0.5 to 4
- row_tenant_owner: int32 [768], P(('groups', 'replica')), parts along dimension 0, may hold values from 0 to 4
Outputs:
- grad_down: float32 [2, 8192, 512], P('section', 'tensor', 'groups'), parts along dimension 2
- grad_up: float32 [2, 512, 8192], P('section', 'groups', 'tensor'), parts along dimension 1
There are 2 independent parts, one for each index of `groups`. A program takes and returns all parts, laid end to end along the dimension named above; an argument that names none is the same for every part. Nothing has to cross between parts.
Inputs may be any that keep to these rules, and one draw needn't show every extreme that they name: `row_tenant_owner`: a row whose owner is 4 is padding and belongs to no tenant.
All inputs are finite; a program needn't handle non-finite values.
Results may differ from a plain program's by a relative error of at most 0.02.
Values may be sent and summed in bfloat16 or wider, within the bound.
No kernel may reach another device: no remote copies, remote signals or barrier semaphores. Data moves between devices by JAX's collectives and lax.ppermute only.
A program may use at most 128 MiB of HBM per device.

v0:
```python
import jax
import jax.numpy as jnp
from jax import lax
from jax.sharding import PartitionSpec as P

D = 8192
TENANT_COUNT = 4
R = 64
MICRO = 3


EPSILON = 1e-05


def from_behind(value, axis, steps):
    count = lax.axis_size(axis)
    leading, last = (max(0, -steps), min(count, count - steps))
    return lax.ppermute(value, axis, [(source, source + steps) for source in range(leading, last)])


def per_tenant(values, coefficients):
    count = values.shape[0]
    return (values.reshape(count, TENANT_COUNT, R) * coefficients[:, :, None]).reshape(
        count, TENANT_COUNT * R
    )


def forward_layer(inputs, gain_row, weight, down_shard, up_shard, coefficients):
    x_float = inputs.astype(jnp.float32)
    scaled = (x_float * gain_row[None, :]).astype(jnp.bfloat16)
    square_part = jnp.sum(x_float * x_float, axis=1)
    rank_part = jnp.dot(scaled, down_shard, preferred_element_type=jnp.float32)
    squares, rank_full = (
        lax.psum(square_part.astype(jnp.bfloat16), "tensor").astype(jnp.float32),
        lax.psum(rank_part.astype(jnp.bfloat16), "tensor").astype(jnp.float32),
    )
    inv_rms = lax.rsqrt(squares / D + EPSILON)
    partial_sum = jnp.dot(scaled, weight, preferred_element_type=jnp.float32)
    base_part = lax.psum_scatter(
        partial_sum.astype(jnp.bfloat16), "tensor", scatter_dimension=1, tiled=True
    ).astype(jnp.float32)
    low_rank = per_tenant(rank_full, coefficients).astype(jnp.bfloat16)
    projected = base_part + jnp.dot(low_rank, up_shard, preferred_element_type=jnp.float32)
    outputs = (x_float + inv_rms[:, None] * projected).astype(jnp.bfloat16)
    return (outputs, (inputs, scaled, inv_rms, projected, low_rank, coefficients))


def backward_layer(out_grad, stored, gain_row, weight, down_shard, up_shard):
    inputs, scaled, inv_rms, projected, low_rank, coefficients = stored
    x_float = inputs.astype(jnp.float32)
    grad_float = out_grad.astype(jnp.float32)
    proj_grad = (inv_rms[:, None] * grad_float).astype(jnp.bfloat16)
    dot_part = jnp.sum(grad_float * projected, axis=1)
    contract_last = (((1,), (1,)), ((), ()))
    value_grad = lax.dot_general(
        lax.all_gather(proj_grad, "tensor", axis=1, tiled=True),
        weight,
        contract_last,
        preferred_element_type=jnp.float32,
    )
    rank_part = lax.dot_general(
        proj_grad, up_shard, contract_last, preferred_element_type=jnp.float32
    )
    row_dot, rank_grad = (
        lax.psum(dot_part.astype(jnp.bfloat16), "tensor").astype(jnp.float32),
        lax.psum(rank_part.astype(jnp.bfloat16), "tensor").astype(jnp.float32),
    )
    low_grad = per_tenant(rank_grad, coefficients).astype(jnp.bfloat16)
    value_grad = value_grad + lax.dot_general(
        low_grad, down_shard, contract_last, preferred_element_type=jnp.float32
    )
    cubed = inv_rms * inv_rms * inv_rms
    in_grad = (
        grad_float + gain_row[None, :] * value_grad - (row_dot * cubed)[:, None] * x_float / D
    ).astype(jnp.bfloat16)
    contract_first = (((0,), (0,)), ((), ()))
    grad_down = lax.dot_general(
        scaled, low_grad, contract_first, preferred_element_type=jnp.float32
    )
    grad_up = lax.dot_general(
        low_rank, proj_grad, contract_first, preferred_element_type=jnp.float32
    )
    return (in_grad, grad_down, grad_up)


def on_device(
    tokens,
    cotangent,
    gain,
    frozen_base_weight,
    adapter_down_factors,
    adapter_up_factors,
    tenant_adapter_scale,
    row_tenant_owner,
):
    section_id = lax.axis_index("section")
    is_first = section_id == 0
    weight = frozen_base_weight[0]
    gain_row = gain[0]
    down_shard = adapter_down_factors[0]
    up_shard = adapter_up_factors[0]
    block_rows = tokens.shape[0] // MICRO
    local_width = tokens.shape[1]
    x_blocks = tokens.reshape(MICRO, block_rows, local_width)
    grad_blocks = cotangent.reshape(MICRO, block_rows, local_width)
    owner_blocks = row_tenant_owner.reshape(MICRO, block_rows)
    tenant_index_list = jnp.arange(TENANT_COUNT, dtype=jnp.int32)
    zero_block = jnp.zeros((block_rows, local_width), jnp.bfloat16)
    received = zero_block
    saved = []
    for step_no in range(MICRO + 1):
        mb_index = jnp.clip(step_no - section_id, 0, MICRO - 1)
        owner_of_row = lax.dynamic_index_in_dim(owner_blocks, mb_index, 0, keepdims=False)
        coefficients = tenant_adapter_scale[None, :] * (
            owner_of_row[:, None] == tenant_index_list[None, :]
        ).astype(jnp.float32)
        inputs = jnp.where(is_first, x_blocks[min(step_no, MICRO - 1)], received)
        outputs, stored = forward_layer(
            inputs, gain_row, weight, down_shard, up_shard, coefficients
        )
        saved.append(stored)
        if step_no < MICRO:
            received = from_behind(outputs, "section", 1)
    total_down = jnp.zeros((local_width, down_shard.shape[1]), jnp.float32)
    total_up = jnp.zeros((up_shard.shape[0], local_width), jnp.float32)
    incoming = zero_block
    for step_no in range(MICRO + 1):
        stored = saved[MICRO - step_no]
        own_grad = grad_blocks[max(MICRO - 1 - step_no, 0)]
        is_live = jnp.where(is_first, step_no >= 1, step_no <= MICRO - 1)
        out_grad = jnp.where(is_live, jnp.where(is_first, incoming, own_grad), zero_block)
        in_grad, part_down, part_up = backward_layer(
            out_grad, stored, gain_row, weight, down_shard, up_shard
        )
        total_down = total_down + part_down
        total_up = total_up + part_up
        if step_no < MICRO:
            incoming = from_behind(in_grad, "section", -1)
    summed = (
        lax.psum(total_down.astype(jnp.bfloat16), "replica").astype(jnp.float32),
        lax.psum(total_up.astype(jnp.bfloat16), "replica").astype(jnp.float32),
    )
    return (summed[0][None], summed[1][None])


def solution(mesh):
    return jax.shard_map(
        on_device,
        mesh=mesh,
        in_specs=(
            P(("groups", "replica"), "tensor"),
            P(("groups", "replica"), "tensor"),
            P("section", "tensor"),
            P("section", "tensor", None),
            P("section", "tensor", None),
            P("section", None, "tensor"),
            P(),
            P(("groups", "replica")),
        ),
        out_specs=(P("section", "tensor", "groups"), P("section", "groups", "tensor")),
        check_vma=False,
    )
```

profile of v0, /device:TPU:0, one launch (start us, length us, event | category | flops | bytes accessed | tf_op | source)
XLA Modules:
  0.0 453.0 jit_solution(657488496592666886)
XLA Ops:
  7.3 17.7 %fusion.14 = bf16[64,8192]{1,0:T(8,128)(2,1)} fusion(bf16[1,2048,8192]{2,1,0:T(8,128)(2,1)} %param.11, f32[2048]{0:T(1024)} %bitcast.83, bf16[192,2048]{1,0:T(8,128)(2,1)} %param.8, pred[]{:T(512)S(6)} %eq.79), kind=kOutput, calls=%fused_computation.14 | convolution fusion | flops 2148532224 | bytes 34873344 | tf_op jit(solution)/shard_map/dot_general | solution.py:38
  26.6 22.3 %all-reduce.6 = (bf16[64]{0:T(256)(128)(2,1)S(1)}, bf16[64,256]{1,0:T(8,128)(2,1)S(1)}) all-reduce(bf16[64]{0:T(256)(128)(2,1)S(1)} %fusion.60, bf16[64,256]{1,0:T(8,128)(2,1)S(1)} %convolution_convert_fusion.7), channel_id=1, replica_groups=mesh['groups'=2,'tensor'=4,'section'=2,'replica'=2] {'tensor'}, use_global_device_ids=true, to_apply=%region_1.2 | all-reduce | flops 16448 | bytes 65792 | tf_op jit(solution)/shard_map/psum | solution.py:34
  48.9 7.1 %reduce-scatter.5.cloned.1.call-done = bf16[64,2048]{1,0:T(8,128)(2,1)} async-done(((bf16[64,8192]{1,0:T(8,128)(2,1)}), bf16[64,2048]{1,0:T(8,128)(2,1)}) %reduce-scatter.5.cloned.1.call-update) | async-done | bytes 262160 | tf_op jit(solution)/shard_map/reduce_scatter | solution.py:39
  60.2 14.6 %fusion.17 = bf16[64,8192]{1,0:T(8,128)(2,1)} fusion(bf16[1,2048,8192]{2,1,0:T(8,128)(2,1)} %param.11, bf16[64,2048]{1,0:T(8,128)(2,1)S(1)} %get-tuple-element.27, f32[2048]{0:T(1024)S(1)} %bitcast.85), kind=kOutput, calls=%fused_computation.15 | convolution fusion | flops 2148401152 | bytes 34873344 | tf_op jit(solution)/shard_map/dot_general | solution.py:38
  75.5 17.8 %all-reduce.5 = (bf16[64,256]{1,0:T(8,128)(2,1)S(1)}, bf16[64]{0:T(256)(128)(2,1)S(1)}) all-reduce(bf16[64,256]{1,0:T(8,128)(2,1)S(1)} %convolution_convert_fusion.6, bf16[64]{0:T(256)(128)(2,1)S(1)} %get-tuple-element.26), channel_id=1, replica_groups=mesh['groups'=2,'tensor'=4,'section'=2,'replica'=2] {'tensor'}, use_global_device_ids=true, to_apply=%region_7.8 | all-reduce | flops 16448 | bytes 65792 | tf_op jit(solution)/shard_map/psum | solution.py:35
  93.4 8.9 %reduce-scatter.7.cloned.1.call-done = bf16[64,2048]{1,0:T(8,128)(2,1)} async-done(((bf16[64,8192]{1,0:T(8,128)(2,1)}), bf16[64,2048]{1,0:T(8,128)(2,1)}) %reduce-scatter.7.cloned.1.call-update) | async-done | bytes 262160 | tf_op jit(solution)/shard_map/reduce_scatter | solution.py:39
  102.3 2.1 fusion.74
  107.2 14.6 %fusion.20 = bf16[64,8192]{1,0:T(8,128)(2,1)} fusion(bf16[1,2048,8192]{2,1,0:T(8,128)(2,1)} %param.11, bf16[64,2048]{1,0:T(8,128)(2,1)S(1)} %get-tuple-element.25, f32[2048]{0:T(1024)S(1)} %bitcast.87), kind=kOutput, calls=%fused_computation.16 | convolution fusion | flops 2148401152 | bytes 34873344 | tf_op jit(solution)/shard_map/dot_general | solution.py:38
  122.5 18.8 %all-reduce.4 = (bf16[64,256]{1,0:T(8,128)(2,1)S(1)}, bf16[64]{0:T(256)(128)(2,1)S(1)}) all-reduce(bf16[64,256]{1,0:T(8,128)(2,1)S(1)} %convolution_convert_fusion.5, bf16[64]{0:T(256)(128)(2,1)S(1)} %get-tuple-element.24), channel_id=1, replica_groups=mesh['groups'=2,'tensor'=4,'section'=2,'replica'=2] {'tensor'}, use_global_device_ids=true, to_apply=%region_11.12 | all-reduce | flops 16448 | bytes 65792 | tf_op jit(solution)/shard_map/psum | solution.py:35
  141.4 7.8 %reduce-scatter.9.cloned.1.call-done = bf16[64,2048]{1,0:T(8,128)(2,1)} async-done(((bf16[64,8192]{1,0:T(8,128)(2,1)}), bf16[64,2048]{1,0:T(8,128)(2,1)}) %reduce-scatter.9.cloned.1.call-update) | async-done | bytes 262160 | tf_op jit(solution)/shard_map/reduce_scatter | solution.py:39
  149.2 2.1 fusion.78
  151.3 1.9 collective-permute-start.2
  155.8 17.4 %all-reduce.3 = (bf16[64,256]{1,0:T(8,128)(2,1)S(1)}, bf16[64]{0:T(256)(128)(2,1)S(1)}) all-reduce(bf16[64,256]{1,0:T(8,128)(2,1)S(1)} %convolution_convert_fusion.3, bf16[64]{0:T(256)(128)(2,1)S(1)} %get-tuple-element.22), channel_id=1, replica_groups=mesh['groups'=2,'tensor'=4,'section'=2,'replica'=2] {'tensor'}, use_global_device_ids=true, to_apply=%region_16.17 | all-reduce | flops 16448 | bytes 65792 | tf_op jit(solution)/shard_map/psum | solution.py:35
  175.1 14.9 %fusion.23 = bf16[64,8192]{1,0:T(8,128)(2,1)} fusion(bf16[1,2048,8192]{2,1,0:T(8,128)(2,1)} %param.11, bf16[64,2048]{1,0:T(8,128)(2,1)S(1)} %get-tuple-element.23, f32[2048]{0:T(1024)S(1)} %bitcast.90), kind=kOutput, calls=%fused_computation.17 | convolution fusion | flops 2148401152 | bytes 34873344 | tf_op jit(solution)/shard_map/dot_general | solution.py:38
  190.6 10.8 %all-gather.4.cloned.1.call-done = bf16[64,8192]{1,0:T(8,128)(2,1)} async-done(((bf16[64,2048]{1,0:T(8,128)(2,1)}), bf16[64,8192]{1,0:T(8,128)(2,1)}) %all-gather.4.cloned.1.call-update) | async-done | bytes 1048592 | tf_op jit(solution)/shard_map/all_gather | solution.py:56
  201.4 16.5 %fusion.6 = f32[64,2048]{1,0:T(8,128)} fusion(bf16[64,8192]{1,0:T(8,128)(2,1)} %all-gather.4.cloned.1.call-done, bf16[1,2048,8192]{2,1,0:T(8,128)(2,1)} %param.11), kind=kOutput, calls=%fused_computation.6 | convolution fusion | flops 2147483648 | bytes 35127296 | tf_op jit(solution)/shard_map/dot_general | solution.py:55
  217.9 12.9 %reduce-scatter.11.cloned.1.call-done = bf16[64,2048]{1,0:T(8,128)(2,1)} async-done(((bf16[64,8192]{1,0:T(8,128)(2,1)}), bf16[64,2048]{1,0:T(8,128)(2,1)}) %reduce-scatter.11.cloned.1.call-update) | async-done | bytes 262160 | tf_op jit(solution)/shard_map/reduce_scatter | solution.py:39
  232.2 17.0 %all-reduce.2 = (bf16[64]{0:T(256)(128)(2,1)S(1)}, bf16[64,256]{1,0:T(8,128)(2,1)S(1)}) all-reduce(bf16[64]{0:T(256)(128)(2,1)S(1)} %fusion.44, bf16[64,256]{1,0:T(8,128)(2,1)S(1)} %convolution_convert_fusion.4), channel_id=1, replica_groups=mesh['groups'=2,'tensor'=4,'section'=2,'replica'=2] {'tensor'}, use_global_device_ids=true, to_apply=%region_18.19 | all-reduce | flops 16448 | bytes 65792 | tf_op jit(solution)/shard_map/psum | solution.py:65
  252.2 2.1 collective-permute-done.3
  256.4 2.0 convolution_convert_fusion.2
  258.4 19.0 %all-reduce.1 = (bf16[64,256]{1,0:T(8,128)(2,1)}, bf16[64]{0:T(256)(128)(2,1)}) all-reduce(bf16[64,256]{1,0:T(8,128)(2,1)} %convolution_convert_fusion.2, bf16[64]{0:T(256)(128)(2,1)S(1)} %get-tuple-element.20), channel_id=1, replica_groups=mesh['groups'=2,'tensor'=4,'section'=2,'replica'=2] {'tensor'}, use_global_device_ids=true, to_apply=%region_19.20 | all-reduce | flops 16448 | bytes 65792 | tf_op jit(solution)/shard_map/psum | solution.py:66
  278.1 6.3 %all-gather.6.cloned.1.call-done = bf16[64,8192]{1,0:T(8,128)(2,1)} async-done(((bf16[64,2048]{1,0:T(8,128)(2,1)}), bf16[64,8192]{1,0:T(8,128)(2,1)}) %all-gather.6.cloned.1.call-update) | async-done | bytes 1048592 | tf_op jit(solution)/shard_map/all_gather | solution.py:56
  284.4 15.2 %fusion.2 = f32[64,2048]{1,0:T(8,128)S(1)} fusion(bf16[64,8192]{1,0:T(8,128)(2,1)} %all-gather.6.cloned.1.call-done, bf16[1,2048,8192]{2,1,0:T(8,128)(2,1)} %param.11), kind=kOutput, calls=%fused_computation.2 | convolution fusion | flops 2147483648 | bytes 35127296 | tf_op jit(solution)/shard_map/dot_general | solution.py:55
  311.4 19.2 %all-reduce = (bf16[64,256]{1,0:T(8,128)(2,1)S(1)}, bf16[64]{0:T(256)(128)(2,1)S(1)}) all-reduce(bf16[64,256]{1,0:T(8,128)(2,1)S(1)} %convolution_convert_fusion.1, bf16[64]{0:T(256)(128)(2,1)S(1)} %get-tuple-element.18), channel_id=1, replica_groups=mesh['groups'=2,'tensor'=4,'section'=2,'replica'=2] {'tensor'}, use_global_device_ids=true, to_apply=%region_22.23 | all-reduce | flops 16448 | bytes 65792 | tf_op jit(solution)/shard_map/psum | solution.py:66
  330.6 3.4 convolution_add_fusion.4
  334.8 15.2 %fusion = f32[64,2048]{1,0:T(8,128)S(1)} fusion(bf16[64,8192]{1,0:T(8,128)(2,1)} %all-gather.8.cloned.1.call-done, bf16[1,2048,8192]{2,1,0:T(8,128)(2,1)} %param.11), kind=kOutput, calls=%fused_computation | convolution fusion | flops 2147483648 | bytes 35127296 | tf_op jit(solution)/shard_map/dot_general | solution.py:55
  354.9 2.0 convolution_convert_fusion
  356.9 18.5 %psum.133 = bf16[64,256]{1,0:T(8,128)(2,1)S(1)} all-reduce(bf16[64,256]{1,0:T(8,128)(2,1)} %convolution_convert_fusion), channel_id=1, replica_groups=mesh['groups'=2,'tensor'=4,'section'=2,'replica'=2] {'tensor'}, use_global_device_ids=true, to_apply=%region_25.26 | all-reduce | flops 16384 | bytes 65536 | tf_op jit(solution)/shard_map/psum | solution.py:66
  375.4 2.5 fusion.29
  377.9 2.4 fusion.28
  380.4 61.4 %all-reduce.10.cloned.1.call-done = (bf16[1,2048,256]{2,1,0:T(8,128)(2,1)}, bf16[1,256,2048]{2,1,0:T(8,128)(2,1)}) async-done(((bf16[1,2048,256]{2,1,0:T(8,128)(2,1)}, bf16[1,256,2048]{2,1,0:T(8,128)(2,1)}), (bf16[1,2048,256]{2,1,0:T(8,128)(2,1)}, bf16[1,256,2048]{2,1,0:T(8,128)(2,1)})) %all-reduce.10.cloned.1.call-update) | async-done | bytes 2097168 | tf_op jit(solution)/shard_map/psum | solution.py:140
  441.8 2.8 broadcast_in_dim.14
  (159 shorter events, 40.8 us)
Async XLA Ops:
  7.2 48.9 %copy-start = (bf16[1,256,2048]{2,1,0:T(8,128)(2,1)S(1)}, bf16[1,256,2048]{2,1,0:T(8,128)(2,1)}, u32[]{:S(2)}) copy-start(bf16[1,256,2048]{2,1,0:T(8,128)(2,1)} %param.13) | copy-start | bytes 3145732
  7.2 48.9 %reduce-scatter.5.cloned.1.call-start = ((), (), s32[]{:S(2)}) async-start(), calls=%async_computation.4 | async-start | bytes 1310720 | tf_op jit(solution)/shard_map/reduce_scatter | solution.py:39
  7.2 17.8 %copy-start.39 = (s32[192]{0:T(256)S(1)}, s32[192]{0:T(256)}, u32[]{:S(2)}) copy-start(s32[192]{0:T(256)} %param.15) | copy-start | bytes 2308
  7.2 17.9 %copy-start.40 = (f32[4]{0:T(128)S(1)}, f32[4]{0:T(128)}, u32[]{:S(2)}) copy-start(f32[4]{0:T(128)} %param.14) | copy-start | bytes 52
  7.3 18.9 %copy-start.6 = (bf16[192,2048]{1,0:T(8,128)(2,1)S(1)}, bf16[192,2048]{1,0:T(8,128)(2,1)}, u32[]{:S(2)}) copy-start(bf16[192,2048]{1,0:T(8,128)(2,1)} %param.8) | copy-start | bytes 2359300
  7.3 19.0 %copy-start.1 = (bf16[1,2048,256]{2,1,0:T(8,128)(2,1)S(1)}, bf16[1,2048,256]{2,1,0:T(8,128)(2,1)}, u32[]{:S(2)}) copy-start(bf16[1,2048,256]{2,1,0:T(8,128)(2,1)} %param.12) | copy-start | bytes 3145732
  7.3 19.0 %copy-start.10 = (f32[1,2048]{1,0:T(1,128)S(1)}, f32[1,2048]{1,0:T(1,128)}, u32[]{:S(2)}) copy-start(f32[1,2048]{1,0:T(1,128)} %param.10) | copy-start | bytes 24580
  25.0 77.3 %reduce-scatter.7.cloned.1.call-start = ((), (), s32[]{:S(2)}) async-start(), calls=%async_computation.5 | async-start | bytes 1310720 | tf_op jit(solution)/shard_map/reduce_scatter | solution.py:39
  26.1 32.8 %copy-start.15 = (f32[64,256]{1,0:T(8,128)}, f32[64,256]{1,0:T(8,128)S(1)}, u32[]{:S(2)}) copy-start(f32[64,256]{1,0:T(8,128)S(1)} %mul.277) | copy-start | bytes 196612
  48.9 26.0 %copy-start.23 = (bf16[64,256]{1,0:T(8,128)(2,1)}, bf16[64,256]{1,0:T(8,128)(2,1)S(1)}, u32[]{:S(2)}) copy-start(bf16[64,256]{1,0:T(8,128)(2,1)S(1)} %get-tuple-element.15) | copy-start | bytes 98308
  57.3 2.7 collective-permute-start
  74.9 74.3 %reduce-scatter.9.cloned.1.call-start = ((), (), s32[]{:S(2)}) async-start(), calls=%async_computation.6 | async-start | bytes 1310720 | tf_op jit(solution)/shard_map/reduce_scatter | solution.py:39
  93.3 28.5 %copy-start.25 = (bf16[64,256]{1,0:T(8,128)(2,1)}, bf16[64,256]{1,0:T(8,128)(2,1)S(1)}, u32[]{:S(2)}) copy-start(bf16[64,256]{1,0:T(8,128)(2,1)S(1)} %get-tuple-element.12) | copy-start | bytes 98308
  104.3 2.7 collective-permute-start.1
  121.9 79.5 %all-gather.4.cloned.1.call-start = ((), (), s32[]{:S(2)}) async-start(), calls=%async_computation.7 | async-start | bytes 1310720 | tf_op jit(solution)/shard_map/all_gather | solution.py:56
  121.9 31.2 %copy-start.32 = (f32[64,4]{1,0:T(8,128)S(1)}, f32[64,4]{1,0:T(8,128)}, u32[]{:S(2)}) copy-start(f32[64,4]{1,0:T(8,128)} %get-tuple-element.32) | copy-start | bytes 3076
  151.3 3.0 collective-permute-start.2
  153.5 95.8 %copy-start.17 = (f32[64,256]{1,0:T(8,128)}, f32[64,256]{1,0:T(8,128)S(1)}, u32[]{:S(2)}) copy-start(f32[64,256]{1,0:T(8,128)S(1)} %mul.302) | copy-start | bytes 196612
  173.2 57.6 %copy-start.33 = (bf16[64,256]{1,0:T(8,128)(2,1)}, bf16[64,256]{1,0:T(8,128)(2,1)S(1)}, u32[]{:S(2)}) copy-start(bf16[64,256]{1,0:T(8,128)(2,1)S(1)} %get-tuple-element.8) | copy-start | bytes 98308
  175.0 55.7 %reduce-scatter.11.cloned.1.call-start = ((), (), s32[]{:S(2)}) async-start(), calls=%async_computation.8 | async-start | bytes 1310720 | tf_op jit(solution)/shard_map/reduce_scatter | solution.py:39
  190.1 94.4 %all-gather.6.cloned.1.call-start = ((), (), s32[]{:S(2)}) async-start(), calls=%async_computation.9 | async-start | bytes 1310720 | tf_op jit(solution)/shard_map/all_gather | solution.py:56
  250.9 3.4 collective-permute-start.3
  256.4 78.4 %all-gather.8.cloned.1.call-start = ((), (), s32[]{:S(2)}) async-start(), calls=%async_computation.10 | async-start | bytes 1310720 | tf_op jit(solution)/shard_map/all_gather | solution.py:56
  300.1 3.4 collective-permute-start.4
  305.7 136.1 %all-reduce.10.cloned.1.call-start = ((), (), s32[]{:S(2)}) async-start(), calls=%async_computation.11 | async-start | bytes 4194304 | tf_op jit(solution)/shard_map/psum | solution.py:140
  309.1 21.4 %copy-start.42 = (bf16[64]{0:T(256)(128)(2,1)S(1)}, bf16[64]{0:T(256)(128)(2,1)}, u32[]{:S(2)}) copy-start(bf16[64]{0:T(256)(128)(2,1)} %copy-done.41) | copy-start | bytes 388
  334.0 16.0 %copy-start.12 = (bf16[64,2048]{1,0:T(8,128)(2,1)S(1)}, bf16[64,2048]{1,0:T(8,128)(2,1)}, u32[]{:S(2)}) copy-start(bf16[64,2048]{1,0:T(8,128)(2,1)} %copy-done.11) | copy-start | bytes 786436
  350.4 24.9 %copy-start.4 = (f32[2048,256]{1,0:T(8,128)S(1)}, f32[2048,256]{1,0:T(8,128)}, u32[]{:S(2)}) copy-start(f32[2048,256]{1,0:T(8,128)} %convolution_add_fusion.4) | copy-start | bytes 6291460
  350.5 24.9 %copy-start.16 = (f32[64,256]{1,0:T(8,128)S(1)}, f32[64,256]{1,0:T(8,128)}, u32[]{:S(2)}) copy-start(f32[64,256]{1,0:T(8,128)} %copy-done.15) | copy-start | bytes 196612
  350.5 3.7 collective-permute-start.5
  356.9 21.1 %copy-start.22 = (bf16[64,2048]{1,0:T(8,128)(2,1)S(1)}, bf16[64,2048]{1,0:T(8,128)(2,1)}, u32[]{:S(2)}) copy-start(bf16[64,2048]{1,0:T(8,128)(2,1)} %copy-done.21) | copy-start | bytes 786436
  356.9 21.1 %copy-start.24 = (bf16[64,256]{1,0:T(8,128)(2,1)S(1)}, bf16[64,256]{1,0:T(8,128)(2,1)}, u32[]{:S(2)}) copy-start(bf16[64,256]{1,0:T(8,128)(2,1)} %copy-done.23) | copy-start | bytes 98308
  (26 other events, 135.2 us)
Sparse Core Ops, SparseCore 0:
  25.1 30.8 reduce-scatter.4
  75.0 27.1 reduce-scatter.6
  122.0 27.1 reduce-scatter.8
  175.1 26.1 all-gather.3
  204.2 26.5 reduce-scatter.10
  256.5 27.8 all-gather.5
  305.8 28.9 all-gather.7
  380.5 61.2 all-reduce.9
where the time goes:
time: 454 us; the launch traced here: 453 us
  blocking collectives  150 us (33%)
  matrix products  141 us (31%)
  waiting for transfers between devices  122 us (27%)
  between operations  14.9 us (3%)
  other arithmetic  13.3 us (3%)
  starting transfers between devices  9.69 us (2%)
    dot_general x4, matrix products, forward_layer(): partial_sum = jnp.dot(scaled, weight, preferred_element_type=jnp.float32)  61.9 us
    psum x1, waiting for transfers between devices, on_device(): lax.psum(total_down.astype(jnp.bfloat16), 'replica').astype(jnp.float32)  61.4 us
    psum x3, blocking collectives, backward_layer(): lax.psum(rank_part.astype(jnp.bfloat16), 'tensor').astype(jnp.float32)  56.6 us
    psum x3, blocking collectives, forward_layer(): lax.psum(rank_part.astype(jnp.bfloat16), 'tensor').astype(jnp.float32)  54 us
    dot_general x3, matrix products, backward_layer(): lax.dot_general(lax.all_gather(proj_grad, 'tensor', axis=1, tiled=True),...  46.8 us
    reduce_scatter x4, waiting for transfers between devices, forward_layer(): lax.psum_scatter(partial_sum.astype(jnp.bfloat16), 'tensor', scatter_dime...  36.8 us
    psum x1, blocking collectives, forward_layer(): lax.psum(square_part.astype(jnp.bfloat16), 'tensor').astype(jnp.float32)  22.3 us
    all_gather x3, waiting for transfers between devices, backward_layer(): lax.all_gather(proj_grad, 'tensor', axis=1, tiled=True)  17.9 us
  transfers between devices with their start and end apart: 14, of which 14 were waited for; matrix products, arithmetic and copies ran while one was open for 11% of the time, Pallas kernels for 0%

commit v1 on v0

v1 whole, which is shorter than its diff:
```python
import functools

import jax
import jax.numpy as jnp
from jax import lax
from jax.experimental import pallas as pl
from jax.experimental.pallas import tpu as pltpu
from jax.sharding import PartitionSpec as P

TENANT_COUNT = 4
EPSILON = 1e-05
CONTRACT_LAST = (((1,), (1,)), ((), ()))
CONTRACT_FIRST = (((0,), (0,)), ((), ()))
BF16 = jnp.bfloat16
F32 = jnp.float32


def block_kernel(table, own_ref, from_left_ref, from_right_ref, weight_ref, right_ref, left_ref, total_ref, *, tile):
    side = pl.program_id(0)
    step = pl.program_id(1)
    section = table[0]
    live = jnp.where(side == 0, table[2], table[4]) == 1
    columns = pl.ds(pl.multiple_of(step * tile, tile), tile)

    @pl.when((side == 0) & (step == 0) & (section == 1))
    def _():
        total_ref[...] = jnp.zeros_like(total_ref)

    @pl.when(live & (section == 0) & (side == 0))
    def _():
        right_ref[:, columns] = jnp.dot(
            own_ref[...], weight_ref[...], preferred_element_type=F32
        ).astype(BF16)

    @pl.when(live & (section == 0) & (side == 1))
    def _():
        left_ref[:, columns] = jnp.dot(
            own_ref[...], weight_ref[...], preferred_element_type=F32
        ).astype(BF16)

    @pl.when(live & (section == 1) & (side == 0))
    def _():
        total_ref[...] += lax.dot_general(
            from_left_ref[:, columns], weight_ref[...], CONTRACT_LAST, preferred_element_type=F32
        )

    @pl.when(live & (section == 1) & (side == 1))
    def _():
        total_ref[...] += lax.dot_general(
            from_right_ref[:, columns], weight_ref[...], CONTRACT_LAST, preferred_element_type=F32
        )


def block_products(table, own, from_left, from_right, weight):
    rows, width = own.shape
    tile = min(512, width)
    tiles = width // tile

    def weight_index(side, step, table):
        first = jnp.where(table[2] == 1, table[1] * tiles + step, table[3] * tiles)
        second = jnp.where(table[4] == 1, table[3] * tiles + step, table[1] * tiles + tiles - 1)
        return (0, jnp.where(side == 0, first, second))

    whole = pl.BlockSpec((rows, width), lambda side, step, table: (0, 0))
    return pl.pallas_call(
        functools.partial(block_kernel, tile=tile),
        grid_spec=pltpu.PrefetchScalarGridSpec(
            num_scalar_prefetch=1,
            grid=(2, tiles),
            in_specs=[whole, whole, whole, pl.BlockSpec((width, tile), weight_index)],
            out_specs=[whole, whole, whole],
        ),
        out_shape=[
            jax.ShapeDtypeStruct((rows, width), BF16),
            jax.ShapeDtypeStruct((rows, width), BF16),
            jax.ShapeDtypeStruct((rows, width), F32),
        ],
        compiler_params=pltpu.CompilerParams(vmem_limit_bytes=24 * 1024 * 1024),
        cost_estimate=pl.CostEstimate(
            flops=2 * rows * width * width, bytes_accessed=2 * width * width, transcendentals=0
        ),
    )(table, own, from_left, from_right, weight)


def sum_over_tensor(value, wire):
    count = lax.axis_size("tensor")
    if count & (count - 1):
        return lax.psum(value.astype(wire), "tensor").astype(F32)
    distance = 1
    while distance < count:
        other = lax.ppermute(
            value.astype(wire), "tensor", [(place, place ^ distance) for place in range(count)]
        )
        value = value + other.astype(F32)
        distance *= 2
    return value


def with_other_replicas(value):
    count = lax.axis_size("replica")
    return [value] + [
        lax.ppermute(value, "replica", [(place, (place + step) % count) for place in range(count)])
        for step in range(1, count)
    ]


def on_device(
    tokens,
    cotangent,
    gain,
    frozen_base_weight,
    adapter_down_factors,
    adapter_up_factors,
    tenant_adapter_scale,
    row_tenant_owner,
):
    section = lax.axis_index("section")
    place = lax.axis_index("tensor")
    count = lax.axis_size("tensor")
    is_first = section == 0
    weight = frozen_base_weight[0]
    gain_row = gain[0][None, :]
    down = adapter_down_factors[0]
    up = adapter_up_factors[0]
    rows, width = tokens.shape
    features = width * count
    rank = down.shape[1] // TENANT_COUNT

    owners = jnp.arange(TENANT_COUNT, dtype=jnp.int32)
    coefficients = tenant_adapter_scale[None, :] * (
        row_tenant_owner[:, None] == owners[None, :]
    ).astype(F32)
    coefficients = jnp.repeat(coefficients, rank, axis=1)

    token_float = tokens.astype(F32)
    early = jnp.where(is_first, (token_float * gain_row).astype(BF16), cotangent)

    def line(value, first_pairs, second_pairs, toward):
        pairs = [(2 * z, 2 * (z + toward)) for z in first_pairs] + [
            (2 * z + 1, 2 * (z + toward) + 1) for z in second_pairs
        ]
        return lax.ppermute(value, ("tensor", "section"), pairs)

    def table_of(first_right, first_right_live, first_left, first_left_live, step):
        from_left, from_right = place - step, place + step
        entries = [
            section,
            jnp.clip(jnp.where(is_first, first_right, from_left), 0, count - 1),
            jnp.where(is_first, first_right_live, from_left >= 0),
            jnp.clip(jnp.where(is_first, first_left, from_right), 0, count - 1),
            jnp.where(is_first, first_left_live, (from_right < count) & (step > 0)),
        ]
        return jnp.stack([entry.astype(jnp.int32) for entry in entries])

    everyone = range(count)
    from_left = line(cotangent, [], [z for z in everyone if z + 1 < count], 1)
    from_right = line(cotangent, [], [z for z in everyone if z > 0], -1)
    early_all = with_other_replicas(early)

    total = jnp.zeros((rows, width), F32)
    arrived_left, arrived_right = early, early
    for step in range(count):
        slot = step + 1
        if slot < count:
            table = table_of(
                count - slot + place, place + 1 <= slot, place + slot - count, place >= count - slot, step
            )
        else:
            table = table_of(place, place >= 0, place, place < 0, step)
        to_right, to_left, part = block_products(table, early, arrived_left, arrived_right, weight)
        total = total + part
        if slot < count:
            arrived_left, arrived_right = from_left, from_right
            to_right = jnp.where(
                is_first, to_right.astype(F32) + from_left.astype(F32), from_left.astype(F32)
            ).astype(BF16)
            to_left = jnp.where(
                is_first, to_left.astype(F32) + from_right.astype(F32), from_right.astype(F32)
            ).astype(BF16)
            passing = slot + 1
            from_left = line(
                to_right,
                [z for z in everyone if z + 1 <= slot and z + 1 < count],
                [z for z in everyone if passing < count and z >= passing - 1 and z + 1 < count],
                1,
            )
            from_right = line(
                to_left,
                [z for z in everyone if z >= count - slot and z > 0],
                [z for z in everyone if passing < count and z <= count - passing and z > 0],
                -1,
            )
    own_block = to_right

    rank_early = jnp.where(
        is_first,
        jnp.dot(early, down, preferred_element_type=F32),
        lax.dot_general(early, up, CONTRACT_LAST, preferred_element_type=F32),
    )
    squares = jnp.sum(token_float * token_float, axis=1, keepdims=True)
    summed = sum_over_tensor(
        jnp.concatenate([rank_early, jnp.broadcast_to(squares, (rows, 128))], axis=1), BF16
    )
    rank_early = summed[:, : down.shape[1]]
    inv_first = lax.rsqrt(summed[:, down.shape[1] :][:, :1] / features + EPSILON)
    small_early = (coefficients * rank_early).astype(BF16)
    low_product = jnp.where(
        is_first,
        jnp.dot(small_early, up, preferred_element_type=F32),
        lax.dot_general(small_early, down, CONTRACT_LAST, preferred_element_type=F32),
    )

    pulled = (gain_row * (total + low_product)).astype(BF16)
    pulled = lax.ppermute(pulled, "section", [(1, 0)]).astype(F32)

    projected = (
        own_block.astype(F32) + from_left.astype(F32) + from_right.astype(F32) + low_product
    )
    hidden = (token_float + inv_first * projected).astype(BF16)
    hidden_on_second = lax.ppermute(hidden, "section", [(0, 1)])
    hidden_float = hidden.astype(F32)
    row_sums = jnp.stack(
        [jnp.sum(hidden_float * hidden_float, axis=1), jnp.sum(hidden_float * pulled, axis=1)]
    )
    row_sums = sum_over_tensor(row_sums, F32)
    inv_second = lax.rsqrt(row_sums[0] / features + EPSILON)
    toward_hidden = row_sums[1] * inv_second * inv_second * inv_second / features
    inv_on_second = lax.ppermute(inv_second, "section", [(0, 1)])
    hidden_grad = (
        cotangent.astype(F32)
        + inv_second[:, None] * pulled
        - toward_hidden[:, None] * hidden_float
    ).astype(BF16)
    late = jnp.where(
        is_first, hidden_grad, (hidden_on_second.astype(F32) * gain_row).astype(BF16)
    )
    late_all = with_other_replicas(late)
    rank_late = jnp.where(
        is_first,
        lax.dot_general(late, up, CONTRACT_LAST, preferred_element_type=F32),
        jnp.dot(late, down, preferred_element_type=F32),
    )
    rank_late = sum_over_tensor(rank_late, BF16)
    row_scale = jnp.where(is_first, inv_first, inv_on_second[:, None])
    small_late = (coefficients * rank_late * row_scale).astype(BF16)
    small_early = (small_early.astype(F32) * row_scale).astype(BF16)
    smalls = jnp.where(
        is_first,
        jnp.concatenate([small_late, small_early], axis=1),
        jnp.concatenate([small_early, small_late], axis=1),
    )
    smalls = jnp.concatenate(with_other_replicas(smalls), axis=0)
    early_all = jnp.concatenate(early_all, axis=0)
    late_all = jnp.concatenate(late_all, axis=0)
    grad_down = lax.dot_general(
        jnp.where(is_first, early_all, late_all),
        smalls[:, : down.shape[1]],
        CONTRACT_FIRST,
        preferred_element_type=F32,
    )
    grad_up = lax.dot_general(
        smalls[:, down.shape[1] :],
        jnp.where(is_first, late_all, early_all),
        CONTRACT_FIRST,
        preferred_element_type=F32,
    )
    return (grad_down[None], grad_up[None])


def solution(mesh):
    return jax.shard_map(
        on_device,
        mesh=mesh,
        in_specs=(
            P(("groups", "replica"), "tensor"),
            P(("groups", "replica"), "tensor"),
            P("section", "tensor"),
            P("section", "tensor", None),
            P("section", "tensor", None),
            P("section", None, "tensor"),
            P(),
            P(("groups", "replica")),
        ),
        out_specs=(P("section", "tensor", "groups"), P("section", "groups", "tensor")),
        check_vma=False,
    )
```

time: 454 us -> 137 us (0.30)
  blocking collectives: 150 us -> 0 us
  matrix products: 141 us -> 9.22 us
  waiting for transfers between devices: 122 us -> 47.7 us
  starting transfers between devices: 9.69 us -> 38.7 us
  Pallas kernels: 0 us -> 24.8 us
  between operations: 14.9 us -> 1.13 us
    psum x8 -> x0, blocking collectives: 150 us -> none  [the longest x3 56.6 us: backward_layer(): lax.psum(rank_part.astype(jnp.bfloat16), 'tensor').astype(jnp.float32)]
    dot_general x30 -> x8, matrix products: 141 us -> 9.22 us  [the longest x1 3.35 us: on_device(): lax.dot_general(jnp.where(is_first, early_all, late_all), smalls[:, :down...]
    psum x1 -> x0, waiting for transfers between devices: 61.4 us -> none  [on_device(): lax.psum(total_down.astype(jnp.bfloat16), 'replica').astype(jnp.float32)]
    ppermute x6 -> x20, waiting for transfers between devices: 5.69 us -> 47.7 us  [the longest x3 27.3 us: with_other_replicas(): lax.ppermute(value, 'replica', [(place, (place + step) % count) for place...]
    reduce_scatter x4 -> x0, waiting for transfers between devices: 36.8 us -> none  [forward_layer(): lax.psum_scatter(partial_sum.astype(jnp.bfloat16), 'tensor', scatter_dime...]
    ppermute x6 -> x20, starting transfers between devices: 9.36 us -> 38.7 us  [the longest x8 16.1 us: line(): return lax.ppermute(value, ('tensor', 'section'), pairs)]
    pallas_call x0 -> x4, Pallas kernels: none -> 24.8 us  [block_products(): pl.pallas_call(functools.partial(block_kernel, tile=tile), grid_spec=pltp...]
    all_gather x3 -> x0, waiting for transfers between devices: 17.9 us -> none  [backward_layer(): lax.all_gather(proj_grad, 'tensor', axis=1, tiled=True)]
  transfers between devices with their start and end apart: 14 -> 20, of which waited for: 14 -> 10; matrix products, arithmetic and copies ran while one was open for 11% -> 10% of each run, Pallas kernels for 0% -> 18%
where the time goes in v1:
time: 137 us; the launch traced here: 136 us
  waiting for transfers between devices  47.7 us (35%)
  starting transfers between devices  38.7 us (28%)
  Pallas kernels  24.8 us (18%)
  other arithmetic  10.9 us (8%)
  matrix products  9.22 us (7%)
  local copies, waits for them, and re-layouts  3.66 us (3%)
    ppermute x3, waiting for transfers between devices, with_other_replicas(): lax.ppermute(value, 'replica', [(place, (place + step) % count) for place...  27.3 us
    pallas_call x4, Pallas kernels, block_products(): pl.pallas_call(functools.partial(block_kernel, tile=tile), grid_spec=pltp...  24.8 us
    ppermute x8, starting transfers between devices, line(): return lax.ppermute(value, ('tensor', 'section'), pairs)  16.1 us
    ppermute x6, starting transfers between devices, sum_over_tensor(): lax.ppermute(value.astype(wire), 'tensor', [(place, place ^ distance) for...  14.5 us
    ppermute x6, waiting for transfers between devices, sum_over_tensor(): lax.ppermute(value.astype(wire), 'tensor', [(place, place ^ distance) for...  8.51 us
    ppermute x8, waiting for transfers between devices, line(): return lax.ppermute(value, ('tensor', 'section'), pairs)  7.82 us
    ppermute x1, waiting for transfers between devices, on_device(): pulled = lax.ppermute(pulled, 'section', [(1, 0)]).astype(F32)  4.03 us
    ppermute x3, starting transfers between devices, with_other_replicas(): lax.ppermute(value, 'replica', [(place, (place + step) % count) for place...  3.46 us
  transfers between devices with their start and end apart: 20, of which 10 were waited for; matrix products, arithmetic and copies ran while one was open for 10% of the time, Pallas kernels for 18%

profile of v1, /device:TPU:0, one launch (start us, length us, event | category | flops | bytes accessed | tf_op | source)
XLA Modules:
  0.0 136.2 jit_solution(11322129220302770873)
XLA Ops:
  2.2 1.4 %fusion.4 = f32[192]{0:T(256)S(1)} fusion(bf16[192,2048]{1,0:T(8,128)(2,1)} %param.8), kind=kLoop, calls=%fused_computation.20 | loop fusion | flops 1179456 | bytes 787200 | tf_op jit(solution)/shard_map/reduce_sum | solution.py:200
  3.6 1.5 %fusion.28.own_ref.from_left_ref.from_right_ref = bf16[192,2048]{1,0:T(8,128)(2,1)S(1)} fusion(bf16[192,2048]{1,0:T(8,128)(2,1)} %param.9, bf16[192,2048]{1,0:T(8,128)(2,1)} %param.8, f32[2048]{0:T(1024)} %bitcast.56, pred[]{:T(512)S(6)} %eq.16), kind=kLoop, calls=%fused_computation.50 | loop fusion | flops 1572864 | bytes 2367489 | tf_op jit(solution)/shard_map/jit(_where)/select_n | solution.py:136
  7.4 3.0 %collective-permute-start.1 = (bf16[192,384]{1,0:T(8,128)(2,1)}, bf16[192,384]{1,0:T(8,128)(2,1)}, u32[]{:S(2)}, u32[]{:S(2)}) collective-permute-start(bf16[192,384]{1,0:T(8,128)(2,1)} %fusion.29), channel_id=1, source_target_pairs={{0,4},{4,0},{8,12},{12,8},{1,5},{5,1},{9,13},{13,9},{2,6},{6,2},{1... | collective-permute-start | bytes 442376 | tf_op jit(solution)/shard_map/ppermute | solution.py:91
  11.2 1.8 %copy.10 = f32[192,256]{1,0:T(8,128)} copy(f32[192,256]{0,1:T(8,128)} %bitcast.55) | data formatting | bytes 393216 | tf_op jit(solution)/shard_map/reshape | solution.py:133
  13.3 2.2 %collective-permute-done.1 = bf16[192,384]{1,0:T(8,128)(2,1)} collective-permute-done((bf16[192,384]{1,0:T(8,128)(2,1)}, bf16[192,384]{1,0:T(8,128)(2,1)}, u32[]{:S(2)}, u32[]{:S(2)}) %collective-permute-start.1) | collective-permute-done | bytes 147488 | tf_op jit(solution)/shard_map/ppermute | solution.py:91
  16.5 3.1 %collective-permute-start.2 = (bf16[192,384]{1,0:T(8,128)(2,1)S(1)}, bf16[192,384]{1,0:T(8,128)(2,1)S(1)}, u32[]{:S(2)}, u32[]{:S(2)}) collective-permute-start(bf16[192,384]{1,0:T(8,128)(2,1)S(1)} %fusion.30), channel_id=1, source_target_pairs={{0,8},{4,12},{8,0},{12,4},{1,9},{5,13},{9,1},{13,5},{2,10},{6,14},... | collective-permute-start | bytes 442376 | tf_op jit(solution)/shard_map/ppermute | solution.py:91
  19.6 6.0 %shard_map.96 = (bf16[192,2048]{1,0:T(8,128)(2,1)S(1)}, bf16[192,2048]{1,0:T(8,128)(2,1)S(1)}, f32[192,2048]{1,0:T(8,128)S(1)}) custom-call(s32[5]{0:T(128)S(1)} %stack.120.table, bf16[192,2048]{1,0:T(8,128)(2,1)S(1)} %fusion.28.own_ref.from_left_ref.from_right_ref, bf16[192,2048]{1,0:T(8,128)(2,1)S(1)} %fusion.28.own_ref.from_left_ref.from_right_ref, ...), custom_call_target="tpu_custom_call" | custom-call | flops 1610612736 | bytes 8388608 | tf_op jit(solution)/shard_map/pallas_call | solution.py:65
  27.0 2.0 %collective-permute-start.5 = (bf16[192,2048]{1,0:T(8,128)(2,1)S(1)}, bf16[192,2048]{1,0:T(8,128)(2,1)S(1)}, u32[]{:S(2)}, u32[]{:S(2)}) collective-permute-start(bf16[192,2048]{1,0:T(8,128)(2,1)S(1)} %fusion.6), channel_id=1, source_target_pairs={{0,4},{6,10},{10,14},{1,5},{7,11},{11,15},{16,20},{22,26},{26,30},... | collective-permute-start | bytes 2359304 | tf_op jit(solution)/shard_map/ppermute | solution.py:142
  30.4 6.0 %shard_map.95 = (bf16[192,2048]{1,0:T(8,128)(2,1)S(1)}, bf16[192,2048]{1,0:T(8,128)(2,1)S(1)}, f32[192,2048]{1,0:T(8,128)S(1)}) custom-call(s32[5]{0:T(128)S(1)} %stack.113.table, bf16[192,2048]{1,0:T(8,128)(2,1)S(1)} %fusion.28.own_ref.from_left_ref.from_right_ref, bf16[192,2048]{1,0:T(8,128)(2,1)S(1)} %collective-permute-done.3.from_left_ref, ...), custom_call_target="tpu_custom_call" | custom-call | flops 1610612736 | bytes 8388608 | tf_op jit(solution)/shard_map/pallas_call | solution.py:65
  36.4 2.0 %collective-permute-done.5.from_left_ref = bf16[192,2048]{1,0:T(8,128)(2,1)S(1)} collective-permute-done((bf16[192,2048]{1,0:T(8,128)(2,1)S(1)}, bf16[192,2048]{1,0:T(8,128)(2,1)S(1)}, u32[]{:S(2)}, u32[]{:S(2)}) %collective-permute-start.5) | collective-permute-done | bytes 786464 | tf_op jit(solution)/shard_map/ppermute | solution.py:142
  38.7 4.6 %collective-permute-start.6 = (bf16[192,2048]{1,0:T(8,128)(2,1)S(1)}, bf16[192,2048]{1,0:T(8,128)(2,1)S(1)}, u32[]{:S(2)}, u32[]{:S(2)}) collective-permute-start(bf16[192,2048]{1,0:T(8,128)(2,1)S(1)} %fusion.7), channel_id=1, source_target_pairs={{0,4},{4,8},{10,14},{1,5},{5,9},{11,15},{16,20},{20,24},{26,30},{1... | collective-permute-start | bytes 2359304 | tf_op jit(solution)/shard_map/ppermute | solution.py:142
  44.8 6.0 %shard_map.98 = (bf16[192,2048]{1,0:T(8,128)(2,1)S(1)}, bf16[192,2048]{1,0:T(8,128)(2,1)S(1)}, f32[192,2048]{1,0:T(8,128)S(1)}) custom-call(s32[5]{0:T(128)S(1)} %stack.127.table, bf16[192,2048]{1,0:T(8,128)(2,1)S(1)} %fusion.28.own_ref.from_left_ref.from_right_ref, bf16[192,2048]{1,0:T(8,128)(2,1)S(1)} %collective-permute-done.5.from_left_ref, ...), custom_call_target="tpu_custom_call" | custom-call | flops 1610612736 | bytes 8388608 | tf_op jit(solution)/shard_map/pallas_call | solution.py:65
  50.8 1.9 %collective-permute-done.6.from_left_ref = bf16[192,2048]{1,0:T(8,128)(2,1)S(1)} collective-permute-done((bf16[192,2048]{1,0:T(8,128)(2,1)S(1)}, bf16[192,2048]{1,0:T(8,128)(2,1)S(1)}, u32[]{:S(2)}, u32[]{:S(2)}) %collective-permute-start.6) | collective-permute-done | bytes 786464 | tf_op jit(solution)/shard_map/ppermute | solution.py:142
  53.0 5.1 %collective-permute-start.9 = (bf16[192,2048]{1,0:T(8,128)(2,1)S(1)}, bf16[192,2048]{1,0:T(8,128)(2,1)S(1)}, u32[]{:S(2)}, u32[]{:S(2)}) collective-permute-start(bf16[192,2048]{1,0:T(8,128)(2,1)S(1)} %fusion.10), channel_id=1, source_target_pairs={{0,4},{4,8},{8,12},{1,5},{5,9},{9,13},{16,20},{20,24},{24,28},{17,... | collective-permute-start | bytes 2359304 | tf_op jit(solution)/shard_map/ppermute | solution.py:142
  58.4 1.5 %collective-permute-start.10 = (bf16[192,2048]{1,0:T(8,128)(2,1)S(1)}, bf16[192,2048]{1,0:T(8,128)(2,1)S(1)}, u32[]{:S(2)}, u32[]{:S(2)}) collective-permute-start(bf16[192,2048]{1,0:T(8,128)(2,1)S(1)} %fusion.11), channel_id=1, source_target_pairs={{4,0},{8,4},{12,8},{5,1},{9,5},{13,9},{20,16},{24,20},{28,24},{21,... | collective-permute-start | bytes 2359304 | tf_op jit(solution)/shard_map/ppermute | solution.py:142
  59.9 6.9 %shard_map.97 = (bf16[192,2048]{1,0:T(8,128)(2,1)S(1)}, bf16[192,2048]{1,0:T(8,128)(2,1)}, f32[192,2048]{1,0:T(8,128)S(1)}) custom-call(s32[5]{0:T(128)S(1)} %stack.106.table, bf16[192,2048]{1,0:T(8,128)(2,1)S(1)} %fusion.28.own_ref.from_left_ref.from_right_ref, bf16[192,2048]{1,0:T(8,128)(2,1)S(1)} %collective-permute-done.6.from_left_ref, ...), custom_call_target="tpu_custom_call" | custom-call | flops 1610612736 | bytes 8388608 | tf_op jit(solution)/shard_map/pallas_call | solution.py:65
  67.6 1.3 collective-permute-start.11
  69.0 3.9 %collective-permute-done.10 = bf16[192,2048]{1,0:T(8,128)(2,1)S(1)} collective-permute-done((bf16[192,2048]{1,0:T(8,128)(2,1)S(1)}, bf16[192,2048]{1,0:T(8,128)(2,1)S(1)}, u32[]{:S(2)}, u32[]{:S(2)}) %collective-permute-start.10) | collective-permute-done | bytes 786464 | tf_op jit(solution)/shard_map/ppermute | solution.py:142
  72.9 4.0 %collective-permute-done.11 = bf16[192,2048]{1,0:T(8,128)(2,1)S(1)} collective-permute-done((bf16[192,2048]{1,0:T(8,128)(2,1)S(1)}, bf16[192,2048]{1,0:T(8,128)(2,1)S(1)}, u32[]{:S(2)}, u32[]{:S(2)}) %collective-permute-start.11) | collective-permute-done | bytes 786464 | tf_op jit(solution)/shard_map/ppermute | solution.py:214
  77.9 2.1 %collective-permute-start.14 = (bf16[192,2048]{1,0:T(8,128)(2,1)S(1)}, bf16[192,2048]{1,0:T(8,128)(2,1)S(1)}, u32[]{:S(2)}, u32[]{:S(2)}) collective-permute-start(bf16[192,2048]{1,0:T(8,128)(2,1)S(1)} %get-tuple-element.26), channel_id=1, source_target_pairs={{0,2},{1,3},{4,6},{5,7},{8,10},{9,11},{12,14},{13,15},{16,18},{17,... | collective-permute-start | bytes 2359304 | tf_op jit(solution)/shard_map/ppermute | solution.py:220
  80.0 1.5 %collective-permute-done.12 = f32[2,192]{1,0:T(2,128)S(1)} collective-permute-done((f32[2,192]{1,0:T(2,128)S(1)}, f32[2,192]{1,0:T(2,128)S(1)}, u32[]{:S(2)}, u32[]{:S(2)}) %collective-permute-start.12) | collective-permute-done | bytes 1568 | tf_op jit(solution)/shard_map/ppermute | solution.py:91
  81.5 3.5 %collective-permute-start.13 = (f32[2,192]{1,0:T(2,128)S(1)}, f32[2,192]{1,0:T(2,128)S(1)}, u32[]{:S(2)}, u32[]{:S(2)}) collective-permute-start(f32[2,192]{1,0:T(2,128)S(1)} %fusion.45), channel_id=1, source_target_pairs={{0,8},{4,12},{8,0},{12,4},{1,9},{5,13},{9,1},{13,5},{2,10},{6,14},... | collective-permute-start | bytes 4616 | tf_op jit(solution)/shard_map/ppermute | solution.py:91
  84.9 1.6 %collective-permute-done.13 = f32[2,192]{1,0:T(2,128)S(1)} collective-permute-done((f32[2,192]{1,0:T(2,128)S(1)}, f32[2,192]{1,0:T(2,128)S(1)}, u32[]{:S(2)}, u32[]{:S(2)}) %collective-permute-start.13) | collective-permute-done | bytes 1568 | tf_op jit(solution)/shard_map/ppermute | solution.py:91
  88.1 1.8 %collective-permute-start.16 = (bf16[192,256]{1,0:T(8,128)(2,1)S(1)}, bf16[192,256]{1,0:T(8,128)(2,1)S(1)}, u32[]{:S(2)}, u32[]{:S(2)}) collective-permute-start(bf16[192,256]{1,0:T(8,128)(2,1)S(1)} %get-tuple-element.31), channel_id=1, source_target_pairs={{0,4},{4,0},{8,12},{12,8},{1,5},{5,1},{9,13},{13,9},{2,6},{6,2},{1... | collective-permute-start | bytes 294920 | tf_op jit(solution)/shard_map/ppermute | solution.py:91
  92.2 1.3 collective-permute-start.15
  93.5 3.0 %collective-permute-start.17 = (bf16[192,256]{1,0:T(8,128)(2,1)S(1)}, bf16[192,256]{1,0:T(8,128)(2,1)S(1)}, u32[]{:S(2)}, u32[]{:S(2)}) collective-permute-start(bf16[192,256]{1,0:T(8,128)(2,1)S(1)} %fusion.35), channel_id=1, source_target_pairs={{0,8},{4,12},{8,0},{12,4},{1,9},{5,13},{9,1},{13,5},{2,10},{6,14},... | collective-permute-start | bytes 294920 | tf_op jit(solution)/shard_map/ppermute | solution.py:91
  97.5 3.3 %collective-permute-done.17 = bf16[192,256]{1,0:T(8,128)(2,1)S(1)} collective-permute-done((bf16[192,256]{1,0:T(8,128)(2,1)S(1)}, bf16[192,256]{1,0:T(8,128)(2,1)S(1)}, u32[]{:S(2)}, u32[]{:S(2)}) %collective-permute-start.17) | collective-permute-done | bytes 98336 | tf_op jit(solution)/shard_map/ppermute | solution.py:91
  101.0 1.3 collective-permute-start.19
  102.3 9.6 %collective-permute-done = bf16[192,2048]{1,0:T(8,128)(2,1)} collective-permute-done((bf16[192,2048]{1,0:T(8,128)(2,1)S(1)}, bf16[192,2048]{1,0:T(8,128)(2,1)}, u32[]{:S(2)}, u32[]{:S(2)}) %collective-permute-start) | collective-permute-done | bytes 786464 | tf_op jit(solution)/shard_map/ppermute | solution.py:102
  111.8 17.8 %collective-permute-done.19 = bf16[192,512]{1,0:T(8,128)(2,1)S(1)} collective-permute-done((bf16[192,512]{1,0:T(8,128)(2,1)S(1)}, bf16[192,512]{1,0:T(8,128)(2,1)S(1)}, u32[]{:S(2)}, u32[]{:S(2)}) %collective-permute-start.19) | collective-permute-done | bytes 196640 | tf_op jit(solution)/shard_map/ppermute | solution.py:102
  129.6 3.2 %convolution_bitcast_fusion = f32[1,256,2048]{2,1,0:T(8,128)} fusion(pred[]{:T(512)S(6)} %eq.16, bf16[192,2048]{1,0:T(8,128)(2,1)S(1)} %collective-permute-done.15, bf16[192,2048]{1,0:T(8,128)(2,1)S(1)} %fusion.27, bf16[192,2048]{1,0:T(8,128)(2,1)} %collective-permute-done, bf16[192,2048]{1,0:T(8,128)(2,1)S(1)} %fusion.28.own_ref.from_left_ref.from_right_ref, ...), kind=kOutput, calls=%fused_computation | convolution fusion | flops 410124288 | bytes 5636097 | tf_op jit(solution)/shard_map/dot_general | solution.py:261
  132.8 3.3 %convolution_bitcast_fusion.1 = f32[1,2048,256]{2,1,0:T(8,128)} fusion(pred[]{:T(512)S(6)} %eq.16, bf16[192,2048]{1,0:T(8,128)(2,1)S(1)} %collective-permute-done.15, bf16[192,2048]{1,0:T(8,128)(2,1)S(1)} %fusion.27, bf16[192,2048]{1,0:T(8,128)(2,1)} %collective-permute-done, bf16[192,2048]{1,0:T(8,128)(2,1)S(1)} %fusion.28.own_ref.from_left_ref.from_right_ref, ...), kind=kOutput, calls=%fused_computation.1 | convolution fusion | flops 410124288 | bytes 5636097 | tf_op jit(solution)/shard_map/dot_general | solution.py:255
  (80 shorter events, 17.8 us)
Async XLA Ops:
  0.6 4.9 %copy-start = (bf16[1,256,2048]{2,1,0:T(8,128)(2,1)S(1)}, bf16[1,256,2048]{2,1,0:T(8,128)(2,1)}, u32[]{:S(2)}) copy-start(bf16[1,256,2048]{2,1,0:T(8,128)(2,1)} %param.13) | copy-start | bytes 3145732
  0.6 26.0 %collective-permute-start.3 = (bf16[192,2048]{1,0:T(8,128)(2,1)}, bf16[192,2048]{1,0:T(8,128)(2,1)S(1)}, u32[]{:S(2)}, u32[]{:S(2)}) collective-permute-start(bf16[192,2048]{1,0:T(8,128)(2,1)} %param.9), channel_id=1, source_target_pairs={{2,6},{6,10},{10,14},{3,7},{7,11},{11,15},{18,22},{22,26},{26,30},... | collective-permute-start | bytes 2359304 | tf_op jit(solution)/shard_map/ppermute | solution.py:142
  1.5 27.5 %collective-permute-start.4 = (bf16[192,2048]{1,0:T(8,128)(2,1)}, bf16[192,2048]{1,0:T(8,128)(2,1)S(1)}, u32[]{:S(2)}, u32[]{:S(2)}) collective-permute-start(bf16[192,2048]{1,0:T(8,128)(2,1)} %param.9), channel_id=1, source_target_pairs={{6,2},{10,6},{14,10},{7,3},{11,7},{15,11},{22,18},{26,22},{30,26},... | collective-permute-start | bytes 2359304 | tf_op jit(solution)/shard_map/ppermute | solution.py:142
  3.6 1.5 %copy-start.1 = (bf16[1,2048,256]{2,1,0:T(8,128)(2,1)S(1)}, bf16[1,2048,256]{2,1,0:T(8,128)(2,1)}, u32[]{:S(2)}) copy-start(bf16[1,2048,256]{2,1,0:T(8,128)(2,1)} %param.12) | copy-start | bytes 3145732
  5.5 4.9 %copy-start.11 = (s32[192]{0:T(256)S(1)}, s32[192]{0:T(256)}, u32[]{:S(2)}) copy-start(s32[192]{0:T(256)} %param.15) | copy-start | bytes 2308
  5.5 4.9 %copy-start.12 = (f32[4]{0:T(128)S(1)}, f32[4]{0:T(128)}, u32[]{:S(2)}) copy-start(f32[4]{0:T(128)} %param.14) | copy-start | bytes 52
  7.4 8.1 %collective-permute-start.1 = (bf16[192,384]{1,0:T(8,128)(2,1)}, bf16[192,384]{1,0:T(8,128)(2,1)}, u32[]{:S(2)}, u32[]{:S(2)}) collective-permute-start(bf16[192,384]{1,0:T(8,128)(2,1)} %fusion.29), channel_id=1, source_target_pairs={{0,4},{4,0},{8,12},{12,8},{1,5},{5,1},{9,13},{13,9},{2,6},{6,2},{1... | collective-permute-start | bytes 442376 | tf_op jit(solution)/shard_map/ppermute | solution.py:91
  16.5 9.1 %collective-permute-start.2 = (bf16[192,384]{1,0:T(8,128)(2,1)S(1)}, bf16[192,384]{1,0:T(8,128)(2,1)S(1)}, u32[]{:S(2)}, u32[]{:S(2)}) collective-permute-start(bf16[192,384]{1,0:T(8,128)(2,1)S(1)} %fusion.30), channel_id=1, source_target_pairs={{0,8},{4,12},{8,0},{12,4},{1,9},{5,13},{9,1},{13,5},{2,10},{6,14},... | collective-permute-start | bytes 442376 | tf_op jit(solution)/shard_map/ppermute | solution.py:91
  19.6 6.0 %copy-start.5 = (f32[192,256]{1,0:T(8,128)S(1)}, f32[192,256]{1,0:T(8,128)}, u32[]{:S(2)}) copy-start(f32[192,256]{1,0:T(8,128)} %copy-done.4) | copy-start | bytes 589828
  19.6 7.0 %copy-start.7 = (f32[192,256]{1,0:T(8,128)S(1)}, f32[192,256]{1,0:T(8,128)}, u32[]{:S(2)}) copy-start(f32[192,256]{1,0:T(8,128)} %copy.10) | copy-start | bytes 589828
  26.6 42.3 %copy-start.9 = (f32[192,384]{1,0:T(8,128)}, f32[192,384]{1,0:T(8,128)S(1)}, u32[]{:S(2)}) copy-start(f32[192,384]{1,0:T(8,128)S(1)} %convert_add_fusion.1) | copy-start | bytes 884740
  27.0 11.5 %collective-permute-start.5 = (bf16[192,2048]{1,0:T(8,128)(2,1)S(1)}, bf16[192,2048]{1,0:T(8,128)(2,1)S(1)}, u32[]{:S(2)}, u32[]{:S(2)}) collective-permute-start(bf16[192,2048]{1,0:T(8,128)(2,1)S(1)} %fusion.6), channel_id=1, source_target_pairs={{0,4},{6,10},{10,14},{1,5},{7,11},{11,15},{16,20},{22,26},{26,30},... | collective-permute-start | bytes 2359304 | tf_op jit(solution)/shard_map/ppermute | solution.py:142
  29.3 14.0 %collective-permute-start.7 = (bf16[192,2048]{1,0:T(8,128)(2,1)S(1)}, bf16[192,2048]{1,0:T(8,128)(2,1)S(1)}, u32[]{:S(2)}, u32[]{:S(2)}) collective-permute-start(bf16[192,2048]{1,0:T(8,128)(2,1)S(1)} %fusion.8), channel_id=1, source_target_pairs={{12,8},{6,2},{10,6},{13,9},{7,3},{11,7},{28,24},{22,18},{26,22},{2... | collective-permute-start | bytes 2359304 | tf_op jit(solution)/shard_map/ppermute | solution.py:142
  38.7 5.6 %copy-start.2 = (bf16[1,2048,256]{2,1,0:T(8,128)(2,1)S(1)}, bf16[1,2048,256]{2,1,0:T(8,128)(2,1)}, u32[]{:S(2)}) copy-start(bf16[1,2048,256]{2,1,0:T(8,128)(2,1)} %param.12) | copy-start | bytes 3145732
  38.7 14.0 %collective-permute-start.6 = (bf16[192,2048]{1,0:T(8,128)(2,1)S(1)}, bf16[192,2048]{1,0:T(8,128)(2,1)S(1)}, u32[]{:S(2)}, u32[]{:S(2)}) collective-permute-start(bf16[192,2048]{1,0:T(8,128)(2,1)S(1)} %fusion.7), channel_id=1, source_target_pairs={{0,4},{4,8},{10,14},{1,5},{5,9},{11,15},{16,20},{20,24},{26,30},{1... | collective-permute-start | bytes 2359304 | tf_op jit(solution)/shard_map/ppermute | solution.py:142
  43.6 14.5 %collective-permute-start.8 = (bf16[192,2048]{1,0:T(8,128)(2,1)S(1)}, bf16[192,2048]{1,0:T(8,128)(2,1)S(1)}, u32[]{:S(2)}, u32[]{:S(2)}) collective-permute-start(bf16[192,2048]{1,0:T(8,128)(2,1)S(1)} %fusion.9), channel_id=1, source_target_pairs={{8,4},{12,8},{6,2},{9,5},{13,9},{7,3},{24,20},{28,24},{22,18},{25,... | collective-permute-start | bytes 2359304 | tf_op jit(solution)/shard_map/ppermute | solution.py:142
  53.0 16.0 %collective-permute-start.9 = (bf16[192,2048]{1,0:T(8,128)(2,1)S(1)}, bf16[192,2048]{1,0:T(8,128)(2,1)S(1)}, u32[]{:S(2)}, u32[]{:S(2)}) collective-permute-start(bf16[192,2048]{1,0:T(8,128)(2,1)S(1)} %fusion.10), channel_id=1, source_target_pairs={{0,4},{4,8},{8,12},{1,5},{5,9},{9,13},{16,20},{20,24},{24,28},{17,... | collective-permute-start | bytes 2359304 | tf_op jit(solution)/shard_map/ppermute | solution.py:142
  58.4 8.4 %copy-start.10 = (f32[1,2048]{1,0:T(1,128)S(1)}, f32[1,2048]{1,0:T(1,128)}, u32[]{:S(2)}) copy-start(f32[1,2048]{1,0:T(1,128)} %param.10) | copy-start | bytes 24580
  58.4 14.5 %collective-permute-start.10 = (bf16[192,2048]{1,0:T(8,128)(2,1)S(1)}, bf16[192,2048]{1,0:T(8,128)(2,1)S(1)}, u32[]{:S(2)}, u32[]{:S(2)}) collective-permute-start(bf16[192,2048]{1,0:T(8,128)(2,1)S(1)} %fusion.11), channel_id=1, source_target_pairs={{4,0},{8,4},{12,8},{5,1},{9,5},{13,9},{20,16},{24,20},{28,24},{21,... | collective-permute-start | bytes 2359304 | tf_op jit(solution)/shard_map/ppermute | solution.py:142
  66.8 10.2 %copy-start.3 = (bf16[192,2048]{1,0:T(8,128)(2,1)S(1)}, bf16[192,2048]{1,0:T(8,128)(2,1)}, u32[]{:S(2)}) copy-start(bf16[192,2048]{1,0:T(8,128)(2,1)} %param.8) | copy-start | bytes 2359300
  67.6 9.3 %collective-permute-start.11 = (bf16[192,2048]{1,0:T(8,128)(2,1)S(1)}, bf16[192,2048]{1,0:T(8,128)(2,1)S(1)}, u32[]{:S(2)}, u32[]{:S(2)}) collective-permute-start(bf16[192,2048]{1,0:T(8,128)(2,1)S(1)} %multiply_convert_fusion.1), channel_id=1, source_target_pairs={{2,0},{3,1},{6,4},{7,5},{10,8},{11,9},{14,12},{15,13},{18,16},{19,... | collective-permute-start | bytes 2359304 | tf_op jit(solution)/shard_map/ppermute | solution.py:214
  76.9 9.6 %copy-start.6 = (bf16[192,2048]{1,0:T(8,128)(2,1)S(1)}, bf16[192,2048]{1,0:T(8,128)(2,1)}, u32[]{:S(2)}) copy-start(bf16[192,2048]{1,0:T(8,128)(2,1)} %param.9) | copy-start | bytes 2359300
  77.8 3.6 %collective-permute-start.12 = (f32[2,192]{1,0:T(2,128)S(1)}, f32[2,192]{1,0:T(2,128)S(1)}, u32[]{:S(2)}, u32[]{:S(2)}) collective-permute-start(f32[2,192]{1,0:T(2,128)S(1)} %pad_maximum_fusion.9), channel_id=1, source_target_pairs={{0,4},{4,0},{8,12},{12,8},{1,5},{5,1},{9,13},{13,9},{2,6},{6,2},{1... | collective-permute-start | bytes 4616 | tf_op jit(solution)/shard_map/ppermute | solution.py:91
  77.9 8.6 %collective-permute-start.14 = (bf16[192,2048]{1,0:T(8,128)(2,1)S(1)}, bf16[192,2048]{1,0:T(8,128)(2,1)S(1)}, u32[]{:S(2)}, u32[]{:S(2)}) collective-permute-start(bf16[192,2048]{1,0:T(8,128)(2,1)S(1)} %get-tuple-element.26), channel_id=1, source_target_pairs={{0,2},{1,3},{4,6},{5,7},{8,10},{9,11},{12,14},{13,15},{16,18},{17,... | collective-permute-start | bytes 2359304 | tf_op jit(solution)/shard_map/ppermute | solution.py:220
  81.5 5.0 %collective-permute-start.13 = (f32[2,192]{1,0:T(2,128)S(1)}, f32[2,192]{1,0:T(2,128)S(1)}, u32[]{:S(2)}, u32[]{:S(2)}) collective-permute-start(f32[2,192]{1,0:T(2,128)S(1)} %fusion.45), channel_id=1, source_target_pairs={{0,8},{4,12},{8,0},{12,4},{1,9},{5,13},{9,1},{13,5},{2,10},{6,14},... | collective-permute-start | bytes 4616 | tf_op jit(solution)/shard_map/ppermute | solution.py:91
  87.5 13.2 %copy-start.8 = (f32[192,256]{1,0:T(8,128)S(1)}, f32[192,256]{1,0:T(8,128)}, u32[]{:S(2)}) copy-start(f32[192,256]{1,0:T(8,128)} %copy.10) | copy-start | bytes 589828
  88.1 5.4 %collective-permute-start.16 = (bf16[192,256]{1,0:T(8,128)(2,1)S(1)}, bf16[192,256]{1,0:T(8,128)(2,1)S(1)}, u32[]{:S(2)}, u32[]{:S(2)}) collective-permute-start(bf16[192,256]{1,0:T(8,128)(2,1)S(1)} %get-tuple-element.31), channel_id=1, source_target_pairs={{0,4},{4,0},{8,12},{12,8},{1,5},{5,1},{9,13},{13,9},{2,6},{6,2},{1... | collective-permute-start | bytes 294920 | tf_op jit(solution)/shard_map/ppermute | solution.py:91
  89.9 2.1 %collective-permute-start.18 = (f32[192]{0:T(256)S(1)}, f32[192]{0:T(256)S(1)}, u32[]{:S(2)}, u32[]{:S(2)}) collective-permute-start(f32[192]{0:T(256)S(1)} %bitcast.67), channel_id=1, source_target_pairs={{0,2},{1,3},{4,6},{5,7},{8,10},{9,11},{12,14},{13,15},{16,18},{17,... | collective-permute-start | bytes 2312 | tf_op jit(solution)/shard_map/ppermute | solution.py:228
  91.2 20.7 %collective-permute-start = (bf16[192,2048]{1,0:T(8,128)(2,1)S(1)}, bf16[192,2048]{1,0:T(8,128)(2,1)}, u32[]{:S(2)}, u32[]{:S(2)}) collective-permute-start(bf16[192,2048]{1,0:T(8,128)(2,1)S(1)} %fusion.28.own_ref.from_left_ref.from_right_ref), channel_id=1, source_target_pairs={{0,1},{1,0},{2,3},{3,2},{4,5},{5,4},{6,7},{7,6},{8,9},{9,8},{10,11... | collective-permute-start | bytes 2359304 | tf_op jit(solution)/shard_map/ppermute | solution.py:102
  92.2 37.4 %collective-permute-start.15 = (bf16[192,2048]{1,0:T(8,128)(2,1)S(1)}, bf16[192,2048]{1,0:T(8,128)(2,1)S(1)}, u32[]{:S(2)}, u32[]{:S(2)}) collective-permute-start(bf16[192,2048]{1,0:T(8,128)(2,1)S(1)} %fusion.27), channel_id=1, source_target_pairs={{0,1},{1,0},{2,3},{3,2},{4,5},{5,4},{6,7},{7,6},{8,9},{9,8},{10,11... | collective-permute-start | bytes 2359304 | tf_op jit(solution)/shard_map/ppermute | solution.py:102
  93.5 7.3 %collective-permute-start.17 = (bf16[192,256]{1,0:T(8,128)(2,1)S(1)}, bf16[192,256]{1,0:T(8,128)(2,1)S(1)}, u32[]{:S(2)}, u32[]{:S(2)}) collective-permute-start(bf16[192,256]{1,0:T(8,128)(2,1)S(1)} %fusion.35), channel_id=1, source_target_pairs={{0,8},{4,12},{8,0},{12,4},{1,9},{5,13},{9,1},{13,5},{2,10},{6,14},... | collective-permute-start | bytes 294920 | tf_op jit(solution)/shard_map/ppermute | solution.py:91
  101.0 28.6 %collective-permute-start.19 = (bf16[192,512]{1,0:T(8,128)(2,1)S(1)}, bf16[192,512]{1,0:T(8,128)(2,1)S(1)}, u32[]{:S(2)}, u32[]{:S(2)}) collective-permute-start(bf16[192,512]{1,0:T(8,128)(2,1)S(1)} %maximum_select_fusion), channel_id=1, source_target_pairs={{0,1},{1,0},{2,3},{3,2},{4,5},{5,4},{6,7},{7,6},{8,9},{9,8},{10,11... | collective-permute-start | bytes 589832 | tf_op jit(solution)/shard_map/ppermute | solution.py:102
  (1 other events, 0.7 us)

commit v2 on v1

--- a/solution.py
+++ b/solution.py
@@ -135,6 +135,13 @@
     token_float = tokens.astype(F32)
     early = jnp.where(is_first, (token_float * gain_row).astype(BF16), cotangent)
 
+    def small_product(value, first_factor, second_factor):
+        return jnp.where(
+            is_first,
+            jnp.dot(value, first_factor, preferred_element_type=F32),
+            lax.dot_general(value, second_factor, CONTRACT_LAST, preferred_element_type=F32),
+        )
+
     def line(value, first_pairs, second_pairs, toward):
         pairs = [(2 * z, 2 * (z + toward)) for z in first_pairs] + [
             (2 * z + 1, 2 * (z + toward) + 1) for z in second_pairs
@@ -159,6 +166,7 @@
 
     total = jnp.zeros((rows, width), F32)
     arrived_left, arrived_right = early, early
+    small_sum = None
     for step in range(count):
         slot = step + 1
         if slot < count:
@@ -169,6 +177,17 @@
             table = table_of(place, place >= 0, place, place < 0, step)
         to_right, to_left, part = block_products(table, early, arrived_left, arrived_right, weight)
         total = total + part
+        if step == 0:
+            after, to_right = lax.optimization_barrier((early, to_right))
+            small_sum = small_product(after, down, up)
+            squares = jnp.sum(token_float * token_float, axis=1, keepdims=True)
+            small_sum = sum_over_tensor(
+                jnp.concatenate([small_sum, jnp.broadcast_to(squares, (rows, 128))], axis=1), BF16
+            )
+        if step == 1:
+            to_right, *early_all = lax.optimization_barrier((to_right, *early_all))
+        if step == count - 2:
+            to_right, small_sum = lax.optimization_barrier((to_right, small_sum))
         if slot < count:
             arrived_left, arrived_right = from_left, from_right
             to_right = jnp.where(
@@ -177,6 +196,9 @@
             to_left = jnp.where(
                 is_first, to_left.astype(F32) + from_right.astype(F32), from_right.astype(F32)
             ).astype(BF16)
+            to_right, to_left, arrived_left, arrived_right = lax.optimization_barrier(
+                (to_right, to_left, arrived_left, arrived_right)
+            )
             passing = slot + 1
             from_left = line(
                 to_right,
@@ -192,17 +214,8 @@
             )
     own_block = to_right
 
-    rank_early = jnp.where(
-        is_first,
-        jnp.dot(early, down, preferred_element_type=F32),
-        lax.dot_general(early, up, CONTRACT_LAST, preferred_element_type=F32),
-    )
-    squares = jnp.sum(token_float * token_float, axis=1, keepdims=True)
-    summed = sum_over_tensor(
-        jnp.concatenate([rank_early, jnp.broadcast_to(squares, (rows, 128))], axis=1), BF16
-    )
-    rank_early = summed[:, : down.shape[1]]
-    inv_first = lax.rsqrt(summed[:, down.shape[1] :][:, :1] / features + EPSILON)
+    rank_early = small_sum[:, : down.shape[1]]
+    inv_first = lax.rsqrt(small_sum[:, down.shape[1] :][:, :1] / features + EPSILON)
     small_early = (coefficients * rank_early).astype(BF16)
     low_product = jnp.where(
         is_first,

time: 137 us -> 142 us (1.036)
  starting transfers between devices: 38.7 us -> 52.8 us
  waiting for transfers between devices: 47.7 us -> 33.7 us
  other arithmetic: 10.9 us -> 14.6 us
  local copies, waits for them, and re-layouts: 3.66 us -> 6.81 us
  matrix products: 9.22 us -> 6.98 us
    ppermute x3, waiting for transfers between devices: 27.3 us -> 9.17 us  [with_other_replicas(): lax.ppermute(value, 'replica', [(place, (place + step) % count) for place...]
    ppermute x8, starting transfers between devices: 16.1 us -> 28.3 us  [line(): return lax.ppermute(value, ('tensor', 'section'), pairs)]
    ppermute x8, waiting for transfers between devices: 7.82 us -> 18.5 us  [line(): return lax.ppermute(value, ('tensor', 'section'), pairs)]
    ppermute x1, waiting for transfers between devices: 4.03 us -> 0.01 us  [on_device(): pulled = lax.ppermute(pulled, 'section', [(1, 0)]).astype(F32)]
    convert_element_type x3, other arithmetic: 0.83 us -> 4.1 us  [on_device(): to_left = jnp.where(is_first, to_left.astype(F32) + from_right.astype(F32...]
    ppermute x6, waiting for transfers between devices: 8.51 us -> 5.99 us  [sum_over_tensor(): lax.ppermute(value.astype(wire), 'tensor', [(place, place ^ distance) for...]
    unnamed x26 -> x43, local copies, waits for them, and re-layouts: 0.65 us -> 2.6 us
    ppermute x3, starting transfers between devices: 3.46 us -> 5.09 us  [with_other_replicas(): lax.ppermute(value, 'replica', [(place, (place + step) % count) for place...]
  transfers between devices with their start and end apart: 20 -> 20, of which waited for: 10 -> 10; matrix products, arithmetic and copies ran while one was open for 10% -> 14% of each run, Pallas kernels for 18% -> 13%
where the time goes in v2:
time: 142 us; the launch traced here: 141 us
  starting transfers between devices  52.8 us (37%)
  waiting for transfers between devices  33.7 us (24%)
  Pallas kernels  25.1 us (18%)
  other arithmetic  14.6 us (10%)
  matrix products  6.98 us (5%)
  local copies, waits for them, and re-layouts  6.81 us (5%)
    ppermute x8, starting transfers between devices, line(): return lax.ppermute(value, ('tensor', 'section'), pairs)  28.3 us
    pallas_call x4, Pallas kernels, block_products(): pl.pallas_call(functools.partial(block_kernel, tile=tile), grid_spec=pltp...  25.1 us
    ppermute x8, waiting for transfers between devices, line(): return lax.ppermute(value, ('tensor', 'section'), pairs)  18.5 us
    ppermute x6, starting transfers between devices, sum_over_tensor(): lax.ppermute(value.astype(wire), 'tensor', [(place, place ^ distance) for...  15.5 us
    ppermute x3, waiting for transfers between devices, with_other_replicas(): lax.ppermute(value, 'replica', [(place, (place + step) % count) for place...  9.17 us
    ppermute x6, waiting for transfers between devices, sum_over_tensor(): lax.ppermute(value.astype(wire), 'tensor', [(place, place ^ distance) for...  5.99 us
    ppermute x3, starting transfers between devices, with_other_replicas(): lax.ppermute(value, 'replica', [(place, (place + step) % count) for place...  5.09 us
    convert_element_type x3, other arithmetic, on_device(): to_left = jnp.where(is_first, to_left.astype(F32) + from_right.astype(F32...  4.1 us
  transfers between devices with their start and end apart: 20, of which 10 were waited for; matrix products, arithmetic and copies ran while one was open for 14% of the time, Pallas kernels for 13%

profile of v2, /device:TPU:0, one launch (start us, length us, event | category | flops | bytes accessed | tf_op | source)
XLA Modules:
  0.0 141.2 jit_solution(12956204966634670808)
XLA Ops:
  2.2 1.4 fusion.28.own_ref.from_left_ref.from_right_ref
  3.6 3.0 %collective-permute-start.2 = (bf16[192,2048]{1,0:T(8,128)(2,1)S(1)}, bf16[192,2048]{1,0:T(8,128)(2,1)}, u32[]{:S(2)}, u32[]{:S(2)}) collective-permute-start(bf16[192,2048]{1,0:T(8,128)(2,1)S(1)} %fusion.28.own_ref.from_left_ref.from_right_ref), channel_id=1, source_target_pairs={{0,1},{1,0},{2,3},{3,2},{4,5},{5,4},{6,7},{7,6},{8,9},{9,8},{10,11... | collective-permute-start | bytes 2359304 | tf_op jit(solution)/shard_map/ppermute | solution.py:102
  6.7 6.0 %shard_map.95 = (bf16[192,2048]{1,0:T(8,128)(2,1)S(1)}, bf16[192,2048]{1,0:T(8,128)(2,1)S(1)}, f32[192,2048]{1,0:T(8,128)S(1)}) custom-call(s32[5]{0:T(128)S(1)} %stack.113.table, bf16[192,2048]{1,0:T(8,128)(2,1)S(1)} %fusion.28.own_ref.from_left_ref.from_right_ref, bf16[192,2048]{1,0:T(8,128)(2,1)S(1)} %fusion.28.own_ref.from_left_ref.from_right_ref, ...), custom_call_target="tpu_custom_call" | custom-call | flops 1610612736 | bytes 8388608 | tf_op jit(solution)/shard_map/pallas_call | solution.py:65
  16.3 2.4 %fusion.7 = bf16[192,2048]{1,0:T(8,128)(2,1)} fusion(bf16[192,2048]{1,0:T(8,128)(2,1)S(1)} %collective-permute-done.1.from_right_ref, bf16[192,2048]{1,0:T(8,128)(2,1)} %copy-done.5, pred[]{:T(512)S(6)} %eq.16), kind=kLoop, calls=%fused_computation.23 | loop fusion | flops 1966080 | bytes 2359297 | tf_op jit(solution)/shard_map/convert_element_type | solution.py:198
  19.9 1.6 %collective-permute-start.4 = (bf16[192,2048]{1,0:T(8,128)(2,1)}, bf16[192,2048]{1,0:T(8,128)(2,1)}, u32[]{:S(2)}, u32[]{:S(2)}) collective-permute-start(bf16[192,2048]{1,0:T(8,128)(2,1)} %fusion.7), channel_id=1, source_target_pairs={{12,8},{6,2},{10,6},{13,9},{7,3},{11,7},{28,24},{22,18},{26,22},{2... | collective-permute-start | bytes 2359304 | tf_op jit(solution)/shard_map/ppermute | solution.py:149
  21.7 1.6 %fusion.30 = bf16[192,384]{1,0:T(8,128)(2,1)} fusion(bf16[192,384]{1,0:T(8,128)(2,1)} %collective-permute-done.5, f32[192,128]{1,0:T(8,128)S(1)} %broadcast_in_dim.10, f32[192,256]{1,0:T(8,128)S(1)} %copy-done.13), kind=kLoop, calls=%fused_computation.56 | loop fusion | flops 294912 | bytes 589824 | tf_op jit(solution)/shard_map/convert_element_type | solution.py:92
  23.3 4.2 %collective-permute-start.6 = (bf16[192,384]{1,0:T(8,128)(2,1)}, bf16[192,384]{1,0:T(8,128)(2,1)}, u32[]{:S(2)}, u32[]{:S(2)}) collective-permute-start(bf16[192,384]{1,0:T(8,128)(2,1)} %fusion.30), channel_id=1, source_target_pairs={{0,8},{4,12},{8,0},{12,4},{1,9},{5,13},{9,1},{13,5},{2,10},{6,14},... | collective-permute-start | bytes 442376 | tf_op jit(solution)/shard_map/ppermute | solution.py:91
  28.3 1.7 %copy.10 = f32[192,256]{1,0:T(8,128)} copy(f32[192,256]{0,1:T(8,128)} %bitcast.55) | data formatting | bytes 393216 | tf_op jit(solution)/shard_map/reshape | solution.py:133
  30.3 5.5 %collective-permute-start.3 = (bf16[192,2048]{1,0:T(8,128)(2,1)}, bf16[192,2048]{1,0:T(8,128)(2,1)S(1)}, u32[]{:S(2)}, u32[]{:S(2)}) collective-permute-start(bf16[192,2048]{1,0:T(8,128)(2,1)} %fusion.6), channel_id=1, source_target_pairs={{0,4},{6,10},{10,14},{1,5},{7,11},{11,15},{16,20},{22,26},{26,30},... | collective-permute-start | bytes 2359304 | tf_op jit(solution)/shard_map/ppermute | solution.py:149
  36.9 6.0 %shard_map.96 = (bf16[192,2048]{1,0:T(8,128)(2,1)S(1)}, bf16[192,2048]{1,0:T(8,128)(2,1)S(1)}, f32[192,2048]{1,0:T(8,128)S(1)}) custom-call(s32[5]{0:T(128)S(1)} %stack.106.table, bf16[192,2048]{1,0:T(8,128)(2,1)S(1)} %fusion.28.own_ref.from_left_ref.from_right_ref, bf16[192,2048]{1,0:T(8,128)(2,1)S(1)} %collective-permute-done.from_left_ref, ...), custom_call_target="tpu_custom_call" | custom-call | flops 1610612736 | bytes 8388608 | tf_op jit(solution)/shard_map/pallas_call | solution.py:65
  43.0 1.4 fusion.9
  46.7 6.3 %shard_map.97 = (bf16[192,2048]{1,0:T(8,128)(2,1)S(1)}, bf16[192,2048]{1,0:T(8,128)(2,1)S(1)}, f32[192,2048]{1,0:T(8,128)S(1)}) custom-call(s32[5]{0:T(128)S(1)} %stack.120.table, bf16[192,2048]{1,0:T(8,128)(2,1)S(1)} %fusion.28.own_ref.from_left_ref.from_right_ref, bf16[192,2048]{1,0:T(8,128)(2,1)S(1)} %collective-permute-done.3.from_left_ref, ...), custom_call_target="tpu_custom_call" | custom-call | flops 1610612736 | bytes 8388608 | tf_op jit(solution)/shard_map/pallas_call | solution.py:65
  53.0 12.4 %collective-permute-start.7 = (bf16[192,2048]{1,0:T(8,128)(2,1)S(1)}, bf16[192,2048]{1,0:T(8,128)(2,1)S(1)}, u32[]{:S(2)}, u32[]{:S(2)}) collective-permute-start(bf16[192,2048]{1,0:T(8,128)(2,1)S(1)} %fusion.8), channel_id=1, source_target_pairs={{0,4},{4,8},{10,14},{1,5},{5,9},{11,15},{16,20},{20,24},{26,30},{1... | collective-permute-start | bytes 2359304 | tf_op jit(solution)/shard_map/ppermute | solution.py:149
  66.7 8.0 %collective-permute-done.7.from_left_ref = bf16[192,2048]{1,0:T(8,128)(2,1)S(1)} collective-permute-done((bf16[192,2048]{1,0:T(8,128)(2,1)S(1)}, bf16[192,2048]{1,0:T(8,128)(2,1)S(1)}, u32[]{:S(2)}, u32[]{:S(2)}) %collective-permute-start.7) | collective-permute-done | bytes 786464 | tf_op jit(solution)/shard_map/ppermute | solution.py:149
  75.0 6.9 %shard_map.98 = (bf16[192,2048]{1,0:T(8,128)(2,1)S(1)}, bf16[192,2048]{1,0:T(8,128)(2,1)}, f32[192,2048]{1,0:T(8,128)S(1)}) custom-call(s32[5]{0:T(128)S(1)} %stack.127.table, bf16[192,2048]{1,0:T(8,128)(2,1)S(1)} %fusion.28.own_ref.from_left_ref.from_right_ref, bf16[192,2048]{1,0:T(8,128)(2,1)S(1)} %collective-permute-done.7.from_left_ref, ...), custom_call_target="tpu_custom_call" | custom-call | flops 1610612736 | bytes 8388608 | tf_op jit(solution)/shard_map/pallas_call | solution.py:65
  82.7 1.3 collective-permute-start.11
  84.0 1.3 collective-permute-start.10
  85.3 5.2 %collective-permute-start.9 = (bf16[192,2048]{1,0:T(8,128)(2,1)S(1)}, bf16[192,2048]{1,0:T(8,128)(2,1)S(1)}, u32[]{:S(2)}, u32[]{:S(2)}) collective-permute-start(bf16[192,2048]{1,0:T(8,128)(2,1)S(1)} %fusion.10), channel_id=1, source_target_pairs={{0,4},{4,8},{8,12},{1,5},{5,9},{9,13},{16,20},{20,24},{24,28},{17,... | collective-permute-start | bytes 2359304 | tf_op jit(solution)/shard_map/ppermute | solution.py:149
  90.7 7.9 %collective-permute-done.10 = bf16[192,2048]{1,0:T(8,128)(2,1)S(1)} collective-permute-done((bf16[192,2048]{1,0:T(8,128)(2,1)S(1)}, bf16[192,2048]{1,0:T(8,128)(2,1)S(1)}, u32[]{:S(2)}, u32[]{:S(2)}) %collective-permute-start.10) | collective-permute-done | bytes 786464 | tf_op jit(solution)/shard_map/ppermute | solution.py:149
  98.5 1.4 %collective-permute-done.9 = bf16[192,2048]{1,0:T(8,128)(2,1)S(1)} collective-permute-done((bf16[192,2048]{1,0:T(8,128)(2,1)S(1)}, bf16[192,2048]{1,0:T(8,128)(2,1)S(1)}, u32[]{:S(2)}, u32[]{:S(2)}) %collective-permute-start.9) | collective-permute-done | bytes 786464 | tf_op jit(solution)/shard_map/ppermute | solution.py:149
  100.9 2.6 %collective-permute-start.12 = (f32[2,192]{1,0:T(2,128)S(1)}, f32[2,192]{1,0:T(2,128)S(1)}, u32[]{:S(2)}, u32[]{:S(2)}) collective-permute-start(f32[2,192]{1,0:T(2,128)S(1)} %pad_maximum_fusion.6), channel_id=1, source_target_pairs={{0,4},{4,0},{8,12},{12,8},{1,5},{5,1},{9,13},{13,9},{2,6},{6,2},{1... | collective-permute-start | bytes 4616 | tf_op jit(solution)/shard_map/ppermute | solution.py:91
  103.4 1.3 collective-permute-start.14
  105.0 4.0 %collective-permute-start.13 = (f32[2,192]{1,0:T(2,128)S(1)}, f32[2,192]{1,0:T(2,128)S(1)}, u32[]{:S(2)}, u32[]{:S(2)}) collective-permute-start(f32[2,192]{1,0:T(2,128)S(1)} %fusion.42), channel_id=1, source_target_pairs={{0,8},{4,12},{8,0},{12,4},{1,9},{5,13},{9,1},{13,5},{2,10},{6,14},... | collective-permute-start | bytes 4616 | tf_op jit(solution)/shard_map/ppermute | solution.py:91
  109.0 1.6 %collective-permute-done.13 = f32[2,192]{1,0:T(2,128)S(1)} collective-permute-done((f32[2,192]{1,0:T(2,128)S(1)}, f32[2,192]{1,0:T(2,128)S(1)}, u32[]{:S(2)}, u32[]{:S(2)}) %collective-permute-start.13) | collective-permute-done | bytes 1568 | tf_op jit(solution)/shard_map/ppermute | solution.py:91
  113.6 2.1 %collective-permute-start.16 = (bf16[192,256]{1,0:T(8,128)(2,1)S(1)}, bf16[192,256]{1,0:T(8,128)(2,1)S(1)}, u32[]{:S(2)}, u32[]{:S(2)}) collective-permute-start(bf16[192,256]{1,0:T(8,128)(2,1)S(1)} %get-tuple-element.69), channel_id=1, source_target_pairs={{0,4},{4,0},{8,12},{12,8},{1,5},{5,1},{9,13},{13,9},{2,6},{6,2},{1... | collective-permute-start | bytes 294920 | tf_op jit(solution)/shard_map/ppermute | solution.py:91
  117.3 1.9 %collective-permute-done.16 = bf16[192,256]{1,0:T(8,128)(2,1)S(1)} collective-permute-done((bf16[192,256]{1,0:T(8,128)(2,1)S(1)}, bf16[192,256]{1,0:T(8,128)(2,1)S(1)}, u32[]{:S(2)}, u32[]{:S(2)}) %collective-permute-start.16) | collective-permute-done | bytes 98336 | tf_op jit(solution)/shard_map/ppermute | solution.py:91
  119.3 2.6 %collective-permute-start.17 = (bf16[192,256]{1,0:T(8,128)(2,1)S(1)}, bf16[192,256]{1,0:T(8,128)(2,1)S(1)}, u32[]{:S(2)}, u32[]{:S(2)}) collective-permute-start(bf16[192,256]{1,0:T(8,128)(2,1)S(1)} %fusion.34), channel_id=1, source_target_pairs={{0,8},{4,12},{8,0},{12,4},{1,9},{5,13},{9,1},{13,5},{2,10},{6,14},... | collective-permute-start | bytes 294920 | tf_op jit(solution)/shard_map/ppermute | solution.py:91
  122.9 2.0 %collective-permute-done.17 = bf16[192,256]{1,0:T(8,128)(2,1)S(1)} collective-permute-done((bf16[192,256]{1,0:T(8,128)(2,1)S(1)}, bf16[192,256]{1,0:T(8,128)(2,1)S(1)}, u32[]{:S(2)}, u32[]{:S(2)}) %collective-permute-start.17) | collective-permute-done | bytes 98336 | tf_op jit(solution)/shard_map/ppermute | solution.py:91
  125.1 1.5 %collective-permute-start.19 = (bf16[192,512]{1,0:T(8,128)(2,1)S(1)}, bf16[192,512]{1,0:T(8,128)(2,1)S(1)}, u32[]{:S(2)}, u32[]{:S(2)}) collective-permute-start(bf16[192,512]{1,0:T(8,128)(2,1)S(1)} %maximum_select_fusion), channel_id=1, source_target_pairs={{0,1},{1,0},{2,3},{3,2},{4,5},{5,4},{6,7},{7,6},{8,9},{9,8},{10,11... | collective-permute-start | bytes 589832 | tf_op jit(solution)/shard_map/ppermute | solution.py:102
  127.8 9.2 %collective-permute-done.19 = bf16[192,512]{1,0:T(8,128)(2,1)S(1)} collective-permute-done((bf16[192,512]{1,0:T(8,128)(2,1)S(1)}, bf16[192,512]{1,0:T(8,128)(2,1)S(1)}, u32[]{:S(2)}, u32[]{:S(2)}) %collective-permute-start.19) | collective-permute-done | bytes 196640 | tf_op jit(solution)/shard_map/ppermute | solution.py:102
  136.9 2.1 %convolution_bitcast_fusion = f32[1,256,2048]{2,1,0:T(8,128)} fusion(bf16[384,2048]{1,0:T(8,128)(2,1)S(1)} %constant_dynamic-update-slice_fusion, pred[]{:T(512)S(6)} %eq.16, bf16[192,2048]{1,0:T(8,128)(2,1)S(1)} %collective-permute-done.15, bf16[192,2048]{1,0:T(8,128)(2,1)S(1)} %copy-done.11, bf16[192,512]{1,0:T(8,128)(2,1)S(1)} %collective-permute-done.19, ...), kind=kOutput, calls=%fused_computation | convolution fusion | flops 406978560 | bytes 5636097 | tf_op jit(solution)/shard_map/dot_general | solution.py:274
  139.0 2.2 %convolution_bitcast_fusion.1 = f32[1,2048,256]{2,1,0:T(8,128)} fusion(bf16[384,2048]{1,0:T(8,128)(2,1)S(1)} %constant_dynamic-update-slice_fusion, pred[]{:T(512)S(6)} %eq.16, bf16[192,2048]{1,0:T(8,128)(2,1)S(1)} %collective-permute-done.15, bf16[192,2048]{1,0:T(8,128)(2,1)S(1)} %copy-done.11, bf16[192,512]{1,0:T(8,128)(2,1)S(1)} %maximum_select_fusion, ...), kind=kOutput, calls=%fused_computation.1 | convolution fusion | flops 406978560 | bytes 5636097 | tf_op jit(solution)/shard_map/dot_general | solution.py:268
  (98 shorter events, 21.6 us)
Async XLA Ops:
  0.6 12.5 %copy-start = (bf16[1,256,2048]{2,1,0:T(8,128)(2,1)S(1)}, bf16[1,256,2048]{2,1,0:T(8,128)(2,1)}, u32[]{:S(2)}) copy-start(bf16[1,256,2048]{2,1,0:T(8,128)(2,1)} %param.13) | copy-start | bytes 3145732
  0.6 15.6 %collective-permute-start.1 = (bf16[192,2048]{1,0:T(8,128)(2,1)}, bf16[192,2048]{1,0:T(8,128)(2,1)S(1)}, u32[]{:S(2)}, u32[]{:S(2)}) collective-permute-start(bf16[192,2048]{1,0:T(8,128)(2,1)} %param.9), channel_id=1, source_target_pairs={{6,2},{10,6},{14,10},{7,3},{11,7},{15,11},{22,18},{26,22},{30,26},... | collective-permute-start | bytes 2359304 | tf_op jit(solution)/shard_map/ppermute | solution.py:149
  1.5 17.2 %collective-permute-start = (bf16[192,2048]{1,0:T(8,128)(2,1)}, bf16[192,2048]{1,0:T(8,128)(2,1)S(1)}, u32[]{:S(2)}, u32[]{:S(2)}) collective-permute-start(bf16[192,2048]{1,0:T(8,128)(2,1)} %param.9), channel_id=1, source_target_pairs={{2,6},{6,10},{10,14},{3,7},{7,11},{11,15},{18,22},{22,26},{26,30},... | collective-permute-start | bytes 2359304 | tf_op jit(solution)/shard_map/ppermute | solution.py:149
  3.6 39.3 %collective-permute-start.2 = (bf16[192,2048]{1,0:T(8,128)(2,1)S(1)}, bf16[192,2048]{1,0:T(8,128)(2,1)}, u32[]{:S(2)}, u32[]{:S(2)}) collective-permute-start(bf16[192,2048]{1,0:T(8,128)(2,1)S(1)} %fusion.28.own_ref.from_left_ref.from_right_ref), channel_id=1, source_target_pairs={{0,1},{1,0},{2,3},{3,2},{4,5},{5,4},{6,7},{7,6},{8,9},{9,8},{10,11... | collective-permute-start | bytes 2359304 | tf_op jit(solution)/shard_map/ppermute | solution.py:102
  6.7 6.0 %copy-start.6 = (bf16[1,2048,256]{2,1,0:T(8,128)(2,1)S(1)}, bf16[1,2048,256]{2,1,0:T(8,128)(2,1)}, u32[]{:S(2)}) copy-start(bf16[1,2048,256]{2,1,0:T(8,128)(2,1)} %param.12) | copy-start | bytes 3145732
  16.2 5.5 %collective-permute-start.5 = (bf16[192,384]{1,0:T(8,128)(2,1)}, bf16[192,384]{1,0:T(8,128)(2,1)}, u32[]{:S(2)}, u32[]{:S(2)}) collective-permute-start(bf16[192,384]{1,0:T(8,128)(2,1)} %fusion.29), channel_id=1, source_target_pairs={{0,4},{4,0},{8,12},{12,8},{1,5},{5,1},{9,13},{13,9},{2,6},{6,2},{1... | collective-permute-start | bytes 442376 | tf_op jit(solution)/shard_map/ppermute | solution.py:91
  18.7 8.8 %copy-start.19 = (s32[192]{0:T(256)S(1)}, s32[192]{0:T(256)}, u32[]{:S(2)}) copy-start(s32[192]{0:T(256)} %param.15) | copy-start | bytes 2308
  18.7 8.8 %copy-start.20 = (f32[4]{0:T(128)S(1)}, f32[4]{0:T(128)}, u32[]{:S(2)}) copy-start(f32[4]{0:T(128)} %param.14) | copy-start | bytes 52
  19.9 23.1 %collective-permute-start.4 = (bf16[192,2048]{1,0:T(8,128)(2,1)}, bf16[192,2048]{1,0:T(8,128)(2,1)}, u32[]{:S(2)}, u32[]{:S(2)}) collective-permute-start(bf16[192,2048]{1,0:T(8,128)(2,1)} %fusion.7), channel_id=1, source_target_pairs={{12,8},{6,2},{10,6},{13,9},{7,3},{11,7},{28,24},{22,18},{26,22},{2... | collective-permute-start | bytes 2359304 | tf_op jit(solution)/shard_map/ppermute | solution.py:149
  23.3 12.5 %collective-permute-start.6 = (bf16[192,384]{1,0:T(8,128)(2,1)}, bf16[192,384]{1,0:T(8,128)(2,1)}, u32[]{:S(2)}, u32[]{:S(2)}) collective-permute-start(bf16[192,384]{1,0:T(8,128)(2,1)} %fusion.30), channel_id=1, source_target_pairs={{0,8},{4,12},{8,0},{12,4},{1,9},{5,13},{9,1},{13,5},{2,10},{6,14},... | collective-permute-start | bytes 442376 | tf_op jit(solution)/shard_map/ppermute | solution.py:91
  30.3 15.2 %collective-permute-start.3 = (bf16[192,2048]{1,0:T(8,128)(2,1)}, bf16[192,2048]{1,0:T(8,128)(2,1)S(1)}, u32[]{:S(2)}, u32[]{:S(2)}) collective-permute-start(bf16[192,2048]{1,0:T(8,128)(2,1)} %fusion.6), channel_id=1, source_target_pairs={{0,4},{6,10},{10,14},{1,5},{7,11},{11,15},{16,20},{22,26},{26,30},... | collective-permute-start | bytes 2359304 | tf_op jit(solution)/shard_map/ppermute | solution.py:149
  36.9 53.6 %copy-start.16 = (f32[192,384]{1,0:T(8,128)}, f32[192,384]{1,0:T(8,128)S(1)}, u32[]{:S(2)}) copy-start(f32[192,384]{1,0:T(8,128)S(1)} %convert_add_fusion.1) | copy-start | bytes 884740
  45.8 19.6 %copy-start.15 = (f32[192,256]{1,0:T(8,128)S(1)}, f32[192,256]{1,0:T(8,128)}, u32[]{:S(2)}) copy-start(f32[192,256]{1,0:T(8,128)} %copy.10) | copy-start | bytes 589828
  45.9 20.5 %collective-permute-start.8 = (bf16[192,2048]{1,0:T(8,128)(2,1)S(1)}, bf16[192,2048]{1,0:T(8,128)(2,1)S(1)}, u32[]{:S(2)}, u32[]{:S(2)}) collective-permute-start(bf16[192,2048]{1,0:T(8,128)(2,1)S(1)} %fusion.9), channel_id=1, source_target_pairs={{8,4},{12,8},{6,2},{9,5},{13,9},{7,3},{24,20},{28,24},{22,18},{25,... | collective-permute-start | bytes 2359304 | tf_op jit(solution)/shard_map/ppermute | solution.py:149
  53.0 12.9 %copy-start.7 = (bf16[1,2048,256]{2,1,0:T(8,128)(2,1)S(1)}, bf16[1,2048,256]{2,1,0:T(8,128)(2,1)}, u32[]{:S(2)}) copy-start(bf16[1,2048,256]{2,1,0:T(8,128)(2,1)} %param.12) | copy-start | bytes 3145732
  53.0 21.7 %collective-permute-start.7 = (bf16[192,2048]{1,0:T(8,128)(2,1)S(1)}, bf16[192,2048]{1,0:T(8,128)(2,1)S(1)}, u32[]{:S(2)}, u32[]{:S(2)}) collective-permute-start(bf16[192,2048]{1,0:T(8,128)(2,1)S(1)} %fusion.8), channel_id=1, source_target_pairs={{0,4},{4,8},{10,14},{1,5},{5,9},{11,15},{16,20},{20,24},{26,30},{1... | collective-permute-start | bytes 2359304 | tf_op jit(solution)/shard_map/ppermute | solution.py:149
  75.0 6.9 %copy-start.2 = (f32[192,2048]{1,0:T(8,128)S(1)}, f32[192,2048]{1,0:T(8,128)}, u32[]{:S(2)}) copy-start(f32[192,2048]{1,0:T(8,128)} %copy-done.1) | copy-start | bytes 4718596
  75.0 6.9 %copy-start.18 = (f32[1,2048]{1,0:T(1,128)S(1)}, f32[1,2048]{1,0:T(1,128)}, u32[]{:S(2)}) copy-start(f32[1,2048]{1,0:T(1,128)} %param.10) | copy-start | bytes 24580
  81.9 18.1 %copy-start.9 = (bf16[192,2048]{1,0:T(8,128)(2,1)S(1)}, bf16[192,2048]{1,0:T(8,128)(2,1)}, u32[]{:S(2)}) copy-start(bf16[192,2048]{1,0:T(8,128)(2,1)} %param.8) | copy-start | bytes 2359300
  82.7 8.0 %collective-permute-start.11 = (bf16[192,2048]{1,0:T(8,128)(2,1)S(1)}, bf16[192,2048]{1,0:T(8,128)(2,1)S(1)}, u32[]{:S(2)}, u32[]{:S(2)}) collective-permute-start(bf16[192,2048]{1,0:T(8,128)(2,1)S(1)} %multiply_convert_fusion.1), channel_id=1, source_target_pairs={{2,0},{3,1},{6,4},{7,5},{10,8},{11,9},{14,12},{15,13},{18,16},{19,... | collective-permute-start | bytes 2359304 | tf_op jit(solution)/shard_map/ppermute | solution.py:227
  84.0 14.5 %collective-permute-start.10 = (bf16[192,2048]{1,0:T(8,128)(2,1)S(1)}, bf16[192,2048]{1,0:T(8,128)(2,1)S(1)}, u32[]{:S(2)}, u32[]{:S(2)}) collective-permute-start(bf16[192,2048]{1,0:T(8,128)(2,1)S(1)} %fusion.11), channel_id=1, source_target_pairs={{4,0},{8,4},{12,8},{5,1},{9,5},{13,9},{20,16},{24,20},{28,24},{21,... | collective-permute-start | bytes 2359304 | tf_op jit(solution)/shard_map/ppermute | solution.py:149
  85.3 14.7 %collective-permute-start.9 = (bf16[192,2048]{1,0:T(8,128)(2,1)S(1)}, bf16[192,2048]{1,0:T(8,128)(2,1)S(1)}, u32[]{:S(2)}, u32[]{:S(2)}) collective-permute-start(bf16[192,2048]{1,0:T(8,128)(2,1)S(1)} %fusion.10), channel_id=1, source_target_pairs={{0,4},{4,8},{8,12},{1,5},{5,9},{9,13},{16,20},{20,24},{24,28},{17,... | collective-permute-start | bytes 2359304 | tf_op jit(solution)/shard_map/ppermute | solution.py:149
  100.0 12.0 %copy-start.14 = (bf16[192,2048]{1,0:T(8,128)(2,1)S(1)}, bf16[192,2048]{1,0:T(8,128)(2,1)}, u32[]{:S(2)}) copy-start(bf16[192,2048]{1,0:T(8,128)(2,1)} %param.9) | copy-start | bytes 2359300
  100.9 4.1 %collective-permute-start.12 = (f32[2,192]{1,0:T(2,128)S(1)}, f32[2,192]{1,0:T(2,128)S(1)}, u32[]{:S(2)}, u32[]{:S(2)}) collective-permute-start(f32[2,192]{1,0:T(2,128)S(1)} %pad_maximum_fusion.6), channel_id=1, source_target_pairs={{0,4},{4,0},{8,12},{12,8},{1,5},{5,1},{9,13},{13,9},{2,6},{6,2},{1... | collective-permute-start | bytes 4616 | tf_op jit(solution)/shard_map/ppermute | solution.py:91
  103.4 8.5 %collective-permute-start.14 = (bf16[192,2048]{1,0:T(8,128)(2,1)S(1)}, bf16[192,2048]{1,0:T(8,128)(2,1)S(1)}, u32[]{:S(2)}, u32[]{:S(2)}) collective-permute-start(bf16[192,2048]{1,0:T(8,128)(2,1)S(1)} %get-tuple-element.64), channel_id=1, source_target_pairs={{0,2},{1,3},{4,6},{5,7},{8,10},{9,11},{12,14},{13,15},{16,18},{17,... | collective-permute-start | bytes 2359304 | tf_op jit(solution)/shard_map/ppermute | solution.py:233
  105.0 5.6 %collective-permute-start.13 = (f32[2,192]{1,0:T(2,128)S(1)}, f32[2,192]{1,0:T(2,128)S(1)}, u32[]{:S(2)}, u32[]{:S(2)}) collective-permute-start(f32[2,192]{1,0:T(2,128)S(1)} %fusion.42), channel_id=1, source_target_pairs={{0,8},{4,12},{8,0},{12,4},{1,9},{5,13},{9,1},{13,5},{2,10},{6,14},... | collective-permute-start | bytes 4616 | tf_op jit(solution)/shard_map/ppermute | solution.py:91
  110.6 6.0 %collective-permute-start.18 = (f32[192]{0:T(256)S(1)}, f32[192]{0:T(256)S(1)}, u32[]{:S(2)}, u32[]{:S(2)}) collective-permute-start(f32[192]{0:T(256)S(1)} %bitcast.65), channel_id=1, source_target_pairs={{0,2},{1,3},{4,6},{5,7},{8,10},{9,11},{12,14},{13,15},{16,18},{17,... | collective-permute-start | bytes 2312 | tf_op jit(solution)/shard_map/ppermute | solution.py:241
  113.6 5.7 %collective-permute-start.16 = (bf16[192,256]{1,0:T(8,128)(2,1)S(1)}, bf16[192,256]{1,0:T(8,128)(2,1)S(1)}, u32[]{:S(2)}, u32[]{:S(2)}) collective-permute-start(bf16[192,256]{1,0:T(8,128)(2,1)S(1)} %get-tuple-element.69), channel_id=1, source_target_pairs={{0,4},{4,0},{8,12},{12,8},{1,5},{5,1},{9,13},{13,9},{2,6},{6,2},{1... | collective-permute-start | bytes 294920 | tf_op jit(solution)/shard_map/ppermute | solution.py:91
  116.7 9.8 %copy-start.17 = (bf16[384,2048]{1,0:T(8,128)(2,1)S(1)}, bf16[384,2048]{1,0:T(8,128)(2,1)}, u32[]{:S(2)}) copy-start(bf16[384,2048]{1,0:T(8,128)(2,1)} %constant_dynamic-update-slice_fusion.1) | copy-start | bytes 4718596
  116.8 20.2 %collective-permute-start.15 = (bf16[192,2048]{1,0:T(8,128)(2,1)S(1)}, bf16[192,2048]{1,0:T(8,128)(2,1)S(1)}, u32[]{:S(2)}, u32[]{:S(2)}) collective-permute-start(bf16[192,2048]{1,0:T(8,128)(2,1)S(1)} %copy-done.11), channel_id=1, source_target_pairs={{0,1},{1,0},{2,3},{3,2},{4,5},{5,4},{6,7},{7,6},{8,9},{9,8},{10,11... | collective-permute-start | bytes 2359304 | tf_op jit(solution)/shard_map/ppermute | solution.py:102
  119.3 5.6 %collective-permute-start.17 = (bf16[192,256]{1,0:T(8,128)(2,1)S(1)}, bf16[192,256]{1,0:T(8,128)(2,1)S(1)}, u32[]{:S(2)}, u32[]{:S(2)}) collective-permute-start(bf16[192,256]{1,0:T(8,128)(2,1)S(1)} %fusion.34), channel_id=1, source_target_pairs={{0,8},{4,12},{8,0},{12,4},{1,9},{5,13},{9,1},{13,5},{2,10},{6,14},... | collective-permute-start | bytes 294920 | tf_op jit(solution)/shard_map/ppermute | solution.py:91
  125.1 11.8 %collective-permute-start.19 = (bf16[192,512]{1,0:T(8,128)(2,1)S(1)}, bf16[192,512]{1,0:T(8,128)(2,1)S(1)}, u32[]{:S(2)}, u32[]{:S(2)}) collective-permute-start(bf16[192,512]{1,0:T(8,128)(2,1)S(1)} %maximum_select_fusion), channel_id=1, source_target_pairs={{0,1},{1,0},{2,3},{3,2},{4,5},{5,4},{6,7},{7,6},{8,9},{9,8},{10,11... | collective-permute-start | bytes 589832 | tf_op jit(solution)/shard_map/ppermute | solution.py:102
  (9 other events, 16.2 us)

commit v3 on v2

v3 whole, which is shorter than its diff:
```python
import functools

import jax
import jax.numpy as jnp
from jax import lax
from jax.experimental import pallas as pl
from jax.experimental.pallas import tpu as pltpu
from jax.sharding import PartitionSpec as P

TENANT_COUNT = 4
EPSILON = 1e-05
CONTRACT_LAST = (((1,), (1,)), ((), ()))
CONTRACT_FIRST = (((0,), (0,)), ((), ()))
BF16 = jnp.bfloat16
F32 = jnp.float32
AHEAD = 2


def block_kernel(table, value_ref, weight_ref, out_ref, wide, tall, arrived, *, stage, tile, tiles):
    section = table[0]
    block = table[1 + stage]
    step = pl.program_id(0)
    width = tile * tiles

    def copy_of(index, is_wide):
        whole = pl.ds(pl.multiple_of(block * width, width), width)
        part = pl.ds(pl.multiple_of(block * width + index * tile, tile), tile)
        if is_wide:
            return pltpu.make_async_copy(weight_ref.at[:, part], wide.at[index], arrived.at[index])
        rows = pl.ds(pl.multiple_of(index * tile, tile), tile)
        return pltpu.make_async_copy(weight_ref.at[rows, whole], tall.at[index], arrived.at[index])

    for number, is_wide in ((0, True), (1, False)):

        @pl.when(section == number)
        def _():
            @pl.when(step == 0)
            def _():
                for index in range(min(AHEAD, tiles)):
                    copy_of(index, is_wide).start()

            @pl.when(step + AHEAD < tiles)
            def _():
                copy_of(step + AHEAD, is_wide).start()

            copy_of(step, is_wide).wait()
            if is_wide:
                out_ref[...] = jnp.dot(value_ref[...], wide[step], preferred_element_type=F32)
            else:
                out_ref[...] = lax.dot_general(
                    value_ref[...], tall[step], CONTRACT_LAST, preferred_element_type=F32
                )


def block_product(table, value, weight, stage):
    rows, width = value.shape
    tile = min(256, width)
    tiles = width // tile
    return pl.pallas_call(
        functools.partial(block_kernel, stage=stage, tile=tile, tiles=tiles),
        grid_spec=pltpu.PrefetchScalarGridSpec(
            num_scalar_prefetch=1,
            grid=(tiles,),
            in_specs=[
                pl.BlockSpec((rows, width), lambda step, table: (0, 0)),
                pl.BlockSpec(memory_space=pl.ANY),
            ],
            out_specs=pl.BlockSpec((rows, tile), lambda step, table: (0, step)),
            scratch_shapes=[
                pltpu.VMEM((tiles, width, tile), BF16),
                pltpu.VMEM((tiles, tile, width), BF16),
                pltpu.SemaphoreType.DMA((tiles,)),
            ],
        ),
        out_shape=jax.ShapeDtypeStruct((rows, width), F32),
        compiler_params=pltpu.CompilerParams(vmem_limit_bytes=24 * 1024 * 1024),
        cost_estimate=pl.CostEstimate(
            flops=2 * rows * width * width, bytes_accessed=2 * width * width, transcendentals=0
        ),
    )(table, value, weight)


def gradient_kernel(table, *refs, replicas):
    early, late, small_early, small_late = (
        refs[kind * replicas : (kind + 1) * replicas] for kind in range(4)
    )
    down_ref, up_ref = refs[4 * replicas :]

    def products(down_rows, down_small, up_rows, up_small):
        down_ref[...] = sum(
            lax.dot_general(a[...], b[...], CONTRACT_FIRST, preferred_element_type=F32)
            for a, b in zip(down_rows, down_small)
        )
        up_ref[...] = sum(
            lax.dot_general(a[...], b[...], CONTRACT_FIRST, preferred_element_type=F32)
            for a, b in zip(up_small, up_rows)
        )

    @pl.when(table[0] == 0)
    def _():
        products(early, small_late, late, small_early)

    @pl.when(table[0] == 1)
    def _():
        products(late, small_early, early, small_late)


def gradients(table, early, late, small_early, small_late):
    replicas = len(early)
    rows, width = early[0].shape
    rank = small_early[0].shape[1]
    tile = min(512, width)
    columns = pl.BlockSpec((rows, tile), lambda step, table: (0, step))
    small = pl.BlockSpec((rows, rank), lambda step, table: (0, 0))
    return pl.pallas_call(
        functools.partial(gradient_kernel, replicas=replicas),
        grid_spec=pltpu.PrefetchScalarGridSpec(
            num_scalar_prefetch=1,
            grid=(width // tile,),
            in_specs=[columns] * (2 * replicas) + [small] * (2 * replicas),
            out_specs=[
                pl.BlockSpec((tile, rank), lambda step, table: (step, 0)),
                pl.BlockSpec((rank, tile), lambda step, table: (0, step)),
            ],
        ),
        out_shape=[
            jax.ShapeDtypeStruct((width, rank), F32),
            jax.ShapeDtypeStruct((rank, width), F32),
        ],
        compiler_params=pltpu.CompilerParams(vmem_limit_bytes=24 * 1024 * 1024),
        cost_estimate=pl.CostEstimate(
            flops=4 * replicas * rows * width * rank,
            bytes_accessed=8 * width * rank + 4 * replicas * rows * width,
            transcendentals=0,
        ),
    )(table, *early, *late, *small_early, *small_late)


def orders(count):
    first, first_slots, second, second_slots = [], [], [], []
    for z in range(count):
        sends = [(slot, 0, count - slot + z) for slot in range(z + 1, count)]
        sends += [(slot, 1, slot - count + z) for slot in range(count - z, count)]
        sends.sort()
        first.append([block for _, _, block in sends] + [z])
        first_slots.append({(slot, side): at for at, (slot, side, _) in enumerate(sends)})
        arrivals = [(slot, 0, z - 1 - slot) for slot in range(z)]
        arrivals += [(slot, 1, z + 1 + slot) for slot in range(count - 1 - z)]
        arrivals.sort()
        second.append([z] + [block for _, _, block in arrivals])
        second_slots.append([None] + [(slot, side) for slot, side, _ in arrivals])
    return first, first_slots, second, second_slots


def pick(place_of, choice, cases):
    if len(cases) == 1:
        return cases[0]
    chosen = jnp.asarray(choice, jnp.int32)[place_of]
    return lax.select_n(chosen, *cases) if len(cases) > 2 else jnp.where(chosen == 0, *cases)


def sum_over_tensor(value, wire):
    count = lax.axis_size("tensor")
    if count & (count - 1):
        return lax.psum(value.astype(wire), "tensor").astype(F32)
    distance = 1
    while distance < count:
        other = lax.ppermute(
            value.astype(wire), "tensor", [(place, place ^ distance) for place in range(count)]
        )
        value = value + other.astype(F32)
        distance *= 2
    return value


def with_other_replicas(value):
    count = lax.axis_size("replica")
    return [value] + [
        lax.ppermute(value, "replica", [(place, (place + step) % count) for place in range(count)])
        for step in range(1, count)
    ]


def on_device(
    tokens,
    cotangent,
    gain,
    frozen_base_weight,
    adapter_down_factors,
    adapter_up_factors,
    tenant_adapter_scale,
    row_tenant_owner,
):
    section = lax.axis_index("section")
    place = lax.axis_index("tensor")
    count = lax.axis_size("tensor")
    is_first = section == 0
    weight = frozen_base_weight[0]
    gain_row = gain[0][None, :]
    down = adapter_down_factors[0]
    up = adapter_up_factors[0]
    rows, width = tokens.shape
    features = width * count
    ranks = down.shape[1]

    tenant_of_column = jnp.arange(ranks, dtype=jnp.int32) // (ranks // TENANT_COUNT)
    coefficients = jnp.where(
        row_tenant_owner[:, None] == tenant_of_column[None, :],
        jnp.repeat(tenant_adapter_scale, ranks // TENANT_COUNT)[None, :],
        0.0,
    )

    first_order, first_slots, second_order, second_slots = orders(count)
    place_of = section * count + place
    table = jnp.concatenate(
        [section[None].astype(jnp.int32), jnp.asarray(first_order + second_order, jnp.int32)[place_of]]
    )

    def small_product(value, first_factor, second_factor):
        return jnp.where(
            is_first,
            jnp.dot(value, first_factor, preferred_element_type=F32),
            lax.dot_general(value, second_factor, CONTRACT_LAST, preferred_element_type=F32),
        )

    def line(value, first_pairs, second_pairs, toward):
        pairs = [(2 * z, 2 * (z + toward)) for z in first_pairs] + [
            (2 * z + 1, 2 * (z + toward) + 1) for z in second_pairs
        ]
        return lax.ppermute(value, ("tensor", "section"), pairs)

    token_float = tokens.astype(F32)
    early = lax.optimization_barrier(
        jnp.where(is_first, (token_float * gain_row).astype(BF16), cotangent)
    )

    everyone = range(count)
    arrivals = [
        (
            line(cotangent, [], [z for z in everyone if z + 1 < count], 1),
            line(cotangent, [], [z for z in everyone if z > 0], -1),
        )
    ]
    early_all = with_other_replicas(early)

    parts = []
    small_sum = None
    for stage in range(count):
        wanted = [None if stage == 0 else second_slots[z][stage] for z in everyone]
        cases = sorted({slot for slot in wanted if slot is not None})
        here = [early] + [arrivals[slot][side] for slot, side in cases]
        if stage > 0:
            *here, _, _ = lax.optimization_barrier((*here, *arrivals[stage - 1]))
        value = pick(
            place_of,
            [0] * count + [0 if slot is None else 1 + cases.index(slot) for slot in wanted],
            here,
        )
        part = block_product(table, value, weight, stage)
        if stage == 0:
            after, part = lax.optimization_barrier((early, part))
            small_sum = small_product(after, down, up)
            squares = jnp.sum(token_float * token_float, axis=1, keepdims=True)
            small_sum = sum_over_tensor(
                jnp.concatenate([small_sum, jnp.broadcast_to(squares, (rows, 128))], axis=1), BF16
            )
        if stage == 1:
            part, *early_all = lax.optimization_barrier((part, *early_all))
        if stage == count - 2:
            part, small_sum = lax.optimization_barrier((part, small_sum))
        parts.append(part)
        slot = stage + 1
        if slot == count:
            break
        sent = []
        for side in (0, 1):
            needed = [first_slots[z].get((slot, side)) for z in everyone]
            stages = sorted({at for at in needed if at is not None})
            own = pick(
                place_of,
                [0 if at is None else stages.index(at) for at in needed] + [0] * count,
                [parts[at] for at in stages],
            )
            arrived = arrivals[-1][side].astype(F32)
            sent.append((arrived + jnp.where(is_first, own, 0.0)).astype(BF16))
        arrivals.append(
            (
                line(
                    sent[0],
                    [z for z in everyone if z < slot and z + 1 < count],
                    [z for z in everyone if slot + 1 < count and z >= slot and z + 1 < count],
                    1,
                ),
                line(
                    sent[1],
                    [z for z in everyone if z >= count - slot and z > 0],
                    [z for z in everyone if slot + 1 < count and z < count - slot and z > 0],
                    -1,
                ),
            )
        )
    from_left, from_right = arrivals[-1]

    inv_first = lax.rsqrt(small_sum[:, ranks:][:, :1] / features + EPSILON)
    small_early = (coefficients * small_sum[:, :ranks]).astype(BF16)
    low_product = jnp.where(
        is_first,
        jnp.dot(small_early, up, preferred_element_type=F32),
        lax.dot_general(small_early, down, CONTRACT_LAST, preferred_element_type=F32),
    )

    parts = lax.optimization_barrier(parts)
    pulled = (gain_row * (sum(parts) + low_product)).astype(BF16)
    pulled = lax.ppermute(pulled, "section", [(1, 0)]).astype(F32)

    projected = parts[-1] + from_left.astype(F32) + from_right.astype(F32) + low_product
    hidden = (token_float + inv_first * projected).astype(BF16)
    hidden_on_second = lax.ppermute(hidden, "section", [(0, 1)])
    hidden_float = hidden.astype(F32)
    row_sums = jnp.stack(
        [jnp.sum(hidden_float * hidden_float, axis=1), jnp.sum(hidden_float * pulled, axis=1)]
    )
    row_sums = sum_over_tensor(row_sums, F32)
    inv_second = lax.rsqrt(row_sums[0] / features + EPSILON)
    toward_hidden = row_sums[1] * inv_second * inv_second * inv_second / features
    inv_on_second = lax.ppermute(inv_second, "section", [(0, 1)])
    hidden_grad = (
        cotangent.astype(F32)
        + inv_second[:, None] * pulled
        - toward_hidden[:, None] * hidden_float
    ).astype(BF16)
    late = jnp.where(
        is_first, hidden_grad, (hidden_on_second.astype(F32) * gain_row).astype(BF16)
    )
    late_all = with_other_replicas(late)
    rank_late = sum_over_tensor(
        jnp.where(
            is_first,
            lax.dot_general(late, up, CONTRACT_LAST, preferred_element_type=F32),
            jnp.dot(late, down, preferred_element_type=F32),
        ),
        BF16,
    )
    row_scale = jnp.where(is_first, inv_first, inv_on_second[:, None])
    small_late = (coefficients * rank_late * row_scale).astype(BF16)
    small_early = (small_early.astype(F32) * row_scale).astype(BF16)
    smalls = with_other_replicas(jnp.concatenate([small_early, small_late], axis=1))
    grad_down, grad_up = gradients(
        table,
        early_all,
        late_all,
        [small[:, :ranks] for small in smalls],
        [small[:, ranks:] for small in smalls],
    )
    return (grad_down[None], grad_up[None])


def solution(mesh):
    return jax.shard_map(
        on_device,
        mesh=mesh,
        in_specs=(
            P(("groups", "replica"), "tensor"),
            P(("groups", "replica"), "tensor"),
            P("section", "tensor"),
            P("section", "tensor", None),
            P("section", "tensor", None),
            P("section", None, "tensor"),
            P(),
            P(("groups", "replica")),
        ),
        out_specs=(P("section", "tensor", "groups"), P("section", "groups", "tensor")),
        check_vma=False,
    )
```

time: 142 us -> 137 us (0.965)
  starting transfers between devices: 52.8 us -> 41.3 us
  between operations: 1.15 us -> 7.96 us
  Pallas kernels: 25.1 us -> 30 us
  matrix products: 6.98 us -> 2.89 us
  waiting for transfers between devices: 33.7 us -> 37.5 us
  other arithmetic: 14.6 us -> 11.1 us
  local copies, waits for them, and re-layouts: 6.81 us -> 4.99 us
    ppermute x8, starting transfers between devices: 28.3 us -> 18.4 us  [line(): return lax.ppermute(value, ('tensor', 'section'), pairs)]
    ppermute x3, waiting for transfers between devices: 9.17 us -> 16.6 us  [with_other_replicas(): lax.ppermute(value, 'replica', [(place, (place + step) % count) for place...]
    ppermute x8, waiting for transfers between devices: 18.5 us -> 11.1 us  [line(): return lax.ppermute(value, ('tensor', 'section'), pairs)]
    pallas_call x4 -> x5, Pallas kernels: 25.1 us -> 30 us  [the longest x4 24.7 us: block_product(): pl.pallas_call(functools.partial(block_kernel, stage=stage, tile=tile, ti...]
    dot_general x2 -> x0, matrix products: 4.31 us -> none  [the longest x1 2.2 us: on_device(): lax.dot_general(jnp.where(is_first, early_all, late_all), smalls[:, :down...]
    convert_element_type x8 -> x3, other arithmetic: 6.66 us -> 2.92 us  [on_device(): sent.append((arrived + jnp.where(is_first, own, 0.0)).astype(BF16))]
    dynamic_slice x0 -> x5, local copies, waits for them, and re-layouts: none -> 3.01 us  [pick(): chosen = jnp.asarray(choice, jnp.int32)[place_of]]
    ppermute x6, waiting for transfers between devices: 5.99 us -> 8.99 us  [sum_over_tensor(): lax.ppermute(value.astype(wire), 'tensor', [(place, place ^ distance) for...]
  transfers between devices with their start and end apart: 20 -> 20, of which waited for: 10 -> 10; matrix products, arithmetic and copies ran while one was open for 14% -> 10% of each run, Pallas kernels for 13% -> 14%
where the time goes in v3:
time: 137 us; the launch traced here: 136 us
  starting transfers between devices  41.3 us (30%)
  waiting for transfers between devices  37.5 us (27%)
  Pallas kernels  30 us (22%)
  other arithmetic  11.1 us (8%)
  between operations  7.96 us (6%)
  local copies, waits for them, and re-layouts  4.99 us (4%)
  matrix products  2.89 us (2%)
    pallas_call x4, Pallas kernels, block_product(): pl.pallas_call(functools.partial(block_kernel, stage=stage, tile=tile, ti...  24.7 us
    ppermute x8, starting transfers between devices, line(): return lax.ppermute(value, ('tensor', 'section'), pairs)  18.4 us
    ppermute x3, waiting for transfers between devices, with_other_replicas(): lax.ppermute(value, 'replica', [(place, (place + step) % count) for place...  16.6 us
    ppermute x6, starting transfers between devices, sum_over_tensor(): lax.ppermute(value.astype(wire), 'tensor', [(place, place ^ distance) for...  16.2 us
    ppermute x8, waiting for transfers between devices, line(): return lax.ppermute(value, ('tensor', 'section'), pairs)  11.1 us
    ppermute x6, waiting for transfers between devices, sum_over_tensor(): lax.ppermute(value.astype(wire), 'tensor', [(place, place ^ distance) for...  8.99 us
    pallas_call x1, Pallas kernels, gradients(): pl.pallas_call(functools.partial(gradient_kernel, replicas=replicas), gri...  5.37 us
    dynamic_slice x5, local copies, waits for them, and re-layouts, pick(): chosen = jnp.asarray(choice, jnp.int32)[place_of]  3.01 us
  transfers between devices with their start and end apart: 20, of which 10 were waited for; matrix products, arithmetic and copies ran while one was open for 10% of the time, Pallas kernels for 14%

profile of v3, /device:TPU:0, one launch (start us, length us, event | category | flops | bytes accessed | tf_op | source)
XLA Modules:
  0.0 135.9 jit_solution(3957159800715053176)
XLA Ops:
  0.6 1.7 %collective-permute-start = (bf16[192,2048]{1,0:T(8,128)(2,1)}, bf16[192,2048]{1,0:T(8,128)(2,1)}, u32[]{:S(2)}, u32[]{:S(2)}) collective-permute-start(bf16[192,2048]{1,0:T(8,128)(2,1)} %param.16), channel_id=1, source_target_pairs={{2,6},{6,10},{10,14},{3,7},{7,11},{11,15},{18,22},{22,26},{26,30},... | collective-permute-start | bytes 2359304 | tf_op jit(solution)/shard_map/ppermute | solution.py:230
  2.4 1.6 %collective-permute-start.1 = (bf16[192,2048]{1,0:T(8,128)(2,1)}, bf16[192,2048]{1,0:T(8,128)(2,1)}, u32[]{:S(2)}, u32[]{:S(2)}) collective-permute-start(bf16[192,2048]{1,0:T(8,128)(2,1)} %param.16), channel_id=1, source_target_pairs={{6,2},{10,6},{14,10},{7,3},{11,7},{15,11},{22,18},{26,22},{30,26},... | collective-permute-start | bytes 2359304 | tf_op jit(solution)/shard_map/ppermute | solution.py:230
  3.9 1.4 %fusion.18.value_ref.refs_0_ = bf16[192,2048]{1,0:T(8,128)(2,1)S(1)} fusion(bf16[192,2048]{1,0:T(8,128)(2,1)} %param.16, bf16[192,2048]{1,0:T(8,128)(2,1)} %param.15, f32[2048]{0:T(1024)} %bitcast.51, pred[]{:T(512)S(6)} %eq.34), kind=kLoop, calls=%fused_computation.36 | loop fusion | flops 1572864 | bytes 2367489 | tf_op jit(solution)/shard_map/jit(_where)/select_n | solution.py:234
  6.1 6.2 %shard_map.159 = f32[192,2048]{1,0:T(8,128)S(1)} custom-call(s32[5]{0:T(128)S(1)} %pad_add_fusion.table, bf16[192,2048]{1,0:T(8,128)(2,1)S(1)} %fusion.18.value_ref.refs_0_, bf16[2048,8192]{1,0:T(8,128)(2,1)} %bitcast.47), custom_call_target="tpu_custom_call" | custom-call | flops 1610612736 | bytes 8388608 | tf_op jit(solution)/shard_map/pallas_call | solution.py:59
  15.1 3.0 %collective-permute-start.5 = (bf16[192,384]{1,0:T(8,128)(2,1)}, bf16[192,384]{1,0:T(8,128)(2,1)}, u32[]{:S(2)}, u32[]{:S(2)}) collective-permute-start(bf16[192,384]{1,0:T(8,128)(2,1)} %fusion.19), channel_id=1, source_target_pairs={{0,4},{4,0},{8,12},{12,8},{1,5},{5,1},{9,13},{13,9},{2,6},{6,2},{1... | collective-permute-start | bytes 442376 | tf_op jit(solution)/shard_map/ppermute | solution.py:168
  18.1 1.5 %collective-permute-start.2 = (bf16[192,2048]{1,0:T(8,128)(2,1)S(1)}, bf16[192,2048]{1,0:T(8,128)(2,1)}, u32[]{:S(2)}, u32[]{:S(2)}) collective-permute-start(bf16[192,2048]{1,0:T(8,128)(2,1)S(1)} %fusion.18.value_ref.refs_0_), channel_id=1, source_target_pairs={{0,1},{1,0},{2,3},{3,2},{4,5},{5,4},{6,7},{7,6},{8,9},{9,8},{10,11... | collective-permute-start | bytes 2359304 | tf_op jit(solution)/shard_map/ppermute | solution.py:179
  29.7 1.0 fusion.20
  30.7 2.6 %collective-permute-start.6 = (bf16[192,384]{1,0:T(8,128)(2,1)S(1)}, bf16[192,384]{1,0:T(8,128)(2,1)S(1)}, u32[]{:S(2)}, u32[]{:S(2)}) collective-permute-start(bf16[192,384]{1,0:T(8,128)(2,1)S(1)} %fusion.20), channel_id=1, source_target_pairs={{0,8},{4,12},{8,0},{12,4},{1,9},{5,13},{9,1},{13,5},{2,10},{6,14},... | collective-permute-start | bytes 442376 | tf_op jit(solution)/shard_map/ppermute | solution.py:168
  33.4 1.8 %add_convert_fusion.4 = (bf16[192,2048]{1,0:T(8,128)(2,1)S(1)}, bf16[192,2048]{1,0:T(8,128)(2,1)S(1)}) fusion(bf16[192,2048]{1,0:T(8,128)(2,1)} %collective-permute-done.1, f32[192,2048]{1,0:T(8,128)S(1)} %shard_map.159, pred[]{:T(512)S(6)} %eq.34, bf16[192,2048]{1,0:T(8,128)(2,1)} %collective-permute-done), kind=kLoop, calls=%fused_computation.22 | loop fusion | flops 2752512 | bytes 4718593 | tf_op jit(solution)/shard_map/convert_element_type | solution.py:285
  35.2 2.4 %collective-permute-start.3 = (bf16[192,2048]{1,0:T(8,128)(2,1)S(1)}, bf16[192,2048]{1,0:T(8,128)(2,1)S(1)}, u32[]{:S(2)}, u32[]{:S(2)}) collective-permute-start(bf16[192,2048]{1,0:T(8,128)(2,1)S(1)} %get-tuple-element.60), channel_id=1, source_target_pairs={{0,4},{6,10},{10,14},{1,5},{7,11},{11,15},{16,20},{22,26},{26,30},... | collective-permute-start | bytes 2359304 | tf_op jit(solution)/shard_map/ppermute | solution.py:230
  38.3 2.8 %collective-permute-done.6 = bf16[192,384]{1,0:T(8,128)(2,1)S(1)} collective-permute-done((bf16[192,384]{1,0:T(8,128)(2,1)S(1)}, bf16[192,384]{1,0:T(8,128)(2,1)S(1)}, u32[]{:S(2)}, u32[]{:S(2)}) %collective-permute-start.6) | collective-permute-done | bytes 147488 | tf_op jit(solution)/shard_map/ppermute | solution.py:168
  42.1 1.4 select_select_fusion.2.value_ref
  43.5 6.2 %shard_map.158 = f32[192,2048]{1,0:T(8,128)S(1)} custom-call(s32[5]{0:T(128)S(1)} %pad_add_fusion.table, bf16[192,2048]{1,0:T(8,128)(2,1)S(1)} %select_select_fusion.2.value_ref, bf16[2048,8192]{1,0:T(8,128)(2,1)} %bitcast.48), custom_call_target="tpu_custom_call" | custom-call | flops 1610612736 | bytes 8388608 | tf_op jit(solution)/shard_map/pallas_call | solution.py:59
  50.2 1.8 %collective-permute-start.7 = (bf16[192,2048]{1,0:T(8,128)(2,1)S(1)}, bf16[192,2048]{1,0:T(8,128)(2,1)S(1)}, u32[]{:S(2)}, u32[]{:S(2)}) collective-permute-start(bf16[192,2048]{1,0:T(8,128)(2,1)S(1)} %get-tuple-element.56), channel_id=1, source_target_pairs={{0,4},{4,8},{10,14},{1,5},{5,9},{11,15},{16,20},{20,24},{26,30},{1... | collective-permute-start | bytes 2359304 | tf_op jit(solution)/shard_map/ppermute | solution.py:230
  53.1 6.2 %shard_map.160 = f32[192,2048]{1,0:T(8,128)S(1)} custom-call(s32[5]{0:T(128)S(1)} %pad_add_fusion.table, bf16[192,2048]{1,0:T(8,128)(2,1)S(1)} %select_select_fusion.1.value_ref, bf16[2048,8192]{1,0:T(8,128)(2,1)} %bitcast.49), custom_call_target="tpu_custom_call" | custom-call | flops 1610612736 | bytes 8388608 | tf_op jit(solution)/shard_map/pallas_call | solution.py:59
  59.7 1.8 %collective-permute-done.7 = bf16[192,2048]{1,0:T(8,128)(2,1)S(1)} collective-permute-done((bf16[192,2048]{1,0:T(8,128)(2,1)S(1)}, bf16[192,2048]{1,0:T(8,128)(2,1)S(1)}, u32[]{:S(2)}, u32[]{:S(2)}) %collective-permute-start.7) | collective-permute-done | bytes 786464 | tf_op jit(solution)/shard_map/ppermute | solution.py:230
  61.8 6.2 %shard_map.161 = f32[192,2048]{1,0:T(8,128)S(1)} custom-call(s32[5]{0:T(128)S(1)} %pad_add_fusion.table, bf16[192,2048]{1,0:T(8,128)(2,1)S(1)} %select_select_fusion.value_ref, bf16[2048,8192]{1,0:T(8,128)(2,1)} %bitcast.50), custom_call_target="tpu_custom_call" | custom-call | flops 1610612736 | bytes 8388608 | tf_op jit(solution)/shard_map/pallas_call | solution.py:59
  68.7 1.4 %collective-permute-start.11 = (bf16[192,2048]{1,0:T(8,128)(2,1)S(1)}, bf16[192,2048]{1,0:T(8,128)(2,1)S(1)}, u32[]{:S(2)}, u32[]{:S(2)}) collective-permute-start(bf16[192,2048]{1,0:T(8,128)(2,1)S(1)} %get-tuple-element.67), channel_id=1, source_target_pairs={{2,0},{3,1},{6,4},{7,5},{10,8},{11,9},{14,12},{15,13},{18,16},{19,... | collective-permute-start | bytes 2359304 | tf_op jit(solution)/shard_map/ppermute | solution.py:314
  70.7 1.3 collective-permute-start.10
  72.0 8.2 %collective-permute-start.9 = (bf16[192,2048]{1,0:T(8,128)(2,1)S(1)}, bf16[192,2048]{1,0:T(8,128)(2,1)S(1)}, u32[]{:S(2)}, u32[]{:S(2)}) collective-permute-start(bf16[192,2048]{1,0:T(8,128)(2,1)S(1)} %get-tuple-element.57), channel_id=1, source_target_pairs={{0,4},{4,8},{8,12},{1,5},{5,9},{9,13},{16,20},{20,24},{24,28},{17,... | collective-permute-start | bytes 2359304 | tf_op jit(solution)/shard_map/ppermute | solution.py:230
  80.3 7.9 %collective-permute-done.10 = bf16[192,2048]{1,0:T(8,128)(2,1)S(1)} collective-permute-done((bf16[192,2048]{1,0:T(8,128)(2,1)S(1)}, bf16[192,2048]{1,0:T(8,128)(2,1)S(1)}, u32[]{:S(2)}, u32[]{:S(2)}) %collective-permute-start.10) | collective-permute-done | bytes 786464 | tf_op jit(solution)/shard_map/ppermute | solution.py:230
  88.2 1.4 %collective-permute-done.9 = bf16[192,2048]{1,0:T(8,128)(2,1)S(1)} collective-permute-done((bf16[192,2048]{1,0:T(8,128)(2,1)S(1)}, bf16[192,2048]{1,0:T(8,128)(2,1)S(1)}, u32[]{:S(2)}, u32[]{:S(2)}) %collective-permute-start.9) | collective-permute-done | bytes 786464 | tf_op jit(solution)/shard_map/ppermute | solution.py:230
  90.4 2.5 %collective-permute-start.12 = (f32[2,192]{1,0:T(2,128)S(1)}, f32[2,192]{1,0:T(2,128)S(1)}, u32[]{:S(2)}, u32[]{:S(2)}) collective-permute-start(f32[2,192]{1,0:T(2,128)S(1)} %pad_maximum_fusion.2), channel_id=1, source_target_pairs={{0,4},{4,0},{8,12},{12,8},{1,5},{5,1},{9,13},{13,9},{2,6},{6,2},{1... | collective-permute-start | bytes 4616 | tf_op jit(solution)/shard_map/ppermute | solution.py:168
  93.0 1.3 collective-permute-start.14
  94.6 3.5 %collective-permute-start.13 = (f32[2,192]{1,0:T(2,128)S(1)}, f32[2,192]{1,0:T(2,128)S(1)}, u32[]{:S(2)}, u32[]{:S(2)}) collective-permute-start(f32[2,192]{1,0:T(2,128)S(1)} %fusion.29), channel_id=1, source_target_pairs={{0,8},{4,12},{8,0},{12,4},{1,9},{5,13},{9,1},{13,5},{2,10},{6,14},... | collective-permute-start | bytes 4616 | tf_op jit(solution)/shard_map/ppermute | solution.py:168
  98.1 1.6 %collective-permute-done.13 = f32[2,192]{1,0:T(2,128)S(1)} collective-permute-done((f32[2,192]{1,0:T(2,128)S(1)}, f32[2,192]{1,0:T(2,128)S(1)}, u32[]{:S(2)}, u32[]{:S(2)}) %collective-permute-start.13) | collective-permute-done | bytes 1568 | tf_op jit(solution)/shard_map/ppermute | solution.py:168
  101.3 1.5 %collective-permute-start.17 = (bf16[192,256]{1,0:T(8,128)(2,1)S(1)}, bf16[192,256]{1,0:T(8,128)(2,1)S(1)}, u32[]{:S(2)}, u32[]{:S(2)}) collective-permute-start(bf16[192,256]{1,0:T(8,128)(2,1)S(1)} %get-tuple-element.69), channel_id=1, source_target_pairs={{0,4},{4,0},{8,12},{12,8},{1,5},{5,1},{9,13},{13,9},{2,6},{6,2},{1... | collective-permute-start | bytes 294920 | tf_op jit(solution)/shard_map/ppermute | solution.py:168
  102.8 1.3 collective-permute-start.16
  106.0 3.0 %collective-permute-start.18 = (bf16[192,256]{1,0:T(8,128)(2,1)S(1)}, bf16[192,256]{1,0:T(8,128)(2,1)S(1)}, u32[]{:S(2)}, u32[]{:S(2)}) collective-permute-start(bf16[192,256]{1,0:T(8,128)(2,1)S(1)} %fusion.24), channel_id=1, source_target_pairs={{0,8},{4,12},{8,0},{12,4},{1,9},{5,13},{9,1},{13,5},{2,10},{6,14},... | collective-permute-start | bytes 294920 | tf_op jit(solution)/shard_map/ppermute | solution.py:168
  109.7 3.5 %collective-permute-done.18 = bf16[192,256]{1,0:T(8,128)(2,1)S(1)} collective-permute-done((bf16[192,256]{1,0:T(8,128)(2,1)S(1)}, bf16[192,256]{1,0:T(8,128)(2,1)S(1)}, u32[]{:S(2)}, u32[]{:S(2)}) %collective-permute-start.18) | collective-permute-done | bytes 98336 | tf_op jit(solution)/shard_map/ppermute | solution.py:168
  113.9 16.6 %collective-permute-done.19 = bf16[192,512]{1,0:T(8,128)(2,1)S(1)} collective-permute-done((bf16[192,512]{1,0:T(8,128)(2,1)S(1)}, bf16[192,512]{1,0:T(8,128)(2,1)S(1)}, u32[]{:S(2)}, u32[]{:S(2)}) %collective-permute-start.19) | collective-permute-done | bytes 196640 | tf_op jit(solution)/shard_map/ppermute | solution.py:179
  130.5 5.4 %shard_map.162 = (f32[2048,256]{1,0:T(8,128)}, f32[256,2048]{1,0:T(8,128)}) custom-call(s32[5]{0:T(128)S(1)} %pad_add_fusion.table, bf16[192,2048]{1,0:T(8,128)(2,1)S(1)} %fusion.18.value_ref.refs_0_, bf16[192,2048]{1,0:T(8,128)(2,1)} %collective-permute-done.2.refs_1_, bf16[192,2048]{1,0:T(8,128)(2,1)S(1)} %fusion.17.refs_2_, ...), custom_call_target="tpu_custom_call" | custom-call | flops 805306368 | bytes 7340032 | tf_op jit(solution)/shard_map/pallas_call | solution.py:115
  (91 shorter events, 18.0 us)
Async XLA Ops:
  0.6 11.7 %copy-start = (bf16[1,2048,256]{2,1,0:T(8,128)(2,1)S(1)}, bf16[1,2048,256]{2,1,0:T(8,128)(2,1)}, u32[]{:S(2)}) copy-start(bf16[1,2048,256]{2,1,0:T(8,128)(2,1)} %param.19) | copy-start | bytes 3145732
  0.6 32.7 %collective-permute-start = (bf16[192,2048]{1,0:T(8,128)(2,1)}, bf16[192,2048]{1,0:T(8,128)(2,1)}, u32[]{:S(2)}, u32[]{:S(2)}) collective-permute-start(bf16[192,2048]{1,0:T(8,128)(2,1)} %param.16), channel_id=1, source_target_pairs={{2,6},{6,10},{10,14},{3,7},{7,11},{11,15},{18,22},{22,26},{26,30},... | collective-permute-start | bytes 2359304 | tf_op jit(solution)/shard_map/ppermute | solution.py:230
  2.4 31.0 %collective-permute-start.1 = (bf16[192,2048]{1,0:T(8,128)(2,1)}, bf16[192,2048]{1,0:T(8,128)(2,1)}, u32[]{:S(2)}, u32[]{:S(2)}) collective-permute-start(bf16[192,2048]{1,0:T(8,128)(2,1)} %param.16), channel_id=1, source_target_pairs={{6,2},{10,6},{14,10},{7,3},{11,7},{15,11},{22,18},{26,22},{30,26},... | collective-permute-start | bytes 2359304 | tf_op jit(solution)/shard_map/ppermute | solution.py:230
  13.8 7.9 %copy-start.16 = (s32[8]{0:T(128)S(1)}, s32[8]{0:T(128)}, u32[]{:S(2)}) copy-start(s32[8]{0:T(128)} %constant.79.clone) | copy-start | bytes 100
  13.8 10.1 %copy-start.15 = (s32[8]{0:T(128)S(1)}, s32[8]{0:T(128)}, u32[]{:S(2)}) copy-start(s32[8]{0:T(128)} %constant.80.clone) | copy-start | bytes 100
  13.8 12.7 %copy-start.14 = (s32[8]{0:T(128)S(1)}, s32[8]{0:T(128)}, u32[]{:S(2)}) copy-start(s32[8]{0:T(128)} %constant.78.clone) | copy-start | bytes 100
  13.8 13.3 %copy-start.13 = (s32[8]{0:T(128)S(1)}, s32[8]{0:T(128)}, u32[]{:S(2)}) copy-start(s32[8]{0:T(128)} %constant.77.clone) | copy-start | bytes 100
  13.8 15.7 %copy-start.12 = (f32[4]{0:T(128)S(1)}, f32[4]{0:T(128)}, u32[]{:S(2)}) copy-start(f32[4]{0:T(128)} %param.21) | copy-start | bytes 52
  15.1 14.5 %collective-permute-start.5 = (bf16[192,384]{1,0:T(8,128)(2,1)}, bf16[192,384]{1,0:T(8,128)(2,1)}, u32[]{:S(2)}, u32[]{:S(2)}) collective-permute-start(bf16[192,384]{1,0:T(8,128)(2,1)} %fusion.19), channel_id=1, source_target_pairs={{0,4},{4,0},{8,12},{12,8},{1,5},{5,1},{9,13},{13,9},{2,6},{6,2},{1... | collective-permute-start | bytes 442376 | tf_op jit(solution)/shard_map/ppermute | solution.py:168
  18.1 31.5 %collective-permute-start.2 = (bf16[192,2048]{1,0:T(8,128)(2,1)S(1)}, bf16[192,2048]{1,0:T(8,128)(2,1)}, u32[]{:S(2)}, u32[]{:S(2)}) collective-permute-start(bf16[192,2048]{1,0:T(8,128)(2,1)S(1)} %fusion.18.value_ref.refs_0_), channel_id=1, source_target_pairs={{0,1},{1,0},{2,3},{3,2},{4,5},{5,4},{6,7},{7,6},{8,9},{9,8},{10,11... | collective-permute-start | bytes 2359304 | tf_op jit(solution)/shard_map/ppermute | solution.py:179
  30.7 10.4 %copy-start.8 = (f32[192,256]{1,0:T(8,128)S(1)}, f32[192,256]{1,0:T(8,128)}, u32[]{:S(2)}) copy-start(f32[192,256]{1,0:T(8,128)} %copy-done.7) | copy-start | bytes 589828
  30.7 10.4 %collective-permute-start.6 = (bf16[192,384]{1,0:T(8,128)(2,1)S(1)}, bf16[192,384]{1,0:T(8,128)(2,1)S(1)}, u32[]{:S(2)}, u32[]{:S(2)}) collective-permute-start(bf16[192,384]{1,0:T(8,128)(2,1)S(1)} %fusion.20), channel_id=1, source_target_pairs={{0,8},{4,12},{8,0},{12,4},{1,9},{5,13},{9,1},{13,5},{2,10},{6,14},... | collective-permute-start | bytes 442376 | tf_op jit(solution)/shard_map/ppermute | solution.py:168
  35.2 14.4 %collective-permute-start.3 = (bf16[192,2048]{1,0:T(8,128)(2,1)S(1)}, bf16[192,2048]{1,0:T(8,128)(2,1)S(1)}, u32[]{:S(2)}, u32[]{:S(2)}) collective-permute-start(bf16[192,2048]{1,0:T(8,128)(2,1)S(1)} %get-tuple-element.60), channel_id=1, source_target_pairs={{0,4},{6,10},{10,14},{1,5},{7,11},{11,15},{16,20},{22,26},{26,30},... | collective-permute-start | bytes 2359304 | tf_op jit(solution)/shard_map/ppermute | solution.py:230
  37.6 12.0 %collective-permute-start.4 = (bf16[192,2048]{1,0:T(8,128)(2,1)S(1)}, bf16[192,2048]{1,0:T(8,128)(2,1)S(1)}, u32[]{:S(2)}, u32[]{:S(2)}) collective-permute-start(bf16[192,2048]{1,0:T(8,128)(2,1)S(1)} %get-tuple-element.59), channel_id=1, source_target_pairs={{12,8},{6,2},{10,6},{13,9},{7,3},{11,7},{28,24},{22,18},{26,22},{2... | collective-permute-start | bytes 2359304 | tf_op jit(solution)/shard_map/ppermute | solution.py:230
  42.1 38.1 %copy-start.5 = (f32[192,384]{1,0:T(8,128)}, f32[192,384]{1,0:T(8,128)S(1)}, u32[]{:S(2)}) copy-start(f32[192,384]{1,0:T(8,128)S(1)} %convert_add_fusion.1) | copy-start | bytes 884740
  50.2 11.3 %collective-permute-start.7 = (bf16[192,2048]{1,0:T(8,128)(2,1)S(1)}, bf16[192,2048]{1,0:T(8,128)(2,1)S(1)}, u32[]{:S(2)}, u32[]{:S(2)}) collective-permute-start(bf16[192,2048]{1,0:T(8,128)(2,1)S(1)} %get-tuple-element.56), channel_id=1, source_target_pairs={{0,4},{4,8},{10,14},{1,5},{5,9},{11,15},{16,20},{20,24},{26,30},{1... | collective-permute-start | bytes 2359304 | tf_op jit(solution)/shard_map/ppermute | solution.py:230
  52.1 9.4 %collective-permute-start.8 = (bf16[192,2048]{1,0:T(8,128)(2,1)S(1)}, bf16[192,2048]{1,0:T(8,128)(2,1)S(1)}, u32[]{:S(2)}, u32[]{:S(2)}) collective-permute-start(bf16[192,2048]{1,0:T(8,128)(2,1)S(1)} %get-tuple-element.55), channel_id=1, source_target_pairs={{8,4},{12,8},{6,2},{9,5},{13,9},{7,3},{24,20},{28,24},{22,18},{25,... | collective-permute-start | bytes 2359304 | tf_op jit(solution)/shard_map/ppermute | solution.py:230
  53.1 6.2 %copy-start.11 = (s32[192]{0:T(256)S(1)}, s32[192]{0:T(256)}, u32[]{:S(2)}) copy-start(s32[192]{0:T(256)} %param.22) | copy-start | bytes 2308
  68.7 20.9 %copy-start.4 = (bf16[192,2048]{1,0:T(8,128)(2,1)S(1)}, bf16[192,2048]{1,0:T(8,128)(2,1)}, u32[]{:S(2)}) copy-start(bf16[192,2048]{1,0:T(8,128)(2,1)} %param.15) | copy-start | bytes 2359300
  68.7 11.6 %collective-permute-start.11 = (bf16[192,2048]{1,0:T(8,128)(2,1)S(1)}, bf16[192,2048]{1,0:T(8,128)(2,1)S(1)}, u32[]{:S(2)}, u32[]{:S(2)}) collective-permute-start(bf16[192,2048]{1,0:T(8,128)(2,1)S(1)} %get-tuple-element.67), channel_id=1, source_target_pairs={{2,0},{3,1},{6,4},{7,5},{10,8},{11,9},{14,12},{15,13},{18,16},{19,... | collective-permute-start | bytes 2359304 | tf_op jit(solution)/shard_map/ppermute | solution.py:314
  70.7 17.5 %collective-permute-start.10 = (bf16[192,2048]{1,0:T(8,128)(2,1)S(1)}, bf16[192,2048]{1,0:T(8,128)(2,1)S(1)}, u32[]{:S(2)}, u32[]{:S(2)}) collective-permute-start(bf16[192,2048]{1,0:T(8,128)(2,1)S(1)} %get-tuple-element.58), channel_id=1, source_target_pairs={{4,0},{8,4},{12,8},{5,1},{9,5},{13,9},{20,16},{24,20},{28,24},{21,... | collective-permute-start | bytes 2359304 | tf_op jit(solution)/shard_map/ppermute | solution.py:230
  72.0 17.6 %collective-permute-start.9 = (bf16[192,2048]{1,0:T(8,128)(2,1)S(1)}, bf16[192,2048]{1,0:T(8,128)(2,1)S(1)}, u32[]{:S(2)}, u32[]{:S(2)}) collective-permute-start(bf16[192,2048]{1,0:T(8,128)(2,1)S(1)} %get-tuple-element.57), channel_id=1, source_target_pairs={{0,4},{4,8},{8,12},{1,5},{5,9},{9,13},{16,20},{20,24},{24,28},{17,... | collective-permute-start | bytes 2359304 | tf_op jit(solution)/shard_map/ppermute | solution.py:230
  89.6 10.1 %copy-start.9 = (bf16[192,2048]{1,0:T(8,128)(2,1)S(1)}, bf16[192,2048]{1,0:T(8,128)(2,1)}, u32[]{:S(2)}) copy-start(bf16[192,2048]{1,0:T(8,128)(2,1)} %param.16) | copy-start | bytes 2359300
  90.4 4.1 %collective-permute-start.12 = (f32[2,192]{1,0:T(2,128)S(1)}, f32[2,192]{1,0:T(2,128)S(1)}, u32[]{:S(2)}, u32[]{:S(2)}) collective-permute-start(f32[2,192]{1,0:T(2,128)S(1)} %pad_maximum_fusion.2), channel_id=1, source_target_pairs={{0,4},{4,0},{8,12},{12,8},{1,5},{5,1},{9,13},{13,9},{2,6},{6,2},{1... | collective-permute-start | bytes 4616 | tf_op jit(solution)/shard_map/ppermute | solution.py:168
  93.0 6.7 %collective-permute-start.14 = (bf16[192,2048]{1,0:T(8,128)(2,1)S(1)}, bf16[192,2048]{1,0:T(8,128)(2,1)S(1)}, u32[]{:S(2)}, u32[]{:S(2)}) collective-permute-start(bf16[192,2048]{1,0:T(8,128)(2,1)S(1)} %get-tuple-element.54), channel_id=1, source_target_pairs={{0,2},{1,3},{4,6},{5,7},{8,10},{9,11},{12,14},{13,15},{16,18},{17,... | collective-permute-start | bytes 2359304 | tf_op jit(solution)/shard_map/ppermute | solution.py:318
  94.6 5.1 %collective-permute-start.13 = (f32[2,192]{1,0:T(2,128)S(1)}, f32[2,192]{1,0:T(2,128)S(1)}, u32[]{:S(2)}, u32[]{:S(2)}) collective-permute-start(f32[2,192]{1,0:T(2,128)S(1)} %fusion.29), channel_id=1, source_target_pairs={{0,8},{4,12},{8,0},{12,4},{1,9},{5,13},{9,1},{13,5},{2,10},{6,14},... | collective-permute-start | bytes 4616 | tf_op jit(solution)/shard_map/ppermute | solution.py:168
  100.8 8.2 %copy-start.6 = (f32[192,384]{1,0:T(8,128)S(1)}, f32[192,384]{1,0:T(8,128)}, u32[]{:S(2)}) copy-start(f32[192,384]{1,0:T(8,128)} %copy-done.5) | copy-start | bytes 884740
  101.3 4.7 %collective-permute-start.17 = (bf16[192,256]{1,0:T(8,128)(2,1)S(1)}, bf16[192,256]{1,0:T(8,128)(2,1)S(1)}, u32[]{:S(2)}, u32[]{:S(2)}) collective-permute-start(bf16[192,256]{1,0:T(8,128)(2,1)S(1)} %get-tuple-element.69), channel_id=1, source_target_pairs={{0,4},{4,0},{8,12},{12,8},{1,5},{5,1},{9,13},{13,9},{2,6},{6,2},{1... | collective-permute-start | bytes 294920 | tf_op jit(solution)/shard_map/ppermute | solution.py:168
  102.8 2.1 %collective-permute-start.16 = (f32[192]{0:T(256)S(1)}, f32[192]{0:T(256)S(1)}, u32[]{:S(2)}, u32[]{:S(2)}) collective-permute-start(f32[192]{0:T(256)S(1)} %bitcast.62), channel_id=1, source_target_pairs={{0,2},{1,3},{4,6},{5,7},{8,10},{9,11},{12,14},{13,15},{16,18},{17,... | collective-permute-start | bytes 2312 | tf_op jit(solution)/shard_map/ppermute | solution.py:326
  106.0 7.2 %collective-permute-start.18 = (bf16[192,256]{1,0:T(8,128)(2,1)S(1)}, bf16[192,256]{1,0:T(8,128)(2,1)S(1)}, u32[]{:S(2)}, u32[]{:S(2)}) collective-permute-start(bf16[192,256]{1,0:T(8,128)(2,1)S(1)} %fusion.24), channel_id=1, source_target_pairs={{0,8},{4,12},{8,0},{12,4},{1,9},{5,13},{9,1},{13,5},{2,10},{6,14},... | collective-permute-start | bytes 294920 | tf_op jit(solution)/shard_map/ppermute | solution.py:168
  109.1 21.4 %collective-permute-start.15 = (bf16[192,2048]{1,0:T(8,128)(2,1)S(1)}, bf16[192,2048]{1,0:T(8,128)(2,1)S(1)}, u32[]{:S(2)}, u32[]{:S(2)}) collective-permute-start(bf16[192,2048]{1,0:T(8,128)(2,1)S(1)} %fusion.17.refs_2_), channel_id=1, source_target_pairs={{0,1},{1,0},{2,3},{3,2},{4,5},{5,4},{6,7},{7,6},{8,9},{9,8},{10,11... | collective-permute-start | bytes 2359304 | tf_op jit(solution)/shard_map/ppermute | solution.py:179
  113.3 17.2 %collective-permute-start.19 = (bf16[192,512]{1,0:T(8,128)(2,1)S(1)}, bf16[192,512]{1,0:T(8,128)(2,1)S(1)}, u32[]{:S(2)}, u32[]{:S(2)}) collective-permute-start(bf16[192,512]{1,0:T(8,128)(2,1)S(1)} %pad_maximum_fusion.1), channel_id=1, source_target_pairs={{0,1},{1,0},{2,3},{3,2},{4,5},{5,4},{6,7},{7,6},{8,9},{9,8},{10,11... | collective-permute-start | bytes 589832 | tf_op jit(solution)/shard_map/ppermute | solution.py:179
  (6 other events, 21.6 us)

commit v4 on v3

v4 whole, which is shorter than its diff:
```python
import functools

import jax
import jax.numpy as jnp
from jax import lax
from jax.experimental import pallas as pl
from jax.experimental.pallas import tpu as pltpu
from jax.sharding import PartitionSpec as P

TENANT_COUNT = 4
EPSILON = 1e-05
CONTRACT_LAST = (((1,), (1,)), ((), ()))
CONTRACT_FIRST = (((0,), (0,)), ((), ()))
BF16 = jnp.bfloat16
F32 = jnp.float32
AHEAD = 2


def is_one_of(number, members):
    return functools.reduce(jnp.logical_or, [number == member for member in members])


def look_up(number, values):
    found = values[0]
    for value in sorted(set(values) - {values[0]}):
        found = jnp.where(
            is_one_of(number, [at for at, other in enumerate(values) if other == value]), value, found
        )
    return found


def block_kernel(table, value_ref, weight_ref, out_ref, wide, tall, arrived, *, blocks, tile, tiles):
    section = table[0]
    block = look_up(table[1], blocks)
    step = pl.program_id(0)
    width = tile * tiles

    def copy_of(index, is_wide):
        whole = pl.ds(pl.multiple_of(block * width, width), width)
        part = pl.ds(pl.multiple_of(block * width + index * tile, tile), tile)
        if is_wide:
            return pltpu.make_async_copy(weight_ref.at[:, part], wide.at[index], arrived.at[index])
        rows = pl.ds(pl.multiple_of(index * tile, tile), tile)
        return pltpu.make_async_copy(weight_ref.at[rows, whole], tall.at[index], arrived.at[index])

    for number, is_wide in ((0, True), (1, False)):

        @pl.when(section == number)
        def _():
            @pl.when(step == 0)
            def _():
                for index in range(min(AHEAD, tiles)):
                    copy_of(index, is_wide).start()

            @pl.when(step + AHEAD < tiles)
            def _():
                copy_of(step + AHEAD, is_wide).start()

            copy_of(step, is_wide).wait()
            if is_wide:
                out_ref[...] = jnp.dot(value_ref[...], wide[step], preferred_element_type=F32)
            else:
                out_ref[...] = lax.dot_general(
                    value_ref[...], tall[step], CONTRACT_LAST, preferred_element_type=F32
                )


def block_product(table, value, weight, blocks):
    rows, width = value.shape
    tile = min(256, width)
    tiles = width // tile
    return pl.pallas_call(
        functools.partial(block_kernel, blocks=blocks, tile=tile, tiles=tiles),
        grid_spec=pltpu.PrefetchScalarGridSpec(
            num_scalar_prefetch=1,
            grid=(tiles,),
            in_specs=[
                pl.BlockSpec((rows, width), lambda step, table: (0, 0)),
                pl.BlockSpec(memory_space=pl.ANY),
            ],
            out_specs=pl.BlockSpec((rows, tile), lambda step, table: (0, step)),
            scratch_shapes=[
                pltpu.VMEM((tiles, width, tile), BF16),
                pltpu.VMEM((tiles, tile, width), BF16),
                pltpu.SemaphoreType.DMA((tiles,)),
            ],
        ),
        out_shape=jax.ShapeDtypeStruct((rows, width), F32),
        compiler_params=pltpu.CompilerParams(vmem_limit_bytes=24 * 1024 * 1024),
        cost_estimate=pl.CostEstimate(
            flops=8 * rows * width * width, bytes_accessed=2 * width * width, transcendentals=0
        ),
    )(table, value, weight)


def gradient_kernel(table, gain_ref, *refs, replicas):
    early, cotangent, pulled, hidden, smalls = (
        refs[kind * replicas : (kind + 1) * replicas] for kind in range(5)
    )
    down_ref, up_ref = refs[5 * replicas :]
    ranks = down_ref.shape[1]

    def products(down_rows, up_rows):
        down_ref[...] = sum(
            lax.dot_general(a, small[:, ranks : 2 * ranks], CONTRACT_FIRST, preferred_element_type=F32)
            for a, small in zip(down_rows, smalls)
        )
        up_ref[...] = sum(
            lax.dot_general(small[:, :ranks], a, CONTRACT_FIRST, preferred_element_type=F32)
            for a, small in zip(up_rows, smalls)
        )

    @pl.when(table[0] == 0)
    def _():
        grads = []
        for at in range(replicas):
            inverse = smalls[at][:, 2 * ranks : 2 * ranks + 1].astype(F32)
            toward = smalls[at][:, 2 * ranks + 64 : 2 * ranks + 65].astype(F32)
            grads.append(
                (
                    cotangent[at][...].astype(F32)
                    + inverse * pulled[at][...].astype(F32)
                    - toward * hidden[at][...].astype(F32)
                ).astype(BF16)
            )
        products([a[...] for a in early], grads)

    @pl.when(table[0] == 1)
    def _():
        scaled = [(a[...].astype(F32) * gain_ref[...]).astype(BF16) for a in hidden]
        products(scaled, [a[...] for a in early])


def gradients(table, gain_row, early, cotangent, pulled, hidden, smalls, ranks):
    replicas = len(early)
    rows, width = early[0].shape
    tile = min(512, width)
    columns = pl.BlockSpec((rows, tile), lambda step, table: (0, step))
    small = pl.BlockSpec(smalls[0].shape, lambda step, table: (0, 0))
    return pl.pallas_call(
        functools.partial(gradient_kernel, replicas=replicas),
        grid_spec=pltpu.PrefetchScalarGridSpec(
            num_scalar_prefetch=1,
            grid=(width // tile,),
            in_specs=[pl.BlockSpec((1, tile), lambda step, table: (0, step))]
            + [columns] * (4 * replicas)
            + [small] * replicas,
            out_specs=[
                pl.BlockSpec((tile, ranks), lambda step, table: (step, 0)),
                pl.BlockSpec((ranks, tile), lambda step, table: (0, step)),
            ],
        ),
        out_shape=[
            jax.ShapeDtypeStruct((width, ranks), F32),
            jax.ShapeDtypeStruct((ranks, width), F32),
        ],
        compiler_params=pltpu.CompilerParams(vmem_limit_bytes=24 * 1024 * 1024),
        cost_estimate=pl.CostEstimate(
            flops=4 * replicas * rows * width * ranks,
            bytes_accessed=8 * width * ranks + 8 * replicas * rows * width,
            transcendentals=0,
        ),
    )(table, gain_row, *early, *cotangent, *pulled, *hidden, *smalls)


def orders(count):
    first, first_slots, second, second_slots = [], [], [], []
    for z in range(count):
        sends = [(slot, 0, count - slot + z) for slot in range(z + 1, count)]
        sends += [(slot, 1, slot - count + z) for slot in range(count - z, count)]
        sends.sort()
        first.append([block for _, _, block in sends] + [z])
        first_slots.append({(slot, side): at for at, (slot, side, _) in enumerate(sends)})
        arrivals = [(slot, 0, z - 1 - slot) for slot in range(z)]
        arrivals += [(slot, 1, z + 1 + slot) for slot in range(count - 1 - z)]
        arrivals.sort()
        second.append([z] + [block for _, _, block in arrivals])
        second_slots.append([None] + [(slot, side) for slot, side, _ in arrivals])
    return first, first_slots, second, second_slots


def pick(number, choice, cases):
    chosen = cases[0]
    for at in range(1, len(cases)):
        members = [device for device, wanted in enumerate(choice) if wanted == at]
        chosen = jnp.where(is_one_of(number, members), cases[at], chosen)
    return chosen


def sum_steps():
    count = lax.axis_size("tensor")
    return [1 << bit for bit in range(count.bit_length() - 1)]


def add_neighbour(value, distance):
    count = lax.axis_size("tensor")
    other = lax.ppermute(
        value.astype(BF16), "tensor", [(place, place ^ distance) for place in range(count)]
    )
    return value + other.astype(F32)


def with_other_replicas(value, sections=(0, 1)):
    count = lax.axis_size("replica")
    return [value] + [
        lax.ppermute(
            value,
            ("section", "replica"),
            [(s * count + r, s * count + (r + step) % count) for s in sections for r in range(count)],
        )
        for step in range(1, count)
    ]


def to_other_core(value, source):
    return lax.ppermute(value, "section", [(source, 1 - source)])


def on_device(
    tokens,
    cotangent,
    gain,
    frozen_base_weight,
    adapter_down_factors,
    adapter_up_factors,
    tenant_adapter_scale,
    row_tenant_owner,
):
    section = lax.axis_index("section")
    place = lax.axis_index("tensor")
    count = lax.axis_size("tensor")
    is_first = section == 0
    weight = frozen_base_weight[0]
    gain_row = gain[0][None, :]
    down = adapter_down_factors[0]
    up = adapter_up_factors[0]
    rows, width = tokens.shape
    features = width * count
    ranks = down.shape[1]

    tenant_of_column = jnp.arange(ranks, dtype=jnp.int32) // (ranks // TENANT_COUNT)
    coefficients = jnp.where(
        row_tenant_owner[:, None] == tenant_of_column[None, :],
        jnp.repeat(tenant_adapter_scale, ranks // TENANT_COUNT)[None, :],
        0.0,
    )

    first_order, first_slots, second_order, second_slots = orders(count)
    place_of = section * count + place
    table = jnp.stack([section, place_of]).astype(jnp.int32)

    def times_down(value):
        return jnp.dot(value, down, preferred_element_type=F32)

    def times_up_transposed(value):
        return lax.dot_general(value, up, CONTRACT_LAST, preferred_element_type=F32)

    def line(value, first_pairs, second_pairs, toward):
        pairs = [(2 * z, 2 * (z + toward)) for z in first_pairs] + [
            (2 * z + 1, 2 * (z + toward) + 1) for z in second_pairs
        ]
        return lax.ppermute(value, ("tensor", "section"), pairs)

    token_float = tokens.astype(F32)
    early = lax.optimization_barrier(
        jnp.where(is_first, (token_float * gain_row).astype(BF16), cotangent)
    )

    everyone = range(count)
    arrivals = [
        (
            line(cotangent, [], [z for z in everyone if z + 1 < count], 1),
            line(cotangent, [], [z for z in everyone if z > 0], -1),
        )
    ]
    early_all = with_other_replicas(early)

    parts = []
    small_sum = None
    steps_left = sum_steps()
    for stage in range(count):
        wanted = [None if stage == 0 else second_slots[z][stage] for z in everyone]
        cases = sorted({slot for slot in wanted if slot is not None})
        here = [early] + [arrivals[slot][side] for slot, side in cases]
        if stage == 1:
            after, again, *_ = lax.optimization_barrier((cotangent, early, *sent))
            squares = jnp.sum(token_float * token_float, axis=1, keepdims=True)
            small_sum = jnp.concatenate(
                [
                    times_up_transposed(after),
                    times_down(again),
                    jnp.broadcast_to(squares, (rows, 128)),
                ],
                axis=1,
            )
        elif stage > 1 and steps_left:
            small_sum = add_neighbour(small_sum, steps_left.pop(0))
        if stage == 2:
            cotangent_all = [cotangent] + [to_other_core(other, 1) for other in early_all[1:]]
        if stage == 3:
            small_sum, *cotangent_all = lax.optimization_barrier((small_sum, *cotangent_all))
        if stage > 0:
            *here, small_sum = lax.optimization_barrier((*here, small_sum, *sent))[: len(here) + 1]
        value = pick(
            place_of,
            [0] * count + [0 if slot is None else 1 + cases.index(slot) for slot in wanted],
            here,
        )
        order = [blocks[stage] for blocks in first_order + second_order]
        part = block_product(table, value, weight, order)
        parts.append(part)
        slot = stage + 1
        if slot == count:
            break
        sent = []
        for side in (0, 1):
            needed = [first_slots[z].get((slot, side)) for z in everyone]
            stages = sorted({at for at in needed if at is not None})
            own = pick(
                place_of,
                [0 if at is None else stages.index(at) for at in needed] + [0] * count,
                [parts[at] for at in stages],
            )
            arrived = arrivals[-1][side].astype(F32)
            sent.append((arrived + jnp.where(is_first, own, 0.0)).astype(BF16))
        arrivals.append(
            (
                line(
                    sent[0],
                    [z for z in everyone if z < slot and z + 1 < count],
                    [z for z in everyone if slot + 1 < count and z >= slot and z + 1 < count],
                    1,
                ),
                line(
                    sent[1],
                    [z for z in everyone if z >= count - slot and z > 0],
                    [z for z in everyone if slot + 1 < count and z < count - slot and z > 0],
                    -1,
                ),
            )
        )
    from_left, from_right = arrivals[-1]

    while steps_left:
        small_sum = add_neighbour(small_sum, steps_left.pop(0))
    rank_up, rank_down = small_sum[:, :ranks], small_sum[:, ranks : 2 * ranks]
    inv_first = lax.rsqrt(small_sum[:, 2 * ranks : 2 * ranks + 1] / features + EPSILON)
    small_early = (coefficients * jnp.where(is_first, rank_down, rank_up)).astype(BF16)
    low_product = jnp.where(
        is_first,
        jnp.dot(small_early, up, preferred_element_type=F32),
        lax.dot_general(small_early, down, CONTRACT_LAST, preferred_element_type=F32),
    )

    pulled = (gain_row * (sum(parts) + low_product)).astype(BF16)
    from_left, from_right, _ = lax.optimization_barrier((from_left, from_right, pulled))
    pulled = to_other_core(pulled, 1)
    pulled_all = with_other_replicas(pulled, (0,))
    pulled_rank = times_up_transposed(pulled)

    projected = parts[-1] + from_left.astype(F32) + from_right.astype(F32) + low_product
    hidden = (token_float + inv_first * projected).astype(BF16)
    hidden_here = jnp.where(is_first, hidden, to_other_core(hidden, 0))
    hidden_others = with_other_replicas(hidden, (0,))[1:]
    hidden_float = hidden_here.astype(F32)
    row_sums = [
        jnp.broadcast_to(jnp.sum(terms, axis=1, keepdims=True), (rows, 64))
        for terms in (hidden_float * hidden_float, hidden_float * pulled.astype(F32))
    ]
    hidden_rank = jnp.where(
        is_first,
        times_up_transposed(hidden_here),
        times_down((hidden_float * gain_row).astype(BF16)),
    )
    late_sum = jnp.concatenate([hidden_rank, pulled_rank, *row_sums], axis=1)
    for at, distance in enumerate(sum_steps()):
        late_sum = add_neighbour(late_sum, distance)
        if at == 0:
            late_sum, *pulled_all = lax.optimization_barrier((late_sum, *pulled_all))
    late_sum, *hidden_others = lax.optimization_barrier((late_sum, *hidden_others))
    hidden_all = [hidden_here] + [
        jnp.where(is_first, other, to_other_core(other, 0)) for other in hidden_others
    ]

    inv_second = lax.rsqrt(late_sum[:, 2 * ranks : 2 * ranks + 1] / features + EPSILON)
    toward_hidden = (
        late_sum[:, 2 * ranks + 64 : 2 * ranks + 65]
        * inv_second * inv_second * inv_second / features
    )
    hidden_rank, pulled_rank = late_sum[:, :ranks], late_sum[:, ranks : 2 * ranks]
    rank_late = jnp.where(
        is_first, rank_up + inv_second * pulled_rank - toward_hidden * hidden_rank, hidden_rank
    )
    row_scale = jnp.where(is_first, inv_first, inv_second)
    small_late = coefficients * rank_late * row_scale
    small_early = small_early.astype(F32) * row_scale
    smalls = jnp.concatenate(
        [
            jnp.where(is_first, small_early, small_late),
            jnp.where(is_first, small_late, small_early),
            jnp.broadcast_to(inv_second, (rows, 64)),
            jnp.broadcast_to(toward_hidden, (rows, 64)),
        ],
        axis=1,
    ).astype(BF16)
    grad_down, grad_up = gradients(
        table,
        gain_row,
        early_all,
        cotangent_all,
        pulled_all,
        hidden_all,
        with_other_replicas(smalls),
        ranks,
    )
    return (grad_down[None], grad_up[None])


def solution(mesh):
    return jax.shard_map(
        on_device,
        mesh=mesh,
        in_specs=(
            P(("groups", "replica"), "tensor"),
            P(("groups", "replica"), "tensor"),
            P("section", "tensor"),
            P("section", "tensor", None),
            P("section", "tensor", None),
            P("section", None, "tensor"),
            P(),
            P(("groups", "replica")),
        ),
        out_specs=(P("section", "tensor", "groups"), P("section", "groups", "tensor")),
        check_vma=False,
    )
```

time: 137 us -> 121 us (0.88)
  between operations: 7.96 us -> 1.17 us
  local copies, waits for them, and re-layouts: 4.99 us -> 0.8 us
  starting transfers between devices: 41.3 us -> 38.1 us
  other arithmetic: 11.1 us -> 8.92 us
    ppermute x12, waiting for transfers between devices: 26.4 us -> 34.8 us  [the longest x4 27.8 us: add_neighbour(): lax.ppermute(value.astype(BF16), 'tensor', [(place, place ^ distance) for...]
    ppermute x8, waiting for transfers between devices: 11.1 us -> 3.13 us  [line(): return lax.ppermute(value, ('tensor', 'section'), pairs)]
    ppermute x8, starting transfers between devices: 18.4 us -> 14.6 us  [line(): return lax.ppermute(value, ('tensor', 'section'), pairs)]
    dynamic_slice x5 -> x0, local copies, waits for them, and re-layouts: 3.01 us -> none  [pick(): chosen = jnp.asarray(choice, jnp.int32)[place_of]]
    select_n x5, other arithmetic: 2.66 us -> 1.1 us  [the longest x3 0.79 us: pick(): chosen = jnp.where(is_one_of(number, members), cases[at], chosen)]
  transfers between devices with their start and end apart: 20 -> 20, of which waited for: 10 -> 7; matrix products, arithmetic and copies ran while one was open for 10% -> 10% of each run, Pallas kernels for 14% -> 21%
where the time goes in v4:
time: 121 us; the launch traced here: 120 us
  starting transfers between devices  38.1 us (31%)
  waiting for transfers between devices  37.9 us (31%)
  Pallas kernels  29.7 us (25%)
  other arithmetic  8.92 us (7%)
  matrix products  3.41 us (3%)
    ppermute x4, waiting for transfers between devices, add_neighbour(): lax.ppermute(value.astype(BF16), 'tensor', [(place, place ^ distance) for...  27.8 us
    pallas_call x4, Pallas kernels, block_product(): pl.pallas_call(functools.partial(block_kernel, blocks=blocks, tile=tile,...  24.8 us
    ppermute x8, starting transfers between devices, line(): return lax.ppermute(value, ('tensor', 'section'), pairs)  14.6 us
    ppermute x4, starting transfers between devices, with_other_replicas(): lax.ppermute(value, ('section', 'replica'), [(s * count + r, s * count +...  9.99 us
    ppermute x4, starting transfers between devices, add_neighbour(): lax.ppermute(value.astype(BF16), 'tensor', [(place, place ^ distance) for...  8.3 us
    ppermute x4, waiting for transfers between devices, with_other_replicas(): lax.ppermute(value, ('section', 'replica'), [(s * count + r, s * count +...  6.94 us
    ppermute x4, starting transfers between devices, to_other_core(): return lax.ppermute(value, 'section', [(source, 1 - source)])  5.26 us
    pallas_call x1, Pallas kernels, gradients(): pl.pallas_call(functools.partial(gradient_kernel, replicas=replicas), gri...  4.87 us
  transfers between devices with their start and end apart: 20, of which 7 were waited for; matrix products, arithmetic and copies ran while one was open for 10% of the time, Pallas kernels for 21%

profile of v4, /device:TPU:0, one launch (start us, length us, event | category | flops | bytes accessed | tf_op | source)
XLA Modules:
  0.0 120.0 jit_solution(5416389473662597290)
XLA Ops:
  0.7 0.8 collective-permute-start.1
  1.5 1.6 %collective-permute-start.2 = (bf16[192,2048]{1,0:T(8,128)(2,1)}, bf16[192,2048]{1,0:T(8,128)(2,1)}, u32[]{:S(2)}, u32[]{:S(2)}) collective-permute-start(bf16[192,2048]{1,0:T(8,128)(2,1)} %refs_2_), channel_id=1, source_target_pairs={{2,6},{6,10},{10,14},{3,7},{7,11},{11,15},{18,22},{22,26},{26,30},... | collective-permute-start | bytes 2359304 | tf_op jit(solution)/shard_map/ppermute | solution.py:262
  3.1 1.4 %fusion.19.value_ref.refs_0_ = bf16[192,2048]{1,0:T(8,128)(2,1)S(1)} fusion(bf16[192,2048]{1,0:T(8,128)(2,1)} %refs_2_, bf16[192,2048]{1,0:T(8,128)(2,1)} %param.8, f32[2048]{0:T(1024)} %bitcast.30, pred[]{:T(512)S(6)} %eq.20), kind=kLoop, calls=%fused_computation.33 | loop fusion | flops 1572864 | bytes 2367489 | tf_op jit(solution)/shard_map/jit(_where)/select_n | solution.py:266
  4.5 3.0 %collective-permute-start = (bf16[192,2048]{1,0:T(8,128)(2,1)S(1)}, bf16[192,2048]{1,0:T(8,128)(2,1)S(1)}, u32[]{:S(2)}, u32[]{:S(2)}) collective-permute-start(bf16[192,2048]{1,0:T(8,128)(2,1)S(1)} %fusion.19.value_ref.refs_0_), channel_id=1, source_target_pairs={{0,1},{1,0},{2,3},{3,2},{4,5},{5,4},{6,7},{7,6},{8,9},{9,8},{10,11... | collective-permute-start | bytes 2359304 | tf_op jit(solution)/shard_map/ppermute | solution.py:206
  7.7 1.4 %fusion.1 = f32[192]{0:T(256)S(1)} fusion(bf16[192,2048]{1,0:T(8,128)(2,1)} %param.8), kind=kLoop, calls=%fused_computation.8 | loop fusion | flops 1179456 | bytes 787200 | tf_op jit(solution)/shard_map/reduce_sum | solution.py:287
  9.1 6.2 %shard_map.95 = f32[192,2048]{1,0:T(8,128)S(1)} custom-call(s32[2]{0:T(128)S(1)} %pad_add_fusion.table, bf16[192,2048]{1,0:T(8,128)(2,1)S(1)} %fusion.19.value_ref.refs_0_, bf16[2048,8192]{1,0:T(8,128)(2,1)} %bitcast.33), custom_call_target="tpu_custom_call" | custom-call | flops 6442450944 | bytes 8388608 | tf_op jit(solution)/shard_map/pallas_call | solution.py:72
  15.3 1.5 %add_convert_fusion.4 = (bf16[192,2048]{1,0:T(8,128)(2,1)S(1)}, bf16[192,2048]{1,0:T(8,128)(2,1)S(1)}) fusion(bf16[192,2048]{1,0:T(8,128)(2,1)S(1)} %collective-permute-done.1, f32[192,2048]{1,0:T(8,128)S(1)} %shard_map.95, pred[]{:T(512)S(6)} %eq.20, bf16[192,2048]{1,0:T(8,128)(2,1)} %collective-permute-done.2), kind=kLoop, calls=%fused_computation.18 | loop fusion | flops 2752512 | bytes 4718593 | tf_op jit(solution)/shard_map/convert_element_type | solution.py:325
  16.9 3.7 %collective-permute-start.3 = (bf16[192,2048]{1,0:T(8,128)(2,1)S(1)}, bf16[192,2048]{1,0:T(8,128)(2,1)S(1)}, u32[]{:S(2)}, u32[]{:S(2)}) collective-permute-start(bf16[192,2048]{1,0:T(8,128)(2,1)S(1)} %get-tuple-element.73), channel_id=1, source_target_pairs={{0,4},{6,10},{10,14},{1,5},{7,11},{11,15},{16,20},{22,26},{26,30},... | collective-permute-start | bytes 2359304 | tf_op jit(solution)/shard_map/ppermute | solution.py:262
  22.6 6.2 %shard_map.96 = f32[192,2048]{1,0:T(8,128)S(1)} custom-call(s32[2]{0:T(128)S(1)} %pad_add_fusion.table, bf16[192,2048]{1,0:T(8,128)(2,1)S(1)} %select_select_fusion.2.value_ref, bf16[2048,8192]{1,0:T(8,128)(2,1)} %bitcast.34), custom_call_target="tpu_custom_call" | custom-call | flops 6442450944 | bytes 8388608 | tf_op jit(solution)/shard_map/pallas_call | solution.py:72
  28.9 1.3 %collective-permute-start.7 = (bf16[192,2048]{1,0:T(8,128)(2,1)S(1)}, bf16[192,2048]{1,0:T(8,128)(2,1)S(1)}, u32[]{:S(2)}, u32[]{:S(2)}) collective-permute-start(bf16[192,2048]{1,0:T(8,128)(2,1)S(1)} %collective-permute-done.refs_1_), channel_id=1, source_target_pairs={{2,0},{3,1},{6,4},{7,5},{10,8},{11,9},{14,12},{15,13},{18,16},{19,... | collective-permute-start | bytes 2359304 | tf_op jit(solution)/shard_map/ppermute | solution.py:216
  30.2 5.1 %collective-permute-done.5 = bf16[192,640]{1,0:T(8,128)(2,1)S(1)} collective-permute-done((bf16[192,640]{1,0:T(8,128)(2,1)S(1)}, bf16[192,640]{1,0:T(8,128)(2,1)S(1)}, u32[]{:S(2)}, u32[]{:S(2)}) %collective-permute-start.5) | collective-permute-done | bytes 245792 | tf_op jit(solution)/shard_map/ppermute | solution.py:197
  35.9 4.4 %collective-permute-start.8 = (bf16[192,2048]{1,0:T(8,128)(2,1)S(1)}, bf16[192,2048]{1,0:T(8,128)(2,1)S(1)}, u32[]{:S(2)}, u32[]{:S(2)}) collective-permute-start(bf16[192,2048]{1,0:T(8,128)(2,1)S(1)} %get-tuple-element.69), channel_id=1, source_target_pairs={{0,4},{4,8},{10,14},{1,5},{5,9},{11,15},{16,20},{20,24},{26,30},{1... | collective-permute-start | bytes 2359304 | tf_op jit(solution)/shard_map/ppermute | solution.py:262
  41.1 5.0 %collective-permute-start.6 = (bf16[192,640]{1,0:T(8,128)(2,1)S(1)}, bf16[192,640]{1,0:T(8,128)(2,1)S(1)}, u32[]{:S(2)}, u32[]{:S(2)}) collective-permute-start(bf16[192,640]{1,0:T(8,128)(2,1)S(1)} %convert_element_type.106), channel_id=1, source_target_pairs={{0,8},{4,12},{8,0},{12,4},{1,9},{5,13},{9,1},{13,5},{2,10},{6,14},... | collective-permute-start | bytes 737288 | tf_op jit(solution)/shard_map/ppermute | solution.py:197
  46.3 6.2 %shard_map.97 = f32[192,2048]{1,0:T(8,128)S(1)} custom-call(s32[2]{0:T(128)S(1)} %pad_add_fusion.table, bf16[192,2048]{1,0:T(8,128)(2,1)S(1)} %select_select_fusion.1.value_ref, bf16[2048,8192]{1,0:T(8,128)(2,1)} %bitcast.35), custom_call_target="tpu_custom_call" | custom-call | flops 6442450944 | bytes 8388608 | tf_op jit(solution)/shard_map/pallas_call | solution.py:72
  52.5 12.2 %collective-permute-done.6 = bf16[192,640]{1,0:T(8,128)(2,1)S(1)} collective-permute-done((bf16[192,640]{1,0:T(8,128)(2,1)S(1)}, bf16[192,640]{1,0:T(8,128)(2,1)S(1)}, u32[]{:S(2)}, u32[]{:S(2)}) %collective-permute-start.6) | collective-permute-done | bytes 245792 | tf_op jit(solution)/shard_map/ppermute | solution.py:197
  65.4 1.3 %collective-permute-start.10 = (bf16[192,2048]{1,0:T(8,128)(2,1)S(1)}, bf16[192,2048]{1,0:T(8,128)(2,1)S(1)}, u32[]{:S(2)}, u32[]{:S(2)}) collective-permute-start(bf16[192,2048]{1,0:T(8,128)(2,1)S(1)} %get-tuple-element.71), channel_id=1, source_target_pairs={{0,4},{4,8},{8,12},{1,5},{5,9},{9,13},{16,20},{20,24},{24,28},{17,... | collective-permute-start | bytes 2359304 | tf_op jit(solution)/shard_map/ppermute | solution.py:262
  66.8 1.3 %collective-permute-start.11 = (bf16[192,2048]{1,0:T(8,128)(2,1)S(1)}, bf16[192,2048]{1,0:T(8,128)(2,1)S(1)}, u32[]{:S(2)}, u32[]{:S(2)}) collective-permute-start(bf16[192,2048]{1,0:T(8,128)(2,1)S(1)} %get-tuple-element.70), channel_id=1, source_target_pairs={{4,0},{8,4},{12,8},{5,1},{9,5},{13,9},{20,16},{24,20},{28,24},{21,... | collective-permute-start | bytes 2359304 | tf_op jit(solution)/shard_map/ppermute | solution.py:262
  68.4 6.2 %shard_map.98 = f32[192,2048]{1,0:T(8,128)S(1)} custom-call(s32[2]{0:T(128)S(1)} %pad_add_fusion.table, bf16[192,2048]{1,0:T(8,128)(2,1)S(1)} %select_select_fusion.value_ref, bf16[2048,8192]{1,0:T(8,128)(2,1)} %bitcast.36), custom_call_target="tpu_custom_call" | custom-call | flops 6442450944 | bytes 8388608 | tf_op jit(solution)/shard_map/pallas_call | solution.py:72
  76.1 1.3 %collective-permute-start.13 = (bf16[192,2048]{1,0:T(8,128)(2,1)S(1)}, bf16[192,2048]{1,0:T(8,128)(2,1)S(1)}, u32[]{:S(2)}, u32[]{:S(2)}) collective-permute-start(bf16[192,2048]{1,0:T(8,128)(2,1)S(1)} %get-tuple-element.74), channel_id=1, source_target_pairs={{2,0},{3,1},{6,4},{7,5},{10,8},{11,9},{14,12},{15,13},{18,16},{19,... | collective-permute-start | bytes 2359304 | tf_op jit(solution)/shard_map/ppermute | solution.py:216
  77.5 3.1 %collective-permute-done.11 = bf16[192,2048]{1,0:T(8,128)(2,1)S(1)} collective-permute-done((bf16[192,2048]{1,0:T(8,128)(2,1)S(1)}, bf16[192,2048]{1,0:T(8,128)(2,1)S(1)}, u32[]{:S(2)}, u32[]{:S(2)}) %collective-permute-start.11) | collective-permute-done | bytes 786464 | tf_op jit(solution)/shard_map/ppermute | solution.py:262
  81.4 1.3 %collective-permute-start.12 = (bf16[192,2048]{1,0:T(8,128)(2,1)S(1)}, bf16[192,2048]{1,0:T(8,128)(2,1)S(1)}, u32[]{:S(2)}, u32[]{:S(2)}) collective-permute-start(bf16[192,2048]{1,0:T(8,128)(2,1)S(1)} %fusion.2), channel_id=1, source_target_pairs={{0,2},{1,3},{4,6},{5,7},{8,10},{9,11},{12,14},{13,15},{16,18},{17,... | collective-permute-start | bytes 2359304 | tf_op jit(solution)/shard_map/ppermute | solution.py:216
  82.7 2.9 %collective-permute-start.15 = (bf16[192,2048]{1,0:T(8,128)(2,1)S(1)}, bf16[192,2048]{1,0:T(8,128)(2,1)S(1)}, u32[]{:S(2)}, u32[]{:S(2)}) collective-permute-start(bf16[192,2048]{1,0:T(8,128)(2,1)S(1)} %collective-permute-done.13.refs_4_), channel_id=1, source_target_pairs={{0,1},{1,0},{4,5},{5,4},{8,9},{9,8},{12,13},{13,12},{16,17},{17,16... | collective-permute-start | bytes 2359304 | tf_op jit(solution)/shard_map/ppermute | solution.py:206
  87.9 1.4 %collective-permute-start.14 = (bf16[192,640]{1,0:T(8,128)(2,1)S(1)}, bf16[192,640]{1,0:T(8,128)(2,1)S(1)}, u32[]{:S(2)}, u32[]{:S(2)}) collective-permute-start(bf16[192,640]{1,0:T(8,128)(2,1)S(1)} %fusion.21), channel_id=1, source_target_pairs={{0,4},{4,0},{8,12},{12,8},{1,5},{5,1},{9,13},{13,9},{2,6},{6,2},{1... | collective-permute-start | bytes 737288 | tf_op jit(solution)/shard_map/ppermute | solution.py:197
  89.3 2.9 %collective-permute-start.17 = (bf16[192,2048]{1,0:T(8,128)(2,1)S(1)}, bf16[192,2048]{1,0:T(8,128)(2,1)S(1)}, u32[]{:S(2)}, u32[]{:S(2)}) collective-permute-start(bf16[192,2048]{1,0:T(8,128)(2,1)S(1)} %fusion.2), channel_id=1, source_target_pairs={{0,1},{1,0},{4,5},{5,4},{8,9},{9,8},{12,13},{13,12},{16,17},{17,16... | collective-permute-start | bytes 2359304 | tf_op jit(solution)/shard_map/ppermute | solution.py:206
  92.2 2.4 %collective-permute-done.14 = bf16[192,640]{1,0:T(8,128)(2,1)S(1)} collective-permute-done((bf16[192,640]{1,0:T(8,128)(2,1)S(1)}, bf16[192,640]{1,0:T(8,128)(2,1)S(1)}, u32[]{:S(2)}, u32[]{:S(2)}) %collective-permute-start.14) | collective-permute-done | bytes 245792 | tf_op jit(solution)/shard_map/ppermute | solution.py:197
  94.7 1.9 %collective-permute-done.15.refs_5_ = bf16[192,2048]{1,0:T(8,128)(2,1)S(1)} collective-permute-done((bf16[192,2048]{1,0:T(8,128)(2,1)S(1)}, bf16[192,2048]{1,0:T(8,128)(2,1)S(1)}, u32[]{:S(2)}, u32[]{:S(2)}) %collective-permute-start.15) | collective-permute-done | bytes 786464 | tf_op jit(solution)/shard_map/ppermute | solution.py:206
  96.6 1.9 %collective-permute-start.16 = (bf16[192,640]{1,0:T(8,128)(2,1)S(1)}, bf16[192,640]{1,0:T(8,128)(2,1)S(1)}, u32[]{:S(2)}, u32[]{:S(2)}) collective-permute-start(bf16[192,640]{1,0:T(8,128)(2,1)S(1)} %convert_element_type.122), channel_id=1, source_target_pairs={{0,8},{4,12},{8,0},{12,4},{1,9},{5,13},{9,1},{13,5},{2,10},{6,14},... | collective-permute-start | bytes 737288 | tf_op jit(solution)/shard_map/ppermute | solution.py:197
  98.5 8.1 %collective-permute-done.16 = bf16[192,640]{1,0:T(8,128)(2,1)S(1)} collective-permute-done((bf16[192,640]{1,0:T(8,128)(2,1)S(1)}, bf16[192,640]{1,0:T(8,128)(2,1)S(1)}, u32[]{:S(2)}, u32[]{:S(2)}) %collective-permute-start.16) | collective-permute-done | bytes 245792 | tf_op jit(solution)/shard_map/ppermute | solution.py:197
  106.7 1.3 %collective-permute-start.18 = (bf16[192,2048]{1,0:T(8,128)(2,1)S(1)}, bf16[192,2048]{1,0:T(8,128)(2,1)S(1)}, u32[]{:S(2)}, u32[]{:S(2)}) collective-permute-start(bf16[192,2048]{1,0:T(8,128)(2,1)S(1)} %collective-permute-done.17), channel_id=1, source_target_pairs={{0,2},{1,3},{4,6},{5,7},{8,10},{9,11},{12,14},{13,15},{16,18},{17,... | collective-permute-start | bytes 2359304 | tf_op jit(solution)/shard_map/ppermute | solution.py:216
  108.9 1.2 collective-permute-start.19
  110.1 5.0 %collective-permute-done.19.refs_9_ = bf16[192,640]{1,0:T(8,128)(2,1)S(1)} collective-permute-done((bf16[192,640]{1,0:T(8,128)(2,1)S(1)}, bf16[192,640]{1,0:T(8,128)(2,1)S(1)}, u32[]{:S(2)}, u32[]{:S(2)}) %collective-permute-start.19) | collective-permute-done | bytes 245792 | tf_op jit(solution)/shard_map/ppermute | solution.py:206
  115.1 4.9 %shard_map.99 = (f32[2048,256]{1,0:T(8,128)}, f32[256,2048]{1,0:T(8,128)}) custom-call(s32[2]{0:T(128)S(1)} %pad_add_fusion.table, f32[1,2048]{1,0:T(1,128)S(1)} %copy-done.2, bf16[192,2048]{1,0:T(8,128)(2,1)S(1)} %fusion.19.value_ref.refs_0_, bf16[192,2048]{1,0:T(8,128)(2,1)S(1)} %collective-permute-done.refs_1_, bf16[192,2048]{1,0:T(8,128)(2,1)S(1)} %copy-done.1, ...), custom_call_target="tpu_custom_call" | custom-call | flops 805306368 | bytes 10485760 | tf_op jit(solution)/shard_map/pallas_call | solution.py:140
  (71 shorter events, 10.4 us)
Async XLA Ops:
  0.6 20.6 %copy-start = (bf16[1,2048,256]{2,1,0:T(8,128)(2,1)S(1)}, bf16[1,2048,256]{2,1,0:T(8,128)(2,1)}, u32[]{:S(2)}) copy-start(bf16[1,2048,256]{2,1,0:T(8,128)(2,1)} %param.12) | copy-start | bytes 3145732
  0.6 6.9 %copy-start.6 = (f32[4]{0:T(128)S(1)}, f32[4]{0:T(128)}, u32[]{:S(2)}) copy-start(f32[4]{0:T(128)} %param.14) | copy-start | bytes 52
  0.7 14.6 %collective-permute-start.1 = (bf16[192,2048]{1,0:T(8,128)(2,1)}, bf16[192,2048]{1,0:T(8,128)(2,1)S(1)}, u32[]{:S(2)}, u32[]{:S(2)}) collective-permute-start(bf16[192,2048]{1,0:T(8,128)(2,1)} %refs_2_), channel_id=1, source_target_pairs={{6,2},{10,6},{14,10},{7,3},{11,7},{15,11},{22,18},{26,22},{30,26},... | collective-permute-start | bytes 2359304 | tf_op jit(solution)/shard_map/ppermute | solution.py:262
  1.5 13.8 %collective-permute-start.2 = (bf16[192,2048]{1,0:T(8,128)(2,1)}, bf16[192,2048]{1,0:T(8,128)(2,1)}, u32[]{:S(2)}, u32[]{:S(2)}) collective-permute-start(bf16[192,2048]{1,0:T(8,128)(2,1)} %refs_2_), channel_id=1, source_target_pairs={{2,6},{6,10},{10,14},{3,7},{7,11},{11,15},{18,22},{22,26},{26,30},... | collective-permute-start | bytes 2359304 | tf_op jit(solution)/shard_map/ppermute | solution.py:262
  4.5 24.4 %collective-permute-start = (bf16[192,2048]{1,0:T(8,128)(2,1)S(1)}, bf16[192,2048]{1,0:T(8,128)(2,1)S(1)}, u32[]{:S(2)}, u32[]{:S(2)}) collective-permute-start(bf16[192,2048]{1,0:T(8,128)(2,1)S(1)} %fusion.19.value_ref.refs_0_), channel_id=1, source_target_pairs={{0,1},{1,0},{2,3},{3,2},{4,5},{5,4},{6,7},{7,6},{8,9},{9,8},{10,11... | collective-permute-start | bytes 2359304 | tf_op jit(solution)/shard_map/ppermute | solution.py:206
  16.8 4.8 %copy-start.1 = (bf16[192,2048]{1,0:T(8,128)(2,1)S(1)}, bf16[192,2048]{1,0:T(8,128)(2,1)}, u32[]{:S(2)}) copy-start(bf16[192,2048]{1,0:T(8,128)(2,1)} %refs_2_) | copy-start | bytes 2359300
  16.8 4.8 %copy-start.3 = (bf16[1,256,2048]{2,1,0:T(8,128)(2,1)S(1)}, bf16[1,256,2048]{2,1,0:T(8,128)(2,1)}, u32[]{:S(2)}) copy-start(bf16[1,256,2048]{2,1,0:T(8,128)(2,1)} %param.13) | copy-start | bytes 3145732
  16.9 18.4 %collective-permute-start.3 = (bf16[192,2048]{1,0:T(8,128)(2,1)S(1)}, bf16[192,2048]{1,0:T(8,128)(2,1)S(1)}, u32[]{:S(2)}, u32[]{:S(2)}) collective-permute-start(bf16[192,2048]{1,0:T(8,128)(2,1)S(1)} %get-tuple-element.73), channel_id=1, source_target_pairs={{0,4},{6,10},{10,14},{1,5},{7,11},{11,15},{16,20},{22,26},{26,30},... | collective-permute-start | bytes 2359304 | tf_op jit(solution)/shard_map/ppermute | solution.py:262
  20.5 14.8 %collective-permute-start.4 = (bf16[192,2048]{1,0:T(8,128)(2,1)S(1)}, bf16[192,2048]{1,0:T(8,128)(2,1)S(1)}, u32[]{:S(2)}, u32[]{:S(2)}) collective-permute-start(bf16[192,2048]{1,0:T(8,128)(2,1)S(1)} %get-tuple-element.72), channel_id=1, source_target_pairs={{12,8},{6,2},{10,6},{13,9},{7,3},{11,7},{28,24},{22,18},{26,22},{2... | collective-permute-start | bytes 2359304 | tf_op jit(solution)/shard_map/ppermute | solution.py:262
  22.3 12.9 %collective-permute-start.5 = (bf16[192,640]{1,0:T(8,128)(2,1)S(1)}, bf16[192,640]{1,0:T(8,128)(2,1)S(1)}, u32[]{:S(2)}, u32[]{:S(2)}) collective-permute-start(bf16[192,640]{1,0:T(8,128)(2,1)S(1)} %convert_element_type.100), channel_id=1, source_target_pairs={{0,4},{4,0},{8,12},{12,8},{1,5},{5,1},{9,13},{13,9},{2,6},{6,2},{1... | collective-permute-start | bytes 737288 | tf_op jit(solution)/shard_map/ppermute | solution.py:197
  28.9 35.9 %collective-permute-start.7 = (bf16[192,2048]{1,0:T(8,128)(2,1)S(1)}, bf16[192,2048]{1,0:T(8,128)(2,1)S(1)}, u32[]{:S(2)}, u32[]{:S(2)}) collective-permute-start(bf16[192,2048]{1,0:T(8,128)(2,1)S(1)} %collective-permute-done.refs_1_), channel_id=1, source_target_pairs={{2,0},{3,1},{6,4},{7,5},{10,8},{11,9},{14,12},{15,13},{18,16},{19,... | collective-permute-start | bytes 2359304 | tf_op jit(solution)/shard_map/ppermute | solution.py:216
  35.9 28.9 %collective-permute-start.8 = (bf16[192,2048]{1,0:T(8,128)(2,1)S(1)}, bf16[192,2048]{1,0:T(8,128)(2,1)S(1)}, u32[]{:S(2)}, u32[]{:S(2)}) collective-permute-start(bf16[192,2048]{1,0:T(8,128)(2,1)S(1)} %get-tuple-element.69), channel_id=1, source_target_pairs={{0,4},{4,8},{10,14},{1,5},{5,9},{11,15},{16,20},{20,24},{26,30},{1... | collective-permute-start | bytes 2359304 | tf_op jit(solution)/shard_map/ppermute | solution.py:262
  40.3 24.5 %collective-permute-start.9 = (bf16[192,2048]{1,0:T(8,128)(2,1)S(1)}, bf16[192,2048]{1,0:T(8,128)(2,1)S(1)}, u32[]{:S(2)}, u32[]{:S(2)}) collective-permute-start(bf16[192,2048]{1,0:T(8,128)(2,1)S(1)} %get-tuple-element.68), channel_id=1, source_target_pairs={{8,4},{12,8},{6,2},{9,5},{13,9},{7,3},{24,20},{28,24},{22,18},{25,... | collective-permute-start | bytes 2359304 | tf_op jit(solution)/shard_map/ppermute | solution.py:262
  41.1 23.7 %collective-permute-start.6 = (bf16[192,640]{1,0:T(8,128)(2,1)S(1)}, bf16[192,640]{1,0:T(8,128)(2,1)S(1)}, u32[]{:S(2)}, u32[]{:S(2)}) collective-permute-start(bf16[192,640]{1,0:T(8,128)(2,1)S(1)} %convert_element_type.106), channel_id=1, source_target_pairs={{0,8},{4,12},{8,0},{12,4},{1,9},{5,13},{9,1},{13,5},{2,10},{6,14},... | collective-permute-start | bytes 737288 | tf_op jit(solution)/shard_map/ppermute | solution.py:197
  65.4 12.1 %collective-permute-start.10 = (bf16[192,2048]{1,0:T(8,128)(2,1)S(1)}, bf16[192,2048]{1,0:T(8,128)(2,1)S(1)}, u32[]{:S(2)}, u32[]{:S(2)}) collective-permute-start(bf16[192,2048]{1,0:T(8,128)(2,1)S(1)} %get-tuple-element.71), channel_id=1, source_target_pairs={{0,4},{4,8},{8,12},{1,5},{5,9},{9,13},{16,20},{20,24},{24,28},{17,... | collective-permute-start | bytes 2359304 | tf_op jit(solution)/shard_map/ppermute | solution.py:262
  66.8 13.9 %collective-permute-start.11 = (bf16[192,2048]{1,0:T(8,128)(2,1)S(1)}, bf16[192,2048]{1,0:T(8,128)(2,1)S(1)}, u32[]{:S(2)}, u32[]{:S(2)}) collective-permute-start(bf16[192,2048]{1,0:T(8,128)(2,1)S(1)} %get-tuple-element.70), channel_id=1, source_target_pairs={{4,0},{8,4},{12,8},{5,1},{9,5},{13,9},{20,16},{24,20},{28,24},{21,... | collective-permute-start | bytes 2359304 | tf_op jit(solution)/shard_map/ppermute | solution.py:262
  68.4 6.2 %copy-start.5 = (s32[192]{0:T(256)S(1)}, s32[192]{0:T(256)}, u32[]{:S(2)}) copy-start(s32[192]{0:T(256)} %param.15) | copy-start | bytes 2308
  74.6 0.7 copy-start.2
  75.3 5.3 %copy-start.4 = (bf16[192,2048]{1,0:T(8,128)(2,1)S(1)}, bf16[192,2048]{1,0:T(8,128)(2,1)}, u32[]{:S(2)}) copy-start(bf16[192,2048]{1,0:T(8,128)(2,1)} %param.8) | copy-start | bytes 2359300
  76.1 6.6 %collective-permute-start.13 = (bf16[192,2048]{1,0:T(8,128)(2,1)S(1)}, bf16[192,2048]{1,0:T(8,128)(2,1)S(1)}, u32[]{:S(2)}, u32[]{:S(2)}) collective-permute-start(bf16[192,2048]{1,0:T(8,128)(2,1)S(1)} %get-tuple-element.74), channel_id=1, source_target_pairs={{2,0},{3,1},{6,4},{7,5},{10,8},{11,9},{14,12},{15,13},{18,16},{19,... | collective-permute-start | bytes 2359304 | tf_op jit(solution)/shard_map/ppermute | solution.py:216
  81.4 4.8 %collective-permute-start.12 = (bf16[192,2048]{1,0:T(8,128)(2,1)S(1)}, bf16[192,2048]{1,0:T(8,128)(2,1)S(1)}, u32[]{:S(2)}, u32[]{:S(2)}) collective-permute-start(bf16[192,2048]{1,0:T(8,128)(2,1)S(1)} %fusion.2), channel_id=1, source_target_pairs={{0,2},{1,3},{4,6},{5,7},{8,10},{9,11},{12,14},{13,15},{16,18},{17,... | collective-permute-start | bytes 2359304 | tf_op jit(solution)/shard_map/ppermute | solution.py:216
  82.7 13.9 %collective-permute-start.15 = (bf16[192,2048]{1,0:T(8,128)(2,1)S(1)}, bf16[192,2048]{1,0:T(8,128)(2,1)S(1)}, u32[]{:S(2)}, u32[]{:S(2)}) collective-permute-start(bf16[192,2048]{1,0:T(8,128)(2,1)S(1)} %collective-permute-done.13.refs_4_), channel_id=1, source_target_pairs={{0,1},{1,0},{4,5},{5,4},{8,9},{9,8},{12,13},{13,12},{16,17},{17,16... | collective-permute-start | bytes 2359304 | tf_op jit(solution)/shard_map/ppermute | solution.py:206
  87.9 6.7 %collective-permute-start.14 = (bf16[192,640]{1,0:T(8,128)(2,1)S(1)}, bf16[192,640]{1,0:T(8,128)(2,1)S(1)}, u32[]{:S(2)}, u32[]{:S(2)}) collective-permute-start(bf16[192,640]{1,0:T(8,128)(2,1)S(1)} %fusion.21), channel_id=1, source_target_pairs={{0,4},{4,0},{8,12},{12,8},{1,5},{5,1},{9,13},{13,9},{2,6},{6,2},{1... | collective-permute-start | bytes 737288 | tf_op jit(solution)/shard_map/ppermute | solution.py:197
  89.3 17.4 %collective-permute-start.17 = (bf16[192,2048]{1,0:T(8,128)(2,1)S(1)}, bf16[192,2048]{1,0:T(8,128)(2,1)S(1)}, u32[]{:S(2)}, u32[]{:S(2)}) collective-permute-start(bf16[192,2048]{1,0:T(8,128)(2,1)S(1)} %fusion.2), channel_id=1, source_target_pairs={{0,1},{1,0},{4,5},{5,4},{8,9},{9,8},{12,13},{13,12},{16,17},{17,16... | collective-permute-start | bytes 2359304 | tf_op jit(solution)/shard_map/ppermute | solution.py:206
  96.6 10.0 %collective-permute-start.16 = (bf16[192,640]{1,0:T(8,128)(2,1)S(1)}, bf16[192,640]{1,0:T(8,128)(2,1)S(1)}, u32[]{:S(2)}, u32[]{:S(2)}) collective-permute-start(bf16[192,640]{1,0:T(8,128)(2,1)S(1)} %convert_element_type.122), channel_id=1, source_target_pairs={{0,8},{4,12},{8,0},{12,4},{1,9},{5,13},{9,1},{13,5},{2,10},{6,14},... | collective-permute-start | bytes 737288 | tf_op jit(solution)/shard_map/ppermute | solution.py:197
  106.7 3.4 %collective-permute-start.18 = (bf16[192,2048]{1,0:T(8,128)(2,1)S(1)}, bf16[192,2048]{1,0:T(8,128)(2,1)S(1)}, u32[]{:S(2)}, u32[]{:S(2)}) collective-permute-start(bf16[192,2048]{1,0:T(8,128)(2,1)S(1)} %collective-permute-done.17), channel_id=1, source_target_pairs={{0,2},{1,3},{4,6},{5,7},{8,10},{9,11},{12,14},{13,15},{16,18},{17,... | collective-permute-start | bytes 2359304 | tf_op jit(solution)/shard_map/ppermute | solution.py:216
  108.9 6.3 %collective-permute-start.19 = (bf16[192,640]{1,0:T(8,128)(2,1)S(1)}, bf16[192,640]{1,0:T(8,128)(2,1)S(1)}, u32[]{:S(2)}, u32[]{:S(2)}) collective-permute-start(bf16[192,640]{1,0:T(8,128)(2,1)S(1)} %pad_maximum_fusion.2.refs_8_), channel_id=1, source_target_pairs={{0,1},{1,0},{2,3},{3,2},{4,5},{5,4},{6,7},{7,6},{8,9},{9,8},{10,11... | collective-permute-start | bytes 737288 | tf_op jit(solution)/shard_map/ppermute | solution.py:206

commit v5 on v4

--- a/solution.py
+++ b/solution.py
@@ -94,49 +94,53 @@
 
 
 def gradient_kernel(table, gain_ref, *refs, replicas):
-    early, cotangent, pulled, hidden, smalls = (
-        refs[kind * replicas : (kind + 1) * replicas] for kind in range(5)
-    )
-    down_ref, up_ref = refs[5 * replicas :]
+    early, cotangent, pulled, hidden, small_early, small_late = (
+        refs[kind * replicas : (kind + 1) * replicas] for kind in range(6)
+    )
+    down_ref, up_ref = refs[6 * replicas :]
     ranks = down_ref.shape[1]
 
-    def products(down_rows, up_rows):
+    def products(down_rows, down_small, up_rows, up_small):
         down_ref[...] = sum(
-            lax.dot_general(a, small[:, ranks : 2 * ranks], CONTRACT_FIRST, preferred_element_type=F32)
-            for a, small in zip(down_rows, smalls)
+            lax.dot_general(a, b, CONTRACT_FIRST, preferred_element_type=F32)
+            for a, b in zip(down_rows, down_small)
         )
         up_ref[...] = sum(
-            lax.dot_general(small[:, :ranks], a, CONTRACT_FIRST, preferred_element_type=F32)
-            for a, small in zip(up_rows, smalls)
-        )
+            lax.dot_general(a, b, CONTRACT_FIRST, preferred_element_type=F32)
+            for a, b in zip(up_small, up_rows)
+        )
+
+    late = [small[:, :ranks] for small in small_late]
+    inverse = [small[:, ranks : ranks + 1].astype(F32) for small in small_late]
+    toward = [small[:, ranks + 64 : ranks + 65].astype(F32) for small in small_late]
 
     @pl.when(table[0] == 0)
     def _():
-        grads = []
-        for at in range(replicas):
-            inverse = smalls[at][:, 2 * ranks : 2 * ranks + 1].astype(F32)
-            toward = smalls[at][:, 2 * ranks + 64 : 2 * ranks + 65].astype(F32)
-            grads.append(
-                (
-                    cotangent[at][...].astype(F32)
-                    + inverse * pulled[at][...].astype(F32)
-                    - toward * hidden[at][...].astype(F32)
-                ).astype(BF16)
-            )
-        products([a[...] for a in early], grads)
+        grads = [
+            (
+                cotangent[at][...].astype(F32)
+                + inverse[at] * pulled[at][...].astype(F32)
+                - toward[at] * hidden[at][...].astype(F32)
+            ).astype(BF16)
+            for at in range(replicas)
+        ]
+        products([a[...] for a in early], late, grads, [a[...] for a in small_early])
 
     @pl.when(table[0] == 1)
     def _():
         scaled = [(a[...].astype(F32) * gain_ref[...]).astype(BF16) for a in hidden]
-        products(scaled, [a[...] for a in early])
-
-
-def gradients(table, gain_row, early, cotangent, pulled, hidden, smalls, ranks):
+        weighed = [
+            (a[...].astype(F32) * inverse[at]).astype(BF16) for at, a in enumerate(small_early)
+        ]
+        products(scaled, weighed, [a[...] for a in early], late)
+
+
+def gradients(table, gain_row, early, cotangent, pulled, hidden, small_early, small_late, ranks):
     replicas = len(early)
     rows, width = early[0].shape
     tile = min(512, width)
     columns = pl.BlockSpec((rows, tile), lambda step, table: (0, step))
-    small = pl.BlockSpec(smalls[0].shape, lambda step, table: (0, 0))
+    smalls = [*small_early, *small_late]
     return pl.pallas_call(
         functools.partial(gradient_kernel, replicas=replicas),
         grid_spec=pltpu.PrefetchScalarGridSpec(
@@ -144,7 +148,7 @@
             grid=(width // tile,),
             in_specs=[pl.BlockSpec((1, tile), lambda step, table: (0, step))]
             + [columns] * (4 * replicas)
-            + [small] * replicas,
+            + [pl.BlockSpec(small.shape, lambda step, table: (0, 0)) for small in smalls],
             out_specs=[
                 pl.BlockSpec((tile, ranks), lambda step, table: (step, 0)),
                 pl.BlockSpec((ranks, tile), lambda step, table: (0, step)),
@@ -187,17 +191,27 @@
     return chosen
 
 
-def sum_steps():
+def doubling_steps():
     count = lax.axis_size("tensor")
-    return [1 << bit for bit in range(count.bit_length() - 1)]
-
-
-def add_neighbour(value, distance):
-    count = lax.axis_size("tensor")
-    other = lax.ppermute(
-        value.astype(BF16), "tensor", [(place, place ^ distance) for place in range(count)]
-    )
-    return value + other.astype(F32)
+    return [
+        ([(place, place ^ (1 << bit)) for place in range(count)], True)
+        for bit in range(count.bit_length() - 1)
+    ]
+
+
+def line_steps():
+    if lax.axis_size("tensor") != 4:
+        return doubling_steps()
+    return [([(0, 1), (3, 2)], True), ([(1, 2), (2, 1)], True), ([(1, 0), (2, 3)], False)]
+
+
+def sum_step(value, step, wire=BF16):
+    pairs, adds = step
+    other = lax.ppermute(value.astype(wire), "tensor", pairs).astype(F32)
+    if adds:
+        return value + other
+    takes = is_one_of(lax.axis_index("tensor"), [target for _, target in pairs])
+    return jnp.where(takes, other, value)
 
 
 def with_other_replicas(value, sections=(0, 1)):
@@ -273,28 +287,26 @@
             line(cotangent, [], [z for z in everyone if z > 0], -1),
         )
     ]
-    early_all = with_other_replicas(early)
-
     parts = []
     small_sum = None
-    steps_left = sum_steps()
+    steps_left = line_steps()
     for stage in range(count):
         wanted = [None if stage == 0 else second_slots[z][stage] for z in everyone]
         cases = sorted({slot for slot in wanted if slot is not None})
         here = [early] + [arrivals[slot][side] for slot, side in cases]
         if stage == 1:
-            after, again, *_ = lax.optimization_barrier((cotangent, early, *sent))
-            squares = jnp.sum(token_float * token_float, axis=1, keepdims=True)
+            after, plain, *_ = lax.optimization_barrier((early, tokens, *sent))
+            plain = plain.astype(F32)
+            squares = jnp.sum(plain * plain, axis=1, keepdims=True)
             small_sum = jnp.concatenate(
                 [
-                    times_up_transposed(after),
-                    times_down(again),
+                    jnp.where(is_first, times_down(after), times_up_transposed(after)),
                     jnp.broadcast_to(squares, (rows, 128)),
                 ],
                 axis=1,
             )
         elif stage > 1 and steps_left:
-            small_sum = add_neighbour(small_sum, steps_left.pop(0))
+            small_sum = sum_step(small_sum, steps_left.pop(0))
         if stage == 2:
             cotangent_all = [cotangent] + [to_other_core(other, 1) for other in early_all[1:]]
         if stage == 3:
@@ -308,6 +320,9 @@
         )
         order = [blocks[stage] for blocks in first_order + second_order]
         part = block_product(table, value, weight, order)
+        if stage == 0:
+            part, after = lax.optimization_barrier((part, early))
+            early_all = [early] + with_other_replicas(after)[1:]
         parts.append(part)
         slot = stage + 1
         if slot == count:
@@ -342,62 +357,65 @@
     from_left, from_right = arrivals[-1]
 
     while steps_left:
-        small_sum = add_neighbour(small_sum, steps_left.pop(0))
-    rank_up, rank_down = small_sum[:, :ranks], small_sum[:, ranks : 2 * ranks]
-    inv_first = lax.rsqrt(small_sum[:, 2 * ranks : 2 * ranks + 1] / features + EPSILON)
-    small_early = (coefficients * jnp.where(is_first, rank_down, rank_up)).astype(BF16)
+        small_sum = sum_step(small_sum, steps_left.pop(0))
+    inv_first = lax.rsqrt(small_sum[:, ranks : ranks + 1] / features + EPSILON)
+    small_early = (coefficients * small_sum[:, :ranks]).astype(BF16)
     low_product = jnp.where(
         is_first,
         jnp.dot(small_early, up, preferred_element_type=F32),
         lax.dot_general(small_early, down, CONTRACT_LAST, preferred_element_type=F32),
     )
+    small_early_all = with_other_replicas(
+        (small_early.astype(F32) * jnp.where(is_first, inv_first, 1.0)).astype(BF16)
+    )
 
     pulled = (gain_row * (sum(parts) + low_product)).astype(BF16)
-    from_left, from_right, _ = lax.optimization_barrier((from_left, from_right, pulled))
+    from_left, from_right, *small_early_all, _ = lax.optimization_barrier(
+        (from_left, from_right, *small_early_all, pulled)
+    )
+    pulled_others = with_other_replicas(pulled, (1,))[1:]
     pulled = to_other_core(pulled, 1)
-    pulled_all = with_other_replicas(pulled, (0,))
-    pulled_rank = times_up_transposed(pulled)
 
     projected = parts[-1] + from_left.astype(F32) + from_right.astype(F32) + low_product
     hidden = (token_float + inv_first * projected).astype(BF16)
     hidden_here = jnp.where(is_first, hidden, to_other_core(hidden, 0))
     hidden_others = with_other_replicas(hidden, (0,))[1:]
     hidden_float = hidden_here.astype(F32)
-    row_sums = [
-        jnp.broadcast_to(jnp.sum(terms, axis=1, keepdims=True), (rows, 64))
-        for terms in (hidden_float * hidden_float, hidden_float * pulled.astype(F32))
+    pulled_float = pulled.astype(F32)
+    row_sums = jnp.stack(
+        [jnp.sum(hidden_float * hidden_float, axis=1), jnp.sum(hidden_float * pulled_float, axis=1)]
+    )
+    for at, step in enumerate(doubling_steps()):
+        row_sums = sum_step(row_sums, step, F32)
+        if at == 0:
+            row_sums, *pulled_others = lax.optimization_barrier((row_sums, *pulled_others))
+    inv_second = lax.rsqrt(row_sums[0] / features + EPSILON)[:, None]
+    toward_hidden = row_sums[1][:, None] * inv_second * inv_second * inv_second / features
+    hidden_grad = cotangent.astype(F32) + inv_second * pulled_float - toward_hidden * hidden_float
+    rank_late = jnp.where(
+        is_first,
+        times_up_transposed(hidden_grad.astype(BF16)),
+        times_down((hidden_float * gain_row).astype(BF16)),
+    )
+    for step in doubling_steps():
+        rank_late = sum_step(rank_late, step)
+
+    rank_late, *swapped = lax.optimization_barrier(
+        (
+            rank_late,
+            *[jnp.where(is_first, *pair) for pair in zip(hidden_others, pulled_others)],
+        )
+    )
+    swapped = [lax.ppermute(other, "section", [(0, 1), (1, 0)]) for other in swapped]
+    hidden_all = [hidden_here] + [
+        jnp.where(is_first, *pair) for pair in zip(hidden_others, swapped)
     ]
-    hidden_rank = jnp.where(
-        is_first,
-        times_up_transposed(hidden_here),
-        times_down((hidden_float * gain_row).astype(BF16)),
-    )
-    late_sum = jnp.concatenate([hidden_rank, pulled_rank, *row_sums], axis=1)
-    for at, distance in enumerate(sum_steps()):
-        late_sum = add_neighbour(late_sum, distance)
-        if at == 0:
-            late_sum, *pulled_all = lax.optimization_barrier((late_sum, *pulled_all))
-    late_sum, *hidden_others = lax.optimization_barrier((late_sum, *hidden_others))
-    hidden_all = [hidden_here] + [
-        jnp.where(is_first, other, to_other_core(other, 0)) for other in hidden_others
-    ]
-
-    inv_second = lax.rsqrt(late_sum[:, 2 * ranks : 2 * ranks + 1] / features + EPSILON)
-    toward_hidden = (
-        late_sum[:, 2 * ranks + 64 : 2 * ranks + 65]
-        * inv_second * inv_second * inv_second / features
-    )
-    hidden_rank, pulled_rank = late_sum[:, :ranks], late_sum[:, ranks : 2 * ranks]
-    rank_late = jnp.where(
-        is_first, rank_up + inv_second * pulled_rank - toward_hidden * hidden_rank, hidden_rank
-    )
-    row_scale = jnp.where(is_first, inv_first, inv_second)
-    small_late = coefficients * rank_late * row_scale
-    small_early = small_early.astype(F32) * row_scale
+    pulled_all = [pulled] + swapped
+
+    small_late = coefficients * rank_late * jnp.where(is_first, inv_first, inv_second)
     smalls = jnp.concatenate(
         [
-            jnp.where(is_first, small_early, small_late),
-            jnp.where(is_first, small_late, small_early),
+            small_late,
             jnp.broadcast_to(inv_second, (rows, 64)),
             jnp.broadcast_to(toward_hidden, (rows, 64)),
         ],
@@ -410,6 +428,7 @@
         cotangent_all,
         pulled_all,
         hidden_all,
+        small_early_all,
         with_other_replicas(smalls),
         ranks,
     )

time: 121 us -> 129 us (1.066)
  starting transfers between devices: 38.1 us -> 53 us
  waiting for transfers between devices: 37.9 us -> 26.2 us
  other arithmetic: 8.92 us -> 12.5 us
    ppermute x4 -> x8, waiting for transfers between devices: 27.8 us -> 14.6 us  [the longest x7 14.6 us: sum_step(): other = lax.ppermute(value.astype(wire), 'tensor', pairs).astype(F32)]
    ppermute x8, starting transfers between devices: 14.6 us -> 26.6 us  [line(): return lax.ppermute(value, ('tensor', 'section'), pairs)]
    ppermute x4 -> x8, starting transfers between devices: 8.3 us -> 12.9 us  [the longest x1 7.45 us: on_device(): lax.ppermute(other, 'section', [(0, 1), (1, 0)])]
    select_n x2 -> x4, other arithmetic: 0.31 us -> 3.31 us  [the longest x2 2.27 us: on_device(): jnp.where(is_first, *pair)]
    ppermute x4 -> x5, waiting for transfers between devices: 6.94 us -> 9.06 us  [with_other_replicas(): lax.ppermute(value, ('section', 'replica'), [(s * count + r, s * count +...]
    ppermute x8, waiting for transfers between devices: 3.13 us -> 1.46 us  [line(): return lax.ppermute(value, ('tensor', 'section'), pairs)]
    ppermute x4 -> x3, starting transfers between devices: 5.26 us -> 3.92 us  [to_other_core(): return lax.ppermute(value, 'section', [(source, 1 - source)])]
    ppermute x4 -> x5, starting transfers between devices: 9.99 us -> 9.54 us  [with_other_replicas(): lax.ppermute(value, ('section', 'replica'), [(s * count + r, s * count +...]
  transfers between devices with their start and end apart: 20 -> 24, of which waited for: 7 -> 10; matrix products, arithmetic and copies ran while one was open for 10% -> 12% of each run, Pallas kernels for 21% -> 19%
where the time goes in v5:
time: 129 us; the launch traced here: 128 us
  starting transfers between devices  53 us (41%)
  Pallas kernels  30.7 us (24%)
  waiting for transfers between devices  26.2 us (20%)
  other arithmetic  12.5 us (10%)
  matrix products  3.12 us (2%)
  between operations  1.29 us (1%)
    ppermute x8, starting transfers between devices, line(): return lax.ppermute(value, ('tensor', 'section'), pairs)  26.6 us
    pallas_call x4, Pallas kernels, block_product(): pl.pallas_call(functools.partial(block_kernel, blocks=blocks, tile=tile,...  24.8 us
    ppermute x7, waiting for transfers between devices, sum_step(): other = lax.ppermute(value.astype(wire), 'tensor', pairs).astype(F32)  14.6 us
    ppermute x5, starting transfers between devices, with_other_replicas(): lax.ppermute(value, ('section', 'replica'), [(s * count + r, s * count +...  9.54 us
    ppermute x5, waiting for transfers between devices, with_other_replicas(): lax.ppermute(value, ('section', 'replica'), [(s * count + r, s * count +...  9.06 us
    ppermute x1, starting transfers between devices, on_device(): lax.ppermute(other, 'section', [(0, 1), (1, 0)])  7.45 us
    pallas_call x1, Pallas kernels, gradients(): pl.pallas_call(functools.partial(gradient_kernel, replicas=replicas), gri...  5.93 us
    ppermute x7, starting transfers between devices, sum_step(): other = lax.ppermute(value.astype(wire), 'tensor', pairs).astype(F32)  5.42 us
  transfers between devices with their start and end apart: 24, of which 10 were waited for; matrix products, arithmetic and copies ran while one was open for 12% of the time, Pallas kernels for 19%

profile of v5, /device:TPU:0, one launch (start us, length us, event | category | flops | bytes accessed | tf_op | source)
XLA Modules:
  0.0 128.1 jit_solution(12505286755354373768)
XLA Ops:
  0.6 1.7 %collective-permute-start.1 = (bf16[192,2048]{1,0:T(8,128)(2,1)}, bf16[192,2048]{1,0:T(8,128)(2,1)}, u32[]{:S(2)}, u32[]{:S(2)}) collective-permute-start(bf16[192,2048]{1,0:T(8,128)(2,1)} %refs_2_), channel_id=1, source_target_pairs={{6,2},{10,6},{14,10},{7,3},{11,7},{15,11},{22,18},{26,22},{30,26},... | collective-permute-start | bytes 2359304 | tf_op jit(solution)/shard_map/ppermute | solution.py:276
  2.4 1.6 %collective-permute-start.2 = (bf16[192,2048]{1,0:T(8,128)(2,1)}, bf16[192,2048]{1,0:T(8,128)(2,1)}, u32[]{:S(2)}, u32[]{:S(2)}) collective-permute-start(bf16[192,2048]{1,0:T(8,128)(2,1)} %refs_2_), channel_id=1, source_target_pairs={{2,6},{6,10},{10,14},{3,7},{7,11},{11,15},{18,22},{22,26},{26,30},... | collective-permute-start | bytes 2359304 | tf_op jit(solution)/shard_map/ppermute | solution.py:276
  3.9 1.4 %fusion.23.value_ref.refs_0_ = bf16[192,2048]{1,0:T(8,128)(2,1)S(1)} fusion(bf16[192,2048]{1,0:T(8,128)(2,1)} %refs_2_, bf16[192,2048]{1,0:T(8,128)(2,1)} %param.8, f32[2048]{0:T(1024)} %bitcast.35, pred[]{:T(512)S(6)} %eq.24), kind=kLoop, calls=%fused_computation.36 | loop fusion | flops 1572864 | bytes 2367489 | tf_op jit(solution)/shard_map/jit(_where)/select_n | solution.py:280
  5.4 6.2 %shard_map.95 = f32[192,2048]{1,0:T(8,128)S(1)} custom-call(s32[2]{0:T(128)S(1)} %pad_add_fusion.table, bf16[192,2048]{1,0:T(8,128)(2,1)S(1)} %fusion.23.value_ref.refs_0_, bf16[2048,8192]{1,0:T(8,128)(2,1)} %bitcast.38), custom_call_target="tpu_custom_call" | custom-call | flops 6442450944 | bytes 8388608 | tf_op jit(solution)/shard_map/pallas_call | solution.py:72
  11.6 3.0 %collective-permute-start = (bf16[192,2048]{1,0:T(8,128)(2,1)S(1)}, bf16[192,2048]{1,0:T(8,128)(2,1)}, u32[]{:S(2)}, u32[]{:S(2)}) collective-permute-start(bf16[192,2048]{1,0:T(8,128)(2,1)S(1)} %fusion.23.value_ref.refs_0_), channel_id=1, source_target_pairs={{0,1},{1,0},{2,3},{3,2},{4,5},{5,4},{6,7},{7,6},{8,9},{9,8},{10,11... | collective-permute-start | bytes 2359304 | tf_op jit(solution)/shard_map/ppermute | solution.py:220
  14.8 2.0 %add_convert_fusion.4 = (bf16[192,2048]{1,0:T(8,128)(2,1)S(1)}, bf16[192,2048]{1,0:T(8,128)(2,1)S(1)}) fusion(bf16[192,2048]{1,0:T(8,128)(2,1)} %collective-permute-done.1, f32[192,2048]{1,0:T(8,128)S(1)} %shard_map.95, pred[]{:T(512)S(6)} %eq.24, bf16[192,2048]{1,0:T(8,128)(2,1)} %collective-permute-done.2), kind=kLoop, calls=%fused_computation.22 | loop fusion | flops 2752512 | bytes 4718593 | tf_op jit(solution)/shard_map/convert_element_type | solution.py:340
  16.8 3.5 %collective-permute-start.3 = (bf16[192,2048]{1,0:T(8,128)(2,1)S(1)}, bf16[192,2048]{1,0:T(8,128)(2,1)S(1)}, u32[]{:S(2)}, u32[]{:S(2)}) collective-permute-start(bf16[192,2048]{1,0:T(8,128)(2,1)S(1)} %get-tuple-element.80), channel_id=1, source_target_pairs={{0,4},{6,10},{10,14},{1,5},{7,11},{11,15},{16,20},{22,26},{26,30},... | collective-permute-start | bytes 2359304 | tf_op jit(solution)/shard_map/ppermute | solution.py:276
  22.4 1.3 %collective-permute-start.5 = (bf16[192,384]{1,0:T(8,128)(2,1)S(1)}, bf16[192,384]{1,0:T(8,128)(2,1)S(1)}, u32[]{:S(2)}, u32[]{:S(2)}) collective-permute-start(bf16[192,384]{1,0:T(8,128)(2,1)S(1)} %convert_element_type.119), channel_id=1, source_target_pairs={{0,4},{12,8},{1,5},{13,9},{2,6},{14,10},{3,7},{15,11},{16,20},{28,... | collective-permute-start | bytes 442376 | tf_op jit(solution)/shard_map/ppermute | solution.py:210
  23.8 6.2 %shard_map.96 = f32[192,2048]{1,0:T(8,128)S(1)} custom-call(s32[2]{0:T(128)S(1)} %pad_add_fusion.table, bf16[192,2048]{1,0:T(8,128)(2,1)S(1)} %select_select_fusion.2.value_ref, bf16[2048,8192]{1,0:T(8,128)(2,1)} %bitcast.39), custom_call_target="tpu_custom_call" | custom-call | flops 6442450944 | bytes 8388608 | tf_op jit(solution)/shard_map/pallas_call | solution.py:72
  30.0 1.3 %collective-permute-start.7 = (bf16[192,2048]{1,0:T(8,128)(2,1)}, bf16[192,2048]{1,0:T(8,128)(2,1)S(1)}, u32[]{:S(2)}, u32[]{:S(2)}) collective-permute-start(bf16[192,2048]{1,0:T(8,128)(2,1)} %collective-permute-done.refs_1_), channel_id=1, source_target_pairs={{2,0},{3,1},{6,4},{7,5},{10,8},{11,9},{14,12},{15,13},{18,16},{19,... | collective-permute-start | bytes 2359304 | tf_op jit(solution)/shard_map/ppermute | solution.py:230
  33.1 4.4 %collective-permute-start.8 = (bf16[192,2048]{1,0:T(8,128)(2,1)S(1)}, bf16[192,2048]{1,0:T(8,128)(2,1)S(1)}, u32[]{:S(2)}, u32[]{:S(2)}) collective-permute-start(bf16[192,2048]{1,0:T(8,128)(2,1)S(1)} %get-tuple-element.76), channel_id=1, source_target_pairs={{0,4},{4,8},{10,14},{1,5},{5,9},{11,15},{16,20},{20,24},{26,30},{1... | collective-permute-start | bytes 2359304 | tf_op jit(solution)/shard_map/ppermute | solution.py:276
  39.2 6.2 %shard_map.97 = f32[192,2048]{1,0:T(8,128)S(1)} custom-call(s32[2]{0:T(128)S(1)} %pad_add_fusion.table, bf16[192,2048]{1,0:T(8,128)(2,1)S(1)} %select_select_fusion.1.value_ref, bf16[2048,8192]{1,0:T(8,128)(2,1)} %bitcast.40), custom_call_target="tpu_custom_call" | custom-call | flops 6442450944 | bytes 8388608 | tf_op jit(solution)/shard_map/pallas_call | solution.py:72
  45.5 1.4 %collective-permute-done.8 = bf16[192,2048]{1,0:T(8,128)(2,1)S(1)} collective-permute-done((bf16[192,2048]{1,0:T(8,128)(2,1)S(1)}, bf16[192,2048]{1,0:T(8,128)(2,1)S(1)}, u32[]{:S(2)}, u32[]{:S(2)}) %collective-permute-start.8) | collective-permute-done | bytes 786464 | tf_op jit(solution)/shard_map/ppermute | solution.py:276
  47.5 12.7 %collective-permute-start.12 = (bf16[192,2048]{1,0:T(8,128)(2,1)S(1)}, bf16[192,2048]{1,0:T(8,128)(2,1)S(1)}, u32[]{:S(2)}, u32[]{:S(2)}) collective-permute-start(bf16[192,2048]{1,0:T(8,128)(2,1)S(1)} %get-tuple-element.78), channel_id=1, source_target_pairs={{0,4},{4,8},{8,12},{1,5},{5,9},{9,13},{16,20},{20,24},{24,28},{17,... | collective-permute-start | bytes 2359304 | tf_op jit(solution)/shard_map/ppermute | solution.py:276
  60.2 1.3 %collective-permute-start.13 = (bf16[192,2048]{1,0:T(8,128)(2,1)S(1)}, bf16[192,2048]{1,0:T(8,128)(2,1)S(1)}, u32[]{:S(2)}, u32[]{:S(2)}) collective-permute-start(bf16[192,2048]{1,0:T(8,128)(2,1)S(1)} %get-tuple-element.77), channel_id=1, source_target_pairs={{4,0},{8,4},{12,8},{5,1},{9,5},{13,9},{20,16},{24,20},{28,24},{21,... | collective-permute-start | bytes 2359304 | tf_op jit(solution)/shard_map/ppermute | solution.py:276
  61.5 1.3 %collective-permute-start.10 = (bf16[192,384]{1,0:T(8,128)(2,1)S(1)}, bf16[192,384]{1,0:T(8,128)(2,1)S(1)}, u32[]{:S(2)}, u32[]{:S(2)}) collective-permute-start(bf16[192,384]{1,0:T(8,128)(2,1)S(1)} %convert_element_type.131), channel_id=1, source_target_pairs={{4,0},{8,12},{5,1},{9,13},{6,2},{10,14},{7,3},{11,15},{20,16},{24,... | collective-permute-start | bytes 442376 | tf_op jit(solution)/shard_map/ppermute | solution.py:210
  63.1 6.2 %shard_map.98 = f32[192,2048]{1,0:T(8,128)S(1)} custom-call(s32[2]{0:T(128)S(1)} %pad_add_fusion.table, bf16[192,2048]{1,0:T(8,128)(2,1)S(1)} %select_select_fusion.value_ref, bf16[2048,8192]{1,0:T(8,128)(2,1)} %bitcast.41), custom_call_target="tpu_custom_call" | custom-call | flops 6442450944 | bytes 8388608 | tf_op jit(solution)/shard_map/pallas_call | solution.py:72
  69.3 6.3 %collective-permute-done.10 = bf16[192,384]{1,0:T(8,128)(2,1)S(1)} collective-permute-done((bf16[192,384]{1,0:T(8,128)(2,1)S(1)}, bf16[192,384]{1,0:T(8,128)(2,1)S(1)}, u32[]{:S(2)}, u32[]{:S(2)}) %collective-permute-start.10) | collective-permute-done | bytes 147488 | tf_op jit(solution)/shard_map/ppermute | solution.py:210
  77.5 1.3 %collective-permute-start.11 = (bf16[192,2048]{1,0:T(8,128)(2,1)S(1)}, bf16[192,2048]{1,0:T(8,128)(2,1)S(1)}, u32[]{:S(2)}, u32[]{:S(2)}) collective-permute-start(bf16[192,2048]{1,0:T(8,128)(2,1)S(1)} %get-tuple-element.83), channel_id=1, source_target_pairs={{2,0},{3,1},{6,4},{7,5},{10,8},{11,9},{14,12},{15,13},{18,16},{19,... | collective-permute-start | bytes 2359304 | tf_op jit(solution)/shard_map/ppermute | solution.py:230
  78.8 1.9 %collective-permute-done.14.refs_9_ = bf16[192,256]{1,0:T(8,128)(2,1)S(1)} collective-permute-done((bf16[192,256]{1,0:T(8,128)(2,1)S(1)}, bf16[192,256]{1,0:T(8,128)(2,1)S(1)}, u32[]{:S(2)}, u32[]{:S(2)}) %collective-permute-start.14) | collective-permute-done | bytes 98336 | tf_op jit(solution)/shard_map/ppermute | solution.py:220
  81.4 1.3 %collective-permute-start.15 = (bf16[192,2048]{1,0:T(8,128)(2,1)S(1)}, bf16[192,2048]{1,0:T(8,128)(2,1)S(1)}, u32[]{:S(2)}, u32[]{:S(2)}) collective-permute-start(bf16[192,2048]{1,0:T(8,128)(2,1)S(1)} %fusion.1), channel_id=1, source_target_pairs={{0,2},{1,3},{4,6},{5,7},{8,10},{9,11},{12,14},{13,15},{16,18},{17,... | collective-permute-start | bytes 2359304 | tf_op jit(solution)/shard_map/ppermute | solution.py:230
  85.2 3.9 %collective-permute-start.21 = (bf16[192,2048]{1,0:T(8,128)(2,1)S(1)}, bf16[192,2048]{1,0:T(8,128)(2,1)S(1)}, u32[]{:S(2)}, u32[]{:S(2)}) collective-permute-start(bf16[192,2048]{1,0:T(8,128)(2,1)S(1)} %fusion.1), channel_id=1, source_target_pairs={{0,1},{1,0},{4,5},{5,4},{8,9},{9,8},{12,13},{13,12},{16,17},{17,16... | collective-permute-start | bytes 2359304 | tf_op jit(solution)/shard_map/ppermute | solution.py:220
  89.7 4.1 %collective-permute-done.18 = f32[2,192]{1,0:T(2,128)S(1)} collective-permute-done((f32[2,192]{1,0:T(2,128)S(1)}, f32[2,192]{1,0:T(2,128)S(1)}, u32[]{:S(2)}, u32[]{:S(2)}) %collective-permute-start.18) | collective-permute-done | bytes 1568 | tf_op jit(solution)/shard_map/ppermute | solution.py:210
  94.5 1.9 %collective-permute-start.19 = (bf16[192,256]{1,0:T(8,128)(2,1)S(1)}, bf16[192,256]{1,0:T(8,128)(2,1)S(1)}, u32[]{:S(2)}, u32[]{:S(2)}) collective-permute-start(bf16[192,256]{1,0:T(8,128)(2,1)S(1)} %get-tuple-element.85), channel_id=1, source_target_pairs={{0,4},{4,0},{8,12},{12,8},{1,5},{5,1},{9,13},{13,9},{2,6},{6,2},{1... | collective-permute-start | bytes 294920 | tf_op jit(solution)/shard_map/ppermute | solution.py:210
  96.4 2.7 %collective-permute-done.19 = bf16[192,256]{1,0:T(8,128)(2,1)S(1)} collective-permute-done((bf16[192,256]{1,0:T(8,128)(2,1)S(1)}, bf16[192,256]{1,0:T(8,128)(2,1)S(1)}, u32[]{:S(2)}, u32[]{:S(2)}) %collective-permute-start.19) | collective-permute-done | bytes 98336 | tf_op jit(solution)/shard_map/ppermute | solution.py:210
  99.3 4.1 %collective-permute-done.21 = bf16[192,2048]{1,0:T(8,128)(2,1)S(1)} collective-permute-done((bf16[192,2048]{1,0:T(8,128)(2,1)S(1)}, bf16[192,2048]{1,0:T(8,128)(2,1)S(1)}, u32[]{:S(2)}, u32[]{:S(2)}) %collective-permute-start.21) | collective-permute-done | bytes 786464 | tf_op jit(solution)/shard_map/ppermute | solution.py:220
  105.5 7.5 %collective-permute-start.22 = (bf16[192,2048]{1,0:T(8,128)(2,1)}, bf16[192,2048]{1,0:T(8,128)(2,1)S(1)}, u32[]{:S(2)}, u32[]{:S(2)}) collective-permute-start(bf16[192,2048]{1,0:T(8,128)(2,1)} %broadcast_select_fusion.1), channel_id=1, source_target_pairs={{0,2},{2,0},{1,3},{3,1},{4,6},{6,4},{5,7},{7,5},{8,10},{10,8},{9,1... | collective-permute-start | bytes 2359304 | tf_op jit(solution)/shard_map/ppermute | solution.py:409
  114.8 1.2 fusion.29
  116.3 1.6 %collective-permute-start.23 = (bf16[192,384]{1,0:T(8,128)(2,1)S(1)}, bf16[192,384]{1,0:T(8,128)(2,1)S(1)}, u32[]{:S(2)}, u32[]{:S(2)}) collective-permute-start(bf16[192,384]{1,0:T(8,128)(2,1)S(1)} %pad_maximum_fusion.1.refs_10_), channel_id=1, source_target_pairs={{0,1},{1,0},{2,3},{3,2},{4,5},{5,4},{6,7},{7,6},{8,9},{9,8},{10,11... | collective-permute-start | bytes 442376 | tf_op jit(solution)/shard_map/ppermute | solution.py:220
  117.9 1.2 broadcast_select_fusion.refs_7_
  119.1 3.0 %collective-permute-done.23.refs_11_ = bf16[192,384]{1,0:T(8,128)(2,1)S(1)} collective-permute-done((bf16[192,384]{1,0:T(8,128)(2,1)S(1)}, bf16[192,384]{1,0:T(8,128)(2,1)S(1)}, u32[]{:S(2)}, u32[]{:S(2)}) %collective-permute-start.23) | collective-permute-done | bytes 147488 | tf_op jit(solution)/shard_map/ppermute | solution.py:220
  122.2 5.9 %shard_map.99 = (f32[2048,256]{1,0:T(8,128)}, f32[256,2048]{1,0:T(8,128)}) custom-call(s32[2]{0:T(128)S(1)} %pad_add_fusion.table, f32[1,2048]{1,0:T(1,128)S(1)} %copy-done.10, bf16[192,2048]{1,0:T(8,128)(2,1)S(1)} %fusion.23.value_ref.refs_0_, bf16[192,2048]{1,0:T(8,128)(2,1)} %collective-permute-done.refs_1_, bf16[192,2048]{1,0:T(8,128)(2,1)S(1)} %copy-done.1, ...), custom_call_target="tpu_custom_call" | custom-call | flops 805306368 | bytes 10485760 | tf_op jit(solution)/shard_map/pallas_call | solution.py:144
  (101 shorter events, 16.9 us)
Async XLA Ops:
  0.6 21.2 %copy-start = (bf16[1,2048,256]{2,1,0:T(8,128)(2,1)S(1)}, bf16[1,2048,256]{2,1,0:T(8,128)(2,1)}, u32[]{:S(2)}) copy-start(bf16[1,2048,256]{2,1,0:T(8,128)(2,1)} %param.12) | copy-start | bytes 3145732
  0.6 14.1 %collective-permute-start.1 = (bf16[192,2048]{1,0:T(8,128)(2,1)}, bf16[192,2048]{1,0:T(8,128)(2,1)}, u32[]{:S(2)}, u32[]{:S(2)}) collective-permute-start(bf16[192,2048]{1,0:T(8,128)(2,1)} %refs_2_), channel_id=1, source_target_pairs={{6,2},{10,6},{14,10},{7,3},{11,7},{15,11},{22,18},{26,22},{30,26},... | collective-permute-start | bytes 2359304 | tf_op jit(solution)/shard_map/ppermute | solution.py:276
  2.4 12.4 %collective-permute-start.2 = (bf16[192,2048]{1,0:T(8,128)(2,1)}, bf16[192,2048]{1,0:T(8,128)(2,1)}, u32[]{:S(2)}, u32[]{:S(2)}) collective-permute-start(bf16[192,2048]{1,0:T(8,128)(2,1)} %refs_2_), channel_id=1, source_target_pairs={{2,6},{6,10},{10,14},{3,7},{7,11},{11,15},{18,22},{22,26},{26,30},... | collective-permute-start | bytes 2359304 | tf_op jit(solution)/shard_map/ppermute | solution.py:276
  5.4 9.2 %copy-start.16 = (f32[4]{0:T(128)S(1)}, f32[4]{0:T(128)}, u32[]{:S(2)}) copy-start(f32[4]{0:T(128)} %param.14) | copy-start | bytes 52
  11.6 18.4 %collective-permute-start = (bf16[192,2048]{1,0:T(8,128)(2,1)S(1)}, bf16[192,2048]{1,0:T(8,128)(2,1)}, u32[]{:S(2)}, u32[]{:S(2)}) collective-permute-start(bf16[192,2048]{1,0:T(8,128)(2,1)S(1)} %fusion.23.value_ref.refs_0_), channel_id=1, source_target_pairs={{0,1},{1,0},{2,3},{3,2},{4,5},{5,4},{6,7},{7,6},{8,9},{9,8},{10,11... | collective-permute-start | bytes 2359304 | tf_op jit(solution)/shard_map/ppermute | solution.py:220
  16.8 15.6 %collective-permute-start.3 = (bf16[192,2048]{1,0:T(8,128)(2,1)S(1)}, bf16[192,2048]{1,0:T(8,128)(2,1)S(1)}, u32[]{:S(2)}, u32[]{:S(2)}) collective-permute-start(bf16[192,2048]{1,0:T(8,128)(2,1)S(1)} %get-tuple-element.80), channel_id=1, source_target_pairs={{0,4},{6,10},{10,14},{1,5},{7,11},{11,15},{16,20},{22,26},{26,30},... | collective-permute-start | bytes 2359304 | tf_op jit(solution)/shard_map/ppermute | solution.py:276
  20.3 12.1 %collective-permute-start.4 = (bf16[192,2048]{1,0:T(8,128)(2,1)S(1)}, bf16[192,2048]{1,0:T(8,128)(2,1)S(1)}, u32[]{:S(2)}, u32[]{:S(2)}) collective-permute-start(bf16[192,2048]{1,0:T(8,128)(2,1)S(1)} %get-tuple-element.79), channel_id=1, source_target_pairs={{12,8},{6,2},{10,6},{13,9},{7,3},{11,7},{28,24},{22,18},{26,22},{2... | collective-permute-start | bytes 2359304 | tf_op jit(solution)/shard_map/ppermute | solution.py:276
  22.4 10.0 %collective-permute-start.5 = (bf16[192,384]{1,0:T(8,128)(2,1)S(1)}, bf16[192,384]{1,0:T(8,128)(2,1)S(1)}, u32[]{:S(2)}, u32[]{:S(2)}) collective-permute-start(bf16[192,384]{1,0:T(8,128)(2,1)S(1)} %convert_element_type.119), channel_id=1, source_target_pairs={{0,4},{12,8},{1,5},{13,9},{2,6},{14,10},{3,7},{15,11},{16,20},{28,... | collective-permute-start | bytes 442376 | tf_op jit(solution)/shard_map/ppermute | solution.py:210
  30.0 15.4 %collective-permute-start.7 = (bf16[192,2048]{1,0:T(8,128)(2,1)}, bf16[192,2048]{1,0:T(8,128)(2,1)S(1)}, u32[]{:S(2)}, u32[]{:S(2)}) collective-permute-start(bf16[192,2048]{1,0:T(8,128)(2,1)} %collective-permute-done.refs_1_), channel_id=1, source_target_pairs={{2,0},{3,1},{6,4},{7,5},{10,8},{11,9},{14,12},{15,13},{18,16},{19,... | collective-permute-start | bytes 2359304 | tf_op jit(solution)/shard_map/ppermute | solution.py:230
  33.1 13.9 %collective-permute-start.8 = (bf16[192,2048]{1,0:T(8,128)(2,1)S(1)}, bf16[192,2048]{1,0:T(8,128)(2,1)S(1)}, u32[]{:S(2)}, u32[]{:S(2)}) collective-permute-start(bf16[192,2048]{1,0:T(8,128)(2,1)S(1)} %get-tuple-element.76), channel_id=1, source_target_pairs={{0,4},{4,8},{10,14},{1,5},{5,9},{11,15},{16,20},{20,24},{26,30},{1... | collective-permute-start | bytes 2359304 | tf_op jit(solution)/shard_map/ppermute | solution.py:276
  37.5 9.4 %collective-permute-start.9 = (bf16[192,2048]{1,0:T(8,128)(2,1)S(1)}, bf16[192,2048]{1,0:T(8,128)(2,1)S(1)}, u32[]{:S(2)}, u32[]{:S(2)}) collective-permute-start(bf16[192,2048]{1,0:T(8,128)(2,1)S(1)} %get-tuple-element.75), channel_id=1, source_target_pairs={{8,4},{12,8},{6,2},{9,5},{13,9},{7,3},{24,20},{28,24},{22,18},{25,... | collective-permute-start | bytes 2359304 | tf_op jit(solution)/shard_map/ppermute | solution.py:276
  38.2 7.2 %collective-permute-start.6 = (bf16[192,384]{1,0:T(8,128)(2,1)S(1)}, bf16[192,384]{1,0:T(8,128)(2,1)S(1)}, u32[]{:S(2)}, u32[]{:S(2)}) collective-permute-start(bf16[192,384]{1,0:T(8,128)(2,1)S(1)} %convert_element_type.125), channel_id=1, source_target_pairs={{4,8},{8,4},{5,9},{9,5},{6,10},{10,6},{7,11},{11,7},{20,24},{24,20... | collective-permute-start | bytes 442376 | tf_op jit(solution)/shard_map/ppermute | solution.py:210
  47.5 33.2 %collective-permute-start.12 = (bf16[192,2048]{1,0:T(8,128)(2,1)S(1)}, bf16[192,2048]{1,0:T(8,128)(2,1)S(1)}, u32[]{:S(2)}, u32[]{:S(2)}) collective-permute-start(bf16[192,2048]{1,0:T(8,128)(2,1)S(1)} %get-tuple-element.78), channel_id=1, source_target_pairs={{0,4},{4,8},{8,12},{1,5},{5,9},{9,13},{16,20},{20,24},{24,28},{17,... | collective-permute-start | bytes 2359304 | tf_op jit(solution)/shard_map/ppermute | solution.py:276
  60.2 20.5 %collective-permute-start.13 = (bf16[192,2048]{1,0:T(8,128)(2,1)S(1)}, bf16[192,2048]{1,0:T(8,128)(2,1)S(1)}, u32[]{:S(2)}, u32[]{:S(2)}) collective-permute-start(bf16[192,2048]{1,0:T(8,128)(2,1)S(1)} %get-tuple-element.77), channel_id=1, source_target_pairs={{4,0},{8,4},{12,8},{5,1},{9,5},{13,9},{20,16},{24,20},{28,24},{21,... | collective-permute-start | bytes 2359304 | tf_op jit(solution)/shard_map/ppermute | solution.py:276
  61.5 14.1 %collective-permute-start.10 = (bf16[192,384]{1,0:T(8,128)(2,1)S(1)}, bf16[192,384]{1,0:T(8,128)(2,1)S(1)}, u32[]{:S(2)}, u32[]{:S(2)}) collective-permute-start(bf16[192,384]{1,0:T(8,128)(2,1)S(1)} %convert_element_type.131), channel_id=1, source_target_pairs={{4,0},{8,12},{5,1},{9,13},{6,2},{10,14},{7,3},{11,15},{20,16},{24,... | collective-permute-start | bytes 442376 | tf_op jit(solution)/shard_map/ppermute | solution.py:210
  63.1 12.8 %copy-start.15 = (s32[192]{0:T(256)S(1)}, s32[192]{0:T(256)}, u32[]{:S(2)}) copy-start(s32[192]{0:T(256)} %param.15) | copy-start | bytes 2308
  76.0 4.7 %collective-permute-start.14 = (bf16[192,256]{1,0:T(8,128)(2,1)S(1)}, bf16[192,256]{1,0:T(8,128)(2,1)S(1)}, u32[]{:S(2)}, u32[]{:S(2)}) collective-permute-start(bf16[192,256]{1,0:T(8,128)(2,1)S(1)} %get-tuple-element.61.refs_8_), channel_id=1, source_target_pairs={{0,1},{1,0},{2,3},{3,2},{4,5},{5,4},{6,7},{7,6},{8,9},{9,8},{10,11... | collective-permute-start | bytes 294920 | tf_op jit(solution)/shard_map/ppermute | solution.py:220
  77.5 6.0 %collective-permute-start.11 = (bf16[192,2048]{1,0:T(8,128)(2,1)S(1)}, bf16[192,2048]{1,0:T(8,128)(2,1)S(1)}, u32[]{:S(2)}, u32[]{:S(2)}) collective-permute-start(bf16[192,2048]{1,0:T(8,128)(2,1)S(1)} %get-tuple-element.83), channel_id=1, source_target_pairs={{2,0},{3,1},{6,4},{7,5},{10,8},{11,9},{14,12},{15,13},{18,16},{19,... | collective-permute-start | bytes 2359304 | tf_op jit(solution)/shard_map/ppermute | solution.py:230
  81.4 3.2 %collective-permute-start.15 = (bf16[192,2048]{1,0:T(8,128)(2,1)S(1)}, bf16[192,2048]{1,0:T(8,128)(2,1)S(1)}, u32[]{:S(2)}, u32[]{:S(2)}) collective-permute-start(bf16[192,2048]{1,0:T(8,128)(2,1)S(1)} %fusion.1), channel_id=1, source_target_pairs={{0,2},{1,3},{4,6},{5,7},{8,10},{9,11},{12,14},{13,15},{16,18},{17,... | collective-permute-start | bytes 2359304 | tf_op jit(solution)/shard_map/ppermute | solution.py:230
  82.7 6.5 %collective-permute-start.17 = (bf16[192,2048]{1,0:T(8,128)(2,1)S(1)}, bf16[192,2048]{1,0:T(8,128)(2,1)S(1)}, u32[]{:S(2)}, u32[]{:S(2)}) collective-permute-start(bf16[192,2048]{1,0:T(8,128)(2,1)S(1)} %get-tuple-element.83), channel_id=1, source_target_pairs={{2,3},{3,2},{6,7},{7,6},{10,11},{11,10},{14,15},{15,14},{18,19},{1... | collective-permute-start | bytes 2359304 | tf_op jit(solution)/shard_map/ppermute | solution.py:220
  83.4 10.3 %copy-start.2 = (bf16[192,2048]{1,0:T(8,128)(2,1)}, bf16[192,2048]{1,0:T(8,128)(2,1)S(1)}, u32[]{:S(2)}) copy-start(bf16[192,2048]{1,0:T(8,128)(2,1)S(1)} %collective-permute-done.11.refs_4_) | copy-start | bytes 2359300
  85.1 9.4 %copy-start.4 = (bf16[192,2048]{1,0:T(8,128)(2,1)}, bf16[192,2048]{1,0:T(8,128)(2,1)S(1)}, u32[]{:S(2)}) copy-start(bf16[192,2048]{1,0:T(8,128)(2,1)S(1)} %get-tuple-element.72.refs_6_) | copy-start | bytes 2359300
  85.1 8.7 %copy-start.1 = (bf16[192,2048]{1,0:T(8,128)(2,1)S(1)}, bf16[192,2048]{1,0:T(8,128)(2,1)}, u32[]{:S(2)}) copy-start(bf16[192,2048]{1,0:T(8,128)(2,1)} %refs_2_) | copy-start | bytes 2359300
  85.1 4.0 %collective-permute-start.16 = (f32[2,192]{1,0:T(2,128)S(1)}, f32[2,192]{1,0:T(2,128)S(1)}, u32[]{:S(2)}, u32[]{:S(2)}) collective-permute-start(f32[2,192]{1,0:T(2,128)S(1)} %pad_maximum_fusion.2), channel_id=1, source_target_pairs={{0,4},{4,0},{8,12},{12,8},{1,5},{5,1},{9,13},{13,9},{2,6},{6,2},{1... | collective-permute-start | bytes 4616 | tf_op jit(solution)/shard_map/ppermute | solution.py:210
  85.2 18.2 %collective-permute-start.21 = (bf16[192,2048]{1,0:T(8,128)(2,1)S(1)}, bf16[192,2048]{1,0:T(8,128)(2,1)S(1)}, u32[]{:S(2)}, u32[]{:S(2)}) collective-permute-start(bf16[192,2048]{1,0:T(8,128)(2,1)S(1)} %fusion.1), channel_id=1, source_target_pairs={{0,1},{1,0},{4,5},{5,4},{8,9},{9,8},{12,13},{13,12},{16,17},{17,16... | collective-permute-start | bytes 2359304 | tf_op jit(solution)/shard_map/ppermute | solution.py:220
  89.2 4.5 %collective-permute-start.18 = (f32[2,192]{1,0:T(2,128)S(1)}, f32[2,192]{1,0:T(2,128)S(1)}, u32[]{:S(2)}, u32[]{:S(2)}) collective-permute-start(f32[2,192]{1,0:T(2,128)S(1)} %fusion.37), channel_id=1, source_target_pairs={{0,8},{4,12},{8,0},{12,4},{1,9},{5,13},{9,1},{13,5},{2,10},{6,14},... | collective-permute-start | bytes 4616 | tf_op jit(solution)/shard_map/ppermute | solution.py:210
  94.5 4.7 %collective-permute-start.19 = (bf16[192,256]{1,0:T(8,128)(2,1)S(1)}, bf16[192,256]{1,0:T(8,128)(2,1)S(1)}, u32[]{:S(2)}, u32[]{:S(2)}) collective-permute-start(bf16[192,256]{1,0:T(8,128)(2,1)S(1)} %get-tuple-element.85), channel_id=1, source_target_pairs={{0,4},{4,0},{8,12},{12,8},{1,5},{5,1},{9,13},{13,9},{2,6},{6,2},{1... | collective-permute-start | bytes 294920 | tf_op jit(solution)/shard_map/ppermute | solution.py:210
  99.2 5.6 %collective-permute-start.20 = (bf16[192,256]{1,0:T(8,128)(2,1)S(1)}, bf16[192,256]{1,0:T(8,128)(2,1)S(1)}, u32[]{:S(2)}, u32[]{:S(2)}) collective-permute-start(bf16[192,256]{1,0:T(8,128)(2,1)S(1)} %fusion.30), channel_id=1, source_target_pairs={{0,8},{4,12},{8,0},{12,4},{1,9},{5,13},{9,1},{13,5},{2,10},{6,14},... | collective-permute-start | bytes 294920 | tf_op jit(solution)/shard_map/ppermute | solution.py:210
  105.5 12.4 %collective-permute-start.22 = (bf16[192,2048]{1,0:T(8,128)(2,1)}, bf16[192,2048]{1,0:T(8,128)(2,1)S(1)}, u32[]{:S(2)}, u32[]{:S(2)}) collective-permute-start(bf16[192,2048]{1,0:T(8,128)(2,1)} %broadcast_select_fusion.1), channel_id=1, source_target_pairs={{0,2},{2,0},{1,3},{3,1},{4,6},{6,4},{5,7},{7,5},{8,10},{10,8},{9,1... | collective-permute-start | bytes 2359304 | tf_op jit(solution)/shard_map/ppermute | solution.py:409
  114.7 7.4 %copy-start.3 = (bf16[192,2048]{1,0:T(8,128)(2,1)S(1)}, bf16[192,2048]{1,0:T(8,128)(2,1)}, u32[]{:S(2)}) copy-start(bf16[192,2048]{1,0:T(8,128)(2,1)} %copy-done.2) | copy-start | bytes 2359300
  114.7 7.4 %copy-start.5 = (bf16[192,2048]{1,0:T(8,128)(2,1)S(1)}, bf16[192,2048]{1,0:T(8,128)(2,1)}, u32[]{:S(2)}) copy-start(bf16[192,2048]{1,0:T(8,128)(2,1)} %copy-done.4) | copy-start | bytes 2359300
  116.3 5.9 %collective-permute-start.23 = (bf16[192,384]{1,0:T(8,128)(2,1)S(1)}, bf16[192,384]{1,0:T(8,128)(2,1)S(1)}, u32[]{:S(2)}, u32[]{:S(2)}) collective-permute-start(bf16[192,384]{1,0:T(8,128)(2,1)S(1)} %pad_maximum_fusion.1.refs_10_), channel_id=1, source_target_pairs={{0,1},{1,0},{2,3},{3,2},{4,5},{5,4},{6,7},{7,6},{8,9},{9,8},{10,11... | collective-permute-start | bytes 442376 | tf_op jit(solution)/shard_map/ppermute | solution.py:220
  (9 other events, 34.3 us)

commit v6 on v4

--- a/solution.py
+++ b/solution.py
@@ -29,7 +29,9 @@
     return found
 
 
-def block_kernel(table, value_ref, weight_ref, out_ref, wide, tall, arrived, *, blocks, tile, tiles):
+def block_kernel(
+    table, value_ref, riding_ref, weight_ref, out_ref, wide, tall, arrived, *, blocks, tile, tiles
+):
     section = table[0]
     block = look_up(table[1], blocks)
     step = pl.program_id(0)
@@ -43,6 +45,11 @@
         rows = pl.ds(pl.multiple_of(index * tile, tile), tile)
         return pltpu.make_async_copy(weight_ref.at[rows, whole], tall.at[index], arrived.at[index])
 
+    @pl.when(step == 0)
+    def _():
+        out_ref[:, width:] = riding_ref[...]
+
+    columns = pl.ds(pl.multiple_of(step * tile, tile), tile)
     for number, is_wide in ((0, True), (1, False)):
 
         @pl.when(section == number)
@@ -58,15 +65,18 @@
 
             copy_of(step, is_wide).wait()
             if is_wide:
-                out_ref[...] = jnp.dot(value_ref[...], wide[step], preferred_element_type=F32)
+                out_ref[:, columns] = jnp.dot(
+                    value_ref[:, :width], wide[step], preferred_element_type=F32
+                )
             else:
-                out_ref[...] = lax.dot_general(
-                    value_ref[...], tall[step], CONTRACT_LAST, preferred_element_type=F32
+                out_ref[:, columns] = lax.dot_general(
+                    value_ref[:, :width], tall[step], CONTRACT_LAST, preferred_element_type=F32
                 )
 
 
-def block_product(table, value, weight, blocks):
-    rows, width = value.shape
+def block_product(table, value, riding, weight, blocks):
+    rows, columns = value.shape
+    width = columns - riding.shape[1]
     tile = min(256, width)
     tiles = width // tile
     return pl.pallas_call(
@@ -75,22 +85,23 @@
             num_scalar_prefetch=1,
             grid=(tiles,),
             in_specs=[
-                pl.BlockSpec((rows, width), lambda step, table: (0, 0)),
+                pl.BlockSpec(value.shape, lambda step, table: (0, 0)),
+                pl.BlockSpec(riding.shape, lambda step, table: (0, 0)),
                 pl.BlockSpec(memory_space=pl.ANY),
             ],
-            out_specs=pl.BlockSpec((rows, tile), lambda step, table: (0, step)),
+            out_specs=pl.BlockSpec(value.shape, lambda step, table: (0, 0)),
             scratch_shapes=[
                 pltpu.VMEM((tiles, width, tile), BF16),
                 pltpu.VMEM((tiles, tile, width), BF16),
                 pltpu.SemaphoreType.DMA((tiles,)),
             ],
         ),
-        out_shape=jax.ShapeDtypeStruct((rows, width), F32),
-        compiler_params=pltpu.CompilerParams(vmem_limit_bytes=24 * 1024 * 1024),
+        out_shape=jax.ShapeDtypeStruct(value.shape, F32),
+        compiler_params=pltpu.CompilerParams(vmem_limit_bytes=28 * 1024 * 1024),
         cost_estimate=pl.CostEstimate(
             flops=8 * rows * width * width, bytes_accessed=2 * width * width, transcendentals=0
         ),
-    )(table, value, weight)
+    )(table, value, riding, weight)
 
 
 def gradient_kernel(table, gain_ref, *refs, replicas):
@@ -187,17 +198,16 @@
     return chosen
 
 
-def sum_steps():
+def doubling_steps():
     count = lax.axis_size("tensor")
-    return [1 << bit for bit in range(count.bit_length() - 1)]
-
-
-def add_neighbour(value, distance):
-    count = lax.axis_size("tensor")
-    other = lax.ppermute(
-        value.astype(BF16), "tensor", [(place, place ^ distance) for place in range(count)]
-    )
-    return value + other.astype(F32)
+    return [
+        [(place, place ^ (1 << bit)) for place in range(count)]
+        for bit in range(count.bit_length() - 1)
+    ]
+
+
+def sum_step(value, pairs, wire=BF16):
+    return value + lax.ppermute(value.astype(wire), "tensor", pairs).astype(F32)
 
 
 def with_other_replicas(value, sections=(0, 1)):
@@ -262,52 +272,43 @@
         return lax.ppermute(value, ("tensor", "section"), pairs)
 
     token_float = tokens.astype(F32)
-    early = lax.optimization_barrier(
-        jnp.where(is_first, (token_float * gain_row).astype(BF16), cotangent)
-    )
+    early = jnp.where(is_first, (token_float * gain_row).astype(BF16), cotangent)
+    riding = jnp.concatenate(
+        [
+            jnp.where(is_first, times_down(early), times_up_transposed(early)),
+            jnp.broadcast_to(jnp.sum(token_float * token_float, axis=1, keepdims=True), (rows, 128)),
+        ],
+        axis=1,
+    )
+    first = jnp.concatenate([early, riding.astype(BF16)], axis=1)
+    early, riding, first = lax.optimization_barrier((early, riding, first))
 
     everyone = range(count)
     arrivals = [
         (
-            line(cotangent, [], [z for z in everyone if z + 1 < count], 1),
-            line(cotangent, [], [z for z in everyone if z > 0], -1),
+            line(first, [], [z for z in everyone if z + 1 < count], 1),
+            line(first, [], [z for z in everyone if z > 0], -1),
         )
     ]
-    early_all = with_other_replicas(early)
-
     parts = []
-    small_sum = None
-    steps_left = sum_steps()
     for stage in range(count):
         wanted = [None if stage == 0 else second_slots[z][stage] for z in everyone]
         cases = sorted({slot for slot in wanted if slot is not None})
-        here = [early] + [arrivals[slot][side] for slot, side in cases]
-        if stage == 1:
-            after, again, *_ = lax.optimization_barrier((cotangent, early, *sent))
-            squares = jnp.sum(token_float * token_float, axis=1, keepdims=True)
-            small_sum = jnp.concatenate(
-                [
-                    times_up_transposed(after),
-                    times_down(again),
-                    jnp.broadcast_to(squares, (rows, 128)),
-                ],
-                axis=1,
-            )
-        elif stage > 1 and steps_left:
-            small_sum = add_neighbour(small_sum, steps_left.pop(0))
-        if stage == 2:
-            cotangent_all = [cotangent] + [to_other_core(other, 1) for other in early_all[1:]]
-        if stage == 3:
-            small_sum, *cotangent_all = lax.optimization_barrier((small_sum, *cotangent_all))
+        here = [first] + [arrivals[slot][side] for slot, side in cases]
         if stage > 0:
-            *here, small_sum = lax.optimization_barrier((*here, small_sum, *sent))[: len(here) + 1]
+            here = lax.optimization_barrier((*here, *sent))[: len(here)]
         value = pick(
             place_of,
             [0] * count + [0 if slot is None else 1 + cases.index(slot) for slot in wanted],
             here,
         )
         order = [blocks[stage] for blocks in first_order + second_order]
-        part = block_product(table, value, weight, order)
+        part = block_product(table, value, riding, weight, order)
+        if stage == 0:
+            part, after = lax.optimization_barrier((part, early))
+            early_all = [early] + with_other_replicas(after)[1:]
+        if stage == 2:
+            part, *early_all = lax.optimization_barrier((part, *early_all))
         parts.append(part)
         slot = stage + 1
         if slot == count:
@@ -341,56 +342,69 @@
         )
     from_left, from_right = arrivals[-1]
 
-    while steps_left:
-        small_sum = add_neighbour(small_sum, steps_left.pop(0))
-    rank_up, rank_down = small_sum[:, :ranks], small_sum[:, ranks : 2 * ranks]
-    inv_first = lax.rsqrt(small_sum[:, 2 * ranks : 2 * ranks + 1] / features + EPSILON)
-    small_early = (coefficients * jnp.where(is_first, rank_down, rank_up)).astype(BF16)
-    low_product = jnp.where(
-        is_first,
-        jnp.dot(small_early, up, preferred_element_type=F32),
-        lax.dot_general(small_early, down, CONTRACT_LAST, preferred_element_type=F32),
-    )
-
-    pulled = (gain_row * (sum(parts) + low_product)).astype(BF16)
-    from_left, from_right, _ = lax.optimization_barrier((from_left, from_right, pulled))
+    passed = sum(
+        (arrived[:, width:].astype(F32) for pair in arrivals[:-1] for arrived in pair), riding
+    )
+
+    def small_factor(rank_sum):
+        return (coefficients * rank_sum).astype(BF16)
+
+    small_second = small_factor(passed[:, :ranks])
+
+    pulled = sum(part[:, :width] for part in parts) + lax.dot_general(
+        small_second, down, CONTRACT_LAST, preferred_element_type=F32
+    )
+    pulled = (gain_row * pulled).astype(BF16)
+    pulled_others = with_other_replicas(pulled, (1,))[1:]
     pulled = to_other_core(pulled, 1)
-    pulled_all = with_other_replicas(pulled, (0,))
-    pulled_rank = times_up_transposed(pulled)
-
-    projected = parts[-1] + from_left.astype(F32) + from_right.astype(F32) + low_product
+    from_left, from_right, pulled = lax.optimization_barrier((from_left, from_right, pulled))
+
+    summed = parts[-1] + from_left.astype(F32) + from_right.astype(F32)
+    small_first = small_factor(summed[:, width : width + ranks])
+    inv_first = lax.rsqrt(summed[:, width + ranks : width + ranks + 1] / features + EPSILON)
+    projected = summed[:, :width] + jnp.dot(small_first, up, preferred_element_type=F32)
     hidden = (token_float + inv_first * projected).astype(BF16)
-    hidden_here = jnp.where(is_first, hidden, to_other_core(hidden, 0))
+    swap = [(0, 1), (1, 0)]
+    swapped = [
+        lax.ppermute(jnp.where(is_first, hidden, other), "section", swap) for other in early_all[1:]
+    ]
+    hidden_on_second = swapped[0] if swapped else to_other_core(hidden, 0)
+    cotangent_all = [cotangent] + swapped
+    hidden_here = jnp.where(is_first, hidden, hidden_on_second)
+    small_early = jnp.where(is_first, small_first, small_second)
     hidden_others = with_other_replicas(hidden, (0,))[1:]
     hidden_float = hidden_here.astype(F32)
-    row_sums = [
-        jnp.broadcast_to(jnp.sum(terms, axis=1, keepdims=True), (rows, 64))
-        for terms in (hidden_float * hidden_float, hidden_float * pulled.astype(F32))
+    pulled_float = pulled.astype(F32)
+    row_sums = jnp.stack(
+        [jnp.sum(hidden_float * hidden_float, axis=1), jnp.sum(hidden_float * pulled_float, axis=1)]
+    )
+    for step in doubling_steps():
+        row_sums = sum_step(row_sums, step, F32)
+    inv_second = lax.rsqrt(row_sums[0] / features + EPSILON)[:, None]
+    toward_hidden = row_sums[1][:, None] * inv_second * inv_second * inv_second / features
+    hidden_grad = cotangent.astype(F32) + inv_second * pulled_float - toward_hidden * hidden_float
+    rank_late = jnp.where(
+        is_first,
+        times_up_transposed(hidden_grad.astype(BF16)),
+        times_down((hidden_float * gain_row).astype(BF16)),
+    )
+    for at, step in enumerate(doubling_steps()):
+        rank_late = sum_step(rank_late, step)
+        if at == 0:
+            rank_late, *pulled_others = lax.optimization_barrier((rank_late, *pulled_others))
+
+    rank_late, *swapped = lax.optimization_barrier(
+        (
+            rank_late,
+            *[jnp.where(is_first, *pair) for pair in zip(hidden_others, pulled_others)],
+        )
+    )
+    swapped = [lax.ppermute(other, "section", swap) for other in swapped]
+    hidden_all = [hidden_here] + [
+        jnp.where(is_first, *pair) for pair in zip(hidden_others, swapped)
     ]
-    hidden_rank = jnp.where(
-        is_first,
-        times_up_transposed(hidden_here),
-        times_down((hidden_float * gain_row).astype(BF16)),
-    )
-    late_sum = jnp.concatenate([hidden_rank, pulled_rank, *row_sums], axis=1)
-    for at, distance in enumerate(sum_steps()):
-        late_sum = add_neighbour(late_sum, distance)
-        if at == 0:
-            late_sum, *pulled_all = lax.optimization_barrier((late_sum, *pulled_all))
-    late_sum, *hidden_others = lax.optimization_barrier((late_sum, *hidden_others))
-    hidden_all = [hidden_here] + [
-        jnp.where(is_first, other, to_other_core(other, 0)) for other in hidden_others
-    ]
-
-    inv_second = lax.rsqrt(late_sum[:, 2 * ranks : 2 * ranks + 1] / features + EPSILON)
-    toward_hidden = (
-        late_sum[:, 2 * ranks + 64 : 2 * ranks + 65]
-        * inv_second * inv_second * inv_second / features
-    )
-    hidden_rank, pulled_rank = late_sum[:, :ranks], late_sum[:, ranks : 2 * ranks]
-    rank_late = jnp.where(
-        is_first, rank_up + inv_second * pulled_rank - toward_hidden * hidden_rank, hidden_rank
-    )
+    pulled_all = [pulled] + swapped
+
     row_scale = jnp.where(is_first, inv_first, inv_second)
     small_late = coefficients * rank_late * row_scale
     small_early = small_early.astype(F32) * row_scale

time: 121 us -> 132 us (1.091)
  other arithmetic: 8.92 us -> 19.8 us
  waiting for transfers between devices: 37.9 us -> 29.6 us
  local copies, waits for them, and re-layouts: 0.8 us -> 3.77 us
  matrix products: 3.41 us -> 5.56 us
  Pallas kernels: 29.7 us -> 31.8 us
    ppermute x4 -> x6, waiting for transfers between devices: 27.8 us -> 8.27 us  [the longest x4 6.36 us: sum_step(): return value + lax.ppermute(value.astype(wire), 'tensor', pairs).astype(F32)]
    ppermute x4, waiting for transfers between devices: 6.94 us -> 13.5 us  [with_other_replicas(): lax.ppermute(value, ('section', 'replica'), [(s * count + r, s * count +...]
    ppermute x8, starting transfers between devices: 14.6 us -> 19.7 us  [line(): return lax.ppermute(value, ('tensor', 'section'), pairs)]
    ppermute x4 -> x1, starting transfers between devices: 5.26 us -> 1.42 us  [to_other_core(): return lax.ppermute(value, 'section', [(source, 1 - source)])]
    select_n x3, other arithmetic: 0.79 us -> 4.39 us  [pick(): chosen = jnp.where(is_one_of(number, members), cases[at], chosen)]
    ppermute x4, starting transfers between devices: 9.99 us -> 6.93 us  [with_other_replicas(): lax.ppermute(value, ('section', 'replica'), [(s * count + r, s * count +...]
    ppermute x4 -> x1, waiting for transfers between devices: 0.01 us -> 2.88 us  [to_other_core(): return lax.ppermute(value, 'section', [(source, 1 - source)])]
    ppermute x4 -> x6, starting transfers between devices: 8.3 us -> 10.9 us  [the longest x4 6.77 us: sum_step(): return value + lax.ppermute(value.astype(wire), 'tensor', pairs).astype(F32)]
  transfers between devices with their start and end apart: 20 -> 19, of which waited for: 7 -> 8; matrix products, arithmetic and copies ran while one was open for 10% -> 12% of each run, Pallas kernels for 21% -> 20%
where the time goes in v6:
time: 132 us; the launch traced here: 131 us
  starting transfers between devices  39 us (30%)
  Pallas kernels  31.8 us (24%)
  waiting for transfers between devices  29.6 us (22%)
  other arithmetic  19.8 us (15%)
  matrix products  5.56 us (4%)
  local copies, waits for them, and re-layouts  3.77 us (3%)
    pallas_call x4, Pallas kernels, block_product(): pl.pallas_call(functools.partial(block_kernel, blocks=blocks, tile=tile,...  25.7 us
    ppermute x8, starting transfers between devices, line(): return lax.ppermute(value, ('tensor', 'section'), pairs)  19.7 us
    ppermute x4, waiting for transfers between devices, with_other_replicas(): lax.ppermute(value, ('section', 'replica'), [(s * count + r, s * count +...  13.5 us
    ppermute x4, starting transfers between devices, with_other_replicas(): lax.ppermute(value, ('section', 'replica'), [(s * count + r, s * count +...  6.93 us
    ppermute x4, starting transfers between devices, sum_step(): return value + lax.ppermute(value.astype(wire), 'tensor', pairs).astype(F32)  6.77 us
    ppermute x4, waiting for transfers between devices, sum_step(): return value + lax.ppermute(value.astype(wire), 'tensor', pairs).astype(F32)  6.36 us
    pallas_call x1, Pallas kernels, gradients(): pl.pallas_call(functools.partial(gradient_kernel, replicas=replicas), gri...  6.05 us
    ppermute x8, waiting for transfers between devices, line(): return lax.ppermute(value, ('tensor', 'section'), pairs)  4.97 us
  transfers between devices with their start and end apart: 19, of which 8 were waited for; matrix products, arithmetic and copies ran while one was open for 12% of the time, Pallas kernels for 20%

profile of v6, /device:TPU:0, one launch (start us, length us, event | category | flops | bytes accessed | tf_op | source)
XLA Modules:
  0.0 130.7 jit_solution(16117641438230865653)
XLA Ops:
  0.7 1.5 %fusion.9 = f32[192]{0:T(256)S(1)} fusion(bf16[192,2048]{1,0:T(8,128)(2,1)} %param.8), kind=kLoop, calls=%fused_computation.25 | loop fusion | flops 1179456 | bytes 787200 | tf_op jit(solution)/shard_map/reduce_sum | solution.py:279
  2.2 2.3 %fusion.27.refs_0_ = bf16[192,2048]{1,0:T(8,128)(2,1)} fusion(bf16[192,2048]{1,0:T(8,128)(2,1)} %refs_2_.1, bf16[192,2048]{1,0:T(8,128)(2,1)} %param.8, f32[2048]{0:T(1024)} %bitcast.34, pred[]{:T(512)S(6)} %eq.21), kind=kLoop, calls=%fused_computation.47 | loop fusion | flops 1572864 | bytes 2367489 | tf_op jit(solution)/shard_map/jit(_where)/select_n | solution.py:275
  4.5 1.5 %fusion.24 = f32[192,256]{1,0:T(8,128)S(1)} fusion(bf16[192,2048]{1,0:T(8,128)(2,1)} %fusion.27.refs_0_, bf16[1,2048,256]{2,1,0:T(8,128)(2,1)S(1)} %copy-done.9), kind=kOutput, calls=%fused_computation.41 | convolution fusion | flops 201326592 | bytes 2031616 | tf_op jit(solution)/shard_map/dot_general | solution.py:263
  6.0 1.6 %convolution_select_fusion = f32[192,256]{1,0:T(8,128)S(1)} fusion(f32[192,256]{1,0:T(8,128)S(1)} %fusion.24, bf16[192,2048]{1,0:T(8,128)(2,1)} %fusion.27.refs_0_, bf16[1,256,2048]{2,1,0:T(8,128)(2,1)S(1)} %copy-done, pred[]{:T(512)S(6)} %eq.21), kind=kOutput, calls=%fused_computation.32 | convolution fusion | flops 201375744 | bytes 2228225 | tf_op jit(solution)/shard_map/dot_general | solution.py:266
  7.8 2.1 %pad_maximum_fusion.value_ref = bf16[192,2432]{1,0:T(8,128)(2,1)} fusion(bf16[192,384]{1,0:T(8,128)(2,1)S(1)} %fusion.47, bf16[192,2048]{1,0:T(8,128)(2,1)} %fusion.27.refs_0_), kind=kLoop, calls=%fused_computation.43 | loop fusion | flops 1867776 | bytes 1867776 | tf_op jit(solution)/shard_map/concatenate | solution.py:283
  9.9 1.6 %collective-permute-start.1 = (bf16[192,2432]{1,0:T(8,128)(2,1)}, bf16[192,2432]{1,0:T(8,128)(2,1)}, u32[]{:S(2)}, u32[]{:S(2)}) collective-permute-start(bf16[192,2432]{1,0:T(8,128)(2,1)} %pad_maximum_fusion.value_ref), channel_id=1, source_target_pairs={{2,6},{6,10},{10,14},{3,7},{7,11},{11,15},{18,22},{22,26},{26,30},... | collective-permute-start | bytes 2801672 | tf_op jit(solution)/shard_map/ppermute | solution.py:272
  11.5 1.6 %collective-permute-start = (bf16[192,2432]{1,0:T(8,128)(2,1)}, bf16[192,2432]{1,0:T(8,128)(2,1)}, u32[]{:S(2)}, u32[]{:S(2)}) collective-permute-start(bf16[192,2432]{1,0:T(8,128)(2,1)} %pad_maximum_fusion.value_ref), channel_id=1, source_target_pairs={{6,2},{10,6},{14,10},{7,3},{11,7},{15,11},{22,18},{26,22},{30,26},... | collective-permute-start | bytes 2801672 | tf_op jit(solution)/shard_map/ppermute | solution.py:272
  13.2 7.3 %shard_map.95 = f32[192,2432]{1,0:T(8,128)S(1)} custom-call(s32[2]{0:T(128)S(1)} %pad_add_fusion.table, bf16[192,2432]{1,0:T(8,128)(2,1)} %pad_maximum_fusion.value_ref, f32[192,384]{1,0:T(8,128)S(1)} %pad_maximum_fusion.1.riding_ref, bf16[2048,8192]{1,0:T(8,128)(2,1)} %bitcast.37), custom_call_target="tpu_custom_call" | custom-call | flops 6442450944 | bytes 8388608 | tf_op jit(solution)/shard_map/pallas_call | solution.py:82
  20.5 3.0 %collective-permute-start.4 = (bf16[192,2048]{1,0:T(8,128)(2,1)}, bf16[192,2048]{1,0:T(8,128)(2,1)}, u32[]{:S(2)}, u32[]{:S(2)}) collective-permute-start(bf16[192,2048]{1,0:T(8,128)(2,1)} %fusion.27.refs_0_), channel_id=1, source_target_pairs={{0,1},{1,0},{2,3},{3,2},{4,5},{5,4},{6,7},{7,6},{8,9},{9,8},{10,11... | collective-permute-start | bytes 2359304 | tf_op jit(solution)/shard_map/ppermute | solution.py:216
  23.7 1.8 %add_convert_fusion.4 = (bf16[192,2432]{1,0:T(8,128)(2,1)S(1)}, bf16[192,2432]{1,0:T(8,128)(2,1)S(1)}) fusion(bf16[192,2432]{1,0:T(8,128)(2,1)} %collective-permute-done, f32[192,2432]{1,0:T(8,128)S(1)} %shard_map.95, pred[]{:T(512)S(6)} %eq.21, bf16[192,2432]{1,0:T(8,128)(2,1)} %collective-permute-done.1), kind=kLoop, calls=%fused_computation.19 | loop fusion | flops 3268608 | bytes 5603329 | tf_op jit(solution)/shard_map/convert_element_type | solution.py:326
  26.2 3.5 %collective-permute-start.2 = (bf16[192,2432]{1,0:T(8,128)(2,1)S(1)}, bf16[192,2432]{1,0:T(8,128)(2,1)S(1)}, u32[]{:S(2)}, u32[]{:S(2)}) collective-permute-start(bf16[192,2432]{1,0:T(8,128)(2,1)S(1)} %get-tuple-element.72), channel_id=1, source_target_pairs={{0,4},{6,10},{10,14},{1,5},{7,11},{11,15},{16,20},{22,26},{26,30},... | collective-permute-start | bytes 2801672 | tf_op jit(solution)/shard_map/ppermute | solution.py:272
  33.0 6.1 %shard_map.96 = f32[192,2432]{1,0:T(8,128)S(1)} custom-call(s32[2]{0:T(128)S(1)} %pad_add_fusion.table, bf16[192,2432]{1,0:T(8,128)(2,1)S(1)} %select_select_fusion.2.value_ref, f32[192,384]{1,0:T(8,128)S(1)} %pad_maximum_fusion.1.riding_ref, bf16[2048,8192]{1,0:T(8,128)(2,1)} %bitcast.38), custom_call_target="tpu_custom_call" | custom-call | flops 6442450944 | bytes 8388608 | tf_op jit(solution)/shard_map/pallas_call | solution.py:82
  39.2 1.6 %collective-permute-done.2 = bf16[192,2432]{1,0:T(8,128)(2,1)S(1)} collective-permute-done((bf16[192,2432]{1,0:T(8,128)(2,1)S(1)}, bf16[192,2432]{1,0:T(8,128)(2,1)S(1)}, u32[]{:S(2)}, u32[]{:S(2)}) %collective-permute-start.2) | collective-permute-done | bytes 933920 | tf_op jit(solution)/shard_map/ppermute | solution.py:272
  42.2 5.0 %collective-permute-start.5 = (bf16[192,2432]{1,0:T(8,128)(2,1)S(1)}, bf16[192,2432]{1,0:T(8,128)(2,1)S(1)}, u32[]{:S(2)}, u32[]{:S(2)}) collective-permute-start(bf16[192,2432]{1,0:T(8,128)(2,1)S(1)} %get-tuple-element.66), channel_id=1, source_target_pairs={{0,4},{4,8},{10,14},{1,5},{5,9},{11,15},{16,20},{20,24},{26,30},{1... | collective-permute-start | bytes 2801672 | tf_op jit(solution)/shard_map/ppermute | solution.py:272
  47.2 1.5 %select_select_fusion.1.value_ref = bf16[192,2432]{1,0:T(8,128)(2,1)S(1)} fusion(bf16[192,2432]{1,0:T(8,128)(2,1)S(1)} %collective-permute-done.3, bf16[192,2432]{1,0:T(8,128)(2,1)S(1)} %collective-permute-done.2, bf16[192,2432]{1,0:T(8,128)(2,1)} %collective-permute-done, bf16[192,2432]{1,0:T(8,128)(2,1)} %pad_maximum_fusion.value_ref, pred[]{:T(512)S(6)} %or.7, ...), kind=kLoop, calls=%fused_computation.45 | loop fusion | flops 1400832 | bytes 4669443 | tf_op jit(solution)/shard_map/jit(_where)/select_n | solution.py:197
  48.7 6.1 %shard_map.97 = f32[192,2432]{1,0:T(8,128)S(1)} custom-call(s32[2]{0:T(128)S(1)} %pad_add_fusion.table, bf16[192,2432]{1,0:T(8,128)(2,1)S(1)} %select_select_fusion.1.value_ref, f32[192,384]{1,0:T(8,128)S(1)} %pad_maximum_fusion.1.riding_ref, bf16[2048,8192]{1,0:T(8,128)(2,1)} %bitcast.39), custom_call_target="tpu_custom_call" | custom-call | flops 6442450944 | bytes 8388608 | tf_op jit(solution)/shard_map/pallas_call | solution.py:82
  54.9 3.3 %collective-permute-done.5 = bf16[192,2432]{1,0:T(8,128)(2,1)S(1)} collective-permute-done((bf16[192,2432]{1,0:T(8,128)(2,1)S(1)}, bf16[192,2432]{1,0:T(8,128)(2,1)S(1)}, u32[]{:S(2)}, u32[]{:S(2)}) %collective-permute-start.5) | collective-permute-done | bytes 933920 | tf_op jit(solution)/shard_map/ppermute | solution.py:272
  60.0 5.2 %collective-permute-start.7 = (bf16[192,2432]{1,0:T(8,128)(2,1)S(1)}, bf16[192,2432]{1,0:T(8,128)(2,1)S(1)}, u32[]{:S(2)}, u32[]{:S(2)}) collective-permute-start(bf16[192,2432]{1,0:T(8,128)(2,1)S(1)} %get-tuple-element.70), channel_id=1, source_target_pairs={{0,4},{4,8},{8,12},{1,5},{5,9},{9,13},{16,20},{20,24},{24,28},{17,... | collective-permute-start | bytes 2801672 | tf_op jit(solution)/shard_map/ppermute | solution.py:272
  65.3 1.5 %select_select_fusion.value_ref = bf16[192,2432]{1,0:T(8,128)(2,1)S(1)} fusion(bf16[192,2432]{1,0:T(8,128)(2,1)S(1)} %collective-permute-done.6, bf16[192,2432]{1,0:T(8,128)(2,1)S(1)} %collective-permute-done.5, bf16[192,2432]{1,0:T(8,128)(2,1)S(1)} %collective-permute-done.3, bf16[192,2432]{1,0:T(8,128)(2,1)S(1)} %collective-permute-done.2, ...), kind=kLoop, calls=%fused_computation.44 | loop fusion | flops 1867776 | bytes 5603332 | tf_op jit(solution)/shard_map/jit(_where)/select_n | solution.py:197
  66.8 6.1 %shard_map.98 = f32[192,2432]{1,0:T(8,128)S(1)} custom-call(s32[2]{0:T(128)S(1)} %pad_add_fusion.table, bf16[192,2432]{1,0:T(8,128)(2,1)S(1)} %select_select_fusion.value_ref, f32[192,384]{1,0:T(8,128)S(1)} %pad_maximum_fusion.1.riding_ref, bf16[2048,8192]{1,0:T(8,128)(2,1)} %bitcast.40), custom_call_target="tpu_custom_call" | custom-call | flops 6442450944 | bytes 8388608 | tf_op jit(solution)/shard_map/pallas_call | solution.py:82
  76.4 2.9 %collective-permute-done.9.refs_4_ = bf16[192,2048]{1,0:T(8,128)(2,1)S(1)} collective-permute-done((bf16[192,2048]{1,0:T(8,128)(2,1)S(1)}, bf16[192,2048]{1,0:T(8,128)(2,1)S(1)}, u32[]{:S(2)}, u32[]{:S(2)}) %collective-permute-start.9) | collective-permute-done | bytes 786464 | tf_op jit(solution)/shard_map/ppermute | solution.py:226
  82.2 1.9 %collective-permute-done.10.refs_3_ = bf16[192,2048]{1,0:T(8,128)(2,1)S(1)} collective-permute-done((bf16[192,2048]{1,0:T(8,128)(2,1)S(1)}, bf16[192,2048]{1,0:T(8,128)(2,1)S(1)}, u32[]{:S(2)}, u32[]{:S(2)}) %collective-permute-start.10) | collective-permute-done | bytes 786464 | tf_op jit(solution)/shard_map/ppermute | solution.py:369
  84.6 2.5 %collective-permute-start.11 = (f32[2,192]{1,0:T(2,128)S(1)}, f32[2,192]{1,0:T(2,128)S(1)}, u32[]{:S(2)}, u32[]{:S(2)}) collective-permute-start(f32[2,192]{1,0:T(2,128)S(1)} %pad_maximum_fusion.3), channel_id=1, source_target_pairs={{0,4},{4,0},{8,12},{12,8},{1,5},{5,1},{9,13},{13,9},{2,6},{6,2},{1... | collective-permute-start | bytes 4616 | tf_op jit(solution)/shard_map/ppermute | solution.py:210
  87.9 2.6 %collective-permute-start.16 = (bf16[192,2048]{1,0:T(8,128)(2,1)S(1)}, bf16[192,2048]{1,0:T(8,128)(2,1)S(1)}, u32[]{:S(2)}, u32[]{:S(2)}) collective-permute-start(bf16[192,2048]{1,0:T(8,128)(2,1)S(1)} %get-tuple-element.76), channel_id=1, source_target_pairs={{0,1},{1,0},{4,5},{5,4},{8,9},{9,8},{12,13},{13,12},{16,17},{17,16... | collective-permute-start | bytes 2359304 | tf_op jit(solution)/shard_map/ppermute | solution.py:216
  90.5 1.8 %collective-permute-start.12 = (f32[2,192]{1,0:T(2,128)S(1)}, f32[2,192]{1,0:T(2,128)S(1)}, u32[]{:S(2)}, u32[]{:S(2)}) collective-permute-start(f32[2,192]{1,0:T(2,128)S(1)} %fusion.46), channel_id=1, source_target_pairs={{0,8},{4,12},{8,0},{12,4},{1,9},{5,13},{9,1},{13,5},{2,10},{6,14},... | collective-permute-start | bytes 4616 | tf_op jit(solution)/shard_map/ppermute | solution.py:210
  92.7 2.3 %collective-permute-done.12 = f32[2,192]{1,0:T(2,128)S(1)} collective-permute-done((f32[2,192]{1,0:T(2,128)S(1)}, f32[2,192]{1,0:T(2,128)S(1)}, u32[]{:S(2)}, u32[]{:S(2)}) %collective-permute-start.12) | collective-permute-done | bytes 1568 | tf_op jit(solution)/shard_map/ppermute | solution.py:210
  96.5 4.0 %collective-permute-done.13 = bf16[192,256]{1,0:T(8,128)(2,1)S(1)} collective-permute-done((bf16[192,256]{1,0:T(8,128)(2,1)S(1)}, bf16[192,256]{1,0:T(8,128)(2,1)S(1)}, u32[]{:S(2)}, u32[]{:S(2)}) %collective-permute-start.13) | collective-permute-done | bytes 98336 | tf_op jit(solution)/shard_map/ppermute | solution.py:210
  100.6 1.8 %collective-permute-start.15 = (bf16[192,256]{1,0:T(8,128)(2,1)S(1)}, bf16[192,256]{1,0:T(8,128)(2,1)S(1)}, u32[]{:S(2)}, u32[]{:S(2)}) collective-permute-start(bf16[192,256]{1,0:T(8,128)(2,1)S(1)} %convert_element_type.146), channel_id=1, source_target_pairs={{0,8},{4,12},{8,0},{12,4},{1,9},{5,13},{9,1},{13,5},{2,10},{6,14},... | collective-permute-start | bytes 294920 | tf_op jit(solution)/shard_map/ppermute | solution.py:210
  102.4 6.2 %collective-permute-done.16 = bf16[192,2048]{1,0:T(8,128)(2,1)S(1)} collective-permute-done((bf16[192,2048]{1,0:T(8,128)(2,1)S(1)}, bf16[192,2048]{1,0:T(8,128)(2,1)S(1)}, u32[]{:S(2)}, u32[]{:S(2)}) %collective-permute-start.16) | collective-permute-done | bytes 786464 | tf_op jit(solution)/shard_map/ppermute | solution.py:216
  110.5 2.7 %collective-permute-start.17 = (bf16[192,2048]{1,0:T(8,128)(2,1)}, bf16[192,2048]{1,0:T(8,128)(2,1)S(1)}, u32[]{:S(2)}, u32[]{:S(2)}) collective-permute-start(bf16[192,2048]{1,0:T(8,128)(2,1)} %broadcast_select_fusion.1), channel_id=1, source_target_pairs={{0,2},{2,0},{1,3},{3,1},{4,6},{6,4},{5,7},{7,5},{8,10},{10,8},{9,1... | collective-permute-start | bytes 2359304 | tf_op jit(solution)/shard_map/ppermute | solution.py:402
  117.4 7.3 %collective-permute-done.18.refs_9_ = bf16[192,640]{1,0:T(8,128)(2,1)S(1)} collective-permute-done((bf16[192,640]{1,0:T(8,128)(2,1)S(1)}, bf16[192,640]{1,0:T(8,128)(2,1)S(1)}, u32[]{:S(2)}, u32[]{:S(2)}) %collective-permute-start.18) | collective-permute-done | bytes 245792 | tf_op jit(solution)/shard_map/ppermute | solution.py:216
  124.6 6.0 %shard_map.99 = (f32[2048,256]{1,0:T(8,128)}, f32[256,2048]{1,0:T(8,128)}) custom-call(s32[2]{0:T(128)S(1)} %pad_add_fusion.table, f32[1,2048]{1,0:T(1,128)S(1)} %copy-done.6, bf16[192,2048]{1,0:T(8,128)(2,1)} %fusion.27.refs_0_, bf16[192,2048]{1,0:T(8,128)(2,1)} %collective-permute-done.4.refs_1_, bf16[192,2048]{1,0:T(8,128)(2,1)S(1)} %copy-done.1, ...), custom_call_target="tpu_custom_call" | custom-call | flops 805306368 | bytes 10485760 | tf_op jit(solution)/shard_map/pallas_call | solution.py:151
  (96 shorter events, 22.8 us)
Async XLA Ops:
  0.6 5.4 %copy-start = (bf16[1,256,2048]{2,1,0:T(8,128)(2,1)S(1)}, bf16[1,256,2048]{2,1,0:T(8,128)(2,1)}, u32[]{:S(2)}) copy-start(bf16[1,256,2048]{2,1,0:T(8,128)(2,1)} %param.13) | copy-start | bytes 3145732
  9.9 13.8 %collective-permute-start.1 = (bf16[192,2432]{1,0:T(8,128)(2,1)}, bf16[192,2432]{1,0:T(8,128)(2,1)}, u32[]{:S(2)}, u32[]{:S(2)}) collective-permute-start(bf16[192,2432]{1,0:T(8,128)(2,1)} %pad_maximum_fusion.value_ref), channel_id=1, source_target_pairs={{2,6},{6,10},{10,14},{3,7},{7,11},{11,15},{18,22},{22,26},{26,30},... | collective-permute-start | bytes 2801672 | tf_op jit(solution)/shard_map/ppermute | solution.py:272
  11.5 12.2 %collective-permute-start = (bf16[192,2432]{1,0:T(8,128)(2,1)}, bf16[192,2432]{1,0:T(8,128)(2,1)}, u32[]{:S(2)}, u32[]{:S(2)}) collective-permute-start(bf16[192,2432]{1,0:T(8,128)(2,1)} %pad_maximum_fusion.value_ref), channel_id=1, source_target_pairs={{6,2},{10,6},{14,10},{7,3},{11,7},{15,11},{22,18},{26,22},{30,26},... | collective-permute-start | bytes 2801672 | tf_op jit(solution)/shard_map/ppermute | solution.py:272
  13.2 10.3 %copy-start.16 = (f32[4]{0:T(128)S(1)}, f32[4]{0:T(128)}, u32[]{:S(2)}) copy-start(f32[4]{0:T(128)} %param.14) | copy-start | bytes 52
  20.5 34.4 %collective-permute-start.4 = (bf16[192,2048]{1,0:T(8,128)(2,1)}, bf16[192,2048]{1,0:T(8,128)(2,1)}, u32[]{:S(2)}, u32[]{:S(2)}) collective-permute-start(bf16[192,2048]{1,0:T(8,128)(2,1)} %fusion.27.refs_0_), channel_id=1, source_target_pairs={{0,1},{1,0},{2,3},{3,2},{4,5},{5,4},{6,7},{7,6},{8,9},{9,8},{10,11... | collective-permute-start | bytes 2359304 | tf_op jit(solution)/shard_map/ppermute | solution.py:216
  25.5 13.6 %collective-permute-start.3 = (bf16[192,2432]{1,0:T(8,128)(2,1)S(1)}, bf16[192,2432]{1,0:T(8,128)(2,1)S(1)}, u32[]{:S(2)}, u32[]{:S(2)}) collective-permute-start(bf16[192,2432]{1,0:T(8,128)(2,1)S(1)} %get-tuple-element.71), channel_id=1, source_target_pairs={{12,8},{6,2},{10,6},{13,9},{7,3},{11,7},{28,24},{22,18},{26,22},{2... | collective-permute-start | bytes 2801672 | tf_op jit(solution)/shard_map/ppermute | solution.py:272
  26.2 14.6 %collective-permute-start.2 = (bf16[192,2432]{1,0:T(8,128)(2,1)S(1)}, bf16[192,2432]{1,0:T(8,128)(2,1)S(1)}, u32[]{:S(2)}, u32[]{:S(2)}) collective-permute-start(bf16[192,2432]{1,0:T(8,128)(2,1)S(1)} %get-tuple-element.72), channel_id=1, source_target_pairs={{0,4},{6,10},{10,14},{1,5},{7,11},{11,15},{16,20},{22,26},{26,30},... | collective-permute-start | bytes 2801672 | tf_op jit(solution)/shard_map/ppermute | solution.py:272
  39.2 26.1 %copy-start.7 = (bf16[192,2432]{1,0:T(8,128)(2,1)}, bf16[192,2432]{1,0:T(8,128)(2,1)S(1)}, u32[]{:S(2)}) copy-start(bf16[192,2432]{1,0:T(8,128)(2,1)S(1)} %collective-permute-done.3) | copy-start | bytes 2801668
  40.8 24.5 %copy-start.8 = (bf16[192,2432]{1,0:T(8,128)(2,1)}, bf16[192,2432]{1,0:T(8,128)(2,1)S(1)}, u32[]{:S(2)}) copy-start(bf16[192,2432]{1,0:T(8,128)(2,1)S(1)} %collective-permute-done.2) | copy-start | bytes 2801668
  41.5 13.4 %collective-permute-start.6 = (bf16[192,2432]{1,0:T(8,128)(2,1)S(1)}, bf16[192,2432]{1,0:T(8,128)(2,1)S(1)}, u32[]{:S(2)}, u32[]{:S(2)}) collective-permute-start(bf16[192,2432]{1,0:T(8,128)(2,1)S(1)} %get-tuple-element.65), channel_id=1, source_target_pairs={{8,4},{12,8},{6,2},{9,5},{13,9},{7,3},{24,20},{28,24},{22,18},{25,... | collective-permute-start | bytes 2801672 | tf_op jit(solution)/shard_map/ppermute | solution.py:272
  42.2 16.0 %collective-permute-start.5 = (bf16[192,2432]{1,0:T(8,128)(2,1)S(1)}, bf16[192,2432]{1,0:T(8,128)(2,1)S(1)}, u32[]{:S(2)}, u32[]{:S(2)}) collective-permute-start(bf16[192,2432]{1,0:T(8,128)(2,1)S(1)} %get-tuple-element.66), channel_id=1, source_target_pairs={{0,4},{4,8},{10,14},{1,5},{5,9},{11,15},{16,20},{20,24},{26,30},{1... | collective-permute-start | bytes 2801672 | tf_op jit(solution)/shard_map/ppermute | solution.py:272
  58.7 20.5 %collective-permute-start.8 = (bf16[192,2432]{1,0:T(8,128)(2,1)S(1)}, bf16[192,2432]{1,0:T(8,128)(2,1)S(1)}, u32[]{:S(2)}, u32[]{:S(2)}) collective-permute-start(bf16[192,2432]{1,0:T(8,128)(2,1)S(1)} %get-tuple-element.69), channel_id=1, source_target_pairs={{4,0},{8,4},{12,8},{5,1},{9,5},{13,9},{20,16},{24,20},{28,24},{21,... | collective-permute-start | bytes 2801672 | tf_op jit(solution)/shard_map/ppermute | solution.py:272
  60.0 19.2 %collective-permute-start.7 = (bf16[192,2432]{1,0:T(8,128)(2,1)S(1)}, bf16[192,2432]{1,0:T(8,128)(2,1)S(1)}, u32[]{:S(2)}, u32[]{:S(2)}) collective-permute-start(bf16[192,2432]{1,0:T(8,128)(2,1)S(1)} %get-tuple-element.70), channel_id=1, source_target_pairs={{0,4},{4,8},{8,12},{1,5},{5,9},{9,13},{16,20},{20,24},{24,28},{17,... | collective-permute-start | bytes 2801672 | tf_op jit(solution)/shard_map/ppermute | solution.py:272
  66.8 6.3 %slice-start = ((bf16[192,2432]{1,0:T(8,128)(2,1)}), bf16[192,384]{1,0:T(8,128)(2,1)S(1)}, s32[]{:S(2)}) async-start(bf16[192,2432]{1,0:T(8,128)(2,1)} %copy-done.7), calls=%async_computation | async-start | bytes 294912 | tf_op jit(solution)/shard_map/slice | solution.py:346
  66.8 6.3 %slice-start.1 = ((bf16[192,2432]{1,0:T(8,128)(2,1)}), bf16[192,384]{1,0:T(8,128)(2,1)S(1)}, s32[]{:S(2)}) async-start(bf16[192,2432]{1,0:T(8,128)(2,1)} %copy-done.8), calls=%async_computation.1 | async-start | bytes 294912 | tf_op jit(solution)/shard_map/slice | solution.py:346
  66.8 6.3 %copy-start.15 = (s32[192]{0:T(256)S(1)}, s32[192]{0:T(256)}, u32[]{:S(2)}) copy-start(s32[192]{0:T(256)} %param.15) | copy-start | bytes 2308
  66.8 6.4 %copy-start.6 = (f32[1,2048]{1,0:T(1,128)S(1)}, f32[1,2048]{1,0:T(1,128)}, u32[]{:S(2)}) copy-start(f32[1,2048]{1,0:T(1,128)} %gain_ref.1) | copy-start | bytes 24580
  74.9 4.3 %collective-permute-start.9 = (bf16[192,2048]{1,0:T(8,128)(2,1)S(1)}, bf16[192,2048]{1,0:T(8,128)(2,1)S(1)}, u32[]{:S(2)}, u32[]{:S(2)}) collective-permute-start(bf16[192,2048]{1,0:T(8,128)(2,1)S(1)} %fusion.4), channel_id=1, source_target_pairs={{2,0},{3,1},{6,4},{7,5},{10,8},{11,9},{14,12},{15,13},{18,16},{19,... | collective-permute-start | bytes 2359304 | tf_op jit(solution)/shard_map/ppermute | solution.py:226
  80.7 3.4 %collective-permute-start.10 = (bf16[192,2048]{1,0:T(8,128)(2,1)S(1)}, bf16[192,2048]{1,0:T(8,128)(2,1)S(1)}, u32[]{:S(2)}, u32[]{:S(2)}) collective-permute-start(bf16[192,2048]{1,0:T(8,128)(2,1)S(1)} %get-tuple-element.75), channel_id=1, source_target_pairs={{0,2},{2,0},{1,3},{3,1},{4,6},{6,4},{5,7},{7,5},{8,10},{10,8},{9,1... | collective-permute-start | bytes 2359304 | tf_op jit(solution)/shard_map/ppermute | solution.py:369
  84.1 8.6 %copy-start.2 = (bf16[192,2048]{1,0:T(8,128)(2,1)}, bf16[192,2048]{1,0:T(8,128)(2,1)S(1)}, u32[]{:S(2)}) copy-start(bf16[192,2048]{1,0:T(8,128)(2,1)S(1)} %collective-permute-done.10.refs_3_) | copy-start | bytes 2359300
  84.6 11.2 %copy-start.4 = (bf16[192,2048]{1,0:T(8,128)(2,1)}, bf16[192,2048]{1,0:T(8,128)(2,1)S(1)}, u32[]{:S(2)}) copy-start(bf16[192,2048]{1,0:T(8,128)(2,1)S(1)} %get-tuple-element.64.refs_6_) | copy-start | bytes 2359300
  84.6 10.5 %copy-start.1 = (bf16[192,2048]{1,0:T(8,128)(2,1)S(1)}, bf16[192,2048]{1,0:T(8,128)(2,1)}, u32[]{:S(2)}) copy-start(bf16[192,2048]{1,0:T(8,128)(2,1)} %refs_2_.1) | copy-start | bytes 2359300
  84.6 5.9 %collective-permute-start.11 = (f32[2,192]{1,0:T(2,128)S(1)}, f32[2,192]{1,0:T(2,128)S(1)}, u32[]{:S(2)}, u32[]{:S(2)}) collective-permute-start(f32[2,192]{1,0:T(2,128)S(1)} %pad_maximum_fusion.3), channel_id=1, source_target_pairs={{0,4},{4,0},{8,12},{12,8},{1,5},{5,1},{9,13},{13,9},{2,6},{6,2},{1... | collective-permute-start | bytes 4616 | tf_op jit(solution)/shard_map/ppermute | solution.py:210
  87.1 13.4 %collective-permute-start.14 = (bf16[192,2048]{1,0:T(8,128)(2,1)S(1)}, bf16[192,2048]{1,0:T(8,128)(2,1)S(1)}, u32[]{:S(2)}, u32[]{:S(2)}) collective-permute-start(bf16[192,2048]{1,0:T(8,128)(2,1)S(1)} %fusion.4), channel_id=1, source_target_pairs={{2,3},{3,2},{6,7},{7,6},{10,11},{11,10},{14,15},{15,14},{18,19},{1... | collective-permute-start | bytes 2359304 | tf_op jit(solution)/shard_map/ppermute | solution.py:216
  87.9 20.7 %collective-permute-start.16 = (bf16[192,2048]{1,0:T(8,128)(2,1)S(1)}, bf16[192,2048]{1,0:T(8,128)(2,1)S(1)}, u32[]{:S(2)}, u32[]{:S(2)}) collective-permute-start(bf16[192,2048]{1,0:T(8,128)(2,1)S(1)} %get-tuple-element.76), channel_id=1, source_target_pairs={{0,1},{1,0},{4,5},{5,4},{8,9},{9,8},{12,13},{13,12},{16,17},{17,16... | collective-permute-start | bytes 2359304 | tf_op jit(solution)/shard_map/ppermute | solution.py:216
  90.5 4.5 %collective-permute-start.12 = (f32[2,192]{1,0:T(2,128)S(1)}, f32[2,192]{1,0:T(2,128)S(1)}, u32[]{:S(2)}, u32[]{:S(2)}) collective-permute-start(f32[2,192]{1,0:T(2,128)S(1)} %fusion.46), channel_id=1, source_target_pairs={{0,8},{4,12},{8,0},{12,4},{1,9},{5,13},{9,1},{13,5},{2,10},{6,14},... | collective-permute-start | bytes 4616 | tf_op jit(solution)/shard_map/ppermute | solution.py:210
  95.8 4.7 %collective-permute-start.13 = (bf16[192,256]{1,0:T(8,128)(2,1)S(1)}, bf16[192,256]{1,0:T(8,128)(2,1)S(1)}, u32[]{:S(2)}, u32[]{:S(2)}) collective-permute-start(bf16[192,256]{1,0:T(8,128)(2,1)S(1)} %get-tuple-element.77), channel_id=1, source_target_pairs={{0,4},{4,0},{8,12},{12,8},{1,5},{5,1},{9,13},{13,9},{2,6},{6,2},{1... | collective-permute-start | bytes 294920 | tf_op jit(solution)/shard_map/ppermute | solution.py:210
  100.6 9.1 %collective-permute-start.15 = (bf16[192,256]{1,0:T(8,128)(2,1)S(1)}, bf16[192,256]{1,0:T(8,128)(2,1)S(1)}, u32[]{:S(2)}, u32[]{:S(2)}) collective-permute-start(bf16[192,256]{1,0:T(8,128)(2,1)S(1)} %convert_element_type.146), channel_id=1, source_target_pairs={{0,8},{4,12},{8,0},{12,4},{1,9},{5,13},{9,1},{13,5},{2,10},{6,14},... | collective-permute-start | bytes 294920 | tf_op jit(solution)/shard_map/ppermute | solution.py:210
  110.5 6.8 %collective-permute-start.17 = (bf16[192,2048]{1,0:T(8,128)(2,1)}, bf16[192,2048]{1,0:T(8,128)(2,1)S(1)}, u32[]{:S(2)}, u32[]{:S(2)}) collective-permute-start(bf16[192,2048]{1,0:T(8,128)(2,1)} %broadcast_select_fusion.1), channel_id=1, source_target_pairs={{0,2},{2,0},{1,3},{3,1},{4,6},{6,4},{5,7},{7,5},{8,10},{10,8},{9,1... | collective-permute-start | bytes 2359304 | tf_op jit(solution)/shard_map/ppermute | solution.py:402
  115.1 9.6 %copy-start.3 = (bf16[192,2048]{1,0:T(8,128)(2,1)S(1)}, bf16[192,2048]{1,0:T(8,128)(2,1)}, u32[]{:S(2)}) copy-start(bf16[192,2048]{1,0:T(8,128)(2,1)} %copy-done.2) | copy-start | bytes 2359300
  115.1 9.6 %copy-start.5 = (bf16[192,2048]{1,0:T(8,128)(2,1)S(1)}, bf16[192,2048]{1,0:T(8,128)(2,1)}, u32[]{:S(2)}) copy-start(bf16[192,2048]{1,0:T(8,128)(2,1)} %copy-done.4) | copy-start | bytes 2359300
  116.7 8.0 %collective-permute-start.18 = (bf16[192,640]{1,0:T(8,128)(2,1)S(1)}, bf16[192,640]{1,0:T(8,128)(2,1)S(1)}, u32[]{:S(2)}, u32[]{:S(2)}) collective-permute-start(bf16[192,640]{1,0:T(8,128)(2,1)S(1)} %pad_maximum_fusion.2.refs_8_), channel_id=1, source_target_pairs={{0,1},{1,0},{2,3},{3,2},{4,5},{5,4},{6,7},{7,6},{8,9},{9,8},{10,11... | collective-permute-start | bytes 737288 | tf_op jit(solution)/shard_map/ppermute | solution.py:216
  (6 other events, 15.5 us)

commit v7 on v6

--- a/solution.py
+++ b/solution.py
@@ -29,9 +29,7 @@
     return found
 
 
-def block_kernel(
-    table, value_ref, riding_ref, weight_ref, out_ref, wide, tall, arrived, *, blocks, tile, tiles
-):
+def block_kernel(table, value_ref, weight_ref, out_ref, wide, tall, arrived, *, blocks, tile, tiles):
     section = table[0]
     block = look_up(table[1], blocks)
     step = pl.program_id(0)
@@ -45,11 +43,6 @@
         rows = pl.ds(pl.multiple_of(index * tile, tile), tile)
         return pltpu.make_async_copy(weight_ref.at[rows, whole], tall.at[index], arrived.at[index])
 
-    @pl.when(step == 0)
-    def _():
-        out_ref[:, width:] = riding_ref[...]
-
-    columns = pl.ds(pl.multiple_of(step * tile, tile), tile)
     for number, is_wide in ((0, True), (1, False)):
 
         @pl.when(section == number)
@@ -65,18 +58,15 @@
 
             copy_of(step, is_wide).wait()
             if is_wide:
-                out_ref[:, columns] = jnp.dot(
-                    value_ref[:, :width], wide[step], preferred_element_type=F32
+                out_ref[...] = jnp.dot(value_ref[...], wide[step], preferred_element_type=F32)
+            else:
+                out_ref[...] = lax.dot_general(
+                    value_ref[...], tall[step], CONTRACT_LAST, preferred_element_type=F32
                 )
-            else:
-                out_ref[:, columns] = lax.dot_general(
-                    value_ref[:, :width], tall[step], CONTRACT_LAST, preferred_element_type=F32
-                )
-
-
-def block_product(table, value, riding, weight, blocks):
-    rows, columns = value.shape
-    width = columns - riding.shape[1]
+
+
+def block_product(table, value, weight, blocks):
+    rows, width = value.shape
     tile = min(256, width)
     tiles = width // tile
     return pl.pallas_call(
@@ -85,23 +75,22 @@
             num_scalar_prefetch=1,
             grid=(tiles,),
             in_specs=[
-                pl.BlockSpec(value.shape, lambda step, table: (0, 0)),
-                pl.BlockSpec(riding.shape, lambda step, table: (0, 0)),
+                pl.BlockSpec((rows, width), lambda step, table: (0, 0)),
                 pl.BlockSpec(memory_space=pl.ANY),
             ],
-            out_specs=pl.BlockSpec(value.shape, lambda step, table: (0, 0)),
+            out_specs=pl.BlockSpec((rows, tile), lambda step, table: (0, step)),
             scratch_shapes=[
                 pltpu.VMEM((tiles, width, tile), BF16),
                 pltpu.VMEM((tiles, tile, width), BF16),
                 pltpu.SemaphoreType.DMA((tiles,)),
             ],
         ),
-        out_shape=jax.ShapeDtypeStruct(value.shape, F32),
-        compiler_params=pltpu.CompilerParams(vmem_limit_bytes=28 * 1024 * 1024),
+        out_shape=jax.ShapeDtypeStruct((rows, width), F32),
+        compiler_params=pltpu.CompilerParams(vmem_limit_bytes=24 * 1024 * 1024),
         cost_estimate=pl.CostEstimate(
             flops=8 * rows * width * width, bytes_accessed=2 * width * width, transcendentals=0
         ),
-    )(table, value, riding, weight)
+    )(table, value, weight)
 
 
 def gradient_kernel(table, gain_ref, *refs, replicas):
@@ -273,28 +262,26 @@
 
     token_float = tokens.astype(F32)
     early = jnp.where(is_first, (token_float * gain_row).astype(BF16), cotangent)
-    riding = jnp.concatenate(
-        [
-            jnp.where(is_first, times_down(early), times_up_transposed(early)),
-            jnp.broadcast_to(jnp.sum(token_float * token_float, axis=1, keepdims=True), (rows, 128)),
-        ],
-        axis=1,
-    )
-    first = jnp.concatenate([early, riding.astype(BF16)], axis=1)
-    early, riding, first = lax.optimization_barrier((early, riding, first))
+    early = lax.optimization_barrier(early)
+    small = jnp.where(is_first, times_down(early), times_up_transposed(early)).astype(BF16)
+    squares = jnp.sum(token_float * token_float, axis=1).astype(BF16)
+    squares = jnp.pad(squares, (0, -rows % ranks)).reshape(-1, ranks)
+    small = jnp.concatenate([small, jnp.pad(squares, ((0, 15), (0, 0)))], axis=0)
+    small_all = lax.all_gather(small, "tensor")
+    early_all = lax.all_gather(early, "replica")
 
     everyone = range(count)
     arrivals = [
         (
-            line(first, [], [z for z in everyone if z + 1 < count], 1),
-            line(first, [], [z for z in everyone if z > 0], -1),
+            line(cotangent, [], [z for z in everyone if z + 1 < count], 1),
+            line(cotangent, [], [z for z in everyone if z > 0], -1),
         )
     ]
     parts = []
     for stage in range(count):
         wanted = [None if stage == 0 else second_slots[z][stage] for z in everyone]
         cases = sorted({slot for slot in wanted if slot is not None})
-        here = [first] + [arrivals[slot][side] for slot, side in cases]
+        here = [early] + [arrivals[slot][side] for slot, side in cases]
         if stage > 0:
             here = lax.optimization_barrier((*here, *sent))[: len(here)]
         value = pick(
@@ -303,12 +290,7 @@
             here,
         )
         order = [blocks[stage] for blocks in first_order + second_order]
-        part = block_product(table, value, riding, weight, order)
-        if stage == 0:
-            part, after = lax.optimization_barrier((part, early))
-            early_all = [early] + with_other_replicas(after)[1:]
-        if stage == 2:
-            part, *early_all = lax.optimization_barrier((part, *early_all))
+        part = block_product(table, value, weight, order)
         parts.append(part)
         slot = stage + 1
         if slot == count:
@@ -342,28 +324,32 @@
         )
     from_left, from_right = arrivals[-1]
 
-    passed = sum(
-        (arrived[:, width:].astype(F32) for pair in arrivals[:-1] for arrived in pair), riding
-    )
-
-    def small_factor(rank_sum):
-        return (coefficients * rank_sum).astype(BF16)
-
-    small_second = small_factor(passed[:, :ranks])
-
-    pulled = sum(part[:, :width] for part in parts) + lax.dot_general(
-        small_second, down, CONTRACT_LAST, preferred_element_type=F32
-    )
-    pulled = (gain_row * pulled).astype(BF16)
-    pulled_others = with_other_replicas(pulled, (1,))[1:]
-    pulled = to_other_core(pulled, 1)
-    from_left, from_right, pulled = lax.optimization_barrier((from_left, from_right, pulled))
-
-    summed = parts[-1] + from_left.astype(F32) + from_right.astype(F32)
-    small_first = small_factor(summed[:, width : width + ranks])
-    inv_first = lax.rsqrt(summed[:, width + ranks : width + ranks + 1] / features + EPSILON)
-    projected = summed[:, :width] + jnp.dot(small_first, up, preferred_element_type=F32)
+    small_all, early_all, _ = lax.optimization_barrier(
+        (small_all, early_all, arrivals[max(count - 2, 0)])
+    )
+    replica, replicas = lax.axis_index("replica"), lax.axis_size("replica")
+    early_all = [early] + [
+        lax.dynamic_index_in_dim(early_all, lax.rem(replica + replicas - step, replicas), 0, False)
+        for step in range(1, replicas)
+    ]
+    small_sum = jnp.sum(small_all.astype(F32), axis=0)
+    inv_first = lax.rsqrt(
+        small_sum[rows:].reshape(-1)[:rows][:, None] / features + EPSILON
+    )
+    small_early = (coefficients * small_sum[:rows]).astype(BF16)
+    low_product = jnp.where(
+        is_first,
+        jnp.dot(small_early, up, preferred_element_type=F32),
+        lax.dot_general(small_early, down, CONTRACT_LAST, preferred_element_type=F32),
+    )
+
+    pulled_here = (gain_row * (sum(parts) + low_product)).astype(BF16)
+    pulled = to_other_core(pulled_here, 1)
+    from_left, from_right, _ = lax.optimization_barrier((from_left, from_right, pulled_here))
+
+    projected = parts[-1] + from_left.astype(F32) + from_right.astype(F32) + low_product
     hidden = (token_float + inv_first * projected).astype(BF16)
+    late_others = with_other_replicas(jnp.where(is_first, hidden, pulled_here))[1:]
     swap = [(0, 1), (1, 0)]
     swapped = [
         lax.ppermute(jnp.where(is_first, hidden, other), "section", swap) for other in early_all[1:]
@@ -371,8 +357,6 @@
     hidden_on_second = swapped[0] if swapped else to_other_core(hidden, 0)
     cotangent_all = [cotangent] + swapped
     hidden_here = jnp.where(is_first, hidden, hidden_on_second)
-    small_early = jnp.where(is_first, small_first, small_second)
-    hidden_others = with_other_replicas(hidden, (0,))[1:]
     hidden_float = hidden_here.astype(F32)
     pulled_float = pulled.astype(F32)
     row_sums = jnp.stack(
@@ -388,20 +372,12 @@
         times_up_transposed(hidden_grad.astype(BF16)),
         times_down((hidden_float * gain_row).astype(BF16)),
     )
-    for at, step in enumerate(doubling_steps()):
+    for step in doubling_steps():
         rank_late = sum_step(rank_late, step)
-        if at == 0:
-            rank_late, *pulled_others = lax.optimization_barrier((rank_late, *pulled_others))
-
-    rank_late, *swapped = lax.optimization_barrier(
-        (
-            rank_late,
-            *[jnp.where(is_first, *pair) for pair in zip(hidden_others, pulled_others)],
-        )
-    )
-    swapped = [lax.ppermute(other, "section", swap) for other in swapped]
+
+    swapped = [lax.ppermute(other, "section", swap) for other in late_others]
     hidden_all = [hidden_here] + [
-        jnp.where(is_first, *pair) for pair in zip(hidden_others, swapped)
+        jnp.where(is_first, *pair) for pair in zip(late_others, swapped)
     ]
     pulled_all = [pulled] + swapped
 

time: 132 us -> 152 us (1.15)
  blocking collectives: 0 us -> 18.1 us
  between operations: 1.19 us -> 14.5 us
  other arithmetic: 19.8 us -> 12.1 us
  starting transfers between devices: 39 us -> 33.6 us
  waiting for transfers between devices: 29.6 us -> 34.9 us
  Pallas kernels: 31.8 us -> 29.6 us
    all_gather x0 -> x1, blocking collectives: none -> 18.1 us  [on_device(): small_all = lax.all_gather(small, 'tensor')]
    ppermute x4, waiting for transfers between devices: 6.36 us -> 11.5 us  [sum_step(): return value + lax.ppermute(value.astype(wire), 'tensor', pairs).astype(F32)]
    select_n x3, other arithmetic: 4.39 us -> 0.65 us  [pick(): chosen = jnp.where(is_one_of(number, members), cases[at], chosen)]
    ppermute x4 -> x2, starting transfers between devices: 6.93 us -> 3.21 us  [with_other_replicas(): lax.ppermute(value, ('section', 'replica'), [(s * count + r, s * count +...]
    ppermute x4 -> x2, waiting for transfers between devices: 13.5 us -> 16.8 us  [with_other_replicas(): lax.ppermute(value, ('section', 'replica'), [(s * count + r, s * count +...]
    ppermute x1, waiting for transfers between devices: 2.88 us -> 0.01 us  [to_other_core(): return lax.ppermute(value, 'section', [(source, 1 - source)])]
    dot_general x2, matrix products: 1.34 us -> 4.1 us  [the longest x1 2.33 us: on_device(): lax.dot_general(small_early, down, CONTRACT_LAST, preferred_element_type=...]
    ppermute x1, starting transfers between devices: 2.74 us -> 0.01 us  [on_device(): swapped = [lax.ppermute(other, 'section', swap) for other in late_others]]
  transfers between devices with their start and end apart: 19 -> 18, of which waited for: 8 -> 7; matrix products, arithmetic and copies ran while one was open for 12% -> 12% of each run, Pallas kernels for 20% -> 16%
where the time goes in v7:
time: 152 us; the launch traced here: 151 us
  waiting for transfers between devices  34.9 us (23%)
  starting transfers between devices  33.6 us (22%)
  Pallas kernels  29.6 us (19%)
  blocking collectives  18.1 us (12%)
  between operations  14.5 us (10%)
  other arithmetic  12.1 us (8%)
  matrix products  6.06 us (4%)
  local copies, waits for them, and re-layouts  2.41 us (2%)
    pallas_call x4, Pallas kernels, block_product(): pl.pallas_call(functools.partial(block_kernel, blocks=blocks, tile=tile,...  24.7 us
    ppermute x8, starting transfers between devices, line(): return lax.ppermute(value, ('tensor', 'section'), pairs)  22.2 us
    all_gather x1, blocking collectives, on_device(): small_all = lax.all_gather(small, 'tensor')  18.1 us
    ppermute x2, waiting for transfers between devices, with_other_replicas(): lax.ppermute(value, ('section', 'replica'), [(s * count + r, s * count +...  16.8 us
    ppermute x4, waiting for transfers between devices, sum_step(): return value + lax.ppermute(value.astype(wire), 'tensor', pairs).astype(F32)  11.5 us
    ppermute x4, starting transfers between devices, sum_step(): return value + lax.ppermute(value.astype(wire), 'tensor', pairs).astype(F32)  5.53 us
    pallas_call x1, Pallas kernels, gradients(): pl.pallas_call(functools.partial(gradient_kernel, replicas=replicas), gri...  4.88 us
    ppermute x8, waiting for transfers between devices, line(): return lax.ppermute(value, ('tensor', 'section'), pairs)  4.68 us
  transfers between devices with their start and end apart: 18, of which 7 were waited for; matrix products, arithmetic and copies ran while one was open for 12% of the time, Pallas kernels for 16%

profile of v7, /device:TPU:0, one launch (start us, length us, event | category | flops | bytes accessed | tf_op | source)
XLA Modules:
  0.0 151.3 jit_solution(11073463469064858201)
XLA Ops:
  7.2 1.7 %collective-permute-start.2 = (bf16[192,2048]{1,0:T(8,128)(2,1)}, bf16[192,2048]{1,0:T(8,128)(2,1)}, u32[]{:S(2)}, u32[]{:S(2)}) collective-permute-start(bf16[192,2048]{1,0:T(8,128)(2,1)} %refs_2_.1), channel_id=1, source_target_pairs={{6,2},{10,6},{14,10},{7,3},{11,7},{15,11},{22,18},{26,22},{30,26},... | collective-permute-start | bytes 2359304 | tf_op jit(solution)/shard_map/ppermute | solution.py:261
  8.9 1.6 %collective-permute-start = (bf16[192,2048]{1,0:T(8,128)(2,1)}, bf16[192,2048]{1,0:T(8,128)(2,1)}, u32[]{:S(2)}, u32[]{:S(2)}) collective-permute-start(bf16[192,2048]{1,0:T(8,128)(2,1)} %refs_2_.1), channel_id=1, source_target_pairs={{2,6},{6,10},{10,14},{3,7},{7,11},{11,15},{18,22},{22,26},{26,30},... | collective-permute-start | bytes 2359304 | tf_op jit(solution)/shard_map/ppermute | solution.py:261
  10.5 2.4 %fusion.24.value_ref.refs_0_ = bf16[192,2048]{1,0:T(8,128)(2,1)} fusion(bf16[192,2048]{1,0:T(8,128)(2,1)} %refs_2_.1, bf16[192,2048]{1,0:T(8,128)(2,1)} %param.8, f32[2048]{0:T(1024)} %bitcast.42, pred[]{:T(512)S(6)} %eq.20), kind=kLoop, calls=%fused_computation.39 | loop fusion | flops 1572864 | bytes 2367489 | tf_op jit(solution)/shard_map/jit(_where)/select_n | solution.py:264
  15.2 18.1 %all-gather = bf16[832,256]{1,0:T(8,128)(2,1)} all-gather(bf16[208,256]{1,0:T(8,128)(2,1)S(1)} %fusion.33), channel_id=2, replica_groups=mesh['groups'=2,'tensor'=4,'section'=2,'replica'=2] {'tensor'}, dimensions={0}, use_global_device_ids=true | all-gather | bytes 532480 | tf_op jit(solution)/shard_map/all_gather | solution.py:270
  33.2 6.2 %shard_map.95 = f32[192,2048]{1,0:T(8,128)S(1)} custom-call(s32[2]{0:T(128)S(1)} %pad_add_fusion.table, bf16[192,2048]{1,0:T(8,128)(2,1)S(1)} %copy-done.1, bf16[2048,8192]{1,0:T(8,128)(2,1)} %bitcast.45), custom_call_target="tpu_custom_call" | custom-call | flops 6442450944 | bytes 8388608 | tf_op jit(solution)/shard_map/pallas_call | solution.py:72
  39.5 1.8 %add_convert_fusion.4 = (bf16[192,2048]{1,0:T(8,128)(2,1)S(1)}, bf16[192,2048]{1,0:T(8,128)(2,1)S(1)}) fusion(bf16[192,2048]{1,0:T(8,128)(2,1)} %collective-permute-done.2, f32[192,2048]{1,0:T(8,128)S(1)} %shard_map.95, pred[]{:T(512)S(6)} %eq.20, bf16[192,2048]{1,0:T(8,128)(2,1)} %collective-permute-done), kind=kLoop, calls=%fused_computation.23 | loop fusion | flops 2752512 | bytes 4718593 | tf_op jit(solution)/shard_map/convert_element_type | solution.py:308
  41.3 3.5 %collective-permute-start.1 = (bf16[192,2048]{1,0:T(8,128)(2,1)S(1)}, bf16[192,2048]{1,0:T(8,128)(2,1)S(1)}, u32[]{:S(2)}, u32[]{:S(2)}) collective-permute-start(bf16[192,2048]{1,0:T(8,128)(2,1)S(1)} %get-tuple-element.52), channel_id=1, source_target_pairs={{0,4},{6,10},{10,14},{1,5},{7,11},{11,15},{16,20},{22,26},{26,30},... | collective-permute-start | bytes 2359304 | tf_op jit(solution)/shard_map/ppermute | solution.py:261
  45.7 6.2 %shard_map.96 = f32[192,2048]{1,0:T(8,128)S(1)} custom-call(s32[2]{0:T(128)S(1)} %pad_add_fusion.table, bf16[192,2048]{1,0:T(8,128)(2,1)S(1)} %select_select_fusion.2.value_ref, bf16[2048,8192]{1,0:T(8,128)(2,1)} %bitcast.46), custom_call_target="tpu_custom_call" | custom-call | flops 6442450944 | bytes 8388608 | tf_op jit(solution)/shard_map/pallas_call | solution.py:72
  51.8 2.4 %collective-permute-done.1 = bf16[192,2048]{1,0:T(8,128)(2,1)S(1)} collective-permute-done((bf16[192,2048]{1,0:T(8,128)(2,1)S(1)}, bf16[192,2048]{1,0:T(8,128)(2,1)S(1)}, u32[]{:S(2)}, u32[]{:S(2)}) %collective-permute-start.1) | collective-permute-done | bytes 786464 | tf_op jit(solution)/shard_map/ppermute | solution.py:261
  54.8 4.4 %collective-permute-start.3 = (bf16[192,2048]{1,0:T(8,128)(2,1)S(1)}, bf16[192,2048]{1,0:T(8,128)(2,1)S(1)}, u32[]{:S(2)}, u32[]{:S(2)}) collective-permute-start(bf16[192,2048]{1,0:T(8,128)(2,1)S(1)} %get-tuple-element.48), channel_id=1, source_target_pairs={{0,4},{4,8},{10,14},{1,5},{5,9},{11,15},{16,20},{20,24},{26,30},{1... | collective-permute-start | bytes 2359304 | tf_op jit(solution)/shard_map/ppermute | solution.py:261
  60.2 6.2 %shard_map.97 = f32[192,2048]{1,0:T(8,128)S(1)} custom-call(s32[2]{0:T(128)S(1)} %pad_add_fusion.table, bf16[192,2048]{1,0:T(8,128)(2,1)S(1)} %select_select_fusion.1.value_ref, bf16[2048,8192]{1,0:T(8,128)(2,1)} %bitcast.47), custom_call_target="tpu_custom_call" | custom-call | flops 6442450944 | bytes 8388608 | tf_op jit(solution)/shard_map/pallas_call | solution.py:72
  66.4 2.3 %collective-permute-done.3 = bf16[192,2048]{1,0:T(8,128)(2,1)S(1)} collective-permute-done((bf16[192,2048]{1,0:T(8,128)(2,1)S(1)}, bf16[192,2048]{1,0:T(8,128)(2,1)S(1)}, u32[]{:S(2)}, u32[]{:S(2)}) %collective-permute-start.3) | collective-permute-done | bytes 786464 | tf_op jit(solution)/shard_map/ppermute | solution.py:261
  68.7 1.8 %add_convert_fusion = (bf16[192,2048]{1,0:T(8,128)(2,1)}, bf16[192,2048]{1,0:T(8,128)(2,1)}) fusion(f32[192,2048]{1,0:T(8,128)S(1)} %shard_map.97, bf16[192,2048]{1,0:T(8,128)(2,1)S(1)} %collective-permute-done.5, pred[]{:T(512)S(6)} %eq.20, f32[192,2048]{1,0:T(8,128)S(1)} %shard_map.96, pred[]{:T(512)S(6)} %eq.21, ...), kind=kLoop, calls=%fused_computation.19 | loop fusion | flops 3538944 | bytes 6291458 | tf_op jit(solution)/shard_map/convert_element_type | solution.py:308
  70.5 8.3 %collective-permute-start.6 = (bf16[192,2048]{1,0:T(8,128)(2,1)}, bf16[192,2048]{1,0:T(8,128)(2,1)}, u32[]{:S(2)}, u32[]{:S(2)}) collective-permute-start(bf16[192,2048]{1,0:T(8,128)(2,1)} %get-tuple-element.50), channel_id=1, source_target_pairs={{0,4},{4,8},{8,12},{1,5},{5,9},{9,13},{16,20},{20,24},{24,28},{17,... | collective-permute-start | bytes 2359304 | tf_op jit(solution)/shard_map/ppermute | solution.py:261
  78.8 1.3 collective-permute-start.7
  80.4 6.2 %shard_map.98 = f32[192,2048]{1,0:T(8,128)S(1)} custom-call(s32[2]{0:T(128)S(1)} %pad_add_fusion.table, bf16[192,2048]{1,0:T(8,128)(2,1)S(1)} %select_select_fusion.value_ref, bf16[2048,8192]{1,0:T(8,128)(2,1)} %bitcast.48), custom_call_target="tpu_custom_call" | custom-call | flops 6442450944 | bytes 8388608 | tf_op jit(solution)/shard_map/pallas_call | solution.py:72
  87.7 1.2 convert_reduce_fusion
  88.9 1.8 %fusion.12 = f32[192,2048]{1,0:T(8,128)S(1)} fusion(bf16[1,256,2048]{2,1,0:T(8,128)(2,1)} %param.13, f32[208,256]{1,0:T(8,128)S(1)} %convert_reduce_fusion, f32[256]{0:T(256)S(1)} %broadcast_in_dim.48, s32[256]{0:T(256)S(1)} %and_select_fusion, s32[192]{0:T(256)S(1)} %copy-done.14), kind=kOutput, calls=%fused_computation.29 | convolution fusion | flops 201523200 | bytes 2821120 | tf_op jit(solution)/shard_map/dot_general | solution.py:342
  90.8 2.3 %multiply_convert_fusion = (bf16[192,2048]{1,0:T(8,128)(2,1)S(1)}, f32[192,2048]{1,0:T(8,128)S(1)}) fusion(f32[192,2048]{1,0:T(8,128)S(1)} %copy-done.5, f32[192,2048]{1,0:T(8,128)} %copy-done.6, f32[192,2048]{1,0:T(8,128)S(1)} %shard_map.95, f32[192,2048]{1,0:T(8,128)S(1)} %copy-done.3, f32[2048]{0:T(1024)S(1)} %bitcast.43, f32[192,2048]{1,0:T(8,128)S(1)} %fusion.12, ...), kind=kOutput, calls=%fused_computation.18 | convolution fusion | flops 204275712 | bytes 11480065 | tf_op jit(solution)/shard_map/dot_general | solution.py:343
  93.1 1.5 collective-permute-start.9
  94.6 2.3 %broadcast_select_fusion.2 = (bf16[192,2048]{1,0:T(8,128)(2,1)S(1)}, bf16[192,2048]{1,0:T(8,128)(2,1)S(1)}) fusion(bf16[192,2048]{1,0:T(8,128)(2,1)S(1)} %get-tuple-element.58, pred[]{:T(512)S(6)} %eq.20, f32[192,2048]{1,0:T(8,128)S(1)} %get-tuple-element.59, bf16[192,2048]{1,0:T(8,128)(2,1)} %collective-permute-done.7, f32[192,2048]{1,0:T(8,128)S(1)} %copy-done.5, ...), kind=kLoop, calls=%fused_computation.49 | loop fusion | flops 3932160 | bytes 7865089 | tf_op jit(solution)/shard_map/jit(_where)/select_n | solution.py:352
  97.1 1.2 collective-permute-start.8
  98.3 1.9 %collective-permute-done.8.refs_3_ = bf16[192,2048]{1,0:T(8,128)(2,1)S(1)} collective-permute-done((bf16[192,2048]{1,0:T(8,128)(2,1)S(1)}, bf16[192,2048]{1,0:T(8,128)(2,1)S(1)}, u32[]{:S(2)}, u32[]{:S(2)}) %collective-permute-start.8) | collective-permute-done | bytes 786464 | tf_op jit(solution)/shard_map/ppermute | solution.py:355
  100.8 2.7 %collective-permute-start.12 = (f32[2,192]{1,0:T(2,128)S(1)}, f32[2,192]{1,0:T(2,128)S(1)}, u32[]{:S(2)}, u32[]{:S(2)}) collective-permute-start(f32[2,192]{1,0:T(2,128)S(1)} %pad_maximum_fusion.1), channel_id=1, source_target_pairs={{0,4},{4,0},{8,12},{12,8},{1,5},{5,1},{9,13},{13,9},{2,6},{6,2},{1... | collective-permute-start | bytes 4616 | tf_op jit(solution)/shard_map/ppermute | solution.py:199
  103.5 1.6 %collective-permute-start.10 = (bf16[192,2048]{1,0:T(8,128)(2,1)S(1)}, bf16[192,2048]{1,0:T(8,128)(2,1)S(1)}, u32[]{:S(2)}, u32[]{:S(2)}) collective-permute-start(bf16[192,2048]{1,0:T(8,128)(2,1)S(1)} %get-tuple-element.43), channel_id=1, source_target_pairs={{0,1},{1,0},{2,3},{3,2},{4,5},{5,4},{6,7},{7,6},{8,9},{9,8},{10,11... | collective-permute-start | bytes 2359304 | tf_op jit(solution)/shard_map/ppermute | solution.py:205
  106.2 3.5 %collective-permute-done.13 = f32[2,192]{1,0:T(2,128)S(1)} collective-permute-done((f32[2,192]{1,0:T(2,128)S(1)}, f32[2,192]{1,0:T(2,128)S(1)}, u32[]{:S(2)}, u32[]{:S(2)}) %collective-permute-start.13) | collective-permute-done | bytes 1568 | tf_op jit(solution)/shard_map/ppermute | solution.py:199
  110.4 2.1 %collective-permute-start.14 = (bf16[192,256]{1,0:T(8,128)(2,1)S(1)}, bf16[192,256]{1,0:T(8,128)(2,1)S(1)}, u32[]{:S(2)}, u32[]{:S(2)}) collective-permute-start(bf16[192,256]{1,0:T(8,128)(2,1)S(1)} %get-tuple-element.60), channel_id=1, source_target_pairs={{0,4},{4,0},{8,12},{12,8},{1,5},{5,1},{9,13},{13,9},{2,6},{6,2},{1... | collective-permute-start | bytes 294920 | tf_op jit(solution)/shard_map/ppermute | solution.py:199
  112.5 10.5 %collective-permute-done.10 = bf16[192,2048]{1,0:T(8,128)(2,1)S(1)} collective-permute-done((bf16[192,2048]{1,0:T(8,128)(2,1)S(1)}, bf16[192,2048]{1,0:T(8,128)(2,1)S(1)}, u32[]{:S(2)}, u32[]{:S(2)}) %collective-permute-start.10) | collective-permute-done | bytes 786464 | tf_op jit(solution)/shard_map/ppermute | solution.py:205
  123.2 8.0 %collective-permute-done.15 = bf16[192,256]{1,0:T(8,128)(2,1)S(1)} collective-permute-done((bf16[192,256]{1,0:T(8,128)(2,1)S(1)}, bf16[192,256]{1,0:T(8,128)(2,1)S(1)}, u32[]{:S(2)}, u32[]{:S(2)}) %collective-permute-start.15) | collective-permute-done | bytes 98336 | tf_op jit(solution)/shard_map/ppermute | solution.py:199
  131.6 1.6 %collective-permute-start.16 = (bf16[192,640]{1,0:T(8,128)(2,1)S(1)}, bf16[192,640]{1,0:T(8,128)(2,1)S(1)}, u32[]{:S(2)}, u32[]{:S(2)}) collective-permute-start(bf16[192,640]{1,0:T(8,128)(2,1)S(1)} %pad_maximum_fusion.refs_8_), channel_id=1, source_target_pairs={{0,1},{1,0},{2,3},{3,2},{4,5},{5,4},{6,7},{7,6},{8,9},{9,8},{10,11... | collective-permute-start | bytes 737288 | tf_op jit(solution)/shard_map/ppermute | solution.py:205
  133.3 6.3 %collective-permute-done.16.refs_9_ = bf16[192,640]{1,0:T(8,128)(2,1)S(1)} collective-permute-done((bf16[192,640]{1,0:T(8,128)(2,1)S(1)}, bf16[192,640]{1,0:T(8,128)(2,1)S(1)}, u32[]{:S(2)}, u32[]{:S(2)}) %collective-permute-start.16) | collective-permute-done | bytes 245792 | tf_op jit(solution)/shard_map/ppermute | solution.py:205
  139.6 4.9 %shard_map.99 = (f32[2048,256]{1,0:T(8,128)}, f32[256,2048]{1,0:T(8,128)}) custom-call(s32[2]{0:T(128)S(1)} %pad_add_fusion.table, f32[1,2048]{1,0:T(1,128)S(1)} %copy-done.8, bf16[192,2048]{1,0:T(8,128)(2,1)S(1)} %copy-done.1, bf16[192,2048]{1,0:T(8,128)(2,1)S(1)} %get-tuple-element.46.refs_1_, bf16[192,2048]{1,0:T(8,128)(2,1)S(1)} %copy-done.7, ...), custom_call_target="tpu_custom_call" | custom-call | flops 805306368 | bytes 10485760 | tf_op jit(solution)/shard_map/pallas_call | solution.py:140
  (83 shorter events, 9.2 us)
Async XLA Ops:
  7.2 6.0 %copy-start = (bf16[1,2048,256]{2,1,0:T(8,128)(2,1)S(1)}, bf16[1,2048,256]{2,1,0:T(8,128)(2,1)}, u32[]{:S(2)}) copy-start(bf16[1,2048,256]{2,1,0:T(8,128)(2,1)} %param.12) | copy-start | bytes 3145732
  7.2 80.5 %all-gather.4.cloned.1.call-start = ((), (), s32[]{:S(2)}) async-start(), calls=%async_computation | async-start | bytes 2359296 | tf_op jit(solution)/shard_map/all_gather | solution.py:271
  7.2 32.2 %collective-permute-start.2 = (bf16[192,2048]{1,0:T(8,128)(2,1)}, bf16[192,2048]{1,0:T(8,128)(2,1)}, u32[]{:S(2)}, u32[]{:S(2)}) collective-permute-start(bf16[192,2048]{1,0:T(8,128)(2,1)} %refs_2_.1), channel_id=1, source_target_pairs={{6,2},{10,6},{14,10},{7,3},{11,7},{15,11},{22,18},{26,22},{30,26},... | collective-permute-start | bytes 2359304 | tf_op jit(solution)/shard_map/ppermute | solution.py:261
  8.9 30.6 %collective-permute-start = (bf16[192,2048]{1,0:T(8,128)(2,1)}, bf16[192,2048]{1,0:T(8,128)(2,1)}, u32[]{:S(2)}, u32[]{:S(2)}) collective-permute-start(bf16[192,2048]{1,0:T(8,128)(2,1)} %refs_2_.1), channel_id=1, source_target_pairs={{2,6},{6,10},{10,14},{3,7},{7,11},{11,15},{18,22},{22,26},{26,30},... | collective-permute-start | bytes 2359304 | tf_op jit(solution)/shard_map/ppermute | solution.py:261
  10.5 2.4 %copy-start.9 = (bf16[192,2048]{1,0:T(8,128)(2,1)S(1)}, bf16[192,2048]{1,0:T(8,128)(2,1)}, u32[]{:S(2)}) copy-start(bf16[192,2048]{1,0:T(8,128)(2,1)} %param.8) | copy-start | bytes 2359300
  13.1 1.3 copy-start.11
  41.3 12.9 %collective-permute-start.1 = (bf16[192,2048]{1,0:T(8,128)(2,1)S(1)}, bf16[192,2048]{1,0:T(8,128)(2,1)S(1)}, u32[]{:S(2)}, u32[]{:S(2)}) collective-permute-start(bf16[192,2048]{1,0:T(8,128)(2,1)S(1)} %get-tuple-element.52), channel_id=1, source_target_pairs={{0,4},{6,10},{10,14},{1,5},{7,11},{11,15},{16,20},{22,26},{26,30},... | collective-permute-start | bytes 2359304 | tf_op jit(solution)/shard_map/ppermute | solution.py:261
  44.8 9.4 %collective-permute-start.4 = (bf16[192,2048]{1,0:T(8,128)(2,1)S(1)}, bf16[192,2048]{1,0:T(8,128)(2,1)S(1)}, u32[]{:S(2)}, u32[]{:S(2)}) collective-permute-start(bf16[192,2048]{1,0:T(8,128)(2,1)S(1)} %get-tuple-element.51), channel_id=1, source_target_pairs={{12,8},{6,2},{10,6},{13,9},{7,3},{11,7},{28,24},{22,18},{26,22},{2... | collective-permute-start | bytes 2359304 | tf_op jit(solution)/shard_map/ppermute | solution.py:261
  51.8 16.9 %copy-start.2 = (f32[192,2048]{1,0:T(8,128)}, f32[192,2048]{1,0:T(8,128)S(1)}, u32[]{:S(2)}) copy-start(f32[192,2048]{1,0:T(8,128)S(1)} %shard_map.96) | copy-start | bytes 4718596
  54.8 13.9 %collective-permute-start.3 = (bf16[192,2048]{1,0:T(8,128)(2,1)S(1)}, bf16[192,2048]{1,0:T(8,128)(2,1)S(1)}, u32[]{:S(2)}, u32[]{:S(2)}) collective-permute-start(bf16[192,2048]{1,0:T(8,128)(2,1)S(1)} %get-tuple-element.48), channel_id=1, source_target_pairs={{0,4},{4,8},{10,14},{1,5},{5,9},{11,15},{16,20},{20,24},{26,30},{1... | collective-permute-start | bytes 2359304 | tf_op jit(solution)/shard_map/ppermute | solution.py:261
  59.3 9.4 %collective-permute-start.5 = (bf16[192,2048]{1,0:T(8,128)(2,1)S(1)}, bf16[192,2048]{1,0:T(8,128)(2,1)S(1)}, u32[]{:S(2)}, u32[]{:S(2)}) collective-permute-start(bf16[192,2048]{1,0:T(8,128)(2,1)S(1)} %get-tuple-element.47), channel_id=1, source_target_pairs={{8,4},{12,8},{6,2},{9,5},{13,9},{7,3},{24,20},{28,24},{22,18},{25,... | collective-permute-start | bytes 2359304 | tf_op jit(solution)/shard_map/ppermute | solution.py:261
  66.4 4.0 %copy-start.6 = (f32[192,2048]{1,0:T(8,128)}, f32[192,2048]{1,0:T(8,128)S(1)}, u32[]{:S(2)}) copy-start(f32[192,2048]{1,0:T(8,128)S(1)} %shard_map.97) | copy-start | bytes 4718596
  70.5 24.1 %collective-permute-start.6 = (bf16[192,2048]{1,0:T(8,128)(2,1)}, bf16[192,2048]{1,0:T(8,128)(2,1)}, u32[]{:S(2)}, u32[]{:S(2)}) collective-permute-start(bf16[192,2048]{1,0:T(8,128)(2,1)} %get-tuple-element.50), channel_id=1, source_target_pairs={{0,4},{4,8},{8,12},{1,5},{5,9},{9,13},{16,20},{20,24},{24,28},{17,... | collective-permute-start | bytes 2359304 | tf_op jit(solution)/shard_map/ppermute | solution.py:261
  78.8 15.8 %collective-permute-start.7 = (bf16[192,2048]{1,0:T(8,128)(2,1)}, bf16[192,2048]{1,0:T(8,128)(2,1)}, u32[]{:S(2)}, u32[]{:S(2)}) collective-permute-start(bf16[192,2048]{1,0:T(8,128)(2,1)} %get-tuple-element.49), channel_id=1, source_target_pairs={{4,0},{8,4},{12,8},{5,1},{9,5},{13,9},{20,16},{24,20},{28,24},{21,... | collective-permute-start | bytes 2359304 | tf_op jit(solution)/shard_map/ppermute | solution.py:261
  80.3 8.6 %copy-start.14 = (s32[192]{0:T(256)S(1)}, s32[192]{0:T(256)}, u32[]{:S(2)}) copy-start(s32[192]{0:T(256)} %param.15) | copy-start | bytes 2308
  86.5 1.1 copy-start.4
  87.7 3.0 %copy-start.5 = (f32[192,2048]{1,0:T(8,128)S(1)}, f32[192,2048]{1,0:T(8,128)}, u32[]{:S(2)}) copy-start(f32[192,2048]{1,0:T(8,128)} %copy-done.4) | copy-start | bytes 4718596
  88.9 1.8 %copy-start.3 = (f32[192,2048]{1,0:T(8,128)S(1)}, f32[192,2048]{1,0:T(8,128)}, u32[]{:S(2)}) copy-start(f32[192,2048]{1,0:T(8,128)} %copy-done.2) | copy-start | bytes 4718596
  88.9 1.8 %copy-start.8 = (f32[1,2048]{1,0:T(1,128)S(1)}, f32[1,2048]{1,0:T(1,128)}, u32[]{:S(2)}) copy-start(f32[1,2048]{1,0:T(1,128)} %gain_ref.1) | copy-start | bytes 24580
  90.8 3.9 %copy-start.10 = (bf16[192,2048]{1,0:T(8,128)(2,1)S(1)}, bf16[192,2048]{1,0:T(8,128)(2,1)}, u32[]{:S(2)}) copy-start(bf16[192,2048]{1,0:T(8,128)(2,1)} %param.8) | copy-start | bytes 2359300
  93.1 5.2 %collective-permute-start.9 = (bf16[192,2048]{1,0:T(8,128)(2,1)S(1)}, bf16[192,2048]{1,0:T(8,128)(2,1)S(1)}, u32[]{:S(2)}, u32[]{:S(2)}) collective-permute-start(bf16[192,2048]{1,0:T(8,128)(2,1)S(1)} %get-tuple-element.58), channel_id=1, source_target_pairs={{2,0},{3,1},{6,4},{7,5},{10,8},{11,9},{14,12},{15,13},{18,16},{19,... | collective-permute-start | bytes 2359304 | tf_op jit(solution)/shard_map/ppermute | solution.py:215
  94.6 2.3 %copy-start.13 = (bf16[384,2048]{1,0:T(8,128)(2,1)S(1)}, bf16[384,2048]{1,0:T(8,128)(2,1)}, u32[]{:S(2)}) copy-start(bf16[384,2048]{1,0:T(8,128)(2,1)} %all-gather.4.cloned.1.call-done) | copy-start | bytes 4718596
  97.1 3.1 %collective-permute-start.8 = (bf16[192,2048]{1,0:T(8,128)(2,1)S(1)}, bf16[192,2048]{1,0:T(8,128)(2,1)S(1)}, u32[]{:S(2)}, u32[]{:S(2)}) collective-permute-start(bf16[192,2048]{1,0:T(8,128)(2,1)S(1)} %get-tuple-element.45), channel_id=1, source_target_pairs={{0,2},{2,0},{1,3},{3,1},{4,6},{6,4},{5,7},{7,5},{8,10},{10,8},{9,1... | collective-permute-start | bytes 2359304 | tf_op jit(solution)/shard_map/ppermute | solution.py:355
  100.8 8.9 %copy-start.7 = (bf16[192,2048]{1,0:T(8,128)(2,1)S(1)}, bf16[192,2048]{1,0:T(8,128)(2,1)}, u32[]{:S(2)}) copy-start(bf16[192,2048]{1,0:T(8,128)(2,1)} %refs_2_.1) | copy-start | bytes 2359300
  100.8 8.9 %copy-start.12 = (bf16[1,256,2048]{2,1,0:T(8,128)(2,1)S(1)}, bf16[1,256,2048]{2,1,0:T(8,128)(2,1)}, u32[]{:S(2)}) copy-start(bf16[1,256,2048]{2,1,0:T(8,128)(2,1)} %param.13) | copy-start | bytes 3145732
  100.8 4.3 %collective-permute-start.12 = (f32[2,192]{1,0:T(2,128)S(1)}, f32[2,192]{1,0:T(2,128)S(1)}, u32[]{:S(2)}, u32[]{:S(2)}) collective-permute-start(f32[2,192]{1,0:T(2,128)S(1)} %pad_maximum_fusion.1), channel_id=1, source_target_pairs={{0,4},{4,0},{8,12},{12,8},{1,5},{5,1},{9,13},{13,9},{2,6},{6,2},{1... | collective-permute-start | bytes 4616 | tf_op jit(solution)/shard_map/ppermute | solution.py:199
  103.5 19.5 %collective-permute-start.10 = (bf16[192,2048]{1,0:T(8,128)(2,1)S(1)}, bf16[192,2048]{1,0:T(8,128)(2,1)S(1)}, u32[]{:S(2)}, u32[]{:S(2)}) collective-permute-start(bf16[192,2048]{1,0:T(8,128)(2,1)S(1)} %get-tuple-element.43), channel_id=1, source_target_pairs={{0,1},{1,0},{2,3},{3,2},{4,5},{5,4},{6,7},{7,6},{8,9},{9,8},{10,11... | collective-permute-start | bytes 2359304 | tf_op jit(solution)/shard_map/ppermute | solution.py:205
  105.1 4.5 %collective-permute-start.13 = (f32[2,192]{1,0:T(2,128)S(1)}, f32[2,192]{1,0:T(2,128)S(1)}, u32[]{:S(2)}, u32[]{:S(2)}) collective-permute-start(f32[2,192]{1,0:T(2,128)S(1)} %fusion.39), channel_id=1, source_target_pairs={{0,8},{4,12},{8,0},{12,4},{1,9},{5,13},{9,1},{13,5},{2,10},{6,14},... | collective-permute-start | bytes 4616 | tf_op jit(solution)/shard_map/ppermute | solution.py:199
  110.4 12.6 %collective-permute-start.14 = (bf16[192,256]{1,0:T(8,128)(2,1)S(1)}, bf16[192,256]{1,0:T(8,128)(2,1)S(1)}, u32[]{:S(2)}, u32[]{:S(2)}) collective-permute-start(bf16[192,256]{1,0:T(8,128)(2,1)S(1)} %get-tuple-element.60), channel_id=1, source_target_pairs={{0,4},{4,0},{8,12},{12,8},{1,5},{5,1},{9,13},{13,9},{2,6},{6,2},{1... | collective-permute-start | bytes 294920 | tf_op jit(solution)/shard_map/ppermute | solution.py:199
  123.1 10.2 %collective-permute-start.11 = (bf16[192,2048]{1,0:T(8,128)(2,1)S(1)}, bf16[192,2048]{1,0:T(8,128)(2,1)S(1)}, u32[]{:S(2)}, u32[]{:S(2)}) collective-permute-start(bf16[192,2048]{1,0:T(8,128)(2,1)S(1)} %collective-permute-done.10), channel_id=1, source_target_pairs={{0,2},{2,0},{1,3},{3,1},{4,6},{6,4},{5,7},{7,5},{8,10},{10,8},{9,1... | collective-permute-start | bytes 2359304 | tf_op jit(solution)/shard_map/ppermute | solution.py:378
  123.1 8.1 %collective-permute-start.15 = (bf16[192,256]{1,0:T(8,128)(2,1)S(1)}, bf16[192,256]{1,0:T(8,128)(2,1)S(1)}, u32[]{:S(2)}, u32[]{:S(2)}) collective-permute-start(bf16[192,256]{1,0:T(8,128)(2,1)S(1)} %fusion.32), channel_id=1, source_target_pairs={{0,8},{4,12},{8,0},{12,4},{1,9},{5,13},{9,1},{13,5},{2,10},{6,14},... | collective-permute-start | bytes 294920 | tf_op jit(solution)/shard_map/ppermute | solution.py:199
  131.6 8.0 %collective-permute-start.16 = (bf16[192,640]{1,0:T(8,128)(2,1)S(1)}, bf16[192,640]{1,0:T(8,128)(2,1)S(1)}, u32[]{:S(2)}, u32[]{:S(2)}) collective-permute-start(bf16[192,640]{1,0:T(8,128)(2,1)S(1)} %pad_maximum_fusion.refs_8_), channel_id=1, source_target_pairs={{0,1},{1,0},{2,3},{3,2},{4,5},{5,4},{6,7},{7,6},{8,9},{9,8},{10,11... | collective-permute-start | bytes 737288 | tf_op jit(solution)/shard_map/ppermute | solution.py:205
  (2 other events, 1.8 us)
Sparse Core Ops, SparseCore 0:
  13.0 31.6 all-gather.3

commit v8 on v7

--- a/solution.py
+++ b/solution.py
@@ -67,7 +67,7 @@
 
 def block_product(table, value, weight, blocks):
     rows, width = value.shape
-    tile = min(256, width)
+    tile = min(512, width)
     tiles = width // tile
     return pl.pallas_call(
         functools.partial(block_kernel, blocks=blocks, tile=tile, tiles=tiles),
@@ -263,12 +263,12 @@
     token_float = tokens.astype(F32)
     early = jnp.where(is_first, (token_float * gain_row).astype(BF16), cotangent)
     early = lax.optimization_barrier(early)
-    small = jnp.where(is_first, times_down(early), times_up_transposed(early)).astype(BF16)
-    squares = jnp.sum(token_float * token_float, axis=1).astype(BF16)
-    squares = jnp.pad(squares, (0, -rows % ranks)).reshape(-1, ranks)
-    small = jnp.concatenate([small, jnp.pad(squares, ((0, 15), (0, 0)))], axis=0)
-    small_all = lax.all_gather(small, "tensor")
-    early_all = lax.all_gather(early, "replica")
+
+    def small_columns(value, plain):
+        small = jnp.where(is_first, times_down(value), times_up_transposed(value))
+        squares = jnp.sum(plain.astype(F32) ** 2, axis=1)
+        squares = jnp.pad(squares, (0, -rows % ranks)).reshape(-1, ranks)
+        return jnp.concatenate([small, jnp.pad(squares, ((0, -len(squares) % 16), (0, 0)))], axis=0)
 
     everyone = range(count)
     arrivals = [
@@ -278,12 +278,18 @@
         )
     ]
     parts = []
+    small_sum = None
+    steps_left = doubling_steps()
     for stage in range(count):
         wanted = [None if stage == 0 else second_slots[z][stage] for z in everyone]
         cases = sorted({slot for slot in wanted if slot is not None})
         here = [early] + [arrivals[slot][side] for slot, side in cases]
+        if stage == 1:
+            small_sum = small_columns(*lax.optimization_barrier((early, tokens, *sent))[:2])
+        elif stage > 1 and steps_left:
+            small_sum = sum_step(small_sum, steps_left.pop(0))
         if stage > 0:
-            here = lax.optimization_barrier((*here, *sent))[: len(here)]
+            *here, small_sum = lax.optimization_barrier((*here, small_sum, *sent))[: len(here) + 1]
         value = pick(
             place_of,
             [0] * count + [0 if slot is None else 1 + cases.index(slot) for slot in wanted],
@@ -291,6 +297,11 @@
         )
         order = [blocks[stage] for blocks in first_order + second_order]
         part = block_product(table, value, weight, order)
+        if stage == 0:
+            part, after = lax.optimization_barrier((part, early))
+            early_all = [early] + with_other_replicas(after)[1:]
+        if stage == 2:
+            part, *early_all = lax.optimization_barrier((part, *early_all))
         parts.append(part)
         slot = stage + 1
         if slot == count:
@@ -304,7 +315,10 @@
                 [0 if at is None else stages.index(at) for at in needed] + [0] * count,
                 [parts[at] for at in stages],
             )
-            arrived = arrivals[-1][side].astype(F32)
+            arrived = arrivals[-1][side]
+            if side == 1:
+                arrived, _ = lax.optimization_barrier((arrived, sent[0]))
+            arrived = arrived.astype(F32)
             sent.append((arrived + jnp.where(is_first, own, 0.0)).astype(BF16))
         arrivals.append(
             (
@@ -324,15 +338,8 @@
         )
     from_left, from_right = arrivals[-1]
 
-    small_all, early_all, _ = lax.optimization_barrier(
-        (small_all, early_all, arrivals[max(count - 2, 0)])
-    )
-    replica, replicas = lax.axis_index("replica"), lax.axis_size("replica")
-    early_all = [early] + [
-        lax.dynamic_index_in_dim(early_all, lax.rem(replica + replicas - step, replicas), 0, False)
-        for step in range(1, replicas)
-    ]
-    small_sum = jnp.sum(small_all.astype(F32), axis=0)
+    while steps_left:
+        small_sum = sum_step(small_sum, steps_left.pop(0))
     inv_first = lax.rsqrt(
         small_sum[rows:].reshape(-1)[:rows][:, None] / features + EPSILON
     )
@@ -375,7 +382,10 @@
     for step in doubling_steps():
         rank_late = sum_step(rank_late, step)
 
-    swapped = [lax.ppermute(other, "section", swap) for other in late_others]
+    swapped = [
+        lax.ppermute(lax.optimization_barrier((other, rank_late))[0], "section", swap)
+        for other in late_others
+    ]
     hidden_all = [hidden_here] + [
         jnp.where(is_first, *pair) for pair in zip(late_others, swapped)
     ]

time: 152 us -> 113 us (0.74)
  blocking collectives: 18.1 us -> 0 us
  between operations: 14.5 us -> 1.14 us
  waiting for transfers between devices: 34.9 us -> 39.4 us
  other arithmetic: 12.1 us -> 8.69 us
  Pallas kernels: 29.6 us -> 26.8 us
  matrix products: 6.06 us -> 3.27 us
  local copies, waits for them, and re-layouts: 2.41 us -> 0.61 us
    all_gather x1 -> x0, blocking collectives: 18.1 us -> none  [on_device(): small_all = lax.all_gather(small, 'tensor')]
    ppermute x4 -> x6, waiting for transfers between devices: 11.5 us -> 25.9 us  [sum_step(): return value + lax.ppermute(value.astype(wire), 'tensor', pairs).astype(F32)]
    ppermute x2 -> x3, waiting for transfers between devices: 16.8 us -> 6.48 us  [with_other_replicas(): lax.ppermute(value, ('section', 'replica'), [(s * count + r, s * count +...]
    ppermute x8, starting transfers between devices: 22.2 us -> 15.4 us  [line(): return lax.ppermute(value, ('tensor', 'section'), pairs)]
    ppermute x4 -> x6, starting transfers between devices: 5.53 us -> 9.89 us  [sum_step(): return value + lax.ppermute(value.astype(wire), 'tensor', pairs).astype(F32)]
    pallas_call x4, Pallas kernels: 24.7 us -> 20.9 us  [block_product(): pl.pallas_call(functools.partial(block_kernel, blocks=blocks, tile=tile,...]
    ppermute x2 -> x3, starting transfers between devices: 3.21 us -> 5.17 us  [with_other_replicas(): lax.ppermute(value, ('section', 'replica'), [(s * count + r, s * count +...]
    unnamed x34 -> x16, local copies, waits for them, and re-layouts: 2.07 us -> 0.28 us
  transfers between devices with their start and end apart: 18 -> 20, of which waited for: 7 -> 10; matrix products, arithmetic and copies ran while one was open for 12% -> 11% of each run, Pallas kernels for 16% -> 19%
where the time goes in v8:
time: 113 us; the launch traced here: 112 us
  waiting for transfers between devices  39.4 us (35%)
  starting transfers between devices  32.1 us (28%)
  Pallas kernels  26.8 us (24%)
  other arithmetic  8.69 us (8%)
  matrix products  3.27 us (3%)
  between operations  1.14 us (1%)
    ppermute x6, waiting for transfers between devices, sum_step(): return value + lax.ppermute(value.astype(wire), 'tensor', pairs).astype(F32)  25.9 us
    pallas_call x4, Pallas kernels, block_product(): pl.pallas_call(functools.partial(block_kernel, blocks=blocks, tile=tile,...  20.9 us
    ppermute x8, starting transfers between devices, line(): return lax.ppermute(value, ('tensor', 'section'), pairs)  15.4 us
    ppermute x6, starting transfers between devices, sum_step(): return value + lax.ppermute(value.astype(wire), 'tensor', pairs).astype(F32)  9.89 us
    ppermute x3, waiting for transfers between devices, with_other_replicas(): lax.ppermute(value, ('section', 'replica'), [(s * count + r, s * count +...  6.48 us
    pallas_call x1, Pallas kernels, gradients(): pl.pallas_call(functools.partial(gradient_kernel, replicas=replicas), gri...  5.85 us
    ppermute x3, starting transfers between devices, with_other_replicas(): lax.ppermute(value, ('section', 'replica'), [(s * count + r, s * count +...  5.17 us
    convert_element_type x6, other arithmetic, on_device(): sent.append((arrived + jnp.where(is_first, own, 0.0)).astype(BF16))  4.09 us
  transfers between devices with their start and end apart: 20, of which 10 were waited for; matrix products, arithmetic and copies ran while one was open for 11% of the time, Pallas kernels for 19%

profile of v8, /device:TPU:0, one launch (start us, length us, event | category | flops | bytes accessed | tf_op | source)
XLA Modules:
  0.0 111.9 jit_solution(12010935221824035816)
XLA Ops:
  0.6 1.7 %collective-permute-start = (bf16[192,2048]{1,0:T(8,128)(2,1)}, bf16[192,2048]{1,0:T(8,128)(2,1)}, u32[]{:S(2)}, u32[]{:S(2)}) collective-permute-start(bf16[192,2048]{1,0:T(8,128)(2,1)} %refs_2_.1), channel_id=1, source_target_pairs={{6,2},{10,6},{14,10},{7,3},{11,7},{15,11},{22,18},{26,22},{30,26},... | collective-permute-start | bytes 2359304 | tf_op jit(solution)/shard_map/ppermute | solution.py:261
  2.3 1.5 %collective-permute-start.1 = (bf16[192,2048]{1,0:T(8,128)(2,1)}, bf16[192,2048]{1,0:T(8,128)(2,1)}, u32[]{:S(2)}, u32[]{:S(2)}) collective-permute-start(bf16[192,2048]{1,0:T(8,128)(2,1)} %refs_2_.1), channel_id=1, source_target_pairs={{2,6},{6,10},{10,14},{3,7},{7,11},{11,15},{18,22},{22,26},{26,30},... | collective-permute-start | bytes 2359304 | tf_op jit(solution)/shard_map/ppermute | solution.py:261
  3.9 1.4 %fusion.23.value_ref.refs_0_ = bf16[192,2048]{1,0:T(8,128)(2,1)S(1)} fusion(bf16[192,2048]{1,0:T(8,128)(2,1)} %refs_2_.1, bf16[192,2048]{1,0:T(8,128)(2,1)} %param.8, f32[2048]{0:T(1024)} %bitcast.38, pred[]{:T(512)S(6)} %eq.21), kind=kLoop, calls=%fused_computation.36 | loop fusion | flops 1572864 | bytes 2367489 | tf_op jit(solution)/shard_map/jit(_where)/select_n | solution.py:264
  5.4 5.2 %shard_map.95 = f32[192,2048]{1,0:T(8,128)S(1)} custom-call(s32[2]{0:T(128)S(1)} %pad_add_fusion.table, bf16[192,2048]{1,0:T(8,128)(2,1)S(1)} %fusion.23.value_ref.refs_0_, bf16[2048,8192]{1,0:T(8,128)(2,1)} %bitcast.41), custom_call_target="tpu_custom_call" | custom-call | flops 6442450944 | bytes 8388608 | tf_op jit(solution)/shard_map/pallas_call | solution.py:72
  10.6 3.0 %collective-permute-start.5 = (bf16[192,2048]{1,0:T(8,128)(2,1)S(1)}, bf16[192,2048]{1,0:T(8,128)(2,1)}, u32[]{:S(2)}, u32[]{:S(2)}) collective-permute-start(bf16[192,2048]{1,0:T(8,128)(2,1)S(1)} %fusion.23.value_ref.refs_0_), channel_id=1, source_target_pairs={{0,1},{1,0},{2,3},{3,2},{4,5},{5,4},{6,7},{7,6},{8,9},{9,8},{10,11... | collective-permute-start | bytes 2359304 | tf_op jit(solution)/shard_map/ppermute | solution.py:205
  13.7 1.3 %add_convert_fusion.5 = bf16[192,2048]{1,0:T(8,128)(2,1)S(1)} fusion(bf16[192,2048]{1,0:T(8,128)(2,1)} %collective-permute-done.1, f32[192,2048]{1,0:T(8,128)S(1)} %shard_map.95, pred[]{:T(512)S(6)} %eq.21), kind=kLoop, calls=%fused_computation.23 | loop fusion | flops 1572864 | bytes 3145729 | tf_op jit(solution)/shard_map/convert_element_type | solution.py:322
  15.1 3.7 %collective-permute-start.2 = (bf16[192,2048]{1,0:T(8,128)(2,1)S(1)}, bf16[192,2048]{1,0:T(8,128)(2,1)S(1)}, u32[]{:S(2)}, u32[]{:S(2)}) collective-permute-start(bf16[192,2048]{1,0:T(8,128)(2,1)S(1)} %add_convert_fusion.5), channel_id=1, source_target_pairs={{0,4},{6,10},{10,14},{1,5},{7,11},{11,15},{16,20},{22,26},{26,30},... | collective-permute-start | bytes 2359304 | tf_op jit(solution)/shard_map/ppermute | solution.py:261
  18.8 1.3 %add_convert_fusion.4 = bf16[192,2048]{1,0:T(8,128)(2,1)S(1)} fusion(bf16[192,2048]{1,0:T(8,128)(2,1)} %collective-permute-done, f32[192,2048]{1,0:T(8,128)S(1)} %shard_map.95, pred[]{:T(512)S(6)} %eq.21), kind=kLoop, calls=%fused_computation.22 | loop fusion | flops 1572864 | bytes 3145729 | tf_op jit(solution)/shard_map/convert_element_type | solution.py:322
  22.3 5.2 %shard_map.96 = f32[192,2048]{1,0:T(8,128)S(1)} custom-call(s32[2]{0:T(128)S(1)} %pad_add_fusion.table, bf16[192,2048]{1,0:T(8,128)(2,1)S(1)} %select_select_fusion.2.value_ref, bf16[2048,8192]{1,0:T(8,128)(2,1)} %bitcast.42), custom_call_target="tpu_custom_call" | custom-call | flops 6442450944 | bytes 8388608 | tf_op jit(solution)/shard_map/pallas_call | solution.py:72
  27.6 2.6 %collective-permute-done.4 = bf16[208,256]{1,0:T(8,128)(2,1)S(1)} collective-permute-done((bf16[208,256]{1,0:T(8,128)(2,1)S(1)}, bf16[208,256]{1,0:T(8,128)(2,1)S(1)}, u32[]{:S(2)}, u32[]{:S(2)}) %collective-permute-start.4) | collective-permute-done | bytes 106528 | tf_op jit(solution)/shard_map/ppermute | solution.py:199
  30.5 4.4 %collective-permute-start.6 = (bf16[192,2048]{1,0:T(8,128)(2,1)S(1)}, bf16[192,2048]{1,0:T(8,128)(2,1)S(1)}, u32[]{:S(2)}, u32[]{:S(2)}) collective-permute-start(bf16[192,2048]{1,0:T(8,128)(2,1)S(1)} %add_convert_fusion.3), channel_id=1, source_target_pairs={{0,4},{4,8},{10,14},{1,5},{5,9},{11,15},{16,20},{20,24},{26,30},{1... | collective-permute-start | bytes 2359304 | tf_op jit(solution)/shard_map/ppermute | solution.py:261
  36.1 6.7 %collective-permute-start.8 = (bf16[208,256]{1,0:T(8,128)(2,1)S(1)}, bf16[208,256]{1,0:T(8,128)(2,1)S(1)}, u32[]{:S(2)}, u32[]{:S(2)}) collective-permute-start(bf16[208,256]{1,0:T(8,128)(2,1)S(1)} %convert_element_type.120), channel_id=1, source_target_pairs={{0,8},{4,12},{8,0},{12,4},{1,9},{5,13},{9,1},{13,5},{2,10},{6,14},... | collective-permute-start | bytes 319496 | tf_op jit(solution)/shard_map/ppermute | solution.py:199
  43.1 5.2 %shard_map.97 = f32[192,2048]{1,0:T(8,128)S(1)} custom-call(s32[2]{0:T(128)S(1)} %pad_add_fusion.table, bf16[192,2048]{1,0:T(8,128)(2,1)S(1)} %select_select_fusion.1.value_ref, bf16[2048,8192]{1,0:T(8,128)(2,1)} %bitcast.43), custom_call_target="tpu_custom_call" | custom-call | flops 6442450944 | bytes 8388608 | tf_op jit(solution)/shard_map/pallas_call | solution.py:72
  48.4 8.4 %collective-permute-done.8 = bf16[208,256]{1,0:T(8,128)(2,1)S(1)} collective-permute-done((bf16[208,256]{1,0:T(8,128)(2,1)S(1)}, bf16[208,256]{1,0:T(8,128)(2,1)S(1)}, u32[]{:S(2)}, u32[]{:S(2)}) %collective-permute-start.8) | collective-permute-done | bytes 106528 | tf_op jit(solution)/shard_map/ppermute | solution.py:199
  57.2 1.3 %collective-permute-start.9 = (bf16[192,2048]{1,0:T(8,128)(2,1)S(1)}, bf16[192,2048]{1,0:T(8,128)(2,1)S(1)}, u32[]{:S(2)}, u32[]{:S(2)}) collective-permute-start(bf16[192,2048]{1,0:T(8,128)(2,1)S(1)} %add_convert_fusion.1), channel_id=1, source_target_pairs={{0,4},{4,8},{8,12},{1,5},{5,9},{9,13},{16,20},{20,24},{24,28},{17,... | collective-permute-start | bytes 2359304 | tf_op jit(solution)/shard_map/ppermute | solution.py:261
  58.8 1.3 %collective-permute-start.10 = (bf16[192,2048]{1,0:T(8,128)(2,1)S(1)}, bf16[192,2048]{1,0:T(8,128)(2,1)S(1)}, u32[]{:S(2)}, u32[]{:S(2)}) collective-permute-start(bf16[192,2048]{1,0:T(8,128)(2,1)S(1)} %add_convert_fusion), channel_id=1, source_target_pairs={{4,0},{8,4},{12,8},{5,1},{9,5},{13,9},{20,16},{24,20},{28,24},{21,... | collective-permute-start | bytes 2359304 | tf_op jit(solution)/shard_map/ppermute | solution.py:261
  60.4 5.2 %shard_map.98 = f32[192,2048]{1,0:T(8,128)S(1)} custom-call(s32[2]{0:T(128)S(1)} %pad_add_fusion.table, bf16[192,2048]{1,0:T(8,128)(2,1)S(1)} %select_select_fusion.value_ref, bf16[2048,8192]{1,0:T(8,128)(2,1)} %bitcast.44), custom_call_target="tpu_custom_call" | custom-call | flops 6442450944 | bytes 8388608 | tf_op jit(solution)/shard_map/pallas_call | solution.py:72
  66.4 0.8 multiply_convert_fusion
  67.2 1.5 %collective-permute-start.12 = (bf16[192,2048]{1,0:T(8,128)(2,1)S(1)}, bf16[192,2048]{1,0:T(8,128)(2,1)S(1)}, u32[]{:S(2)}, u32[]{:S(2)}) collective-permute-start(bf16[192,2048]{1,0:T(8,128)(2,1)S(1)} %get-tuple-element.74), channel_id=1, source_target_pairs={{2,0},{3,1},{6,4},{7,5},{10,8},{11,9},{14,12},{15,13},{18,16},{19,... | collective-permute-start | bytes 2359304 | tf_op jit(solution)/shard_map/ppermute | solution.py:215
  68.7 4.0 %collective-permute-done.10 = bf16[192,2048]{1,0:T(8,128)(2,1)S(1)} collective-permute-done((bf16[192,2048]{1,0:T(8,128)(2,1)S(1)}, bf16[192,2048]{1,0:T(8,128)(2,1)S(1)}, u32[]{:S(2)}, u32[]{:S(2)}) %collective-permute-start.10) | collective-permute-done | bytes 786464 | tf_op jit(solution)/shard_map/ppermute | solution.py:261
  72.7 0.9 broadcast_select_fusion.2
  73.8 2.3 %collective-permute-done.11.refs_3_ = bf16[192,2048]{1,0:T(8,128)(2,1)S(1)} collective-permute-done((bf16[192,2048]{1,0:T(8,128)(2,1)S(1)}, bf16[192,2048]{1,0:T(8,128)(2,1)S(1)}, u32[]{:S(2)}, u32[]{:S(2)}) %collective-permute-start.11) | collective-permute-done | bytes 786464 | tf_op jit(solution)/shard_map/ppermute | solution.py:362
  77.4 1.0 collective-permute-start.13
  78.4 1.9 %collective-permute-done.14 = f32[2,192]{1,0:T(2,128)S(1)} collective-permute-done((f32[2,192]{1,0:T(2,128)S(1)}, f32[2,192]{1,0:T(2,128)S(1)}, u32[]{:S(2)}, u32[]{:S(2)}) %collective-permute-start.14) | collective-permute-done | bytes 1568 | tf_op jit(solution)/shard_map/ppermute | solution.py:199
  80.3 0.8 collective-permute-start.15
  81.5 3.4 %collective-permute-done.15 = f32[2,192]{1,0:T(2,128)S(1)} collective-permute-done((f32[2,192]{1,0:T(2,128)S(1)}, f32[2,192]{1,0:T(2,128)S(1)}, u32[]{:S(2)}, u32[]{:S(2)}) %collective-permute-start.15) | collective-permute-done | bytes 1568 | tf_op jit(solution)/shard_map/ppermute | solution.py:199
  86.4 3.9 %collective-permute-done.16 = bf16[192,256]{1,0:T(8,128)(2,1)S(1)} collective-permute-done((bf16[192,256]{1,0:T(8,128)(2,1)S(1)}, bf16[192,256]{1,0:T(8,128)(2,1)S(1)}, u32[]{:S(2)}, u32[]{:S(2)}) %collective-permute-start.16) | collective-permute-done | bytes 98336 | tf_op jit(solution)/shard_map/ppermute | solution.py:199
  90.4 0.8 collective-permute-start.17
  91.2 5.8 %collective-permute-done.17 = bf16[192,256]{1,0:T(8,128)(2,1)S(1)} collective-permute-done((bf16[192,256]{1,0:T(8,128)(2,1)S(1)}, bf16[192,256]{1,0:T(8,128)(2,1)S(1)}, u32[]{:S(2)}, u32[]{:S(2)}) %collective-permute-start.17) | collective-permute-done | bytes 98336 | tf_op jit(solution)/shard_map/ppermute | solution.py:199
  97.7 1.1 collective-permute-start.19
  99.6 6.5 %collective-permute-done.19.refs_9_ = bf16[192,640]{1,0:T(8,128)(2,1)S(1)} collective-permute-done((bf16[192,640]{1,0:T(8,128)(2,1)S(1)}, bf16[192,640]{1,0:T(8,128)(2,1)S(1)}, u32[]{:S(2)}, u32[]{:S(2)}) %collective-permute-start.19) | collective-permute-done | bytes 245792 | tf_op jit(solution)/shard_map/ppermute | solution.py:205
  106.1 5.8 %shard_map.99 = (f32[2048,256]{1,0:T(8,128)}, f32[256,2048]{1,0:T(8,128)}) custom-call(s32[2]{0:T(128)S(1)} %pad_add_fusion.table, f32[1,2048]{1,0:T(1,128)S(1)} %copy-done.2, bf16[192,2048]{1,0:T(8,128)(2,1)S(1)} %fusion.23.value_ref.refs_0_, bf16[192,2048]{1,0:T(8,128)(2,1)} %collective-permute-done.5.refs_1_, bf16[192,2048]{1,0:T(8,128)(2,1)S(1)} %copy-done.1, ...), custom_call_target="tpu_custom_call" | custom-call | flops 805306368 | bytes 10485760 | tf_op jit(solution)/shard_map/pallas_call | solution.py:140
  (73 shorter events, 10.6 us)
Async XLA Ops:
  0.6 21.0 %copy-start = (bf16[1,2048,256]{2,1,0:T(8,128)(2,1)S(1)}, bf16[1,2048,256]{2,1,0:T(8,128)(2,1)}, u32[]{:S(2)}) copy-start(bf16[1,2048,256]{2,1,0:T(8,128)(2,1)} %param.12) | copy-start | bytes 3145732
  0.6 18.1 %collective-permute-start = (bf16[192,2048]{1,0:T(8,128)(2,1)}, bf16[192,2048]{1,0:T(8,128)(2,1)}, u32[]{:S(2)}, u32[]{:S(2)}) collective-permute-start(bf16[192,2048]{1,0:T(8,128)(2,1)} %refs_2_.1), channel_id=1, source_target_pairs={{6,2},{10,6},{14,10},{7,3},{11,7},{15,11},{22,18},{26,22},{30,26},... | collective-permute-start | bytes 2359304 | tf_op jit(solution)/shard_map/ppermute | solution.py:261
  2.3 11.4 %collective-permute-start.1 = (bf16[192,2048]{1,0:T(8,128)(2,1)}, bf16[192,2048]{1,0:T(8,128)(2,1)}, u32[]{:S(2)}, u32[]{:S(2)}) collective-permute-start(bf16[192,2048]{1,0:T(8,128)(2,1)} %refs_2_.1), channel_id=1, source_target_pairs={{2,6},{6,10},{10,14},{3,7},{7,11},{11,15},{18,22},{22,26},{26,30},... | collective-permute-start | bytes 2359304 | tf_op jit(solution)/shard_map/ppermute | solution.py:261
  5.4 8.2 %copy-start.6 = (f32[4]{0:T(128)S(1)}, f32[4]{0:T(128)}, u32[]{:S(2)}) copy-start(f32[4]{0:T(128)} %param.14) | copy-start | bytes 52
  10.6 37.8 %collective-permute-start.5 = (bf16[192,2048]{1,0:T(8,128)(2,1)S(1)}, bf16[192,2048]{1,0:T(8,128)(2,1)}, u32[]{:S(2)}, u32[]{:S(2)}) collective-permute-start(bf16[192,2048]{1,0:T(8,128)(2,1)S(1)} %fusion.23.value_ref.refs_0_), channel_id=1, source_target_pairs={{0,1},{1,0},{2,3},{3,2},{4,5},{5,4},{6,7},{7,6},{8,9},{9,8},{10,11... | collective-permute-start | bytes 2359304 | tf_op jit(solution)/shard_map/ppermute | solution.py:205
  15.1 5.8 %copy-start.3 = (bf16[192,2048]{1,0:T(8,128)(2,1)S(1)}, bf16[192,2048]{1,0:T(8,128)(2,1)}, u32[]{:S(2)}) copy-start(bf16[192,2048]{1,0:T(8,128)(2,1)} %param.8) | copy-start | bytes 2359300
  15.1 6.0 %copy-start.4 = (bf16[1,256,2048]{2,1,0:T(8,128)(2,1)S(1)}, bf16[1,256,2048]{2,1,0:T(8,128)(2,1)}, u32[]{:S(2)}) copy-start(bf16[1,256,2048]{2,1,0:T(8,128)(2,1)} %param.13) | copy-start | bytes 3145732
  15.1 15.0 %collective-permute-start.2 = (bf16[192,2048]{1,0:T(8,128)(2,1)S(1)}, bf16[192,2048]{1,0:T(8,128)(2,1)S(1)}, u32[]{:S(2)}, u32[]{:S(2)}) collective-permute-start(bf16[192,2048]{1,0:T(8,128)(2,1)S(1)} %add_convert_fusion.5), channel_id=1, source_target_pairs={{0,4},{6,10},{10,14},{1,5},{7,11},{11,15},{16,20},{22,26},{26,30},... | collective-permute-start | bytes 2359304 | tf_op jit(solution)/shard_map/ppermute | solution.py:261
  20.2 14.8 %collective-permute-start.3 = (bf16[192,2048]{1,0:T(8,128)(2,1)S(1)}, bf16[192,2048]{1,0:T(8,128)(2,1)S(1)}, u32[]{:S(2)}, u32[]{:S(2)}) collective-permute-start(bf16[192,2048]{1,0:T(8,128)(2,1)S(1)} %add_convert_fusion.4), channel_id=1, source_target_pairs={{12,8},{6,2},{10,6},{13,9},{7,3},{11,7},{28,24},{22,18},{26,22},{2... | collective-permute-start | bytes 2359304 | tf_op jit(solution)/shard_map/ppermute | solution.py:261
  22.1 8.0 %collective-permute-start.4 = (bf16[208,256]{1,0:T(8,128)(2,1)S(1)}, bf16[208,256]{1,0:T(8,128)(2,1)S(1)}, u32[]{:S(2)}, u32[]{:S(2)}) collective-permute-start(bf16[208,256]{1,0:T(8,128)(2,1)S(1)} %convert_element_type.114), channel_id=1, source_target_pairs={{0,4},{4,0},{8,12},{12,8},{1,5},{5,1},{9,13},{13,9},{2,6},{6,2},{1... | collective-permute-start | bytes 319496 | tf_op jit(solution)/shard_map/ppermute | solution.py:199
  30.5 26.2 %collective-permute-start.6 = (bf16[192,2048]{1,0:T(8,128)(2,1)S(1)}, bf16[192,2048]{1,0:T(8,128)(2,1)S(1)}, u32[]{:S(2)}, u32[]{:S(2)}) collective-permute-start(bf16[192,2048]{1,0:T(8,128)(2,1)S(1)} %add_convert_fusion.3), channel_id=1, source_target_pairs={{0,4},{4,8},{10,14},{1,5},{5,9},{11,15},{16,20},{20,24},{26,30},{1... | collective-permute-start | bytes 2359304 | tf_op jit(solution)/shard_map/ppermute | solution.py:261
  35.4 23.1 %collective-permute-start.7 = (bf16[192,2048]{1,0:T(8,128)(2,1)S(1)}, bf16[192,2048]{1,0:T(8,128)(2,1)S(1)}, u32[]{:S(2)}, u32[]{:S(2)}) collective-permute-start(bf16[192,2048]{1,0:T(8,128)(2,1)S(1)} %add_convert_fusion.2), channel_id=1, source_target_pairs={{8,4},{12,8},{6,2},{9,5},{13,9},{7,3},{24,20},{28,24},{22,18},{25,... | collective-permute-start | bytes 2359304 | tf_op jit(solution)/shard_map/ppermute | solution.py:261
  36.1 20.6 %collective-permute-start.8 = (bf16[208,256]{1,0:T(8,128)(2,1)S(1)}, bf16[208,256]{1,0:T(8,128)(2,1)S(1)}, u32[]{:S(2)}, u32[]{:S(2)}) collective-permute-start(bf16[208,256]{1,0:T(8,128)(2,1)S(1)} %convert_element_type.120), channel_id=1, source_target_pairs={{0,8},{4,12},{8,0},{12,4},{1,9},{5,13},{9,1},{13,5},{2,10},{6,14},... | collective-permute-start | bytes 319496 | tf_op jit(solution)/shard_map/ppermute | solution.py:199
  57.2 11.5 %collective-permute-start.9 = (bf16[192,2048]{1,0:T(8,128)(2,1)S(1)}, bf16[192,2048]{1,0:T(8,128)(2,1)S(1)}, u32[]{:S(2)}, u32[]{:S(2)}) collective-permute-start(bf16[192,2048]{1,0:T(8,128)(2,1)S(1)} %add_convert_fusion.1), channel_id=1, source_target_pairs={{0,4},{4,8},{8,12},{1,5},{5,9},{9,13},{16,20},{20,24},{24,28},{17,... | collective-permute-start | bytes 2359304 | tf_op jit(solution)/shard_map/ppermute | solution.py:261
  58.8 13.9 %collective-permute-start.10 = (bf16[192,2048]{1,0:T(8,128)(2,1)S(1)}, bf16[192,2048]{1,0:T(8,128)(2,1)S(1)}, u32[]{:S(2)}, u32[]{:S(2)}) collective-permute-start(bf16[192,2048]{1,0:T(8,128)(2,1)S(1)} %add_convert_fusion), channel_id=1, source_target_pairs={{4,0},{8,4},{12,8},{5,1},{9,5},{13,9},{20,16},{24,20},{28,24},{21,... | collective-permute-start | bytes 2359304 | tf_op jit(solution)/shard_map/ppermute | solution.py:261
  60.4 5.3 %copy-start.5 = (s32[192]{0:T(256)S(1)}, s32[192]{0:T(256)}, u32[]{:S(2)}) copy-start(s32[192]{0:T(256)} %param.15) | copy-start | bytes 2308
  65.7 0.7 copy-start.2
  67.2 6.6 %collective-permute-start.12 = (bf16[192,2048]{1,0:T(8,128)(2,1)S(1)}, bf16[192,2048]{1,0:T(8,128)(2,1)S(1)}, u32[]{:S(2)}, u32[]{:S(2)}) collective-permute-start(bf16[192,2048]{1,0:T(8,128)(2,1)S(1)} %get-tuple-element.74), channel_id=1, source_target_pairs={{2,0},{3,1},{6,4},{7,5},{10,8},{11,9},{14,12},{15,13},{18,16},{19,... | collective-permute-start | bytes 2359304 | tf_op jit(solution)/shard_map/ppermute | solution.py:215
  73.7 2.4 %collective-permute-start.11 = (bf16[192,2048]{1,0:T(8,128)(2,1)S(1)}, bf16[192,2048]{1,0:T(8,128)(2,1)S(1)}, u32[]{:S(2)}, u32[]{:S(2)}) collective-permute-start(bf16[192,2048]{1,0:T(8,128)(2,1)S(1)} %broadcast_select_fusion.3), channel_id=1, source_target_pairs={{0,2},{2,0},{1,3},{3,1},{4,6},{6,4},{5,7},{7,5},{8,10},{10,8},{9,1... | collective-permute-start | bytes 2359304 | tf_op jit(solution)/shard_map/ppermute | solution.py:362
  76.6 8.3 %copy-start.1 = (bf16[192,2048]{1,0:T(8,128)(2,1)S(1)}, bf16[192,2048]{1,0:T(8,128)(2,1)}, u32[]{:S(2)}) copy-start(bf16[192,2048]{1,0:T(8,128)(2,1)} %refs_2_.1) | copy-start | bytes 2359300
  76.6 3.7 %collective-permute-start.14 = (f32[2,192]{1,0:T(2,128)S(1)}, f32[2,192]{1,0:T(2,128)S(1)}, u32[]{:S(2)}, u32[]{:S(2)}) collective-permute-start(f32[2,192]{1,0:T(2,128)S(1)} %pad_maximum_fusion.1), channel_id=1, source_target_pairs={{0,4},{4,0},{8,12},{12,8},{1,5},{5,1},{9,13},{13,9},{2,6},{6,2},{1... | collective-permute-start | bytes 4616 | tf_op jit(solution)/shard_map/ppermute | solution.py:199
  77.4 19.8 %collective-permute-start.13 = (bf16[192,2048]{1,0:T(8,128)(2,1)S(1)}, bf16[192,2048]{1,0:T(8,128)(2,1)S(1)}, u32[]{:S(2)}, u32[]{:S(2)}) collective-permute-start(bf16[192,2048]{1,0:T(8,128)(2,1)S(1)} %get-tuple-element.69), channel_id=1, source_target_pairs={{0,1},{1,0},{2,3},{3,2},{4,5},{5,4},{6,7},{7,6},{8,9},{9,8},{10,11... | collective-permute-start | bytes 2359304 | tf_op jit(solution)/shard_map/ppermute | solution.py:205
  80.3 4.5 %collective-permute-start.15 = (f32[2,192]{1,0:T(2,128)S(1)}, f32[2,192]{1,0:T(2,128)S(1)}, u32[]{:S(2)}, u32[]{:S(2)}) collective-permute-start(f32[2,192]{1,0:T(2,128)S(1)} %fusion.35), channel_id=1, source_target_pairs={{0,8},{4,12},{8,0},{12,4},{1,9},{5,13},{9,1},{13,5},{2,10},{6,14},... | collective-permute-start | bytes 4616 | tf_op jit(solution)/shard_map/ppermute | solution.py:199
  85.7 4.7 %collective-permute-start.16 = (bf16[192,256]{1,0:T(8,128)(2,1)S(1)}, bf16[192,256]{1,0:T(8,128)(2,1)S(1)}, u32[]{:S(2)}, u32[]{:S(2)}) collective-permute-start(bf16[192,256]{1,0:T(8,128)(2,1)S(1)} %get-tuple-element.76), channel_id=1, source_target_pairs={{0,4},{4,0},{8,12},{12,8},{1,5},{5,1},{9,13},{13,9},{2,6},{6,2},{1... | collective-permute-start | bytes 294920 | tf_op jit(solution)/shard_map/ppermute | solution.py:199
  90.4 6.6 %collective-permute-start.17 = (bf16[192,256]{1,0:T(8,128)(2,1)S(1)}, bf16[192,256]{1,0:T(8,128)(2,1)S(1)}, u32[]{:S(2)}, u32[]{:S(2)}) collective-permute-start(bf16[192,256]{1,0:T(8,128)(2,1)S(1)} %fusion.29), channel_id=1, source_target_pairs={{0,8},{4,12},{8,0},{12,4},{1,9},{5,13},{9,1},{13,5},{2,10},{6,14},... | collective-permute-start | bytes 294920 | tf_op jit(solution)/shard_map/ppermute | solution.py:199
  97.2 2.4 %collective-permute-start.18 = (bf16[192,2048]{1,0:T(8,128)(2,1)S(1)}, bf16[192,2048]{1,0:T(8,128)(2,1)S(1)}, u32[]{:S(2)}, u32[]{:S(2)}) collective-permute-start(bf16[192,2048]{1,0:T(8,128)(2,1)S(1)} %collective-permute-done.13), channel_id=1, source_target_pairs={{0,2},{2,0},{1,3},{3,1},{4,6},{6,4},{5,7},{7,5},{8,10},{10,8},{9,1... | collective-permute-start | bytes 2359304 | tf_op jit(solution)/shard_map/ppermute | solution.py:386
  97.7 8.4 %collective-permute-start.19 = (bf16[192,640]{1,0:T(8,128)(2,1)S(1)}, bf16[192,640]{1,0:T(8,128)(2,1)S(1)}, u32[]{:S(2)}, u32[]{:S(2)}) collective-permute-start(bf16[192,640]{1,0:T(8,128)(2,1)S(1)} %pad_maximum_fusion.refs_8_), channel_id=1, source_target_pairs={{0,1},{1,0},{2,3},{3,2},{4,5},{5,4},{6,7},{7,6},{8,9},{9,8},{10,11... | collective-permute-start | bytes 737288 | tf_op jit(solution)/shard_map/ppermute | solution.py:205

commit v9 on v8

--- a/solution.py
+++ b/solution.py
@@ -93,74 +93,77 @@
     )(table, value, weight)
 
 
-def gradient_kernel(table, gain_ref, *refs, replicas):
-    early, cotangent, pulled, hidden, smalls = (
-        refs[kind * replicas : (kind + 1) * replicas] for kind in range(5)
-    )
-    down_ref, up_ref = refs[5 * replicas :]
-    ranks = down_ref.shape[1]
-
-    def products(down_rows, up_rows):
-        down_ref[...] = sum(
-            lax.dot_general(a, small[:, ranks : 2 * ranks], CONTRACT_FIRST, preferred_element_type=F32)
-            for a, small in zip(down_rows, smalls)
-        )
-        up_ref[...] = sum(
-            lax.dot_general(small[:, :ranks], a, CONTRACT_FIRST, preferred_element_type=F32)
-            for a, small in zip(up_rows, smalls)
-        )
-
+def transposed_times(left, right):
+    return lax.dot_general(left, right, CONTRACT_FIRST, preferred_element_type=F32)
+
+
+def own_gradient_kernel(table, early, late, small_early, small_late, down_ref, up_ref):
     @pl.when(table[0] == 0)
     def _():
-        grads = []
-        for at in range(replicas):
-            inverse = smalls[at][:, 2 * ranks : 2 * ranks + 1].astype(F32)
-            toward = smalls[at][:, 2 * ranks + 64 : 2 * ranks + 65].astype(F32)
-            grads.append(
-                (
-                    cotangent[at][...].astype(F32)
-                    + inverse * pulled[at][...].astype(F32)
-                    - toward * hidden[at][...].astype(F32)
-                ).astype(BF16)
-            )
-        products([a[...] for a in early], grads)
+        down_ref[...] = transposed_times(early[...], small_late[...])
+        up_ref[...] = transposed_times(small_early[...], late[...])
 
     @pl.when(table[0] == 1)
     def _():
-        scaled = [(a[...].astype(F32) * gain_ref[...]).astype(BF16) for a in hidden]
-        products(scaled, [a[...] for a in early])
-
-
-def gradients(table, gain_row, early, cotangent, pulled, hidden, smalls, ranks):
-    replicas = len(early)
-    rows, width = early[0].shape
+        down_ref[...] = transposed_times(late[...], small_early[...])
+        up_ref[...] = transposed_times(small_late[...], early[...])
+
+
+def other_gradient_kernel(
+    table, gain_ref, down_sum, up_sum, early, cotangent, pulled, hidden, small_early, small_late,
+    down_ref, up_ref,
+):
+    ranks = down_ref.shape[1]
+    late = small_late[:, :ranks]
+    inverse = small_late[:, ranks : ranks + 1].astype(F32)
+    toward = small_late[:, ranks + 64 : ranks + 65].astype(F32)
+
+    @pl.when(table[0] == 0)
+    def _():
+        grad = (
+            cotangent[...].astype(F32)
+            + inverse * pulled[...].astype(F32)
+            - toward * hidden[...].astype(F32)
+        ).astype(BF16)
+        down_ref[...] = down_sum[...] + transposed_times(early[...], late)
+        up_ref[...] = up_sum[...] + transposed_times(small_early[...], grad)
+
+    @pl.when(table[0] == 1)
+    def _():
+        scaled = (hidden[...].astype(F32) * gain_ref[...]).astype(BF16)
+        weighed = (small_early[...].astype(F32) * inverse).astype(BF16)
+        down_ref[...] = down_sum[...] + transposed_times(scaled, weighed)
+        up_ref[...] = up_sum[...] + transposed_times(late, early[...])
+
+
+def gradient_call(kernel, table, sums, by_column, whole, width, ranks, rows):
     tile = min(512, width)
-    columns = pl.BlockSpec((rows, tile), lambda step, table: (0, step))
-    small = pl.BlockSpec(smalls[0].shape, lambda step, table: (0, 0))
+    down_spec = pl.BlockSpec((tile, ranks), lambda step, table: (step, 0))
+    up_spec = pl.BlockSpec((ranks, tile), lambda step, table: (0, step))
+    leading = [array for array in by_column if array.shape[0] == 1]
+    columns = [array for array in by_column if array.shape[0] != 1]
     return pl.pallas_call(
-        functools.partial(gradient_kernel, replicas=replicas),
+        kernel,
         grid_spec=pltpu.PrefetchScalarGridSpec(
             num_scalar_prefetch=1,
             grid=(width // tile,),
-            in_specs=[pl.BlockSpec((1, tile), lambda step, table: (0, step))]
-            + [columns] * (4 * replicas)
-            + [small] * replicas,
-            out_specs=[
-                pl.BlockSpec((tile, ranks), lambda step, table: (step, 0)),
-                pl.BlockSpec((ranks, tile), lambda step, table: (0, step)),
-            ],
+            in_specs=[pl.BlockSpec((1, tile), lambda step, table: (0, step)) for _ in leading]
+            + [down_spec, up_spec][: len(sums)]
+            + [pl.BlockSpec((rows, tile), lambda step, table: (0, step)) for _ in columns]
+            + [pl.BlockSpec(array.shape, lambda step, table: (0, 0)) for array in whole],
+            out_specs=[down_spec, up_spec],
         ),
         out_shape=[
             jax.ShapeDtypeStruct((width, ranks), F32),
             jax.ShapeDtypeStruct((ranks, width), F32),
         ],
-        compiler_params=pltpu.CompilerParams(vmem_limit_bytes=24 * 1024 * 1024),
+        compiler_params=pltpu.CompilerParams(vmem_limit_bytes=20 * 1024 * 1024),
         cost_estimate=pl.CostEstimate(
-            flops=4 * replicas * rows * width * ranks,
-            bytes_accessed=8 * width * ranks + 8 * replicas * rows * width,
+            flops=4 * rows * width * ranks,
+            bytes_accessed=8 * width * ranks * (1 + len(sums) // 2) + 2 * rows * width * len(columns),
             transcendentals=0,
         ),
-    )(table, gain_row, *early, *cotangent, *pulled, *hidden, *smalls)
+    )(table, *leading, *sums, *columns, *whole)
 
 
 def orders(count):
@@ -235,6 +238,7 @@
     up = adapter_up_factors[0]
     rows, width = tokens.shape
     features = width * count
+    replicas = lax.axis_size("replica")
     ranks = down.shape[1]
 
     tenant_of_column = jnp.arange(ranks, dtype=jnp.int32) // (ranks // TENANT_COUNT)
@@ -270,26 +274,28 @@
         squares = jnp.pad(squares, (0, -rows % ranks)).reshape(-1, ranks)
         return jnp.concatenate([small, jnp.pad(squares, ((0, -len(squares) % 16), (0, 0)))], axis=0)
 
+    steps_left = doubling_steps()
+    small_sum = small_columns(early, tokens)
+    sent_first, small_sum = lax.optimization_barrier((cotangent, small_sum))
+    if steps_left:
+        small_sum = sum_step(small_sum, steps_left.pop(0))
+
     everyone = range(count)
     arrivals = [
         (
-            line(cotangent, [], [z for z in everyone if z + 1 < count], 1),
-            line(cotangent, [], [z for z in everyone if z > 0], -1),
+            line(sent_first, [], [z for z in everyone if z + 1 < count], 1),
+            line(sent_first, [], [z for z in everyone if z > 0], -1),
         )
     ]
     parts = []
-    small_sum = None
-    steps_left = doubling_steps()
     for stage in range(count):
         wanted = [None if stage == 0 else second_slots[z][stage] for z in everyone]
         cases = sorted({slot for slot in wanted if slot is not None})
         here = [early] + [arrivals[slot][side] for slot, side in cases]
-        if stage == 1:
-            small_sum = small_columns(*lax.optimization_barrier((early, tokens, *sent))[:2])
-        elif stage > 1 and steps_left:
-            small_sum = sum_step(small_sum, steps_left.pop(0))
-        if stage > 0:
+        if stage == 2:
             *here, small_sum = lax.optimization_barrier((*here, small_sum, *sent))[: len(here) + 1]
+        elif stage > 0:
+            here = lax.optimization_barrier((*here, *sent))[: len(here)]
         value = pick(
             place_of,
             [0] * count + [0 if slot is None else 1 + cases.index(slot) for slot in wanted],
@@ -297,10 +303,13 @@
         )
         order = [blocks[stage] for blocks in first_order + second_order]
         part = block_product(table, value, weight, order)
-        if stage == 0:
+        if steps_left:
+            part, small_sum = lax.optimization_barrier((part, small_sum))
+            small_sum = sum_step(small_sum, steps_left.pop(0))
+        if stage == 1:
             part, after = lax.optimization_barrier((part, early))
             early_all = [early] + with_other_replicas(after)[1:]
-        if stage == 2:
+        if stage == count - 1:
             part, *early_all = lax.optimization_barrier((part, *early_all))
         parts.append(part)
         slot = stage + 1
@@ -344,6 +353,9 @@
         small_sum[rows:].reshape(-1)[:rows][:, None] / features + EPSILON
     )
     small_early = (coefficients * small_sum[:rows]).astype(BF16)
+    small_early_all = with_other_replicas(
+        (small_early.astype(F32) * jnp.where(is_first, inv_first, 1.0)).astype(BF16)
+    )
     low_product = jnp.where(
         is_first,
         jnp.dot(small_early, up, preferred_element_type=F32),
@@ -352,7 +364,9 @@
 
     pulled_here = (gain_row * (sum(parts) + low_product)).astype(BF16)
     pulled = to_other_core(pulled_here, 1)
-    from_left, from_right, _ = lax.optimization_barrier((from_left, from_right, pulled_here))
+    from_left, from_right, *small_early_all, _ = lax.optimization_barrier(
+        (from_left, from_right, *small_early_all, pulled_here)
+    )
 
     projected = parts[-1] + from_left.astype(F32) + from_right.astype(F32) + low_product
     hidden = (token_float + inv_first * projected).astype(BF16)
@@ -369,16 +383,21 @@
     row_sums = jnp.stack(
         [jnp.sum(hidden_float * hidden_float, axis=1), jnp.sum(hidden_float * pulled_float, axis=1)]
     )
-    for step in doubling_steps():
-        row_sums = sum_step(row_sums, step, F32)
+    if count <= 4:
+        row_sums = row_sums + sum(
+            lax.ppermute(row_sums, "tensor", [(z, (z + step) % count) for z in everyone])
+            for step in range(1, count)
+        )
+    else:
+        for step in doubling_steps():
+            row_sums = sum_step(row_sums, step, F32)
     inv_second = lax.rsqrt(row_sums[0] / features + EPSILON)[:, None]
     toward_hidden = row_sums[1][:, None] * inv_second * inv_second * inv_second / features
     hidden_grad = cotangent.astype(F32) + inv_second * pulled_float - toward_hidden * hidden_float
-    rank_late = jnp.where(
-        is_first,
-        times_up_transposed(hidden_grad.astype(BF16)),
-        times_down((hidden_float * gain_row).astype(BF16)),
-    )
+    late = jnp.where(
+        is_first, hidden_grad.astype(BF16), (hidden_float * gain_row).astype(BF16)
+    )
+    rank_late = jnp.where(is_first, times_up_transposed(late), times_down(late))
     for step in doubling_steps():
         rank_late = sum_step(rank_late, step)
 
@@ -391,28 +410,36 @@
     ]
     pulled_all = [pulled] + swapped
 
-    row_scale = jnp.where(is_first, inv_first, inv_second)
-    small_late = coefficients * rank_late * row_scale
-    small_early = small_early.astype(F32) * row_scale
-    smalls = jnp.concatenate(
-        [
-            jnp.where(is_first, small_early, small_late),
-            jnp.where(is_first, small_late, small_early),
-            jnp.broadcast_to(inv_second, (rows, 64)),
-            jnp.broadcast_to(toward_hidden, (rows, 64)),
-        ],
-        axis=1,
+    small_late = (coefficients * rank_late * jnp.where(is_first, inv_first, inv_second)).astype(BF16)
+    small_late_all = with_other_replicas(
+        jnp.concatenate(
+            [
+                small_late,
+                jnp.broadcast_to(inv_second, (rows, 64)).astype(BF16),
+                jnp.broadcast_to(toward_hidden, (rows, 64)).astype(BF16),
+            ],
+            axis=1,
+        )
+    )
+    small_early_own = (
+        small_early.astype(F32) * jnp.where(is_first, inv_first, inv_second)
     ).astype(BF16)
-    grad_down, grad_up = gradients(
-        table,
-        gain_row,
-        early_all,
-        cotangent_all,
-        pulled_all,
-        hidden_all,
-        with_other_replicas(smalls),
-        ranks,
-    )
+    sums = gradient_call(
+        own_gradient_kernel,
+        table, [], [early, late], [small_early_own, small_late], width, ranks, rows,
+    )
+    for at in range(1, replicas):
+        sums = gradient_call(
+            other_gradient_kernel,
+            table,
+            sums,
+            [gain_row, early_all[at], cotangent_all[at], pulled_all[at], hidden_all[at]],
+            [small_early_all[at], small_late_all[at]],
+            width,
+            ranks,
+            rows,
+        )
+    grad_down, grad_up = sums
     return (grad_down[None], grad_up[None])
 
 

time: 113 us -> 115 us (1.018)
  waiting for transfers between devices: 39.4 us -> 30.5 us
  other arithmetic: 8.69 us -> 15.2 us
  starting transfers between devices: 32.1 us -> 35.8 us
    ppermute x6 -> x4, waiting for transfers between devices: 25.9 us -> 14.4 us  [sum_step(): return value + lax.ppermute(value.astype(wire), 'tensor', pairs).astype(F32)]
    ppermute x8, waiting for transfers between devices: 4 us -> 7.79 us  [line(): return lax.ppermute(value, ('tensor', 'section'), pairs)]
    ppermute x6 -> x4, starting transfers between devices: 9.89 us -> 6.46 us  [sum_step(): return value + lax.ppermute(value.astype(wire), 'tensor', pairs).astype(F32)]
    ppermute x3 -> x4, waiting for transfers between devices: 6.48 us -> 3.51 us  [with_other_replicas(): lax.ppermute(value, ('section', 'replica'), [(s * count + r, s * count +...]
    ppermute x0 -> x3, waiting for transfers between devices: none -> 2.96 us  [on_device(): lax.ppermute(row_sums, 'tensor', [(z, (z + step) % count) for z in everyo...]
    add x4 -> x2, other arithmetic: 0.06 us -> 2.62 us  [sum_step(): return value + lax.ppermute(value.astype(wire), 'tensor', pairs).astype(F32)]
    ppermute x1, starting transfers between devices: 0.07 us -> 2.5 us  [on_device(): lax.ppermute(jnp.where(is_first, hidden, other), 'section', swap)]
    ppermute x0 -> x3, starting transfers between devices: none -> 2.08 us  [on_device(): lax.ppermute(row_sums, 'tensor', [(z, (z + step) % count) for z in everyo...]
  transfers between devices with their start and end apart: 20 -> 22, of which waited for: 10 -> 13; matrix products, arithmetic and copies ran while one was open for 11% -> 12% of each run, Pallas kernels for 19% -> 20%
where the time goes in v9:
time: 115 us; the launch traced here: 114 us
  starting transfers between devices  35.8 us (31%)
  waiting for transfers between devices  30.5 us (27%)
  Pallas kernels  27.4 us (24%)
  other arithmetic  15.2 us (13%)
  matrix products  2.97 us (3%)
  local copies, waits for them, and re-layouts  1.2 us (1%)
    pallas_call x4, Pallas kernels, block_product(): pl.pallas_call(functools.partial(block_kernel, blocks=blocks, tile=tile,...  20.9 us
    ppermute x8, starting transfers between devices, line(): return lax.ppermute(value, ('tensor', 'section'), pairs)  17.2 us
    ppermute x4, waiting for transfers between devices, sum_step(): return value + lax.ppermute(value.astype(wire), 'tensor', pairs).astype(F32)  14.4 us
    ppermute x8, waiting for transfers between devices, line(): return lax.ppermute(value, ('tensor', 'section'), pairs)  7.79 us
    ppermute x4, starting transfers between devices, sum_step(): return value + lax.ppermute(value.astype(wire), 'tensor', pairs).astype(F32)  6.46 us
    pallas_call x2, Pallas kernels, gradient_call(): pl.pallas_call(kernel, grid_spec=pltpu.PrefetchScalarGridSpec(num_scalar_...  6.46 us
    ppermute x4, starting transfers between devices, with_other_replicas(): lax.ppermute(value, ('section', 'replica'), [(s * count + r, s * count +...  6.18 us
    convert_element_type x6, other arithmetic, on_device(): sent.append((arrived + jnp.where(is_first, own, 0.0)).astype(BF16))  4.13 us
  transfers between devices with their start and end apart: 22, of which 13 were waited for; matrix products, arithmetic and copies ran while one was open for 12% of the time, Pallas kernels for 20%

profile of v9, /device:TPU:0, one launch (start us, length us, event | category | flops | bytes accessed | tf_op | source)
XLA Modules:
  0.0 114.2 jit_solution(10072640096919784758)
XLA Ops:
  0.7 1.5 %fusion.4 = f32[192]{0:T(256)S(1)} fusion(bf16[192,2048]{1,0:T(8,128)(2,1)} %param.8), kind=kLoop, calls=%fused_computation.13 | loop fusion | flops 1179456 | bytes 787200 | tf_op jit(solution)/shard_map/reduce_sum | solution.py:273
  2.1 1.4 %fusion.19.value_ref.early = bf16[192,2048]{1,0:T(8,128)(2,1)S(1)} fusion(bf16[192,2048]{1,0:T(8,128)(2,1)} %param.9, bf16[192,2048]{1,0:T(8,128)(2,1)} %param.8, f32[2048]{0:T(1024)} %bitcast.38, pred[]{:T(512)S(6)} %eq.20), kind=kLoop, calls=%fused_computation.37 | loop fusion | flops 1572864 | bytes 2367489 | tf_op jit(solution)/shard_map/jit(_where)/select_n | solution.py:268
  5.3 1.6 %collective-permute-start.1 = (bf16[192,2048]{1,0:T(8,128)(2,1)}, bf16[192,2048]{1,0:T(8,128)(2,1)}, u32[]{:S(2)}, u32[]{:S(2)}) collective-permute-start(bf16[192,2048]{1,0:T(8,128)(2,1)} %param.9), channel_id=1, source_target_pairs={{2,6},{6,10},{10,14},{3,7},{7,11},{11,15},{18,22},{22,26},{26,30},... | collective-permute-start | bytes 2359304 | tf_op jit(solution)/shard_map/ppermute | solution.py:265
  6.9 1.6 %collective-permute-start = (bf16[192,2048]{1,0:T(8,128)(2,1)}, bf16[192,2048]{1,0:T(8,128)(2,1)}, u32[]{:S(2)}, u32[]{:S(2)}) collective-permute-start(bf16[192,2048]{1,0:T(8,128)(2,1)} %param.9), channel_id=1, source_target_pairs={{6,2},{10,6},{14,10},{7,3},{11,7},{15,11},{22,18},{26,22},{30,26},... | collective-permute-start | bytes 2359304 | tf_op jit(solution)/shard_map/ppermute | solution.py:265
  8.5 3.1 %collective-permute-start.2 = (bf16[208,256]{1,0:T(8,128)(2,1)S(1)}, bf16[208,256]{1,0:T(8,128)(2,1)}, u32[]{:S(2)}, u32[]{:S(2)}) collective-permute-start(bf16[208,256]{1,0:T(8,128)(2,1)S(1)} %convert_element_type.126), channel_id=1, source_target_pairs={{0,4},{4,0},{8,12},{12,8},{1,5},{5,1},{9,13},{13,9},{2,6},{6,2},{1... | collective-permute-start | bytes 319496 | tf_op jit(solution)/shard_map/ppermute | solution.py:202
  11.6 5.2 %shard_map.95 = f32[192,2048]{1,0:T(8,128)S(1)} custom-call(s32[2]{0:T(128)S(1)} %pad_add_fusion.table, bf16[192,2048]{1,0:T(8,128)(2,1)S(1)} %fusion.19.value_ref.early, bf16[2048,8192]{1,0:T(8,128)(2,1)} %bitcast.41), custom_call_target="tpu_custom_call" | custom-call | flops 6442450944 | bytes 8388608 | tf_op jit(solution)/shard_map/pallas_call | solution.py:72
  16.9 1.6 %convert_add_fusion.2 = f32[208,256]{1,0:T(8,128)} fusion(f32[208,256]{1,0:T(8,128)S(1)} %copy-done.6, bf16[208,256]{1,0:T(8,128)(2,1)} %collective-permute-done.2), kind=kLoop, calls=%fused_computation.52 | loop fusion | flops 106496 | bytes 532480 | tf_op jit(solution)/shard_map/add | solution.py:202
  19.4 2.6 %collective-permute-start.5 = (bf16[208,256]{1,0:T(8,128)(2,1)S(1)}, bf16[208,256]{1,0:T(8,128)(2,1)}, u32[]{:S(2)}, u32[]{:S(2)}) collective-permute-start(bf16[208,256]{1,0:T(8,128)(2,1)S(1)} %convert_element_type.131), channel_id=1, source_target_pairs={{0,8},{4,12},{8,0},{12,4},{1,9},{5,13},{9,1},{13,5},{2,10},{6,14},... | collective-permute-start | bytes 319496 | tf_op jit(solution)/shard_map/ppermute | solution.py:202
  22.2 4.3 %collective-permute-done.5 = bf16[208,256]{1,0:T(8,128)(2,1)} collective-permute-done((bf16[208,256]{1,0:T(8,128)(2,1)S(1)}, bf16[208,256]{1,0:T(8,128)(2,1)}, u32[]{:S(2)}, u32[]{:S(2)}) %collective-permute-start.5) | collective-permute-done | bytes 106528 | tf_op jit(solution)/shard_map/ppermute | solution.py:202
  27.6 1.4 %add_convert_fusion.5 = bf16[192,2048]{1,0:T(8,128)(2,1)S(1)} fusion(bf16[192,2048]{1,0:T(8,128)(2,1)} %collective-permute-done.1, f32[192,2048]{1,0:T(8,128)S(1)} %shard_map.95, pred[]{:T(512)S(6)} %eq.20), kind=kLoop, calls=%fused_computation.24 | loop fusion | flops 1572864 | bytes 3145729 | tf_op jit(solution)/shard_map/convert_element_type | solution.py:331
  29.0 2.5 %collective-permute-start.3 = (bf16[192,2048]{1,0:T(8,128)(2,1)S(1)}, bf16[192,2048]{1,0:T(8,128)(2,1)S(1)}, u32[]{:S(2)}, u32[]{:S(2)}) collective-permute-start(bf16[192,2048]{1,0:T(8,128)(2,1)S(1)} %add_convert_fusion.5), channel_id=1, source_target_pairs={{0,4},{6,10},{10,14},{1,5},{7,11},{11,15},{16,20},{22,26},{26,30},... | collective-permute-start | bytes 2359304 | tf_op jit(solution)/shard_map/ppermute | solution.py:265
  31.5 1.4 %add_convert_fusion.4 = bf16[192,2048]{1,0:T(8,128)(2,1)S(1)} fusion(bf16[192,2048]{1,0:T(8,128)(2,1)} %collective-permute-done, f32[192,2048]{1,0:T(8,128)S(1)} %shard_map.95, pred[]{:T(512)S(6)} %eq.20), kind=kLoop, calls=%fused_computation.23 | loop fusion | flops 1572864 | bytes 3145729 | tf_op jit(solution)/shard_map/convert_element_type | solution.py:331
  33.8 5.3 %shard_map.96 = f32[192,2048]{1,0:T(8,128)S(1)} custom-call(s32[2]{0:T(128)S(1)} %pad_add_fusion.table, bf16[192,2048]{1,0:T(8,128)(2,1)S(1)} %select_select_fusion.2.value_ref, bf16[2048,8192]{1,0:T(8,128)(2,1)} %bitcast.42), custom_call_target="tpu_custom_call" | custom-call | flops 6442450944 | bytes 8388608 | tf_op jit(solution)/shard_map/pallas_call | solution.py:72
  39.0 1.5 %collective-permute-start.8 = (bf16[192,2048]{1,0:T(8,128)(2,1)S(1)}, bf16[192,2048]{1,0:T(8,128)(2,1)S(1)}, u32[]{:S(2)}, u32[]{:S(2)}) collective-permute-start(bf16[192,2048]{1,0:T(8,128)(2,1)S(1)} %fusion.19.value_ref.early), channel_id=1, source_target_pairs={{0,1},{1,0},{2,3},{3,2},{4,5},{5,4},{6,7},{7,6},{8,9},{9,8},{10,11... | collective-permute-start | bytes 2359304 | tf_op jit(solution)/shard_map/ppermute | solution.py:208
  41.3 4.4 %collective-permute-start.6 = (bf16[192,2048]{1,0:T(8,128)(2,1)S(1)}, bf16[192,2048]{1,0:T(8,128)(2,1)S(1)}, u32[]{:S(2)}, u32[]{:S(2)}) collective-permute-start(bf16[192,2048]{1,0:T(8,128)(2,1)S(1)} %add_convert_fusion.3), channel_id=1, source_target_pairs={{0,4},{4,8},{10,14},{1,5},{5,9},{11,15},{16,20},{20,24},{26,30},{1... | collective-permute-start | bytes 2359304 | tf_op jit(solution)/shard_map/ppermute | solution.py:265
  47.1 1.5 %collective-permute-start.11 = (bf16[192,256]{1,0:T(8,128)(2,1)S(1)}, bf16[192,256]{1,0:T(8,128)(2,1)S(1)}, u32[]{:S(2)}, u32[]{:S(2)}) collective-permute-start(bf16[192,256]{1,0:T(8,128)(2,1)S(1)} %get-tuple-element.75), channel_id=1, source_target_pairs={{0,1},{1,0},{2,3},{3,2},{4,5},{5,4},{6,7},{7,6},{8,9},{9,8},{10,11... | collective-permute-start | bytes 294920 | tf_op jit(solution)/shard_map/ppermute | solution.py:208
  48.9 5.2 %shard_map.97 = f32[192,2048]{1,0:T(8,128)S(1)} custom-call(s32[2]{0:T(128)S(1)} %pad_add_fusion.table, bf16[192,2048]{1,0:T(8,128)(2,1)S(1)} %select_select_fusion.1.value_ref, bf16[2048,8192]{1,0:T(8,128)(2,1)} %bitcast.43), custom_call_target="tpu_custom_call" | custom-call | flops 6442450944 | bytes 8388608 | tf_op jit(solution)/shard_map/pallas_call | solution.py:72
  55.6 4.4 %collective-permute-start.9 = (bf16[192,2048]{1,0:T(8,128)(2,1)S(1)}, bf16[192,2048]{1,0:T(8,128)(2,1)S(1)}, u32[]{:S(2)}, u32[]{:S(2)}) collective-permute-start(bf16[192,2048]{1,0:T(8,128)(2,1)S(1)} %add_convert_fusion.1), channel_id=1, source_target_pairs={{0,4},{4,8},{8,12},{1,5},{5,9},{9,13},{16,20},{20,24},{24,28},{17,... | collective-permute-start | bytes 2359304 | tf_op jit(solution)/shard_map/ppermute | solution.py:265
  61.9 5.3 %shard_map.98 = f32[192,2048]{1,0:T(8,128)S(1)} custom-call(s32[2]{0:T(128)S(1)} %pad_add_fusion.table, bf16[192,2048]{1,0:T(8,128)(2,1)S(1)} %select_select_fusion.value_ref, bf16[2048,8192]{1,0:T(8,128)(2,1)} %bitcast.44), custom_call_target="tpu_custom_call" | custom-call | flops 6442450944 | bytes 8388608 | tf_op jit(solution)/shard_map/pallas_call | solution.py:72
  69.5 6.6 %collective-permute-done.10 = bf16[192,2048]{1,0:T(8,128)(2,1)S(1)} collective-permute-done((bf16[192,2048]{1,0:T(8,128)(2,1)S(1)}, bf16[192,2048]{1,0:T(8,128)(2,1)S(1)}, u32[]{:S(2)}, u32[]{:S(2)}) %collective-permute-start.10) | collective-permute-done | bytes 786464 | tf_op jit(solution)/shard_map/ppermute | solution.py:265
  77.1 2.5 %collective-permute-start.12 = (bf16[192,2048]{1,0:T(8,128)(2,1)S(1)}, bf16[192,2048]{1,0:T(8,128)(2,1)S(1)}, u32[]{:S(2)}, u32[]{:S(2)}) collective-permute-start(bf16[192,2048]{1,0:T(8,128)(2,1)S(1)} %broadcast_select_fusion.3), channel_id=1, source_target_pairs={{0,2},{2,0},{1,3},{3,1},{4,6},{6,4},{5,7},{7,5},{8,10},{10,8},{9,1... | collective-permute-start | bytes 2359304 | tf_op jit(solution)/shard_map/ppermute | solution.py:376
  80.2 1.4 %collective-permute-done.12.cotangent = bf16[192,2048]{1,0:T(8,128)(2,1)S(1)} collective-permute-done((bf16[192,2048]{1,0:T(8,128)(2,1)S(1)}, bf16[192,2048]{1,0:T(8,128)(2,1)S(1)}, u32[]{:S(2)}, u32[]{:S(2)}) %collective-permute-start.12) | collective-permute-done | bytes 786464 | tf_op jit(solution)/shard_map/ppermute | solution.py:376
  82.1 2.0 %collective-permute-start.14 = (f32[2,192]{1,0:T(2,128)S(1)}, f32[2,192]{1,0:T(2,128)S(1)}, u32[]{:S(2)}, u32[]{:S(2)}) collective-permute-start(f32[2,192]{1,0:T(2,128)S(1)} %pad_maximum_fusion.1), channel_id=1, source_target_pairs={{0,4},{4,8},{8,12},{12,0},{1,5},{5,9},{9,13},{13,1},{2,6},{6,10},{... | collective-permute-start | bytes 4616 | tf_op jit(solution)/shard_map/ppermute | solution.py:388
  84.2 1.5 %collective-permute-start.19 = (bf16[192,2048]{1,0:T(8,128)(2,1)S(1)}, bf16[192,2048]{1,0:T(8,128)(2,1)S(1)}, u32[]{:S(2)}, u32[]{:S(2)}) collective-permute-start(bf16[192,2048]{1,0:T(8,128)(2,1)S(1)} %get-tuple-element.70), channel_id=1, source_target_pairs={{0,1},{1,0},{2,3},{3,2},{4,5},{5,4},{6,7},{7,6},{8,9},{9,8},{10,11... | collective-permute-start | bytes 2359304 | tf_op jit(solution)/shard_map/ppermute | solution.py:208
  85.7 2.0 %collective-permute-done.14 = f32[2,192]{1,0:T(2,128)S(1)} collective-permute-done((f32[2,192]{1,0:T(2,128)S(1)}, f32[2,192]{1,0:T(2,128)S(1)}, u32[]{:S(2)}, u32[]{:S(2)}) %collective-permute-start.14) | collective-permute-done | bytes 1568 | tf_op jit(solution)/shard_map/ppermute | solution.py:388
  88.7 1.7 %fusion.18.late = bf16[192,2048]{1,0:T(8,128)(2,1)S(1)} fusion(bf16[192,2048]{1,0:T(8,128)(2,1)S(1)} %get-tuple-element.74, bf16[192,2048]{1,0:T(8,128)(2,1)S(1)} %collective-permute-done.13, bf16[192,2048]{1,0:T(8,128)(2,1)} %param.9, f32[192]{0:T(256)S(1)} %get-tuple-element.69, f32[192]{0:T(256)S(1)} %bitcast.52, f32[2048]{0:T(1024)S(1)} %bitcast.40, ...), kind=kLoop, calls=%fused_computation.36 | loop fusion | flops 4325376 | bytes 3155457 | tf_op jit(solution)/shard_map/jit(_where)/select_n | solution.py:397
  91.4 4.6 %collective-permute-done.17 = bf16[192,256]{1,0:T(8,128)(2,1)S(1)} collective-permute-done((bf16[192,256]{1,0:T(8,128)(2,1)S(1)}, bf16[192,256]{1,0:T(8,128)(2,1)S(1)}, u32[]{:S(2)}, u32[]{:S(2)}) %collective-permute-start.17) | collective-permute-done | bytes 98336 | tf_op jit(solution)/shard_map/ppermute | solution.py:202
  96.7 5.4 %collective-permute-done.18 = bf16[192,256]{1,0:T(8,128)(2,1)S(1)} collective-permute-done((bf16[192,256]{1,0:T(8,128)(2,1)S(1)}, bf16[192,256]{1,0:T(8,128)(2,1)S(1)}, u32[]{:S(2)}, u32[]{:S(2)}) %collective-permute-start.18) | collective-permute-done | bytes 98336 | tf_op jit(solution)/shard_map/ppermute | solution.py:202
  103.7 1.6 %collective-permute-start.21 = (bf16[192,384]{1,0:T(8,128)(2,1)S(1)}, bf16[192,384]{1,0:T(8,128)(2,1)S(1)}, u32[]{:S(2)}, u32[]{:S(2)}) collective-permute-start(bf16[192,384]{1,0:T(8,128)(2,1)S(1)} %pad_maximum_fusion), channel_id=1, source_target_pairs={{0,1},{1,0},{2,3},{3,2},{4,5},{5,4},{6,7},{7,6},{8,9},{9,8},{10,11... | collective-permute-start | bytes 442376 | tf_op jit(solution)/shard_map/ppermute | solution.py:208
  105.3 2.3 %shard_map.99 = (f32[2048,256]{1,0:T(8,128)S(1)}, f32[256,2048]{1,0:T(8,128)S(1)}) custom-call(s32[2]{0:T(128)S(1)} %pad_add_fusion.table, bf16[192,2048]{1,0:T(8,128)(2,1)S(1)} %fusion.19.value_ref.early, bf16[192,2048]{1,0:T(8,128)(2,1)S(1)} %fusion.18.late, bf16[192,256]{1,0:T(8,128)(2,1)S(1)} %get-tuple-element.81.small_early, ...), custom_call_target="tpu_custom_call" | custom-call | flops 402653184 | bytes 5767168 | tf_op jit(solution)/shard_map/pallas_call | solution.py:145
  107.7 2.3 %collective-permute-done.21.small_late = bf16[192,384]{1,0:T(8,128)(2,1)S(1)} collective-permute-done((bf16[192,384]{1,0:T(8,128)(2,1)S(1)}, bf16[192,384]{1,0:T(8,128)(2,1)S(1)}, u32[]{:S(2)}, u32[]{:S(2)}) %collective-permute-start.21) | collective-permute-done | bytes 147488 | tf_op jit(solution)/shard_map/ppermute | solution.py:208
  110.0 4.2 %shard_map.100 = (f32[2048,256]{1,0:T(8,128)}, f32[256,2048]{1,0:T(8,128)}) custom-call(s32[2]{0:T(128)S(1)} %pad_add_fusion.table, f32[1,2048]{1,0:T(1,128)S(1)} %copy-done.1, f32[2048,256]{1,0:T(8,128)S(1)} %get-tuple-element.60.down_sum, f32[256,2048]{1,0:T(8,128)S(1)} %get-tuple-element.61.up_sum, bf16[192,2048]{1,0:T(8,128)(2,1)S(1)} %collective-permute-done.8.early, ...), custom_call_target="tpu_custom_call" | custom-call | flops 402653184 | bytes 11534336 | tf_op jit(solution)/shard_map/pallas_call | solution.py:145
  (82 shorter events, 19.1 us)
Async XLA Ops:
  0.6 2.9 %copy-start = (bf16[1,2048,256]{2,1,0:T(8,128)(2,1)S(1)}, bf16[1,2048,256]{2,1,0:T(8,128)(2,1)}, u32[]{:S(2)}) copy-start(bf16[1,2048,256]{2,1,0:T(8,128)(2,1)} %param.12) | copy-start | bytes 3145732
  3.5 1.2 %copy-start.2 = (bf16[1,256,2048]{2,1,0:T(8,128)(2,1)S(1)}, bf16[1,256,2048]{2,1,0:T(8,128)(2,1)}, u32[]{:S(2)}) copy-start(bf16[1,256,2048]{2,1,0:T(8,128)(2,1)} %param.13) | copy-start | bytes 3145732
  5.3 6.4 %copy-start.5 = (f32[208,256]{1,0:T(8,128)}, f32[208,256]{1,0:T(8,128)S(1)}, u32[]{:S(2)}) copy-start(f32[208,256]{1,0:T(8,128)S(1)} %select_maximum_fusion) | copy-start | bytes 638980
  5.3 22.3 %collective-permute-start.1 = (bf16[192,2048]{1,0:T(8,128)(2,1)}, bf16[192,2048]{1,0:T(8,128)(2,1)}, u32[]{:S(2)}, u32[]{:S(2)}) collective-permute-start(bf16[192,2048]{1,0:T(8,128)(2,1)} %param.9), channel_id=1, source_target_pairs={{2,6},{6,10},{10,14},{3,7},{7,11},{11,15},{18,22},{22,26},{26,30},... | collective-permute-start | bytes 2359304 | tf_op jit(solution)/shard_map/ppermute | solution.py:265
  6.9 24.6 %collective-permute-start = (bf16[192,2048]{1,0:T(8,128)(2,1)}, bf16[192,2048]{1,0:T(8,128)(2,1)}, u32[]{:S(2)}, u32[]{:S(2)}) collective-permute-start(bf16[192,2048]{1,0:T(8,128)(2,1)} %param.9), channel_id=1, source_target_pairs={{6,2},{10,6},{14,10},{7,3},{11,7},{15,11},{22,18},{26,22},{30,26},... | collective-permute-start | bytes 2359304 | tf_op jit(solution)/shard_map/ppermute | solution.py:265
  8.5 8.4 %collective-permute-start.2 = (bf16[208,256]{1,0:T(8,128)(2,1)S(1)}, bf16[208,256]{1,0:T(8,128)(2,1)}, u32[]{:S(2)}, u32[]{:S(2)}) collective-permute-start(bf16[208,256]{1,0:T(8,128)(2,1)S(1)} %convert_element_type.126), channel_id=1, source_target_pairs={{0,4},{4,0},{8,12},{12,8},{1,5},{5,1},{9,13},{13,9},{2,6},{6,2},{1... | collective-permute-start | bytes 319496 | tf_op jit(solution)/shard_map/ppermute | solution.py:202
  11.6 5.2 %copy-start.6 = (f32[208,256]{1,0:T(8,128)S(1)}, f32[208,256]{1,0:T(8,128)}, u32[]{:S(2)}) copy-start(f32[208,256]{1,0:T(8,128)} %copy-done.5) | copy-start | bytes 638980
  11.6 10.4 %copy-start.8 = (f32[4]{0:T(128)S(1)}, f32[4]{0:T(128)}, u32[]{:S(2)}) copy-start(f32[4]{0:T(128)} %param.14) | copy-start | bytes 52
  19.4 7.1 %collective-permute-start.5 = (bf16[208,256]{1,0:T(8,128)(2,1)S(1)}, bf16[208,256]{1,0:T(8,128)(2,1)}, u32[]{:S(2)}, u32[]{:S(2)}) collective-permute-start(bf16[208,256]{1,0:T(8,128)(2,1)S(1)} %convert_element_type.131), channel_id=1, source_target_pairs={{0,8},{4,12},{8,0},{12,4},{1,9},{5,13},{9,1},{13,5},{2,10},{6,14},... | collective-permute-start | bytes 319496 | tf_op jit(solution)/shard_map/ppermute | solution.py:202
  29.0 11.9 %collective-permute-start.3 = (bf16[192,2048]{1,0:T(8,128)(2,1)S(1)}, bf16[192,2048]{1,0:T(8,128)(2,1)S(1)}, u32[]{:S(2)}, u32[]{:S(2)}) collective-permute-start(bf16[192,2048]{1,0:T(8,128)(2,1)S(1)} %add_convert_fusion.5), channel_id=1, source_target_pairs={{0,4},{6,10},{10,14},{1,5},{7,11},{11,15},{16,20},{22,26},{26,30},... | collective-permute-start | bytes 2359304 | tf_op jit(solution)/shard_map/ppermute | solution.py:265
  32.9 12.9 %collective-permute-start.4 = (bf16[192,2048]{1,0:T(8,128)(2,1)S(1)}, bf16[192,2048]{1,0:T(8,128)(2,1)S(1)}, u32[]{:S(2)}, u32[]{:S(2)}) collective-permute-start(bf16[192,2048]{1,0:T(8,128)(2,1)S(1)} %add_convert_fusion.4), channel_id=1, source_target_pairs={{12,8},{6,2},{10,6},{13,9},{7,3},{11,7},{28,24},{22,18},{26,22},{2... | collective-permute-start | bytes 2359304 | tf_op jit(solution)/shard_map/ppermute | solution.py:265
  39.0 28.2 %collective-permute-start.8 = (bf16[192,2048]{1,0:T(8,128)(2,1)S(1)}, bf16[192,2048]{1,0:T(8,128)(2,1)S(1)}, u32[]{:S(2)}, u32[]{:S(2)}) collective-permute-start(bf16[192,2048]{1,0:T(8,128)(2,1)S(1)} %fusion.19.value_ref.early), channel_id=1, source_target_pairs={{0,1},{1,0},{2,3},{3,2},{4,5},{5,4},{6,7},{7,6},{8,9},{9,8},{10,11... | collective-permute-start | bytes 2359304 | tf_op jit(solution)/shard_map/ppermute | solution.py:208
  41.3 5.6 %copy-start.7 = (s32[192]{0:T(256)S(1)}, s32[192]{0:T(256)}, u32[]{:S(2)}) copy-start(s32[192]{0:T(256)} %param.15) | copy-start | bytes 2308
  41.3 13.9 %collective-permute-start.6 = (bf16[192,2048]{1,0:T(8,128)(2,1)S(1)}, bf16[192,2048]{1,0:T(8,128)(2,1)S(1)}, u32[]{:S(2)}, u32[]{:S(2)}) collective-permute-start(bf16[192,2048]{1,0:T(8,128)(2,1)S(1)} %add_convert_fusion.3), channel_id=1, source_target_pairs={{0,4},{4,8},{10,14},{1,5},{5,9},{11,15},{16,20},{20,24},{26,30},{1... | collective-permute-start | bytes 2359304 | tf_op jit(solution)/shard_map/ppermute | solution.py:265
  46.2 13.8 %collective-permute-start.7 = (bf16[192,2048]{1,0:T(8,128)(2,1)S(1)}, bf16[192,2048]{1,0:T(8,128)(2,1)S(1)}, u32[]{:S(2)}, u32[]{:S(2)}) collective-permute-start(bf16[192,2048]{1,0:T(8,128)(2,1)S(1)} %add_convert_fusion.2), channel_id=1, source_target_pairs={{8,4},{12,8},{6,2},{9,5},{13,9},{7,3},{24,20},{28,24},{22,18},{25,... | collective-permute-start | bytes 2359304 | tf_op jit(solution)/shard_map/ppermute | solution.py:265
  47.1 22.3 %collective-permute-start.11 = (bf16[192,256]{1,0:T(8,128)(2,1)S(1)}, bf16[192,256]{1,0:T(8,128)(2,1)S(1)}, u32[]{:S(2)}, u32[]{:S(2)}) collective-permute-start(bf16[192,256]{1,0:T(8,128)(2,1)S(1)} %get-tuple-element.75), channel_id=1, source_target_pairs={{0,1},{1,0},{2,3},{3,2},{4,5},{5,4},{6,7},{7,6},{8,9},{9,8},{10,11... | collective-permute-start | bytes 294920 | tf_op jit(solution)/shard_map/ppermute | solution.py:208
  48.9 5.2 %copy-start.3 = (bf16[1,256,2048]{2,1,0:T(8,128)(2,1)S(1)}, bf16[1,256,2048]{2,1,0:T(8,128)(2,1)}, u32[]{:S(2)}) copy-start(bf16[1,256,2048]{2,1,0:T(8,128)(2,1)} %param.13) | copy-start | bytes 3145732
  55.6 13.9 %collective-permute-start.9 = (bf16[192,2048]{1,0:T(8,128)(2,1)S(1)}, bf16[192,2048]{1,0:T(8,128)(2,1)S(1)}, u32[]{:S(2)}, u32[]{:S(2)}) collective-permute-start(bf16[192,2048]{1,0:T(8,128)(2,1)S(1)} %add_convert_fusion.1), channel_id=1, source_target_pairs={{0,4},{4,8},{8,12},{1,5},{5,9},{9,13},{16,20},{20,24},{24,28},{17,... | collective-permute-start | bytes 2359304 | tf_op jit(solution)/shard_map/ppermute | solution.py:265
  60.3 15.8 %collective-permute-start.10 = (bf16[192,2048]{1,0:T(8,128)(2,1)S(1)}, bf16[192,2048]{1,0:T(8,128)(2,1)S(1)}, u32[]{:S(2)}, u32[]{:S(2)}) collective-permute-start(bf16[192,2048]{1,0:T(8,128)(2,1)S(1)} %add_convert_fusion), channel_id=1, source_target_pairs={{4,0},{8,4},{12,8},{5,1},{9,5},{13,9},{20,16},{24,20},{28,24},{21,... | collective-permute-start | bytes 2359304 | tf_op jit(solution)/shard_map/ppermute | solution.py:265
  61.9 5.3 %copy-start.1 = (f32[1,2048]{1,0:T(1,128)S(1)}, f32[1,2048]{1,0:T(1,128)}, u32[]{:S(2)}) copy-start(f32[1,2048]{1,0:T(1,128)} %gain_ref.1) | copy-start | bytes 24580
  67.2 8.9 %copy-start.4 = (bf16[192,2048]{1,0:T(8,128)(2,1)S(1)}, bf16[192,2048]{1,0:T(8,128)(2,1)}, u32[]{:S(2)}) copy-start(bf16[192,2048]{1,0:T(8,128)(2,1)} %param.8) | copy-start | bytes 2359300
  68.0 12.1 %collective-permute-start.13 = (bf16[192,2048]{1,0:T(8,128)(2,1)S(1)}, bf16[192,2048]{1,0:T(8,128)(2,1)S(1)}, u32[]{:S(2)}, u32[]{:S(2)}) collective-permute-start(bf16[192,2048]{1,0:T(8,128)(2,1)S(1)} %get-tuple-element.83), channel_id=1, source_target_pairs={{2,0},{3,1},{6,4},{7,5},{10,8},{11,9},{14,12},{15,13},{18,16},{19,... | collective-permute-start | bytes 2359304 | tf_op jit(solution)/shard_map/ppermute | solution.py:218
  77.1 4.4 %collective-permute-start.12 = (bf16[192,2048]{1,0:T(8,128)(2,1)S(1)}, bf16[192,2048]{1,0:T(8,128)(2,1)S(1)}, u32[]{:S(2)}, u32[]{:S(2)}) collective-permute-start(bf16[192,2048]{1,0:T(8,128)(2,1)S(1)} %broadcast_select_fusion.3), channel_id=1, source_target_pairs={{0,2},{2,0},{1,3},{3,1},{4,6},{6,4},{5,7},{7,5},{8,10},{10,8},{9,1... | collective-permute-start | bytes 2359304 | tf_op jit(solution)/shard_map/ppermute | solution.py:376
  82.1 3.6 %collective-permute-start.16 = (f32[2,192]{1,0:T(2,128)S(1)}, f32[2,192]{1,0:T(2,128)S(1)}, u32[]{:S(2)}, u32[]{:S(2)}) collective-permute-start(f32[2,192]{1,0:T(2,128)S(1)} %pad_maximum_fusion.1), channel_id=1, source_target_pairs={{0,12},{4,0},{8,4},{12,8},{1,13},{5,1},{9,5},{13,9},{2,14},{6,2},{... | collective-permute-start | bytes 4616 | tf_op jit(solution)/shard_map/ppermute | solution.py:388
  82.1 5.6 %collective-permute-start.14 = (f32[2,192]{1,0:T(2,128)S(1)}, f32[2,192]{1,0:T(2,128)S(1)}, u32[]{:S(2)}, u32[]{:S(2)}) collective-permute-start(f32[2,192]{1,0:T(2,128)S(1)} %pad_maximum_fusion.1), channel_id=1, source_target_pairs={{0,4},{4,8},{8,12},{12,0},{1,5},{5,9},{9,13},{13,1},{2,6},{6,10},{... | collective-permute-start | bytes 4616 | tf_op jit(solution)/shard_map/ppermute | solution.py:388
  84.2 4.5 %collective-permute-start.15 = (f32[2,192]{1,0:T(2,128)S(1)}, f32[2,192]{1,0:T(2,128)S(1)}, u32[]{:S(2)}, u32[]{:S(2)}) collective-permute-start(f32[2,192]{1,0:T(2,128)S(1)} %pad_maximum_fusion.1), channel_id=1, source_target_pairs={{0,8},{4,12},{8,0},{12,4},{1,9},{5,13},{9,1},{13,5},{2,10},{6,14},... | collective-permute-start | bytes 4616 | tf_op jit(solution)/shard_map/ppermute | solution.py:388
  84.2 19.2 %collective-permute-start.19 = (bf16[192,2048]{1,0:T(8,128)(2,1)S(1)}, bf16[192,2048]{1,0:T(8,128)(2,1)S(1)}, u32[]{:S(2)}, u32[]{:S(2)}) collective-permute-start(bf16[192,2048]{1,0:T(8,128)(2,1)S(1)} %get-tuple-element.70), channel_id=1, source_target_pairs={{0,1},{1,0},{2,3},{3,2},{4,5},{5,4},{6,7},{7,6},{8,9},{9,8},{10,11... | collective-permute-start | bytes 2359304 | tf_op jit(solution)/shard_map/ppermute | solution.py:208
  91.4 4.7 %collective-permute-start.17 = (bf16[192,256]{1,0:T(8,128)(2,1)S(1)}, bf16[192,256]{1,0:T(8,128)(2,1)S(1)}, u32[]{:S(2)}, u32[]{:S(2)}) collective-permute-start(bf16[192,256]{1,0:T(8,128)(2,1)S(1)} %get-tuple-element.85), channel_id=1, source_target_pairs={{0,4},{4,0},{8,12},{12,8},{1,5},{5,1},{9,13},{13,9},{2,6},{6,2},{1... | collective-permute-start | bytes 294920 | tf_op jit(solution)/shard_map/ppermute | solution.py:202
  96.1 6.1 %collective-permute-start.18 = (bf16[192,256]{1,0:T(8,128)(2,1)S(1)}, bf16[192,256]{1,0:T(8,128)(2,1)S(1)}, u32[]{:S(2)}, u32[]{:S(2)}) collective-permute-start(bf16[192,256]{1,0:T(8,128)(2,1)S(1)} %fusion.25), channel_id=1, source_target_pairs={{0,8},{4,12},{8,0},{12,4},{1,9},{5,13},{9,1},{13,5},{2,10},{6,14},... | collective-permute-start | bytes 294920 | tf_op jit(solution)/shard_map/ppermute | solution.py:202
  103.4 4.2 %collective-permute-start.20 = (bf16[192,2048]{1,0:T(8,128)(2,1)S(1)}, bf16[192,2048]{1,0:T(8,128)(2,1)S(1)}, u32[]{:S(2)}, u32[]{:S(2)}) collective-permute-start(bf16[192,2048]{1,0:T(8,128)(2,1)S(1)} %collective-permute-done.19), channel_id=1, source_target_pairs={{0,2},{2,0},{1,3},{3,1},{4,6},{6,4},{5,7},{7,5},{8,10},{10,8},{9,1... | collective-permute-start | bytes 2359304 | tf_op jit(solution)/shard_map/ppermute | solution.py:405
  103.7 6.3 %collective-permute-start.21 = (bf16[192,384]{1,0:T(8,128)(2,1)S(1)}, bf16[192,384]{1,0:T(8,128)(2,1)S(1)}, u32[]{:S(2)}, u32[]{:S(2)}) collective-permute-start(bf16[192,384]{1,0:T(8,128)(2,1)S(1)} %pad_maximum_fusion), channel_id=1, source_target_pairs={{0,1},{1,0},{2,3},{3,2},{4,5},{5,4},{6,7},{7,6},{8,9},{9,8},{10,11... | collective-permute-start | bytes 442376 | tf_op jit(solution)/shard_map/ppermute | solution.py:208

commit v10 on v9

--- a/solution.py
+++ b/solution.py
@@ -198,8 +198,11 @@
     ]
 
 
-def sum_step(value, pairs, wire=BF16):
-    return value + lax.ppermute(value.astype(wire), "tensor", pairs).astype(F32)
+def sum_step(value, pairs, wire=BF16, after=()):
+    other = lax.ppermute(value.astype(wire), "tensor", pairs)
+    if after:
+        other = lax.optimization_barrier((other, *after))[0]
+    return value + other.astype(F32)
 
 
 def with_other_replicas(value, sections=(0, 1)):
@@ -274,17 +277,16 @@
         squares = jnp.pad(squares, (0, -rows % ranks)).reshape(-1, ranks)
         return jnp.concatenate([small, jnp.pad(squares, ((0, -len(squares) % 16), (0, 0)))], axis=0)
 
+    everyone = range(count)
     steps_left = doubling_steps()
-    small_sum = small_columns(early, tokens)
-    sent_first, small_sum = lax.optimization_barrier((cotangent, small_sum))
-    if steps_left:
-        small_sum = sum_step(small_sum, steps_left.pop(0))
-
-    everyone = range(count)
     arrivals = [
         (
-            line(sent_first, [], [z for z in everyone if z + 1 < count], 1),
-            line(sent_first, [], [z for z in everyone if z > 0], -1),
+            lax.ppermute(
+                cotangent,
+                ("tensor", "section"),
+                [(2 * z, 2 * (z + 1) + 1) for z in everyone if z + 1 < count],
+            ),
+            line(cotangent, [], [z for z in everyone if z > 0], -1),
         )
     ]
     parts = []
@@ -292,10 +294,12 @@
         wanted = [None if stage == 0 else second_slots[z][stage] for z in everyone]
         cases = sorted({slot for slot in wanted if slot is not None})
         here = [early] + [arrivals[slot][side] for slot, side in cases]
-        if stage == 2:
+        if stage == 1:
+            small_sum = small_columns(*lax.optimization_barrier((early, tokens, *sent))[:2])
+        elif stage > 1 and steps_left:
+            small_sum = sum_step(small_sum, steps_left.pop(0), after=sent)
+        if stage > 0:
             *here, small_sum = lax.optimization_barrier((*here, small_sum, *sent))[: len(here) + 1]
-        elif stage > 0:
-            here = lax.optimization_barrier((*here, *sent))[: len(here)]
         value = pick(
             place_of,
             [0] * count + [0 if slot is None else 1 + cases.index(slot) for slot in wanted],
@@ -303,9 +307,6 @@
         )
         order = [blocks[stage] for blocks in first_order + second_order]
         part = block_product(table, value, weight, order)
-        if steps_left:
-            part, small_sum = lax.optimization_barrier((part, small_sum))
-            small_sum = sum_step(small_sum, steps_left.pop(0))
         if stage == 1:
             part, after = lax.optimization_barrier((part, early))
             early_all = [early] + with_other_replicas(after)[1:]

time: 115 us -> 104 us (0.904)
  waiting for transfers between devices: 30.5 us -> 22.6 us
  other arithmetic: 15.2 us -> 9.33 us
  starting transfers between devices: 35.8 us -> 39.9 us
    ppermute x4 -> x5, starting transfers between devices: 6.46 us -> 13.2 us  [the longest x4 7.8 us: sum_step(): other = lax.ppermute(value.astype(wire), 'tensor', pairs)]
    ppermute x8 -> x7, waiting for transfers between devices: 7.79 us -> 1.07 us  [line(): return lax.ppermute(value, ('tensor', 'section'), pairs)]
    ppermute x4 -> x5, waiting for transfers between devices: 14.4 us -> 8.72 us  [the longest x4 8.29 us: sum_step(): other = lax.ppermute(value.astype(wire), 'tensor', pairs)]
    ppermute x4, waiting for transfers between devices: 3.51 us -> 8.43 us  [with_other_replicas(): lax.ppermute(value, ('section', 'replica'), [(s * count + r, s * count +...]
    add x2, other arithmetic: 2.62 us -> 0.04 us  [sum_step(): return value + other.astype(F32)]
    ppermute x1, starting transfers between devices: 2.5 us -> 0.07 us  [on_device(): lax.ppermute(jnp.where(is_first, hidden, other), 'section', swap)]
    ppermute x4, starting transfers between devices: 6.18 us -> 3.91 us  [with_other_replicas(): lax.ppermute(value, ('section', 'replica'), [(s * count + r, s * count +...]
    ppermute x3, starting transfers between devices: 2.08 us -> 4.12 us  [on_device(): lax.ppermute(row_sums, 'tensor', [(z, (z + step) % count) for z in everyo...]
  transfers between devices with their start and end apart: 22 -> 22, of which waited for: 13 -> 10; matrix products, arithmetic and copies ran while one was open for 12% -> 12% of each run, Pallas kernels for 20% -> 22%
where the time goes in v10:
time: 104 us
  starting transfers between devices  39.9 us (38%)
  Pallas kernels  27.3 us (26%)
  waiting for transfers between devices  22.6 us (22%)
  other arithmetic  9.33 us (9%)
  matrix products  2.96 us (3%)
  between operations  1.16 us (1%)
    pallas_call x4, Pallas kernels, block_product(): pl.pallas_call(functools.partial(block_kernel, blocks=blocks, tile=tile,...  20.9 us
    ppermute x7, starting transfers between devices, line(): return lax.ppermute(value, ('tensor', 'section'), pairs)  17.3 us
    ppermute x4, waiting for transfers between devices, with_other_replicas(): lax.ppermute(value, ('section', 'replica'), [(s * count + r, s * count +...  8.43 us
    ppermute x4, waiting for transfers between devices, sum_step(): other = lax.ppermute(value.astype(wire), 'tensor', pairs)  8.29 us
    ppermute x4, starting transfers between devices, sum_step(): other = lax.ppermute(value.astype(wire), 'tensor', pairs)  7.8 us
    pallas_call x2, Pallas kernels, gradient_call(): pl.pallas_call(kernel, grid_spec=pltpu.PrefetchScalarGridSpec(num_scalar_...  6.46 us
    ppermute x1, starting transfers between devices, on_device(): lax.ppermute(cotangent, ('tensor', 'section'), [(2 * z, 2 * (z + 1) + 1)...  5.45 us
    ppermute x3, starting transfers between devices, on_device(): lax.ppermute(row_sums, 'tensor', [(z, (z + step) % count) for z in everyo...  4.12 us
  transfers between devices with their start and end apart: 22, of which 10 were waited for; matrix products, arithmetic and copies ran while one was open for 12% of the time, Pallas kernels for 22%

profile of v10, /device:TPU:0, one launch (start us, length us, event | category | flops | bytes accessed | tf_op | source)
XLA Modules:
  0.0 103.7 jit_solution(12005383086326674296)
XLA Ops:
  0.6 5.4 %collective-permute-start = (bf16[192,2048]{1,0:T(8,128)(2,1)}, bf16[192,2048]{1,0:T(8,128)(2,1)}, u32[]{:S(2)}, u32[]{:S(2)}) collective-permute-start(bf16[192,2048]{1,0:T(8,128)(2,1)} %param.9), channel_id=1, source_target_pairs={{0,6},{4,10},{8,14},{1,7},{5,11},{9,15},{16,22},{20,26},{24,30},{1... | collective-permute-start | bytes 2359304 | tf_op jit(solution)/shard_map/ppermute | solution.py:284
  6.1 1.6 %collective-permute-start.2 = (bf16[192,2048]{1,0:T(8,128)(2,1)}, bf16[192,2048]{1,0:T(8,128)(2,1)}, u32[]{:S(2)}, u32[]{:S(2)}) collective-permute-start(bf16[192,2048]{1,0:T(8,128)(2,1)} %param.9), channel_id=1, source_target_pairs={{6,2},{10,6},{14,10},{7,3},{11,7},{15,11},{22,18},{26,22},{30,26},... | collective-permute-start | bytes 2359304 | tf_op jit(solution)/shard_map/ppermute | solution.py:268
  7.7 1.4 %fusion.18.value_ref.early = bf16[192,2048]{1,0:T(8,128)(2,1)S(1)} fusion(bf16[192,2048]{1,0:T(8,128)(2,1)} %param.9, bf16[192,2048]{1,0:T(8,128)(2,1)} %param.8, f32[2048]{0:T(1024)} %bitcast.38, pred[]{:T(512)S(6)} %eq.20), kind=kLoop, calls=%fused_computation.36 | loop fusion | flops 1572864 | bytes 2367489 | tf_op jit(solution)/shard_map/jit(_where)/select_n | solution.py:271
  9.1 5.2 %shard_map.95 = f32[192,2048]{1,0:T(8,128)S(1)} custom-call(s32[2]{0:T(128)S(1)} %pad_add_fusion.table, bf16[192,2048]{1,0:T(8,128)(2,1)S(1)} %fusion.18.value_ref.early, bf16[2048,8192]{1,0:T(8,128)(2,1)} %bitcast.41), custom_call_target="tpu_custom_call" | custom-call | flops 6442450944 | bytes 8388608 | tf_op jit(solution)/shard_map/pallas_call | solution.py:72
  15.0 1.4 %add_convert_fusion.5 = bf16[192,2048]{1,0:T(8,128)(2,1)S(1)} fusion(bf16[192,2048]{1,0:T(8,128)(2,1)} %collective-permute-done, f32[192,2048]{1,0:T(8,128)S(1)} %shard_map.95, pred[]{:T(512)S(6)} %eq.20), kind=kLoop, calls=%fused_computation.23 | loop fusion | flops 1572864 | bytes 3145729 | tf_op jit(solution)/shard_map/convert_element_type | solution.py:332
  16.4 3.7 %collective-permute-start.1 = (bf16[192,2048]{1,0:T(8,128)(2,1)S(1)}, bf16[192,2048]{1,0:T(8,128)(2,1)S(1)}, u32[]{:S(2)}, u32[]{:S(2)}) collective-permute-start(bf16[192,2048]{1,0:T(8,128)(2,1)S(1)} %add_convert_fusion.5), channel_id=1, source_target_pairs={{0,4},{6,10},{10,14},{1,5},{7,11},{11,15},{16,20},{22,26},{26,30},... | collective-permute-start | bytes 2359304 | tf_op jit(solution)/shard_map/ppermute | solution.py:268
  20.1 1.3 %add_convert_fusion.4 = bf16[192,2048]{1,0:T(8,128)(2,1)S(1)} fusion(bf16[192,2048]{1,0:T(8,128)(2,1)} %collective-permute-done.2, f32[192,2048]{1,0:T(8,128)S(1)} %shard_map.95, pred[]{:T(512)S(6)} %eq.20), kind=kLoop, calls=%fused_computation.22 | loop fusion | flops 1572864 | bytes 3145729 | tf_op jit(solution)/shard_map/convert_element_type | solution.py:332
  23.5 5.2 %shard_map.96 = f32[192,2048]{1,0:T(8,128)S(1)} custom-call(s32[2]{0:T(128)S(1)} %pad_add_fusion.table, bf16[192,2048]{1,0:T(8,128)(2,1)S(1)} %select_select_fusion.2.value_ref, bf16[2048,8192]{1,0:T(8,128)(2,1)} %bitcast.42), custom_call_target="tpu_custom_call" | custom-call | flops 6442450944 | bytes 8388608 | tf_op jit(solution)/shard_map/pallas_call | solution.py:72
  28.8 1.6 %collective-permute-start.8 = (bf16[192,2048]{1,0:T(8,128)(2,1)S(1)}, bf16[192,2048]{1,0:T(8,128)(2,1)S(1)}, u32[]{:S(2)}, u32[]{:S(2)}) collective-permute-start(bf16[192,2048]{1,0:T(8,128)(2,1)S(1)} %fusion.18.value_ref.early), channel_id=1, source_target_pairs={{0,1},{1,0},{2,3},{3,2},{4,5},{5,4},{6,7},{7,6},{8,9},{9,8},{10,11... | collective-permute-start | bytes 2359304 | tf_op jit(solution)/shard_map/ppermute | solution.py:211
  30.8 3.9 %collective-permute-start.4 = (bf16[192,2048]{1,0:T(8,128)(2,1)S(1)}, bf16[192,2048]{1,0:T(8,128)(2,1)S(1)}, u32[]{:S(2)}, u32[]{:S(2)}) collective-permute-start(bf16[192,2048]{1,0:T(8,128)(2,1)S(1)} %add_convert_fusion.3), channel_id=1, source_target_pairs={{0,4},{4,8},{10,14},{1,5},{5,9},{11,15},{16,20},{20,24},{26,30},{1... | collective-permute-start | bytes 2359304 | tf_op jit(solution)/shard_map/ppermute | solution.py:268
  35.9 4.3 %collective-permute-start.7 = (bf16[208,256]{1,0:T(8,128)(2,1)S(1)}, bf16[208,256]{1,0:T(8,128)(2,1)S(1)}, u32[]{:S(2)}, u32[]{:S(2)}) collective-permute-start(bf16[208,256]{1,0:T(8,128)(2,1)S(1)} %convert_element_type.138), channel_id=1, source_target_pairs={{0,8},{4,12},{8,0},{12,4},{1,9},{5,13},{9,1},{13,5},{2,10},{6,14},... | collective-permute-start | bytes 319496 | tf_op jit(solution)/shard_map/ppermute | solution.py:202
  40.4 5.2 %shard_map.97 = f32[192,2048]{1,0:T(8,128)S(1)} custom-call(s32[2]{0:T(128)S(1)} %pad_add_fusion.table, bf16[192,2048]{1,0:T(8,128)(2,1)S(1)} %select_select_fusion.1.value_ref, bf16[2048,8192]{1,0:T(8,128)(2,1)} %bitcast.43), custom_call_target="tpu_custom_call" | custom-call | flops 6442450944 | bytes 8388608 | tf_op jit(solution)/shard_map/pallas_call | solution.py:72
  46.0 5.4 %collective-permute-start.9 = (bf16[192,2048]{1,0:T(8,128)(2,1)S(1)}, bf16[192,2048]{1,0:T(8,128)(2,1)S(1)}, u32[]{:S(2)}, u32[]{:S(2)}) collective-permute-start(bf16[192,2048]{1,0:T(8,128)(2,1)S(1)} %add_convert_fusion.1), channel_id=1, source_target_pairs={{0,4},{4,8},{8,12},{1,5},{5,9},{9,13},{16,20},{20,24},{24,28},{17,... | collective-permute-start | bytes 2359304 | tf_op jit(solution)/shard_map/ppermute | solution.py:268
  51.7 1.3 %collective-permute-start.10 = (bf16[192,2048]{1,0:T(8,128)(2,1)S(1)}, bf16[192,2048]{1,0:T(8,128)(2,1)S(1)}, u32[]{:S(2)}, u32[]{:S(2)}) collective-permute-start(bf16[192,2048]{1,0:T(8,128)(2,1)S(1)} %add_convert_fusion), channel_id=1, source_target_pairs={{4,0},{8,4},{12,8},{5,1},{9,5},{13,9},{20,16},{24,20},{28,24},{21,... | collective-permute-start | bytes 2359304 | tf_op jit(solution)/shard_map/ppermute | solution.py:268
  53.0 1.5 %collective-permute-done.7 = bf16[208,256]{1,0:T(8,128)(2,1)S(1)} collective-permute-done((bf16[208,256]{1,0:T(8,128)(2,1)S(1)}, bf16[208,256]{1,0:T(8,128)(2,1)S(1)}, u32[]{:S(2)}, u32[]{:S(2)}) %collective-permute-start.7) | collective-permute-done | bytes 106528 | tf_op jit(solution)/shard_map/ppermute | solution.py:202
  54.9 5.2 %shard_map.98 = f32[192,2048]{1,0:T(8,128)S(1)} custom-call(s32[2]{0:T(128)S(1)} %pad_add_fusion.table, bf16[192,2048]{1,0:T(8,128)(2,1)S(1)} %select_select_fusion.value_ref, bf16[2048,8192]{1,0:T(8,128)(2,1)} %bitcast.44), custom_call_target="tpu_custom_call" | custom-call | flops 6442450944 | bytes 8388608 | tf_op jit(solution)/shard_map/pallas_call | solution.py:72
  62.1 1.3 %collective-permute-start.13 = (bf16[192,2048]{1,0:T(8,128)(2,1)S(1)}, bf16[192,2048]{1,0:T(8,128)(2,1)S(1)}, u32[]{:S(2)}, u32[]{:S(2)}) collective-permute-start(bf16[192,2048]{1,0:T(8,128)(2,1)S(1)} %get-tuple-element.87), channel_id=1, source_target_pairs={{2,0},{3,1},{6,4},{7,5},{10,8},{11,9},{14,12},{15,13},{18,16},{19,... | collective-permute-start | bytes 2359304 | tf_op jit(solution)/shard_map/ppermute | solution.py:221
  63.4 1.6 %collective-permute-done.11.small_early = bf16[192,256]{1,0:T(8,128)(2,1)S(1)} collective-permute-done((bf16[192,256]{1,0:T(8,128)(2,1)S(1)}, bf16[192,256]{1,0:T(8,128)(2,1)S(1)}, u32[]{:S(2)}, u32[]{:S(2)}) %collective-permute-start.11) | collective-permute-done | bytes 98336 | tf_op jit(solution)/shard_map/ppermute | solution.py:211
  65.0 1.1 %collective-permute-done.10 = bf16[192,2048]{1,0:T(8,128)(2,1)S(1)} collective-permute-done((bf16[192,2048]{1,0:T(8,128)(2,1)S(1)}, bf16[192,2048]{1,0:T(8,128)(2,1)S(1)}, u32[]{:S(2)}, u32[]{:S(2)}) %collective-permute-start.10) | collective-permute-done | bytes 786464 | tf_op jit(solution)/shard_map/ppermute | solution.py:268
  67.2 2.3 %collective-permute-done.12.cotangent = bf16[192,2048]{1,0:T(8,128)(2,1)S(1)} collective-permute-done((bf16[192,2048]{1,0:T(8,128)(2,1)S(1)}, bf16[192,2048]{1,0:T(8,128)(2,1)S(1)}, u32[]{:S(2)}, u32[]{:S(2)}) %collective-permute-start.12) | collective-permute-done | bytes 786464 | tf_op jit(solution)/shard_map/ppermute | solution.py:377
  70.0 1.5 %collective-permute-start.16 = (f32[2,192]{1,0:T(2,128)S(1)}, f32[2,192]{1,0:T(2,128)S(1)}, u32[]{:S(2)}, u32[]{:S(2)}) collective-permute-start(f32[2,192]{1,0:T(2,128)S(1)} %pad_maximum_fusion.1), channel_id=1, source_target_pairs={{0,12},{4,0},{8,4},{12,8},{1,13},{5,1},{9,5},{13,9},{2,14},{6,2},{... | collective-permute-start | bytes 4616 | tf_op jit(solution)/shard_map/ppermute | solution.py:389
  72.3 1.8 %collective-permute-start.15 = (f32[2,192]{1,0:T(2,128)S(1)}, f32[2,192]{1,0:T(2,128)S(1)}, u32[]{:S(2)}, u32[]{:S(2)}) collective-permute-start(f32[2,192]{1,0:T(2,128)S(1)} %pad_maximum_fusion.1), channel_id=1, source_target_pairs={{0,8},{4,12},{8,0},{12,4},{1,9},{5,13},{9,1},{13,5},{2,10},{6,14},... | collective-permute-start | bytes 4616 | tf_op jit(solution)/shard_map/ppermute | solution.py:389
  74.8 2.1 %collective-permute-done.14 = f32[2,192]{1,0:T(2,128)S(1)} collective-permute-done((f32[2,192]{1,0:T(2,128)S(1)}, f32[2,192]{1,0:T(2,128)S(1)}, u32[]{:S(2)}, u32[]{:S(2)}) %collective-permute-start.14) | collective-permute-done | bytes 1568 | tf_op jit(solution)/shard_map/ppermute | solution.py:389
  78.5 1.7 %collective-permute-start.17 = (bf16[192,256]{1,0:T(8,128)(2,1)S(1)}, bf16[192,256]{1,0:T(8,128)(2,1)S(1)}, u32[]{:S(2)}, u32[]{:S(2)}) collective-permute-start(bf16[192,256]{1,0:T(8,128)(2,1)S(1)} %get-tuple-element.89), channel_id=1, source_target_pairs={{0,4},{4,0},{8,12},{12,8},{1,5},{5,1},{9,13},{13,9},{2,6},{6,2},{1... | collective-permute-start | bytes 294920 | tf_op jit(solution)/shard_map/ppermute | solution.py:202
  80.2 3.0 %collective-permute-done.17 = bf16[192,256]{1,0:T(8,128)(2,1)S(1)} collective-permute-done((bf16[192,256]{1,0:T(8,128)(2,1)S(1)}, bf16[192,256]{1,0:T(8,128)(2,1)S(1)}, u32[]{:S(2)}, u32[]{:S(2)}) %collective-permute-start.17) | collective-permute-done | bytes 98336 | tf_op jit(solution)/shard_map/ppermute | solution.py:202
  83.2 1.7 %collective-permute-start.18 = (bf16[192,256]{1,0:T(8,128)(2,1)S(1)}, bf16[192,256]{1,0:T(8,128)(2,1)S(1)}, u32[]{:S(2)}, u32[]{:S(2)}) collective-permute-start(bf16[192,256]{1,0:T(8,128)(2,1)S(1)} %fusion.24), channel_id=1, source_target_pairs={{0,8},{4,12},{8,0},{12,4},{1,9},{5,13},{9,1},{13,5},{2,10},{6,14},... | collective-permute-start | bytes 294920 | tf_op jit(solution)/shard_map/ppermute | solution.py:202
  85.0 3.8 %collective-permute-done.18 = bf16[192,256]{1,0:T(8,128)(2,1)S(1)} collective-permute-done((bf16[192,256]{1,0:T(8,128)(2,1)S(1)}, bf16[192,256]{1,0:T(8,128)(2,1)S(1)}, u32[]{:S(2)}, u32[]{:S(2)}) %collective-permute-start.18) | collective-permute-done | bytes 98336 | tf_op jit(solution)/shard_map/ppermute | solution.py:202
  88.9 3.9 %collective-permute-done.19 = bf16[192,2048]{1,0:T(8,128)(2,1)S(1)} collective-permute-done((bf16[192,2048]{1,0:T(8,128)(2,1)S(1)}, bf16[192,2048]{1,0:T(8,128)(2,1)S(1)}, u32[]{:S(2)}, u32[]{:S(2)}) %collective-permute-start.19) | collective-permute-done | bytes 786464 | tf_op jit(solution)/shard_map/ppermute | solution.py:211
  93.1 1.0 collective-permute-start.21
  94.2 2.3 %shard_map.99 = (f32[2048,256]{1,0:T(8,128)S(1)}, f32[256,2048]{1,0:T(8,128)S(1)}) custom-call(s32[2]{0:T(128)S(1)} %pad_add_fusion.table, bf16[192,2048]{1,0:T(8,128)(2,1)S(1)} %fusion.18.value_ref.early, bf16[192,2048]{1,0:T(8,128)(2,1)S(1)} %fusion.17.late, bf16[192,256]{1,0:T(8,128)(2,1)S(1)} %get-tuple-element.85.small_early, ...), custom_call_target="tpu_custom_call" | custom-call | flops 402653184 | bytes 5767168 | tf_op jit(solution)/shard_map/pallas_call | solution.py:145
  96.6 2.9 %collective-permute-done.21.small_late = bf16[192,384]{1,0:T(8,128)(2,1)S(1)} collective-permute-done((bf16[192,384]{1,0:T(8,128)(2,1)S(1)}, bf16[192,384]{1,0:T(8,128)(2,1)S(1)}, u32[]{:S(2)}, u32[]{:S(2)}) %collective-permute-start.21) | collective-permute-done | bytes 147488 | tf_op jit(solution)/shard_map/ppermute | solution.py:211
  99.5 4.2 %shard_map.100 = (f32[2048,256]{1,0:T(8,128)}, f32[256,2048]{1,0:T(8,128)}) custom-call(s32[2]{0:T(128)S(1)} %pad_add_fusion.table, f32[1,2048]{1,0:T(1,128)S(1)} %copy-done.1, f32[2048,256]{1,0:T(8,128)S(1)} %get-tuple-element.64.down_sum, f32[256,2048]{1,0:T(8,128)S(1)} %get-tuple-element.65.up_sum, bf16[192,2048]{1,0:T(8,128)(2,1)S(1)} %collective-permute-done.8.early, ...), custom_call_target="tpu_custom_call" | custom-call | flops 402653184 | bytes 11534336 | tf_op jit(solution)/shard_map/pallas_call | solution.py:145
  (78 shorter events, 12.7 us)
Async XLA Ops:
  0.6 22.3 %copy-start = (bf16[1,2048,256]{2,1,0:T(8,128)(2,1)S(1)}, bf16[1,2048,256]{2,1,0:T(8,128)(2,1)}, u32[]{:S(2)}) copy-start(bf16[1,2048,256]{2,1,0:T(8,128)(2,1)} %param.12) | copy-start | bytes 3145732
  0.6 14.3 %collective-permute-start = (bf16[192,2048]{1,0:T(8,128)(2,1)}, bf16[192,2048]{1,0:T(8,128)(2,1)}, u32[]{:S(2)}, u32[]{:S(2)}) collective-permute-start(bf16[192,2048]{1,0:T(8,128)(2,1)} %param.9), channel_id=1, source_target_pairs={{0,6},{4,10},{8,14},{1,7},{5,11},{9,15},{16,22},{20,26},{24,30},{1... | collective-permute-start | bytes 2359304 | tf_op jit(solution)/shard_map/ppermute | solution.py:284
  6.1 14.0 %collective-permute-start.2 = (bf16[192,2048]{1,0:T(8,128)(2,1)}, bf16[192,2048]{1,0:T(8,128)(2,1)}, u32[]{:S(2)}, u32[]{:S(2)}) collective-permute-start(bf16[192,2048]{1,0:T(8,128)(2,1)} %param.9), channel_id=1, source_target_pairs={{6,2},{10,6},{14,10},{7,3},{11,7},{15,11},{22,18},{26,22},{30,26},... | collective-permute-start | bytes 2359304 | tf_op jit(solution)/shard_map/ppermute | solution.py:268
  9.1 5.2 %copy-start.6 = (f32[4]{0:T(128)S(1)}, f32[4]{0:T(128)}, u32[]{:S(2)}) copy-start(f32[4]{0:T(128)} %param.14) | copy-start | bytes 52
  16.4 5.8 %copy-start.3 = (bf16[192,2048]{1,0:T(8,128)(2,1)S(1)}, bf16[192,2048]{1,0:T(8,128)(2,1)}, u32[]{:S(2)}) copy-start(bf16[192,2048]{1,0:T(8,128)(2,1)} %param.8) | copy-start | bytes 2359300
  16.4 6.0 %copy-start.2 = (bf16[1,256,2048]{2,1,0:T(8,128)(2,1)S(1)}, bf16[1,256,2048]{2,1,0:T(8,128)(2,1)}, u32[]{:S(2)}) copy-start(bf16[1,256,2048]{2,1,0:T(8,128)(2,1)} %param.13) | copy-start | bytes 3145732
  16.4 14.0 %collective-permute-start.1 = (bf16[192,2048]{1,0:T(8,128)(2,1)S(1)}, bf16[192,2048]{1,0:T(8,128)(2,1)S(1)}, u32[]{:S(2)}, u32[]{:S(2)}) collective-permute-start(bf16[192,2048]{1,0:T(8,128)(2,1)S(1)} %add_convert_fusion.5), channel_id=1, source_target_pairs={{0,4},{6,10},{10,14},{1,5},{7,11},{11,15},{16,20},{22,26},{26,30},... | collective-permute-start | bytes 2359304 | tf_op jit(solution)/shard_map/ppermute | solution.py:268
  21.4 13.3 %collective-permute-start.3 = (bf16[192,2048]{1,0:T(8,128)(2,1)S(1)}, bf16[192,2048]{1,0:T(8,128)(2,1)S(1)}, u32[]{:S(2)}, u32[]{:S(2)}) collective-permute-start(bf16[192,2048]{1,0:T(8,128)(2,1)S(1)} %add_convert_fusion.4), channel_id=1, source_target_pairs={{12,8},{6,2},{10,6},{13,9},{7,3},{11,7},{28,24},{22,18},{26,22},{2... | collective-permute-start | bytes 2359304 | tf_op jit(solution)/shard_map/ppermute | solution.py:268
  28.8 7.0 %collective-permute-start.6 = (bf16[208,256]{1,0:T(8,128)(2,1)S(1)}, bf16[208,256]{1,0:T(8,128)(2,1)S(1)}, u32[]{:S(2)}, u32[]{:S(2)}) collective-permute-start(bf16[208,256]{1,0:T(8,128)(2,1)S(1)} %convert_element_type.136), channel_id=1, source_target_pairs={{0,4},{4,0},{8,12},{12,8},{1,5},{5,1},{9,13},{13,9},{2,6},{6,2},{1... | collective-permute-start | bytes 319496 | tf_op jit(solution)/shard_map/ppermute | solution.py:202
  28.8 31.3 %collective-permute-start.8 = (bf16[192,2048]{1,0:T(8,128)(2,1)S(1)}, bf16[192,2048]{1,0:T(8,128)(2,1)S(1)}, u32[]{:S(2)}, u32[]{:S(2)}) collective-permute-start(bf16[192,2048]{1,0:T(8,128)(2,1)S(1)} %fusion.18.value_ref.early), channel_id=1, source_target_pairs={{0,1},{1,0},{2,3},{3,2},{4,5},{5,4},{6,7},{7,6},{8,9},{9,8},{10,11... | collective-permute-start | bytes 2359304 | tf_op jit(solution)/shard_map/ppermute | solution.py:211
  30.8 14.8 %collective-permute-start.4 = (bf16[192,2048]{1,0:T(8,128)(2,1)S(1)}, bf16[192,2048]{1,0:T(8,128)(2,1)S(1)}, u32[]{:S(2)}, u32[]{:S(2)}) collective-permute-start(bf16[192,2048]{1,0:T(8,128)(2,1)S(1)} %add_convert_fusion.3), channel_id=1, source_target_pairs={{0,4},{4,8},{10,14},{1,5},{5,9},{11,15},{16,20},{20,24},{26,30},{1... | collective-permute-start | bytes 2359304 | tf_op jit(solution)/shard_map/ppermute | solution.py:268
  35.1 16.4 %collective-permute-start.5 = (bf16[192,2048]{1,0:T(8,128)(2,1)S(1)}, bf16[192,2048]{1,0:T(8,128)(2,1)S(1)}, u32[]{:S(2)}, u32[]{:S(2)}) collective-permute-start(bf16[192,2048]{1,0:T(8,128)(2,1)S(1)} %add_convert_fusion.2), channel_id=1, source_target_pairs={{8,4},{12,8},{6,2},{9,5},{13,9},{7,3},{24,20},{28,24},{22,18},{25,... | collective-permute-start | bytes 2359304 | tf_op jit(solution)/shard_map/ppermute | solution.py:268
  35.9 18.6 %collective-permute-start.7 = (bf16[208,256]{1,0:T(8,128)(2,1)S(1)}, bf16[208,256]{1,0:T(8,128)(2,1)S(1)}, u32[]{:S(2)}, u32[]{:S(2)}) collective-permute-start(bf16[208,256]{1,0:T(8,128)(2,1)S(1)} %convert_element_type.138), channel_id=1, source_target_pairs={{0,8},{4,12},{8,0},{12,4},{1,9},{5,13},{9,1},{13,5},{2,10},{6,14},... | collective-permute-start | bytes 319496 | tf_op jit(solution)/shard_map/ppermute | solution.py:202
  46.0 19.0 %collective-permute-start.9 = (bf16[192,2048]{1,0:T(8,128)(2,1)S(1)}, bf16[192,2048]{1,0:T(8,128)(2,1)S(1)}, u32[]{:S(2)}, u32[]{:S(2)}) collective-permute-start(bf16[192,2048]{1,0:T(8,128)(2,1)S(1)} %add_convert_fusion.1), channel_id=1, source_target_pairs={{0,4},{4,8},{8,12},{1,5},{5,9},{9,13},{16,20},{20,24},{24,28},{17,... | collective-permute-start | bytes 2359304 | tf_op jit(solution)/shard_map/ppermute | solution.py:268
  51.7 14.3 %collective-permute-start.10 = (bf16[192,2048]{1,0:T(8,128)(2,1)S(1)}, bf16[192,2048]{1,0:T(8,128)(2,1)S(1)}, u32[]{:S(2)}, u32[]{:S(2)}) collective-permute-start(bf16[192,2048]{1,0:T(8,128)(2,1)S(1)} %add_convert_fusion), channel_id=1, source_target_pairs={{4,0},{8,4},{12,8},{5,1},{9,5},{13,9},{20,16},{24,20},{28,24},{21,... | collective-permute-start | bytes 2359304 | tf_op jit(solution)/shard_map/ppermute | solution.py:268
  54.9 5.3 %copy-start.5 = (s32[192]{0:T(256)S(1)}, s32[192]{0:T(256)}, u32[]{:S(2)}) copy-start(s32[192]{0:T(256)} %param.15) | copy-start | bytes 2308
  60.1 1.2 %copy-start.1 = (f32[1,2048]{1,0:T(1,128)S(1)}, f32[1,2048]{1,0:T(1,128)}, u32[]{:S(2)}) copy-start(f32[1,2048]{1,0:T(1,128)} %gain_ref.1) | copy-start | bytes 24580
  60.3 4.7 %collective-permute-start.11 = (bf16[192,256]{1,0:T(8,128)(2,1)S(1)}, bf16[192,256]{1,0:T(8,128)(2,1)S(1)}, u32[]{:S(2)}, u32[]{:S(2)}) collective-permute-start(bf16[192,256]{1,0:T(8,128)(2,1)S(1)} %get-tuple-element.79), channel_id=1, source_target_pairs={{0,1},{1,0},{2,3},{3,2},{4,5},{5,4},{6,7},{7,6},{8,9},{9,8},{10,11... | collective-permute-start | bytes 294920 | tf_op jit(solution)/shard_map/ppermute | solution.py:211
  62.1 5.1 %collective-permute-start.13 = (bf16[192,2048]{1,0:T(8,128)(2,1)S(1)}, bf16[192,2048]{1,0:T(8,128)(2,1)S(1)}, u32[]{:S(2)}, u32[]{:S(2)}) collective-permute-start(bf16[192,2048]{1,0:T(8,128)(2,1)S(1)} %get-tuple-element.87), channel_id=1, source_target_pairs={{2,0},{3,1},{6,4},{7,5},{10,8},{11,9},{14,12},{15,13},{18,16},{19,... | collective-permute-start | bytes 2359304 | tf_op jit(solution)/shard_map/ppermute | solution.py:221
  67.1 9.9 %copy-start.4 = (bf16[192,2048]{1,0:T(8,128)(2,1)S(1)}, bf16[192,2048]{1,0:T(8,128)(2,1)}, u32[]{:S(2)}) copy-start(bf16[192,2048]{1,0:T(8,128)(2,1)} %param.9) | copy-start | bytes 2359300
  67.1 2.4 %collective-permute-start.12 = (bf16[192,2048]{1,0:T(8,128)(2,1)S(1)}, bf16[192,2048]{1,0:T(8,128)(2,1)S(1)}, u32[]{:S(2)}, u32[]{:S(2)}) collective-permute-start(bf16[192,2048]{1,0:T(8,128)(2,1)S(1)} %broadcast_select_fusion.3), channel_id=1, source_target_pairs={{0,2},{2,0},{1,3},{3,1},{4,6},{6,4},{5,7},{7,5},{8,10},{10,8},{9,1... | collective-permute-start | bytes 2359304 | tf_op jit(solution)/shard_map/ppermute | solution.py:377
  70.0 4.9 %collective-permute-start.16 = (f32[2,192]{1,0:T(2,128)S(1)}, f32[2,192]{1,0:T(2,128)S(1)}, u32[]{:S(2)}, u32[]{:S(2)}) collective-permute-start(f32[2,192]{1,0:T(2,128)S(1)} %pad_maximum_fusion.1), channel_id=1, source_target_pairs={{0,12},{4,0},{8,4},{12,8},{1,13},{5,1},{9,5},{13,9},{2,14},{6,2},{... | collective-permute-start | bytes 4616 | tf_op jit(solution)/shard_map/ppermute | solution.py:389
  71.5 5.4 %collective-permute-start.14 = (f32[2,192]{1,0:T(2,128)S(1)}, f32[2,192]{1,0:T(2,128)S(1)}, u32[]{:S(2)}, u32[]{:S(2)}) collective-permute-start(f32[2,192]{1,0:T(2,128)S(1)} %pad_maximum_fusion.1), channel_id=1, source_target_pairs={{0,4},{4,8},{8,12},{12,0},{1,5},{5,9},{9,13},{13,1},{2,6},{6,10},{... | collective-permute-start | bytes 4616 | tf_op jit(solution)/shard_map/ppermute | solution.py:389
  72.3 4.6 %collective-permute-start.15 = (f32[2,192]{1,0:T(2,128)S(1)}, f32[2,192]{1,0:T(2,128)S(1)}, u32[]{:S(2)}, u32[]{:S(2)}) collective-permute-start(f32[2,192]{1,0:T(2,128)S(1)} %pad_maximum_fusion.1), channel_id=1, source_target_pairs={{0,8},{4,12},{8,0},{12,4},{1,9},{5,13},{9,1},{13,5},{2,10},{6,14},... | collective-permute-start | bytes 4616 | tf_op jit(solution)/shard_map/ppermute | solution.py:389
  74.1 18.7 %collective-permute-start.19 = (bf16[192,2048]{1,0:T(8,128)(2,1)S(1)}, bf16[192,2048]{1,0:T(8,128)(2,1)S(1)}, u32[]{:S(2)}, u32[]{:S(2)}) collective-permute-start(bf16[192,2048]{1,0:T(8,128)(2,1)S(1)} %get-tuple-element.74), channel_id=1, source_target_pairs={{0,1},{1,0},{2,3},{3,2},{4,5},{5,4},{6,7},{7,6},{8,9},{9,8},{10,11... | collective-permute-start | bytes 2359304 | tf_op jit(solution)/shard_map/ppermute | solution.py:211
  78.5 4.7 %collective-permute-start.17 = (bf16[192,256]{1,0:T(8,128)(2,1)S(1)}, bf16[192,256]{1,0:T(8,128)(2,1)S(1)}, u32[]{:S(2)}, u32[]{:S(2)}) collective-permute-start(bf16[192,256]{1,0:T(8,128)(2,1)S(1)} %get-tuple-element.89), channel_id=1, source_target_pairs={{0,4},{4,0},{8,12},{12,8},{1,5},{5,1},{9,13},{13,9},{2,6},{6,2},{1... | collective-permute-start | bytes 294920 | tf_op jit(solution)/shard_map/ppermute | solution.py:202
  83.2 5.6 %collective-permute-start.18 = (bf16[192,256]{1,0:T(8,128)(2,1)S(1)}, bf16[192,256]{1,0:T(8,128)(2,1)S(1)}, u32[]{:S(2)}, u32[]{:S(2)}) collective-permute-start(bf16[192,256]{1,0:T(8,128)(2,1)S(1)} %fusion.24), channel_id=1, source_target_pairs={{0,8},{4,12},{8,0},{12,4},{1,9},{5,13},{9,1},{13,5},{2,10},{6,14},... | collective-permute-start | bytes 294920 | tf_op jit(solution)/shard_map/ppermute | solution.py:202
  92.9 3.6 %collective-permute-start.20 = (bf16[192,2048]{1,0:T(8,128)(2,1)S(1)}, bf16[192,2048]{1,0:T(8,128)(2,1)S(1)}, u32[]{:S(2)}, u32[]{:S(2)}) collective-permute-start(bf16[192,2048]{1,0:T(8,128)(2,1)S(1)} %collective-permute-done.19), channel_id=1, source_target_pairs={{0,2},{2,0},{1,3},{3,1},{4,6},{6,4},{5,7},{7,5},{8,10},{10,8},{9,1... | collective-permute-start | bytes 2359304 | tf_op jit(solution)/shard_map/ppermute | solution.py:406
  93.1 6.3 %collective-permute-start.21 = (bf16[192,384]{1,0:T(8,128)(2,1)S(1)}, bf16[192,384]{1,0:T(8,128)(2,1)S(1)}, u32[]{:S(2)}, u32[]{:S(2)}) collective-permute-start(bf16[192,384]{1,0:T(8,128)(2,1)S(1)} %pad_maximum_fusion), channel_id=1, source_target_pairs={{0,1},{1,0},{2,3},{3,2},{4,5},{5,4},{6,7},{7,6},{8,9},{9,8},{10,11... | collective-permute-start | bytes 442376 | tf_op jit(solution)/shard_map/ppermute | solution.py:211

commit v11 on v10

--- a/solution.py
+++ b/solution.py
@@ -110,46 +110,35 @@
 
 
 def other_gradient_kernel(
-    table, gain_ref, down_sum, up_sum, early, cotangent, pulled, hidden, small_early, small_late,
-    down_ref, up_ref,
+    table, down_sum, up_sum, early, late, small_early, beside, down_ref, up_ref
 ):
     ranks = down_ref.shape[1]
-    late = small_late[:, :ranks]
-    inverse = small_late[:, ranks : ranks + 1].astype(F32)
-    toward = small_late[:, ranks + 64 : ranks + 65].astype(F32)
+    small_late = beside[:, :ranks]
 
     @pl.when(table[0] == 0)
     def _():
-        grad = (
-            cotangent[...].astype(F32)
-            + inverse * pulled[...].astype(F32)
-            - toward * hidden[...].astype(F32)
-        ).astype(BF16)
-        down_ref[...] = down_sum[...] + transposed_times(early[...], late)
-        up_ref[...] = up_sum[...] + transposed_times(small_early[...], grad)
+        down_ref[...] = down_sum[...] + transposed_times(early[...], small_late)
+        up_ref[...] = up_sum[...] + transposed_times(small_early[...], late[...])
 
     @pl.when(table[0] == 1)
     def _():
-        scaled = (hidden[...].astype(F32) * gain_ref[...]).astype(BF16)
-        weighed = (small_early[...].astype(F32) * inverse).astype(BF16)
-        down_ref[...] = down_sum[...] + transposed_times(scaled, weighed)
-        up_ref[...] = up_sum[...] + transposed_times(late, early[...])
+        scale = beside[:, ranks : ranks + 1].astype(F32)
+        weighed = (small_early[...].astype(F32) * scale).astype(BF16)
+        down_ref[...] = down_sum[...] + transposed_times(late[...], weighed)
+        up_ref[...] = up_sum[...] + transposed_times(small_late, early[...])
 
 
 def gradient_call(kernel, table, sums, by_column, whole, width, ranks, rows):
     tile = min(512, width)
     down_spec = pl.BlockSpec((tile, ranks), lambda step, table: (step, 0))
     up_spec = pl.BlockSpec((ranks, tile), lambda step, table: (0, step))
-    leading = [array for array in by_column if array.shape[0] == 1]
-    columns = [array for array in by_column if array.shape[0] != 1]
     return pl.pallas_call(
         kernel,
         grid_spec=pltpu.PrefetchScalarGridSpec(
             num_scalar_prefetch=1,
             grid=(width // tile,),
-            in_specs=[pl.BlockSpec((1, tile), lambda step, table: (0, step)) for _ in leading]
-            + [down_spec, up_spec][: len(sums)]
-            + [pl.BlockSpec((rows, tile), lambda step, table: (0, step)) for _ in columns]
+            in_specs=[down_spec, up_spec][: len(sums)]
+            + [pl.BlockSpec((rows, tile), lambda step, table: (0, step)) for _ in by_column]
             + [pl.BlockSpec(array.shape, lambda step, table: (0, 0)) for array in whole],
             out_specs=[down_spec, up_spec],
         ),
@@ -160,10 +149,10 @@
         compiler_params=pltpu.CompilerParams(vmem_limit_bytes=20 * 1024 * 1024),
         cost_estimate=pl.CostEstimate(
             flops=4 * rows * width * ranks,
-            bytes_accessed=8 * width * ranks * (1 + len(sums) // 2) + 2 * rows * width * len(columns),
+            bytes_accessed=8 * width * ranks * (1 + len(sums) // 2) + 2 * rows * width * len(by_column),
             transcendentals=0,
         ),
-    )(table, *leading, *sums, *columns, *whole)
+    )(table, *sums, *by_column, *whole)
 
 
 def orders(count):
@@ -241,7 +230,6 @@
     up = adapter_up_factors[0]
     rows, width = tokens.shape
     features = width * count
-    replicas = lax.axis_size("replica")
     ranks = down.shape[1]
 
     tenant_of_column = jnp.arange(ranks, dtype=jnp.int32) // (ranks // TENANT_COUNT)
@@ -289,6 +277,8 @@
             line(cotangent, [], [z for z in everyone if z > 0], -1),
         )
     ]
+    token_others = with_other_replicas(tokens, (0,))[1:]
+
     parts = []
     for stage in range(count):
         wanted = [None if stage == 0 else second_slots[z][stage] for z in everyone]
@@ -298,6 +288,8 @@
             small_sum = small_columns(*lax.optimization_barrier((early, tokens, *sent))[:2])
         elif stage > 1 and steps_left:
             small_sum = sum_step(small_sum, steps_left.pop(0), after=sent)
+        if stage == 1:
+            small_sum, *token_others = lax.optimization_barrier((small_sum, *token_others))
         if stage > 0:
             *here, small_sum = lax.optimization_barrier((*here, small_sum, *sent))[: len(here) + 1]
         value = pick(
@@ -307,11 +299,6 @@
         )
         order = [blocks[stage] for blocks in first_order + second_order]
         part = block_product(table, value, weight, order)
-        if stage == 1:
-            part, after = lax.optimization_barrier((part, early))
-            early_all = [early] + with_other_replicas(after)[1:]
-        if stage == count - 1:
-            part, *early_all = lax.optimization_barrier((part, *early_all))
         parts.append(part)
         slot = stage + 1
         if slot == count:
@@ -350,6 +337,9 @@
 
     while steps_left:
         small_sum = sum_step(small_sum, steps_left.pop(0))
+    cotangent_others = with_other_replicas(
+        lax.optimization_barrier((cotangent, *sent))[0], (1,)
+    )[1:]
     inv_first = lax.rsqrt(
         small_sum[rows:].reshape(-1)[:rows][:, None] / features + EPSILON
     )
@@ -365,80 +355,71 @@
 
     pulled_here = (gain_row * (sum(parts) + low_product)).astype(BF16)
     pulled = to_other_core(pulled_here, 1)
-    from_left, from_right, *small_early_all, _ = lax.optimization_barrier(
-        (from_left, from_right, *small_early_all, pulled_here)
+    from_left, from_right, _, *cotangent_others = lax.optimization_barrier(
+        (from_left, from_right, pulled_here, *cotangent_others)
     )
 
     projected = parts[-1] + from_left.astype(F32) + from_right.astype(F32) + low_product
     hidden = (token_float + inv_first * projected).astype(BF16)
-    late_others = with_other_replicas(jnp.where(is_first, hidden, pulled_here))[1:]
-    swap = [(0, 1), (1, 0)]
-    swapped = [
-        lax.ppermute(jnp.where(is_first, hidden, other), "section", swap) for other in early_all[1:]
+    hidden_on_second = to_other_core(hidden, 0)
+    scaled_second = lax.optimization_barrier(
+        (hidden_on_second.astype(F32) * gain_row).astype(BF16)
+    )
+    scaled_others = with_other_replicas(scaled_second, (1,))[1:]
+    early_others = [
+        jnp.where(is_first, (other.astype(F32) * gain_row).astype(BF16), same)
+        for other, same in zip(token_others, cotangent_others)
     ]
-    hidden_on_second = swapped[0] if swapped else to_other_core(hidden, 0)
-    cotangent_all = [cotangent] + swapped
-    hidden_here = jnp.where(is_first, hidden, hidden_on_second)
-    hidden_float = hidden_here.astype(F32)
+
+    hidden_float = hidden.astype(F32)
     pulled_float = pulled.astype(F32)
     row_sums = jnp.stack(
         [jnp.sum(hidden_float * hidden_float, axis=1), jnp.sum(hidden_float * pulled_float, axis=1)]
     )
+
+    def on_first(value, pairs):
+        return lax.ppermute(value, ("tensor", "section"), [(2 * z, 2 * to) for z, to in pairs])
+
     if count <= 4:
         row_sums = row_sums + sum(
-            lax.ppermute(row_sums, "tensor", [(z, (z + step) % count) for z in everyone])
+            on_first(row_sums, [(z, (z + step) % count) for z in everyone])
             for step in range(1, count)
         )
     else:
         for step in doubling_steps():
-            row_sums = sum_step(row_sums, step, F32)
-    inv_second = lax.rsqrt(row_sums[0] / features + EPSILON)[:, None]
+            row_sums = row_sums + on_first(row_sums, step)
+    row_sums, *small_early_all = lax.optimization_barrier((row_sums, *small_early_all))
+    inv_second = lax.rsqrt(row_sums[0] / features + EPSILON)
+    inv_on_second = to_other_core(inv_second, 0)[:, None]
+    inv_second = inv_second[:, None]
     toward_hidden = row_sums[1][:, None] * inv_second * inv_second * inv_second / features
     hidden_grad = cotangent.astype(F32) + inv_second * pulled_float - toward_hidden * hidden_float
-    late = jnp.where(
-        is_first, hidden_grad.astype(BF16), (hidden_float * gain_row).astype(BF16)
-    )
+    late = jnp.where(is_first, hidden_grad.astype(BF16), scaled_second)
+    grad_others = with_other_replicas(late, (0,))[1:]
     rank_late = jnp.where(is_first, times_up_transposed(late), times_down(late))
-    for step in doubling_steps():
+    for at, step in enumerate(doubling_steps()):
         rank_late = sum_step(rank_late, step)
-
-    swapped = [
-        lax.ppermute(lax.optimization_barrier((other, rank_late))[0], "section", swap)
-        for other in late_others
-    ]
-    hidden_all = [hidden_here] + [
-        jnp.where(is_first, *pair) for pair in zip(late_others, swapped)
-    ]
-    pulled_all = [pulled] + swapped
-
-    small_late = (coefficients * rank_late * jnp.where(is_first, inv_first, inv_second)).astype(BF16)
-    small_late_all = with_other_replicas(
-        jnp.concatenate(
-            [
-                small_late,
-                jnp.broadcast_to(inv_second, (rows, 64)).astype(BF16),
-                jnp.broadcast_to(toward_hidden, (rows, 64)).astype(BF16),
-            ],
-            axis=1,
-        )
-    )
-    small_early_own = (
-        small_early.astype(F32) * jnp.where(is_first, inv_first, inv_second)
-    ).astype(BF16)
+        if at == 0:
+            rank_late, *scaled_others = lax.optimization_barrier((rank_late, *scaled_others))
+    row_scale = jnp.where(is_first, inv_first, inv_on_second)
+    small_late = (coefficients * rank_late * row_scale).astype(BF16)
+    beside = jnp.concatenate(
+        [small_late, jnp.broadcast_to(inv_on_second, (rows, 128)).astype(BF16)], axis=1
+    )
+    beside, *grad_others = lax.optimization_barrier((beside, *grad_others))
+    small_late_others = with_other_replicas(beside)[1:]
+    late_others = [jnp.where(is_first, *pair) for pair in zip(grad_others, scaled_others)]
+    small_early_own = (small_early.astype(F32) * row_scale).astype(BF16)
     sums = gradient_call(
         own_gradient_kernel,
         table, [], [early, late], [small_early_own, small_late], width, ranks, rows,
     )
-    for at in range(1, replicas):
+    for early_other, late_other, small_other, beside_other in zip(
+        early_others, late_others, small_early_all[1:], small_late_others
+    ):
         sums = gradient_call(
             other_gradient_kernel,
-            table,
-            sums,
-            [gain_row, early_all[at], cotangent_all[at], pulled_all[at], hidden_all[at]],
-            [small_early_all[at], small_late_all[at]],
-            width,
-            ranks,
-            rows,
+            table, sums, [early_other, late_other], [small_other, beside_other], width, ranks, rows,
         )
     grad_down, grad_up = sums
     return (grad_down[None], grad_up[None])

time: 104 us -> 121 us (1.16)
  starting transfers between devices: 39.9 us -> 56.9 us
  waiting for transfers between devices: 22.6 us -> 21 us
    ppermute x4 -> x6, starting transfers between devices: 3.91 us -> 11.3 us  [with_other_replicas(): lax.ppermute(value, ('section', 'replica'), [(s * count + r, s * count +...]
    ppermute x1 -> x3, starting transfers between devices: 1.29 us -> 7.52 us  [to_other_core(): return lax.ppermute(value, 'section', [(source, 1 - source)])]
    ppermute x5 -> x3, starting transfers between devices: 4.19 us -> 8.81 us  [on_first(): lax.ppermute(value, ('tensor', 'section'), [(2 * z, 2 * to) for z, to in...]
    ppermute x7, waiting for transfers between devices: 1.07 us -> 5.02 us  [line(): return lax.ppermute(value, ('tensor', 'section'), pairs)]
    ppermute x4, waiting for transfers between devices: 8.29 us -> 6.09 us  [sum_step(): other = lax.ppermute(value.astype(wire), 'tensor', pairs)]
    ppermute x5 -> x3, waiting for transfers between devices: 4.33 us -> 2.34 us  [on_first(): lax.ppermute(value, ('tensor', 'section'), [(2 * z, 2 * to) for z, to in...]
    ppermute x4 -> x6, waiting for transfers between devices: 8.43 us -> 7.57 us  [with_other_replicas(): lax.ppermute(value, ('section', 'replica'), [(s * count + r, s * count +...]
  transfers between devices with their start and end apart: 22 -> 24, of which waited for: 10 -> 10; matrix products, arithmetic and copies ran while one was open for 12% -> 10% of each run, Pallas kernels for 22% -> 19%
where the time goes in v11:
time: 121 us; the launch traced here: 120 us
  starting transfers between devices  56.9 us (47%)
  Pallas kernels  27.1 us (22%)
  waiting for transfers between devices  21 us (17%)
  other arithmetic  9.9 us (8%)
  matrix products  2.93 us (2%)
  between operations  1.26 us (1%)
    pallas_call x4, Pallas kernels, block_product(): pl.pallas_call(functools.partial(block_kernel, blocks=blocks, tile=tile,...  20.9 us
    ppermute x7, starting transfers between devices, line(): return lax.ppermute(value, ('tensor', 'section'), pairs)  16.8 us
    ppermute x6, starting transfers between devices, with_other_replicas(): lax.ppermute(value, ('section', 'replica'), [(s * count + r, s * count +...  11.3 us
    ppermute x3, starting transfers between devices, on_first(): lax.ppermute(value, ('tensor', 'section'), [(2 * z, 2 * to) for z, to in...  8.81 us
    ppermute x6, waiting for transfers between devices, with_other_replicas(): lax.ppermute(value, ('section', 'replica'), [(s * count + r, s * count +...  7.57 us
    ppermute x3, starting transfers between devices, to_other_core(): return lax.ppermute(value, 'section', [(source, 1 - source)])  7.52 us
    ppermute x4, starting transfers between devices, sum_step(): other = lax.ppermute(value.astype(wire), 'tensor', pairs)  7.02 us
    pallas_call x2, Pallas kernels, gradient_call(): pl.pallas_call(kernel, grid_spec=pltpu.PrefetchScalarGridSpec(num_scalar_...  6.15 us
  transfers between devices with their start and end apart: 24, of which 10 were waited for; matrix products, arithmetic and copies ran while one was open for 10% of the time, Pallas kernels for 19%

profile of v11, /device:TPU:0, one launch (start us, length us, event | category | flops | bytes accessed | tf_op | source)
XLA Modules:
  0.0 119.9 jit_solution(3426207005607618035)
XLA Ops:
  0.6 5.4 %collective-permute-start = (bf16[192,2048]{1,0:T(8,128)(2,1)}, bf16[192,2048]{1,0:T(8,128)(2,1)}, u32[]{:S(2)}, u32[]{:S(2)}) collective-permute-start(bf16[192,2048]{1,0:T(8,128)(2,1)} %param.9), channel_id=1, source_target_pairs={{0,6},{4,10},{8,14},{1,7},{5,11},{9,15},{16,22},{20,26},{24,30},{1... | collective-permute-start | bytes 2359304 | tf_op jit(solution)/shard_map/ppermute | solution.py:272
  6.1 1.6 %collective-permute-start.2 = (bf16[192,2048]{1,0:T(8,128)(2,1)}, bf16[192,2048]{1,0:T(8,128)(2,1)}, u32[]{:S(2)}, u32[]{:S(2)}) collective-permute-start(bf16[192,2048]{1,0:T(8,128)(2,1)} %param.9), channel_id=1, source_target_pairs={{6,2},{10,6},{14,10},{7,3},{11,7},{15,11},{22,18},{26,22},{30,26},... | collective-permute-start | bytes 2359304 | tf_op jit(solution)/shard_map/ppermute | solution.py:256
  7.6 3.4 %collective-permute-start.4 = (bf16[192,2048]{1,0:T(8,128)(2,1)}, bf16[192,2048]{1,0:T(8,128)(2,1)}, u32[]{:S(2)}, u32[]{:S(2)}) collective-permute-start(bf16[192,2048]{1,0:T(8,128)(2,1)} %param.8), channel_id=1, source_target_pairs={{0,1},{1,0},{4,5},{5,4},{8,9},{9,8},{12,13},{13,12},{16,17},{17,16... | collective-permute-start | bytes 2359304 | tf_op jit(solution)/shard_map/ppermute | solution.py:200
  11.1 1.4 %fusion.18.value_ref.early = bf16[192,2048]{1,0:T(8,128)(2,1)S(1)} fusion(bf16[192,2048]{1,0:T(8,128)(2,1)} %param.9, bf16[192,2048]{1,0:T(8,128)(2,1)} %param.8, f32[2048]{0:T(1024)} %bitcast.42, pred[]{:T(512)S(6)} %eq.20), kind=kLoop, calls=%fused_computation.37 | loop fusion | flops 1572864 | bytes 2367489 | tf_op jit(solution)/shard_map/jit(_where)/select_n | solution.py:259
  12.6 5.2 %shard_map.95 = f32[192,2048]{1,0:T(8,128)S(1)} custom-call(s32[2]{0:T(128)S(1)} %pad_add_fusion.table, bf16[192,2048]{1,0:T(8,128)(2,1)S(1)} %fusion.18.value_ref.early, bf16[2048,8192]{1,0:T(8,128)(2,1)} %bitcast.38), custom_call_target="tpu_custom_call" | custom-call | flops 6442450944 | bytes 8388608 | tf_op jit(solution)/shard_map/pallas_call | solution.py:72
  18.0 1.3 %add_convert_fusion.5 = bf16[192,2048]{1,0:T(8,128)(2,1)S(1)} fusion(bf16[192,2048]{1,0:T(8,128)(2,1)} %collective-permute-done, f32[192,2048]{1,0:T(8,128)S(1)} %shard_map.95, pred[]{:T(512)S(6)} %eq.20), kind=kLoop, calls=%fused_computation.23 | loop fusion | flops 1572864 | bytes 3145729 | tf_op jit(solution)/shard_map/convert_element_type | solution.py:319
  19.3 3.7 %collective-permute-start.1 = (bf16[192,2048]{1,0:T(8,128)(2,1)S(1)}, bf16[192,2048]{1,0:T(8,128)(2,1)S(1)}, u32[]{:S(2)}, u32[]{:S(2)}) collective-permute-start(bf16[192,2048]{1,0:T(8,128)(2,1)S(1)} %add_convert_fusion.5), channel_id=1, source_target_pairs={{0,4},{6,10},{10,14},{1,5},{7,11},{11,15},{16,20},{22,26},{26,30},... | collective-permute-start | bytes 2359304 | tf_op jit(solution)/shard_map/ppermute | solution.py:256
  23.0 1.4 %add_convert_fusion.4 = bf16[192,2048]{1,0:T(8,128)(2,1)S(1)} fusion(bf16[192,2048]{1,0:T(8,128)(2,1)} %collective-permute-done.2, f32[192,2048]{1,0:T(8,128)S(1)} %shard_map.95, pred[]{:T(512)S(6)} %eq.20), kind=kLoop, calls=%fused_computation.22 | loop fusion | flops 1572864 | bytes 3145729 | tf_op jit(solution)/shard_map/convert_element_type | solution.py:319
  26.5 5.2 %shard_map.96 = f32[192,2048]{1,0:T(8,128)S(1)} custom-call(s32[2]{0:T(128)S(1)} %pad_add_fusion.table, bf16[192,2048]{1,0:T(8,128)(2,1)S(1)} %select_select_fusion.2.value_ref, bf16[2048,8192]{1,0:T(8,128)(2,1)} %bitcast.39), custom_call_target="tpu_custom_call" | custom-call | flops 6442450944 | bytes 8388608 | tf_op jit(solution)/shard_map/pallas_call | solution.py:72
  32.8 4.4 %collective-permute-start.5 = (bf16[192,2048]{1,0:T(8,128)(2,1)S(1)}, bf16[192,2048]{1,0:T(8,128)(2,1)S(1)}, u32[]{:S(2)}, u32[]{:S(2)}) collective-permute-start(bf16[192,2048]{1,0:T(8,128)(2,1)S(1)} %add_convert_fusion.3), channel_id=1, source_target_pairs={{0,4},{4,8},{10,14},{1,5},{5,9},{11,15},{16,20},{20,24},{26,30},{1... | collective-permute-start | bytes 2359304 | tf_op jit(solution)/shard_map/ppermute | solution.py:256
  38.5 3.2 %collective-permute-start.8 = (bf16[208,256]{1,0:T(8,128)(2,1)S(1)}, bf16[208,256]{1,0:T(8,128)(2,1)S(1)}, u32[]{:S(2)}, u32[]{:S(2)}) collective-permute-start(bf16[208,256]{1,0:T(8,128)(2,1)S(1)} %convert_element_type.143), channel_id=1, source_target_pairs={{0,8},{4,12},{8,0},{12,4},{1,9},{5,13},{9,1},{13,5},{2,10},{6,14},... | collective-permute-start | bytes 319496 | tf_op jit(solution)/shard_map/ppermute | solution.py:191
  41.9 5.2 %shard_map.97 = f32[192,2048]{1,0:T(8,128)S(1)} custom-call(s32[2]{0:T(128)S(1)} %pad_add_fusion.table, bf16[192,2048]{1,0:T(8,128)(2,1)S(1)} %select_select_fusion.1.value_ref, bf16[2048,8192]{1,0:T(8,128)(2,1)} %bitcast.40), custom_call_target="tpu_custom_call" | custom-call | flops 6442450944 | bytes 8388608 | tf_op jit(solution)/shard_map/pallas_call | solution.py:72
  48.2 4.4 %collective-permute-start.9 = (bf16[192,2048]{1,0:T(8,128)(2,1)S(1)}, bf16[192,2048]{1,0:T(8,128)(2,1)S(1)}, u32[]{:S(2)}, u32[]{:S(2)}) collective-permute-start(bf16[192,2048]{1,0:T(8,128)(2,1)S(1)} %add_convert_fusion.1), channel_id=1, source_target_pairs={{0,4},{4,8},{8,12},{1,5},{5,9},{9,13},{16,20},{20,24},{24,28},{17,... | collective-permute-start | bytes 2359304 | tf_op jit(solution)/shard_map/ppermute | solution.py:256
  52.9 1.3 %collective-permute-start.10 = (bf16[192,2048]{1,0:T(8,128)(2,1)S(1)}, bf16[192,2048]{1,0:T(8,128)(2,1)S(1)}, u32[]{:S(2)}, u32[]{:S(2)}) collective-permute-start(bf16[192,2048]{1,0:T(8,128)(2,1)S(1)} %add_convert_fusion), channel_id=1, source_target_pairs={{4,0},{8,4},{12,8},{5,1},{9,5},{13,9},{20,16},{24,20},{28,24},{21,... | collective-permute-start | bytes 2359304 | tf_op jit(solution)/shard_map/ppermute | solution.py:256
  54.6 5.3 %shard_map.98 = f32[192,2048]{1,0:T(8,128)S(1)} custom-call(s32[2]{0:T(128)S(1)} %pad_add_fusion.table, bf16[192,2048]{1,0:T(8,128)(2,1)S(1)} %select_select_fusion.value_ref, bf16[2048,8192]{1,0:T(8,128)(2,1)} %bitcast.41), custom_call_target="tpu_custom_call" | custom-call | flops 6442450944 | bytes 8388608 | tf_op jit(solution)/shard_map/pallas_call | solution.py:72
  62.5 1.3 %collective-permute-start.12 = (bf16[192,2048]{1,0:T(8,128)(2,1)S(1)}, bf16[192,2048]{1,0:T(8,128)(2,1)S(1)}, u32[]{:S(2)}, u32[]{:S(2)}) collective-permute-start(bf16[192,2048]{1,0:T(8,128)(2,1)S(1)} %get-tuple-element.91), channel_id=1, source_target_pairs={{2,0},{3,1},{6,4},{7,5},{10,8},{11,9},{14,12},{15,13},{18,16},{19,... | collective-permute-start | bytes 2359304 | tf_op jit(solution)/shard_map/ppermute | solution.py:210
  63.8 3.6 %collective-permute-done.10 = bf16[192,2048]{1,0:T(8,128)(2,1)S(1)} collective-permute-done((bf16[192,2048]{1,0:T(8,128)(2,1)S(1)}, bf16[192,2048]{1,0:T(8,128)(2,1)S(1)}, u32[]{:S(2)}, u32[]{:S(2)}) %collective-permute-start.10) | collective-permute-done | bytes 786464 | tf_op jit(solution)/shard_map/ppermute | solution.py:256
  68.3 4.9 %collective-permute-start.17 = (bf16[192,2048]{1,0:T(8,128)(2,1)S(1)}, bf16[192,2048]{1,0:T(8,128)(2,1)S(1)}, u32[]{:S(2)}, u32[]{:S(2)}) collective-permute-start(bf16[192,2048]{1,0:T(8,128)(2,1)S(1)} %get-tuple-element.82), channel_id=1, source_target_pairs={{0,2},{1,3},{4,6},{5,7},{8,10},{9,11},{12,14},{13,15},{16,18},{17,... | collective-permute-start | bytes 2359304 | tf_op jit(solution)/shard_map/ppermute | solution.py:210
  73.2 4.3 %collective-permute-start.15 = (f32[2,192]{1,0:T(2,128)S(1)}, f32[2,192]{1,0:T(2,128)S(1)}, u32[]{:S(2)}, u32[]{:S(2)}) collective-permute-start(f32[2,192]{1,0:T(2,128)S(1)} %pad_maximum_fusion.1), channel_id=1, source_target_pairs={{0,12},{4,0},{8,4},{12,8},{1,13},{5,1},{9,5},{13,9},{16,28},{20,16... | collective-permute-start | bytes 4616 | tf_op jit(solution)/shard_map/ppermute | solution.py:381
  77.5 1.9 %collective-permute-start.13 = (f32[2,192]{1,0:T(2,128)S(1)}, f32[2,192]{1,0:T(2,128)S(1)}, u32[]{:S(2)}, u32[]{:S(2)}) collective-permute-start(f32[2,192]{1,0:T(2,128)S(1)} %pad_maximum_fusion.1), channel_id=1, source_target_pairs={{0,4},{4,8},{8,12},{12,0},{1,5},{5,9},{9,13},{13,1},{16,20},{20,24... | collective-permute-start | bytes 4616 | tf_op jit(solution)/shard_map/ppermute | solution.py:381
  79.4 2.6 %collective-permute-start.14 = (f32[2,192]{1,0:T(2,128)S(1)}, f32[2,192]{1,0:T(2,128)S(1)}, u32[]{:S(2)}, u32[]{:S(2)}) collective-permute-start(f32[2,192]{1,0:T(2,128)S(1)} %pad_maximum_fusion.1), channel_id=1, source_target_pairs={{0,8},{4,12},{8,0},{12,4},{1,9},{5,13},{9,1},{13,5},{16,24},{20,28... | collective-permute-start | bytes 4616 | tf_op jit(solution)/shard_map/ppermute | solution.py:381
  82.1 1.4 %collective-permute-start.16 = (bf16[192,256]{1,0:T(8,128)(2,1)S(1)}, bf16[192,256]{1,0:T(8,128)(2,1)S(1)}, u32[]{:S(2)}, u32[]{:S(2)}) collective-permute-start(bf16[192,256]{1,0:T(8,128)(2,1)S(1)} %get-tuple-element.80), channel_id=1, source_target_pairs={{0,1},{1,0},{2,3},{3,2},{4,5},{5,4},{6,7},{7,6},{8,9},{9,8},{10,11... | collective-permute-start | bytes 294920 | tf_op jit(solution)/shard_map/ppermute | solution.py:200
  83.5 1.3 %collective-permute-done.13 = f32[2,192]{1,0:T(2,128)S(1)} collective-permute-done((f32[2,192]{1,0:T(2,128)S(1)}, f32[2,192]{1,0:T(2,128)S(1)}, u32[]{:S(2)}, u32[]{:S(2)}) %collective-permute-start.13) | collective-permute-done | bytes 1568 | tf_op jit(solution)/shard_map/ppermute | solution.py:381
  85.8 2.0 %collective-permute-done.16.small_early = bf16[192,256]{1,0:T(8,128)(2,1)S(1)} collective-permute-done((bf16[192,256]{1,0:T(8,128)(2,1)S(1)}, bf16[192,256]{1,0:T(8,128)(2,1)S(1)}, u32[]{:S(2)}, u32[]{:S(2)}) %collective-permute-start.16) | collective-permute-done | bytes 98336 | tf_op jit(solution)/shard_map/ppermute | solution.py:200
  90.4 3.7 %collective-permute-start.19 = (bf16[192,256]{1,0:T(8,128)(2,1)S(1)}, bf16[192,256]{1,0:T(8,128)(2,1)S(1)}, u32[]{:S(2)}, u32[]{:S(2)}) collective-permute-start(bf16[192,256]{1,0:T(8,128)(2,1)S(1)} %get-tuple-element.93), channel_id=1, source_target_pairs={{0,4},{4,0},{8,12},{12,8},{1,5},{5,1},{9,13},{13,9},{2,6},{6,2},{1... | collective-permute-start | bytes 294920 | tf_op jit(solution)/shard_map/ppermute | solution.py:191
  94.1 1.4 %fusion.16.early = bf16[192,2048]{1,0:T(8,128)(2,1)S(1)} fusion(bf16[192,2048]{1,0:T(8,128)(2,1)S(1)} %collective-permute-done.11, bf16[192,2048]{1,0:T(8,128)(2,1)} %collective-permute-done.4, f32[2048]{0:T(1024)S(1)} %bitcast.45, pred[]{:T(512)S(6)} %eq.20), kind=kLoop, calls=%fused_computation.35 | loop fusion | flops 1572864 | bytes 2367489 | tf_op jit(solution)/shard_map/jit(_where)/select_n | solution.py:370
  96.9 3.4 %collective-permute-start.22 = (bf16[192,2048]{1,0:T(8,128)(2,1)S(1)}, bf16[192,2048]{1,0:T(8,128)(2,1)S(1)}, u32[]{:S(2)}, u32[]{:S(2)}) collective-permute-start(bf16[192,2048]{1,0:T(8,128)(2,1)S(1)} %fusion.17.late), channel_id=1, source_target_pairs={{0,1},{1,0},{4,5},{5,4},{8,9},{9,8},{12,13},{13,12},{16,17},{17,16... | collective-permute-start | bytes 2359304 | tf_op jit(solution)/shard_map/ppermute | solution.py:200
  100.4 6.0 %collective-permute-done.21 = bf16[192,256]{1,0:T(8,128)(2,1)S(1)} collective-permute-done((bf16[192,256]{1,0:T(8,128)(2,1)S(1)}, bf16[192,256]{1,0:T(8,128)(2,1)S(1)}, u32[]{:S(2)}, u32[]{:S(2)}) %collective-permute-start.21) | collective-permute-done | bytes 98336 | tf_op jit(solution)/shard_map/ppermute | solution.py:191
  106.7 4.2 %collective-permute-done.22 = bf16[192,2048]{1,0:T(8,128)(2,1)S(1)} collective-permute-done((bf16[192,2048]{1,0:T(8,128)(2,1)S(1)}, bf16[192,2048]{1,0:T(8,128)(2,1)S(1)}, u32[]{:S(2)}, u32[]{:S(2)}) %collective-permute-start.22) | collective-permute-done | bytes 786464 | tf_op jit(solution)/shard_map/ppermute | solution.py:200
  110.9 1.5 %collective-permute-start.23 = (bf16[192,384]{1,0:T(8,128)(2,1)S(1)}, bf16[192,384]{1,0:T(8,128)(2,1)S(1)}, u32[]{:S(2)}, u32[]{:S(2)}) collective-permute-start(bf16[192,384]{1,0:T(8,128)(2,1)S(1)} %pad_maximum_fusion), channel_id=1, source_target_pairs={{0,1},{1,0},{2,3},{3,2},{4,5},{5,4},{6,7},{7,6},{8,9},{9,8},{10,11... | collective-permute-start | bytes 442376 | tf_op jit(solution)/shard_map/ppermute | solution.py:200
  112.5 2.3 %shard_map.99 = (f32[2048,256]{1,0:T(8,128)S(1)}, f32[256,2048]{1,0:T(8,128)S(1)}) custom-call(s32[2]{0:T(128)S(1)} %pad_add_fusion.table, bf16[192,2048]{1,0:T(8,128)(2,1)S(1)} %fusion.18.value_ref.early, bf16[192,2048]{1,0:T(8,128)(2,1)S(1)} %fusion.17.late, bf16[192,256]{1,0:T(8,128)(2,1)S(1)} %get-tuple-element.90.small_early, ...), custom_call_target="tpu_custom_call" | custom-call | flops 402653184 | bytes 5767168 | tf_op jit(solution)/shard_map/pallas_call | solution.py:135
  116.1 3.9 %shard_map.100 = (f32[2048,256]{1,0:T(8,128)}, f32[256,2048]{1,0:T(8,128)}) custom-call(s32[2]{0:T(128)S(1)} %pad_add_fusion.table, f32[2048,256]{1,0:T(8,128)S(1)} %get-tuple-element.68.down_sum, f32[256,2048]{1,0:T(8,128)S(1)} %get-tuple-element.69.up_sum, bf16[192,2048]{1,0:T(8,128)(2,1)S(1)} %fusion.16.early, ...), custom_call_target="tpu_custom_call" | custom-call | flops 402653184 | bytes 9961472 | tf_op jit(solution)/shard_map/pallas_call | solution.py:135
  (82 shorter events, 16.4 us)
Async XLA Ops:
  0.6 25.3 %copy-start = (bf16[1,2048,256]{2,1,0:T(8,128)(2,1)S(1)}, bf16[1,2048,256]{2,1,0:T(8,128)(2,1)}, u32[]{:S(2)}) copy-start(bf16[1,2048,256]{2,1,0:T(8,128)(2,1)} %param.12) | copy-start | bytes 3145732
  0.6 17.3 %collective-permute-start = (bf16[192,2048]{1,0:T(8,128)(2,1)}, bf16[192,2048]{1,0:T(8,128)(2,1)}, u32[]{:S(2)}, u32[]{:S(2)}) collective-permute-start(bf16[192,2048]{1,0:T(8,128)(2,1)} %param.9), channel_id=1, source_target_pairs={{0,6},{4,10},{8,14},{1,7},{5,11},{9,15},{16,22},{20,26},{24,30},{1... | collective-permute-start | bytes 2359304 | tf_op jit(solution)/shard_map/ppermute | solution.py:272
  6.1 16.9 %collective-permute-start.2 = (bf16[192,2048]{1,0:T(8,128)(2,1)}, bf16[192,2048]{1,0:T(8,128)(2,1)}, u32[]{:S(2)}, u32[]{:S(2)}) collective-permute-start(bf16[192,2048]{1,0:T(8,128)(2,1)} %param.9), channel_id=1, source_target_pairs={{6,2},{10,6},{14,10},{7,3},{11,7},{15,11},{22,18},{26,22},{30,26},... | collective-permute-start | bytes 2359304 | tf_op jit(solution)/shard_map/ppermute | solution.py:256
  7.6 18.7 %collective-permute-start.4 = (bf16[192,2048]{1,0:T(8,128)(2,1)}, bf16[192,2048]{1,0:T(8,128)(2,1)}, u32[]{:S(2)}, u32[]{:S(2)}) collective-permute-start(bf16[192,2048]{1,0:T(8,128)(2,1)} %param.8), channel_id=1, source_target_pairs={{0,1},{1,0},{4,5},{5,4},{8,9},{9,8},{12,13},{13,12},{16,17},{17,16... | collective-permute-start | bytes 2359304 | tf_op jit(solution)/shard_map/ppermute | solution.py:200
  12.6 5.2 %copy-start.6 = (f32[4]{0:T(128)S(1)}, f32[4]{0:T(128)}, u32[]{:S(2)}) copy-start(f32[4]{0:T(128)} %param.14) | copy-start | bytes 52
  19.3 5.8 %copy-start.2 = (bf16[192,2048]{1,0:T(8,128)(2,1)S(1)}, bf16[192,2048]{1,0:T(8,128)(2,1)}, u32[]{:S(2)}) copy-start(bf16[192,2048]{1,0:T(8,128)(2,1)} %param.8) | copy-start | bytes 2359300
  19.3 6.1 %copy-start.1 = (bf16[1,256,2048]{2,1,0:T(8,128)(2,1)S(1)}, bf16[1,256,2048]{2,1,0:T(8,128)(2,1)}, u32[]{:S(2)}) copy-start(bf16[1,256,2048]{2,1,0:T(8,128)(2,1)} %param.13) | copy-start | bytes 3145732
  19.3 13.1 %collective-permute-start.1 = (bf16[192,2048]{1,0:T(8,128)(2,1)S(1)}, bf16[192,2048]{1,0:T(8,128)(2,1)S(1)}, u32[]{:S(2)}, u32[]{:S(2)}) collective-permute-start(bf16[192,2048]{1,0:T(8,128)(2,1)S(1)} %add_convert_fusion.5), channel_id=1, source_target_pairs={{0,4},{6,10},{10,14},{1,5},{7,11},{11,15},{16,20},{22,26},{26,30},... | collective-permute-start | bytes 2359304 | tf_op jit(solution)/shard_map/ppermute | solution.py:256
  24.4 12.9 %collective-permute-start.3 = (bf16[192,2048]{1,0:T(8,128)(2,1)S(1)}, bf16[192,2048]{1,0:T(8,128)(2,1)S(1)}, u32[]{:S(2)}, u32[]{:S(2)}) collective-permute-start(bf16[192,2048]{1,0:T(8,128)(2,1)S(1)} %add_convert_fusion.4), channel_id=1, source_target_pairs={{12,8},{6,2},{10,6},{13,9},{7,3},{11,7},{28,24},{22,18},{26,22},{2... | collective-permute-start | bytes 2359304 | tf_op jit(solution)/shard_map/ppermute | solution.py:256
  31.7 6.7 %collective-permute-start.7 = (bf16[208,256]{1,0:T(8,128)(2,1)S(1)}, bf16[208,256]{1,0:T(8,128)(2,1)S(1)}, u32[]{:S(2)}, u32[]{:S(2)}) collective-permute-start(bf16[208,256]{1,0:T(8,128)(2,1)S(1)} %convert_element_type.141), channel_id=1, source_target_pairs={{0,4},{4,0},{8,12},{12,8},{1,5},{5,1},{9,13},{13,9},{2,6},{6,2},{1... | collective-permute-start | bytes 319496 | tf_op jit(solution)/shard_map/ppermute | solution.py:191
  32.8 15.0 %collective-permute-start.5 = (bf16[192,2048]{1,0:T(8,128)(2,1)S(1)}, bf16[192,2048]{1,0:T(8,128)(2,1)S(1)}, u32[]{:S(2)}, u32[]{:S(2)}) collective-permute-start(bf16[192,2048]{1,0:T(8,128)(2,1)S(1)} %add_convert_fusion.3), channel_id=1, source_target_pairs={{0,4},{4,8},{10,14},{1,5},{5,9},{11,15},{16,20},{20,24},{26,30},{1... | collective-permute-start | bytes 2359304 | tf_op jit(solution)/shard_map/ppermute | solution.py:256
  37.7 15.0 %collective-permute-start.6 = (bf16[192,2048]{1,0:T(8,128)(2,1)S(1)}, bf16[192,2048]{1,0:T(8,128)(2,1)S(1)}, u32[]{:S(2)}, u32[]{:S(2)}) collective-permute-start(bf16[192,2048]{1,0:T(8,128)(2,1)S(1)} %add_convert_fusion.2), channel_id=1, source_target_pairs={{8,4},{12,8},{6,2},{9,5},{13,9},{7,3},{24,20},{28,24},{22,18},{25,... | collective-permute-start | bytes 2359304 | tf_op jit(solution)/shard_map/ppermute | solution.py:256
  38.5 15.8 %collective-permute-start.8 = (bf16[208,256]{1,0:T(8,128)(2,1)S(1)}, bf16[208,256]{1,0:T(8,128)(2,1)S(1)}, u32[]{:S(2)}, u32[]{:S(2)}) collective-permute-start(bf16[208,256]{1,0:T(8,128)(2,1)S(1)} %convert_element_type.143), channel_id=1, source_target_pairs={{0,8},{4,12},{8,0},{12,4},{1,9},{5,13},{9,1},{13,5},{2,10},{6,14},... | collective-permute-start | bytes 319496 | tf_op jit(solution)/shard_map/ppermute | solution.py:191
  48.2 15.6 %collective-permute-start.9 = (bf16[192,2048]{1,0:T(8,128)(2,1)S(1)}, bf16[192,2048]{1,0:T(8,128)(2,1)S(1)}, u32[]{:S(2)}, u32[]{:S(2)}) collective-permute-start(bf16[192,2048]{1,0:T(8,128)(2,1)S(1)} %add_convert_fusion.1), channel_id=1, source_target_pairs={{0,4},{4,8},{8,12},{1,5},{5,9},{9,13},{16,20},{20,24},{24,28},{17,... | collective-permute-start | bytes 2359304 | tf_op jit(solution)/shard_map/ppermute | solution.py:256
  52.9 14.6 %collective-permute-start.10 = (bf16[192,2048]{1,0:T(8,128)(2,1)S(1)}, bf16[192,2048]{1,0:T(8,128)(2,1)S(1)}, u32[]{:S(2)}, u32[]{:S(2)}) collective-permute-start(bf16[192,2048]{1,0:T(8,128)(2,1)S(1)} %add_convert_fusion), channel_id=1, source_target_pairs={{4,0},{8,4},{12,8},{5,1},{9,5},{13,9},{20,16},{24,20},{28,24},{21,... | collective-permute-start | bytes 2359304 | tf_op jit(solution)/shard_map/ppermute | solution.py:256
  54.6 5.3 %copy-start.5 = (s32[192]{0:T(256)S(1)}, s32[192]{0:T(256)}, u32[]{:S(2)}) copy-start(s32[192]{0:T(256)} %param.15) | copy-start | bytes 2308
  59.9 1.1 copy-start.3
  59.9 1.8 %copy-start.4 = (f32[1,2048]{1,0:T(1,128)S(1)}, f32[1,2048]{1,0:T(1,128)}, u32[]{:S(2)}) copy-start(f32[1,2048]{1,0:T(1,128)} %param.10) | copy-start | bytes 24580
  61.0 6.5 %collective-permute-start.11 = (bf16[192,2048]{1,0:T(8,128)(2,1)S(1)}, bf16[192,2048]{1,0:T(8,128)(2,1)S(1)}, u32[]{:S(2)}, u32[]{:S(2)}) collective-permute-start(bf16[192,2048]{1,0:T(8,128)(2,1)S(1)} %copy-done.3), channel_id=1, source_target_pairs={{2,3},{3,2},{6,7},{7,6},{10,11},{11,10},{14,15},{15,14},{18,19},{1... | collective-permute-start | bytes 2359304 | tf_op jit(solution)/shard_map/ppermute | solution.py:200
  62.5 5.0 %collective-permute-start.12 = (bf16[192,2048]{1,0:T(8,128)(2,1)S(1)}, bf16[192,2048]{1,0:T(8,128)(2,1)S(1)}, u32[]{:S(2)}, u32[]{:S(2)}) collective-permute-start(bf16[192,2048]{1,0:T(8,128)(2,1)S(1)} %get-tuple-element.91), channel_id=1, source_target_pairs={{2,0},{3,1},{6,4},{7,5},{10,8},{11,9},{14,12},{15,13},{18,16},{19,... | collective-permute-start | bytes 2359304 | tf_op jit(solution)/shard_map/ppermute | solution.py:210
  68.3 19.6 %collective-permute-start.17 = (bf16[192,2048]{1,0:T(8,128)(2,1)S(1)}, bf16[192,2048]{1,0:T(8,128)(2,1)S(1)}, u32[]{:S(2)}, u32[]{:S(2)}) collective-permute-start(bf16[192,2048]{1,0:T(8,128)(2,1)S(1)} %get-tuple-element.82), channel_id=1, source_target_pairs={{0,2},{1,3},{4,6},{5,7},{8,10},{9,11},{12,14},{13,15},{16,18},{17,... | collective-permute-start | bytes 2359304 | tf_op jit(solution)/shard_map/ppermute | solution.py:210
  73.2 10.2 %collective-permute-start.15 = (f32[2,192]{1,0:T(2,128)S(1)}, f32[2,192]{1,0:T(2,128)S(1)}, u32[]{:S(2)}, u32[]{:S(2)}) collective-permute-start(f32[2,192]{1,0:T(2,128)S(1)} %pad_maximum_fusion.1), channel_id=1, source_target_pairs={{0,12},{4,0},{8,4},{12,8},{1,13},{5,1},{9,5},{13,9},{16,28},{20,16... | collective-permute-start | bytes 4616 | tf_op jit(solution)/shard_map/ppermute | solution.py:381
  77.5 7.3 %collective-permute-start.13 = (f32[2,192]{1,0:T(2,128)S(1)}, f32[2,192]{1,0:T(2,128)S(1)}, u32[]{:S(2)}, u32[]{:S(2)}) collective-permute-start(f32[2,192]{1,0:T(2,128)S(1)} %pad_maximum_fusion.1), channel_id=1, source_target_pairs={{0,4},{4,8},{8,12},{12,0},{1,5},{5,9},{9,13},{13,1},{16,20},{20,24... | collective-permute-start | bytes 4616 | tf_op jit(solution)/shard_map/ppermute | solution.py:381
  79.4 6.4 %collective-permute-start.14 = (f32[2,192]{1,0:T(2,128)S(1)}, f32[2,192]{1,0:T(2,128)S(1)}, u32[]{:S(2)}, u32[]{:S(2)}) collective-permute-start(f32[2,192]{1,0:T(2,128)S(1)} %pad_maximum_fusion.1), channel_id=1, source_target_pairs={{0,8},{4,12},{8,0},{12,4},{1,9},{5,13},{9,1},{13,5},{16,24},{20,28... | collective-permute-start | bytes 4616 | tf_op jit(solution)/shard_map/ppermute | solution.py:381
  82.1 5.8 %collective-permute-start.16 = (bf16[192,256]{1,0:T(8,128)(2,1)S(1)}, bf16[192,256]{1,0:T(8,128)(2,1)S(1)}, u32[]{:S(2)}, u32[]{:S(2)}) collective-permute-start(bf16[192,256]{1,0:T(8,128)(2,1)S(1)} %get-tuple-element.80), channel_id=1, source_target_pairs={{0,1},{1,0},{2,3},{3,2},{4,5},{5,4},{6,7},{7,6},{8,9},{9,8},{10,11... | collective-permute-start | bytes 294920 | tf_op jit(solution)/shard_map/ppermute | solution.py:200
  88.1 12.2 %collective-permute-start.20 = (bf16[192,2048]{1,0:T(8,128)(2,1)S(1)}, bf16[192,2048]{1,0:T(8,128)(2,1)S(1)}, u32[]{:S(2)}, u32[]{:S(2)}) collective-permute-start(bf16[192,2048]{1,0:T(8,128)(2,1)S(1)} %multiply_convert_fusion.1), channel_id=1, source_target_pairs={{2,3},{3,2},{6,7},{7,6},{10,11},{11,10},{14,15},{15,14},{18,19},{1... | collective-permute-start | bytes 2359304 | tf_op jit(solution)/shard_map/ppermute | solution.py:200
  90.4 9.8 %collective-permute-start.19 = (bf16[192,256]{1,0:T(8,128)(2,1)S(1)}, bf16[192,256]{1,0:T(8,128)(2,1)S(1)}, u32[]{:S(2)}, u32[]{:S(2)}) collective-permute-start(bf16[192,256]{1,0:T(8,128)(2,1)S(1)} %get-tuple-element.93), channel_id=1, source_target_pairs={{0,4},{4,0},{8,12},{12,8},{1,5},{5,1},{9,13},{13,9},{2,6},{6,2},{1... | collective-permute-start | bytes 294920 | tf_op jit(solution)/shard_map/ppermute | solution.py:191
  95.6 4.9 %collective-permute-start.18 = (f32[192]{0:T(256)S(1)}, f32[192]{0:T(256)S(1)}, u32[]{:S(2)}, u32[]{:S(2)}) collective-permute-start(f32[192]{0:T(256)S(1)} %bitcast.54), channel_id=1, source_target_pairs={{0,2},{1,3},{4,6},{5,7},{8,10},{9,11},{12,14},{13,15},{16,18},{17,... | collective-permute-start | bytes 2312 | tf_op jit(solution)/shard_map/ppermute | solution.py:210
  96.9 14.1 %collective-permute-start.22 = (bf16[192,2048]{1,0:T(8,128)(2,1)S(1)}, bf16[192,2048]{1,0:T(8,128)(2,1)S(1)}, u32[]{:S(2)}, u32[]{:S(2)}) collective-permute-start(bf16[192,2048]{1,0:T(8,128)(2,1)S(1)} %fusion.17.late), channel_id=1, source_target_pairs={{0,1},{1,0},{4,5},{5,4},{8,9},{9,8},{12,13},{13,12},{16,17},{17,16... | collective-permute-start | bytes 2359304 | tf_op jit(solution)/shard_map/ppermute | solution.py:200
  100.3 6.1 %collective-permute-start.21 = (bf16[192,256]{1,0:T(8,128)(2,1)S(1)}, bf16[192,256]{1,0:T(8,128)(2,1)S(1)}, u32[]{:S(2)}, u32[]{:S(2)}) collective-permute-start(bf16[192,256]{1,0:T(8,128)(2,1)S(1)} %convert_element_type.164), channel_id=1, source_target_pairs={{0,8},{4,12},{8,0},{12,4},{1,9},{5,13},{9,1},{13,5},{2,10},{6,14},... | collective-permute-start | bytes 294920 | tf_op jit(solution)/shard_map/ppermute | solution.py:191
  110.9 5.1 %collective-permute-start.23 = (bf16[192,384]{1,0:T(8,128)(2,1)S(1)}, bf16[192,384]{1,0:T(8,128)(2,1)S(1)}, u32[]{:S(2)}, u32[]{:S(2)}) collective-permute-start(bf16[192,384]{1,0:T(8,128)(2,1)S(1)} %pad_maximum_fusion), channel_id=1, source_target_pairs={{0,1},{1,0},{2,3},{3,2},{4,5},{5,4},{6,7},{7,6},{8,9},{9,8},{10,11... | collective-permute-start | bytes 442376 | tf_op jit(solution)/shard_map/ppermute | solution.py:200

commit v12 on v10

--- a/solution.py
+++ b/solution.py
@@ -215,10 +215,6 @@
         )
         for step in range(1, count)
     ]
-
-
-def to_other_core(value, source):
-    return lax.ppermute(value, "section", [(source, 1 - source)])
 
 
 def on_device(
@@ -364,22 +360,22 @@
     )
 
     pulled_here = (gain_row * (sum(parts) + low_product)).astype(BF16)
-    pulled = to_other_core(pulled_here, 1)
-    from_left, from_right, *small_early_all, _ = lax.optimization_barrier(
-        (from_left, from_right, *small_early_all, pulled_here)
+    swap = [(0, 1), (1, 0)]
+    pulled = lax.ppermute(pulled_here, "section", swap)
+    pulled_others = with_other_replicas(pulled_here, (1,))[1:]
+    from_left, from_right, _, *pulled_others = lax.optimization_barrier(
+        (from_left, from_right, pulled_here, *pulled_others)
     )
 
     projected = parts[-1] + from_left.astype(F32) + from_right.astype(F32) + low_product
     hidden = (token_float + inv_first * projected).astype(BF16)
-    late_others = with_other_replicas(jnp.where(is_first, hidden, pulled_here))[1:]
-    swap = [(0, 1), (1, 0)]
+    hidden_others = with_other_replicas(hidden, (0,))[1:]
     swapped = [
         lax.ppermute(jnp.where(is_first, hidden, other), "section", swap) for other in early_all[1:]
     ]
-    hidden_on_second = swapped[0] if swapped else to_other_core(hidden, 0)
+    hidden_on_second = swapped[0] if swapped else lax.ppermute(hidden, "section", swap)
     cotangent_all = [cotangent] + swapped
-    hidden_here = jnp.where(is_first, hidden, hidden_on_second)
-    hidden_float = hidden_here.astype(F32)
+    hidden_float = hidden.astype(F32)
     pulled_float = pulled.astype(F32)
     row_sums = jnp.stack(
         [jnp.sum(hidden_float * hidden_float, axis=1), jnp.sum(hidden_float * pulled_float, axis=1)]
@@ -392,39 +388,42 @@
     else:
         for step in doubling_steps():
             row_sums = sum_step(row_sums, step, F32)
-    inv_second = lax.rsqrt(row_sums[0] / features + EPSILON)[:, None]
+    row_sums, *small_early_all = lax.optimization_barrier((row_sums, *small_early_all))
+    inv_second = lax.rsqrt(row_sums[0] / features + EPSILON)
+    inv_on_second = lax.ppermute(inv_second, "section", swap)[:, None]
+    inv_second = inv_second[:, None]
     toward_hidden = row_sums[1][:, None] * inv_second * inv_second * inv_second / features
     hidden_grad = cotangent.astype(F32) + inv_second * pulled_float - toward_hidden * hidden_float
     late = jnp.where(
-        is_first, hidden_grad.astype(BF16), (hidden_float * gain_row).astype(BF16)
+        is_first,
+        hidden_grad.astype(BF16),
+        (hidden_on_second.astype(F32) * gain_row).astype(BF16),
     )
     rank_late = jnp.where(is_first, times_up_transposed(late), times_down(late))
     for step in doubling_steps():
         rank_late = sum_step(rank_late, step)
 
+    inv_second = jnp.where(is_first, inv_second, inv_on_second)
+    row_scale = jnp.where(is_first, inv_first, inv_second)
+    small_late = (coefficients * rank_late * row_scale).astype(BF16)
+    beside = jnp.concatenate(
+        [
+            small_late,
+            jnp.broadcast_to(inv_second, (rows, 64)).astype(BF16),
+            jnp.broadcast_to(toward_hidden, (rows, 64)).astype(BF16),
+        ],
+        axis=1,
+    )
+    small_late_all = with_other_replicas(beside)
     swapped = [
-        lax.ppermute(lax.optimization_barrier((other, rank_late))[0], "section", swap)
-        for other in late_others
+        lax.ppermute(
+            lax.optimization_barrier((jnp.where(is_first, *pair), beside))[0], "section", swap
+        )
+        for pair in zip(hidden_others, pulled_others)
     ]
-    hidden_all = [hidden_here] + [
-        jnp.where(is_first, *pair) for pair in zip(late_others, swapped)
-    ]
+    hidden_all = [hidden] + [jnp.where(is_first, *pair) for pair in zip(hidden_others, swapped)]
     pulled_all = [pulled] + swapped
-
-    small_late = (coefficients * rank_late * jnp.where(is_first, inv_first, inv_second)).astype(BF16)
-    small_late_all = with_other_replicas(
-        jnp.concatenate(
-            [
-                small_late,
-                jnp.broadcast_to(inv_second, (rows, 64)).astype(BF16),
-                jnp.broadcast_to(toward_hidden, (rows, 64)).astype(BF16),
-            ],
-            axis=1,
-        )
-    )
-    small_early_own = (
-        small_early.astype(F32) * jnp.where(is_first, inv_first, inv_second)
-    ).astype(BF16)
+    small_early_own = (small_early.astype(F32) * row_scale).astype(BF16)
     sums = gradient_call(
         own_gradient_kernel,
         table, [], [early, late], [small_early_own, small_late], width, ranks, rows,

time: 104 us -> 109 us (1.048)
  starting transfers between devices: 39.9 us -> 47.1 us
  waiting for transfers between devices: 22.6 us -> 20.2 us
    ppermute x1, starting transfers between devices: 0.07 us -> 5.62 us  [on_device(): lax.ppermute(jnp.where(is_first, hidden, other), 'section', swap)]
    ppermute x4 -> x5, waiting for transfers between devices: 8.43 us -> 5.05 us  [with_other_replicas(): lax.ppermute(value, ('section', 'replica'), [(s * count + r, s * count +...]
    ppermute x4 -> x5, starting transfers between devices: 3.91 us -> 6.75 us  [with_other_replicas(): lax.ppermute(value, ('section', 'replica'), [(s * count + r, s * count +...]
    ppermute x7, waiting for transfers between devices: 1.07 us -> 3.61 us  [line(): return lax.ppermute(value, ('tensor', 'section'), pairs)]
    ppermute x1, waiting for transfers between devices: 2.26 us -> 0.01 us  [on_device(): lax.ppermute(jnp.where(is_first, hidden, other), 'section', swap)]
    ppermute x3, waiting for transfers between devices: 2.06 us -> 4.22 us  [on_device(): lax.ppermute(row_sums, 'tensor', [(z, (z + step) % count) for z in everyo...]
    ppermute x4, waiting for transfers between devices: 8.29 us -> 6.89 us  [sum_step(): other = lax.ppermute(value.astype(wire), 'tensor', pairs)]
  transfers between devices with their start and end apart: 22 -> 24, of which waited for: 10 -> 9; matrix products, arithmetic and copies ran while one was open for 12% -> 10% of each run, Pallas kernels for 22% -> 21%
where the time goes in v12:
time: 109 us; the launch traced here: 108 us
  starting transfers between devices  47.1 us (43%)
  Pallas kernels  27.4 us (25%)
  waiting for transfers between devices  20.2 us (19%)
  other arithmetic  8.85 us (8%)
  matrix products  2.95 us (3%)
  between operations  1.19 us (1%)
    pallas_call x4, Pallas kernels, block_product(): pl.pallas_call(functools.partial(block_kernel, blocks=blocks, tile=tile,...  20.9 us
    ppermute x7, starting transfers between devices, line(): return lax.ppermute(value, ('tensor', 'section'), pairs)  17.3 us
    ppermute x4, starting transfers between devices, sum_step(): other = lax.ppermute(value.astype(wire), 'tensor', pairs)  8.48 us
    ppermute x4, waiting for transfers between devices, sum_step(): other = lax.ppermute(value.astype(wire), 'tensor', pairs)  6.89 us
    ppermute x5, starting transfers between devices, with_other_replicas(): lax.ppermute(value, ('section', 'replica'), [(s * count + r, s * count +...  6.75 us
    pallas_call x2, Pallas kernels, gradient_call(): pl.pallas_call(kernel, grid_spec=pltpu.PrefetchScalarGridSpec(num_scalar_...  6.46 us
    ppermute x1, starting transfers between devices, on_device(): lax.ppermute(jnp.where(is_first, hidden, other), 'section', swap)  5.62 us
    ppermute x1, starting transfers between devices, on_device(): lax.ppermute(cotangent, ('tensor', 'section'), [(2 * z, 2 * (z + 1) + 1)...  5.44 us
  transfers between devices with their start and end apart: 24, of which 9 were waited for; matrix products, arithmetic and copies ran while one was open for 10% of the time, Pallas kernels for 21%

profile of v12, /device:TPU:0, one launch (start us, length us, event | category | flops | bytes accessed | tf_op | source)
XLA Modules:
  0.0 108.2 jit_solution(620385533807560697)
XLA Ops:
  0.6 5.4 %collective-permute-start = (bf16[192,2048]{1,0:T(8,128)(2,1)}, bf16[192,2048]{1,0:T(8,128)(2,1)}, u32[]{:S(2)}, u32[]{:S(2)}) collective-permute-start(bf16[192,2048]{1,0:T(8,128)(2,1)} %param.9), channel_id=1, source_target_pairs={{0,6},{4,10},{8,14},{1,7},{5,11},{9,15},{16,22},{20,26},{24,30},{1... | collective-permute-start | bytes 2359304 | tf_op jit(solution)/shard_map/ppermute | solution.py:280
  6.1 1.6 %collective-permute-start.2 = (bf16[192,2048]{1,0:T(8,128)(2,1)}, bf16[192,2048]{1,0:T(8,128)(2,1)}, u32[]{:S(2)}, u32[]{:S(2)}) collective-permute-start(bf16[192,2048]{1,0:T(8,128)(2,1)} %param.9), channel_id=1, source_target_pairs={{6,2},{10,6},{14,10},{7,3},{11,7},{15,11},{22,18},{26,22},{30,26},... | collective-permute-start | bytes 2359304 | tf_op jit(solution)/shard_map/ppermute | solution.py:264
  7.6 1.4 %fusion.17.value_ref.early = bf16[192,2048]{1,0:T(8,128)(2,1)S(1)} fusion(bf16[192,2048]{1,0:T(8,128)(2,1)} %param.9, bf16[192,2048]{1,0:T(8,128)(2,1)} %param.8, f32[2048]{0:T(1024)} %bitcast.38, pred[]{:T(512)S(6)} %eq.20), kind=kLoop, calls=%fused_computation.35 | loop fusion | flops 1572864 | bytes 2367489 | tf_op jit(solution)/shard_map/jit(_where)/select_n | solution.py:267
  9.1 5.2 %shard_map.95 = f32[192,2048]{1,0:T(8,128)S(1)} custom-call(s32[2]{0:T(128)S(1)} %pad_add_fusion.table, bf16[192,2048]{1,0:T(8,128)(2,1)S(1)} %fusion.17.value_ref.early, bf16[2048,8192]{1,0:T(8,128)(2,1)} %bitcast.41), custom_call_target="tpu_custom_call" | custom-call | flops 6442450944 | bytes 8388608 | tf_op jit(solution)/shard_map/pallas_call | solution.py:72
  15.0 1.4 %add_convert_fusion.5 = bf16[192,2048]{1,0:T(8,128)(2,1)S(1)} fusion(bf16[192,2048]{1,0:T(8,128)(2,1)} %collective-permute-done, f32[192,2048]{1,0:T(8,128)S(1)} %shard_map.95, pred[]{:T(512)S(6)} %eq.20), kind=kLoop, calls=%fused_computation.22 | loop fusion | flops 1572864 | bytes 3145729 | tf_op jit(solution)/shard_map/convert_element_type | solution.py:328
  16.4 3.7 %collective-permute-start.1 = (bf16[192,2048]{1,0:T(8,128)(2,1)S(1)}, bf16[192,2048]{1,0:T(8,128)(2,1)S(1)}, u32[]{:S(2)}, u32[]{:S(2)}) collective-permute-start(bf16[192,2048]{1,0:T(8,128)(2,1)S(1)} %add_convert_fusion.5), channel_id=1, source_target_pairs={{0,4},{6,10},{10,14},{1,5},{7,11},{11,15},{16,20},{22,26},{26,30},... | collective-permute-start | bytes 2359304 | tf_op jit(solution)/shard_map/ppermute | solution.py:264
  20.1 1.3 %add_convert_fusion.4 = bf16[192,2048]{1,0:T(8,128)(2,1)S(1)} fusion(bf16[192,2048]{1,0:T(8,128)(2,1)} %collective-permute-done.2, f32[192,2048]{1,0:T(8,128)S(1)} %shard_map.95, pred[]{:T(512)S(6)} %eq.20), kind=kLoop, calls=%fused_computation.21 | loop fusion | flops 1572864 | bytes 3145729 | tf_op jit(solution)/shard_map/convert_element_type | solution.py:328
  21.4 0.7 collective-permute-start.3
  23.5 5.2 %shard_map.96 = f32[192,2048]{1,0:T(8,128)S(1)} custom-call(s32[2]{0:T(128)S(1)} %pad_add_fusion.table, bf16[192,2048]{1,0:T(8,128)(2,1)S(1)} %select_select_fusion.2.value_ref, bf16[2048,8192]{1,0:T(8,128)(2,1)} %bitcast.42), custom_call_target="tpu_custom_call" | custom-call | flops 6442450944 | bytes 8388608 | tf_op jit(solution)/shard_map/pallas_call | solution.py:72
  28.8 1.6 %collective-permute-start.8 = (bf16[192,2048]{1,0:T(8,128)(2,1)S(1)}, bf16[192,2048]{1,0:T(8,128)(2,1)S(1)}, u32[]{:S(2)}, u32[]{:S(2)}) collective-permute-start(bf16[192,2048]{1,0:T(8,128)(2,1)S(1)} %fusion.17.value_ref.early), channel_id=1, source_target_pairs={{0,1},{1,0},{2,3},{3,2},{4,5},{5,4},{6,7},{7,6},{8,9},{9,8},{10,11... | collective-permute-start | bytes 2359304 | tf_op jit(solution)/shard_map/ppermute | solution.py:211
  30.8 3.9 %collective-permute-start.4 = (bf16[192,2048]{1,0:T(8,128)(2,1)S(1)}, bf16[192,2048]{1,0:T(8,128)(2,1)S(1)}, u32[]{:S(2)}, u32[]{:S(2)}) collective-permute-start(bf16[192,2048]{1,0:T(8,128)(2,1)S(1)} %add_convert_fusion.3), channel_id=1, source_target_pairs={{0,4},{4,8},{10,14},{1,5},{5,9},{11,15},{16,20},{20,24},{26,30},{1... | collective-permute-start | bytes 2359304 | tf_op jit(solution)/shard_map/ppermute | solution.py:264
  35.9 4.3 %collective-permute-start.7 = (bf16[208,256]{1,0:T(8,128)(2,1)S(1)}, bf16[208,256]{1,0:T(8,128)(2,1)S(1)}, u32[]{:S(2)}, u32[]{:S(2)}) collective-permute-start(bf16[208,256]{1,0:T(8,128)(2,1)S(1)} %convert_element_type.141), channel_id=1, source_target_pairs={{0,8},{4,12},{8,0},{12,4},{1,9},{5,13},{9,1},{13,5},{2,10},{6,14},... | collective-permute-start | bytes 319496 | tf_op jit(solution)/shard_map/ppermute | solution.py:202
  40.4 5.2 %shard_map.97 = f32[192,2048]{1,0:T(8,128)S(1)} custom-call(s32[2]{0:T(128)S(1)} %pad_add_fusion.table, bf16[192,2048]{1,0:T(8,128)(2,1)S(1)} %select_select_fusion.1.value_ref, bf16[2048,8192]{1,0:T(8,128)(2,1)} %bitcast.43), custom_call_target="tpu_custom_call" | custom-call | flops 6442450944 | bytes 8388608 | tf_op jit(solution)/shard_map/pallas_call | solution.py:72
  46.0 5.4 %collective-permute-start.9 = (bf16[192,2048]{1,0:T(8,128)(2,1)S(1)}, bf16[192,2048]{1,0:T(8,128)(2,1)S(1)}, u32[]{:S(2)}, u32[]{:S(2)}) collective-permute-start(bf16[192,2048]{1,0:T(8,128)(2,1)S(1)} %add_convert_fusion.1), channel_id=1, source_target_pairs={{0,4},{4,8},{8,12},{1,5},{5,9},{9,13},{16,20},{20,24},{24,28},{17,... | collective-permute-start | bytes 2359304 | tf_op jit(solution)/shard_map/ppermute | solution.py:264
  51.7 1.3 %collective-permute-start.10 = (bf16[192,2048]{1,0:T(8,128)(2,1)S(1)}, bf16[192,2048]{1,0:T(8,128)(2,1)S(1)}, u32[]{:S(2)}, u32[]{:S(2)}) collective-permute-start(bf16[192,2048]{1,0:T(8,128)(2,1)S(1)} %add_convert_fusion), channel_id=1, source_target_pairs={{4,0},{8,4},{12,8},{5,1},{9,5},{13,9},{20,16},{24,20},{28,24},{21,... | collective-permute-start | bytes 2359304 | tf_op jit(solution)/shard_map/ppermute | solution.py:264
  53.0 1.5 %collective-permute-done.7 = bf16[208,256]{1,0:T(8,128)(2,1)S(1)} collective-permute-done((bf16[208,256]{1,0:T(8,128)(2,1)S(1)}, bf16[208,256]{1,0:T(8,128)(2,1)S(1)}, u32[]{:S(2)}, u32[]{:S(2)}) %collective-permute-start.7) | collective-permute-done | bytes 106528 | tf_op jit(solution)/shard_map/ppermute | solution.py:202
  54.9 5.3 %shard_map.98 = f32[192,2048]{1,0:T(8,128)S(1)} custom-call(s32[2]{0:T(128)S(1)} %pad_add_fusion.table, bf16[192,2048]{1,0:T(8,128)(2,1)S(1)} %select_select_fusion.value_ref, bf16[2048,8192]{1,0:T(8,128)(2,1)} %bitcast.44), custom_call_target="tpu_custom_call" | custom-call | flops 6442450944 | bytes 8388608 | tf_op jit(solution)/shard_map/pallas_call | solution.py:72
  60.8 0.8 multiply_convert_fusion.1
  62.4 3.6 %collective-permute-done.10 = bf16[192,2048]{1,0:T(8,128)(2,1)S(1)} collective-permute-done((bf16[192,2048]{1,0:T(8,128)(2,1)S(1)}, bf16[192,2048]{1,0:T(8,128)(2,1)S(1)}, u32[]{:S(2)}, u32[]{:S(2)}) %collective-permute-start.10) | collective-permute-done | bytes 786464 | tf_op jit(solution)/shard_map/ppermute | solution.py:264
  66.0 0.9 fusion.5
  67.1 5.6 %collective-permute-start.17 = (bf16[192,2048]{1,0:T(8,128)(2,1)S(1)}, bf16[192,2048]{1,0:T(8,128)(2,1)S(1)}, u32[]{:S(2)}, u32[]{:S(2)}) collective-permute-start(bf16[192,2048]{1,0:T(8,128)(2,1)S(1)} %broadcast_select_fusion.2), channel_id=1, source_target_pairs={{0,2},{2,0},{1,3},{3,1},{4,6},{6,4},{5,7},{7,5},{8,10},{10,8},{9,1... | collective-permute-start | bytes 2359304 | tf_op jit(solution)/shard_map/ppermute | solution.py:374
  72.7 2.7 %collective-permute-start.15 = (f32[2,192]{1,0:T(2,128)S(1)}, f32[2,192]{1,0:T(2,128)S(1)}, u32[]{:S(2)}, u32[]{:S(2)}) collective-permute-start(f32[2,192]{1,0:T(2,128)S(1)} %pad_maximum_fusion.1), channel_id=1, source_target_pairs={{0,12},{4,0},{8,4},{12,8},{1,13},{5,1},{9,5},{13,9},{2,14},{6,2},{... | collective-permute-start | bytes 4616 | tf_op jit(solution)/shard_map/ppermute | solution.py:385
  76.7 4.1 %collective-permute-done.13 = f32[2,192]{1,0:T(2,128)S(1)} collective-permute-done((f32[2,192]{1,0:T(2,128)S(1)}, f32[2,192]{1,0:T(2,128)S(1)}, u32[]{:S(2)}, u32[]{:S(2)}) %collective-permute-start.13) | collective-permute-done | bytes 1568 | tf_op jit(solution)/shard_map/ppermute | solution.py:385
  80.9 2.6 %collective-permute-start.21 = (bf16[192,2048]{1,0:T(8,128)(2,1)S(1)}, bf16[192,2048]{1,0:T(8,128)(2,1)S(1)}, u32[]{:S(2)}, u32[]{:S(2)}) collective-permute-start(bf16[192,2048]{1,0:T(8,128)(2,1)S(1)} %get-tuple-element.80), channel_id=1, source_target_pairs={{0,1},{1,0},{4,5},{5,4},{8,9},{9,8},{12,13},{13,12},{16,17},{17,16... | collective-permute-start | bytes 2359304 | tf_op jit(solution)/shard_map/ppermute | solution.py:211
  85.1 3.6 %collective-permute-start.19 = (bf16[192,256]{1,0:T(8,128)(2,1)S(1)}, bf16[192,256]{1,0:T(8,128)(2,1)S(1)}, u32[]{:S(2)}, u32[]{:S(2)}) collective-permute-start(bf16[192,256]{1,0:T(8,128)(2,1)S(1)} %get-tuple-element.90), channel_id=1, source_target_pairs={{0,4},{4,0},{8,12},{12,8},{1,5},{5,1},{9,13},{13,9},{2,6},{6,2},{1... | collective-permute-start | bytes 294920 | tf_op jit(solution)/shard_map/ppermute | solution.py:202
  88.7 3.0 %collective-permute-done.19 = bf16[192,256]{1,0:T(8,128)(2,1)S(1)} collective-permute-done((bf16[192,256]{1,0:T(8,128)(2,1)S(1)}, bf16[192,256]{1,0:T(8,128)(2,1)S(1)}, u32[]{:S(2)}, u32[]{:S(2)}) %collective-permute-start.19) | collective-permute-done | bytes 98336 | tf_op jit(solution)/shard_map/ppermute | solution.py:202
  92.2 2.5 %collective-permute-done.21 = bf16[192,2048]{1,0:T(8,128)(2,1)S(1)} collective-permute-done((bf16[192,2048]{1,0:T(8,128)(2,1)S(1)}, bf16[192,2048]{1,0:T(8,128)(2,1)S(1)}, u32[]{:S(2)}, u32[]{:S(2)}) %collective-permute-start.21) | collective-permute-done | bytes 786464 | tf_op jit(solution)/shard_map/ppermute | solution.py:211
  94.9 2.4 %collective-permute-done.20 = bf16[192,256]{1,0:T(8,128)(2,1)S(1)} collective-permute-done((bf16[192,256]{1,0:T(8,128)(2,1)S(1)}, bf16[192,256]{1,0:T(8,128)(2,1)S(1)}, u32[]{:S(2)}, u32[]{:S(2)}) %collective-permute-start.20) | collective-permute-done | bytes 98336 | tf_op jit(solution)/shard_map/ppermute | solution.py:202
  97.7 1.3 %collective-permute-start.23 = (bf16[192,384]{1,0:T(8,128)(2,1)S(1)}, bf16[192,384]{1,0:T(8,128)(2,1)S(1)}, u32[]{:S(2)}, u32[]{:S(2)}) collective-permute-start(bf16[192,384]{1,0:T(8,128)(2,1)S(1)} %pad_maximum_fusion), channel_id=1, source_target_pairs={{0,1},{1,0},{2,3},{3,2},{4,5},{5,4},{6,7},{7,6},{8,9},{9,8},{10,11... | collective-permute-start | bytes 442376 | tf_op jit(solution)/shard_map/ppermute | solution.py:211
  99.1 2.3 %shard_map.99 = (f32[2048,256]{1,0:T(8,128)S(1)}, f32[256,2048]{1,0:T(8,128)S(1)}) custom-call(s32[2]{0:T(128)S(1)} %pad_add_fusion.table, bf16[192,2048]{1,0:T(8,128)(2,1)S(1)} %fusion.17.value_ref.early, bf16[192,2048]{1,0:T(8,128)(2,1)S(1)} %fusion.16.late, bf16[192,256]{1,0:T(8,128)(2,1)S(1)} %get-tuple-element.86.small_early, ...), custom_call_target="tpu_custom_call" | custom-call | flops 402653184 | bytes 5767168 | tf_op jit(solution)/shard_map/pallas_call | solution.py:145
  101.5 2.5 %collective-permute-done.23.small_late = bf16[192,384]{1,0:T(8,128)(2,1)S(1)} collective-permute-done((bf16[192,384]{1,0:T(8,128)(2,1)S(1)}, bf16[192,384]{1,0:T(8,128)(2,1)S(1)}, u32[]{:S(2)}, u32[]{:S(2)}) %collective-permute-start.23) | collective-permute-done | bytes 147488 | tf_op jit(solution)/shard_map/ppermute | solution.py:211
  104.0 4.2 %shard_map.100 = (f32[2048,256]{1,0:T(8,128)}, f32[256,2048]{1,0:T(8,128)}) custom-call(s32[2]{0:T(128)S(1)} %pad_add_fusion.table, f32[1,2048]{1,0:T(1,128)S(1)} %copy-done.1, f32[2048,256]{1,0:T(8,128)S(1)} %get-tuple-element.67.down_sum, f32[256,2048]{1,0:T(8,128)S(1)} %get-tuple-element.68.up_sum, bf16[192,2048]{1,0:T(8,128)(2,1)S(1)} %collective-permute-done.8.early, ...), custom_call_target="tpu_custom_call" | custom-call | flops 402653184 | bytes 11534336 | tf_op jit(solution)/shard_map/pallas_call | solution.py:145
  (82 shorter events, 10.6 us)
Async XLA Ops:
  0.6 22.3 %copy-start = (bf16[1,2048,256]{2,1,0:T(8,128)(2,1)S(1)}, bf16[1,2048,256]{2,1,0:T(8,128)(2,1)}, u32[]{:S(2)}) copy-start(bf16[1,2048,256]{2,1,0:T(8,128)(2,1)} %param.12) | copy-start | bytes 3145732
  0.6 14.3 %collective-permute-start = (bf16[192,2048]{1,0:T(8,128)(2,1)}, bf16[192,2048]{1,0:T(8,128)(2,1)}, u32[]{:S(2)}, u32[]{:S(2)}) collective-permute-start(bf16[192,2048]{1,0:T(8,128)(2,1)} %param.9), channel_id=1, source_target_pairs={{0,6},{4,10},{8,14},{1,7},{5,11},{9,15},{16,22},{20,26},{24,30},{1... | collective-permute-start | bytes 2359304 | tf_op jit(solution)/shard_map/ppermute | solution.py:280
  6.1 14.0 %collective-permute-start.2 = (bf16[192,2048]{1,0:T(8,128)(2,1)}, bf16[192,2048]{1,0:T(8,128)(2,1)}, u32[]{:S(2)}, u32[]{:S(2)}) collective-permute-start(bf16[192,2048]{1,0:T(8,128)(2,1)} %param.9), channel_id=1, source_target_pairs={{6,2},{10,6},{14,10},{7,3},{11,7},{15,11},{22,18},{26,22},{30,26},... | collective-permute-start | bytes 2359304 | tf_op jit(solution)/shard_map/ppermute | solution.py:264
  9.1 5.2 %copy-start.6 = (f32[4]{0:T(128)S(1)}, f32[4]{0:T(128)}, u32[]{:S(2)}) copy-start(f32[4]{0:T(128)} %param.14) | copy-start | bytes 52
  16.4 5.8 %copy-start.3 = (bf16[192,2048]{1,0:T(8,128)(2,1)S(1)}, bf16[192,2048]{1,0:T(8,128)(2,1)}, u32[]{:S(2)}) copy-start(bf16[192,2048]{1,0:T(8,128)(2,1)} %param.8) | copy-start | bytes 2359300
  16.4 6.0 %copy-start.2 = (bf16[1,256,2048]{2,1,0:T(8,128)(2,1)S(1)}, bf16[1,256,2048]{2,1,0:T(8,128)(2,1)}, u32[]{:S(2)}) copy-start(bf16[1,256,2048]{2,1,0:T(8,128)(2,1)} %param.13) | copy-start | bytes 3145732
  16.4 14.0 %collective-permute-start.1 = (bf16[192,2048]{1,0:T(8,128)(2,1)S(1)}, bf16[192,2048]{1,0:T(8,128)(2,1)S(1)}, u32[]{:S(2)}, u32[]{:S(2)}) collective-permute-start(bf16[192,2048]{1,0:T(8,128)(2,1)S(1)} %add_convert_fusion.5), channel_id=1, source_target_pairs={{0,4},{6,10},{10,14},{1,5},{7,11},{11,15},{16,20},{22,26},{26,30},... | collective-permute-start | bytes 2359304 | tf_op jit(solution)/shard_map/ppermute | solution.py:264
  21.4 13.3 %collective-permute-start.3 = (bf16[192,2048]{1,0:T(8,128)(2,1)S(1)}, bf16[192,2048]{1,0:T(8,128)(2,1)S(1)}, u32[]{:S(2)}, u32[]{:S(2)}) collective-permute-start(bf16[192,2048]{1,0:T(8,128)(2,1)S(1)} %add_convert_fusion.4), channel_id=1, source_target_pairs={{12,8},{6,2},{10,6},{13,9},{7,3},{11,7},{28,24},{22,18},{26,22},{2... | collective-permute-start | bytes 2359304 | tf_op jit(solution)/shard_map/ppermute | solution.py:264
  28.8 7.0 %collective-permute-start.6 = (bf16[208,256]{1,0:T(8,128)(2,1)S(1)}, bf16[208,256]{1,0:T(8,128)(2,1)S(1)}, u32[]{:S(2)}, u32[]{:S(2)}) collective-permute-start(bf16[208,256]{1,0:T(8,128)(2,1)S(1)} %convert_element_type.139), channel_id=1, source_target_pairs={{0,4},{4,0},{8,12},{12,8},{1,5},{5,1},{9,13},{13,9},{2,6},{6,2},{1... | collective-permute-start | bytes 319496 | tf_op jit(solution)/shard_map/ppermute | solution.py:202
  28.8 31.3 %collective-permute-start.8 = (bf16[192,2048]{1,0:T(8,128)(2,1)S(1)}, bf16[192,2048]{1,0:T(8,128)(2,1)S(1)}, u32[]{:S(2)}, u32[]{:S(2)}) collective-permute-start(bf16[192,2048]{1,0:T(8,128)(2,1)S(1)} %fusion.17.value_ref.early), channel_id=1, source_target_pairs={{0,1},{1,0},{2,3},{3,2},{4,5},{5,4},{6,7},{7,6},{8,9},{9,8},{10,11... | collective-permute-start | bytes 2359304 | tf_op jit(solution)/shard_map/ppermute | solution.py:211
  30.8 14.8 %collective-permute-start.4 = (bf16[192,2048]{1,0:T(8,128)(2,1)S(1)}, bf16[192,2048]{1,0:T(8,128)(2,1)S(1)}, u32[]{:S(2)}, u32[]{:S(2)}) collective-permute-start(bf16[192,2048]{1,0:T(8,128)(2,1)S(1)} %add_convert_fusion.3), channel_id=1, source_target_pairs={{0,4},{4,8},{10,14},{1,5},{5,9},{11,15},{16,20},{20,24},{26,30},{1... | collective-permute-start | bytes 2359304 | tf_op jit(solution)/shard_map/ppermute | solution.py:264
  35.1 16.4 %collective-permute-start.5 = (bf16[192,2048]{1,0:T(8,128)(2,1)S(1)}, bf16[192,2048]{1,0:T(8,128)(2,1)S(1)}, u32[]{:S(2)}, u32[]{:S(2)}) collective-permute-start(bf16[192,2048]{1,0:T(8,128)(2,1)S(1)} %add_convert_fusion.2), channel_id=1, source_target_pairs={{8,4},{12,8},{6,2},{9,5},{13,9},{7,3},{24,20},{28,24},{22,18},{25,... | collective-permute-start | bytes 2359304 | tf_op jit(solution)/shard_map/ppermute | solution.py:264
  35.9 18.6 %collective-permute-start.7 = (bf16[208,256]{1,0:T(8,128)(2,1)S(1)}, bf16[208,256]{1,0:T(8,128)(2,1)S(1)}, u32[]{:S(2)}, u32[]{:S(2)}) collective-permute-start(bf16[208,256]{1,0:T(8,128)(2,1)S(1)} %convert_element_type.141), channel_id=1, source_target_pairs={{0,8},{4,12},{8,0},{12,4},{1,9},{5,13},{9,1},{13,5},{2,10},{6,14},... | collective-permute-start | bytes 319496 | tf_op jit(solution)/shard_map/ppermute | solution.py:202
  46.0 16.4 %collective-permute-start.9 = (bf16[192,2048]{1,0:T(8,128)(2,1)S(1)}, bf16[192,2048]{1,0:T(8,128)(2,1)S(1)}, u32[]{:S(2)}, u32[]{:S(2)}) collective-permute-start(bf16[192,2048]{1,0:T(8,128)(2,1)S(1)} %add_convert_fusion.1), channel_id=1, source_target_pairs={{0,4},{4,8},{8,12},{1,5},{5,9},{9,13},{16,20},{20,24},{24,28},{17,... | collective-permute-start | bytes 2359304 | tf_op jit(solution)/shard_map/ppermute | solution.py:264
  51.7 14.3 %collective-permute-start.10 = (bf16[192,2048]{1,0:T(8,128)(2,1)S(1)}, bf16[192,2048]{1,0:T(8,128)(2,1)S(1)}, u32[]{:S(2)}, u32[]{:S(2)}) collective-permute-start(bf16[192,2048]{1,0:T(8,128)(2,1)S(1)} %add_convert_fusion), channel_id=1, source_target_pairs={{4,0},{8,4},{12,8},{5,1},{9,5},{13,9},{20,16},{24,20},{28,24},{21,... | collective-permute-start | bytes 2359304 | tf_op jit(solution)/shard_map/ppermute | solution.py:264
  54.9 5.3 %copy-start.5 = (s32[192]{0:T(256)S(1)}, s32[192]{0:T(256)}, u32[]{:S(2)}) copy-start(s32[192]{0:T(256)} %param.15) | copy-start | bytes 2308
  60.1 0.7 copy-start.1
  61.6 4.4 %collective-permute-start.11 = (bf16[192,2048]{1,0:T(8,128)(2,1)S(1)}, bf16[192,2048]{1,0:T(8,128)(2,1)S(1)}, u32[]{:S(2)}, u32[]{:S(2)}) collective-permute-start(bf16[192,2048]{1,0:T(8,128)(2,1)S(1)} %get-tuple-element.88), channel_id=1, source_target_pairs={{2,3},{3,2},{6,7},{7,6},{10,11},{11,10},{14,15},{15,14},{18,19},{1... | collective-permute-start | bytes 2359304 | tf_op jit(solution)/shard_map/ppermute | solution.py:211
  62.4 3.7 %collective-permute-start.12 = (bf16[192,2048]{1,0:T(8,128)(2,1)S(1)}, bf16[192,2048]{1,0:T(8,128)(2,1)S(1)}, u32[]{:S(2)}, u32[]{:S(2)}) collective-permute-start(bf16[192,2048]{1,0:T(8,128)(2,1)S(1)} %get-tuple-element.88), channel_id=1, source_target_pairs={{0,2},{2,0},{1,3},{3,1},{4,6},{6,4},{5,7},{7,5},{8,10},{10,8},{9,1... | collective-permute-start | bytes 2359304 | tf_op jit(solution)/shard_map/ppermute | solution.py:364
  66.9 16.6 %copy-start.4 = (bf16[192,2048]{1,0:T(8,128)(2,1)S(1)}, bf16[192,2048]{1,0:T(8,128)(2,1)}, u32[]{:S(2)}) copy-start(bf16[192,2048]{1,0:T(8,128)(2,1)} %param.9) | copy-start | bytes 2359300
  67.1 16.5 %collective-permute-start.17 = (bf16[192,2048]{1,0:T(8,128)(2,1)S(1)}, bf16[192,2048]{1,0:T(8,128)(2,1)S(1)}, u32[]{:S(2)}, u32[]{:S(2)}) collective-permute-start(bf16[192,2048]{1,0:T(8,128)(2,1)S(1)} %broadcast_select_fusion.2), channel_id=1, source_target_pairs={{0,2},{2,0},{1,3},{3,1},{4,6},{6,4},{5,7},{7,5},{8,10},{10,8},{9,1... | collective-permute-start | bytes 2359304 | tf_op jit(solution)/shard_map/ppermute | solution.py:374
  72.7 4.0 %collective-permute-start.15 = (f32[2,192]{1,0:T(2,128)S(1)}, f32[2,192]{1,0:T(2,128)S(1)}, u32[]{:S(2)}, u32[]{:S(2)}) collective-permute-start(f32[2,192]{1,0:T(2,128)S(1)} %pad_maximum_fusion.1), channel_id=1, source_target_pairs={{0,12},{4,0},{8,4},{12,8},{1,13},{5,1},{9,5},{13,9},{2,14},{6,2},{... | collective-permute-start | bytes 4616 | tf_op jit(solution)/shard_map/ppermute | solution.py:385
  75.4 5.4 %collective-permute-start.13 = (f32[2,192]{1,0:T(2,128)S(1)}, f32[2,192]{1,0:T(2,128)S(1)}, u32[]{:S(2)}, u32[]{:S(2)}) collective-permute-start(f32[2,192]{1,0:T(2,128)S(1)} %pad_maximum_fusion.1), channel_id=1, source_target_pairs={{0,4},{4,8},{8,12},{12,0},{1,5},{5,9},{9,13},{13,1},{2,6},{6,10},{... | collective-permute-start | bytes 4616 | tf_op jit(solution)/shard_map/ppermute | solution.py:385
  75.4 5.4 %collective-permute-start.14 = (f32[2,192]{1,0:T(2,128)S(1)}, f32[2,192]{1,0:T(2,128)S(1)}, u32[]{:S(2)}, u32[]{:S(2)}) collective-permute-start(f32[2,192]{1,0:T(2,128)S(1)} %pad_maximum_fusion.1), channel_id=1, source_target_pairs={{0,8},{4,12},{8,0},{12,4},{1,9},{5,13},{9,1},{13,5},{2,10},{6,14},... | collective-permute-start | bytes 4616 | tf_op jit(solution)/shard_map/ppermute | solution.py:385
  76.0 4.8 %collective-permute-start.16 = (bf16[192,256]{1,0:T(8,128)(2,1)S(1)}, bf16[192,256]{1,0:T(8,128)(2,1)S(1)}, u32[]{:S(2)}, u32[]{:S(2)}) collective-permute-start(bf16[192,256]{1,0:T(8,128)(2,1)S(1)} %get-tuple-element.78), channel_id=1, source_target_pairs={{0,1},{1,0},{2,3},{3,2},{4,5},{5,4},{6,7},{7,6},{8,9},{9,8},{10,11... | collective-permute-start | bytes 294920 | tf_op jit(solution)/shard_map/ppermute | solution.py:211
  80.8 2.7 %collective-permute-start.18 = (f32[192]{0:T(256)S(1)}, f32[192]{0:T(256)S(1)}, u32[]{:S(2)}, u32[]{:S(2)}) collective-permute-start(f32[192]{0:T(256)S(1)} %bitcast.47), channel_id=1, source_target_pairs={{0,2},{2,0},{1,3},{3,1},{4,6},{6,4},{5,7},{7,5},{8,10},{10,8},{9,1... | collective-permute-start | bytes 2312 | tf_op jit(solution)/shard_map/ppermute | solution.py:393
  80.9 13.9 %collective-permute-start.21 = (bf16[192,2048]{1,0:T(8,128)(2,1)S(1)}, bf16[192,2048]{1,0:T(8,128)(2,1)S(1)}, u32[]{:S(2)}, u32[]{:S(2)}) collective-permute-start(bf16[192,2048]{1,0:T(8,128)(2,1)S(1)} %get-tuple-element.80), channel_id=1, source_target_pairs={{0,1},{1,0},{4,5},{5,4},{8,9},{9,8},{12,13},{13,12},{16,17},{17,16... | collective-permute-start | bytes 2359304 | tf_op jit(solution)/shard_map/ppermute | solution.py:211
  85.1 6.6 %collective-permute-start.19 = (bf16[192,256]{1,0:T(8,128)(2,1)S(1)}, bf16[192,256]{1,0:T(8,128)(2,1)S(1)}, u32[]{:S(2)}, u32[]{:S(2)}) collective-permute-start(bf16[192,256]{1,0:T(8,128)(2,1)S(1)} %get-tuple-element.90), channel_id=1, source_target_pairs={{0,4},{4,0},{8,12},{12,8},{1,5},{5,1},{9,13},{13,9},{2,6},{6,2},{1... | collective-permute-start | bytes 294920 | tf_op jit(solution)/shard_map/ppermute | solution.py:202
  91.7 5.6 %collective-permute-start.20 = (bf16[192,256]{1,0:T(8,128)(2,1)S(1)}, bf16[192,256]{1,0:T(8,128)(2,1)S(1)}, u32[]{:S(2)}, u32[]{:S(2)}) collective-permute-start(bf16[192,256]{1,0:T(8,128)(2,1)S(1)} %fusion.23), channel_id=1, source_target_pairs={{0,8},{4,12},{8,0},{12,4},{1,9},{5,13},{9,1},{13,5},{2,10},{6,14},... | collective-permute-start | bytes 294920 | tf_op jit(solution)/shard_map/ppermute | solution.py:202
  97.7 3.7 %collective-permute-start.22 = (bf16[192,2048]{1,0:T(8,128)(2,1)S(1)}, bf16[192,2048]{1,0:T(8,128)(2,1)S(1)}, u32[]{:S(2)}, u32[]{:S(2)}) collective-permute-start(bf16[192,2048]{1,0:T(8,128)(2,1)S(1)} %broadcast_select_fusion.1), channel_id=1, source_target_pairs={{0,2},{2,0},{1,3},{3,1},{4,6},{6,4},{5,7},{7,5},{8,10},{10,8},{9,1... | collective-permute-start | bytes 2359304 | tf_op jit(solution)/shard_map/ppermute | solution.py:419
  97.7 6.3 %collective-permute-start.23 = (bf16[192,384]{1,0:T(8,128)(2,1)S(1)}, bf16[192,384]{1,0:T(8,128)(2,1)S(1)}, u32[]{:S(2)}, u32[]{:S(2)}) collective-permute-start(bf16[192,384]{1,0:T(8,128)(2,1)S(1)} %pad_maximum_fusion), channel_id=1, source_target_pairs={{0,1},{1,0},{2,3},{3,2},{4,5},{5,4},{6,7},{7,6},{8,9},{9,8},{10,11... | collective-permute-start | bytes 442376 | tf_op jit(solution)/shard_map/ppermute | solution.py:211

commit v13 on v12

--- a/solution.py
+++ b/solution.py
@@ -277,12 +277,8 @@
     steps_left = doubling_steps()
     arrivals = [
         (
-            lax.ppermute(
-                cotangent,
-                ("tensor", "section"),
-                [(2 * z, 2 * (z + 1) + 1) for z in everyone if z + 1 < count],
-            ),
-            line(cotangent, [], [z for z in everyone if z > 0], -1),
+            line(early, [], [z for z in everyone if z + 1 < count], 1),
+            line(early, [], [z for z in everyone if z > 0], -1),
         )
     ]
     parts = []
@@ -363,13 +359,10 @@
     swap = [(0, 1), (1, 0)]
     pulled = lax.ppermute(pulled_here, "section", swap)
     pulled_others = with_other_replicas(pulled_here, (1,))[1:]
-    from_left, from_right, _, *pulled_others = lax.optimization_barrier(
-        (from_left, from_right, pulled_here, *pulled_others)
-    )
+    from_left, from_right, _ = lax.optimization_barrier((from_left, from_right, pulled_here))
 
     projected = parts[-1] + from_left.astype(F32) + from_right.astype(F32) + low_product
     hidden = (token_float + inv_first * projected).astype(BF16)
-    hidden_others = with_other_replicas(hidden, (0,))[1:]
     swapped = [
         lax.ppermute(jnp.where(is_first, hidden, other), "section", swap) for other in early_all[1:]
     ]
@@ -388,7 +381,7 @@
     else:
         for step in doubling_steps():
             row_sums = sum_step(row_sums, step, F32)
-    row_sums, *small_early_all = lax.optimization_barrier((row_sums, *small_early_all))
+    row_sums, *pulled_others = lax.optimization_barrier((row_sums, *pulled_others))
     inv_second = lax.rsqrt(row_sums[0] / features + EPSILON)
     inv_on_second = lax.ppermute(inv_second, "section", swap)[:, None]
     inv_second = inv_second[:, None]
@@ -400,8 +393,13 @@
         (hidden_on_second.astype(F32) * gain_row).astype(BF16),
     )
     rank_late = jnp.where(is_first, times_up_transposed(late), times_down(late))
-    for step in doubling_steps():
+    hidden_others = with_other_replicas(
+        lax.optimization_barrier((hidden, rank_late))[0], (0,)
+    )[1:]
+    for at, step in enumerate(doubling_steps()):
         rank_late = sum_step(rank_late, step)
+        if at == 0:
+            rank_late, *small_early_all = lax.optimization_barrier((rank_late, *small_early_all))
 
     inv_second = jnp.where(is_first, inv_second, inv_on_second)
     row_scale = jnp.where(is_first, inv_first, inv_second)

time: 109 us -> 105 us (0.963)
  starting transfers between devices: 47.1 us -> 43.4 us
    ppermute x1 -> x0, starting transfers between devices: 5.44 us -> none  [on_device(): lax.ppermute(cotangent, ('tensor', 'section'), [(2 * z, 2 * (z + 1) + 1)...]
    ppermute x1, starting transfers between devices: 5.62 us -> 0.84 us  [on_device(): lax.ppermute(jnp.where(is_first, hidden, other), 'section', swap)]
    ppermute x3, starting transfers between devices: 3.31 us -> 5.8 us  [on_device(): lax.ppermute(row_sums, 'tensor', [(z, (z + step) % count) for z in everyo...]
    ppermute x7 -> x8, waiting for transfers between devices: 3.61 us -> 1.7 us  [line(): return lax.ppermute(value, ('tensor', 'section'), pairs)]
    ppermute x7 -> x8, starting transfers between devices: 17.3 us -> 19.2 us  [line(): return lax.ppermute(value, ('tensor', 'section'), pairs)]
    ppermute x1, starting transfers between devices: 0.07 us -> 1.89 us  [on_device(): pulled = lax.ppermute(pulled_here, 'section', swap)]
    ppermute x1, waiting for transfers between devices: 0.01 us -> 1.13 us  [on_device(): inv_on_second = lax.ppermute(inv_second, 'section', swap)[:, None]]
  transfers between devices with their start and end apart: 24 -> 24, of which waited for: 9 -> 10; matrix products, arithmetic and copies ran while one was open for 10% -> 9% of each run, Pallas kernels for 21% -> 22%
where the time goes in v13:
time: 105 us; the launch traced here: 104 us
  starting transfers between devices  43.4 us (41%)
  Pallas kernels  27.4 us (26%)
  waiting for transfers between devices  19.9 us (19%)
  other arithmetic  8.91 us (8%)
  matrix products  2.96 us (3%)
  between operations  1.18 us (1%)
    pallas_call x4, Pallas kernels, block_product(): pl.pallas_call(functools.partial(block_kernel, blocks=blocks, tile=tile,...  20.9 us
    ppermute x8, starting transfers between devices, line(): return lax.ppermute(value, ('tensor', 'section'), pairs)  19.2 us
    ppermute x4, starting transfers between devices, sum_step(): other = lax.ppermute(value.astype(wire), 'tensor', pairs)  8.08 us
    ppermute x5, starting transfers between devices, with_other_replicas(): lax.ppermute(value, ('section', 'replica'), [(s * count + r, s * count +...  7.45 us
    ppermute x4, waiting for transfers between devices, sum_step(): other = lax.ppermute(value.astype(wire), 'tensor', pairs)  7.37 us
    pallas_call x2, Pallas kernels, gradient_call(): pl.pallas_call(kernel, grid_spec=pltpu.PrefetchScalarGridSpec(num_scalar_...  6.46 us
    ppermute x3, starting transfers between devices, on_device(): lax.ppermute(row_sums, 'tensor', [(z, (z + step) % count) for z in everyo...  5.8 us
    ppermute x5, waiting for transfers between devices, with_other_replicas(): lax.ppermute(value, ('section', 'replica'), [(s * count + r, s * count +...  5.15 us
  transfers between devices with their start and end apart: 24, of which 10 were waited for; matrix products, arithmetic and copies ran while one was open for 9% of the time, Pallas kernels for 22%

profile of v13, /device:TPU:0, one launch (start us, length us, event | category | flops | bytes accessed | tf_op | source)
XLA Modules:
  0.0 104.3 jit_solution(12616237247006182692)
XLA Ops:
  0.7 1.5 %fusion.17.value_ref.early = bf16[192,2048]{1,0:T(8,128)(2,1)S(1)} fusion(bf16[192,2048]{1,0:T(8,128)(2,1)} %param.9, bf16[192,2048]{1,0:T(8,128)(2,1)} %param.8, f32[2048]{0:T(1024)} %bitcast.38, pred[]{:T(512)S(6)} %eq.20), kind=kLoop, calls=%fused_computation.35 | loop fusion | flops 1572864 | bytes 2367489 | tf_op jit(solution)/shard_map/jit(_where)/select_n | solution.py:267
  2.1 1.6 %collective-permute-start = (bf16[192,2048]{1,0:T(8,128)(2,1)S(1)}, bf16[192,2048]{1,0:T(8,128)(2,1)}, u32[]{:S(2)}, u32[]{:S(2)}) collective-permute-start(bf16[192,2048]{1,0:T(8,128)(2,1)S(1)} %fusion.17.value_ref.early), channel_id=1, source_target_pairs={{2,6},{6,10},{10,14},{3,7},{7,11},{11,15},{18,22},{22,26},{26,30},... | collective-permute-start | bytes 2359304 | tf_op jit(solution)/shard_map/ppermute | solution.py:264
  3.8 1.6 %collective-permute-start.2 = (bf16[192,2048]{1,0:T(8,128)(2,1)S(1)}, bf16[192,2048]{1,0:T(8,128)(2,1)}, u32[]{:S(2)}, u32[]{:S(2)}) collective-permute-start(bf16[192,2048]{1,0:T(8,128)(2,1)S(1)} %fusion.17.value_ref.early), channel_id=1, source_target_pairs={{6,2},{10,6},{14,10},{7,3},{11,7},{15,11},{22,18},{26,22},{30,26},... | collective-permute-start | bytes 2359304 | tf_op jit(solution)/shard_map/ppermute | solution.py:264
  5.4 5.2 %shard_map.95 = f32[192,2048]{1,0:T(8,128)S(1)} custom-call(s32[2]{0:T(128)S(1)} %pad_add_fusion.table, bf16[192,2048]{1,0:T(8,128)(2,1)S(1)} %fusion.17.value_ref.early, bf16[2048,8192]{1,0:T(8,128)(2,1)} %bitcast.41), custom_call_target="tpu_custom_call" | custom-call | flops 6442450944 | bytes 8388608 | tf_op jit(solution)/shard_map/pallas_call | solution.py:72
  10.8 1.4 %add_convert_fusion.5 = bf16[192,2048]{1,0:T(8,128)(2,1)S(1)} fusion(bf16[192,2048]{1,0:T(8,128)(2,1)} %collective-permute-done, f32[192,2048]{1,0:T(8,128)S(1)} %shard_map.95, pred[]{:T(512)S(6)} %eq.20), kind=kLoop, calls=%fused_computation.22 | loop fusion | flops 1572864 | bytes 3145729 | tf_op jit(solution)/shard_map/convert_element_type | solution.py:324
  12.2 5.1 %collective-permute-start.1 = (bf16[192,2048]{1,0:T(8,128)(2,1)S(1)}, bf16[192,2048]{1,0:T(8,128)(2,1)S(1)}, u32[]{:S(2)}, u32[]{:S(2)}) collective-permute-start(bf16[192,2048]{1,0:T(8,128)(2,1)S(1)} %add_convert_fusion.5), channel_id=1, source_target_pairs={{0,4},{6,10},{10,14},{1,5},{7,11},{11,15},{16,20},{22,26},{26,30},... | collective-permute-start | bytes 2359304 | tf_op jit(solution)/shard_map/ppermute | solution.py:264
  17.3 1.3 %add_convert_fusion.4 = bf16[192,2048]{1,0:T(8,128)(2,1)S(1)} fusion(bf16[192,2048]{1,0:T(8,128)(2,1)} %collective-permute-done.2, f32[192,2048]{1,0:T(8,128)S(1)} %shard_map.95, pred[]{:T(512)S(6)} %eq.20), kind=kLoop, calls=%fused_computation.21 | loop fusion | flops 1572864 | bytes 3145729 | tf_op jit(solution)/shard_map/convert_element_type | solution.py:324
  20.7 5.2 %shard_map.96 = f32[192,2048]{1,0:T(8,128)S(1)} custom-call(s32[2]{0:T(128)S(1)} %pad_add_fusion.table, bf16[192,2048]{1,0:T(8,128)(2,1)S(1)} %select_select_fusion.2.value_ref, bf16[2048,8192]{1,0:T(8,128)(2,1)} %bitcast.42), custom_call_target="tpu_custom_call" | custom-call | flops 6442450944 | bytes 8388608 | tf_op jit(solution)/shard_map/pallas_call | solution.py:72
  26.1 1.6 %collective-permute-start.8 = (bf16[192,2048]{1,0:T(8,128)(2,1)S(1)}, bf16[192,2048]{1,0:T(8,128)(2,1)S(1)}, u32[]{:S(2)}, u32[]{:S(2)}) collective-permute-start(bf16[192,2048]{1,0:T(8,128)(2,1)S(1)} %fusion.17.value_ref.early), channel_id=1, source_target_pairs={{0,1},{1,0},{2,3},{3,2},{4,5},{5,4},{6,7},{7,6},{8,9},{9,8},{10,11... | collective-permute-start | bytes 2359304 | tf_op jit(solution)/shard_map/ppermute | solution.py:211
  28.0 3.9 %collective-permute-start.4 = (bf16[192,2048]{1,0:T(8,128)(2,1)S(1)}, bf16[192,2048]{1,0:T(8,128)(2,1)S(1)}, u32[]{:S(2)}, u32[]{:S(2)}) collective-permute-start(bf16[192,2048]{1,0:T(8,128)(2,1)S(1)} %add_convert_fusion.3), channel_id=1, source_target_pairs={{0,4},{4,8},{10,14},{1,5},{5,9},{11,15},{16,20},{20,24},{26,30},{1... | collective-permute-start | bytes 2359304 | tf_op jit(solution)/shard_map/ppermute | solution.py:264
  33.1 4.3 %collective-permute-start.7 = (bf16[208,256]{1,0:T(8,128)(2,1)S(1)}, bf16[208,256]{1,0:T(8,128)(2,1)S(1)}, u32[]{:S(2)}, u32[]{:S(2)}) collective-permute-start(bf16[208,256]{1,0:T(8,128)(2,1)S(1)} %convert_element_type.141), channel_id=1, source_target_pairs={{0,8},{4,12},{8,0},{12,4},{1,9},{5,13},{9,1},{13,5},{2,10},{6,14},... | collective-permute-start | bytes 319496 | tf_op jit(solution)/shard_map/ppermute | solution.py:202
  37.6 5.2 %shard_map.97 = f32[192,2048]{1,0:T(8,128)S(1)} custom-call(s32[2]{0:T(128)S(1)} %pad_add_fusion.table, bf16[192,2048]{1,0:T(8,128)(2,1)S(1)} %select_select_fusion.1.value_ref, bf16[2048,8192]{1,0:T(8,128)(2,1)} %bitcast.43), custom_call_target="tpu_custom_call" | custom-call | flops 6442450944 | bytes 8388608 | tf_op jit(solution)/shard_map/pallas_call | solution.py:72
  43.2 4.3 %collective-permute-start.9 = (bf16[192,2048]{1,0:T(8,128)(2,1)S(1)}, bf16[192,2048]{1,0:T(8,128)(2,1)S(1)}, u32[]{:S(2)}, u32[]{:S(2)}) collective-permute-start(bf16[192,2048]{1,0:T(8,128)(2,1)S(1)} %add_convert_fusion.1), channel_id=1, source_target_pairs={{0,4},{4,8},{8,12},{1,5},{5,9},{9,13},{16,20},{20,24},{24,28},{17,... | collective-permute-start | bytes 2359304 | tf_op jit(solution)/shard_map/ppermute | solution.py:264
  47.8 1.3 %collective-permute-start.10 = (bf16[192,2048]{1,0:T(8,128)(2,1)S(1)}, bf16[192,2048]{1,0:T(8,128)(2,1)S(1)}, u32[]{:S(2)}, u32[]{:S(2)}) collective-permute-start(bf16[192,2048]{1,0:T(8,128)(2,1)S(1)} %add_convert_fusion), channel_id=1, source_target_pairs={{4,0},{8,4},{12,8},{5,1},{9,5},{13,9},{20,16},{24,20},{28,24},{21,... | collective-permute-start | bytes 2359304 | tf_op jit(solution)/shard_map/ppermute | solution.py:264
  49.1 2.7 %collective-permute-done.7 = bf16[208,256]{1,0:T(8,128)(2,1)S(1)} collective-permute-done((bf16[208,256]{1,0:T(8,128)(2,1)S(1)}, bf16[208,256]{1,0:T(8,128)(2,1)S(1)}, u32[]{:S(2)}, u32[]{:S(2)}) %collective-permute-start.7) | collective-permute-done | bytes 106528 | tf_op jit(solution)/shard_map/ppermute | solution.py:202
  52.2 5.3 %shard_map.98 = f32[192,2048]{1,0:T(8,128)S(1)} custom-call(s32[2]{0:T(128)S(1)} %pad_add_fusion.table, bf16[192,2048]{1,0:T(8,128)(2,1)S(1)} %select_select_fusion.value_ref, bf16[2048,8192]{1,0:T(8,128)(2,1)} %bitcast.44), custom_call_target="tpu_custom_call" | custom-call | flops 6442450944 | bytes 8388608 | tf_op jit(solution)/shard_map/pallas_call | solution.py:72
  59.0 1.9 %collective-permute-start.11 = (bf16[192,2048]{1,0:T(8,128)(2,1)S(1)}, bf16[192,2048]{1,0:T(8,128)(2,1)S(1)}, u32[]{:S(2)}, u32[]{:S(2)}) collective-permute-start(bf16[192,2048]{1,0:T(8,128)(2,1)S(1)} %get-tuple-element.92), channel_id=1, source_target_pairs={{0,2},{2,0},{1,3},{3,1},{4,6},{6,4},{5,7},{7,5},{8,10},{10,8},{9,1... | collective-permute-start | bytes 2359304 | tf_op jit(solution)/shard_map/ppermute | solution.py:360
  61.6 1.7 %collective-permute-done.10 = bf16[192,2048]{1,0:T(8,128)(2,1)S(1)} collective-permute-done((bf16[192,2048]{1,0:T(8,128)(2,1)S(1)}, bf16[192,2048]{1,0:T(8,128)(2,1)S(1)}, u32[]{:S(2)}, u32[]{:S(2)}) %collective-permute-start.10) | collective-permute-done | bytes 786464 | tf_op jit(solution)/shard_map/ppermute | solution.py:264
  63.3 0.9 fusion.5
  64.3 0.8 collective-permute-start.16
  65.1 5.0 %collective-permute-start.14 = (f32[2,192]{1,0:T(2,128)S(1)}, f32[2,192]{1,0:T(2,128)S(1)}, u32[]{:S(2)}, u32[]{:S(2)}) collective-permute-start(f32[2,192]{1,0:T(2,128)S(1)} %pad_maximum_fusion.1), channel_id=1, source_target_pairs={{0,12},{4,0},{8,4},{12,8},{1,13},{5,1},{9,5},{13,9},{2,14},{6,2},{... | collective-permute-start | bytes 4616 | tf_op jit(solution)/shard_map/ppermute | solution.py:378
  71.4 4.1 %collective-permute-done.12 = f32[2,192]{1,0:T(2,128)S(1)} collective-permute-done((f32[2,192]{1,0:T(2,128)S(1)}, f32[2,192]{1,0:T(2,128)S(1)}, u32[]{:S(2)}, u32[]{:S(2)}) %collective-permute-start.12) | collective-permute-done | bytes 1568 | tf_op jit(solution)/shard_map/ppermute | solution.py:378
  75.6 1.1 %collective-permute-done.17 = f32[192]{0:T(256)S(1)} collective-permute-done((f32[192]{0:T(256)S(1)}, f32[192]{0:T(256)S(1)}, u32[]{:S(2)}, u32[]{:S(2)}) %collective-permute-start.17) | collective-permute-done | bytes 800 | tf_op jit(solution)/shard_map/ppermute | solution.py:386
  79.0 0.8 collective-permute-start.19
  79.8 3.1 %collective-permute-start.21 = (bf16[192,2048]{1,0:T(8,128)(2,1)S(1)}, bf16[192,2048]{1,0:T(8,128)(2,1)S(1)}, u32[]{:S(2)}, u32[]{:S(2)}) collective-permute-start(bf16[192,2048]{1,0:T(8,128)(2,1)S(1)} %get-tuple-element.72), channel_id=1, source_target_pairs={{0,1},{1,0},{4,5},{5,4},{8,9},{9,8},{12,13},{13,12},{16,17},{17,16... | collective-permute-start | bytes 2359304 | tf_op jit(solution)/shard_map/ppermute | solution.py:211
  83.6 3.1 %collective-permute-start.20 = (bf16[192,256]{1,0:T(8,128)(2,1)S(1)}, bf16[192,256]{1,0:T(8,128)(2,1)S(1)}, u32[]{:S(2)}, u32[]{:S(2)}) collective-permute-start(bf16[192,256]{1,0:T(8,128)(2,1)S(1)} %convert_element_type.162), channel_id=1, source_target_pairs={{0,8},{4,12},{8,0},{12,4},{1,9},{5,13},{9,1},{13,5},{2,10},{6,14},... | collective-permute-start | bytes 294920 | tf_op jit(solution)/shard_map/ppermute | solution.py:202
  86.7 4.3 %collective-permute-done.20 = bf16[192,256]{1,0:T(8,128)(2,1)S(1)} collective-permute-done((bf16[192,256]{1,0:T(8,128)(2,1)S(1)}, bf16[192,256]{1,0:T(8,128)(2,1)S(1)}, u32[]{:S(2)}, u32[]{:S(2)}) %collective-permute-start.20) | collective-permute-done | bytes 98336 | tf_op jit(solution)/shard_map/ppermute | solution.py:202
  91.4 2.3 %collective-permute-done.21 = bf16[192,2048]{1,0:T(8,128)(2,1)S(1)} collective-permute-done((bf16[192,2048]{1,0:T(8,128)(2,1)S(1)}, bf16[192,2048]{1,0:T(8,128)(2,1)S(1)}, u32[]{:S(2)}, u32[]{:S(2)}) %collective-permute-start.21) | collective-permute-done | bytes 786464 | tf_op jit(solution)/shard_map/ppermute | solution.py:211
  93.8 1.3 %collective-permute-start.23 = (bf16[192,384]{1,0:T(8,128)(2,1)S(1)}, bf16[192,384]{1,0:T(8,128)(2,1)S(1)}, u32[]{:S(2)}, u32[]{:S(2)}) collective-permute-start(bf16[192,384]{1,0:T(8,128)(2,1)S(1)} %pad_maximum_fusion), channel_id=1, source_target_pairs={{0,1},{1,0},{2,3},{3,2},{4,5},{5,4},{6,7},{7,6},{8,9},{9,8},{10,11... | collective-permute-start | bytes 442376 | tf_op jit(solution)/shard_map/ppermute | solution.py:211
  95.1 2.3 %shard_map.99 = (f32[2048,256]{1,0:T(8,128)S(1)}, f32[256,2048]{1,0:T(8,128)S(1)}) custom-call(s32[2]{0:T(128)S(1)} %pad_add_fusion.table, bf16[192,2048]{1,0:T(8,128)(2,1)S(1)} %fusion.17.value_ref.early, bf16[192,2048]{1,0:T(8,128)(2,1)S(1)} %fusion.16.late, bf16[192,256]{1,0:T(8,128)(2,1)S(1)} %get-tuple-element.90.small_early, ...), custom_call_target="tpu_custom_call" | custom-call | flops 402653184 | bytes 5767168 | tf_op jit(solution)/shard_map/pallas_call | solution.py:145
  97.5 2.6 %collective-permute-done.23.small_late = bf16[192,384]{1,0:T(8,128)(2,1)S(1)} collective-permute-done((bf16[192,384]{1,0:T(8,128)(2,1)S(1)}, bf16[192,384]{1,0:T(8,128)(2,1)S(1)}, u32[]{:S(2)}, u32[]{:S(2)}) %collective-permute-start.23) | collective-permute-done | bytes 147488 | tf_op jit(solution)/shard_map/ppermute | solution.py:211
  100.1 4.2 %shard_map.100 = (f32[2048,256]{1,0:T(8,128)}, f32[256,2048]{1,0:T(8,128)}) custom-call(s32[2]{0:T(128)S(1)} %pad_add_fusion.table, f32[1,2048]{1,0:T(1,128)S(1)} %copy-done.1, f32[2048,256]{1,0:T(8,128)S(1)} %get-tuple-element.70.down_sum, f32[256,2048]{1,0:T(8,128)S(1)} %get-tuple-element.71.up_sum, bf16[192,2048]{1,0:T(8,128)(2,1)S(1)} %collective-permute-done.8.early, ...), custom_call_target="tpu_custom_call" | custom-call | flops 402653184 | bytes 11534336 | tf_op jit(solution)/shard_map/pallas_call | solution.py:145
  (83 shorter events, 12.3 us)
Async XLA Ops:
  0.6 19.6 %copy-start = (bf16[1,2048,256]{2,1,0:T(8,128)(2,1)S(1)}, bf16[1,2048,256]{2,1,0:T(8,128)(2,1)}, u32[]{:S(2)}) copy-start(bf16[1,2048,256]{2,1,0:T(8,128)(2,1)} %param.12) | copy-start | bytes 3145732
  2.1 8.6 %collective-permute-start = (bf16[192,2048]{1,0:T(8,128)(2,1)S(1)}, bf16[192,2048]{1,0:T(8,128)(2,1)}, u32[]{:S(2)}, u32[]{:S(2)}) collective-permute-start(bf16[192,2048]{1,0:T(8,128)(2,1)S(1)} %fusion.17.value_ref.early), channel_id=1, source_target_pairs={{2,6},{6,10},{10,14},{3,7},{7,11},{11,15},{18,22},{22,26},{26,30},... | collective-permute-start | bytes 2359304 | tf_op jit(solution)/shard_map/ppermute | solution.py:264
  3.8 13.6 %collective-permute-start.2 = (bf16[192,2048]{1,0:T(8,128)(2,1)S(1)}, bf16[192,2048]{1,0:T(8,128)(2,1)}, u32[]{:S(2)}, u32[]{:S(2)}) collective-permute-start(bf16[192,2048]{1,0:T(8,128)(2,1)S(1)} %fusion.17.value_ref.early), channel_id=1, source_target_pairs={{6,2},{10,6},{14,10},{7,3},{11,7},{15,11},{22,18},{26,22},{30,26},... | collective-permute-start | bytes 2359304 | tf_op jit(solution)/shard_map/ppermute | solution.py:264
  5.4 5.2 %copy-start.6 = (f32[4]{0:T(128)S(1)}, f32[4]{0:T(128)}, u32[]{:S(2)}) copy-start(f32[4]{0:T(128)} %param.14) | copy-start | bytes 52
  12.2 7.2 %copy-start.3 = (bf16[192,2048]{1,0:T(8,128)(2,1)S(1)}, bf16[192,2048]{1,0:T(8,128)(2,1)}, u32[]{:S(2)}) copy-start(bf16[192,2048]{1,0:T(8,128)(2,1)} %param.8) | copy-start | bytes 2359300
  12.2 7.5 %copy-start.2 = (bf16[1,256,2048]{2,1,0:T(8,128)(2,1)S(1)}, bf16[1,256,2048]{2,1,0:T(8,128)(2,1)}, u32[]{:S(2)}) copy-start(bf16[1,256,2048]{2,1,0:T(8,128)(2,1)} %param.13) | copy-start | bytes 3145732
  12.2 15.5 %collective-permute-start.1 = (bf16[192,2048]{1,0:T(8,128)(2,1)S(1)}, bf16[192,2048]{1,0:T(8,128)(2,1)S(1)}, u32[]{:S(2)}, u32[]{:S(2)}) collective-permute-start(bf16[192,2048]{1,0:T(8,128)(2,1)S(1)} %add_convert_fusion.5), channel_id=1, source_target_pairs={{0,4},{6,10},{10,14},{1,5},{7,11},{11,15},{16,20},{22,26},{26,30},... | collective-permute-start | bytes 2359304 | tf_op jit(solution)/shard_map/ppermute | solution.py:264
  18.7 13.3 %collective-permute-start.3 = (bf16[192,2048]{1,0:T(8,128)(2,1)S(1)}, bf16[192,2048]{1,0:T(8,128)(2,1)S(1)}, u32[]{:S(2)}, u32[]{:S(2)}) collective-permute-start(bf16[192,2048]{1,0:T(8,128)(2,1)S(1)} %add_convert_fusion.4), channel_id=1, source_target_pairs={{12,8},{6,2},{10,6},{13,9},{7,3},{11,7},{28,24},{22,18},{26,22},{2... | collective-permute-start | bytes 2359304 | tf_op jit(solution)/shard_map/ppermute | solution.py:264
  26.0 7.0 %collective-permute-start.6 = (bf16[208,256]{1,0:T(8,128)(2,1)S(1)}, bf16[208,256]{1,0:T(8,128)(2,1)S(1)}, u32[]{:S(2)}, u32[]{:S(2)}) collective-permute-start(bf16[208,256]{1,0:T(8,128)(2,1)S(1)} %convert_element_type.139), channel_id=1, source_target_pairs={{0,4},{4,0},{8,12},{12,8},{1,5},{5,1},{9,13},{13,9},{2,6},{6,2},{1... | collective-permute-start | bytes 319496 | tf_op jit(solution)/shard_map/ppermute | solution.py:202
  26.1 31.4 %collective-permute-start.8 = (bf16[192,2048]{1,0:T(8,128)(2,1)S(1)}, bf16[192,2048]{1,0:T(8,128)(2,1)S(1)}, u32[]{:S(2)}, u32[]{:S(2)}) collective-permute-start(bf16[192,2048]{1,0:T(8,128)(2,1)S(1)} %fusion.17.value_ref.early), channel_id=1, source_target_pairs={{0,1},{1,0},{2,3},{3,2},{4,5},{5,4},{6,7},{7,6},{8,9},{9,8},{10,11... | collective-permute-start | bytes 2359304 | tf_op jit(solution)/shard_map/ppermute | solution.py:211
  28.0 14.8 %collective-permute-start.4 = (bf16[192,2048]{1,0:T(8,128)(2,1)S(1)}, bf16[192,2048]{1,0:T(8,128)(2,1)S(1)}, u32[]{:S(2)}, u32[]{:S(2)}) collective-permute-start(bf16[192,2048]{1,0:T(8,128)(2,1)S(1)} %add_convert_fusion.3), channel_id=1, source_target_pairs={{0,4},{4,8},{10,14},{1,5},{5,9},{11,15},{16,20},{20,24},{26,30},{1... | collective-permute-start | bytes 2359304 | tf_op jit(solution)/shard_map/ppermute | solution.py:264
  32.3 15.2 %collective-permute-start.5 = (bf16[192,2048]{1,0:T(8,128)(2,1)S(1)}, bf16[192,2048]{1,0:T(8,128)(2,1)S(1)}, u32[]{:S(2)}, u32[]{:S(2)}) collective-permute-start(bf16[192,2048]{1,0:T(8,128)(2,1)S(1)} %add_convert_fusion.2), channel_id=1, source_target_pairs={{8,4},{12,8},{6,2},{9,5},{13,9},{7,3},{24,20},{28,24},{22,18},{25,... | collective-permute-start | bytes 2359304 | tf_op jit(solution)/shard_map/ppermute | solution.py:264
  33.1 18.7 %collective-permute-start.7 = (bf16[208,256]{1,0:T(8,128)(2,1)S(1)}, bf16[208,256]{1,0:T(8,128)(2,1)S(1)}, u32[]{:S(2)}, u32[]{:S(2)}) collective-permute-start(bf16[208,256]{1,0:T(8,128)(2,1)S(1)} %convert_element_type.141), channel_id=1, source_target_pairs={{0,8},{4,12},{8,0},{12,4},{1,9},{5,13},{9,1},{13,5},{2,10},{6,14},... | collective-permute-start | bytes 319496 | tf_op jit(solution)/shard_map/ppermute | solution.py:202
  43.2 18.4 %collective-permute-start.9 = (bf16[192,2048]{1,0:T(8,128)(2,1)S(1)}, bf16[192,2048]{1,0:T(8,128)(2,1)S(1)}, u32[]{:S(2)}, u32[]{:S(2)}) collective-permute-start(bf16[192,2048]{1,0:T(8,128)(2,1)S(1)} %add_convert_fusion.1), channel_id=1, source_target_pairs={{0,4},{4,8},{8,12},{1,5},{5,9},{9,13},{16,20},{20,24},{24,28},{17,... | collective-permute-start | bytes 2359304 | tf_op jit(solution)/shard_map/ppermute | solution.py:264
  47.8 15.5 %collective-permute-start.10 = (bf16[192,2048]{1,0:T(8,128)(2,1)S(1)}, bf16[192,2048]{1,0:T(8,128)(2,1)S(1)}, u32[]{:S(2)}, u32[]{:S(2)}) collective-permute-start(bf16[192,2048]{1,0:T(8,128)(2,1)S(1)} %add_convert_fusion), channel_id=1, source_target_pairs={{4,0},{8,4},{12,8},{5,1},{9,5},{13,9},{20,16},{24,20},{28,24},{21,... | collective-permute-start | bytes 2359304 | tf_op jit(solution)/shard_map/ppermute | solution.py:264
  52.2 5.3 %copy-start.5 = (s32[192]{0:T(256)S(1)}, s32[192]{0:T(256)}, u32[]{:S(2)}) copy-start(s32[192]{0:T(256)} %param.15) | copy-start | bytes 2308
  57.5 0.7 copy-start.1
  59.0 4.3 %collective-permute-start.11 = (bf16[192,2048]{1,0:T(8,128)(2,1)S(1)}, bf16[192,2048]{1,0:T(8,128)(2,1)S(1)}, u32[]{:S(2)}, u32[]{:S(2)}) collective-permute-start(bf16[192,2048]{1,0:T(8,128)(2,1)S(1)} %get-tuple-element.92), channel_id=1, source_target_pairs={{0,2},{2,0},{1,3},{3,1},{4,6},{6,4},{5,7},{7,5},{8,10},{10,8},{9,1... | collective-permute-start | bytes 2359304 | tf_op jit(solution)/shard_map/ppermute | solution.py:360
  60.9 14.6 %collective-permute-start.15 = (bf16[192,2048]{1,0:T(8,128)(2,1)S(1)}, bf16[192,2048]{1,0:T(8,128)(2,1)S(1)}, u32[]{:S(2)}, u32[]{:S(2)}) collective-permute-start(bf16[192,2048]{1,0:T(8,128)(2,1)S(1)} %get-tuple-element.92), channel_id=1, source_target_pairs={{2,3},{3,2},{6,7},{7,6},{10,11},{11,10},{14,15},{15,14},{18,19},{1... | collective-permute-start | bytes 2359304 | tf_op jit(solution)/shard_map/ppermute | solution.py:211
  64.2 12.6 %copy-start.4 = (bf16[192,2048]{1,0:T(8,128)(2,1)S(1)}, bf16[192,2048]{1,0:T(8,128)(2,1)}, u32[]{:S(2)}) copy-start(bf16[192,2048]{1,0:T(8,128)(2,1)} %param.9) | copy-start | bytes 2359300
  64.3 12.5 %collective-permute-start.16 = (bf16[192,2048]{1,0:T(8,128)(2,1)S(1)}, bf16[192,2048]{1,0:T(8,128)(2,1)S(1)}, u32[]{:S(2)}, u32[]{:S(2)}) collective-permute-start(bf16[192,2048]{1,0:T(8,128)(2,1)S(1)} %broadcast_select_fusion.2), channel_id=1, source_target_pairs={{0,2},{2,0},{1,3},{3,1},{4,6},{6,4},{5,7},{7,5},{8,10},{10,8},{9,1... | collective-permute-start | bytes 2359304 | tf_op jit(solution)/shard_map/ppermute | solution.py:367
  65.1 6.3 %collective-permute-start.14 = (f32[2,192]{1,0:T(2,128)S(1)}, f32[2,192]{1,0:T(2,128)S(1)}, u32[]{:S(2)}, u32[]{:S(2)}) collective-permute-start(f32[2,192]{1,0:T(2,128)S(1)} %pad_maximum_fusion.1), channel_id=1, source_target_pairs={{0,12},{4,0},{8,4},{12,8},{1,13},{5,1},{9,5},{13,9},{2,14},{6,2},{... | collective-permute-start | bytes 4616 | tf_op jit(solution)/shard_map/ppermute | solution.py:378
  70.1 5.4 %collective-permute-start.12 = (f32[2,192]{1,0:T(2,128)S(1)}, f32[2,192]{1,0:T(2,128)S(1)}, u32[]{:S(2)}, u32[]{:S(2)}) collective-permute-start(f32[2,192]{1,0:T(2,128)S(1)} %pad_maximum_fusion.1), channel_id=1, source_target_pairs={{0,4},{4,8},{8,12},{12,0},{1,5},{5,9},{9,13},{13,1},{2,6},{6,10},{... | collective-permute-start | bytes 4616 | tf_op jit(solution)/shard_map/ppermute | solution.py:378
  70.1 5.4 %collective-permute-start.13 = (f32[2,192]{1,0:T(2,128)S(1)}, f32[2,192]{1,0:T(2,128)S(1)}, u32[]{:S(2)}, u32[]{:S(2)}) collective-permute-start(f32[2,192]{1,0:T(2,128)S(1)} %pad_maximum_fusion.1), channel_id=1, source_target_pairs={{0,8},{4,12},{8,0},{12,4},{1,9},{5,13},{9,1},{13,5},{2,10},{6,14},... | collective-permute-start | bytes 4616 | tf_op jit(solution)/shard_map/ppermute | solution.py:378
  75.6 1.2 %collective-permute-start.17 = (f32[192]{0:T(256)S(1)}, f32[192]{0:T(256)S(1)}, u32[]{:S(2)}, u32[]{:S(2)}) collective-permute-start(f32[192]{0:T(256)S(1)} %bitcast.47), channel_id=1, source_target_pairs={{0,2},{2,0},{1,3},{3,1},{4,6},{6,4},{5,7},{7,5},{8,10},{10,8},{9,1... | collective-permute-start | bytes 2312 | tf_op jit(solution)/shard_map/ppermute | solution.py:386
  78.3 5.0 %collective-permute-start.18 = (bf16[192,256]{1,0:T(8,128)(2,1)S(1)}, bf16[192,256]{1,0:T(8,128)(2,1)S(1)}, u32[]{:S(2)}, u32[]{:S(2)}) collective-permute-start(bf16[192,256]{1,0:T(8,128)(2,1)S(1)} %get-tuple-element.94), channel_id=1, source_target_pairs={{0,4},{4,0},{8,12},{12,8},{1,5},{5,1},{9,13},{13,9},{2,6},{6,2},{1... | collective-permute-start | bytes 294920 | tf_op jit(solution)/shard_map/ppermute | solution.py:202
  79.0 4.6 %collective-permute-start.19 = (bf16[192,256]{1,0:T(8,128)(2,1)S(1)}, bf16[192,256]{1,0:T(8,128)(2,1)S(1)}, u32[]{:S(2)}, u32[]{:S(2)}) collective-permute-start(bf16[192,256]{1,0:T(8,128)(2,1)S(1)} %get-tuple-element.82), channel_id=1, source_target_pairs={{0,1},{1,0},{2,3},{3,2},{4,5},{5,4},{6,7},{7,6},{8,9},{9,8},{10,11... | collective-permute-start | bytes 294920 | tf_op jit(solution)/shard_map/ppermute | solution.py:211
  79.8 13.9 %collective-permute-start.21 = (bf16[192,2048]{1,0:T(8,128)(2,1)S(1)}, bf16[192,2048]{1,0:T(8,128)(2,1)S(1)}, u32[]{:S(2)}, u32[]{:S(2)}) collective-permute-start(bf16[192,2048]{1,0:T(8,128)(2,1)S(1)} %get-tuple-element.72), channel_id=1, source_target_pairs={{0,1},{1,0},{4,5},{5,4},{8,9},{9,8},{12,13},{13,12},{16,17},{17,16... | collective-permute-start | bytes 2359304 | tf_op jit(solution)/shard_map/ppermute | solution.py:211
  83.6 7.4 %collective-permute-start.20 = (bf16[192,256]{1,0:T(8,128)(2,1)S(1)}, bf16[192,256]{1,0:T(8,128)(2,1)S(1)}, u32[]{:S(2)}, u32[]{:S(2)}) collective-permute-start(bf16[192,256]{1,0:T(8,128)(2,1)S(1)} %convert_element_type.162), channel_id=1, source_target_pairs={{0,8},{4,12},{8,0},{12,4},{1,9},{5,13},{9,1},{13,5},{2,10},{6,14},... | collective-permute-start | bytes 294920 | tf_op jit(solution)/shard_map/ppermute | solution.py:202
  93.7 3.6 %collective-permute-start.22 = (bf16[192,2048]{1,0:T(8,128)(2,1)S(1)}, bf16[192,2048]{1,0:T(8,128)(2,1)S(1)}, u32[]{:S(2)}, u32[]{:S(2)}) collective-permute-start(bf16[192,2048]{1,0:T(8,128)(2,1)S(1)} %broadcast_select_fusion.1), channel_id=1, source_target_pairs={{0,2},{2,0},{1,3},{3,1},{4,6},{6,4},{5,7},{7,5},{8,10},{10,8},{9,1... | collective-permute-start | bytes 2359304 | tf_op jit(solution)/shard_map/ppermute | solution.py:417
  93.8 6.3 %collective-permute-start.23 = (bf16[192,384]{1,0:T(8,128)(2,1)S(1)}, bf16[192,384]{1,0:T(8,128)(2,1)S(1)}, u32[]{:S(2)}, u32[]{:S(2)}) collective-permute-start(bf16[192,384]{1,0:T(8,128)(2,1)S(1)} %pad_maximum_fusion), channel_id=1, source_target_pairs={{0,1},{1,0},{2,3},{3,2},{4,5},{5,4},{6,7},{7,6},{8,9},{9,8},{10,11... | collective-permute-start | bytes 442376 | tf_op jit(solution)/shard_map/ppermute | solution.py:211

commit v14 on v13

--- a/solution.py
+++ b/solution.py
@@ -299,10 +299,10 @@
         )
         order = [blocks[stage] for blocks in first_order + second_order]
         part = block_product(table, value, weight, order)
-        if stage == 1:
+        if stage == 0:
             part, after = lax.optimization_barrier((part, early))
             early_all = [early] + with_other_replicas(after)[1:]
-        if stage == count - 1:
+        if stage == min(2, count - 1):
             part, *early_all = lax.optimization_barrier((part, *early_all))
         parts.append(part)
         slot = stage + 1

time: 105 us -> 107 us (1.019)
  Pallas kernels: 27.4 us -> 28.5 us
    ppermute x8, waiting for transfers between devices: 1.7 us -> 4.68 us  [line(): return lax.ppermute(value, ('tensor', 'section'), pairs)]
    ppermute x4, waiting for transfers between devices: 7.37 us -> 5.04 us  [sum_step(): other = lax.ppermute(value.astype(wire), 'tensor', pairs)]
    ppermute x5, starting transfers between devices: 7.45 us -> 9.11 us  [with_other_replicas(): lax.ppermute(value, ('section', 'replica'), [(s * count + r, s * count +...]
    ppermute x4, starting transfers between devices: 8.08 us -> 6.85 us  [sum_step(): other = lax.ppermute(value.astype(wire), 'tensor', pairs)]
    pallas_call x2, Pallas kernels: 6.46 us -> 7.6 us  [gradient_call(): pl.pallas_call(kernel, grid_spec=pltpu.PrefetchScalarGridSpec(num_scalar_...]
  transfers between devices with their start and end apart: 24 -> 24, of which waited for: 10 -> 12; matrix products, arithmetic and copies ran while one was open for 9% -> 8% of each run, Pallas kernels for 22% -> 22%
where the time goes in v14:
time: 107 us; the launch traced here: 106 us
  starting transfers between devices  43.7 us (41%)
  Pallas kernels  28.5 us (27%)
  waiting for transfers between devices  20.7 us (19%)
  other arithmetic  8.8 us (8%)
  matrix products  2.95 us (3%)
  between operations  1.17 us (1%)
    pallas_call x4, Pallas kernels, block_product(): pl.pallas_call(functools.partial(block_kernel, blocks=blocks, tile=tile,...  20.9 us
    ppermute x8, starting transfers between devices, line(): return lax.ppermute(value, ('tensor', 'section'), pairs)  18.4 us
    ppermute x5, starting transfers between devices, with_other_replicas(): lax.ppermute(value, ('section', 'replica'), [(s * count + r, s * count +...  9.11 us
    pallas_call x2, Pallas kernels, gradient_call(): pl.pallas_call(kernel, grid_spec=pltpu.PrefetchScalarGridSpec(num_scalar_...  7.6 us
    ppermute x4, starting transfers between devices, sum_step(): other = lax.ppermute(value.astype(wire), 'tensor', pairs)  6.85 us
    ppermute x3, starting transfers between devices, on_device(): lax.ppermute(row_sums, 'tensor', [(z, (z + step) % count) for z in everyo...  5.8 us
    ppermute x5, waiting for transfers between devices, with_other_replicas(): lax.ppermute(value, ('section', 'replica'), [(s * count + r, s * count +...  5.25 us
    ppermute x4, waiting for transfers between devices, sum_step(): other = lax.ppermute(value.astype(wire), 'tensor', pairs)  5.04 us
  transfers between devices with their start and end apart: 24, of which 12 were waited for; matrix products, arithmetic and copies ran while one was open for 8% of the time, Pallas kernels for 22%

profile of v14, /device:TPU:0, one launch (start us, length us, event | category | flops | bytes accessed | tf_op | source)
XLA Modules:
  0.0 106.3 jit_solution(10813647521661953569)
XLA Ops:
  0.7 1.5 %fusion.17.value_ref.early = bf16[192,2048]{1,0:T(8,128)(2,1)S(1)} fusion(bf16[192,2048]{1,0:T(8,128)(2,1)} %param.9, bf16[192,2048]{1,0:T(8,128)(2,1)} %param.8, f32[2048]{0:T(1024)} %bitcast.38, pred[]{:T(512)S(6)} %eq.20), kind=kLoop, calls=%fused_computation.35 | loop fusion | flops 1572864 | bytes 2367489 | tf_op jit(solution)/shard_map/jit(_where)/select_n | solution.py:267
  2.1 1.6 %collective-permute-start = (bf16[192,2048]{1,0:T(8,128)(2,1)S(1)}, bf16[192,2048]{1,0:T(8,128)(2,1)}, u32[]{:S(2)}, u32[]{:S(2)}) collective-permute-start(bf16[192,2048]{1,0:T(8,128)(2,1)S(1)} %fusion.17.value_ref.early), channel_id=1, source_target_pairs={{2,6},{6,10},{10,14},{3,7},{7,11},{11,15},{18,22},{22,26},{26,30},... | collective-permute-start | bytes 2359304 | tf_op jit(solution)/shard_map/ppermute | solution.py:264
  3.8 1.6 %collective-permute-start.2 = (bf16[192,2048]{1,0:T(8,128)(2,1)S(1)}, bf16[192,2048]{1,0:T(8,128)(2,1)}, u32[]{:S(2)}, u32[]{:S(2)}) collective-permute-start(bf16[192,2048]{1,0:T(8,128)(2,1)S(1)} %fusion.17.value_ref.early), channel_id=1, source_target_pairs={{6,2},{10,6},{14,10},{7,3},{11,7},{15,11},{22,18},{26,22},{30,26},... | collective-permute-start | bytes 2359304 | tf_op jit(solution)/shard_map/ppermute | solution.py:264
  5.4 5.2 %shard_map.95 = f32[192,2048]{1,0:T(8,128)S(1)} custom-call(s32[2]{0:T(128)S(1)} %pad_add_fusion.table, bf16[192,2048]{1,0:T(8,128)(2,1)S(1)} %fusion.17.value_ref.early, bf16[2048,8192]{1,0:T(8,128)(2,1)} %bitcast.41), custom_call_target="tpu_custom_call" | custom-call | flops 6442450944 | bytes 8388608 | tf_op jit(solution)/shard_map/pallas_call | solution.py:72
  10.6 3.0 %collective-permute-start.8 = (bf16[192,2048]{1,0:T(8,128)(2,1)S(1)}, bf16[192,2048]{1,0:T(8,128)(2,1)}, u32[]{:S(2)}, u32[]{:S(2)}) collective-permute-start(bf16[192,2048]{1,0:T(8,128)(2,1)S(1)} %fusion.17.value_ref.early), channel_id=1, source_target_pairs={{0,1},{1,0},{2,3},{3,2},{4,5},{5,4},{6,7},{7,6},{8,9},{9,8},{10,11... | collective-permute-start | bytes 2359304 | tf_op jit(solution)/shard_map/ppermute | solution.py:211
  13.8 1.3 %add_convert_fusion.5 = bf16[192,2048]{1,0:T(8,128)(2,1)S(1)} fusion(bf16[192,2048]{1,0:T(8,128)(2,1)} %collective-permute-done, f32[192,2048]{1,0:T(8,128)S(1)} %shard_map.95, pred[]{:T(512)S(6)} %eq.20), kind=kLoop, calls=%fused_computation.22 | loop fusion | flops 1572864 | bytes 3145729 | tf_op jit(solution)/shard_map/convert_element_type | solution.py:324
  15.1 3.7 %collective-permute-start.1 = (bf16[192,2048]{1,0:T(8,128)(2,1)S(1)}, bf16[192,2048]{1,0:T(8,128)(2,1)S(1)}, u32[]{:S(2)}, u32[]{:S(2)}) collective-permute-start(bf16[192,2048]{1,0:T(8,128)(2,1)S(1)} %add_convert_fusion.5), channel_id=1, source_target_pairs={{0,4},{6,10},{10,14},{1,5},{7,11},{11,15},{16,20},{22,26},{26,30},... | collective-permute-start | bytes 2359304 | tf_op jit(solution)/shard_map/ppermute | solution.py:264
  18.8 1.4 %add_convert_fusion.4 = bf16[192,2048]{1,0:T(8,128)(2,1)S(1)} fusion(bf16[192,2048]{1,0:T(8,128)(2,1)} %collective-permute-done.2, f32[192,2048]{1,0:T(8,128)S(1)} %shard_map.95, pred[]{:T(512)S(6)} %eq.20), kind=kLoop, calls=%fused_computation.21 | loop fusion | flops 1572864 | bytes 3145729 | tf_op jit(solution)/shard_map/convert_element_type | solution.py:324
  22.3 5.2 %shard_map.96 = f32[192,2048]{1,0:T(8,128)S(1)} custom-call(s32[2]{0:T(128)S(1)} %pad_add_fusion.table, bf16[192,2048]{1,0:T(8,128)(2,1)S(1)} %select_select_fusion.2.value_ref, bf16[2048,8192]{1,0:T(8,128)(2,1)} %bitcast.42), custom_call_target="tpu_custom_call" | custom-call | flops 6442450944 | bytes 8388608 | tf_op jit(solution)/shard_map/pallas_call | solution.py:72
  28.6 4.4 %collective-permute-start.4 = (bf16[192,2048]{1,0:T(8,128)(2,1)S(1)}, bf16[192,2048]{1,0:T(8,128)(2,1)S(1)}, u32[]{:S(2)}, u32[]{:S(2)}) collective-permute-start(bf16[192,2048]{1,0:T(8,128)(2,1)S(1)} %add_convert_fusion.3), channel_id=1, source_target_pairs={{0,4},{4,8},{10,14},{1,5},{5,9},{11,15},{16,20},{20,24},{26,30},{1... | collective-permute-start | bytes 2359304 | tf_op jit(solution)/shard_map/ppermute | solution.py:264
  34.2 3.2 %collective-permute-start.7 = (bf16[208,256]{1,0:T(8,128)(2,1)S(1)}, bf16[208,256]{1,0:T(8,128)(2,1)S(1)}, u32[]{:S(2)}, u32[]{:S(2)}) collective-permute-start(bf16[208,256]{1,0:T(8,128)(2,1)S(1)} %convert_element_type.141), channel_id=1, source_target_pairs={{0,8},{4,12},{8,0},{12,4},{1,9},{5,13},{9,1},{13,5},{2,10},{6,14},... | collective-permute-start | bytes 319496 | tf_op jit(solution)/shard_map/ppermute | solution.py:202
  37.7 5.2 %shard_map.97 = f32[192,2048]{1,0:T(8,128)S(1)} custom-call(s32[2]{0:T(128)S(1)} %pad_add_fusion.table, bf16[192,2048]{1,0:T(8,128)(2,1)S(1)} %select_select_fusion.1.value_ref, bf16[2048,8192]{1,0:T(8,128)(2,1)} %bitcast.43), custom_call_target="tpu_custom_call" | custom-call | flops 6442450944 | bytes 8388608 | tf_op jit(solution)/shard_map/pallas_call | solution.py:72
  42.9 1.9 %collective-permute-done.4 = bf16[192,2048]{1,0:T(8,128)(2,1)S(1)} collective-permute-done((bf16[192,2048]{1,0:T(8,128)(2,1)S(1)}, bf16[192,2048]{1,0:T(8,128)(2,1)S(1)}, u32[]{:S(2)}, u32[]{:S(2)}) %collective-permute-start.4) | collective-permute-done | bytes 786464 | tf_op jit(solution)/shard_map/ppermute | solution.py:264
  45.1 4.4 %collective-permute-start.9 = (bf16[192,2048]{1,0:T(8,128)(2,1)S(1)}, bf16[192,2048]{1,0:T(8,128)(2,1)S(1)}, u32[]{:S(2)}, u32[]{:S(2)}) collective-permute-start(bf16[192,2048]{1,0:T(8,128)(2,1)S(1)} %add_convert_fusion.1), channel_id=1, source_target_pairs={{0,4},{4,8},{8,12},{1,5},{5,9},{9,13},{16,20},{20,24},{24,28},{17,... | collective-permute-start | bytes 2359304 | tf_op jit(solution)/shard_map/ppermute | solution.py:264
  49.8 1.3 %collective-permute-start.10 = (bf16[192,2048]{1,0:T(8,128)(2,1)S(1)}, bf16[192,2048]{1,0:T(8,128)(2,1)S(1)}, u32[]{:S(2)}, u32[]{:S(2)}) collective-permute-start(bf16[192,2048]{1,0:T(8,128)(2,1)S(1)} %add_convert_fusion), channel_id=1, source_target_pairs={{4,0},{8,4},{12,8},{5,1},{9,5},{13,9},{20,16},{24,20},{28,24},{21,... | collective-permute-start | bytes 2359304 | tf_op jit(solution)/shard_map/ppermute | solution.py:264
  52.2 5.2 %shard_map.98 = f32[192,2048]{1,0:T(8,128)S(1)} custom-call(s32[2]{0:T(128)S(1)} %pad_add_fusion.table, bf16[192,2048]{1,0:T(8,128)(2,1)S(1)} %select_select_fusion.value_ref, bf16[2048,8192]{1,0:T(8,128)(2,1)} %bitcast.44), custom_call_target="tpu_custom_call" | custom-call | flops 6442450944 | bytes 8388608 | tf_op jit(solution)/shard_map/pallas_call | solution.py:72
  59.0 1.8 %collective-permute-start.11 = (bf16[192,2048]{1,0:T(8,128)(2,1)S(1)}, bf16[192,2048]{1,0:T(8,128)(2,1)S(1)}, u32[]{:S(2)}, u32[]{:S(2)}) collective-permute-start(bf16[192,2048]{1,0:T(8,128)(2,1)S(1)} %get-tuple-element.92), channel_id=1, source_target_pairs={{0,2},{2,0},{1,3},{3,1},{4,6},{6,4},{5,7},{7,5},{8,10},{10,8},{9,1... | collective-permute-start | bytes 2359304 | tf_op jit(solution)/shard_map/ppermute | solution.py:360
  61.5 2.2 %collective-permute-done.10 = bf16[192,2048]{1,0:T(8,128)(2,1)S(1)} collective-permute-done((bf16[192,2048]{1,0:T(8,128)(2,1)S(1)}, bf16[192,2048]{1,0:T(8,128)(2,1)S(1)}, u32[]{:S(2)}, u32[]{:S(2)}) %collective-permute-start.10) | collective-permute-done | bytes 786464 | tf_op jit(solution)/shard_map/ppermute | solution.py:264
  63.7 0.9 fusion.5
  64.7 1.5 %collective-permute-start.16 = (bf16[192,2048]{1,0:T(8,128)(2,1)S(1)}, bf16[192,2048]{1,0:T(8,128)(2,1)S(1)}, u32[]{:S(2)}, u32[]{:S(2)}) collective-permute-start(bf16[192,2048]{1,0:T(8,128)(2,1)S(1)} %broadcast_select_fusion.2), channel_id=1, source_target_pairs={{0,2},{2,0},{1,3},{3,1},{4,6},{6,4},{5,7},{7,5},{8,10},{10,8},{9,1... | collective-permute-start | bytes 2359304 | tf_op jit(solution)/shard_map/ppermute | solution.py:367
  66.2 5.0 %collective-permute-start.14 = (f32[2,192]{1,0:T(2,128)S(1)}, f32[2,192]{1,0:T(2,128)S(1)}, u32[]{:S(2)}, u32[]{:S(2)}) collective-permute-start(f32[2,192]{1,0:T(2,128)S(1)} %pad_maximum_fusion.1), channel_id=1, source_target_pairs={{0,12},{4,0},{8,4},{12,8},{1,13},{5,1},{9,5},{13,9},{2,14},{6,2},{... | collective-permute-start | bytes 4616 | tf_op jit(solution)/shard_map/ppermute | solution.py:378
  71.2 0.8 collective-permute-start.13
  72.5 4.1 %collective-permute-done.12 = f32[2,192]{1,0:T(2,128)S(1)} collective-permute-done((f32[2,192]{1,0:T(2,128)S(1)}, f32[2,192]{1,0:T(2,128)S(1)}, u32[]{:S(2)}, u32[]{:S(2)}) %collective-permute-start.12) | collective-permute-done | bytes 1568 | tf_op jit(solution)/shard_map/ppermute | solution.py:378
  76.7 1.1 %collective-permute-done.17 = f32[192]{0:T(256)S(1)} collective-permute-done((f32[192]{0:T(256)S(1)}, f32[192]{0:T(256)S(1)}, u32[]{:S(2)}, u32[]{:S(2)}) %collective-permute-start.17) | collective-permute-done | bytes 800 | tf_op jit(solution)/shard_map/ppermute | solution.py:386
  80.7 3.3 %collective-permute-start.21 = (bf16[192,2048]{1,0:T(8,128)(2,1)S(1)}, bf16[192,2048]{1,0:T(8,128)(2,1)S(1)}, u32[]{:S(2)}, u32[]{:S(2)}) collective-permute-start(bf16[192,2048]{1,0:T(8,128)(2,1)S(1)} %get-tuple-element.72), channel_id=1, source_target_pairs={{0,1},{1,0},{4,5},{5,4},{8,9},{9,8},{12,13},{13,12},{16,17},{17,16... | collective-permute-start | bytes 2359304 | tf_op jit(solution)/shard_map/ppermute | solution.py:211
  84.7 3.0 %collective-permute-start.20 = (bf16[192,256]{1,0:T(8,128)(2,1)S(1)}, bf16[192,256]{1,0:T(8,128)(2,1)S(1)}, u32[]{:S(2)}, u32[]{:S(2)}) collective-permute-start(bf16[192,256]{1,0:T(8,128)(2,1)S(1)} %convert_element_type.162), channel_id=1, source_target_pairs={{0,8},{4,12},{8,0},{12,4},{1,9},{5,13},{9,1},{13,5},{2,10},{6,14},... | collective-permute-start | bytes 294920 | tf_op jit(solution)/shard_map/ppermute | solution.py:202
  87.7 3.9 %collective-permute-done.20 = bf16[192,256]{1,0:T(8,128)(2,1)S(1)} collective-permute-done((bf16[192,256]{1,0:T(8,128)(2,1)S(1)}, bf16[192,256]{1,0:T(8,128)(2,1)S(1)}, u32[]{:S(2)}, u32[]{:S(2)}) %collective-permute-start.20) | collective-permute-done | bytes 98336 | tf_op jit(solution)/shard_map/ppermute | solution.py:202
  92.0 2.6 %collective-permute-done.21 = bf16[192,2048]{1,0:T(8,128)(2,1)S(1)} collective-permute-done((bf16[192,2048]{1,0:T(8,128)(2,1)S(1)}, bf16[192,2048]{1,0:T(8,128)(2,1)S(1)}, u32[]{:S(2)}, u32[]{:S(2)}) %collective-permute-start.21) | collective-permute-done | bytes 786464 | tf_op jit(solution)/shard_map/ppermute | solution.py:211
  94.7 1.5 %collective-permute-start.23 = (bf16[192,384]{1,0:T(8,128)(2,1)S(1)}, bf16[192,384]{1,0:T(8,128)(2,1)S(1)}, u32[]{:S(2)}, u32[]{:S(2)}) collective-permute-start(bf16[192,384]{1,0:T(8,128)(2,1)S(1)} %pad_maximum_fusion), channel_id=1, source_target_pairs={{0,1},{1,0},{2,3},{3,2},{4,5},{5,4},{6,7},{7,6},{8,9},{9,8},{10,11... | collective-permute-start | bytes 442376 | tf_op jit(solution)/shard_map/ppermute | solution.py:211
  96.2 2.3 %shard_map.99 = (f32[2048,256]{1,0:T(8,128)S(1)}, f32[256,2048]{1,0:T(8,128)S(1)}) custom-call(s32[2]{0:T(128)S(1)} %pad_add_fusion.table, bf16[192,2048]{1,0:T(8,128)(2,1)S(1)} %fusion.17.value_ref.early, bf16[192,2048]{1,0:T(8,128)(2,1)S(1)} %fusion.16.late, bf16[192,256]{1,0:T(8,128)(2,1)S(1)} %get-tuple-element.90.small_early, ...), custom_call_target="tpu_custom_call" | custom-call | flops 402653184 | bytes 5767168 | tf_op jit(solution)/shard_map/pallas_call | solution.py:145
  98.6 2.4 %collective-permute-done.23.small_late = bf16[192,384]{1,0:T(8,128)(2,1)S(1)} collective-permute-done((bf16[192,384]{1,0:T(8,128)(2,1)S(1)}, bf16[192,384]{1,0:T(8,128)(2,1)S(1)}, u32[]{:S(2)}, u32[]{:S(2)}) %collective-permute-start.23) | collective-permute-done | bytes 147488 | tf_op jit(solution)/shard_map/ppermute | solution.py:211
  101.0 5.3 %shard_map.100 = (f32[2048,256]{1,0:T(8,128)}, f32[256,2048]{1,0:T(8,128)}) custom-call(s32[2]{0:T(128)S(1)} %pad_add_fusion.table, f32[1,2048]{1,0:T(1,128)S(1)} %copy-done.1, f32[2048,256]{1,0:T(8,128)S(1)} %get-tuple-element.70.down_sum, f32[256,2048]{1,0:T(8,128)S(1)} %get-tuple-element.71.up_sum, bf16[192,2048]{1,0:T(8,128)(2,1)} %collective-permute-done.8.early, ...), custom_call_target="tpu_custom_call" | custom-call | flops 402653184 | bytes 11534336 | tf_op jit(solution)/shard_map/pallas_call | solution.py:145
  (83 shorter events, 13.3 us)
Async XLA Ops:
  0.6 21.1 %copy-start = (bf16[1,2048,256]{2,1,0:T(8,128)(2,1)S(1)}, bf16[1,2048,256]{2,1,0:T(8,128)(2,1)}, u32[]{:S(2)}) copy-start(bf16[1,2048,256]{2,1,0:T(8,128)(2,1)} %param.12) | copy-start | bytes 3145732
  2.1 11.6 %collective-permute-start = (bf16[192,2048]{1,0:T(8,128)(2,1)S(1)}, bf16[192,2048]{1,0:T(8,128)(2,1)}, u32[]{:S(2)}, u32[]{:S(2)}) collective-permute-start(bf16[192,2048]{1,0:T(8,128)(2,1)S(1)} %fusion.17.value_ref.early), channel_id=1, source_target_pairs={{2,6},{6,10},{10,14},{3,7},{7,11},{11,15},{18,22},{22,26},{26,30},... | collective-permute-start | bytes 2359304 | tf_op jit(solution)/shard_map/ppermute | solution.py:264
  3.8 15.1 %collective-permute-start.2 = (bf16[192,2048]{1,0:T(8,128)(2,1)S(1)}, bf16[192,2048]{1,0:T(8,128)(2,1)}, u32[]{:S(2)}, u32[]{:S(2)}) collective-permute-start(bf16[192,2048]{1,0:T(8,128)(2,1)S(1)} %fusion.17.value_ref.early), channel_id=1, source_target_pairs={{6,2},{10,6},{14,10},{7,3},{11,7},{15,11},{22,18},{26,22},{30,26},... | collective-permute-start | bytes 2359304 | tf_op jit(solution)/shard_map/ppermute | solution.py:264
  5.4 8.2 %copy-start.6 = (f32[4]{0:T(128)S(1)}, f32[4]{0:T(128)}, u32[]{:S(2)}) copy-start(f32[4]{0:T(128)} %param.14) | copy-start | bytes 52
  10.6 32.3 %collective-permute-start.8 = (bf16[192,2048]{1,0:T(8,128)(2,1)S(1)}, bf16[192,2048]{1,0:T(8,128)(2,1)}, u32[]{:S(2)}, u32[]{:S(2)}) collective-permute-start(bf16[192,2048]{1,0:T(8,128)(2,1)S(1)} %fusion.17.value_ref.early), channel_id=1, source_target_pairs={{0,1},{1,0},{2,3},{3,2},{4,5},{5,4},{6,7},{7,6},{8,9},{9,8},{10,11... | collective-permute-start | bytes 2359304 | tf_op jit(solution)/shard_map/ppermute | solution.py:211
  15.1 5.8 %copy-start.3 = (bf16[192,2048]{1,0:T(8,128)(2,1)S(1)}, bf16[192,2048]{1,0:T(8,128)(2,1)}, u32[]{:S(2)}) copy-start(bf16[192,2048]{1,0:T(8,128)(2,1)} %param.8) | copy-start | bytes 2359300
  15.1 6.1 %copy-start.2 = (bf16[1,256,2048]{2,1,0:T(8,128)(2,1)S(1)}, bf16[1,256,2048]{2,1,0:T(8,128)(2,1)}, u32[]{:S(2)}) copy-start(bf16[1,256,2048]{2,1,0:T(8,128)(2,1)} %param.13) | copy-start | bytes 3145732
  15.1 13.1 %collective-permute-start.1 = (bf16[192,2048]{1,0:T(8,128)(2,1)S(1)}, bf16[192,2048]{1,0:T(8,128)(2,1)S(1)}, u32[]{:S(2)}, u32[]{:S(2)}) collective-permute-start(bf16[192,2048]{1,0:T(8,128)(2,1)S(1)} %add_convert_fusion.5), channel_id=1, source_target_pairs={{0,4},{6,10},{10,14},{1,5},{7,11},{11,15},{16,20},{22,26},{26,30},... | collective-permute-start | bytes 2359304 | tf_op jit(solution)/shard_map/ppermute | solution.py:264
  20.2 12.9 %collective-permute-start.3 = (bf16[192,2048]{1,0:T(8,128)(2,1)S(1)}, bf16[192,2048]{1,0:T(8,128)(2,1)S(1)}, u32[]{:S(2)}, u32[]{:S(2)}) collective-permute-start(bf16[192,2048]{1,0:T(8,128)(2,1)S(1)} %add_convert_fusion.4), channel_id=1, source_target_pairs={{12,8},{6,2},{10,6},{13,9},{7,3},{11,7},{28,24},{22,18},{26,22},{2... | collective-permute-start | bytes 2359304 | tf_op jit(solution)/shard_map/ppermute | solution.py:264
  27.5 6.6 %collective-permute-start.6 = (bf16[208,256]{1,0:T(8,128)(2,1)S(1)}, bf16[208,256]{1,0:T(8,128)(2,1)S(1)}, u32[]{:S(2)}, u32[]{:S(2)}) collective-permute-start(bf16[208,256]{1,0:T(8,128)(2,1)S(1)} %convert_element_type.139), channel_id=1, source_target_pairs={{0,4},{4,0},{8,12},{12,8},{1,5},{5,1},{9,13},{13,9},{2,6},{6,2},{1... | collective-permute-start | bytes 319496 | tf_op jit(solution)/shard_map/ppermute | solution.py:202
  28.6 16.2 %collective-permute-start.4 = (bf16[192,2048]{1,0:T(8,128)(2,1)S(1)}, bf16[192,2048]{1,0:T(8,128)(2,1)S(1)}, u32[]{:S(2)}, u32[]{:S(2)}) collective-permute-start(bf16[192,2048]{1,0:T(8,128)(2,1)S(1)} %add_convert_fusion.3), channel_id=1, source_target_pairs={{0,4},{4,8},{10,14},{1,5},{5,9},{11,15},{16,20},{20,24},{26,30},{1... | collective-permute-start | bytes 2359304 | tf_op jit(solution)/shard_map/ppermute | solution.py:264
  33.5 16.1 %collective-permute-start.5 = (bf16[192,2048]{1,0:T(8,128)(2,1)S(1)}, bf16[192,2048]{1,0:T(8,128)(2,1)S(1)}, u32[]{:S(2)}, u32[]{:S(2)}) collective-permute-start(bf16[192,2048]{1,0:T(8,128)(2,1)S(1)} %add_convert_fusion.2), channel_id=1, source_target_pairs={{8,4},{12,8},{6,2},{9,5},{13,9},{7,3},{24,20},{28,24},{22,18},{25,... | collective-permute-start | bytes 2359304 | tf_op jit(solution)/shard_map/ppermute | solution.py:264
  34.2 17.7 %collective-permute-start.7 = (bf16[208,256]{1,0:T(8,128)(2,1)S(1)}, bf16[208,256]{1,0:T(8,128)(2,1)S(1)}, u32[]{:S(2)}, u32[]{:S(2)}) collective-permute-start(bf16[208,256]{1,0:T(8,128)(2,1)S(1)} %convert_element_type.141), channel_id=1, source_target_pairs={{0,8},{4,12},{8,0},{12,4},{1,9},{5,13},{9,1},{13,5},{2,10},{6,14},... | collective-permute-start | bytes 319496 | tf_op jit(solution)/shard_map/ppermute | solution.py:202
  45.1 16.4 %collective-permute-start.9 = (bf16[192,2048]{1,0:T(8,128)(2,1)S(1)}, bf16[192,2048]{1,0:T(8,128)(2,1)S(1)}, u32[]{:S(2)}, u32[]{:S(2)}) collective-permute-start(bf16[192,2048]{1,0:T(8,128)(2,1)S(1)} %add_convert_fusion.1), channel_id=1, source_target_pairs={{0,4},{4,8},{8,12},{1,5},{5,9},{9,13},{16,20},{20,24},{24,28},{17,... | collective-permute-start | bytes 2359304 | tf_op jit(solution)/shard_map/ppermute | solution.py:264
  49.8 13.9 %collective-permute-start.10 = (bf16[192,2048]{1,0:T(8,128)(2,1)S(1)}, bf16[192,2048]{1,0:T(8,128)(2,1)S(1)}, u32[]{:S(2)}, u32[]{:S(2)}) collective-permute-start(bf16[192,2048]{1,0:T(8,128)(2,1)S(1)} %add_convert_fusion), channel_id=1, source_target_pairs={{4,0},{8,4},{12,8},{5,1},{9,5},{13,9},{20,16},{24,20},{28,24},{21,... | collective-permute-start | bytes 2359304 | tf_op jit(solution)/shard_map/ppermute | solution.py:264
  52.2 5.3 %copy-start.5 = (s32[192]{0:T(256)S(1)}, s32[192]{0:T(256)}, u32[]{:S(2)}) copy-start(s32[192]{0:T(256)} %param.15) | copy-start | bytes 2308
  57.5 0.7 copy-start.1
  59.0 4.8 %collective-permute-start.11 = (bf16[192,2048]{1,0:T(8,128)(2,1)S(1)}, bf16[192,2048]{1,0:T(8,128)(2,1)S(1)}, u32[]{:S(2)}, u32[]{:S(2)}) collective-permute-start(bf16[192,2048]{1,0:T(8,128)(2,1)S(1)} %get-tuple-element.92), channel_id=1, source_target_pairs={{0,2},{2,0},{1,3},{3,1},{4,6},{6,4},{5,7},{7,5},{8,10},{10,8},{9,1... | collective-permute-start | bytes 2359304 | tf_op jit(solution)/shard_map/ppermute | solution.py:360
  60.8 15.8 %collective-permute-start.15 = (bf16[192,2048]{1,0:T(8,128)(2,1)S(1)}, bf16[192,2048]{1,0:T(8,128)(2,1)S(1)}, u32[]{:S(2)}, u32[]{:S(2)}) collective-permute-start(bf16[192,2048]{1,0:T(8,128)(2,1)S(1)} %get-tuple-element.92), channel_id=1, source_target_pairs={{2,3},{3,2},{6,7},{7,6},{10,11},{11,10},{14,15},{15,14},{18,19},{1... | collective-permute-start | bytes 2359304 | tf_op jit(solution)/shard_map/ppermute | solution.py:211
  64.6 13.3 %copy-start.4 = (bf16[192,2048]{1,0:T(8,128)(2,1)S(1)}, bf16[192,2048]{1,0:T(8,128)(2,1)}, u32[]{:S(2)}) copy-start(bf16[192,2048]{1,0:T(8,128)(2,1)} %param.9) | copy-start | bytes 2359300
  64.7 13.2 %collective-permute-start.16 = (bf16[192,2048]{1,0:T(8,128)(2,1)S(1)}, bf16[192,2048]{1,0:T(8,128)(2,1)S(1)}, u32[]{:S(2)}, u32[]{:S(2)}) collective-permute-start(bf16[192,2048]{1,0:T(8,128)(2,1)S(1)} %broadcast_select_fusion.2), channel_id=1, source_target_pairs={{0,2},{2,0},{1,3},{3,1},{4,6},{6,4},{5,7},{7,5},{8,10},{10,8},{9,1... | collective-permute-start | bytes 2359304 | tf_op jit(solution)/shard_map/ppermute | solution.py:367
  66.2 6.3 %collective-permute-start.14 = (f32[2,192]{1,0:T(2,128)S(1)}, f32[2,192]{1,0:T(2,128)S(1)}, u32[]{:S(2)}, u32[]{:S(2)}) collective-permute-start(f32[2,192]{1,0:T(2,128)S(1)} %pad_maximum_fusion.1), channel_id=1, source_target_pairs={{0,12},{4,0},{8,4},{12,8},{1,13},{5,1},{9,5},{13,9},{2,14},{6,2},{... | collective-permute-start | bytes 4616 | tf_op jit(solution)/shard_map/ppermute | solution.py:378
  71.2 5.4 %collective-permute-start.12 = (f32[2,192]{1,0:T(2,128)S(1)}, f32[2,192]{1,0:T(2,128)S(1)}, u32[]{:S(2)}, u32[]{:S(2)}) collective-permute-start(f32[2,192]{1,0:T(2,128)S(1)} %pad_maximum_fusion.1), channel_id=1, source_target_pairs={{0,4},{4,8},{8,12},{12,0},{1,5},{5,9},{9,13},{13,1},{2,6},{6,10},{... | collective-permute-start | bytes 4616 | tf_op jit(solution)/shard_map/ppermute | solution.py:378
  71.2 5.4 %collective-permute-start.13 = (f32[2,192]{1,0:T(2,128)S(1)}, f32[2,192]{1,0:T(2,128)S(1)}, u32[]{:S(2)}, u32[]{:S(2)}) collective-permute-start(f32[2,192]{1,0:T(2,128)S(1)} %pad_maximum_fusion.1), channel_id=1, source_target_pairs={{0,8},{4,12},{8,0},{12,4},{1,9},{5,13},{9,1},{13,5},{2,10},{6,14},... | collective-permute-start | bytes 4616 | tf_op jit(solution)/shard_map/ppermute | solution.py:378
  76.7 1.2 %collective-permute-start.17 = (f32[192]{0:T(256)S(1)}, f32[192]{0:T(256)S(1)}, u32[]{:S(2)}, u32[]{:S(2)}) collective-permute-start(f32[192]{0:T(256)S(1)} %bitcast.47), channel_id=1, source_target_pairs={{0,2},{2,0},{1,3},{3,1},{4,6},{6,4},{5,7},{7,5},{8,10},{10,8},{9,1... | collective-permute-start | bytes 2312 | tf_op jit(solution)/shard_map/ppermute | solution.py:386
  79.4 5.0 %collective-permute-start.18 = (bf16[192,256]{1,0:T(8,128)(2,1)S(1)}, bf16[192,256]{1,0:T(8,128)(2,1)S(1)}, u32[]{:S(2)}, u32[]{:S(2)}) collective-permute-start(bf16[192,256]{1,0:T(8,128)(2,1)S(1)} %get-tuple-element.94), channel_id=1, source_target_pairs={{0,4},{4,0},{8,12},{12,8},{1,5},{5,1},{9,13},{13,9},{2,6},{6,2},{1... | collective-permute-start | bytes 294920 | tf_op jit(solution)/shard_map/ppermute | solution.py:202
  80.1 4.6 %collective-permute-start.19 = (bf16[192,256]{1,0:T(8,128)(2,1)S(1)}, bf16[192,256]{1,0:T(8,128)(2,1)S(1)}, u32[]{:S(2)}, u32[]{:S(2)}) collective-permute-start(bf16[192,256]{1,0:T(8,128)(2,1)S(1)} %get-tuple-element.82), channel_id=1, source_target_pairs={{0,1},{1,0},{2,3},{3,2},{4,5},{5,4},{6,7},{7,6},{8,9},{9,8},{10,11... | collective-permute-start | bytes 294920 | tf_op jit(solution)/shard_map/ppermute | solution.py:211
  80.7 13.9 %collective-permute-start.21 = (bf16[192,2048]{1,0:T(8,128)(2,1)S(1)}, bf16[192,2048]{1,0:T(8,128)(2,1)S(1)}, u32[]{:S(2)}, u32[]{:S(2)}) collective-permute-start(bf16[192,2048]{1,0:T(8,128)(2,1)S(1)} %get-tuple-element.72), channel_id=1, source_target_pairs={{0,1},{1,0},{4,5},{5,4},{8,9},{9,8},{12,13},{13,12},{16,17},{17,16... | collective-permute-start | bytes 2359304 | tf_op jit(solution)/shard_map/ppermute | solution.py:211
  84.7 6.9 %collective-permute-start.20 = (bf16[192,256]{1,0:T(8,128)(2,1)S(1)}, bf16[192,256]{1,0:T(8,128)(2,1)S(1)}, u32[]{:S(2)}, u32[]{:S(2)}) collective-permute-start(bf16[192,256]{1,0:T(8,128)(2,1)S(1)} %convert_element_type.162), channel_id=1, source_target_pairs={{0,8},{4,12},{8,0},{12,4},{1,9},{5,13},{9,1},{13,5},{2,10},{6,14},... | collective-permute-start | bytes 294920 | tf_op jit(solution)/shard_map/ppermute | solution.py:202
  94.6 3.9 %collective-permute-start.22 = (bf16[192,2048]{1,0:T(8,128)(2,1)S(1)}, bf16[192,2048]{1,0:T(8,128)(2,1)S(1)}, u32[]{:S(2)}, u32[]{:S(2)}) collective-permute-start(bf16[192,2048]{1,0:T(8,128)(2,1)S(1)} %broadcast_select_fusion.1), channel_id=1, source_target_pairs={{0,2},{2,0},{1,3},{3,1},{4,6},{6,4},{5,7},{7,5},{8,10},{10,8},{9,1... | collective-permute-start | bytes 2359304 | tf_op jit(solution)/shard_map/ppermute | solution.py:417
  94.7 6.3 %collective-permute-start.23 = (bf16[192,384]{1,0:T(8,128)(2,1)S(1)}, bf16[192,384]{1,0:T(8,128)(2,1)S(1)}, u32[]{:S(2)}, u32[]{:S(2)}) collective-permute-start(bf16[192,384]{1,0:T(8,128)(2,1)S(1)} %pad_maximum_fusion), channel_id=1, source_target_pairs={{0,1},{1,0},{2,3},{3,2},{4,5},{5,4},{6,7},{7,6},{8,9},{9,8},{10,11... | collective-permute-start | bytes 442376 | tf_op jit(solution)/shard_map/ppermute | solution.py:211

commit v15 on v14

--- a/solution.py
+++ b/solution.py
@@ -358,11 +358,11 @@
     pulled_here = (gain_row * (sum(parts) + low_product)).astype(BF16)
     swap = [(0, 1), (1, 0)]
     pulled = lax.ppermute(pulled_here, "section", swap)
-    pulled_others = with_other_replicas(pulled_here, (1,))[1:]
     from_left, from_right, _ = lax.optimization_barrier((from_left, from_right, pulled_here))
 
     projected = parts[-1] + from_left.astype(F32) + from_right.astype(F32) + low_product
     hidden = (token_float + inv_first * projected).astype(BF16)
+    late_others = with_other_replicas(jnp.where(is_first, hidden, pulled_here))[1:]
     swapped = [
         lax.ppermute(jnp.where(is_first, hidden, other), "section", swap) for other in early_all[1:]
     ]
@@ -381,7 +381,7 @@
     else:
         for step in doubling_steps():
             row_sums = sum_step(row_sums, step, F32)
-    row_sums, *pulled_others = lax.optimization_barrier((row_sums, *pulled_others))
+    row_sums, *small_early_all = lax.optimization_barrier((row_sums, *small_early_all))
     inv_second = lax.rsqrt(row_sums[0] / features + EPSILON)
     inv_on_second = lax.ppermute(inv_second, "section", swap)[:, None]
     inv_second = inv_second[:, None]
@@ -393,39 +393,33 @@
         (hidden_on_second.astype(F32) * gain_row).astype(BF16),
     )
     rank_late = jnp.where(is_first, times_up_transposed(late), times_down(late))
-    hidden_others = with_other_replicas(
-        lax.optimization_barrier((hidden, rank_late))[0], (0,)
-    )[1:]
-    for at, step in enumerate(doubling_steps()):
+    for step in doubling_steps():
         rank_late = sum_step(rank_late, step)
-        if at == 0:
-            rank_late, *small_early_all = lax.optimization_barrier((rank_late, *small_early_all))
 
     inv_second = jnp.where(is_first, inv_second, inv_on_second)
     row_scale = jnp.where(is_first, inv_first, inv_second)
     small_late = (coefficients * rank_late * row_scale).astype(BF16)
-    beside = jnp.concatenate(
-        [
-            small_late,
-            jnp.broadcast_to(inv_second, (rows, 64)).astype(BF16),
-            jnp.broadcast_to(toward_hidden, (rows, 64)).astype(BF16),
-        ],
-        axis=1,
-    )
-    small_late_all = with_other_replicas(beside)
-    swapped = [
-        lax.ppermute(
-            lax.optimization_barrier((jnp.where(is_first, *pair), beside))[0], "section", swap
-        )
-        for pair in zip(hidden_others, pulled_others)
-    ]
-    hidden_all = [hidden] + [jnp.where(is_first, *pair) for pair in zip(hidden_others, swapped)]
-    pulled_all = [pulled] + swapped
+    small_late_all = with_other_replicas(
+        jnp.concatenate(
+            [
+                small_late,
+                jnp.broadcast_to(inv_second, (rows, 64)).astype(BF16),
+                jnp.broadcast_to(toward_hidden, (rows, 64)).astype(BF16),
+            ],
+            axis=1,
+        )
+    )
     small_early_own = (small_early.astype(F32) * row_scale).astype(BF16)
     sums = gradient_call(
         own_gradient_kernel,
         table, [], [early, late], [small_early_own, small_late], width, ranks, rows,
     )
+    swapped = [
+        lax.ppermute(lax.optimization_barrier((other, *sums))[0], "section", swap)
+        for other in late_others
+    ]
+    hidden_all = [hidden] + [jnp.where(is_first, *pair) for pair in zip(late_others, swapped)]
+    pulled_all = [pulled] + swapped
     for at in range(1, replicas):
         sums = gradient_call(
             other_gradient_kernel,

time: 107 us -> 107 us (level)
  starting transfers between devices: 43.7 us -> 40 us
  waiting for transfers between devices: 20.7 us -> 23.4 us
    ppermute x4, waiting for transfers between devices: 5.04 us -> 11 us  [sum_step(): other = lax.ppermute(value.astype(wire), 'tensor', pairs)]
    ppermute x3, waiting for transfers between devices: 4.57 us -> 0.99 us  [on_device(): lax.ppermute(row_sums, 'tensor', [(z, (z + step) % count) for z in everyo...]
    ppermute x3, starting transfers between devices: 5.8 us -> 3.12 us  [on_device(): lax.ppermute(row_sums, 'tensor', [(z, (z + step) % count) for z in everyo...]
    ppermute x1, starting transfers between devices: 1.51 us -> 0.07 us  [on_device(): lax.ppermute(jnp.where(is_first, hidden, other), 'section', swap)]
    ppermute x1, waiting for transfers between devices: 1.13 us -> 0.01 us  [on_device(): inv_on_second = lax.ppermute(inv_second, 'section', swap)[:, None]]
    ppermute x5 -> x4, waiting for transfers between devices: 5.25 us -> 5.84 us  [with_other_replicas(): lax.ppermute(value, ('section', 'replica'), [(s * count + r, s * count +...]
    ppermute x5 -> x4, starting transfers between devices: 9.11 us -> 9.34 us  [with_other_replicas(): lax.ppermute(value, ('section', 'replica'), [(s * count + r, s * count +...]
  transfers between devices with their start and end apart: 24 -> 23, of which waited for: 12 -> 11; matrix products, arithmetic and copies ran while one was open for 8% -> 10% of each run, Pallas kernels for 22% -> 22%
where the time goes in v15:
time: 107 us; the launch traced here: 106 us
  starting transfers between devices  40 us (37%)
  Pallas kernels  28.5 us (27%)
  waiting for transfers between devices  23.4 us (22%)
  other arithmetic  9.17 us (9%)
  matrix products  2.96 us (3%)
  between operations  1.14 us (1%)
    pallas_call x4, Pallas kernels, block_product(): pl.pallas_call(functools.partial(block_kernel, blocks=blocks, tile=tile,...  20.9 us
    ppermute x8, starting transfers between devices, line(): return lax.ppermute(value, ('tensor', 'section'), pairs)  18.4 us
    ppermute x4, waiting for transfers between devices, sum_step(): other = lax.ppermute(value.astype(wire), 'tensor', pairs)  11 us
    ppermute x4, starting transfers between devices, with_other_replicas(): lax.ppermute(value, ('section', 'replica'), [(s * count + r, s * count +...  9.34 us
    pallas_call x2, Pallas kernels, gradient_call(): pl.pallas_call(kernel, grid_spec=pltpu.PrefetchScalarGridSpec(num_scalar_...  7.6 us
    ppermute x4, starting transfers between devices, sum_step(): other = lax.ppermute(value.astype(wire), 'tensor', pairs)  7.16 us
    ppermute x4, waiting for transfers between devices, with_other_replicas(): lax.ppermute(value, ('section', 'replica'), [(s * count + r, s * count +...  5.84 us
    ppermute x8, waiting for transfers between devices, line(): return lax.ppermute(value, ('tensor', 'section'), pairs)  5.4 us
  transfers between devices with their start and end apart: 23, of which 11 were waited for; matrix products, arithmetic and copies ran while one was open for 10% of the time, Pallas kernels for 22%

profile of v15, /device:TPU:0, one launch (start us, length us, event | category | flops | bytes accessed | tf_op | source)
XLA Modules:
  0.0 105.8 jit_solution(2563753311119904823)
XLA Ops:
  0.7 1.5 %fusion.17.value_ref.early = bf16[192,2048]{1,0:T(8,128)(2,1)S(1)} fusion(bf16[192,2048]{1,0:T(8,128)(2,1)} %param.9, bf16[192,2048]{1,0:T(8,128)(2,1)} %param.8, f32[2048]{0:T(1024)} %bitcast.38, pred[]{:T(512)S(6)} %eq.20), kind=kLoop, calls=%fused_computation.35 | loop fusion | flops 1572864 | bytes 2367489 | tf_op jit(solution)/shard_map/jit(_where)/select_n | solution.py:267
  2.1 1.6 %collective-permute-start = (bf16[192,2048]{1,0:T(8,128)(2,1)S(1)}, bf16[192,2048]{1,0:T(8,128)(2,1)}, u32[]{:S(2)}, u32[]{:S(2)}) collective-permute-start(bf16[192,2048]{1,0:T(8,128)(2,1)S(1)} %fusion.17.value_ref.early), channel_id=1, source_target_pairs={{2,6},{6,10},{10,14},{3,7},{7,11},{11,15},{18,22},{22,26},{26,30},... | collective-permute-start | bytes 2359304 | tf_op jit(solution)/shard_map/ppermute | solution.py:264
  3.8 1.6 %collective-permute-start.2 = (bf16[192,2048]{1,0:T(8,128)(2,1)S(1)}, bf16[192,2048]{1,0:T(8,128)(2,1)}, u32[]{:S(2)}, u32[]{:S(2)}) collective-permute-start(bf16[192,2048]{1,0:T(8,128)(2,1)S(1)} %fusion.17.value_ref.early), channel_id=1, source_target_pairs={{6,2},{10,6},{14,10},{7,3},{11,7},{15,11},{22,18},{26,22},{30,26},... | collective-permute-start | bytes 2359304 | tf_op jit(solution)/shard_map/ppermute | solution.py:264
  5.4 5.2 %shard_map.95 = f32[192,2048]{1,0:T(8,128)S(1)} custom-call(s32[2]{0:T(128)S(1)} %pad_add_fusion.table, bf16[192,2048]{1,0:T(8,128)(2,1)S(1)} %fusion.17.value_ref.early, bf16[2048,8192]{1,0:T(8,128)(2,1)} %bitcast.41), custom_call_target="tpu_custom_call" | custom-call | flops 6442450944 | bytes 8388608 | tf_op jit(solution)/shard_map/pallas_call | solution.py:72
  10.6 3.0 %collective-permute-start.8 = (bf16[192,2048]{1,0:T(8,128)(2,1)S(1)}, bf16[192,2048]{1,0:T(8,128)(2,1)}, u32[]{:S(2)}, u32[]{:S(2)}) collective-permute-start(bf16[192,2048]{1,0:T(8,128)(2,1)S(1)} %fusion.17.value_ref.early), channel_id=1, source_target_pairs={{0,1},{1,0},{2,3},{3,2},{4,5},{5,4},{6,7},{7,6},{8,9},{9,8},{10,11... | collective-permute-start | bytes 2359304 | tf_op jit(solution)/shard_map/ppermute | solution.py:211
  13.8 1.3 %add_convert_fusion.5 = bf16[192,2048]{1,0:T(8,128)(2,1)S(1)} fusion(bf16[192,2048]{1,0:T(8,128)(2,1)} %collective-permute-done, f32[192,2048]{1,0:T(8,128)S(1)} %shard_map.95, pred[]{:T(512)S(6)} %eq.20), kind=kLoop, calls=%fused_computation.22 | loop fusion | flops 1572864 | bytes 3145729 | tf_op jit(solution)/shard_map/convert_element_type | solution.py:324
  15.1 3.7 %collective-permute-start.1 = (bf16[192,2048]{1,0:T(8,128)(2,1)S(1)}, bf16[192,2048]{1,0:T(8,128)(2,1)S(1)}, u32[]{:S(2)}, u32[]{:S(2)}) collective-permute-start(bf16[192,2048]{1,0:T(8,128)(2,1)S(1)} %add_convert_fusion.5), channel_id=1, source_target_pairs={{0,4},{6,10},{10,14},{1,5},{7,11},{11,15},{16,20},{22,26},{26,30},... | collective-permute-start | bytes 2359304 | tf_op jit(solution)/shard_map/ppermute | solution.py:264
  18.8 1.4 %add_convert_fusion.4 = bf16[192,2048]{1,0:T(8,128)(2,1)S(1)} fusion(bf16[192,2048]{1,0:T(8,128)(2,1)} %collective-permute-done.2, f32[192,2048]{1,0:T(8,128)S(1)} %shard_map.95, pred[]{:T(512)S(6)} %eq.20), kind=kLoop, calls=%fused_computation.21 | loop fusion | flops 1572864 | bytes 3145729 | tf_op jit(solution)/shard_map/convert_element_type | solution.py:324
  22.3 5.2 %shard_map.96 = f32[192,2048]{1,0:T(8,128)S(1)} custom-call(s32[2]{0:T(128)S(1)} %pad_add_fusion.table, bf16[192,2048]{1,0:T(8,128)(2,1)S(1)} %select_select_fusion.2.value_ref, bf16[2048,8192]{1,0:T(8,128)(2,1)} %bitcast.42), custom_call_target="tpu_custom_call" | custom-call | flops 6442450944 | bytes 8388608 | tf_op jit(solution)/shard_map/pallas_call | solution.py:72
  28.6 4.4 %collective-permute-start.4 = (bf16[192,2048]{1,0:T(8,128)(2,1)S(1)}, bf16[192,2048]{1,0:T(8,128)(2,1)S(1)}, u32[]{:S(2)}, u32[]{:S(2)}) collective-permute-start(bf16[192,2048]{1,0:T(8,128)(2,1)S(1)} %add_convert_fusion.3), channel_id=1, source_target_pairs={{0,4},{4,8},{10,14},{1,5},{5,9},{11,15},{16,20},{20,24},{26,30},{1... | collective-permute-start | bytes 2359304 | tf_op jit(solution)/shard_map/ppermute | solution.py:264
  34.2 3.2 %collective-permute-start.7 = (bf16[208,256]{1,0:T(8,128)(2,1)S(1)}, bf16[208,256]{1,0:T(8,128)(2,1)S(1)}, u32[]{:S(2)}, u32[]{:S(2)}) collective-permute-start(bf16[208,256]{1,0:T(8,128)(2,1)S(1)} %convert_element_type.141), channel_id=1, source_target_pairs={{0,8},{4,12},{8,0},{12,4},{1,9},{5,13},{9,1},{13,5},{2,10},{6,14},... | collective-permute-start | bytes 319496 | tf_op jit(solution)/shard_map/ppermute | solution.py:202
  37.7 5.2 %shard_map.97 = f32[192,2048]{1,0:T(8,128)S(1)} custom-call(s32[2]{0:T(128)S(1)} %pad_add_fusion.table, bf16[192,2048]{1,0:T(8,128)(2,1)S(1)} %select_select_fusion.1.value_ref, bf16[2048,8192]{1,0:T(8,128)(2,1)} %bitcast.43), custom_call_target="tpu_custom_call" | custom-call | flops 6442450944 | bytes 8388608 | tf_op jit(solution)/shard_map/pallas_call | solution.py:72
  42.9 1.9 %collective-permute-done.4 = bf16[192,2048]{1,0:T(8,128)(2,1)S(1)} collective-permute-done((bf16[192,2048]{1,0:T(8,128)(2,1)S(1)}, bf16[192,2048]{1,0:T(8,128)(2,1)S(1)}, u32[]{:S(2)}, u32[]{:S(2)}) %collective-permute-start.4) | collective-permute-done | bytes 786464 | tf_op jit(solution)/shard_map/ppermute | solution.py:264
  45.1 4.4 %collective-permute-start.9 = (bf16[192,2048]{1,0:T(8,128)(2,1)S(1)}, bf16[192,2048]{1,0:T(8,128)(2,1)S(1)}, u32[]{:S(2)}, u32[]{:S(2)}) collective-permute-start(bf16[192,2048]{1,0:T(8,128)(2,1)S(1)} %add_convert_fusion.1), channel_id=1, source_target_pairs={{0,4},{4,8},{8,12},{1,5},{5,9},{9,13},{16,20},{20,24},{24,28},{17,... | collective-permute-start | bytes 2359304 | tf_op jit(solution)/shard_map/ppermute | solution.py:264
  49.8 1.3 %collective-permute-start.10 = (bf16[192,2048]{1,0:T(8,128)(2,1)S(1)}, bf16[192,2048]{1,0:T(8,128)(2,1)S(1)}, u32[]{:S(2)}, u32[]{:S(2)}) collective-permute-start(bf16[192,2048]{1,0:T(8,128)(2,1)S(1)} %add_convert_fusion), channel_id=1, source_target_pairs={{4,0},{8,4},{12,8},{5,1},{9,5},{13,9},{20,16},{24,20},{28,24},{21,... | collective-permute-start | bytes 2359304 | tf_op jit(solution)/shard_map/ppermute | solution.py:264
  52.2 5.2 %shard_map.98 = f32[192,2048]{1,0:T(8,128)S(1)} custom-call(s32[2]{0:T(128)S(1)} %pad_add_fusion.table, bf16[192,2048]{1,0:T(8,128)(2,1)S(1)} %select_select_fusion.value_ref, bf16[2048,8192]{1,0:T(8,128)(2,1)} %bitcast.44), custom_call_target="tpu_custom_call" | custom-call | flops 6442450944 | bytes 8388608 | tf_op jit(solution)/shard_map/pallas_call | solution.py:72
  58.2 0.8 multiply_convert_fusion.1
  59.0 1.8 %collective-permute-start.11 = (bf16[192,2048]{1,0:T(8,128)(2,1)S(1)}, bf16[192,2048]{1,0:T(8,128)(2,1)S(1)}, u32[]{:S(2)}, u32[]{:S(2)}) collective-permute-start(bf16[192,2048]{1,0:T(8,128)(2,1)S(1)} %get-tuple-element.87), channel_id=1, source_target_pairs={{0,2},{2,0},{1,3},{3,1},{4,6},{6,4},{5,7},{7,5},{8,10},{10,8},{9,1... | collective-permute-start | bytes 2359304 | tf_op jit(solution)/shard_map/ppermute | solution.py:360
  60.8 2.9 %collective-permute-done.10 = bf16[192,2048]{1,0:T(8,128)(2,1)S(1)} collective-permute-done((bf16[192,2048]{1,0:T(8,128)(2,1)S(1)}, bf16[192,2048]{1,0:T(8,128)(2,1)S(1)}, u32[]{:S(2)}, u32[]{:S(2)}) %collective-permute-start.10) | collective-permute-done | bytes 786464 | tf_op jit(solution)/shard_map/ppermute | solution.py:264
  63.7 0.9 broadcast_select_fusion.1
  66.0 1.4 %collective-permute-start.12 = (f32[2,192]{1,0:T(2,128)S(1)}, f32[2,192]{1,0:T(2,128)S(1)}, u32[]{:S(2)}, u32[]{:S(2)}) collective-permute-start(f32[2,192]{1,0:T(2,128)S(1)} %pad_maximum_fusion.1), channel_id=1, source_target_pairs={{0,4},{4,8},{8,12},{12,0},{1,5},{5,9},{9,13},{13,1},{2,6},{6,10},{... | collective-permute-start | bytes 4616 | tf_op jit(solution)/shard_map/ppermute | solution.py:378
  67.3 1.0 collective-permute-start.13
  68.4 2.5 %collective-permute-start.15 = (bf16[192,256]{1,0:T(8,128)(2,1)S(1)}, bf16[192,256]{1,0:T(8,128)(2,1)S(1)}, u32[]{:S(2)}, u32[]{:S(2)}) collective-permute-start(bf16[192,256]{1,0:T(8,128)(2,1)S(1)} %get-tuple-element.78), channel_id=1, source_target_pairs={{0,1},{1,0},{2,3},{3,2},{4,5},{5,4},{6,7},{7,6},{8,9},{9,8},{10,11... | collective-permute-start | bytes 294920 | tf_op jit(solution)/shard_map/ppermute | solution.py:211
  71.9 1.6 %collective-permute-done.15.small_early = bf16[192,256]{1,0:T(8,128)(2,1)S(1)} collective-permute-done((bf16[192,256]{1,0:T(8,128)(2,1)S(1)}, bf16[192,256]{1,0:T(8,128)(2,1)S(1)}, u32[]{:S(2)}, u32[]{:S(2)}) %collective-permute-start.15) | collective-permute-done | bytes 98336 | tf_op jit(solution)/shard_map/ppermute | solution.py:211
  73.5 2.2 %collective-permute-start.20 = (bf16[192,2048]{1,0:T(8,128)(2,1)S(1)}, bf16[192,2048]{1,0:T(8,128)(2,1)S(1)}, u32[]{:S(2)}, u32[]{:S(2)}) collective-permute-start(bf16[192,2048]{1,0:T(8,128)(2,1)S(1)} %get-tuple-element.76), channel_id=1, source_target_pairs={{0,1},{1,0},{2,3},{3,2},{4,5},{5,4},{6,7},{7,6},{8,9},{9,8},{10,11... | collective-permute-start | bytes 2359304 | tf_op jit(solution)/shard_map/ppermute | solution.py:211
  77.2 3.6 %collective-permute-start.18 = (bf16[192,256]{1,0:T(8,128)(2,1)S(1)}, bf16[192,256]{1,0:T(8,128)(2,1)S(1)}, u32[]{:S(2)}, u32[]{:S(2)}) collective-permute-start(bf16[192,256]{1,0:T(8,128)(2,1)S(1)} %get-tuple-element.89), channel_id=1, source_target_pairs={{0,4},{4,0},{8,12},{12,8},{1,5},{5,1},{9,13},{13,9},{2,6},{6,2},{1... | collective-permute-start | bytes 294920 | tf_op jit(solution)/shard_map/ppermute | solution.py:202
  80.8 3.1 %collective-permute-done.18 = bf16[192,256]{1,0:T(8,128)(2,1)S(1)} collective-permute-done((bf16[192,256]{1,0:T(8,128)(2,1)S(1)}, bf16[192,256]{1,0:T(8,128)(2,1)S(1)}, u32[]{:S(2)}, u32[]{:S(2)}) %collective-permute-start.18) | collective-permute-done | bytes 98336 | tf_op jit(solution)/shard_map/ppermute | solution.py:202
  84.3 7.1 %collective-permute-done.19 = bf16[192,256]{1,0:T(8,128)(2,1)S(1)} collective-permute-done((bf16[192,256]{1,0:T(8,128)(2,1)S(1)}, bf16[192,256]{1,0:T(8,128)(2,1)S(1)}, u32[]{:S(2)}, u32[]{:S(2)}) %collective-permute-start.19) | collective-permute-done | bytes 98336 | tf_op jit(solution)/shard_map/ppermute | solution.py:202
  91.5 2.3 %shard_map.99 = (f32[2048,256]{1,0:T(8,128)S(1)}, f32[256,2048]{1,0:T(8,128)S(1)}) custom-call(s32[2]{0:T(128)S(1)} %pad_add_fusion.table, bf16[192,2048]{1,0:T(8,128)(2,1)S(1)} %fusion.17.value_ref.early, bf16[192,2048]{1,0:T(8,128)(2,1)S(1)} %fusion.16.late, bf16[192,256]{1,0:T(8,128)(2,1)S(1)} %get-tuple-element.85.small_early, ...), custom_call_target="tpu_custom_call" | custom-call | flops 402653184 | bytes 5767168 | tf_op jit(solution)/shard_map/pallas_call | solution.py:145
  94.1 1.7 %collective-permute-start.22 = (bf16[192,384]{1,0:T(8,128)(2,1)S(1)}, bf16[192,384]{1,0:T(8,128)(2,1)S(1)}, u32[]{:S(2)}, u32[]{:S(2)}) collective-permute-start(bf16[192,384]{1,0:T(8,128)(2,1)S(1)} %pad_maximum_fusion), channel_id=1, source_target_pairs={{0,1},{1,0},{2,3},{3,2},{4,5},{5,4},{6,7},{7,6},{8,9},{9,8},{10,11... | collective-permute-start | bytes 442376 | tf_op jit(solution)/shard_map/ppermute | solution.py:211
  96.2 4.2 %collective-permute-done.22.small_late = bf16[192,384]{1,0:T(8,128)(2,1)S(1)} collective-permute-done((bf16[192,384]{1,0:T(8,128)(2,1)S(1)}, bf16[192,384]{1,0:T(8,128)(2,1)S(1)}, u32[]{:S(2)}, u32[]{:S(2)}) %collective-permute-start.22) | collective-permute-done | bytes 147488 | tf_op jit(solution)/shard_map/ppermute | solution.py:211
  100.4 5.3 %shard_map.100 = (f32[2048,256]{1,0:T(8,128)}, f32[256,2048]{1,0:T(8,128)}) custom-call(s32[2]{0:T(128)S(1)} %pad_add_fusion.table, f32[1,2048]{1,0:T(1,128)S(1)} %copy-done.1, f32[2048,256]{1,0:T(8,128)S(1)} %get-tuple-element.66.down_sum, f32[256,2048]{1,0:T(8,128)S(1)} %get-tuple-element.67.up_sum, bf16[192,2048]{1,0:T(8,128)(2,1)} %collective-permute-done.8.early, ...), custom_call_target="tpu_custom_call" | custom-call | flops 402653184 | bytes 11534336 | tf_op jit(solution)/shard_map/pallas_call | solution.py:145
  (80 shorter events, 12.0 us)
Async XLA Ops:
  0.6 21.1 %copy-start = (bf16[1,2048,256]{2,1,0:T(8,128)(2,1)S(1)}, bf16[1,2048,256]{2,1,0:T(8,128)(2,1)}, u32[]{:S(2)}) copy-start(bf16[1,2048,256]{2,1,0:T(8,128)(2,1)} %param.12) | copy-start | bytes 3145732
  2.1 11.6 %collective-permute-start = (bf16[192,2048]{1,0:T(8,128)(2,1)S(1)}, bf16[192,2048]{1,0:T(8,128)(2,1)}, u32[]{:S(2)}, u32[]{:S(2)}) collective-permute-start(bf16[192,2048]{1,0:T(8,128)(2,1)S(1)} %fusion.17.value_ref.early), channel_id=1, source_target_pairs={{2,6},{6,10},{10,14},{3,7},{7,11},{11,15},{18,22},{22,26},{26,30},... | collective-permute-start | bytes 2359304 | tf_op jit(solution)/shard_map/ppermute | solution.py:264
  3.8 15.1 %collective-permute-start.2 = (bf16[192,2048]{1,0:T(8,128)(2,1)S(1)}, bf16[192,2048]{1,0:T(8,128)(2,1)}, u32[]{:S(2)}, u32[]{:S(2)}) collective-permute-start(bf16[192,2048]{1,0:T(8,128)(2,1)S(1)} %fusion.17.value_ref.early), channel_id=1, source_target_pairs={{6,2},{10,6},{14,10},{7,3},{11,7},{15,11},{22,18},{26,22},{30,26},... | collective-permute-start | bytes 2359304 | tf_op jit(solution)/shard_map/ppermute | solution.py:264
  5.4 8.2 %copy-start.6 = (f32[4]{0:T(128)S(1)}, f32[4]{0:T(128)}, u32[]{:S(2)}) copy-start(f32[4]{0:T(128)} %param.14) | copy-start | bytes 52
  10.6 32.3 %collective-permute-start.8 = (bf16[192,2048]{1,0:T(8,128)(2,1)S(1)}, bf16[192,2048]{1,0:T(8,128)(2,1)}, u32[]{:S(2)}, u32[]{:S(2)}) collective-permute-start(bf16[192,2048]{1,0:T(8,128)(2,1)S(1)} %fusion.17.value_ref.early), channel_id=1, source_target_pairs={{0,1},{1,0},{2,3},{3,2},{4,5},{5,4},{6,7},{7,6},{8,9},{9,8},{10,11... | collective-permute-start | bytes 2359304 | tf_op jit(solution)/shard_map/ppermute | solution.py:211
  15.1 5.8 %copy-start.3 = (bf16[192,2048]{1,0:T(8,128)(2,1)S(1)}, bf16[192,2048]{1,0:T(8,128)(2,1)}, u32[]{:S(2)}) copy-start(bf16[192,2048]{1,0:T(8,128)(2,1)} %param.8) | copy-start | bytes 2359300
  15.1 6.1 %copy-start.2 = (bf16[1,256,2048]{2,1,0:T(8,128)(2,1)S(1)}, bf16[1,256,2048]{2,1,0:T(8,128)(2,1)}, u32[]{:S(2)}) copy-start(bf16[1,256,2048]{2,1,0:T(8,128)(2,1)} %param.13) | copy-start | bytes 3145732
  15.1 13.1 %collective-permute-start.1 = (bf16[192,2048]{1,0:T(8,128)(2,1)S(1)}, bf16[192,2048]{1,0:T(8,128)(2,1)S(1)}, u32[]{:S(2)}, u32[]{:S(2)}) collective-permute-start(bf16[192,2048]{1,0:T(8,128)(2,1)S(1)} %add_convert_fusion.5), channel_id=1, source_target_pairs={{0,4},{6,10},{10,14},{1,5},{7,11},{11,15},{16,20},{22,26},{26,30},... | collective-permute-start | bytes 2359304 | tf_op jit(solution)/shard_map/ppermute | solution.py:264
  20.2 12.9 %collective-permute-start.3 = (bf16[192,2048]{1,0:T(8,128)(2,1)S(1)}, bf16[192,2048]{1,0:T(8,128)(2,1)S(1)}, u32[]{:S(2)}, u32[]{:S(2)}) collective-permute-start(bf16[192,2048]{1,0:T(8,128)(2,1)S(1)} %add_convert_fusion.4), channel_id=1, source_target_pairs={{12,8},{6,2},{10,6},{13,9},{7,3},{11,7},{28,24},{22,18},{26,22},{2... | collective-permute-start | bytes 2359304 | tf_op jit(solution)/shard_map/ppermute | solution.py:264
  27.5 6.6 %collective-permute-start.6 = (bf16[208,256]{1,0:T(8,128)(2,1)S(1)}, bf16[208,256]{1,0:T(8,128)(2,1)S(1)}, u32[]{:S(2)}, u32[]{:S(2)}) collective-permute-start(bf16[208,256]{1,0:T(8,128)(2,1)S(1)} %convert_element_type.139), channel_id=1, source_target_pairs={{0,4},{4,0},{8,12},{12,8},{1,5},{5,1},{9,13},{13,9},{2,6},{6,2},{1... | collective-permute-start | bytes 319496 | tf_op jit(solution)/shard_map/ppermute | solution.py:202
  28.6 16.2 %collective-permute-start.4 = (bf16[192,2048]{1,0:T(8,128)(2,1)S(1)}, bf16[192,2048]{1,0:T(8,128)(2,1)S(1)}, u32[]{:S(2)}, u32[]{:S(2)}) collective-permute-start(bf16[192,2048]{1,0:T(8,128)(2,1)S(1)} %add_convert_fusion.3), channel_id=1, source_target_pairs={{0,4},{4,8},{10,14},{1,5},{5,9},{11,15},{16,20},{20,24},{26,30},{1... | collective-permute-start | bytes 2359304 | tf_op jit(solution)/shard_map/ppermute | solution.py:264
  33.5 16.1 %collective-permute-start.5 = (bf16[192,2048]{1,0:T(8,128)(2,1)S(1)}, bf16[192,2048]{1,0:T(8,128)(2,1)S(1)}, u32[]{:S(2)}, u32[]{:S(2)}) collective-permute-start(bf16[192,2048]{1,0:T(8,128)(2,1)S(1)} %add_convert_fusion.2), channel_id=1, source_target_pairs={{8,4},{12,8},{6,2},{9,5},{13,9},{7,3},{24,20},{28,24},{22,18},{25,... | collective-permute-start | bytes 2359304 | tf_op jit(solution)/shard_map/ppermute | solution.py:264
  34.2 17.7 %collective-permute-start.7 = (bf16[208,256]{1,0:T(8,128)(2,1)S(1)}, bf16[208,256]{1,0:T(8,128)(2,1)S(1)}, u32[]{:S(2)}, u32[]{:S(2)}) collective-permute-start(bf16[208,256]{1,0:T(8,128)(2,1)S(1)} %convert_element_type.141), channel_id=1, source_target_pairs={{0,8},{4,12},{8,0},{12,4},{1,9},{5,13},{9,1},{13,5},{2,10},{6,14},... | collective-permute-start | bytes 319496 | tf_op jit(solution)/shard_map/ppermute | solution.py:202
  45.1 15.6 %collective-permute-start.9 = (bf16[192,2048]{1,0:T(8,128)(2,1)S(1)}, bf16[192,2048]{1,0:T(8,128)(2,1)S(1)}, u32[]{:S(2)}, u32[]{:S(2)}) collective-permute-start(bf16[192,2048]{1,0:T(8,128)(2,1)S(1)} %add_convert_fusion.1), channel_id=1, source_target_pairs={{0,4},{4,8},{8,12},{1,5},{5,9},{9,13},{16,20},{20,24},{24,28},{17,... | collective-permute-start | bytes 2359304 | tf_op jit(solution)/shard_map/ppermute | solution.py:264
  49.8 13.9 %collective-permute-start.10 = (bf16[192,2048]{1,0:T(8,128)(2,1)S(1)}, bf16[192,2048]{1,0:T(8,128)(2,1)S(1)}, u32[]{:S(2)}, u32[]{:S(2)}) collective-permute-start(bf16[192,2048]{1,0:T(8,128)(2,1)S(1)} %add_convert_fusion), channel_id=1, source_target_pairs={{4,0},{8,4},{12,8},{5,1},{9,5},{13,9},{20,16},{24,20},{28,24},{21,... | collective-permute-start | bytes 2359304 | tf_op jit(solution)/shard_map/ppermute | solution.py:264
  52.2 5.3 %copy-start.5 = (s32[192]{0:T(256)S(1)}, s32[192]{0:T(256)}, u32[]{:S(2)}) copy-start(s32[192]{0:T(256)} %param.15) | copy-start | bytes 2308
  57.5 0.7 copy-start.1
  59.0 5.9 %collective-permute-start.11 = (bf16[192,2048]{1,0:T(8,128)(2,1)S(1)}, bf16[192,2048]{1,0:T(8,128)(2,1)S(1)}, u32[]{:S(2)}, u32[]{:S(2)}) collective-permute-start(bf16[192,2048]{1,0:T(8,128)(2,1)S(1)} %get-tuple-element.87), channel_id=1, source_target_pairs={{0,2},{2,0},{1,3},{3,1},{4,6},{6,4},{5,7},{7,5},{8,10},{10,8},{9,1... | collective-permute-start | bytes 2359304 | tf_op jit(solution)/shard_map/ppermute | solution.py:360
  64.7 11.0 %copy-start.4 = (bf16[192,2048]{1,0:T(8,128)(2,1)S(1)}, bf16[192,2048]{1,0:T(8,128)(2,1)}, u32[]{:S(2)}) copy-start(bf16[192,2048]{1,0:T(8,128)(2,1)} %param.9) | copy-start | bytes 2359300
  64.8 10.9 %collective-permute-start.16 = (bf16[192,2048]{1,0:T(8,128)(2,1)S(1)}, bf16[192,2048]{1,0:T(8,128)(2,1)S(1)}, u32[]{:S(2)}, u32[]{:S(2)}) collective-permute-start(bf16[192,2048]{1,0:T(8,128)(2,1)S(1)} %broadcast_select_fusion.2), channel_id=1, source_target_pairs={{0,2},{2,0},{1,3},{3,1},{4,6},{6,4},{5,7},{7,5},{8,10},{10,8},{9,1... | collective-permute-start | bytes 2359304 | tf_op jit(solution)/shard_map/ppermute | solution.py:367
  65.3 5.6 %collective-permute-start.14 = (f32[2,192]{1,0:T(2,128)S(1)}, f32[2,192]{1,0:T(2,128)S(1)}, u32[]{:S(2)}, u32[]{:S(2)}) collective-permute-start(f32[2,192]{1,0:T(2,128)S(1)} %pad_maximum_fusion.1), channel_id=1, source_target_pairs={{0,12},{4,0},{8,4},{12,8},{1,13},{5,1},{9,5},{13,9},{2,14},{6,2},{... | collective-permute-start | bytes 4616 | tf_op jit(solution)/shard_map/ppermute | solution.py:378
  66.0 5.4 %collective-permute-start.12 = (f32[2,192]{1,0:T(2,128)S(1)}, f32[2,192]{1,0:T(2,128)S(1)}, u32[]{:S(2)}, u32[]{:S(2)}) collective-permute-start(f32[2,192]{1,0:T(2,128)S(1)} %pad_maximum_fusion.1), channel_id=1, source_target_pairs={{0,4},{4,8},{8,12},{12,0},{1,5},{5,9},{9,13},{13,1},{2,6},{6,10},{... | collective-permute-start | bytes 4616 | tf_op jit(solution)/shard_map/ppermute | solution.py:378
  67.3 4.5 %collective-permute-start.13 = (f32[2,192]{1,0:T(2,128)S(1)}, f32[2,192]{1,0:T(2,128)S(1)}, u32[]{:S(2)}, u32[]{:S(2)}) collective-permute-start(f32[2,192]{1,0:T(2,128)S(1)} %pad_maximum_fusion.1), channel_id=1, source_target_pairs={{0,8},{4,12},{8,0},{12,4},{1,9},{5,13},{9,1},{13,5},{2,10},{6,14},... | collective-permute-start | bytes 4616 | tf_op jit(solution)/shard_map/ppermute | solution.py:378
  68.4 5.0 %collective-permute-start.15 = (bf16[192,256]{1,0:T(8,128)(2,1)S(1)}, bf16[192,256]{1,0:T(8,128)(2,1)S(1)}, u32[]{:S(2)}, u32[]{:S(2)}) collective-permute-start(bf16[192,256]{1,0:T(8,128)(2,1)S(1)} %get-tuple-element.78), channel_id=1, source_target_pairs={{0,1},{1,0},{2,3},{3,2},{4,5},{5,4},{6,7},{7,6},{8,9},{9,8},{10,11... | collective-permute-start | bytes 294920 | tf_op jit(solution)/shard_map/ppermute | solution.py:211
  73.4 2.2 %collective-permute-start.17 = (f32[192]{0:T(256)S(1)}, f32[192]{0:T(256)S(1)}, u32[]{:S(2)}, u32[]{:S(2)}) collective-permute-start(f32[192]{0:T(256)S(1)} %bitcast.47), channel_id=1, source_target_pairs={{0,2},{2,0},{1,3},{3,1},{4,6},{6,4},{5,7},{7,5},{8,10},{10,8},{9,1... | collective-permute-start | bytes 2312 | tf_op jit(solution)/shard_map/ppermute | solution.py:386
  73.5 20.3 %collective-permute-start.20 = (bf16[192,2048]{1,0:T(8,128)(2,1)S(1)}, bf16[192,2048]{1,0:T(8,128)(2,1)S(1)}, u32[]{:S(2)}, u32[]{:S(2)}) collective-permute-start(bf16[192,2048]{1,0:T(8,128)(2,1)S(1)} %get-tuple-element.76), channel_id=1, source_target_pairs={{0,1},{1,0},{2,3},{3,2},{4,5},{5,4},{6,7},{7,6},{8,9},{9,8},{10,11... | collective-permute-start | bytes 2359304 | tf_op jit(solution)/shard_map/ppermute | solution.py:211
  77.2 6.7 %collective-permute-start.18 = (bf16[192,256]{1,0:T(8,128)(2,1)S(1)}, bf16[192,256]{1,0:T(8,128)(2,1)S(1)}, u32[]{:S(2)}, u32[]{:S(2)}) collective-permute-start(bf16[192,256]{1,0:T(8,128)(2,1)S(1)} %get-tuple-element.89), channel_id=1, source_target_pairs={{0,4},{4,0},{8,12},{12,8},{1,5},{5,1},{9,13},{13,9},{2,6},{6,2},{1... | collective-permute-start | bytes 294920 | tf_op jit(solution)/shard_map/ppermute | solution.py:202
  83.9 7.4 %collective-permute-start.19 = (bf16[192,256]{1,0:T(8,128)(2,1)S(1)}, bf16[192,256]{1,0:T(8,128)(2,1)S(1)}, u32[]{:S(2)}, u32[]{:S(2)}) collective-permute-start(bf16[192,256]{1,0:T(8,128)(2,1)S(1)} %fusion.23), channel_id=1, source_target_pairs={{0,8},{4,12},{8,0},{12,4},{1,9},{5,13},{9,1},{13,5},{2,10},{6,14},... | collective-permute-start | bytes 294920 | tf_op jit(solution)/shard_map/ppermute | solution.py:202
  93.8 2.4 %collective-permute-start.21 = (bf16[192,2048]{1,0:T(8,128)(2,1)S(1)}, bf16[192,2048]{1,0:T(8,128)(2,1)S(1)}, u32[]{:S(2)}, u32[]{:S(2)}) collective-permute-start(bf16[192,2048]{1,0:T(8,128)(2,1)S(1)} %collective-permute-done.20), channel_id=1, source_target_pairs={{0,2},{2,0},{1,3},{3,1},{4,6},{6,4},{5,7},{7,5},{8,10},{10,8},{9,1... | collective-permute-start | bytes 2359304 | tf_op jit(solution)/shard_map/ppermute | solution.py:418
  94.1 6.3 %collective-permute-start.22 = (bf16[192,384]{1,0:T(8,128)(2,1)S(1)}, bf16[192,384]{1,0:T(8,128)(2,1)S(1)}, u32[]{:S(2)}, u32[]{:S(2)}) collective-permute-start(bf16[192,384]{1,0:T(8,128)(2,1)S(1)} %pad_maximum_fusion), channel_id=1, source_target_pairs={{0,1},{1,0},{2,3},{3,2},{4,5},{5,4},{6,7},{7,6},{8,9},{9,8},{10,11... | collective-permute-start | bytes 442376 | tf_op jit(solution)/shard_map/ppermute | solution.py:211

commit v16 on v15

--- a/solution.py
+++ b/solution.py
@@ -299,10 +299,10 @@
         )
         order = [blocks[stage] for blocks in first_order + second_order]
         part = block_product(table, value, weight, order)
-        if stage == 0:
+        if stage == 1:
             part, after = lax.optimization_barrier((part, early))
             early_all = [early] + with_other_replicas(after)[1:]
-        if stage == min(2, count - 1):
+        if stage == count - 1:
             part, *early_all = lax.optimization_barrier((part, *early_all))
         parts.append(part)
         slot = stage + 1
@@ -358,7 +358,9 @@
     pulled_here = (gain_row * (sum(parts) + low_product)).astype(BF16)
     swap = [(0, 1), (1, 0)]
     pulled = lax.ppermute(pulled_here, "section", swap)
-    from_left, from_right, _ = lax.optimization_barrier((from_left, from_right, pulled_here))
+    from_left, from_right, *small_early_all, _ = lax.optimization_barrier(
+        (from_left, from_right, *small_early_all, pulled_here)
+    )
 
     projected = parts[-1] + from_left.astype(F32) + from_right.astype(F32) + low_product
     hidden = (token_float + inv_first * projected).astype(BF16)
@@ -381,9 +383,7 @@
     else:
         for step in doubling_steps():
             row_sums = sum_step(row_sums, step, F32)
-    row_sums, *small_early_all = lax.optimization_barrier((row_sums, *small_early_all))
     inv_second = lax.rsqrt(row_sums[0] / features + EPSILON)
-    inv_on_second = lax.ppermute(inv_second, "section", swap)[:, None]
     inv_second = inv_second[:, None]
     toward_hidden = row_sums[1][:, None] * inv_second * inv_second * inv_second / features
     hidden_grad = cotangent.astype(F32) + inv_second * pulled_float - toward_hidden * hidden_float
@@ -393,6 +393,9 @@
         (hidden_on_second.astype(F32) * gain_row).astype(BF16),
     )
     rank_late = jnp.where(is_first, times_up_transposed(late), times_down(late))
+    inv_on_second = lax.ppermute(
+        lax.optimization_barrier((inv_second[:, 0], rank_late))[0], "section", swap
+    )[:, None]
     for step in doubling_steps():
         rank_late = sum_step(rank_late, step)
 
@@ -415,7 +418,7 @@
         table, [], [early, late], [small_early_own, small_late], width, ranks, rows,
     )
     swapped = [
-        lax.ppermute(lax.optimization_barrier((other, *sums))[0], "section", swap)
+        lax.ppermute(lax.optimization_barrier((other, rank_late))[0], "section", swap)
         for other in late_others
     ]
     hidden_all = [hidden] + [jnp.where(is_first, *pair) for pair in zip(late_others, swapped)]

time: 107 us -> 106 us (level); the launches traced: 106 us -> 106 us
  waiting for transfers between devices: 23.4 us -> 26.1 us
  starting transfers between devices: 40 us -> 38.8 us
  Pallas kernels: 28.5 us -> 27.4 us
    ppermute x4, starting transfers between devices: 9.34 us -> 4.66 us  [with_other_replicas(): lax.ppermute(value, ('section', 'replica'), [(s * count + r, s * count +...]
    ppermute x8, waiting for transfers between devices: 5.4 us -> 0.73 us  [line(): return lax.ppermute(value, ('tensor', 'section'), pairs)]
    ppermute x4, waiting for transfers between devices: 5.84 us -> 10.1 us  [with_other_replicas(): lax.ppermute(value, ('section', 'replica'), [(s * count + r, s * count +...]
    ppermute x3, waiting for transfers between devices: 0.99 us -> 4.57 us  [on_device(): lax.ppermute(row_sums, 'tensor', [(z, (z + step) % count) for z in everyo...]
    ppermute x3, starting transfers between devices: 3.12 us -> 5.7 us  [on_device(): lax.ppermute(row_sums, 'tensor', [(z, (z + step) % count) for z in everyo...]
    pallas_call x2, Pallas kernels: 7.6 us -> 6.46 us  [gradient_call(): pl.pallas_call(kernel, grid_spec=pltpu.PrefetchScalarGridSpec(num_scalar_...]
  transfers between devices with their start and end apart: 23 -> 23, of which waited for: 11 -> 9; matrix products, arithmetic and copies ran while one was open for 10% -> 9% of each run, Pallas kernels for 22% -> 22%
where the time goes in v16:
time: 106 us
  starting transfers between devices  38.8 us (37%)
  Pallas kernels  27.4 us (26%)
  waiting for transfers between devices  26.1 us (25%)
  other arithmetic  9.29 us (9%)
  matrix products  2.96 us (3%)
  between operations  1.15 us (1%)
    pallas_call x4, Pallas kernels, block_product(): pl.pallas_call(functools.partial(block_kernel, blocks=blocks, tile=tile,...  20.9 us
    ppermute x8, starting transfers between devices, line(): return lax.ppermute(value, ('tensor', 'section'), pairs)  19.2 us
    ppermute x4, waiting for transfers between devices, sum_step(): other = lax.ppermute(value.astype(wire), 'tensor', pairs)  10.6 us
    ppermute x4, waiting for transfers between devices, with_other_replicas(): lax.ppermute(value, ('section', 'replica'), [(s * count + r, s * count +...  10.1 us
    ppermute x4, starting transfers between devices, sum_step(): other = lax.ppermute(value.astype(wire), 'tensor', pairs)  6.51 us
    pallas_call x2, Pallas kernels, gradient_call(): pl.pallas_call(kernel, grid_spec=pltpu.PrefetchScalarGridSpec(num_scalar_...  6.46 us
    ppermute x3, starting transfers between devices, on_device(): lax.ppermute(row_sums, 'tensor', [(z, (z + step) % count) for z in everyo...  5.7 us
    ppermute x4, starting transfers between devices, with_other_replicas(): lax.ppermute(value, ('section', 'replica'), [(s * count + r, s * count +...  4.66 us
  transfers between devices with their start and end apart: 23, of which 9 were waited for; matrix products, arithmetic and copies ran while one was open for 9% of the time, Pallas kernels for 22%

profile of v16, /device:TPU:0, one launch (start us, length us, event | category | flops | bytes accessed | tf_op | source)
XLA Modules:
  0.0 106.0 jit_solution(15702243419303975197)
XLA Ops:
  0.7 1.5 %fusion.17.value_ref.early = bf16[192,2048]{1,0:T(8,128)(2,1)S(1)} fusion(bf16[192,2048]{1,0:T(8,128)(2,1)} %param.9, bf16[192,2048]{1,0:T(8,128)(2,1)} %param.8, f32[2048]{0:T(1024)} %bitcast.38, pred[]{:T(512)S(6)} %eq.20), kind=kLoop, calls=%fused_computation.35 | loop fusion | flops 1572864 | bytes 2367489 | tf_op jit(solution)/shard_map/jit(_where)/select_n | solution.py:267
  2.1 1.6 %collective-permute-start = (bf16[192,2048]{1,0:T(8,128)(2,1)S(1)}, bf16[192,2048]{1,0:T(8,128)(2,1)}, u32[]{:S(2)}, u32[]{:S(2)}) collective-permute-start(bf16[192,2048]{1,0:T(8,128)(2,1)S(1)} %fusion.17.value_ref.early), channel_id=1, source_target_pairs={{2,6},{6,10},{10,14},{3,7},{7,11},{11,15},{18,22},{22,26},{26,30},... | collective-permute-start | bytes 2359304 | tf_op jit(solution)/shard_map/ppermute | solution.py:264
  3.8 1.6 %collective-permute-start.2 = (bf16[192,2048]{1,0:T(8,128)(2,1)S(1)}, bf16[192,2048]{1,0:T(8,128)(2,1)}, u32[]{:S(2)}, u32[]{:S(2)}) collective-permute-start(bf16[192,2048]{1,0:T(8,128)(2,1)S(1)} %fusion.17.value_ref.early), channel_id=1, source_target_pairs={{6,2},{10,6},{14,10},{7,3},{11,7},{15,11},{22,18},{26,22},{30,26},... | collective-permute-start | bytes 2359304 | tf_op jit(solution)/shard_map/ppermute | solution.py:264
  5.4 5.2 %shard_map.95 = f32[192,2048]{1,0:T(8,128)S(1)} custom-call(s32[2]{0:T(128)S(1)} %pad_add_fusion.table, bf16[192,2048]{1,0:T(8,128)(2,1)S(1)} %fusion.17.value_ref.early, bf16[2048,8192]{1,0:T(8,128)(2,1)} %bitcast.41), custom_call_target="tpu_custom_call" | custom-call | flops 6442450944 | bytes 8388608 | tf_op jit(solution)/shard_map/pallas_call | solution.py:72
  10.8 1.4 %add_convert_fusion.5 = bf16[192,2048]{1,0:T(8,128)(2,1)S(1)} fusion(bf16[192,2048]{1,0:T(8,128)(2,1)} %collective-permute-done, f32[192,2048]{1,0:T(8,128)S(1)} %shard_map.95, pred[]{:T(512)S(6)} %eq.20), kind=kLoop, calls=%fused_computation.22 | loop fusion | flops 1572864 | bytes 3145729 | tf_op jit(solution)/shard_map/convert_element_type | solution.py:324
  12.2 5.1 %collective-permute-start.1 = (bf16[192,2048]{1,0:T(8,128)(2,1)S(1)}, bf16[192,2048]{1,0:T(8,128)(2,1)S(1)}, u32[]{:S(2)}, u32[]{:S(2)}) collective-permute-start(bf16[192,2048]{1,0:T(8,128)(2,1)S(1)} %add_convert_fusion.5), channel_id=1, source_target_pairs={{0,4},{6,10},{10,14},{1,5},{7,11},{11,15},{16,20},{22,26},{26,30},... | collective-permute-start | bytes 2359304 | tf_op jit(solution)/shard_map/ppermute | solution.py:264
  17.3 1.3 %add_convert_fusion.4 = bf16[192,2048]{1,0:T(8,128)(2,1)S(1)} fusion(bf16[192,2048]{1,0:T(8,128)(2,1)} %collective-permute-done.2, f32[192,2048]{1,0:T(8,128)S(1)} %shard_map.95, pred[]{:T(512)S(6)} %eq.20), kind=kLoop, calls=%fused_computation.21 | loop fusion | flops 1572864 | bytes 3145729 | tf_op jit(solution)/shard_map/convert_element_type | solution.py:324
  20.7 5.2 %shard_map.96 = f32[192,2048]{1,0:T(8,128)S(1)} custom-call(s32[2]{0:T(128)S(1)} %pad_add_fusion.table, bf16[192,2048]{1,0:T(8,128)(2,1)S(1)} %select_select_fusion.2.value_ref, bf16[2048,8192]{1,0:T(8,128)(2,1)} %bitcast.42), custom_call_target="tpu_custom_call" | custom-call | flops 6442450944 | bytes 8388608 | tf_op jit(solution)/shard_map/pallas_call | solution.py:72
  26.1 1.6 %collective-permute-start.8 = (bf16[192,2048]{1,0:T(8,128)(2,1)S(1)}, bf16[192,2048]{1,0:T(8,128)(2,1)S(1)}, u32[]{:S(2)}, u32[]{:S(2)}) collective-permute-start(bf16[192,2048]{1,0:T(8,128)(2,1)S(1)} %fusion.17.value_ref.early), channel_id=1, source_target_pairs={{0,1},{1,0},{2,3},{3,2},{4,5},{5,4},{6,7},{7,6},{8,9},{9,8},{10,11... | collective-permute-start | bytes 2359304 | tf_op jit(solution)/shard_map/ppermute | solution.py:211
  28.0 3.9 %collective-permute-start.4 = (bf16[192,2048]{1,0:T(8,128)(2,1)S(1)}, bf16[192,2048]{1,0:T(8,128)(2,1)S(1)}, u32[]{:S(2)}, u32[]{:S(2)}) collective-permute-start(bf16[192,2048]{1,0:T(8,128)(2,1)S(1)} %add_convert_fusion.3), channel_id=1, source_target_pairs={{0,4},{4,8},{10,14},{1,5},{5,9},{11,15},{16,20},{20,24},{26,30},{1... | collective-permute-start | bytes 2359304 | tf_op jit(solution)/shard_map/ppermute | solution.py:264
  33.1 4.3 %collective-permute-start.7 = (bf16[208,256]{1,0:T(8,128)(2,1)S(1)}, bf16[208,256]{1,0:T(8,128)(2,1)S(1)}, u32[]{:S(2)}, u32[]{:S(2)}) collective-permute-start(bf16[208,256]{1,0:T(8,128)(2,1)S(1)} %convert_element_type.141), channel_id=1, source_target_pairs={{0,8},{4,12},{8,0},{12,4},{1,9},{5,13},{9,1},{13,5},{2,10},{6,14},... | collective-permute-start | bytes 319496 | tf_op jit(solution)/shard_map/ppermute | solution.py:202
  37.6 5.2 %shard_map.97 = f32[192,2048]{1,0:T(8,128)S(1)} custom-call(s32[2]{0:T(128)S(1)} %pad_add_fusion.table, bf16[192,2048]{1,0:T(8,128)(2,1)S(1)} %select_select_fusion.1.value_ref, bf16[2048,8192]{1,0:T(8,128)(2,1)} %bitcast.43), custom_call_target="tpu_custom_call" | custom-call | flops 6442450944 | bytes 8388608 | tf_op jit(solution)/shard_map/pallas_call | solution.py:72
  43.2 4.3 %collective-permute-start.9 = (bf16[192,2048]{1,0:T(8,128)(2,1)S(1)}, bf16[192,2048]{1,0:T(8,128)(2,1)S(1)}, u32[]{:S(2)}, u32[]{:S(2)}) collective-permute-start(bf16[192,2048]{1,0:T(8,128)(2,1)S(1)} %add_convert_fusion.1), channel_id=1, source_target_pairs={{0,4},{4,8},{8,12},{1,5},{5,9},{9,13},{16,20},{20,24},{24,28},{17,... | collective-permute-start | bytes 2359304 | tf_op jit(solution)/shard_map/ppermute | solution.py:264
  47.8 1.3 %collective-permute-start.10 = (bf16[192,2048]{1,0:T(8,128)(2,1)S(1)}, bf16[192,2048]{1,0:T(8,128)(2,1)S(1)}, u32[]{:S(2)}, u32[]{:S(2)}) collective-permute-start(bf16[192,2048]{1,0:T(8,128)(2,1)S(1)} %add_convert_fusion), channel_id=1, source_target_pairs={{4,0},{8,4},{12,8},{5,1},{9,5},{13,9},{20,16},{24,20},{28,24},{21,... | collective-permute-start | bytes 2359304 | tf_op jit(solution)/shard_map/ppermute | solution.py:264
  49.1 2.7 %collective-permute-done.7 = bf16[208,256]{1,0:T(8,128)(2,1)S(1)} collective-permute-done((bf16[208,256]{1,0:T(8,128)(2,1)S(1)}, bf16[208,256]{1,0:T(8,128)(2,1)S(1)}, u32[]{:S(2)}, u32[]{:S(2)}) %collective-permute-start.7) | collective-permute-done | bytes 106528 | tf_op jit(solution)/shard_map/ppermute | solution.py:202
  52.2 5.3 %shard_map.98 = f32[192,2048]{1,0:T(8,128)S(1)} custom-call(s32[2]{0:T(128)S(1)} %pad_add_fusion.table, bf16[192,2048]{1,0:T(8,128)(2,1)S(1)} %select_select_fusion.value_ref, bf16[2048,8192]{1,0:T(8,128)(2,1)} %bitcast.44), custom_call_target="tpu_custom_call" | custom-call | flops 6442450944 | bytes 8388608 | tf_op jit(solution)/shard_map/pallas_call | solution.py:72
  58.7 0.8 multiply_convert_fusion.1
  59.5 2.6 %collective-permute-start.12 = (bf16[192,2048]{1,0:T(8,128)(2,1)S(1)}, bf16[192,2048]{1,0:T(8,128)(2,1)S(1)}, u32[]{:S(2)}, u32[]{:S(2)}) collective-permute-start(bf16[192,2048]{1,0:T(8,128)(2,1)S(1)} %get-tuple-element.87), channel_id=1, source_target_pairs={{0,2},{2,0},{1,3},{3,1},{4,6},{6,4},{5,7},{7,5},{8,10},{10,8},{9,1... | collective-permute-start | bytes 2359304 | tf_op jit(solution)/shard_map/ppermute | solution.py:360
  62.6 0.7 collective-permute-done.10
  63.3 0.9 broadcast_select_fusion.1
  65.0 4.9 %collective-permute-start.15 = (f32[2,192]{1,0:T(2,128)S(1)}, f32[2,192]{1,0:T(2,128)S(1)}, u32[]{:S(2)}, u32[]{:S(2)}) collective-permute-start(f32[2,192]{1,0:T(2,128)S(1)} %pad_maximum_fusion.1), channel_id=1, source_target_pairs={{0,12},{4,0},{8,4},{12,8},{1,13},{5,1},{9,5},{13,9},{2,14},{6,2},{... | collective-permute-start | bytes 4616 | tf_op jit(solution)/shard_map/ppermute | solution.py:380
  69.9 0.8 collective-permute-start.14
  71.2 4.1 %collective-permute-done.13 = f32[2,192]{1,0:T(2,128)S(1)} collective-permute-done((f32[2,192]{1,0:T(2,128)S(1)}, f32[2,192]{1,0:T(2,128)S(1)}, u32[]{:S(2)}, u32[]{:S(2)}) %collective-permute-start.13) | collective-permute-done | bytes 1568 | tf_op jit(solution)/shard_map/ppermute | solution.py:380
  77.5 1.2 %collective-permute-start.20 = (bf16[192,2048]{1,0:T(8,128)(2,1)S(1)}, bf16[192,2048]{1,0:T(8,128)(2,1)S(1)}, u32[]{:S(2)}, u32[]{:S(2)}) collective-permute-start(bf16[192,2048]{1,0:T(8,128)(2,1)S(1)} %get-tuple-element.76), channel_id=1, source_target_pairs={{0,1},{1,0},{2,3},{3,2},{4,5},{5,4},{6,7},{7,6},{8,9},{9,8},{10,11... | collective-permute-start | bytes 2359304 | tf_op jit(solution)/shard_map/ppermute | solution.py:211
  78.7 2.8 %collective-permute-done.18 = bf16[192,256]{1,0:T(8,128)(2,1)S(1)} collective-permute-done((bf16[192,256]{1,0:T(8,128)(2,1)S(1)}, bf16[192,256]{1,0:T(8,128)(2,1)S(1)}, u32[]{:S(2)}, u32[]{:S(2)}) %collective-permute-start.18) | collective-permute-done | bytes 98336 | tf_op jit(solution)/shard_map/ppermute | solution.py:202
  81.5 1.5 %collective-permute-start.19 = (bf16[192,256]{1,0:T(8,128)(2,1)S(1)}, bf16[192,256]{1,0:T(8,128)(2,1)S(1)}, u32[]{:S(2)}, u32[]{:S(2)}) collective-permute-start(bf16[192,256]{1,0:T(8,128)(2,1)S(1)} %fusion.23), channel_id=1, source_target_pairs={{0,8},{4,12},{8,0},{12,4},{1,9},{5,13},{9,1},{13,5},{2,10},{6,14},... | collective-permute-start | bytes 294920 | tf_op jit(solution)/shard_map/ppermute | solution.py:202
  83.1 5.1 %collective-permute-done.19 = bf16[192,256]{1,0:T(8,128)(2,1)S(1)} collective-permute-done((bf16[192,256]{1,0:T(8,128)(2,1)S(1)}, bf16[192,256]{1,0:T(8,128)(2,1)S(1)}, u32[]{:S(2)}, u32[]{:S(2)}) %collective-permute-start.19) | collective-permute-done | bytes 98336 | tf_op jit(solution)/shard_map/ppermute | solution.py:202
  88.3 6.9 %collective-permute-done.20 = bf16[192,2048]{1,0:T(8,128)(2,1)S(1)} collective-permute-done((bf16[192,2048]{1,0:T(8,128)(2,1)S(1)}, bf16[192,2048]{1,0:T(8,128)(2,1)S(1)}, u32[]{:S(2)}, u32[]{:S(2)}) %collective-permute-start.20) | collective-permute-done | bytes 786464 | tf_op jit(solution)/shard_map/ppermute | solution.py:211
  95.5 1.3 %collective-permute-start.22 = (bf16[192,384]{1,0:T(8,128)(2,1)S(1)}, bf16[192,384]{1,0:T(8,128)(2,1)S(1)}, u32[]{:S(2)}, u32[]{:S(2)}) collective-permute-start(bf16[192,384]{1,0:T(8,128)(2,1)S(1)} %pad_maximum_fusion), channel_id=1, source_target_pairs={{0,1},{1,0},{2,3},{3,2},{4,5},{5,4},{6,7},{7,6},{8,9},{9,8},{10,11... | collective-permute-start | bytes 442376 | tf_op jit(solution)/shard_map/ppermute | solution.py:211
  96.8 2.3 %shard_map.99 = (f32[2048,256]{1,0:T(8,128)S(1)}, f32[256,2048]{1,0:T(8,128)S(1)}) custom-call(s32[2]{0:T(128)S(1)} %pad_add_fusion.table, bf16[192,2048]{1,0:T(8,128)(2,1)S(1)} %fusion.17.value_ref.early, bf16[192,2048]{1,0:T(8,128)(2,1)S(1)} %fusion.16.late, bf16[192,256]{1,0:T(8,128)(2,1)S(1)} %get-tuple-element.86.small_early, ...), custom_call_target="tpu_custom_call" | custom-call | flops 402653184 | bytes 5767168 | tf_op jit(solution)/shard_map/pallas_call | solution.py:145
  99.2 2.6 %collective-permute-done.22.small_late = bf16[192,384]{1,0:T(8,128)(2,1)S(1)} collective-permute-done((bf16[192,384]{1,0:T(8,128)(2,1)S(1)}, bf16[192,384]{1,0:T(8,128)(2,1)S(1)}, u32[]{:S(2)}, u32[]{:S(2)}) %collective-permute-start.22) | collective-permute-done | bytes 147488 | tf_op jit(solution)/shard_map/ppermute | solution.py:211
  101.9 4.2 %shard_map.100 = (f32[2048,256]{1,0:T(8,128)}, f32[256,2048]{1,0:T(8,128)}) custom-call(s32[2]{0:T(128)S(1)} %pad_add_fusion.table, f32[1,2048]{1,0:T(1,128)S(1)} %copy-done.1, f32[2048,256]{1,0:T(8,128)S(1)} %get-tuple-element.66.down_sum, f32[256,2048]{1,0:T(8,128)S(1)} %get-tuple-element.67.up_sum, bf16[192,2048]{1,0:T(8,128)(2,1)S(1)} %collective-permute-done.8.early, ...), custom_call_target="tpu_custom_call" | custom-call | flops 402653184 | bytes 11534336 | tf_op jit(solution)/shard_map/pallas_call | solution.py:145
  (81 shorter events, 10.7 us)
Async XLA Ops:
  0.6 19.6 %copy-start = (bf16[1,2048,256]{2,1,0:T(8,128)(2,1)S(1)}, bf16[1,2048,256]{2,1,0:T(8,128)(2,1)}, u32[]{:S(2)}) copy-start(bf16[1,2048,256]{2,1,0:T(8,128)(2,1)} %param.12) | copy-start | bytes 3145732
  2.1 8.6 %collective-permute-start = (bf16[192,2048]{1,0:T(8,128)(2,1)S(1)}, bf16[192,2048]{1,0:T(8,128)(2,1)}, u32[]{:S(2)}, u32[]{:S(2)}) collective-permute-start(bf16[192,2048]{1,0:T(8,128)(2,1)S(1)} %fusion.17.value_ref.early), channel_id=1, source_target_pairs={{2,6},{6,10},{10,14},{3,7},{7,11},{11,15},{18,22},{22,26},{26,30},... | collective-permute-start | bytes 2359304 | tf_op jit(solution)/shard_map/ppermute | solution.py:264
  3.8 13.6 %collective-permute-start.2 = (bf16[192,2048]{1,0:T(8,128)(2,1)S(1)}, bf16[192,2048]{1,0:T(8,128)(2,1)}, u32[]{:S(2)}, u32[]{:S(2)}) collective-permute-start(bf16[192,2048]{1,0:T(8,128)(2,1)S(1)} %fusion.17.value_ref.early), channel_id=1, source_target_pairs={{6,2},{10,6},{14,10},{7,3},{11,7},{15,11},{22,18},{26,22},{30,26},... | collective-permute-start | bytes 2359304 | tf_op jit(solution)/shard_map/ppermute | solution.py:264
  5.4 5.2 %copy-start.6 = (f32[4]{0:T(128)S(1)}, f32[4]{0:T(128)}, u32[]{:S(2)}) copy-start(f32[4]{0:T(128)} %param.14) | copy-start | bytes 52
  12.2 7.2 %copy-start.3 = (bf16[192,2048]{1,0:T(8,128)(2,1)S(1)}, bf16[192,2048]{1,0:T(8,128)(2,1)}, u32[]{:S(2)}) copy-start(bf16[192,2048]{1,0:T(8,128)(2,1)} %param.8) | copy-start | bytes 2359300
  12.2 7.5 %copy-start.2 = (bf16[1,256,2048]{2,1,0:T(8,128)(2,1)S(1)}, bf16[1,256,2048]{2,1,0:T(8,128)(2,1)}, u32[]{:S(2)}) copy-start(bf16[1,256,2048]{2,1,0:T(8,128)(2,1)} %param.13) | copy-start | bytes 3145732
  12.2 15.5 %collective-permute-start.1 = (bf16[192,2048]{1,0:T(8,128)(2,1)S(1)}, bf16[192,2048]{1,0:T(8,128)(2,1)S(1)}, u32[]{:S(2)}, u32[]{:S(2)}) collective-permute-start(bf16[192,2048]{1,0:T(8,128)(2,1)S(1)} %add_convert_fusion.5), channel_id=1, source_target_pairs={{0,4},{6,10},{10,14},{1,5},{7,11},{11,15},{16,20},{22,26},{26,30},... | collective-permute-start | bytes 2359304 | tf_op jit(solution)/shard_map/ppermute | solution.py:264
  18.7 13.3 %collective-permute-start.3 = (bf16[192,2048]{1,0:T(8,128)(2,1)S(1)}, bf16[192,2048]{1,0:T(8,128)(2,1)S(1)}, u32[]{:S(2)}, u32[]{:S(2)}) collective-permute-start(bf16[192,2048]{1,0:T(8,128)(2,1)S(1)} %add_convert_fusion.4), channel_id=1, source_target_pairs={{12,8},{6,2},{10,6},{13,9},{7,3},{11,7},{28,24},{22,18},{26,22},{2... | collective-permute-start | bytes 2359304 | tf_op jit(solution)/shard_map/ppermute | solution.py:264
  26.0 7.0 %collective-permute-start.6 = (bf16[208,256]{1,0:T(8,128)(2,1)S(1)}, bf16[208,256]{1,0:T(8,128)(2,1)S(1)}, u32[]{:S(2)}, u32[]{:S(2)}) collective-permute-start(bf16[208,256]{1,0:T(8,128)(2,1)S(1)} %convert_element_type.139), channel_id=1, source_target_pairs={{0,4},{4,0},{8,12},{12,8},{1,5},{5,1},{9,13},{13,9},{2,6},{6,2},{1... | collective-permute-start | bytes 319496 | tf_op jit(solution)/shard_map/ppermute | solution.py:202
  26.1 31.4 %collective-permute-start.8 = (bf16[192,2048]{1,0:T(8,128)(2,1)S(1)}, bf16[192,2048]{1,0:T(8,128)(2,1)S(1)}, u32[]{:S(2)}, u32[]{:S(2)}) collective-permute-start(bf16[192,2048]{1,0:T(8,128)(2,1)S(1)} %fusion.17.value_ref.early), channel_id=1, source_target_pairs={{0,1},{1,0},{2,3},{3,2},{4,5},{5,4},{6,7},{7,6},{8,9},{9,8},{10,11... | collective-permute-start | bytes 2359304 | tf_op jit(solution)/shard_map/ppermute | solution.py:211
  28.0 14.8 %collective-permute-start.4 = (bf16[192,2048]{1,0:T(8,128)(2,1)S(1)}, bf16[192,2048]{1,0:T(8,128)(2,1)S(1)}, u32[]{:S(2)}, u32[]{:S(2)}) collective-permute-start(bf16[192,2048]{1,0:T(8,128)(2,1)S(1)} %add_convert_fusion.3), channel_id=1, source_target_pairs={{0,4},{4,8},{10,14},{1,5},{5,9},{11,15},{16,20},{20,24},{26,30},{1... | collective-permute-start | bytes 2359304 | tf_op jit(solution)/shard_map/ppermute | solution.py:264
  32.3 15.2 %collective-permute-start.5 = (bf16[192,2048]{1,0:T(8,128)(2,1)S(1)}, bf16[192,2048]{1,0:T(8,128)(2,1)S(1)}, u32[]{:S(2)}, u32[]{:S(2)}) collective-permute-start(bf16[192,2048]{1,0:T(8,128)(2,1)S(1)} %add_convert_fusion.2), channel_id=1, source_target_pairs={{8,4},{12,8},{6,2},{9,5},{13,9},{7,3},{24,20},{28,24},{22,18},{25,... | collective-permute-start | bytes 2359304 | tf_op jit(solution)/shard_map/ppermute | solution.py:264
  33.1 18.7 %collective-permute-start.7 = (bf16[208,256]{1,0:T(8,128)(2,1)S(1)}, bf16[208,256]{1,0:T(8,128)(2,1)S(1)}, u32[]{:S(2)}, u32[]{:S(2)}) collective-permute-start(bf16[208,256]{1,0:T(8,128)(2,1)S(1)} %convert_element_type.141), channel_id=1, source_target_pairs={{0,8},{4,12},{8,0},{12,4},{1,9},{5,13},{9,1},{13,5},{2,10},{6,14},... | collective-permute-start | bytes 319496 | tf_op jit(solution)/shard_map/ppermute | solution.py:202
  43.2 19.3 %collective-permute-start.9 = (bf16[192,2048]{1,0:T(8,128)(2,1)S(1)}, bf16[192,2048]{1,0:T(8,128)(2,1)S(1)}, u32[]{:S(2)}, u32[]{:S(2)}) collective-permute-start(bf16[192,2048]{1,0:T(8,128)(2,1)S(1)} %add_convert_fusion.1), channel_id=1, source_target_pairs={{0,4},{4,8},{8,12},{1,5},{5,9},{9,13},{16,20},{20,24},{24,28},{17,... | collective-permute-start | bytes 2359304 | tf_op jit(solution)/shard_map/ppermute | solution.py:264
  47.8 15.5 %collective-permute-start.10 = (bf16[192,2048]{1,0:T(8,128)(2,1)S(1)}, bf16[192,2048]{1,0:T(8,128)(2,1)S(1)}, u32[]{:S(2)}, u32[]{:S(2)}) collective-permute-start(bf16[192,2048]{1,0:T(8,128)(2,1)S(1)} %add_convert_fusion), channel_id=1, source_target_pairs={{4,0},{8,4},{12,8},{5,1},{9,5},{13,9},{20,16},{24,20},{28,24},{21,... | collective-permute-start | bytes 2359304 | tf_op jit(solution)/shard_map/ppermute | solution.py:264
  52.2 5.3 %copy-start.5 = (s32[192]{0:T(256)S(1)}, s32[192]{0:T(256)}, u32[]{:S(2)}) copy-start(s32[192]{0:T(256)} %param.15) | copy-start | bytes 2308
  57.5 1.2 %copy-start.1 = (f32[1,2048]{1,0:T(1,128)S(1)}, f32[1,2048]{1,0:T(1,128)}, u32[]{:S(2)}) copy-start(f32[1,2048]{1,0:T(1,128)} %gain_ref.1) | copy-start | bytes 24580
  57.7 4.9 %collective-permute-start.11 = (bf16[192,256]{1,0:T(8,128)(2,1)S(1)}, bf16[192,256]{1,0:T(8,128)(2,1)S(1)}, u32[]{:S(2)}, u32[]{:S(2)}) collective-permute-start(bf16[192,256]{1,0:T(8,128)(2,1)S(1)} %get-tuple-element.80), channel_id=1, source_target_pairs={{0,1},{1,0},{2,3},{3,2},{4,5},{5,4},{6,7},{7,6},{8,9},{9,8},{10,11... | collective-permute-start | bytes 294920 | tf_op jit(solution)/shard_map/ppermute | solution.py:211
  59.5 5.1 %collective-permute-start.12 = (bf16[192,2048]{1,0:T(8,128)(2,1)S(1)}, bf16[192,2048]{1,0:T(8,128)(2,1)S(1)}, u32[]{:S(2)}, u32[]{:S(2)}) collective-permute-start(bf16[192,2048]{1,0:T(8,128)(2,1)S(1)} %get-tuple-element.87), channel_id=1, source_target_pairs={{0,2},{2,0},{1,3},{3,1},{4,6},{6,4},{5,7},{7,5},{8,10},{10,8},{9,1... | collective-permute-start | bytes 2359304 | tf_op jit(solution)/shard_map/ppermute | solution.py:360
  64.2 11.1 %copy-start.4 = (bf16[192,2048]{1,0:T(8,128)(2,1)S(1)}, bf16[192,2048]{1,0:T(8,128)(2,1)}, u32[]{:S(2)}) copy-start(bf16[192,2048]{1,0:T(8,128)(2,1)} %param.9) | copy-start | bytes 2359300
  64.4 10.9 %collective-permute-start.16 = (bf16[192,2048]{1,0:T(8,128)(2,1)S(1)}, bf16[192,2048]{1,0:T(8,128)(2,1)S(1)}, u32[]{:S(2)}, u32[]{:S(2)}) collective-permute-start(bf16[192,2048]{1,0:T(8,128)(2,1)S(1)} %broadcast_select_fusion.2), channel_id=1, source_target_pairs={{0,2},{2,0},{1,3},{3,1},{4,6},{6,4},{5,7},{7,5},{8,10},{10,8},{9,1... | collective-permute-start | bytes 2359304 | tf_op jit(solution)/shard_map/ppermute | solution.py:369
  65.0 6.2 %collective-permute-start.15 = (f32[2,192]{1,0:T(2,128)S(1)}, f32[2,192]{1,0:T(2,128)S(1)}, u32[]{:S(2)}, u32[]{:S(2)}) collective-permute-start(f32[2,192]{1,0:T(2,128)S(1)} %pad_maximum_fusion.1), channel_id=1, source_target_pairs={{0,12},{4,0},{8,4},{12,8},{1,13},{5,1},{9,5},{13,9},{2,14},{6,2},{... | collective-permute-start | bytes 4616 | tf_op jit(solution)/shard_map/ppermute | solution.py:380
  69.9 5.4 %collective-permute-start.13 = (f32[2,192]{1,0:T(2,128)S(1)}, f32[2,192]{1,0:T(2,128)S(1)}, u32[]{:S(2)}, u32[]{:S(2)}) collective-permute-start(f32[2,192]{1,0:T(2,128)S(1)} %pad_maximum_fusion.1), channel_id=1, source_target_pairs={{0,4},{4,8},{8,12},{12,0},{1,5},{5,9},{9,13},{13,1},{2,6},{6,10},{... | collective-permute-start | bytes 4616 | tf_op jit(solution)/shard_map/ppermute | solution.py:380
  69.9 5.4 %collective-permute-start.14 = (f32[2,192]{1,0:T(2,128)S(1)}, f32[2,192]{1,0:T(2,128)S(1)}, u32[]{:S(2)}, u32[]{:S(2)}) collective-permute-start(f32[2,192]{1,0:T(2,128)S(1)} %pad_maximum_fusion.1), channel_id=1, source_target_pairs={{0,8},{4,12},{8,0},{12,4},{1,9},{5,13},{9,1},{13,5},{2,10},{6,14},... | collective-permute-start | bytes 4616 | tf_op jit(solution)/shard_map/ppermute | solution.py:380
  76.8 4.7 %collective-permute-start.18 = (bf16[192,256]{1,0:T(8,128)(2,1)S(1)}, bf16[192,256]{1,0:T(8,128)(2,1)S(1)}, u32[]{:S(2)}, u32[]{:S(2)}) collective-permute-start(bf16[192,256]{1,0:T(8,128)(2,1)S(1)} %get-tuple-element.89), channel_id=1, source_target_pairs={{0,4},{4,0},{8,12},{12,8},{1,5},{5,1},{9,13},{13,9},{2,6},{6,2},{1... | collective-permute-start | bytes 294920 | tf_op jit(solution)/shard_map/ppermute | solution.py:202
  77.5 17.8 %collective-permute-start.20 = (bf16[192,2048]{1,0:T(8,128)(2,1)S(1)}, bf16[192,2048]{1,0:T(8,128)(2,1)S(1)}, u32[]{:S(2)}, u32[]{:S(2)}) collective-permute-start(bf16[192,2048]{1,0:T(8,128)(2,1)S(1)} %get-tuple-element.76), channel_id=1, source_target_pairs={{0,1},{1,0},{2,3},{3,2},{4,5},{5,4},{6,7},{7,6},{8,9},{9,8},{10,11... | collective-permute-start | bytes 2359304 | tf_op jit(solution)/shard_map/ppermute | solution.py:211
  78.7 4.4 %collective-permute-start.17 = (f32[192]{0:T(256)S(1)}, f32[192]{0:T(256)S(1)}, u32[]{:S(2)}, u32[]{:S(2)}) collective-permute-start(f32[192]{0:T(256)S(1)} %bitcast.47), channel_id=1, source_target_pairs={{0,2},{2,0},{1,3},{3,1},{4,6},{6,4},{5,7},{7,5},{8,10},{10,8},{9,1... | collective-permute-start | bytes 2312 | tf_op jit(solution)/shard_map/ppermute | solution.py:396
  81.5 6.6 %collective-permute-start.19 = (bf16[192,256]{1,0:T(8,128)(2,1)S(1)}, bf16[192,256]{1,0:T(8,128)(2,1)S(1)}, u32[]{:S(2)}, u32[]{:S(2)}) collective-permute-start(bf16[192,256]{1,0:T(8,128)(2,1)S(1)} %fusion.23), channel_id=1, source_target_pairs={{0,8},{4,12},{8,0},{12,4},{1,9},{5,13},{9,1},{13,5},{2,10},{6,14},... | collective-permute-start | bytes 294920 | tf_op jit(solution)/shard_map/ppermute | solution.py:202
  95.2 3.9 %collective-permute-start.21 = (bf16[192,2048]{1,0:T(8,128)(2,1)S(1)}, bf16[192,2048]{1,0:T(8,128)(2,1)S(1)}, u32[]{:S(2)}, u32[]{:S(2)}) collective-permute-start(bf16[192,2048]{1,0:T(8,128)(2,1)S(1)} %collective-permute-done.20), channel_id=1, source_target_pairs={{0,2},{2,0},{1,3},{3,1},{4,6},{6,4},{5,7},{7,5},{8,10},{10,8},{9,1... | collective-permute-start | bytes 2359304 | tf_op jit(solution)/shard_map/ppermute | solution.py:421
  95.5 6.3 %collective-permute-start.22 = (bf16[192,384]{1,0:T(8,128)(2,1)S(1)}, bf16[192,384]{1,0:T(8,128)(2,1)S(1)}, u32[]{:S(2)}, u32[]{:S(2)}) collective-permute-start(bf16[192,384]{1,0:T(8,128)(2,1)S(1)} %pad_maximum_fusion), channel_id=1, source_target_pairs={{0,1},{1,0},{2,3},{3,2},{4,5},{5,4},{6,7},{7,6},{8,9},{9,8},{10,11... | collective-permute-start | bytes 442376 | tf_op jit(solution)/shard_map/ppermute | solution.py:211

commit v17 on v16

--- a/solution.py
+++ b/solution.py
@@ -299,10 +299,10 @@
         )
         order = [blocks[stage] for blocks in first_order + second_order]
         part = block_product(table, value, weight, order)
-        if stage == 1:
+        if stage == 0:
             part, after = lax.optimization_barrier((part, early))
             early_all = [early] + with_other_replicas(after)[1:]
-        if stage == count - 1:
+        if stage == min(2, count - 1):
             part, *early_all = lax.optimization_barrier((part, *early_all))
         parts.append(part)
         slot = stage + 1

time: 106 us -> 108 us (1.019)
  Pallas kernels: 27.4 us -> 28.5 us
    ppermute x8, waiting for transfers between devices: 0.73 us -> 3.59 us  [line(): return lax.ppermute(value, ('tensor', 'section'), pairs)]
    ppermute x4, starting transfers between devices: 4.66 us -> 7.14 us  [with_other_replicas(): lax.ppermute(value, ('section', 'replica'), [(s * count + r, s * count +...]
    ppermute x4, waiting for transfers between devices: 10.6 us -> 8.16 us  [sum_step(): other = lax.ppermute(value.astype(wire), 'tensor', pairs)]
    pallas_call x2, Pallas kernels: 6.46 us -> 7.59 us  [gradient_call(): pl.pallas_call(kernel, grid_spec=pltpu.PrefetchScalarGridSpec(num_scalar_...]
    ppermute x4, starting transfers between devices: 6.51 us -> 5.42 us  [sum_step(): other = lax.ppermute(value.astype(wire), 'tensor', pairs)]
  transfers between devices with their start and end apart: 23 -> 23, of which waited for: 9 -> 11; matrix products, arithmetic and copies ran while one was open for 9% -> 9% of each run, Pallas kernels for 22% -> 22%
where the time goes in v17:
time: 108 us
  starting transfers between devices  39.5 us (37%)
  Pallas kernels  28.5 us (26%)
  waiting for transfers between devices  26.1 us (24%)
  other arithmetic  9.15 us (8%)
  matrix products  2.96 us (3%)
  between operations  1.14 us (1%)
    pallas_call x4, Pallas kernels, block_product(): pl.pallas_call(functools.partial(block_kernel, blocks=blocks, tile=tile,...  20.9 us
    ppermute x8, starting transfers between devices, line(): return lax.ppermute(value, ('tensor', 'section'), pairs)  18.4 us
    ppermute x4, waiting for transfers between devices, with_other_replicas(): lax.ppermute(value, ('section', 'replica'), [(s * count + r, s * count +...  9.74 us
    ppermute x4, waiting for transfers between devices, sum_step(): other = lax.ppermute(value.astype(wire), 'tensor', pairs)  8.16 us
    pallas_call x2, Pallas kernels, gradient_call(): pl.pallas_call(kernel, grid_spec=pltpu.PrefetchScalarGridSpec(num_scalar_...  7.59 us
    ppermute x4, starting transfers between devices, with_other_replicas(): lax.ppermute(value, ('section', 'replica'), [(s * count + r, s * count +...  7.14 us
    ppermute x4, starting transfers between devices, sum_step(): other = lax.ppermute(value.astype(wire), 'tensor', pairs)  5.42 us
    ppermute x3, starting transfers between devices, on_device(): lax.ppermute(row_sums, 'tensor', [(z, (z + step) % count) for z in everyo...  5.01 us
  transfers between devices with their start and end apart: 23, of which 11 were waited for; matrix products, arithmetic and copies ran while one was open for 9% of the time, Pallas kernels for 22%

profile of v17, /device:TPU:0, one launch (start us, length us, event | category | flops | bytes accessed | tf_op | source)
XLA Modules:
  0.0 107.8 jit_solution(7535694604248862249)
XLA Ops:
  0.7 1.5 %fusion.17.value_ref.early = bf16[192,2048]{1,0:T(8,128)(2,1)S(1)} fusion(bf16[192,2048]{1,0:T(8,128)(2,1)} %param.9, bf16[192,2048]{1,0:T(8,128)(2,1)} %param.8, f32[2048]{0:T(1024)} %bitcast.38, pred[]{:T(512)S(6)} %eq.20), kind=kLoop, calls=%fused_computation.35 | loop fusion | flops 1572864 | bytes 2367489 | tf_op jit(solution)/shard_map/jit(_where)/select_n | solution.py:267
  2.1 1.6 %collective-permute-start = (bf16[192,2048]{1,0:T(8,128)(2,1)S(1)}, bf16[192,2048]{1,0:T(8,128)(2,1)}, u32[]{:S(2)}, u32[]{:S(2)}) collective-permute-start(bf16[192,2048]{1,0:T(8,128)(2,1)S(1)} %fusion.17.value_ref.early), channel_id=1, source_target_pairs={{2,6},{6,10},{10,14},{3,7},{7,11},{11,15},{18,22},{22,26},{26,30},... | collective-permute-start | bytes 2359304 | tf_op jit(solution)/shard_map/ppermute | solution.py:264
  3.8 1.6 %collective-permute-start.2 = (bf16[192,2048]{1,0:T(8,128)(2,1)S(1)}, bf16[192,2048]{1,0:T(8,128)(2,1)}, u32[]{:S(2)}, u32[]{:S(2)}) collective-permute-start(bf16[192,2048]{1,0:T(8,128)(2,1)S(1)} %fusion.17.value_ref.early), channel_id=1, source_target_pairs={{6,2},{10,6},{14,10},{7,3},{11,7},{15,11},{22,18},{26,22},{30,26},... | collective-permute-start | bytes 2359304 | tf_op jit(solution)/shard_map/ppermute | solution.py:264
  5.4 5.2 %shard_map.95 = f32[192,2048]{1,0:T(8,128)S(1)} custom-call(s32[2]{0:T(128)S(1)} %pad_add_fusion.table, bf16[192,2048]{1,0:T(8,128)(2,1)S(1)} %fusion.17.value_ref.early, bf16[2048,8192]{1,0:T(8,128)(2,1)} %bitcast.41), custom_call_target="tpu_custom_call" | custom-call | flops 6442450944 | bytes 8388608 | tf_op jit(solution)/shard_map/pallas_call | solution.py:72
  10.6 3.0 %collective-permute-start.8 = (bf16[192,2048]{1,0:T(8,128)(2,1)S(1)}, bf16[192,2048]{1,0:T(8,128)(2,1)}, u32[]{:S(2)}, u32[]{:S(2)}) collective-permute-start(bf16[192,2048]{1,0:T(8,128)(2,1)S(1)} %fusion.17.value_ref.early), channel_id=1, source_target_pairs={{0,1},{1,0},{2,3},{3,2},{4,5},{5,4},{6,7},{7,6},{8,9},{9,8},{10,11... | collective-permute-start | bytes 2359304 | tf_op jit(solution)/shard_map/ppermute | solution.py:211
  13.8 1.3 %add_convert_fusion.5 = bf16[192,2048]{1,0:T(8,128)(2,1)S(1)} fusion(bf16[192,2048]{1,0:T(8,128)(2,1)} %collective-permute-done, f32[192,2048]{1,0:T(8,128)S(1)} %shard_map.95, pred[]{:T(512)S(6)} %eq.20), kind=kLoop, calls=%fused_computation.22 | loop fusion | flops 1572864 | bytes 3145729 | tf_op jit(solution)/shard_map/convert_element_type | solution.py:324
  15.1 3.7 %collective-permute-start.1 = (bf16[192,2048]{1,0:T(8,128)(2,1)S(1)}, bf16[192,2048]{1,0:T(8,128)(2,1)S(1)}, u32[]{:S(2)}, u32[]{:S(2)}) collective-permute-start(bf16[192,2048]{1,0:T(8,128)(2,1)S(1)} %add_convert_fusion.5), channel_id=1, source_target_pairs={{0,4},{6,10},{10,14},{1,5},{7,11},{11,15},{16,20},{22,26},{26,30},... | collective-permute-start | bytes 2359304 | tf_op jit(solution)/shard_map/ppermute | solution.py:264
  18.8 1.4 %add_convert_fusion.4 = bf16[192,2048]{1,0:T(8,128)(2,1)S(1)} fusion(bf16[192,2048]{1,0:T(8,128)(2,1)} %collective-permute-done.2, f32[192,2048]{1,0:T(8,128)S(1)} %shard_map.95, pred[]{:T(512)S(6)} %eq.20), kind=kLoop, calls=%fused_computation.21 | loop fusion | flops 1572864 | bytes 3145729 | tf_op jit(solution)/shard_map/convert_element_type | solution.py:324
  22.3 5.2 %shard_map.96 = f32[192,2048]{1,0:T(8,128)S(1)} custom-call(s32[2]{0:T(128)S(1)} %pad_add_fusion.table, bf16[192,2048]{1,0:T(8,128)(2,1)S(1)} %select_select_fusion.2.value_ref, bf16[2048,8192]{1,0:T(8,128)(2,1)} %bitcast.42), custom_call_target="tpu_custom_call" | custom-call | flops 6442450944 | bytes 8388608 | tf_op jit(solution)/shard_map/pallas_call | solution.py:72
  28.6 4.4 %collective-permute-start.4 = (bf16[192,2048]{1,0:T(8,128)(2,1)S(1)}, bf16[192,2048]{1,0:T(8,128)(2,1)S(1)}, u32[]{:S(2)}, u32[]{:S(2)}) collective-permute-start(bf16[192,2048]{1,0:T(8,128)(2,1)S(1)} %add_convert_fusion.3), channel_id=1, source_target_pairs={{0,4},{4,8},{10,14},{1,5},{5,9},{11,15},{16,20},{20,24},{26,30},{1... | collective-permute-start | bytes 2359304 | tf_op jit(solution)/shard_map/ppermute | solution.py:264
  34.2 3.2 %collective-permute-start.7 = (bf16[208,256]{1,0:T(8,128)(2,1)S(1)}, bf16[208,256]{1,0:T(8,128)(2,1)S(1)}, u32[]{:S(2)}, u32[]{:S(2)}) collective-permute-start(bf16[208,256]{1,0:T(8,128)(2,1)S(1)} %convert_element_type.141), channel_id=1, source_target_pairs={{0,8},{4,12},{8,0},{12,4},{1,9},{5,13},{9,1},{13,5},{2,10},{6,14},... | collective-permute-start | bytes 319496 | tf_op jit(solution)/shard_map/ppermute | solution.py:202
  37.7 5.2 %shard_map.97 = f32[192,2048]{1,0:T(8,128)S(1)} custom-call(s32[2]{0:T(128)S(1)} %pad_add_fusion.table, bf16[192,2048]{1,0:T(8,128)(2,1)S(1)} %select_select_fusion.1.value_ref, bf16[2048,8192]{1,0:T(8,128)(2,1)} %bitcast.43), custom_call_target="tpu_custom_call" | custom-call | flops 6442450944 | bytes 8388608 | tf_op jit(solution)/shard_map/pallas_call | solution.py:72
  42.9 1.9 %collective-permute-done.4 = bf16[192,2048]{1,0:T(8,128)(2,1)S(1)} collective-permute-done((bf16[192,2048]{1,0:T(8,128)(2,1)S(1)}, bf16[192,2048]{1,0:T(8,128)(2,1)S(1)}, u32[]{:S(2)}, u32[]{:S(2)}) %collective-permute-start.4) | collective-permute-done | bytes 786464 | tf_op jit(solution)/shard_map/ppermute | solution.py:264
  45.1 4.4 %collective-permute-start.9 = (bf16[192,2048]{1,0:T(8,128)(2,1)S(1)}, bf16[192,2048]{1,0:T(8,128)(2,1)S(1)}, u32[]{:S(2)}, u32[]{:S(2)}) collective-permute-start(bf16[192,2048]{1,0:T(8,128)(2,1)S(1)} %add_convert_fusion.1), channel_id=1, source_target_pairs={{0,4},{4,8},{8,12},{1,5},{5,9},{9,13},{16,20},{20,24},{24,28},{17,... | collective-permute-start | bytes 2359304 | tf_op jit(solution)/shard_map/ppermute | solution.py:264
  49.8 1.3 %collective-permute-start.10 = (bf16[192,2048]{1,0:T(8,128)(2,1)S(1)}, bf16[192,2048]{1,0:T(8,128)(2,1)S(1)}, u32[]{:S(2)}, u32[]{:S(2)}) collective-permute-start(bf16[192,2048]{1,0:T(8,128)(2,1)S(1)} %add_convert_fusion), channel_id=1, source_target_pairs={{4,0},{8,4},{12,8},{5,1},{9,5},{13,9},{20,16},{24,20},{28,24},{21,... | collective-permute-start | bytes 2359304 | tf_op jit(solution)/shard_map/ppermute | solution.py:264
  52.2 5.2 %shard_map.98 = f32[192,2048]{1,0:T(8,128)S(1)} custom-call(s32[2]{0:T(128)S(1)} %pad_add_fusion.table, bf16[192,2048]{1,0:T(8,128)(2,1)S(1)} %select_select_fusion.value_ref, bf16[2048,8192]{1,0:T(8,128)(2,1)} %bitcast.44), custom_call_target="tpu_custom_call" | custom-call | flops 6442450944 | bytes 8388608 | tf_op jit(solution)/shard_map/pallas_call | solution.py:72
  59.4 2.5 %collective-permute-start.12 = (bf16[192,2048]{1,0:T(8,128)(2,1)S(1)}, bf16[192,2048]{1,0:T(8,128)(2,1)S(1)}, u32[]{:S(2)}, u32[]{:S(2)}) collective-permute-start(bf16[192,2048]{1,0:T(8,128)(2,1)S(1)} %get-tuple-element.87), channel_id=1, source_target_pairs={{0,2},{2,0},{1,3},{3,1},{4,6},{6,4},{5,7},{7,5},{8,10},{10,8},{9,1... | collective-permute-start | bytes 2359304 | tf_op jit(solution)/shard_map/ppermute | solution.py:360
  62.6 1.1 %collective-permute-done.10 = bf16[192,2048]{1,0:T(8,128)(2,1)S(1)} collective-permute-done((bf16[192,2048]{1,0:T(8,128)(2,1)S(1)}, bf16[192,2048]{1,0:T(8,128)(2,1)S(1)}, u32[]{:S(2)}, u32[]{:S(2)}) %collective-permute-start.10) | collective-permute-done | bytes 786464 | tf_op jit(solution)/shard_map/ppermute | solution.py:264
  63.7 0.9 broadcast_select_fusion.1
  64.8 1.1 collective-permute-start.16
  66.2 4.2 %collective-permute-start.15 = (f32[2,192]{1,0:T(2,128)S(1)}, f32[2,192]{1,0:T(2,128)S(1)}, u32[]{:S(2)}, u32[]{:S(2)}) collective-permute-start(f32[2,192]{1,0:T(2,128)S(1)} %pad_maximum_fusion.1), channel_id=1, source_target_pairs={{0,12},{4,0},{8,4},{12,8},{1,13},{5,1},{9,5},{13,9},{2,14},{6,2},{... | collective-permute-start | bytes 4616 | tf_op jit(solution)/shard_map/ppermute | solution.py:380
  70.4 0.8 collective-permute-start.14
  71.7 4.1 %collective-permute-done.13 = f32[2,192]{1,0:T(2,128)S(1)} collective-permute-done((f32[2,192]{1,0:T(2,128)S(1)}, f32[2,192]{1,0:T(2,128)S(1)}, u32[]{:S(2)}, u32[]{:S(2)}) %collective-permute-start.13) | collective-permute-done | bytes 1568 | tf_op jit(solution)/shard_map/ppermute | solution.py:380
  78.1 1.7 %collective-permute-start.20 = (bf16[192,2048]{1,0:T(8,128)(2,1)S(1)}, bf16[192,2048]{1,0:T(8,128)(2,1)S(1)}, u32[]{:S(2)}, u32[]{:S(2)}) collective-permute-start(bf16[192,2048]{1,0:T(8,128)(2,1)S(1)} %get-tuple-element.76), channel_id=1, source_target_pairs={{0,1},{1,0},{2,3},{3,2},{4,5},{5,4},{6,7},{7,6},{8,9},{9,8},{10,11... | collective-permute-start | bytes 2359304 | tf_op jit(solution)/shard_map/ppermute | solution.py:211
  79.8 2.3 %collective-permute-done.18 = bf16[192,256]{1,0:T(8,128)(2,1)S(1)} collective-permute-done((bf16[192,256]{1,0:T(8,128)(2,1)S(1)}, bf16[192,256]{1,0:T(8,128)(2,1)S(1)}, u32[]{:S(2)}, u32[]{:S(2)}) %collective-permute-start.18) | collective-permute-done | bytes 98336 | tf_op jit(solution)/shard_map/ppermute | solution.py:202
  82.1 1.5 %collective-permute-start.19 = (bf16[192,256]{1,0:T(8,128)(2,1)S(1)}, bf16[192,256]{1,0:T(8,128)(2,1)S(1)}, u32[]{:S(2)}, u32[]{:S(2)}) collective-permute-start(bf16[192,256]{1,0:T(8,128)(2,1)S(1)} %fusion.23), channel_id=1, source_target_pairs={{0,8},{4,12},{8,0},{12,4},{1,9},{5,13},{9,1},{13,5},{2,10},{6,14},... | collective-permute-start | bytes 294920 | tf_op jit(solution)/shard_map/ppermute | solution.py:202
  83.7 5.1 %collective-permute-done.19 = bf16[192,256]{1,0:T(8,128)(2,1)S(1)} collective-permute-done((bf16[192,256]{1,0:T(8,128)(2,1)S(1)}, bf16[192,256]{1,0:T(8,128)(2,1)S(1)}, u32[]{:S(2)}, u32[]{:S(2)}) %collective-permute-start.19) | collective-permute-done | bytes 98336 | tf_op jit(solution)/shard_map/ppermute | solution.py:202
  88.9 6.9 %collective-permute-done.20 = bf16[192,2048]{1,0:T(8,128)(2,1)S(1)} collective-permute-done((bf16[192,2048]{1,0:T(8,128)(2,1)S(1)}, bf16[192,2048]{1,0:T(8,128)(2,1)S(1)}, u32[]{:S(2)}, u32[]{:S(2)}) %collective-permute-start.20) | collective-permute-done | bytes 786464 | tf_op jit(solution)/shard_map/ppermute | solution.py:211
  96.1 1.8 %collective-permute-start.22 = (bf16[192,384]{1,0:T(8,128)(2,1)S(1)}, bf16[192,384]{1,0:T(8,128)(2,1)S(1)}, u32[]{:S(2)}, u32[]{:S(2)}) collective-permute-start(bf16[192,384]{1,0:T(8,128)(2,1)S(1)} %pad_maximum_fusion), channel_id=1, source_target_pairs={{0,1},{1,0},{2,3},{3,2},{4,5},{5,4},{6,7},{7,6},{8,9},{9,8},{10,11... | collective-permute-start | bytes 442376 | tf_op jit(solution)/shard_map/ppermute | solution.py:211
  97.9 2.3 %shard_map.99 = (f32[2048,256]{1,0:T(8,128)S(1)}, f32[256,2048]{1,0:T(8,128)S(1)}) custom-call(s32[2]{0:T(128)S(1)} %pad_add_fusion.table, bf16[192,2048]{1,0:T(8,128)(2,1)S(1)} %fusion.17.value_ref.early, bf16[192,2048]{1,0:T(8,128)(2,1)S(1)} %fusion.16.late, bf16[192,256]{1,0:T(8,128)(2,1)S(1)} %get-tuple-element.86.small_early, ...), custom_call_target="tpu_custom_call" | custom-call | flops 402653184 | bytes 5767168 | tf_op jit(solution)/shard_map/pallas_call | solution.py:145
  100.3 2.1 %collective-permute-done.22.small_late = bf16[192,384]{1,0:T(8,128)(2,1)S(1)} collective-permute-done((bf16[192,384]{1,0:T(8,128)(2,1)S(1)}, bf16[192,384]{1,0:T(8,128)(2,1)S(1)}, u32[]{:S(2)}, u32[]{:S(2)}) %collective-permute-start.22) | collective-permute-done | bytes 147488 | tf_op jit(solution)/shard_map/ppermute | solution.py:211
  102.4 5.3 %shard_map.100 = (f32[2048,256]{1,0:T(8,128)}, f32[256,2048]{1,0:T(8,128)}) custom-call(s32[2]{0:T(128)S(1)} %pad_add_fusion.table, f32[1,2048]{1,0:T(1,128)S(1)} %copy-done.1, f32[2048,256]{1,0:T(8,128)S(1)} %get-tuple-element.66.down_sum, f32[256,2048]{1,0:T(8,128)S(1)} %get-tuple-element.67.up_sum, bf16[192,2048]{1,0:T(8,128)(2,1)} %collective-permute-done.8.early, ...), custom_call_target="tpu_custom_call" | custom-call | flops 402653184 | bytes 11534336 | tf_op jit(solution)/shard_map/pallas_call | solution.py:145
  (81 shorter events, 12.7 us)
Async XLA Ops:
  0.6 21.1 %copy-start = (bf16[1,2048,256]{2,1,0:T(8,128)(2,1)S(1)}, bf16[1,2048,256]{2,1,0:T(8,128)(2,1)}, u32[]{:S(2)}) copy-start(bf16[1,2048,256]{2,1,0:T(8,128)(2,1)} %param.12) | copy-start | bytes 3145732
  2.1 11.6 %collective-permute-start = (bf16[192,2048]{1,0:T(8,128)(2,1)S(1)}, bf16[192,2048]{1,0:T(8,128)(2,1)}, u32[]{:S(2)}, u32[]{:S(2)}) collective-permute-start(bf16[192,2048]{1,0:T(8,128)(2,1)S(1)} %fusion.17.value_ref.early), channel_id=1, source_target_pairs={{2,6},{6,10},{10,14},{3,7},{7,11},{11,15},{18,22},{22,26},{26,30},... | collective-permute-start | bytes 2359304 | tf_op jit(solution)/shard_map/ppermute | solution.py:264
  3.8 15.1 %collective-permute-start.2 = (bf16[192,2048]{1,0:T(8,128)(2,1)S(1)}, bf16[192,2048]{1,0:T(8,128)(2,1)}, u32[]{:S(2)}, u32[]{:S(2)}) collective-permute-start(bf16[192,2048]{1,0:T(8,128)(2,1)S(1)} %fusion.17.value_ref.early), channel_id=1, source_target_pairs={{6,2},{10,6},{14,10},{7,3},{11,7},{15,11},{22,18},{26,22},{30,26},... | collective-permute-start | bytes 2359304 | tf_op jit(solution)/shard_map/ppermute | solution.py:264
  5.4 8.2 %copy-start.6 = (f32[4]{0:T(128)S(1)}, f32[4]{0:T(128)}, u32[]{:S(2)}) copy-start(f32[4]{0:T(128)} %param.14) | copy-start | bytes 52
  10.6 32.3 %collective-permute-start.8 = (bf16[192,2048]{1,0:T(8,128)(2,1)S(1)}, bf16[192,2048]{1,0:T(8,128)(2,1)}, u32[]{:S(2)}, u32[]{:S(2)}) collective-permute-start(bf16[192,2048]{1,0:T(8,128)(2,1)S(1)} %fusion.17.value_ref.early), channel_id=1, source_target_pairs={{0,1},{1,0},{2,3},{3,2},{4,5},{5,4},{6,7},{7,6},{8,9},{9,8},{10,11... | collective-permute-start | bytes 2359304 | tf_op jit(solution)/shard_map/ppermute | solution.py:211
  15.1 5.8 %copy-start.3 = (bf16[192,2048]{1,0:T(8,128)(2,1)S(1)}, bf16[192,2048]{1,0:T(8,128)(2,1)}, u32[]{:S(2)}) copy-start(bf16[192,2048]{1,0:T(8,128)(2,1)} %param.8) | copy-start | bytes 2359300
  15.1 6.1 %copy-start.2 = (bf16[1,256,2048]{2,1,0:T(8,128)(2,1)S(1)}, bf16[1,256,2048]{2,1,0:T(8,128)(2,1)}, u32[]{:S(2)}) copy-start(bf16[1,256,2048]{2,1,0:T(8,128)(2,1)} %param.13) | copy-start | bytes 3145732
  15.1 13.1 %collective-permute-start.1 = (bf16[192,2048]{1,0:T(8,128)(2,1)S(1)}, bf16[192,2048]{1,0:T(8,128)(2,1)S(1)}, u32[]{:S(2)}, u32[]{:S(2)}) collective-permute-start(bf16[192,2048]{1,0:T(8,128)(2,1)S(1)} %add_convert_fusion.5), channel_id=1, source_target_pairs={{0,4},{6,10},{10,14},{1,5},{7,11},{11,15},{16,20},{22,26},{26,30},... | collective-permute-start | bytes 2359304 | tf_op jit(solution)/shard_map/ppermute | solution.py:264
  20.2 12.9 %collective-permute-start.3 = (bf16[192,2048]{1,0:T(8,128)(2,1)S(1)}, bf16[192,2048]{1,0:T(8,128)(2,1)S(1)}, u32[]{:S(2)}, u32[]{:S(2)}) collective-permute-start(bf16[192,2048]{1,0:T(8,128)(2,1)S(1)} %add_convert_fusion.4), channel_id=1, source_target_pairs={{12,8},{6,2},{10,6},{13,9},{7,3},{11,7},{28,24},{22,18},{26,22},{2... | collective-permute-start | bytes 2359304 | tf_op jit(solution)/shard_map/ppermute | solution.py:264
  27.5 6.6 %collective-permute-start.6 = (bf16[208,256]{1,0:T(8,128)(2,1)S(1)}, bf16[208,256]{1,0:T(8,128)(2,1)S(1)}, u32[]{:S(2)}, u32[]{:S(2)}) collective-permute-start(bf16[208,256]{1,0:T(8,128)(2,1)S(1)} %convert_element_type.139), channel_id=1, source_target_pairs={{0,4},{4,0},{8,12},{12,8},{1,5},{5,1},{9,13},{13,9},{2,6},{6,2},{1... | collective-permute-start | bytes 319496 | tf_op jit(solution)/shard_map/ppermute | solution.py:202
  28.6 16.2 %collective-permute-start.4 = (bf16[192,2048]{1,0:T(8,128)(2,1)S(1)}, bf16[192,2048]{1,0:T(8,128)(2,1)S(1)}, u32[]{:S(2)}, u32[]{:S(2)}) collective-permute-start(bf16[192,2048]{1,0:T(8,128)(2,1)S(1)} %add_convert_fusion.3), channel_id=1, source_target_pairs={{0,4},{4,8},{10,14},{1,5},{5,9},{11,15},{16,20},{20,24},{26,30},{1... | collective-permute-start | bytes 2359304 | tf_op jit(solution)/shard_map/ppermute | solution.py:264
  33.5 16.1 %collective-permute-start.5 = (bf16[192,2048]{1,0:T(8,128)(2,1)S(1)}, bf16[192,2048]{1,0:T(8,128)(2,1)S(1)}, u32[]{:S(2)}, u32[]{:S(2)}) collective-permute-start(bf16[192,2048]{1,0:T(8,128)(2,1)S(1)} %add_convert_fusion.2), channel_id=1, source_target_pairs={{8,4},{12,8},{6,2},{9,5},{13,9},{7,3},{24,20},{28,24},{22,18},{25,... | collective-permute-start | bytes 2359304 | tf_op jit(solution)/shard_map/ppermute | solution.py:264
  34.2 17.7 %collective-permute-start.7 = (bf16[208,256]{1,0:T(8,128)(2,1)S(1)}, bf16[208,256]{1,0:T(8,128)(2,1)S(1)}, u32[]{:S(2)}, u32[]{:S(2)}) collective-permute-start(bf16[208,256]{1,0:T(8,128)(2,1)S(1)} %convert_element_type.141), channel_id=1, source_target_pairs={{0,8},{4,12},{8,0},{12,4},{1,9},{5,13},{9,1},{13,5},{2,10},{6,14},... | collective-permute-start | bytes 319496 | tf_op jit(solution)/shard_map/ppermute | solution.py:202
  45.1 17.5 %collective-permute-start.9 = (bf16[192,2048]{1,0:T(8,128)(2,1)S(1)}, bf16[192,2048]{1,0:T(8,128)(2,1)S(1)}, u32[]{:S(2)}, u32[]{:S(2)}) collective-permute-start(bf16[192,2048]{1,0:T(8,128)(2,1)S(1)} %add_convert_fusion.1), channel_id=1, source_target_pairs={{0,4},{4,8},{8,12},{1,5},{5,9},{9,13},{16,20},{20,24},{24,28},{17,... | collective-permute-start | bytes 2359304 | tf_op jit(solution)/shard_map/ppermute | solution.py:264
  49.8 13.9 %collective-permute-start.10 = (bf16[192,2048]{1,0:T(8,128)(2,1)S(1)}, bf16[192,2048]{1,0:T(8,128)(2,1)S(1)}, u32[]{:S(2)}, u32[]{:S(2)}) collective-permute-start(bf16[192,2048]{1,0:T(8,128)(2,1)S(1)} %add_convert_fusion), channel_id=1, source_target_pairs={{4,0},{8,4},{12,8},{5,1},{9,5},{13,9},{20,16},{24,20},{28,24},{21,... | collective-permute-start | bytes 2359304 | tf_op jit(solution)/shard_map/ppermute | solution.py:264
  52.2 5.3 %copy-start.5 = (s32[192]{0:T(256)S(1)}, s32[192]{0:T(256)}, u32[]{:S(2)}) copy-start(s32[192]{0:T(256)} %param.15) | copy-start | bytes 2308
  57.5 1.2 %copy-start.1 = (f32[1,2048]{1,0:T(1,128)S(1)}, f32[1,2048]{1,0:T(1,128)}, u32[]{:S(2)}) copy-start(f32[1,2048]{1,0:T(1,128)} %gain_ref.1) | copy-start | bytes 24580
  57.6 5.0 %collective-permute-start.11 = (bf16[192,256]{1,0:T(8,128)(2,1)S(1)}, bf16[192,256]{1,0:T(8,128)(2,1)S(1)}, u32[]{:S(2)}, u32[]{:S(2)}) collective-permute-start(bf16[192,256]{1,0:T(8,128)(2,1)S(1)} %get-tuple-element.80), channel_id=1, source_target_pairs={{0,1},{1,0},{2,3},{3,2},{4,5},{5,4},{6,7},{7,6},{8,9},{9,8},{10,11... | collective-permute-start | bytes 294920 | tf_op jit(solution)/shard_map/ppermute | solution.py:211
  59.4 6.4 %collective-permute-start.12 = (bf16[192,2048]{1,0:T(8,128)(2,1)S(1)}, bf16[192,2048]{1,0:T(8,128)(2,1)S(1)}, u32[]{:S(2)}, u32[]{:S(2)}) collective-permute-start(bf16[192,2048]{1,0:T(8,128)(2,1)S(1)} %get-tuple-element.87), channel_id=1, source_target_pairs={{0,2},{2,0},{1,3},{3,1},{4,6},{6,4},{5,7},{7,5},{8,10},{10,8},{9,1... | collective-permute-start | bytes 2359304 | tf_op jit(solution)/shard_map/ppermute | solution.py:360
  64.7 11.2 %copy-start.4 = (bf16[192,2048]{1,0:T(8,128)(2,1)S(1)}, bf16[192,2048]{1,0:T(8,128)(2,1)}, u32[]{:S(2)}) copy-start(bf16[192,2048]{1,0:T(8,128)(2,1)} %param.9) | copy-start | bytes 2359300
  64.8 11.1 %collective-permute-start.16 = (bf16[192,2048]{1,0:T(8,128)(2,1)S(1)}, bf16[192,2048]{1,0:T(8,128)(2,1)S(1)}, u32[]{:S(2)}, u32[]{:S(2)}) collective-permute-start(bf16[192,2048]{1,0:T(8,128)(2,1)S(1)} %broadcast_select_fusion.2), channel_id=1, source_target_pairs={{0,2},{2,0},{1,3},{3,1},{4,6},{6,4},{5,7},{7,5},{8,10},{10,8},{9,1... | collective-permute-start | bytes 2359304 | tf_op jit(solution)/shard_map/ppermute | solution.py:369
  66.2 5.5 %collective-permute-start.15 = (f32[2,192]{1,0:T(2,128)S(1)}, f32[2,192]{1,0:T(2,128)S(1)}, u32[]{:S(2)}, u32[]{:S(2)}) collective-permute-start(f32[2,192]{1,0:T(2,128)S(1)} %pad_maximum_fusion.1), channel_id=1, source_target_pairs={{0,12},{4,0},{8,4},{12,8},{1,13},{5,1},{9,5},{13,9},{2,14},{6,2},{... | collective-permute-start | bytes 4616 | tf_op jit(solution)/shard_map/ppermute | solution.py:380
  70.4 5.4 %collective-permute-start.13 = (f32[2,192]{1,0:T(2,128)S(1)}, f32[2,192]{1,0:T(2,128)S(1)}, u32[]{:S(2)}, u32[]{:S(2)}) collective-permute-start(f32[2,192]{1,0:T(2,128)S(1)} %pad_maximum_fusion.1), channel_id=1, source_target_pairs={{0,4},{4,8},{8,12},{12,0},{1,5},{5,9},{9,13},{13,1},{2,6},{6,10},{... | collective-permute-start | bytes 4616 | tf_op jit(solution)/shard_map/ppermute | solution.py:380
  70.4 5.4 %collective-permute-start.14 = (f32[2,192]{1,0:T(2,128)S(1)}, f32[2,192]{1,0:T(2,128)S(1)}, u32[]{:S(2)}, u32[]{:S(2)}) collective-permute-start(f32[2,192]{1,0:T(2,128)S(1)} %pad_maximum_fusion.1), channel_id=1, source_target_pairs={{0,8},{4,12},{8,0},{12,4},{1,9},{5,13},{9,1},{13,5},{2,10},{6,14},... | collective-permute-start | bytes 4616 | tf_op jit(solution)/shard_map/ppermute | solution.py:380
  77.4 4.7 %collective-permute-start.18 = (bf16[192,256]{1,0:T(8,128)(2,1)S(1)}, bf16[192,256]{1,0:T(8,128)(2,1)S(1)}, u32[]{:S(2)}, u32[]{:S(2)}) collective-permute-start(bf16[192,256]{1,0:T(8,128)(2,1)S(1)} %get-tuple-element.89), channel_id=1, source_target_pairs={{0,4},{4,0},{8,12},{12,8},{1,5},{5,1},{9,13},{13,9},{2,6},{6,2},{1... | collective-permute-start | bytes 294920 | tf_op jit(solution)/shard_map/ppermute | solution.py:202
  78.1 17.8 %collective-permute-start.20 = (bf16[192,2048]{1,0:T(8,128)(2,1)S(1)}, bf16[192,2048]{1,0:T(8,128)(2,1)S(1)}, u32[]{:S(2)}, u32[]{:S(2)}) collective-permute-start(bf16[192,2048]{1,0:T(8,128)(2,1)S(1)} %get-tuple-element.76), channel_id=1, source_target_pairs={{0,1},{1,0},{2,3},{3,2},{4,5},{5,4},{6,7},{7,6},{8,9},{9,8},{10,11... | collective-permute-start | bytes 2359304 | tf_op jit(solution)/shard_map/ppermute | solution.py:211
  79.8 3.9 %collective-permute-start.17 = (f32[192]{0:T(256)S(1)}, f32[192]{0:T(256)S(1)}, u32[]{:S(2)}, u32[]{:S(2)}) collective-permute-start(f32[192]{0:T(256)S(1)} %bitcast.47), channel_id=1, source_target_pairs={{0,2},{2,0},{1,3},{3,1},{4,6},{6,4},{5,7},{7,5},{8,10},{10,8},{9,1... | collective-permute-start | bytes 2312 | tf_op jit(solution)/shard_map/ppermute | solution.py:396
  82.1 6.6 %collective-permute-start.19 = (bf16[192,256]{1,0:T(8,128)(2,1)S(1)}, bf16[192,256]{1,0:T(8,128)(2,1)S(1)}, u32[]{:S(2)}, u32[]{:S(2)}) collective-permute-start(bf16[192,256]{1,0:T(8,128)(2,1)S(1)} %fusion.23), channel_id=1, source_target_pairs={{0,8},{4,12},{8,0},{12,4},{1,9},{5,13},{9,1},{13,5},{2,10},{6,14},... | collective-permute-start | bytes 294920 | tf_op jit(solution)/shard_map/ppermute | solution.py:202
  95.8 4.4 %collective-permute-start.21 = (bf16[192,2048]{1,0:T(8,128)(2,1)S(1)}, bf16[192,2048]{1,0:T(8,128)(2,1)S(1)}, u32[]{:S(2)}, u32[]{:S(2)}) collective-permute-start(bf16[192,2048]{1,0:T(8,128)(2,1)S(1)} %collective-permute-done.20), channel_id=1, source_target_pairs={{0,2},{2,0},{1,3},{3,1},{4,6},{6,4},{5,7},{7,5},{8,10},{10,8},{9,1... | collective-permute-start | bytes 2359304 | tf_op jit(solution)/shard_map/ppermute | solution.py:421
  96.1 6.3 %collective-permute-start.22 = (bf16[192,384]{1,0:T(8,128)(2,1)S(1)}, bf16[192,384]{1,0:T(8,128)(2,1)S(1)}, u32[]{:S(2)}, u32[]{:S(2)}) collective-permute-start(bf16[192,384]{1,0:T(8,128)(2,1)S(1)} %pad_maximum_fusion), channel_id=1, source_target_pairs={{0,1},{1,0},{2,3},{3,2},{4,5},{5,4},{6,7},{7,6},{8,9},{9,8},{10,11... | collective-permute-start | bytes 442376 | tf_op jit(solution)/shard_map/ppermute | solution.py:211

commit v18 on v16

--- a/solution.py
+++ b/solution.py
@@ -277,8 +277,12 @@
     steps_left = doubling_steps()
     arrivals = [
         (
-            line(early, [], [z for z in everyone if z + 1 < count], 1),
-            line(early, [], [z for z in everyone if z > 0], -1),
+            lax.ppermute(
+                cotangent,
+                ("tensor", "section"),
+                [(2 * z, 2 * (z + 1) + 1) for z in everyone if z + 1 < count],
+            ),
+            line(cotangent, [], [z for z in everyone if z > 0], -1),
         )
     ]
     parts = []
@@ -364,7 +368,10 @@
 
     projected = parts[-1] + from_left.astype(F32) + from_right.astype(F32) + low_product
     hidden = (token_float + inv_first * projected).astype(BF16)
-    late_others = with_other_replicas(jnp.where(is_first, hidden, pulled_here))[1:]
+    half = width // 2 if width % 256 == 0 else width
+    exchanged = jnp.where(is_first, hidden, pulled_here)
+    first_halves = with_other_replicas(exchanged[:, :half])[1:]
+    second_halves = with_other_replicas(exchanged[:, half:])[1:] if half < width else None
     swapped = [
         lax.ppermute(jnp.where(is_first, hidden, other), "section", swap) for other in early_all[1:]
     ]
@@ -383,6 +390,7 @@
     else:
         for step in doubling_steps():
             row_sums = sum_step(row_sums, step, F32)
+    row_sums, *first_halves = lax.optimization_barrier((row_sums, *first_halves))
     inv_second = lax.rsqrt(row_sums[0] / features + EPSILON)
     inv_second = inv_second[:, None]
     toward_hidden = row_sums[1][:, None] * inv_second * inv_second * inv_second / features
@@ -399,6 +407,12 @@
     for step in doubling_steps():
         rank_late = sum_step(rank_late, step)
 
+    late_others = first_halves
+    if second_halves is not None:
+        *second_halves, _ = lax.optimization_barrier((*second_halves, rank_late))
+        late_others = [
+            jnp.concatenate(halves, axis=1) for halves in zip(first_halves, second_halves)
+        ]
     inv_second = jnp.where(is_first, inv_second, inv_on_second)
     row_scale = jnp.where(is_first, inv_first, inv_second)
     small_late = (coefficients * rank_late * row_scale).astype(BF16)

time: 106 us -> 103 us (0.972)
  waiting for transfers between devices: 26.1 us -> 20.4 us
  starting transfers between devices: 38.8 us -> 40.5 us
    ppermute x0 -> x1, starting transfers between devices: none -> 5.44 us  [on_device(): lax.ppermute(cotangent, ('tensor', 'section'), [(2 * z, 2 * (z + 1) + 1)...]
    ppermute x3, waiting for transfers between devices: 4.57 us -> 1.31 us  [on_device(): lax.ppermute(row_sums, 'tensor', [(z, (z + step) % count) for z in everyo...]
    ppermute x4, waiting for transfers between devices: 10.6 us -> 7.44 us  [sum_step(): other = lax.ppermute(value.astype(wire), 'tensor', pairs)]
    ppermute x1, starting transfers between devices: 2.57 us -> 0.07 us  [on_device(): pulled = lax.ppermute(pulled_here, 'section', swap)]
    ppermute x4, starting transfers between devices: 6.51 us -> 8.52 us  [sum_step(): other = lax.ppermute(value.astype(wire), 'tensor', pairs)]
    ppermute x8 -> x7, starting transfers between devices: 19.2 us -> 17.3 us  [line(): return lax.ppermute(value, ('tensor', 'section'), pairs)]
    ppermute x3, starting transfers between devices: 5.7 us -> 4.1 us  [on_device(): lax.ppermute(row_sums, 'tensor', [(z, (z + step) % count) for z in everyo...]
    ppermute x4 -> x5, starting transfers between devices: 4.66 us -> 4.85 us  [with_other_replicas(): lax.ppermute(value, ('section', 'replica'), [(s * count + r, s * count +...]
  transfers between devices with their start and end apart: 23 -> 24, of which waited for: 9 -> 9; matrix products, arithmetic and copies ran while one was open for 9% -> 12% of each run, Pallas kernels for 22% -> 23%
where the time goes in v18:
time: 103 us; the launch traced here: 102 us
  starting transfers between devices  40.5 us (39%)
  Pallas kernels  27.3 us (27%)
  waiting for transfers between devices  20.4 us (20%)
  other arithmetic  9.19 us (9%)
  matrix products  2.96 us (3%)
  between operations  1.2 us (1%)
    pallas_call x4, Pallas kernels, block_product(): pl.pallas_call(functools.partial(block_kernel, blocks=blocks, tile=tile,...  20.9 us
    ppermute x7, starting transfers between devices, line(): return lax.ppermute(value, ('tensor', 'section'), pairs)  17.3 us
    ppermute x5, waiting for transfers between devices, with_other_replicas(): lax.ppermute(value, ('section', 'replica'), [(s * count + r, s * count +...  10.2 us
    ppermute x4, starting transfers between devices, sum_step(): other = lax.ppermute(value.astype(wire), 'tensor', pairs)  8.52 us
    ppermute x4, waiting for transfers between devices, sum_step(): other = lax.ppermute(value.astype(wire), 'tensor', pairs)  7.44 us
    pallas_call x2, Pallas kernels, gradient_call(): pl.pallas_call(kernel, grid_spec=pltpu.PrefetchScalarGridSpec(num_scalar_...  6.46 us
    ppermute x1, starting transfers between devices, on_device(): lax.ppermute(cotangent, ('tensor', 'section'), [(2 * z, 2 * (z + 1) + 1)...  5.44 us
    ppermute x5, starting transfers between devices, with_other_replicas(): lax.ppermute(value, ('section', 'replica'), [(s * count + r, s * count +...  4.85 us
  transfers between devices with their start and end apart: 24, of which 9 were waited for; matrix products, arithmetic and copies ran while one was open for 12% of the time, Pallas kernels for 23%

profile of v18, /device:TPU:0, one launch (start us, length us, event | category | flops | bytes accessed | tf_op | source)
XLA Modules:
  0.0 102.1 jit_solution(16795340871103789061)
XLA Ops:
  0.6 5.4 %collective-permute-start = (bf16[192,2048]{1,0:T(8,128)(2,1)}, bf16[192,2048]{1,0:T(8,128)(2,1)}, u32[]{:S(2)}, u32[]{:S(2)}) collective-permute-start(bf16[192,2048]{1,0:T(8,128)(2,1)} %param.9), channel_id=1, source_target_pairs={{0,6},{4,10},{8,14},{1,7},{5,11},{9,15},{16,22},{20,26},{24,30},{1... | collective-permute-start | bytes 2359304 | tf_op jit(solution)/shard_map/ppermute | solution.py:280
  6.1 1.6 %collective-permute-start.2 = (bf16[192,2048]{1,0:T(8,128)(2,1)}, bf16[192,2048]{1,0:T(8,128)(2,1)}, u32[]{:S(2)}, u32[]{:S(2)}) collective-permute-start(bf16[192,2048]{1,0:T(8,128)(2,1)} %param.9), channel_id=1, source_target_pairs={{6,2},{10,6},{14,10},{7,3},{11,7},{15,11},{22,18},{26,22},{30,26},... | collective-permute-start | bytes 2359304 | tf_op jit(solution)/shard_map/ppermute | solution.py:264
  7.6 1.4 %fusion.17.value_ref.early = bf16[192,2048]{1,0:T(8,128)(2,1)S(1)} fusion(bf16[192,2048]{1,0:T(8,128)(2,1)} %param.9, bf16[192,2048]{1,0:T(8,128)(2,1)} %param.8, f32[2048]{0:T(1024)} %bitcast.38, pred[]{:T(512)S(6)} %eq.20), kind=kLoop, calls=%fused_computation.35 | loop fusion | flops 1572864 | bytes 2367489 | tf_op jit(solution)/shard_map/jit(_where)/select_n | solution.py:267
  9.1 5.2 %shard_map.95 = f32[192,2048]{1,0:T(8,128)S(1)} custom-call(s32[2]{0:T(128)S(1)} %pad_add_fusion.table, bf16[192,2048]{1,0:T(8,128)(2,1)S(1)} %fusion.17.value_ref.early, bf16[2048,8192]{1,0:T(8,128)(2,1)} %bitcast.41), custom_call_target="tpu_custom_call" | custom-call | flops 6442450944 | bytes 8388608 | tf_op jit(solution)/shard_map/pallas_call | solution.py:72
  15.0 1.4 %add_convert_fusion.5 = bf16[192,2048]{1,0:T(8,128)(2,1)S(1)} fusion(bf16[192,2048]{1,0:T(8,128)(2,1)} %collective-permute-done, f32[192,2048]{1,0:T(8,128)S(1)} %shard_map.95, pred[]{:T(512)S(6)} %eq.20), kind=kLoop, calls=%fused_computation.22 | loop fusion | flops 1572864 | bytes 3145729 | tf_op jit(solution)/shard_map/convert_element_type | solution.py:328
  16.4 3.7 %collective-permute-start.1 = (bf16[192,2048]{1,0:T(8,128)(2,1)S(1)}, bf16[192,2048]{1,0:T(8,128)(2,1)S(1)}, u32[]{:S(2)}, u32[]{:S(2)}) collective-permute-start(bf16[192,2048]{1,0:T(8,128)(2,1)S(1)} %add_convert_fusion.5), channel_id=1, source_target_pairs={{0,4},{6,10},{10,14},{1,5},{7,11},{11,15},{16,20},{22,26},{26,30},... | collective-permute-start | bytes 2359304 | tf_op jit(solution)/shard_map/ppermute | solution.py:264
  20.1 1.3 %add_convert_fusion.4 = bf16[192,2048]{1,0:T(8,128)(2,1)S(1)} fusion(bf16[192,2048]{1,0:T(8,128)(2,1)} %collective-permute-done.2, f32[192,2048]{1,0:T(8,128)S(1)} %shard_map.95, pred[]{:T(512)S(6)} %eq.20), kind=kLoop, calls=%fused_computation.21 | loop fusion | flops 1572864 | bytes 3145729 | tf_op jit(solution)/shard_map/convert_element_type | solution.py:328
  23.5 5.2 %shard_map.96 = f32[192,2048]{1,0:T(8,128)S(1)} custom-call(s32[2]{0:T(128)S(1)} %pad_add_fusion.table, bf16[192,2048]{1,0:T(8,128)(2,1)S(1)} %select_select_fusion.2.value_ref, bf16[2048,8192]{1,0:T(8,128)(2,1)} %bitcast.42), custom_call_target="tpu_custom_call" | custom-call | flops 6442450944 | bytes 8388608 | tf_op jit(solution)/shard_map/pallas_call | solution.py:72
  28.8 1.6 %collective-permute-start.8 = (bf16[192,2048]{1,0:T(8,128)(2,1)S(1)}, bf16[192,2048]{1,0:T(8,128)(2,1)S(1)}, u32[]{:S(2)}, u32[]{:S(2)}) collective-permute-start(bf16[192,2048]{1,0:T(8,128)(2,1)S(1)} %fusion.17.value_ref.early), channel_id=1, source_target_pairs={{0,1},{1,0},{2,3},{3,2},{4,5},{5,4},{6,7},{7,6},{8,9},{9,8},{10,11... | collective-permute-start | bytes 2359304 | tf_op jit(solution)/shard_map/ppermute | solution.py:211
  30.8 3.9 %collective-permute-start.4 = (bf16[192,2048]{1,0:T(8,128)(2,1)S(1)}, bf16[192,2048]{1,0:T(8,128)(2,1)S(1)}, u32[]{:S(2)}, u32[]{:S(2)}) collective-permute-start(bf16[192,2048]{1,0:T(8,128)(2,1)S(1)} %add_convert_fusion.3), channel_id=1, source_target_pairs={{0,4},{4,8},{10,14},{1,5},{5,9},{11,15},{16,20},{20,24},{26,30},{1... | collective-permute-start | bytes 2359304 | tf_op jit(solution)/shard_map/ppermute | solution.py:264
  35.9 4.3 %collective-permute-start.7 = (bf16[208,256]{1,0:T(8,128)(2,1)S(1)}, bf16[208,256]{1,0:T(8,128)(2,1)S(1)}, u32[]{:S(2)}, u32[]{:S(2)}) collective-permute-start(bf16[208,256]{1,0:T(8,128)(2,1)S(1)} %convert_element_type.141), channel_id=1, source_target_pairs={{0,8},{4,12},{8,0},{12,4},{1,9},{5,13},{9,1},{13,5},{2,10},{6,14},... | collective-permute-start | bytes 319496 | tf_op jit(solution)/shard_map/ppermute | solution.py:202
  40.4 5.2 %shard_map.97 = f32[192,2048]{1,0:T(8,128)S(1)} custom-call(s32[2]{0:T(128)S(1)} %pad_add_fusion.table, bf16[192,2048]{1,0:T(8,128)(2,1)S(1)} %select_select_fusion.1.value_ref, bf16[2048,8192]{1,0:T(8,128)(2,1)} %bitcast.43), custom_call_target="tpu_custom_call" | custom-call | flops 6442450944 | bytes 8388608 | tf_op jit(solution)/shard_map/pallas_call | solution.py:72
  46.0 5.4 %collective-permute-start.9 = (bf16[192,2048]{1,0:T(8,128)(2,1)S(1)}, bf16[192,2048]{1,0:T(8,128)(2,1)S(1)}, u32[]{:S(2)}, u32[]{:S(2)}) collective-permute-start(bf16[192,2048]{1,0:T(8,128)(2,1)S(1)} %add_convert_fusion.1), channel_id=1, source_target_pairs={{0,4},{4,8},{8,12},{1,5},{5,9},{9,13},{16,20},{20,24},{24,28},{17,... | collective-permute-start | bytes 2359304 | tf_op jit(solution)/shard_map/ppermute | solution.py:264
  51.7 1.3 %collective-permute-start.10 = (bf16[192,2048]{1,0:T(8,128)(2,1)S(1)}, bf16[192,2048]{1,0:T(8,128)(2,1)S(1)}, u32[]{:S(2)}, u32[]{:S(2)}) collective-permute-start(bf16[192,2048]{1,0:T(8,128)(2,1)S(1)} %add_convert_fusion), channel_id=1, source_target_pairs={{4,0},{8,4},{12,8},{5,1},{9,5},{13,9},{20,16},{24,20},{28,24},{21,... | collective-permute-start | bytes 2359304 | tf_op jit(solution)/shard_map/ppermute | solution.py:264
  53.0 1.5 %collective-permute-done.7 = bf16[208,256]{1,0:T(8,128)(2,1)S(1)} collective-permute-done((bf16[208,256]{1,0:T(8,128)(2,1)S(1)}, bf16[208,256]{1,0:T(8,128)(2,1)S(1)}, u32[]{:S(2)}, u32[]{:S(2)}) %collective-permute-start.7) | collective-permute-done | bytes 106528 | tf_op jit(solution)/shard_map/ppermute | solution.py:202
  54.9 5.2 %shard_map.98 = f32[192,2048]{1,0:T(8,128)S(1)} custom-call(s32[2]{0:T(128)S(1)} %pad_add_fusion.table, bf16[192,2048]{1,0:T(8,128)(2,1)S(1)} %select_select_fusion.value_ref, bf16[2048,8192]{1,0:T(8,128)(2,1)} %bitcast.44), custom_call_target="tpu_custom_call" | custom-call | flops 6442450944 | bytes 8388608 | tf_op jit(solution)/shard_map/pallas_call | solution.py:72
  61.3 0.8 multiply_convert_fusion.1
  62.2 2.8 %collective-permute-done.11.small_early = bf16[192,256]{1,0:T(8,128)(2,1)S(1)} collective-permute-done((bf16[192,256]{1,0:T(8,128)(2,1)S(1)}, bf16[192,256]{1,0:T(8,128)(2,1)S(1)}, u32[]{:S(2)}, u32[]{:S(2)}) %collective-permute-start.11) | collective-permute-done | bytes 98336 | tf_op jit(solution)/shard_map/ppermute | solution.py:211
  65.0 1.1 %collective-permute-done.10 = bf16[192,2048]{1,0:T(8,128)(2,1)S(1)} collective-permute-done((bf16[192,2048]{1,0:T(8,128)(2,1)S(1)}, bf16[192,2048]{1,0:T(8,128)(2,1)S(1)}, u32[]{:S(2)}, u32[]{:S(2)}) %collective-permute-start.10) | collective-permute-done | bytes 786464 | tf_op jit(solution)/shard_map/ppermute | solution.py:264
  66.0 0.9 broadcast_select_fusion.2
  68.3 1.5 %collective-permute-start.15 = (f32[2,192]{1,0:T(2,128)S(1)}, f32[2,192]{1,0:T(2,128)S(1)}, u32[]{:S(2)}, u32[]{:S(2)}) collective-permute-start(f32[2,192]{1,0:T(2,128)S(1)} %pad_maximum_fusion.1), channel_id=1, source_target_pairs={{0,12},{4,0},{8,4},{12,8},{1,13},{5,1},{9,5},{13,9},{2,14},{6,2},{... | collective-permute-start | bytes 4616 | tf_op jit(solution)/shard_map/ppermute | solution.py:387
  70.6 1.8 %collective-permute-start.14 = (f32[2,192]{1,0:T(2,128)S(1)}, f32[2,192]{1,0:T(2,128)S(1)}, u32[]{:S(2)}, u32[]{:S(2)}) collective-permute-start(f32[2,192]{1,0:T(2,128)S(1)} %pad_maximum_fusion.1), channel_id=1, source_target_pairs={{0,8},{4,12},{8,0},{12,4},{1,9},{5,13},{9,1},{13,5},{2,10},{6,14},... | collective-permute-start | bytes 4616 | tf_op jit(solution)/shard_map/ppermute | solution.py:387
  72.4 1.5 %collective-permute-start.21 = (bf16[192,1024]{1,0:T(8,128)(2,1)S(1)}, bf16[192,1024]{1,0:T(8,128)(2,1)S(1)}, u32[]{:S(2)}, u32[]{:S(2)}) collective-permute-start(bf16[192,1024]{1,0:T(8,128)(2,1)S(1)} %get-tuple-element.88), channel_id=1, source_target_pairs={{0,1},{1,0},{2,3},{3,2},{4,5},{5,4},{6,7},{7,6},{8,9},{9,8},{10,11... | collective-permute-start | bytes 1179656 | tf_op jit(solution)/shard_map/ppermute | solution.py:211
  73.9 1.3 %collective-permute-done.13 = f32[2,192]{1,0:T(2,128)S(1)} collective-permute-done((f32[2,192]{1,0:T(2,128)S(1)}, f32[2,192]{1,0:T(2,128)S(1)}, u32[]{:S(2)}, u32[]{:S(2)}) %collective-permute-start.13) | collective-permute-done | bytes 1568 | tf_op jit(solution)/shard_map/ppermute | solution.py:387
  75.2 4.0 %collective-permute-done.16 = bf16[192,1024]{1,0:T(8,128)(2,1)S(1)} collective-permute-done((bf16[192,1024]{1,0:T(8,128)(2,1)S(1)}, bf16[192,1024]{1,0:T(8,128)(2,1)S(1)}, u32[]{:S(2)}, u32[]{:S(2)}) %collective-permute-start.16) | collective-permute-done | bytes 393248 | tf_op jit(solution)/shard_map/ppermute | solution.py:211
  80.8 2.1 %collective-permute-start.19 = (bf16[192,256]{1,0:T(8,128)(2,1)S(1)}, bf16[192,256]{1,0:T(8,128)(2,1)S(1)}, u32[]{:S(2)}, u32[]{:S(2)}) collective-permute-start(bf16[192,256]{1,0:T(8,128)(2,1)S(1)} %get-tuple-element.97), channel_id=1, source_target_pairs={{0,4},{4,0},{8,12},{12,8},{1,5},{5,1},{9,13},{13,9},{2,6},{6,2},{1... | collective-permute-start | bytes 294920 | tf_op jit(solution)/shard_map/ppermute | solution.py:202
  83.0 2.5 %collective-permute-done.19 = bf16[192,256]{1,0:T(8,128)(2,1)S(1)} collective-permute-done((bf16[192,256]{1,0:T(8,128)(2,1)S(1)}, bf16[192,256]{1,0:T(8,128)(2,1)S(1)}, u32[]{:S(2)}, u32[]{:S(2)}) %collective-permute-start.19) | collective-permute-done | bytes 98336 | tf_op jit(solution)/shard_map/ppermute | solution.py:202
  85.5 2.1 %collective-permute-start.20 = (bf16[192,256]{1,0:T(8,128)(2,1)S(1)}, bf16[192,256]{1,0:T(8,128)(2,1)S(1)}, u32[]{:S(2)}, u32[]{:S(2)}) collective-permute-start(bf16[192,256]{1,0:T(8,128)(2,1)S(1)} %fusion.23), channel_id=1, source_target_pairs={{0,8},{4,12},{8,0},{12,4},{1,9},{5,13},{9,1},{13,5},{2,10},{6,14},... | collective-permute-start | bytes 294920 | tf_op jit(solution)/shard_map/ppermute | solution.py:202
  87.6 3.5 %collective-permute-done.20 = bf16[192,256]{1,0:T(8,128)(2,1)S(1)} collective-permute-done((bf16[192,256]{1,0:T(8,128)(2,1)S(1)}, bf16[192,256]{1,0:T(8,128)(2,1)S(1)}, u32[]{:S(2)}, u32[]{:S(2)}) %collective-permute-start.20) | collective-permute-done | bytes 98336 | tf_op jit(solution)/shard_map/ppermute | solution.py:202
  92.2 2.3 %shard_map.99 = (f32[2048,256]{1,0:T(8,128)S(1)}, f32[256,2048]{1,0:T(8,128)S(1)}) custom-call(s32[2]{0:T(128)S(1)} %pad_add_fusion.table, bf16[192,2048]{1,0:T(8,128)(2,1)S(1)} %fusion.17.value_ref.early, bf16[192,2048]{1,0:T(8,128)(2,1)S(1)} %fusion.16.late, bf16[192,256]{1,0:T(8,128)(2,1)S(1)} %get-tuple-element.94.small_early, ...), custom_call_target="tpu_custom_call" | custom-call | flops 402653184 | bytes 5767168 | tf_op jit(solution)/shard_map/pallas_call | solution.py:145
  94.6 3.3 %collective-permute-done.23.small_late = bf16[192,384]{1,0:T(8,128)(2,1)S(1)} collective-permute-done((bf16[192,384]{1,0:T(8,128)(2,1)S(1)}, bf16[192,384]{1,0:T(8,128)(2,1)S(1)}, u32[]{:S(2)}, u32[]{:S(2)}) %collective-permute-start.23) | collective-permute-done | bytes 147488 | tf_op jit(solution)/shard_map/ppermute | solution.py:211
  97.9 4.2 %shard_map.100 = (f32[2048,256]{1,0:T(8,128)}, f32[256,2048]{1,0:T(8,128)}) custom-call(s32[2]{0:T(128)S(1)} %pad_add_fusion.table, f32[1,2048]{1,0:T(1,128)S(1)} %copy-done.1, f32[2048,256]{1,0:T(8,128)S(1)} %get-tuple-element.70.down_sum, f32[256,2048]{1,0:T(8,128)S(1)} %get-tuple-element.71.up_sum, bf16[192,2048]{1,0:T(8,128)(2,1)S(1)} %collective-permute-done.8.early, ...), custom_call_target="tpu_custom_call" | custom-call | flops 402653184 | bytes 11534336 | tf_op jit(solution)/shard_map/pallas_call | solution.py:145
  (86 shorter events, 11.6 us)
Async XLA Ops:
  0.6 22.3 %copy-start = (bf16[1,2048,256]{2,1,0:T(8,128)(2,1)S(1)}, bf16[1,2048,256]{2,1,0:T(8,128)(2,1)}, u32[]{:S(2)}) copy-start(bf16[1,2048,256]{2,1,0:T(8,128)(2,1)} %param.12) | copy-start | bytes 3145732
  0.6 14.3 %collective-permute-start = (bf16[192,2048]{1,0:T(8,128)(2,1)}, bf16[192,2048]{1,0:T(8,128)(2,1)}, u32[]{:S(2)}, u32[]{:S(2)}) collective-permute-start(bf16[192,2048]{1,0:T(8,128)(2,1)} %param.9), channel_id=1, source_target_pairs={{0,6},{4,10},{8,14},{1,7},{5,11},{9,15},{16,22},{20,26},{24,30},{1... | collective-permute-start | bytes 2359304 | tf_op jit(solution)/shard_map/ppermute | solution.py:280
  6.1 14.0 %collective-permute-start.2 = (bf16[192,2048]{1,0:T(8,128)(2,1)}, bf16[192,2048]{1,0:T(8,128)(2,1)}, u32[]{:S(2)}, u32[]{:S(2)}) collective-permute-start(bf16[192,2048]{1,0:T(8,128)(2,1)} %param.9), channel_id=1, source_target_pairs={{6,2},{10,6},{14,10},{7,3},{11,7},{15,11},{22,18},{26,22},{30,26},... | collective-permute-start | bytes 2359304 | tf_op jit(solution)/shard_map/ppermute | solution.py:264
  9.1 5.2 %copy-start.6 = (f32[4]{0:T(128)S(1)}, f32[4]{0:T(128)}, u32[]{:S(2)}) copy-start(f32[4]{0:T(128)} %param.14) | copy-start | bytes 52
  16.4 5.8 %copy-start.3 = (bf16[192,2048]{1,0:T(8,128)(2,1)S(1)}, bf16[192,2048]{1,0:T(8,128)(2,1)}, u32[]{:S(2)}) copy-start(bf16[192,2048]{1,0:T(8,128)(2,1)} %param.8) | copy-start | bytes 2359300
  16.4 6.0 %copy-start.2 = (bf16[1,256,2048]{2,1,0:T(8,128)(2,1)S(1)}, bf16[1,256,2048]{2,1,0:T(8,128)(2,1)}, u32[]{:S(2)}) copy-start(bf16[1,256,2048]{2,1,0:T(8,128)(2,1)} %param.13) | copy-start | bytes 3145732
  16.4 14.0 %collective-permute-start.1 = (bf16[192,2048]{1,0:T(8,128)(2,1)S(1)}, bf16[192,2048]{1,0:T(8,128)(2,1)S(1)}, u32[]{:S(2)}, u32[]{:S(2)}) collective-permute-start(bf16[192,2048]{1,0:T(8,128)(2,1)S(1)} %add_convert_fusion.5), channel_id=1, source_target_pairs={{0,4},{6,10},{10,14},{1,5},{7,11},{11,15},{16,20},{22,26},{26,30},... | collective-permute-start | bytes 2359304 | tf_op jit(solution)/shard_map/ppermute | solution.py:264
  21.4 13.3 %collective-permute-start.3 = (bf16[192,2048]{1,0:T(8,128)(2,1)S(1)}, bf16[192,2048]{1,0:T(8,128)(2,1)S(1)}, u32[]{:S(2)}, u32[]{:S(2)}) collective-permute-start(bf16[192,2048]{1,0:T(8,128)(2,1)S(1)} %add_convert_fusion.4), channel_id=1, source_target_pairs={{12,8},{6,2},{10,6},{13,9},{7,3},{11,7},{28,24},{22,18},{26,22},{2... | collective-permute-start | bytes 2359304 | tf_op jit(solution)/shard_map/ppermute | solution.py:264
  28.8 7.0 %collective-permute-start.6 = (bf16[208,256]{1,0:T(8,128)(2,1)S(1)}, bf16[208,256]{1,0:T(8,128)(2,1)S(1)}, u32[]{:S(2)}, u32[]{:S(2)}) collective-permute-start(bf16[208,256]{1,0:T(8,128)(2,1)S(1)} %convert_element_type.139), channel_id=1, source_target_pairs={{0,4},{4,0},{8,12},{12,8},{1,5},{5,1},{9,13},{13,9},{2,6},{6,2},{1... | collective-permute-start | bytes 319496 | tf_op jit(solution)/shard_map/ppermute | solution.py:202
  28.8 31.3 %collective-permute-start.8 = (bf16[192,2048]{1,0:T(8,128)(2,1)S(1)}, bf16[192,2048]{1,0:T(8,128)(2,1)S(1)}, u32[]{:S(2)}, u32[]{:S(2)}) collective-permute-start(bf16[192,2048]{1,0:T(8,128)(2,1)S(1)} %fusion.17.value_ref.early), channel_id=1, source_target_pairs={{0,1},{1,0},{2,3},{3,2},{4,5},{5,4},{6,7},{7,6},{8,9},{9,8},{10,11... | collective-permute-start | bytes 2359304 | tf_op jit(solution)/shard_map/ppermute | solution.py:211
  30.8 14.8 %collective-permute-start.4 = (bf16[192,2048]{1,0:T(8,128)(2,1)S(1)}, bf16[192,2048]{1,0:T(8,128)(2,1)S(1)}, u32[]{:S(2)}, u32[]{:S(2)}) collective-permute-start(bf16[192,2048]{1,0:T(8,128)(2,1)S(1)} %add_convert_fusion.3), channel_id=1, source_target_pairs={{0,4},{4,8},{10,14},{1,5},{5,9},{11,15},{16,20},{20,24},{26,30},{1... | collective-permute-start | bytes 2359304 | tf_op jit(solution)/shard_map/ppermute | solution.py:264
  35.1 16.4 %collective-permute-start.5 = (bf16[192,2048]{1,0:T(8,128)(2,1)S(1)}, bf16[192,2048]{1,0:T(8,128)(2,1)S(1)}, u32[]{:S(2)}, u32[]{:S(2)}) collective-permute-start(bf16[192,2048]{1,0:T(8,128)(2,1)S(1)} %add_convert_fusion.2), channel_id=1, source_target_pairs={{8,4},{12,8},{6,2},{9,5},{13,9},{7,3},{24,20},{28,24},{22,18},{25,... | collective-permute-start | bytes 2359304 | tf_op jit(solution)/shard_map/ppermute | solution.py:264
  35.9 18.6 %collective-permute-start.7 = (bf16[208,256]{1,0:T(8,128)(2,1)S(1)}, bf16[208,256]{1,0:T(8,128)(2,1)S(1)}, u32[]{:S(2)}, u32[]{:S(2)}) collective-permute-start(bf16[208,256]{1,0:T(8,128)(2,1)S(1)} %convert_element_type.141), channel_id=1, source_target_pairs={{0,8},{4,12},{8,0},{12,4},{1,9},{5,13},{9,1},{13,5},{2,10},{6,14},... | collective-permute-start | bytes 319496 | tf_op jit(solution)/shard_map/ppermute | solution.py:202
  46.0 19.0 %collective-permute-start.9 = (bf16[192,2048]{1,0:T(8,128)(2,1)S(1)}, bf16[192,2048]{1,0:T(8,128)(2,1)S(1)}, u32[]{:S(2)}, u32[]{:S(2)}) collective-permute-start(bf16[192,2048]{1,0:T(8,128)(2,1)S(1)} %add_convert_fusion.1), channel_id=1, source_target_pairs={{0,4},{4,8},{8,12},{1,5},{5,9},{9,13},{16,20},{20,24},{24,28},{17,... | collective-permute-start | bytes 2359304 | tf_op jit(solution)/shard_map/ppermute | solution.py:264
  51.7 14.3 %collective-permute-start.10 = (bf16[192,2048]{1,0:T(8,128)(2,1)S(1)}, bf16[192,2048]{1,0:T(8,128)(2,1)S(1)}, u32[]{:S(2)}, u32[]{:S(2)}) collective-permute-start(bf16[192,2048]{1,0:T(8,128)(2,1)S(1)} %add_convert_fusion), channel_id=1, source_target_pairs={{4,0},{8,4},{12,8},{5,1},{9,5},{13,9},{20,16},{24,20},{28,24},{21,... | collective-permute-start | bytes 2359304 | tf_op jit(solution)/shard_map/ppermute | solution.py:264
  54.9 5.3 %copy-start.5 = (s32[192]{0:T(256)S(1)}, s32[192]{0:T(256)}, u32[]{:S(2)}) copy-start(s32[192]{0:T(256)} %param.15) | copy-start | bytes 2308
  60.1 1.2 %copy-start.1 = (f32[1,2048]{1,0:T(1,128)S(1)}, f32[1,2048]{1,0:T(1,128)}, u32[]{:S(2)}) copy-start(f32[1,2048]{1,0:T(1,128)} %gain_ref.1) | copy-start | bytes 24580
  60.3 4.7 %collective-permute-start.11 = (bf16[192,256]{1,0:T(8,128)(2,1)S(1)}, bf16[192,256]{1,0:T(8,128)(2,1)S(1)}, u32[]{:S(2)}, u32[]{:S(2)}) collective-permute-start(bf16[192,256]{1,0:T(8,128)(2,1)S(1)} %get-tuple-element.86), channel_id=1, source_target_pairs={{0,1},{1,0},{2,3},{3,2},{4,5},{5,4},{6,7},{7,6},{8,9},{9,8},{10,11... | collective-permute-start | bytes 294920 | tf_op jit(solution)/shard_map/ppermute | solution.py:211
  62.1 5.8 %collective-permute-start.12 = (bf16[192,2048]{1,0:T(8,128)(2,1)S(1)}, bf16[192,2048]{1,0:T(8,128)(2,1)S(1)}, u32[]{:S(2)}, u32[]{:S(2)}) collective-permute-start(bf16[192,2048]{1,0:T(8,128)(2,1)S(1)} %get-tuple-element.95), channel_id=1, source_target_pairs={{0,2},{2,0},{1,3},{3,1},{4,6},{6,4},{5,7},{7,5},{8,10},{10,8},{9,1... | collective-permute-start | bytes 2359304 | tf_op jit(solution)/shard_map/ppermute | solution.py:364
  67.1 12.2 %collective-permute-start.17 = (bf16[192,2048]{1,0:T(8,128)(2,1)S(1)}, bf16[192,2048]{1,0:T(8,128)(2,1)S(1)}, u32[]{:S(2)}, u32[]{:S(2)}) collective-permute-start(bf16[192,2048]{1,0:T(8,128)(2,1)S(1)} %broadcast_select_fusion.1), channel_id=1, source_target_pairs={{0,2},{2,0},{1,3},{3,1},{4,6},{6,4},{5,7},{7,5},{8,10},{10,8},{9,1... | collective-permute-start | bytes 2359304 | tf_op jit(solution)/shard_map/ppermute | solution.py:376
  67.2 12.1 %copy-start.4 = (bf16[192,2048]{1,0:T(8,128)(2,1)S(1)}, bf16[192,2048]{1,0:T(8,128)(2,1)}, u32[]{:S(2)}) copy-start(bf16[192,2048]{1,0:T(8,128)(2,1)} %param.9) | copy-start | bytes 2359300
  67.3 12.0 %collective-permute-start.16 = (bf16[192,1024]{1,0:T(8,128)(2,1)S(1)}, bf16[192,1024]{1,0:T(8,128)(2,1)S(1)}, u32[]{:S(2)}, u32[]{:S(2)}) collective-permute-start(bf16[192,1024]{1,0:T(8,128)(2,1)S(1)} %get-tuple-element.89), channel_id=1, source_target_pairs={{0,1},{1,0},{2,3},{3,2},{4,5},{5,4},{6,7},{7,6},{8,9},{9,8},{10,11... | collective-permute-start | bytes 1179656 | tf_op jit(solution)/shard_map/ppermute | solution.py:211
  68.3 4.1 %collective-permute-start.15 = (f32[2,192]{1,0:T(2,128)S(1)}, f32[2,192]{1,0:T(2,128)S(1)}, u32[]{:S(2)}, u32[]{:S(2)}) collective-permute-start(f32[2,192]{1,0:T(2,128)S(1)} %pad_maximum_fusion.1), channel_id=1, source_target_pairs={{0,12},{4,0},{8,4},{12,8},{1,13},{5,1},{9,5},{13,9},{2,14},{6,2},{... | collective-permute-start | bytes 4616 | tf_op jit(solution)/shard_map/ppermute | solution.py:387
  69.8 5.4 %collective-permute-start.13 = (f32[2,192]{1,0:T(2,128)S(1)}, f32[2,192]{1,0:T(2,128)S(1)}, u32[]{:S(2)}, u32[]{:S(2)}) collective-permute-start(f32[2,192]{1,0:T(2,128)S(1)} %pad_maximum_fusion.1), channel_id=1, source_target_pairs={{0,4},{4,8},{8,12},{12,0},{1,5},{5,9},{9,13},{13,1},{2,6},{6,10},{... | collective-permute-start | bytes 4616 | tf_op jit(solution)/shard_map/ppermute | solution.py:387
  70.6 4.6 %collective-permute-start.14 = (f32[2,192]{1,0:T(2,128)S(1)}, f32[2,192]{1,0:T(2,128)S(1)}, u32[]{:S(2)}, u32[]{:S(2)}) collective-permute-start(f32[2,192]{1,0:T(2,128)S(1)} %pad_maximum_fusion.1), channel_id=1, source_target_pairs={{0,8},{4,12},{8,0},{12,4},{1,9},{5,13},{9,1},{13,5},{2,10},{6,14},... | collective-permute-start | bytes 4616 | tf_op jit(solution)/shard_map/ppermute | solution.py:387
  72.4 18.8 %collective-permute-start.21 = (bf16[192,1024]{1,0:T(8,128)(2,1)S(1)}, bf16[192,1024]{1,0:T(8,128)(2,1)S(1)}, u32[]{:S(2)}, u32[]{:S(2)}) collective-permute-start(bf16[192,1024]{1,0:T(8,128)(2,1)S(1)} %get-tuple-element.88), channel_id=1, source_target_pairs={{0,1},{1,0},{2,3},{3,2},{4,5},{5,4},{6,7},{7,6},{8,9},{9,8},{10,11... | collective-permute-start | bytes 1179656 | tf_op jit(solution)/shard_map/ppermute | solution.py:211
  80.8 4.7 %collective-permute-start.19 = (bf16[192,256]{1,0:T(8,128)(2,1)S(1)}, bf16[192,256]{1,0:T(8,128)(2,1)S(1)}, u32[]{:S(2)}, u32[]{:S(2)}) collective-permute-start(bf16[192,256]{1,0:T(8,128)(2,1)S(1)} %get-tuple-element.97), channel_id=1, source_target_pairs={{0,4},{4,0},{8,12},{12,8},{1,5},{5,1},{9,13},{13,9},{2,6},{6,2},{1... | collective-permute-start | bytes 294920 | tf_op jit(solution)/shard_map/ppermute | solution.py:202
  82.9 4.7 %collective-permute-start.18 = (f32[192]{0:T(256)S(1)}, f32[192]{0:T(256)S(1)}, u32[]{:S(2)}, u32[]{:S(2)}) collective-permute-start(f32[192]{0:T(256)S(1)} %bitcast.47), channel_id=1, source_target_pairs={{0,2},{2,0},{1,3},{3,1},{4,6},{6,4},{5,7},{7,5},{8,10},{10,8},{9,1... | collective-permute-start | bytes 2312 | tf_op jit(solution)/shard_map/ppermute | solution.py:404
  85.5 5.6 %collective-permute-start.20 = (bf16[192,256]{1,0:T(8,128)(2,1)S(1)}, bf16[192,256]{1,0:T(8,128)(2,1)S(1)}, u32[]{:S(2)}, u32[]{:S(2)}) collective-permute-start(bf16[192,256]{1,0:T(8,128)(2,1)S(1)} %fusion.23), channel_id=1, source_target_pairs={{0,8},{4,12},{8,0},{12,4},{1,9},{5,13},{9,1},{13,5},{2,10},{6,14},... | collective-permute-start | bytes 294920 | tf_op jit(solution)/shard_map/ppermute | solution.py:202
  91.2 3.3 %collective-permute-start.22 = (bf16[192,2048]{1,0:T(8,128)(2,1)S(1)}, bf16[192,2048]{1,0:T(8,128)(2,1)S(1)}, u32[]{:S(2)}, u32[]{:S(2)}) collective-permute-start(bf16[192,2048]{1,0:T(8,128)(2,1)S(1)} %constant_dynamic-update-slice_fusion), channel_id=1, source_target_pairs={{0,2},{2,0},{1,3},{3,1},{4,6},{6,4},{5,7},{7,5},{8,10},{10,8},{9,1... | collective-permute-start | bytes 2359304 | tf_op jit(solution)/shard_map/ppermute | solution.py:435
  91.6 6.3 %collective-permute-start.23 = (bf16[192,384]{1,0:T(8,128)(2,1)S(1)}, bf16[192,384]{1,0:T(8,128)(2,1)S(1)}, u32[]{:S(2)}, u32[]{:S(2)}) collective-permute-start(bf16[192,384]{1,0:T(8,128)(2,1)S(1)} %pad_maximum_fusion), channel_id=1, source_target_pairs={{0,1},{1,0},{2,3},{3,2},{4,5},{5,4},{6,7},{7,6},{8,9},{9,8},{10,11... | collective-permute-start | bytes 442376 | tf_op jit(solution)/shard_map/ppermute | solution.py:211

commit v19 on v18

--- a/solution.py
+++ b/solution.py
@@ -368,10 +368,10 @@
 
     projected = parts[-1] + from_left.astype(F32) + from_right.astype(F32) + low_product
     hidden = (token_float + inv_first * projected).astype(BF16)
-    half = width // 2 if width % 256 == 0 else width
+    cut = width // 4 if width % 512 == 0 else width
     exchanged = jnp.where(is_first, hidden, pulled_here)
-    first_halves = with_other_replicas(exchanged[:, :half])[1:]
-    second_halves = with_other_replicas(exchanged[:, half:])[1:] if half < width else None
+    first_columns = with_other_replicas(exchanged[:, :cut])[1:]
+    other_columns = with_other_replicas(exchanged[:, cut:])[1:] if cut < width else None
     swapped = [
         lax.ppermute(jnp.where(is_first, hidden, other), "section", swap) for other in early_all[1:]
     ]
@@ -390,7 +390,7 @@
     else:
         for step in doubling_steps():
             row_sums = sum_step(row_sums, step, F32)
-    row_sums, *first_halves = lax.optimization_barrier((row_sums, *first_halves))
+    row_sums, *first_columns = lax.optimization_barrier((row_sums, *first_columns))
     inv_second = lax.rsqrt(row_sums[0] / features + EPSILON)
     inv_second = inv_second[:, None]
     toward_hidden = row_sums[1][:, None] * inv_second * inv_second * inv_second / features
@@ -407,11 +407,11 @@
     for step in doubling_steps():
         rank_late = sum_step(rank_late, step)
 
-    late_others = first_halves
-    if second_halves is not None:
-        *second_halves, _ = lax.optimization_barrier((*second_halves, rank_late))
+    late_others = first_columns
+    if other_columns is not None:
+        *other_columns, _ = lax.optimization_barrier((*other_columns, rank_late))
         late_others = [
-            jnp.concatenate(halves, axis=1) for halves in zip(first_halves, second_halves)
+            jnp.concatenate(both, axis=1) for both in zip(first_columns, other_columns)
         ]
     inv_second = jnp.where(is_first, inv_second, inv_on_second)
     row_scale = jnp.where(is_first, inv_first, inv_second)

time: 103 us -> 103 us (level)
  waiting for transfers between devices: 20.4 us -> 22.1 us
  starting transfers between devices: 40.5 us -> 39.3 us
    ppermute x4, waiting for transfers between devices: 7.44 us -> 8.64 us  [sum_step(): other = lax.ppermute(value.astype(wire), 'tensor', pairs)]
    ppermute x4, starting transfers between devices: 8.52 us -> 7.33 us  [sum_step(): other = lax.ppermute(value.astype(wire), 'tensor', pairs)]
    ppermute x5, waiting for transfers between devices: 10.2 us -> 11.3 us  [with_other_replicas(): lax.ppermute(value, ('section', 'replica'), [(s * count + r, s * count +...]
where the time goes in v19:
time: 103 us
  starting transfers between devices  39.3 us (38%)
  Pallas kernels  27.3 us (27%)
  waiting for transfers between devices  22.1 us (21%)
  other arithmetic  9.2 us (9%)
  matrix products  2.96 us (3%)
  between operations  1.21 us (1%)
    pallas_call x4, Pallas kernels, block_product(): pl.pallas_call(functools.partial(block_kernel, blocks=blocks, tile=tile,...  20.9 us
    ppermute x7, starting transfers between devices, line(): return lax.ppermute(value, ('tensor', 'section'), pairs)  17.3 us
    ppermute x5, waiting for transfers between devices, with_other_replicas(): lax.ppermute(value, ('section', 'replica'), [(s * count + r, s * count +...  11.3 us
    ppermute x4, waiting for transfers between devices, sum_step(): other = lax.ppermute(value.astype(wire), 'tensor', pairs)  8.64 us
    ppermute x4, starting transfers between devices, sum_step(): other = lax.ppermute(value.astype(wire), 'tensor', pairs)  7.33 us
    pallas_call x2, Pallas kernels, gradient_call(): pl.pallas_call(kernel, grid_spec=pltpu.PrefetchScalarGridSpec(num_scalar_...  6.46 us
    ppermute x1, starting transfers between devices, on_device(): lax.ppermute(cotangent, ('tensor', 'section'), [(2 * z, 2 * (z + 1) + 1)...  5.44 us
    ppermute x5, starting transfers between devices, with_other_replicas(): lax.ppermute(value, ('section', 'replica'), [(s * count + r, s * count +...  4.83 us
  transfers between devices with their start and end apart: 24, of which 9 were waited for; matrix products, arithmetic and copies ran while one was open for 12% of the time, Pallas kernels for 23%

profile of v19, /device:TPU:0, one launch (start us, length us, event | category | flops | bytes accessed | tf_op | source)
XLA Modules:
  0.0 102.6 jit_solution(16231578713988184630)
XLA Ops:
  0.6 5.4 %collective-permute-start = (bf16[192,2048]{1,0:T(8,128)(2,1)}, bf16[192,2048]{1,0:T(8,128)(2,1)}, u32[]{:S(2)}, u32[]{:S(2)}) collective-permute-start(bf16[192,2048]{1,0:T(8,128)(2,1)} %param.9), channel_id=1, source_target_pairs={{0,6},{4,10},{8,14},{1,7},{5,11},{9,15},{16,22},{20,26},{24,30},{1... | collective-permute-start | bytes 2359304 | tf_op jit(solution)/shard_map/ppermute | solution.py:280
  6.1 1.6 %collective-permute-start.2 = (bf16[192,2048]{1,0:T(8,128)(2,1)}, bf16[192,2048]{1,0:T(8,128)(2,1)}, u32[]{:S(2)}, u32[]{:S(2)}) collective-permute-start(bf16[192,2048]{1,0:T(8,128)(2,1)} %param.9), channel_id=1, source_target_pairs={{6,2},{10,6},{14,10},{7,3},{11,7},{15,11},{22,18},{26,22},{30,26},... | collective-permute-start | bytes 2359304 | tf_op jit(solution)/shard_map/ppermute | solution.py:264
  7.6 1.4 %fusion.17.value_ref.early = bf16[192,2048]{1,0:T(8,128)(2,1)S(1)} fusion(bf16[192,2048]{1,0:T(8,128)(2,1)} %param.9, bf16[192,2048]{1,0:T(8,128)(2,1)} %param.8, f32[2048]{0:T(1024)} %bitcast.38, pred[]{:T(512)S(6)} %eq.20), kind=kLoop, calls=%fused_computation.35 | loop fusion | flops 1572864 | bytes 2367489 | tf_op jit(solution)/shard_map/jit(_where)/select_n | solution.py:267
  9.1 5.2 %shard_map.95 = f32[192,2048]{1,0:T(8,128)S(1)} custom-call(s32[2]{0:T(128)S(1)} %pad_add_fusion.table, bf16[192,2048]{1,0:T(8,128)(2,1)S(1)} %fusion.17.value_ref.early, bf16[2048,8192]{1,0:T(8,128)(2,1)} %bitcast.41), custom_call_target="tpu_custom_call" | custom-call | flops 6442450944 | bytes 8388608 | tf_op jit(solution)/shard_map/pallas_call | solution.py:72
  15.0 1.4 %add_convert_fusion.5 = bf16[192,2048]{1,0:T(8,128)(2,1)S(1)} fusion(bf16[192,2048]{1,0:T(8,128)(2,1)} %collective-permute-done, f32[192,2048]{1,0:T(8,128)S(1)} %shard_map.95, pred[]{:T(512)S(6)} %eq.20), kind=kLoop, calls=%fused_computation.22 | loop fusion | flops 1572864 | bytes 3145729 | tf_op jit(solution)/shard_map/convert_element_type | solution.py:328
  16.4 3.7 %collective-permute-start.1 = (bf16[192,2048]{1,0:T(8,128)(2,1)S(1)}, bf16[192,2048]{1,0:T(8,128)(2,1)S(1)}, u32[]{:S(2)}, u32[]{:S(2)}) collective-permute-start(bf16[192,2048]{1,0:T(8,128)(2,1)S(1)} %add_convert_fusion.5), channel_id=1, source_target_pairs={{0,4},{6,10},{10,14},{1,5},{7,11},{11,15},{16,20},{22,26},{26,30},... | collective-permute-start | bytes 2359304 | tf_op jit(solution)/shard_map/ppermute | solution.py:264
  20.1 1.3 %add_convert_fusion.4 = bf16[192,2048]{1,0:T(8,128)(2,1)S(1)} fusion(bf16[192,2048]{1,0:T(8,128)(2,1)} %collective-permute-done.2, f32[192,2048]{1,0:T(8,128)S(1)} %shard_map.95, pred[]{:T(512)S(6)} %eq.20), kind=kLoop, calls=%fused_computation.21 | loop fusion | flops 1572864 | bytes 3145729 | tf_op jit(solution)/shard_map/convert_element_type | solution.py:328
  23.5 5.2 %shard_map.96 = f32[192,2048]{1,0:T(8,128)S(1)} custom-call(s32[2]{0:T(128)S(1)} %pad_add_fusion.table, bf16[192,2048]{1,0:T(8,128)(2,1)S(1)} %select_select_fusion.2.value_ref, bf16[2048,8192]{1,0:T(8,128)(2,1)} %bitcast.42), custom_call_target="tpu_custom_call" | custom-call | flops 6442450944 | bytes 8388608 | tf_op jit(solution)/shard_map/pallas_call | solution.py:72
  28.8 1.6 %collective-permute-start.8 = (bf16[192,2048]{1,0:T(8,128)(2,1)S(1)}, bf16[192,2048]{1,0:T(8,128)(2,1)S(1)}, u32[]{:S(2)}, u32[]{:S(2)}) collective-permute-start(bf16[192,2048]{1,0:T(8,128)(2,1)S(1)} %fusion.17.value_ref.early), channel_id=1, source_target_pairs={{0,1},{1,0},{2,3},{3,2},{4,5},{5,4},{6,7},{7,6},{8,9},{9,8},{10,11... | collective-permute-start | bytes 2359304 | tf_op jit(solution)/shard_map/ppermute | solution.py:211
  30.8 3.9 %collective-permute-start.4 = (bf16[192,2048]{1,0:T(8,128)(2,1)S(1)}, bf16[192,2048]{1,0:T(8,128)(2,1)S(1)}, u32[]{:S(2)}, u32[]{:S(2)}) collective-permute-start(bf16[192,2048]{1,0:T(8,128)(2,1)S(1)} %add_convert_fusion.3), channel_id=1, source_target_pairs={{0,4},{4,8},{10,14},{1,5},{5,9},{11,15},{16,20},{20,24},{26,30},{1... | collective-permute-start | bytes 2359304 | tf_op jit(solution)/shard_map/ppermute | solution.py:264
  35.9 4.3 %collective-permute-start.7 = (bf16[208,256]{1,0:T(8,128)(2,1)S(1)}, bf16[208,256]{1,0:T(8,128)(2,1)S(1)}, u32[]{:S(2)}, u32[]{:S(2)}) collective-permute-start(bf16[208,256]{1,0:T(8,128)(2,1)S(1)} %convert_element_type.141), channel_id=1, source_target_pairs={{0,8},{4,12},{8,0},{12,4},{1,9},{5,13},{9,1},{13,5},{2,10},{6,14},... | collective-permute-start | bytes 319496 | tf_op jit(solution)/shard_map/ppermute | solution.py:202
  40.4 5.2 %shard_map.97 = f32[192,2048]{1,0:T(8,128)S(1)} custom-call(s32[2]{0:T(128)S(1)} %pad_add_fusion.table, bf16[192,2048]{1,0:T(8,128)(2,1)S(1)} %select_select_fusion.1.value_ref, bf16[2048,8192]{1,0:T(8,128)(2,1)} %bitcast.43), custom_call_target="tpu_custom_call" | custom-call | flops 6442450944 | bytes 8388608 | tf_op jit(solution)/shard_map/pallas_call | solution.py:72
  46.0 5.4 %collective-permute-start.9 = (bf16[192,2048]{1,0:T(8,128)(2,1)S(1)}, bf16[192,2048]{1,0:T(8,128)(2,1)S(1)}, u32[]{:S(2)}, u32[]{:S(2)}) collective-permute-start(bf16[192,2048]{1,0:T(8,128)(2,1)S(1)} %add_convert_fusion.1), channel_id=1, source_target_pairs={{0,4},{4,8},{8,12},{1,5},{5,9},{9,13},{16,20},{20,24},{24,28},{17,... | collective-permute-start | bytes 2359304 | tf_op jit(solution)/shard_map/ppermute | solution.py:264
  51.7 1.3 %collective-permute-start.10 = (bf16[192,2048]{1,0:T(8,128)(2,1)S(1)}, bf16[192,2048]{1,0:T(8,128)(2,1)S(1)}, u32[]{:S(2)}, u32[]{:S(2)}) collective-permute-start(bf16[192,2048]{1,0:T(8,128)(2,1)S(1)} %add_convert_fusion), channel_id=1, source_target_pairs={{4,0},{8,4},{12,8},{5,1},{9,5},{13,9},{20,16},{24,20},{28,24},{21,... | collective-permute-start | bytes 2359304 | tf_op jit(solution)/shard_map/ppermute | solution.py:264
  53.0 1.5 %collective-permute-done.7 = bf16[208,256]{1,0:T(8,128)(2,1)S(1)} collective-permute-done((bf16[208,256]{1,0:T(8,128)(2,1)S(1)}, bf16[208,256]{1,0:T(8,128)(2,1)S(1)}, u32[]{:S(2)}, u32[]{:S(2)}) %collective-permute-start.7) | collective-permute-done | bytes 106528 | tf_op jit(solution)/shard_map/ppermute | solution.py:202
  54.9 5.2 %shard_map.98 = f32[192,2048]{1,0:T(8,128)S(1)} custom-call(s32[2]{0:T(128)S(1)} %pad_add_fusion.table, bf16[192,2048]{1,0:T(8,128)(2,1)S(1)} %select_select_fusion.value_ref, bf16[2048,8192]{1,0:T(8,128)(2,1)} %bitcast.44), custom_call_target="tpu_custom_call" | custom-call | flops 6442450944 | bytes 8388608 | tf_op jit(solution)/shard_map/pallas_call | solution.py:72
  61.3 0.8 multiply_convert_fusion.1
  62.2 2.8 %collective-permute-done.11.small_early = bf16[192,256]{1,0:T(8,128)(2,1)S(1)} collective-permute-done((bf16[192,256]{1,0:T(8,128)(2,1)S(1)}, bf16[192,256]{1,0:T(8,128)(2,1)S(1)}, u32[]{:S(2)}, u32[]{:S(2)}) %collective-permute-start.11) | collective-permute-done | bytes 98336 | tf_op jit(solution)/shard_map/ppermute | solution.py:211
  65.0 1.1 %collective-permute-done.10 = bf16[192,2048]{1,0:T(8,128)(2,1)S(1)} collective-permute-done((bf16[192,2048]{1,0:T(8,128)(2,1)S(1)}, bf16[192,2048]{1,0:T(8,128)(2,1)S(1)}, u32[]{:S(2)}, u32[]{:S(2)}) %collective-permute-start.10) | collective-permute-done | bytes 786464 | tf_op jit(solution)/shard_map/ppermute | solution.py:264
  66.0 0.9 broadcast_select_fusion.2
  67.6 1.5 %collective-permute-start.15 = (f32[2,192]{1,0:T(2,128)S(1)}, f32[2,192]{1,0:T(2,128)S(1)}, u32[]{:S(2)}, u32[]{:S(2)}) collective-permute-start(f32[2,192]{1,0:T(2,128)S(1)} %pad_maximum_fusion.1), channel_id=1, source_target_pairs={{0,12},{4,0},{8,4},{12,8},{1,13},{5,1},{9,5},{13,9},{2,14},{6,2},{... | collective-permute-start | bytes 4616 | tf_op jit(solution)/shard_map/ppermute | solution.py:387
  69.1 0.8 collective-permute-start.13
  69.9 1.8 %collective-permute-start.14 = (f32[2,192]{1,0:T(2,128)S(1)}, f32[2,192]{1,0:T(2,128)S(1)}, u32[]{:S(2)}, u32[]{:S(2)}) collective-permute-start(f32[2,192]{1,0:T(2,128)S(1)} %pad_maximum_fusion.1), channel_id=1, source_target_pairs={{0,8},{4,12},{8,0},{12,4},{1,9},{5,13},{9,1},{13,5},{2,10},{6,14},... | collective-permute-start | bytes 4616 | tf_op jit(solution)/shard_map/ppermute | solution.py:387
  72.4 1.5 %collective-permute-start.21 = (bf16[192,1536]{1,0:T(8,128)(2,1)S(1)}, bf16[192,1536]{1,0:T(8,128)(2,1)S(1)}, u32[]{:S(2)}, u32[]{:S(2)}) collective-permute-start(bf16[192,1536]{1,0:T(8,128)(2,1)S(1)} %slice.30), channel_id=1, source_target_pairs={{0,1},{1,0},{2,3},{3,2},{4,5},{5,4},{6,7},{7,6},{8,9},{9,8},{10,11... | collective-permute-start | bytes 1769480 | tf_op jit(solution)/shard_map/ppermute | solution.py:211
  74.5 5.1 %collective-permute-done.16 = bf16[192,512]{1,0:T(8,128)(2,1)S(1)} collective-permute-done((bf16[192,512]{1,0:T(8,128)(2,1)S(1)}, bf16[192,512]{1,0:T(8,128)(2,1)S(1)}, u32[]{:S(2)}, u32[]{:S(2)}) %collective-permute-start.16) | collective-permute-done | bytes 196640 | tf_op jit(solution)/shard_map/ppermute | solution.py:211
  81.2 1.9 %collective-permute-start.19 = (bf16[192,256]{1,0:T(8,128)(2,1)S(1)}, bf16[192,256]{1,0:T(8,128)(2,1)S(1)}, u32[]{:S(2)}, u32[]{:S(2)}) collective-permute-start(bf16[192,256]{1,0:T(8,128)(2,1)S(1)} %get-tuple-element.95), channel_id=1, source_target_pairs={{0,4},{4,0},{8,12},{12,8},{1,5},{5,1},{9,13},{13,9},{2,6},{6,2},{1... | collective-permute-start | bytes 294920 | tf_op jit(solution)/shard_map/ppermute | solution.py:202
  83.2 2.7 %collective-permute-done.19 = bf16[192,256]{1,0:T(8,128)(2,1)S(1)} collective-permute-done((bf16[192,256]{1,0:T(8,128)(2,1)S(1)}, bf16[192,256]{1,0:T(8,128)(2,1)S(1)}, u32[]{:S(2)}, u32[]{:S(2)}) %collective-permute-start.19) | collective-permute-done | bytes 98336 | tf_op jit(solution)/shard_map/ppermute | solution.py:202
  85.9 1.1 %collective-permute-start.20 = (bf16[192,256]{1,0:T(8,128)(2,1)S(1)}, bf16[192,256]{1,0:T(8,128)(2,1)S(1)}, u32[]{:S(2)}, u32[]{:S(2)}) collective-permute-start(bf16[192,256]{1,0:T(8,128)(2,1)S(1)} %fusion.23), channel_id=1, source_target_pairs={{0,8},{4,12},{8,0},{12,4},{1,9},{5,13},{9,1},{13,5},{2,10},{6,14},... | collective-permute-start | bytes 294920 | tf_op jit(solution)/shard_map/ppermute | solution.py:202
  87.1 4.4 %collective-permute-done.20 = bf16[192,256]{1,0:T(8,128)(2,1)S(1)} collective-permute-done((bf16[192,256]{1,0:T(8,128)(2,1)S(1)}, bf16[192,256]{1,0:T(8,128)(2,1)S(1)}, u32[]{:S(2)}, u32[]{:S(2)}) %collective-permute-start.20) | collective-permute-done | bytes 98336 | tf_op jit(solution)/shard_map/ppermute | solution.py:202
  92.7 2.3 %shard_map.99 = (f32[2048,256]{1,0:T(8,128)S(1)}, f32[256,2048]{1,0:T(8,128)S(1)}) custom-call(s32[2]{0:T(128)S(1)} %pad_add_fusion.table, bf16[192,2048]{1,0:T(8,128)(2,1)S(1)} %fusion.17.value_ref.early, bf16[192,2048]{1,0:T(8,128)(2,1)S(1)} %fusion.16.late, bf16[192,256]{1,0:T(8,128)(2,1)S(1)} %get-tuple-element.92.small_early, ...), custom_call_target="tpu_custom_call" | custom-call | flops 402653184 | bytes 5767168 | tf_op jit(solution)/shard_map/pallas_call | solution.py:145
  95.1 3.3 %collective-permute-done.23.small_late = bf16[192,384]{1,0:T(8,128)(2,1)S(1)} collective-permute-done((bf16[192,384]{1,0:T(8,128)(2,1)S(1)}, bf16[192,384]{1,0:T(8,128)(2,1)S(1)}, u32[]{:S(2)}, u32[]{:S(2)}) %collective-permute-start.23) | collective-permute-done | bytes 147488 | tf_op jit(solution)/shard_map/ppermute | solution.py:211
  98.4 4.2 %shard_map.100 = (f32[2048,256]{1,0:T(8,128)}, f32[256,2048]{1,0:T(8,128)}) custom-call(s32[2]{0:T(128)S(1)} %pad_add_fusion.table, f32[1,2048]{1,0:T(1,128)S(1)} %copy-done.1, f32[2048,256]{1,0:T(8,128)S(1)} %get-tuple-element.70.down_sum, f32[256,2048]{1,0:T(8,128)S(1)} %get-tuple-element.71.up_sum, bf16[192,2048]{1,0:T(8,128)(2,1)S(1)} %collective-permute-done.8.early, ...), custom_call_target="tpu_custom_call" | custom-call | flops 402653184 | bytes 11534336 | tf_op jit(solution)/shard_map/pallas_call | solution.py:145
  (87 shorter events, 11.5 us)
Async XLA Ops:
  0.6 22.3 %copy-start = (bf16[1,2048,256]{2,1,0:T(8,128)(2,1)S(1)}, bf16[1,2048,256]{2,1,0:T(8,128)(2,1)}, u32[]{:S(2)}) copy-start(bf16[1,2048,256]{2,1,0:T(8,128)(2,1)} %param.12) | copy-start | bytes 3145732
  0.6 14.3 %collective-permute-start = (bf16[192,2048]{1,0:T(8,128)(2,1)}, bf16[192,2048]{1,0:T(8,128)(2,1)}, u32[]{:S(2)}, u32[]{:S(2)}) collective-permute-start(bf16[192,2048]{1,0:T(8,128)(2,1)} %param.9), channel_id=1, source_target_pairs={{0,6},{4,10},{8,14},{1,7},{5,11},{9,15},{16,22},{20,26},{24,30},{1... | collective-permute-start | bytes 2359304 | tf_op jit(solution)/shard_map/ppermute | solution.py:280
  6.1 14.0 %collective-permute-start.2 = (bf16[192,2048]{1,0:T(8,128)(2,1)}, bf16[192,2048]{1,0:T(8,128)(2,1)}, u32[]{:S(2)}, u32[]{:S(2)}) collective-permute-start(bf16[192,2048]{1,0:T(8,128)(2,1)} %param.9), channel_id=1, source_target_pairs={{6,2},{10,6},{14,10},{7,3},{11,7},{15,11},{22,18},{26,22},{30,26},... | collective-permute-start | bytes 2359304 | tf_op jit(solution)/shard_map/ppermute | solution.py:264
  9.1 5.2 %copy-start.6 = (f32[4]{0:T(128)S(1)}, f32[4]{0:T(128)}, u32[]{:S(2)}) copy-start(f32[4]{0:T(128)} %param.14) | copy-start | bytes 52
  16.4 5.8 %copy-start.3 = (bf16[192,2048]{1,0:T(8,128)(2,1)S(1)}, bf16[192,2048]{1,0:T(8,128)(2,1)}, u32[]{:S(2)}) copy-start(bf16[192,2048]{1,0:T(8,128)(2,1)} %param.8) | copy-start | bytes 2359300
  16.4 6.0 %copy-start.2 = (bf16[1,256,2048]{2,1,0:T(8,128)(2,1)S(1)}, bf16[1,256,2048]{2,1,0:T(8,128)(2,1)}, u32[]{:S(2)}) copy-start(bf16[1,256,2048]{2,1,0:T(8,128)(2,1)} %param.13) | copy-start | bytes 3145732
  16.4 14.0 %collective-permute-start.1 = (bf16[192,2048]{1,0:T(8,128)(2,1)S(1)}, bf16[192,2048]{1,0:T(8,128)(2,1)S(1)}, u32[]{:S(2)}, u32[]{:S(2)}) collective-permute-start(bf16[192,2048]{1,0:T(8,128)(2,1)S(1)} %add_convert_fusion.5), channel_id=1, source_target_pairs={{0,4},{6,10},{10,14},{1,5},{7,11},{11,15},{16,20},{22,26},{26,30},... | collective-permute-start | bytes 2359304 | tf_op jit(solution)/shard_map/ppermute | solution.py:264
  21.4 13.3 %collective-permute-start.3 = (bf16[192,2048]{1,0:T(8,128)(2,1)S(1)}, bf16[192,2048]{1,0:T(8,128)(2,1)S(1)}, u32[]{:S(2)}, u32[]{:S(2)}) collective-permute-start(bf16[192,2048]{1,0:T(8,128)(2,1)S(1)} %add_convert_fusion.4), channel_id=1, source_target_pairs={{12,8},{6,2},{10,6},{13,9},{7,3},{11,7},{28,24},{22,18},{26,22},{2... | collective-permute-start | bytes 2359304 | tf_op jit(solution)/shard_map/ppermute | solution.py:264
  28.8 7.0 %collective-permute-start.6 = (bf16[208,256]{1,0:T(8,128)(2,1)S(1)}, bf16[208,256]{1,0:T(8,128)(2,1)S(1)}, u32[]{:S(2)}, u32[]{:S(2)}) collective-permute-start(bf16[208,256]{1,0:T(8,128)(2,1)S(1)} %convert_element_type.139), channel_id=1, source_target_pairs={{0,4},{4,0},{8,12},{12,8},{1,5},{5,1},{9,13},{13,9},{2,6},{6,2},{1... | collective-permute-start | bytes 319496 | tf_op jit(solution)/shard_map/ppermute | solution.py:202
  28.8 31.3 %collective-permute-start.8 = (bf16[192,2048]{1,0:T(8,128)(2,1)S(1)}, bf16[192,2048]{1,0:T(8,128)(2,1)S(1)}, u32[]{:S(2)}, u32[]{:S(2)}) collective-permute-start(bf16[192,2048]{1,0:T(8,128)(2,1)S(1)} %fusion.17.value_ref.early), channel_id=1, source_target_pairs={{0,1},{1,0},{2,3},{3,2},{4,5},{5,4},{6,7},{7,6},{8,9},{9,8},{10,11... | collective-permute-start | bytes 2359304 | tf_op jit(solution)/shard_map/ppermute | solution.py:211
  30.8 14.8 %collective-permute-start.4 = (bf16[192,2048]{1,0:T(8,128)(2,1)S(1)}, bf16[192,2048]{1,0:T(8,128)(2,1)S(1)}, u32[]{:S(2)}, u32[]{:S(2)}) collective-permute-start(bf16[192,2048]{1,0:T(8,128)(2,1)S(1)} %add_convert_fusion.3), channel_id=1, source_target_pairs={{0,4},{4,8},{10,14},{1,5},{5,9},{11,15},{16,20},{20,24},{26,30},{1... | collective-permute-start | bytes 2359304 | tf_op jit(solution)/shard_map/ppermute | solution.py:264
  35.1 16.4 %collective-permute-start.5 = (bf16[192,2048]{1,0:T(8,128)(2,1)S(1)}, bf16[192,2048]{1,0:T(8,128)(2,1)S(1)}, u32[]{:S(2)}, u32[]{:S(2)}) collective-permute-start(bf16[192,2048]{1,0:T(8,128)(2,1)S(1)} %add_convert_fusion.2), channel_id=1, source_target_pairs={{8,4},{12,8},{6,2},{9,5},{13,9},{7,3},{24,20},{28,24},{22,18},{25,... | collective-permute-start | bytes 2359304 | tf_op jit(solution)/shard_map/ppermute | solution.py:264
  35.9 18.6 %collective-permute-start.7 = (bf16[208,256]{1,0:T(8,128)(2,1)S(1)}, bf16[208,256]{1,0:T(8,128)(2,1)S(1)}, u32[]{:S(2)}, u32[]{:S(2)}) collective-permute-start(bf16[208,256]{1,0:T(8,128)(2,1)S(1)} %convert_element_type.141), channel_id=1, source_target_pairs={{0,8},{4,12},{8,0},{12,4},{1,9},{5,13},{9,1},{13,5},{2,10},{6,14},... | collective-permute-start | bytes 319496 | tf_op jit(solution)/shard_map/ppermute | solution.py:202
  46.0 19.0 %collective-permute-start.9 = (bf16[192,2048]{1,0:T(8,128)(2,1)S(1)}, bf16[192,2048]{1,0:T(8,128)(2,1)S(1)}, u32[]{:S(2)}, u32[]{:S(2)}) collective-permute-start(bf16[192,2048]{1,0:T(8,128)(2,1)S(1)} %add_convert_fusion.1), channel_id=1, source_target_pairs={{0,4},{4,8},{8,12},{1,5},{5,9},{9,13},{16,20},{20,24},{24,28},{17,... | collective-permute-start | bytes 2359304 | tf_op jit(solution)/shard_map/ppermute | solution.py:264
  51.7 14.3 %collective-permute-start.10 = (bf16[192,2048]{1,0:T(8,128)(2,1)S(1)}, bf16[192,2048]{1,0:T(8,128)(2,1)S(1)}, u32[]{:S(2)}, u32[]{:S(2)}) collective-permute-start(bf16[192,2048]{1,0:T(8,128)(2,1)S(1)} %add_convert_fusion), channel_id=1, source_target_pairs={{4,0},{8,4},{12,8},{5,1},{9,5},{13,9},{20,16},{24,20},{28,24},{21,... | collective-permute-start | bytes 2359304 | tf_op jit(solution)/shard_map/ppermute | solution.py:264
  54.9 5.3 %copy-start.5 = (s32[192]{0:T(256)S(1)}, s32[192]{0:T(256)}, u32[]{:S(2)}) copy-start(s32[192]{0:T(256)} %param.15) | copy-start | bytes 2308
  60.1 1.2 %copy-start.1 = (f32[1,2048]{1,0:T(1,128)S(1)}, f32[1,2048]{1,0:T(1,128)}, u32[]{:S(2)}) copy-start(f32[1,2048]{1,0:T(1,128)} %gain_ref.1) | copy-start | bytes 24580
  60.3 4.7 %collective-permute-start.11 = (bf16[192,256]{1,0:T(8,128)(2,1)S(1)}, bf16[192,256]{1,0:T(8,128)(2,1)S(1)}, u32[]{:S(2)}, u32[]{:S(2)}) collective-permute-start(bf16[192,256]{1,0:T(8,128)(2,1)S(1)} %get-tuple-element.86), channel_id=1, source_target_pairs={{0,1},{1,0},{2,3},{3,2},{4,5},{5,4},{6,7},{7,6},{8,9},{9,8},{10,11... | collective-permute-start | bytes 294920 | tf_op jit(solution)/shard_map/ppermute | solution.py:211
  62.1 5.1 %collective-permute-start.12 = (bf16[192,2048]{1,0:T(8,128)(2,1)S(1)}, bf16[192,2048]{1,0:T(8,128)(2,1)S(1)}, u32[]{:S(2)}, u32[]{:S(2)}) collective-permute-start(bf16[192,2048]{1,0:T(8,128)(2,1)S(1)} %get-tuple-element.93), channel_id=1, source_target_pairs={{0,2},{2,0},{1,3},{3,1},{4,6},{6,4},{5,7},{7,5},{8,10},{10,8},{9,1... | collective-permute-start | bytes 2359304 | tf_op jit(solution)/shard_map/ppermute | solution.py:364
  67.1 12.6 %copy-start.4 = (bf16[192,2048]{1,0:T(8,128)(2,1)S(1)}, bf16[192,2048]{1,0:T(8,128)(2,1)}, u32[]{:S(2)}) copy-start(bf16[192,2048]{1,0:T(8,128)(2,1)} %param.9) | copy-start | bytes 2359300
  67.1 12.6 %collective-permute-start.17 = (bf16[192,2048]{1,0:T(8,128)(2,1)S(1)}, bf16[192,2048]{1,0:T(8,128)(2,1)S(1)}, u32[]{:S(2)}, u32[]{:S(2)}) collective-permute-start(bf16[192,2048]{1,0:T(8,128)(2,1)S(1)} %broadcast_select_fusion.1), channel_id=1, source_target_pairs={{0,2},{2,0},{1,3},{3,1},{4,6},{6,4},{5,7},{7,5},{8,10},{10,8},{9,1... | collective-permute-start | bytes 2359304 | tf_op jit(solution)/shard_map/ppermute | solution.py:376
  67.6 4.8 %collective-permute-start.15 = (f32[2,192]{1,0:T(2,128)S(1)}, f32[2,192]{1,0:T(2,128)S(1)}, u32[]{:S(2)}, u32[]{:S(2)}) collective-permute-start(f32[2,192]{1,0:T(2,128)S(1)} %pad_maximum_fusion.1), channel_id=1, source_target_pairs={{0,12},{4,0},{8,4},{12,8},{1,13},{5,1},{9,5},{13,9},{2,14},{6,2},{... | collective-permute-start | bytes 4616 | tf_op jit(solution)/shard_map/ppermute | solution.py:387
  69.1 5.4 %collective-permute-start.13 = (f32[2,192]{1,0:T(2,128)S(1)}, f32[2,192]{1,0:T(2,128)S(1)}, u32[]{:S(2)}, u32[]{:S(2)}) collective-permute-start(f32[2,192]{1,0:T(2,128)S(1)} %pad_maximum_fusion.1), channel_id=1, source_target_pairs={{0,4},{4,8},{8,12},{12,0},{1,5},{5,9},{9,13},{13,1},{2,6},{6,10},{... | collective-permute-start | bytes 4616 | tf_op jit(solution)/shard_map/ppermute | solution.py:387
  69.9 4.6 %collective-permute-start.14 = (f32[2,192]{1,0:T(2,128)S(1)}, f32[2,192]{1,0:T(2,128)S(1)}, u32[]{:S(2)}, u32[]{:S(2)}) collective-permute-start(f32[2,192]{1,0:T(2,128)S(1)} %pad_maximum_fusion.1), channel_id=1, source_target_pairs={{0,8},{4,12},{8,0},{12,4},{1,9},{5,13},{9,1},{13,5},{2,10},{6,14},... | collective-permute-start | bytes 4616 | tf_op jit(solution)/shard_map/ppermute | solution.py:387
  71.8 7.9 %collective-permute-start.16 = (bf16[192,512]{1,0:T(8,128)(2,1)S(1)}, bf16[192,512]{1,0:T(8,128)(2,1)S(1)}, u32[]{:S(2)}, u32[]{:S(2)}) collective-permute-start(bf16[192,512]{1,0:T(8,128)(2,1)S(1)} %slice.29), channel_id=1, source_target_pairs={{0,1},{1,0},{2,3},{3,2},{4,5},{5,4},{6,7},{7,6},{8,9},{9,8},{10,11... | collective-permute-start | bytes 589832 | tf_op jit(solution)/shard_map/ppermute | solution.py:211
  72.4 19.3 %collective-permute-start.21 = (bf16[192,1536]{1,0:T(8,128)(2,1)S(1)}, bf16[192,1536]{1,0:T(8,128)(2,1)S(1)}, u32[]{:S(2)}, u32[]{:S(2)}) collective-permute-start(bf16[192,1536]{1,0:T(8,128)(2,1)S(1)} %slice.30), channel_id=1, source_target_pairs={{0,1},{1,0},{2,3},{3,2},{4,5},{5,4},{6,7},{7,6},{8,9},{9,8},{10,11... | collective-permute-start | bytes 1769480 | tf_op jit(solution)/shard_map/ppermute | solution.py:211
  81.2 4.7 %collective-permute-start.19 = (bf16[192,256]{1,0:T(8,128)(2,1)S(1)}, bf16[192,256]{1,0:T(8,128)(2,1)S(1)}, u32[]{:S(2)}, u32[]{:S(2)}) collective-permute-start(bf16[192,256]{1,0:T(8,128)(2,1)S(1)} %get-tuple-element.95), channel_id=1, source_target_pairs={{0,4},{4,0},{8,12},{12,8},{1,5},{5,1},{9,13},{13,9},{2,6},{6,2},{1... | collective-permute-start | bytes 294920 | tf_op jit(solution)/shard_map/ppermute | solution.py:202
  83.1 4.0 %collective-permute-start.18 = (f32[192]{0:T(256)S(1)}, f32[192]{0:T(256)S(1)}, u32[]{:S(2)}, u32[]{:S(2)}) collective-permute-start(f32[192]{0:T(256)S(1)} %bitcast.47), channel_id=1, source_target_pairs={{0,2},{2,0},{1,3},{3,1},{4,6},{6,4},{5,7},{7,5},{8,10},{10,8},{9,1... | collective-permute-start | bytes 2312 | tf_op jit(solution)/shard_map/ppermute | solution.py:404
  85.9 5.6 %collective-permute-start.20 = (bf16[192,256]{1,0:T(8,128)(2,1)S(1)}, bf16[192,256]{1,0:T(8,128)(2,1)S(1)}, u32[]{:S(2)}, u32[]{:S(2)}) collective-permute-start(bf16[192,256]{1,0:T(8,128)(2,1)S(1)} %fusion.23), channel_id=1, source_target_pairs={{0,8},{4,12},{8,0},{12,4},{1,9},{5,13},{9,1},{13,5},{2,10},{6,14},... | collective-permute-start | bytes 294920 | tf_op jit(solution)/shard_map/ppermute | solution.py:202
  91.7 3.2 %collective-permute-start.22 = (bf16[192,2048]{1,0:T(8,128)(2,1)S(1)}, bf16[192,2048]{1,0:T(8,128)(2,1)S(1)}, u32[]{:S(2)}, u32[]{:S(2)}) collective-permute-start(bf16[192,2048]{1,0:T(8,128)(2,1)S(1)} %constant_dynamic-update-slice_fusion), channel_id=1, source_target_pairs={{0,2},{2,0},{1,3},{3,1},{4,6},{6,4},{5,7},{7,5},{8,10},{10,8},{9,1... | collective-permute-start | bytes 2359304 | tf_op jit(solution)/shard_map/ppermute | solution.py:435
  92.1 6.3 %collective-permute-start.23 = (bf16[192,384]{1,0:T(8,128)(2,1)S(1)}, bf16[192,384]{1,0:T(8,128)(2,1)S(1)}, u32[]{:S(2)}, u32[]{:S(2)}) collective-permute-start(bf16[192,384]{1,0:T(8,128)(2,1)S(1)} %pad_maximum_fusion), channel_id=1, source_target_pairs={{0,1},{1,0},{2,3},{3,2},{4,5},{5,4},{6,7},{7,6},{8,9},{9,8},{10,11... | collective-permute-start | bytes 442376 | tf_op jit(solution)/shard_map/ppermute | solution.py:211

commit v20 on v18

--- a/solution.py
+++ b/solution.py
@@ -371,7 +371,7 @@
     half = width // 2 if width % 256 == 0 else width
     exchanged = jnp.where(is_first, hidden, pulled_here)
     first_halves = with_other_replicas(exchanged[:, :half])[1:]
-    second_halves = with_other_replicas(exchanged[:, half:])[1:] if half < width else None
+    second_halves = None
     swapped = [
         lax.ppermute(jnp.where(is_first, hidden, other), "section", swap) for other in early_all[1:]
     ]
@@ -401,6 +401,10 @@
         (hidden_on_second.astype(F32) * gain_row).astype(BF16),
     )
     rank_late = jnp.where(is_first, times_up_transposed(late), times_down(late))
+    if half < width:
+        second_halves = with_other_replicas(
+            lax.optimization_barrier((exchanged[:, half:], rank_late))[0]
+        )[1:]
     inv_on_second = lax.ppermute(
         lax.optimization_barrier((inv_second[:, 0], rank_late))[0], "section", swap
     )[:, None]

time: 103 us -> 105 us (1.019)
  waiting for transfers between devices: 20.4 us -> 24.3 us
    ppermute x5, waiting for transfers between devices: 10.2 us -> 12.8 us  [with_other_replicas(): lax.ppermute(value, ('section', 'replica'), [(s * count + r, s * count +...]
    ppermute x3, waiting for transfers between devices: 1.31 us -> 2.83 us  [on_device(): lax.ppermute(row_sums, 'tensor', [(z, (z + step) % count) for z in everyo...]
  transfers between devices with their start and end apart: 24 -> 24, of which waited for: 9 -> 10; matrix products, arithmetic and copies ran while one was open for 12% -> 11% of each run, Pallas kernels for 23% -> 22%
where the time goes in v20:
time: 105 us
  starting transfers between devices  39.5 us (38%)
  Pallas kernels  27.3 us (26%)
  waiting for transfers between devices  24.3 us (23%)
  other arithmetic  9.19 us (9%)
  matrix products  2.96 us (3%)
  between operations  1.19 us (1%)
    pallas_call x4, Pallas kernels, block_product(): pl.pallas_call(functools.partial(block_kernel, blocks=blocks, tile=tile,...  20.9 us
    ppermute x7, starting transfers between devices, line(): return lax.ppermute(value, ('tensor', 'section'), pairs)  17.3 us
    ppermute x5, waiting for transfers between devices, with_other_replicas(): lax.ppermute(value, ('section', 'replica'), [(s * count + r, s * count +...  12.8 us
    ppermute x4, starting transfers between devices, sum_step(): other = lax.ppermute(value.astype(wire), 'tensor', pairs)  8.45 us
    ppermute x4, waiting for transfers between devices, sum_step(): other = lax.ppermute(value.astype(wire), 'tensor', pairs)  7.24 us
    pallas_call x2, Pallas kernels, gradient_call(): pl.pallas_call(kernel, grid_spec=pltpu.PrefetchScalarGridSpec(num_scalar_...  6.46 us
    ppermute x1, starting transfers between devices, on_device(): lax.ppermute(cotangent, ('tensor', 'section'), [(2 * z, 2 * (z + 1) + 1)...  5.44 us
    ppermute x3, starting transfers between devices, on_device(): lax.ppermute(row_sums, 'tensor', [(z, (z + step) % count) for z in everyo...  4.1 us
  transfers between devices with their start and end apart: 24, of which 10 were waited for; matrix products, arithmetic and copies ran while one was open for 11% of the time, Pallas kernels for 22%

profile of v20, /device:TPU:0, one launch (start us, length us, event | category | flops | bytes accessed | tf_op | source)
XLA Modules:
  0.0 105.0 jit_solution(12263273155072140060)
XLA Ops:
  0.6 5.4 %collective-permute-start = (bf16[192,2048]{1,0:T(8,128)(2,1)}, bf16[192,2048]{1,0:T(8,128)(2,1)}, u32[]{:S(2)}, u32[]{:S(2)}) collective-permute-start(bf16[192,2048]{1,0:T(8,128)(2,1)} %param.9), channel_id=1, source_target_pairs={{0,6},{4,10},{8,14},{1,7},{5,11},{9,15},{16,22},{20,26},{24,30},{1... | collective-permute-start | bytes 2359304 | tf_op jit(solution)/shard_map/ppermute | solution.py:280
  6.1 1.6 %collective-permute-start.2 = (bf16[192,2048]{1,0:T(8,128)(2,1)}, bf16[192,2048]{1,0:T(8,128)(2,1)}, u32[]{:S(2)}, u32[]{:S(2)}) collective-permute-start(bf16[192,2048]{1,0:T(8,128)(2,1)} %param.9), channel_id=1, source_target_pairs={{6,2},{10,6},{14,10},{7,3},{11,7},{15,11},{22,18},{26,22},{30,26},... | collective-permute-start | bytes 2359304 | tf_op jit(solution)/shard_map/ppermute | solution.py:264
  7.6 1.4 %fusion.17.value_ref.early = bf16[192,2048]{1,0:T(8,128)(2,1)S(1)} fusion(bf16[192,2048]{1,0:T(8,128)(2,1)} %param.9, bf16[192,2048]{1,0:T(8,128)(2,1)} %param.8, f32[2048]{0:T(1024)} %bitcast.38, pred[]{:T(512)S(6)} %eq.20), kind=kLoop, calls=%fused_computation.35 | loop fusion | flops 1572864 | bytes 2367489 | tf_op jit(solution)/shard_map/jit(_where)/select_n | solution.py:267
  9.1 5.2 %shard_map.95 = f32[192,2048]{1,0:T(8,128)S(1)} custom-call(s32[2]{0:T(128)S(1)} %pad_add_fusion.table, bf16[192,2048]{1,0:T(8,128)(2,1)S(1)} %fusion.17.value_ref.early, bf16[2048,8192]{1,0:T(8,128)(2,1)} %bitcast.41), custom_call_target="tpu_custom_call" | custom-call | flops 6442450944 | bytes 8388608 | tf_op jit(solution)/shard_map/pallas_call | solution.py:72
  15.0 1.4 %add_convert_fusion.5 = bf16[192,2048]{1,0:T(8,128)(2,1)S(1)} fusion(bf16[192,2048]{1,0:T(8,128)(2,1)} %collective-permute-done, f32[192,2048]{1,0:T(8,128)S(1)} %shard_map.95, pred[]{:T(512)S(6)} %eq.20), kind=kLoop, calls=%fused_computation.22 | loop fusion | flops 1572864 | bytes 3145729 | tf_op jit(solution)/shard_map/convert_element_type | solution.py:328
  16.4 3.7 %collective-permute-start.1 = (bf16[192,2048]{1,0:T(8,128)(2,1)S(1)}, bf16[192,2048]{1,0:T(8,128)(2,1)S(1)}, u32[]{:S(2)}, u32[]{:S(2)}) collective-permute-start(bf16[192,2048]{1,0:T(8,128)(2,1)S(1)} %add_convert_fusion.5), channel_id=1, source_target_pairs={{0,4},{6,10},{10,14},{1,5},{7,11},{11,15},{16,20},{22,26},{26,30},... | collective-permute-start | bytes 2359304 | tf_op jit(solution)/shard_map/ppermute | solution.py:264
  20.1 1.3 %add_convert_fusion.4 = bf16[192,2048]{1,0:T(8,128)(2,1)S(1)} fusion(bf16[192,2048]{1,0:T(8,128)(2,1)} %collective-permute-done.2, f32[192,2048]{1,0:T(8,128)S(1)} %shard_map.95, pred[]{:T(512)S(6)} %eq.20), kind=kLoop, calls=%fused_computation.21 | loop fusion | flops 1572864 | bytes 3145729 | tf_op jit(solution)/shard_map/convert_element_type | solution.py:328
  23.5 5.2 %shard_map.96 = f32[192,2048]{1,0:T(8,128)S(1)} custom-call(s32[2]{0:T(128)S(1)} %pad_add_fusion.table, bf16[192,2048]{1,0:T(8,128)(2,1)S(1)} %select_select_fusion.2.value_ref, bf16[2048,8192]{1,0:T(8,128)(2,1)} %bitcast.42), custom_call_target="tpu_custom_call" | custom-call | flops 6442450944 | bytes 8388608 | tf_op jit(solution)/shard_map/pallas_call | solution.py:72
  28.8 1.6 %collective-permute-start.8 = (bf16[192,2048]{1,0:T(8,128)(2,1)S(1)}, bf16[192,2048]{1,0:T(8,128)(2,1)S(1)}, u32[]{:S(2)}, u32[]{:S(2)}) collective-permute-start(bf16[192,2048]{1,0:T(8,128)(2,1)S(1)} %fusion.17.value_ref.early), channel_id=1, source_target_pairs={{0,1},{1,0},{2,3},{3,2},{4,5},{5,4},{6,7},{7,6},{8,9},{9,8},{10,11... | collective-permute-start | bytes 2359304 | tf_op jit(solution)/shard_map/ppermute | solution.py:211
  30.8 3.9 %collective-permute-start.4 = (bf16[192,2048]{1,0:T(8,128)(2,1)S(1)}, bf16[192,2048]{1,0:T(8,128)(2,1)S(1)}, u32[]{:S(2)}, u32[]{:S(2)}) collective-permute-start(bf16[192,2048]{1,0:T(8,128)(2,1)S(1)} %add_convert_fusion.3), channel_id=1, source_target_pairs={{0,4},{4,8},{10,14},{1,5},{5,9},{11,15},{16,20},{20,24},{26,30},{1... | collective-permute-start | bytes 2359304 | tf_op jit(solution)/shard_map/ppermute | solution.py:264
  35.9 4.3 %collective-permute-start.7 = (bf16[208,256]{1,0:T(8,128)(2,1)S(1)}, bf16[208,256]{1,0:T(8,128)(2,1)S(1)}, u32[]{:S(2)}, u32[]{:S(2)}) collective-permute-start(bf16[208,256]{1,0:T(8,128)(2,1)S(1)} %convert_element_type.141), channel_id=1, source_target_pairs={{0,8},{4,12},{8,0},{12,4},{1,9},{5,13},{9,1},{13,5},{2,10},{6,14},... | collective-permute-start | bytes 319496 | tf_op jit(solution)/shard_map/ppermute | solution.py:202
  40.4 5.2 %shard_map.97 = f32[192,2048]{1,0:T(8,128)S(1)} custom-call(s32[2]{0:T(128)S(1)} %pad_add_fusion.table, bf16[192,2048]{1,0:T(8,128)(2,1)S(1)} %select_select_fusion.1.value_ref, bf16[2048,8192]{1,0:T(8,128)(2,1)} %bitcast.43), custom_call_target="tpu_custom_call" | custom-call | flops 6442450944 | bytes 8388608 | tf_op jit(solution)/shard_map/pallas_call | solution.py:72
  46.0 5.4 %collective-permute-start.9 = (bf16[192,2048]{1,0:T(8,128)(2,1)S(1)}, bf16[192,2048]{1,0:T(8,128)(2,1)S(1)}, u32[]{:S(2)}, u32[]{:S(2)}) collective-permute-start(bf16[192,2048]{1,0:T(8,128)(2,1)S(1)} %add_convert_fusion.1), channel_id=1, source_target_pairs={{0,4},{4,8},{8,12},{1,5},{5,9},{9,13},{16,20},{20,24},{24,28},{17,... | collective-permute-start | bytes 2359304 | tf_op jit(solution)/shard_map/ppermute | solution.py:264
  51.7 1.3 %collective-permute-start.10 = (bf16[192,2048]{1,0:T(8,128)(2,1)S(1)}, bf16[192,2048]{1,0:T(8,128)(2,1)S(1)}, u32[]{:S(2)}, u32[]{:S(2)}) collective-permute-start(bf16[192,2048]{1,0:T(8,128)(2,1)S(1)} %add_convert_fusion), channel_id=1, source_target_pairs={{4,0},{8,4},{12,8},{5,1},{9,5},{13,9},{20,16},{24,20},{28,24},{21,... | collective-permute-start | bytes 2359304 | tf_op jit(solution)/shard_map/ppermute | solution.py:264
  53.0 1.5 %collective-permute-done.7 = bf16[208,256]{1,0:T(8,128)(2,1)S(1)} collective-permute-done((bf16[208,256]{1,0:T(8,128)(2,1)S(1)}, bf16[208,256]{1,0:T(8,128)(2,1)S(1)}, u32[]{:S(2)}, u32[]{:S(2)}) %collective-permute-start.7) | collective-permute-done | bytes 106528 | tf_op jit(solution)/shard_map/ppermute | solution.py:202
  54.9 5.2 %shard_map.98 = f32[192,2048]{1,0:T(8,128)S(1)} custom-call(s32[2]{0:T(128)S(1)} %pad_add_fusion.table, bf16[192,2048]{1,0:T(8,128)(2,1)S(1)} %select_select_fusion.value_ref, bf16[2048,8192]{1,0:T(8,128)(2,1)} %bitcast.44), custom_call_target="tpu_custom_call" | custom-call | flops 6442450944 | bytes 8388608 | tf_op jit(solution)/shard_map/pallas_call | solution.py:72
  61.3 0.8 multiply_convert_fusion.1
  62.2 2.8 %collective-permute-done.11.small_early = bf16[192,256]{1,0:T(8,128)(2,1)S(1)} collective-permute-done((bf16[192,256]{1,0:T(8,128)(2,1)S(1)}, bf16[192,256]{1,0:T(8,128)(2,1)S(1)}, u32[]{:S(2)}, u32[]{:S(2)}) %collective-permute-start.11) | collective-permute-done | bytes 98336 | tf_op jit(solution)/shard_map/ppermute | solution.py:211
  65.0 1.1 %collective-permute-done.10 = bf16[192,2048]{1,0:T(8,128)(2,1)S(1)} collective-permute-done((bf16[192,2048]{1,0:T(8,128)(2,1)S(1)}, bf16[192,2048]{1,0:T(8,128)(2,1)S(1)}, u32[]{:S(2)}, u32[]{:S(2)}) %collective-permute-start.10) | collective-permute-done | bytes 786464 | tf_op jit(solution)/shard_map/ppermute | solution.py:264
  66.0 0.9 broadcast_select_fusion.2
  68.3 1.5 %collective-permute-start.15 = (f32[2,192]{1,0:T(2,128)S(1)}, f32[2,192]{1,0:T(2,128)S(1)}, u32[]{:S(2)}, u32[]{:S(2)}) collective-permute-start(f32[2,192]{1,0:T(2,128)S(1)} %pad_maximum_fusion.1), channel_id=1, source_target_pairs={{0,12},{4,0},{8,4},{12,8},{1,13},{5,1},{9,5},{13,9},{2,14},{6,2},{... | collective-permute-start | bytes 4616 | tf_op jit(solution)/shard_map/ppermute | solution.py:387
  70.6 1.8 %collective-permute-start.14 = (f32[2,192]{1,0:T(2,128)S(1)}, f32[2,192]{1,0:T(2,128)S(1)}, u32[]{:S(2)}, u32[]{:S(2)}) collective-permute-start(f32[2,192]{1,0:T(2,128)S(1)} %pad_maximum_fusion.1), channel_id=1, source_target_pairs={{0,8},{4,12},{8,0},{12,4},{1,9},{5,13},{9,1},{13,5},{2,10},{6,14},... | collective-permute-start | bytes 4616 | tf_op jit(solution)/shard_map/ppermute | solution.py:387
  72.4 2.8 %collective-permute-done.13 = f32[2,192]{1,0:T(2,128)S(1)} collective-permute-done((f32[2,192]{1,0:T(2,128)S(1)}, f32[2,192]{1,0:T(2,128)S(1)}, u32[]{:S(2)}, u32[]{:S(2)}) %collective-permute-start.13) | collective-permute-done | bytes 1568 | tf_op jit(solution)/shard_map/ppermute | solution.py:387
  75.2 3.6 %collective-permute-done.16 = bf16[192,1024]{1,0:T(8,128)(2,1)S(1)} collective-permute-done((bf16[192,1024]{1,0:T(8,128)(2,1)S(1)}, bf16[192,1024]{1,0:T(8,128)(2,1)S(1)}, u32[]{:S(2)}, u32[]{:S(2)}) %collective-permute-start.16) | collective-permute-done | bytes 393248 | tf_op jit(solution)/shard_map/ppermute | solution.py:211
  80.4 2.1 %collective-permute-start.19 = (bf16[192,256]{1,0:T(8,128)(2,1)S(1)}, bf16[192,256]{1,0:T(8,128)(2,1)S(1)}, u32[]{:S(2)}, u32[]{:S(2)}) collective-permute-start(bf16[192,256]{1,0:T(8,128)(2,1)S(1)} %get-tuple-element.99), channel_id=1, source_target_pairs={{0,4},{4,0},{8,12},{12,8},{1,5},{5,1},{9,13},{13,9},{2,6},{6,2},{1... | collective-permute-start | bytes 294920 | tf_op jit(solution)/shard_map/ppermute | solution.py:202
  83.2 2.0 %collective-permute-done.19 = bf16[192,256]{1,0:T(8,128)(2,1)S(1)} collective-permute-done((bf16[192,256]{1,0:T(8,128)(2,1)S(1)}, bf16[192,256]{1,0:T(8,128)(2,1)S(1)}, u32[]{:S(2)}, u32[]{:S(2)}) %collective-permute-start.19) | collective-permute-done | bytes 98336 | tf_op jit(solution)/shard_map/ppermute | solution.py:202
  85.1 2.0 %collective-permute-start.20 = (bf16[192,256]{1,0:T(8,128)(2,1)S(1)}, bf16[192,256]{1,0:T(8,128)(2,1)S(1)}, u32[]{:S(2)}, u32[]{:S(2)}) collective-permute-start(bf16[192,256]{1,0:T(8,128)(2,1)S(1)} %fusion.23), channel_id=1, source_target_pairs={{0,8},{4,12},{8,0},{12,4},{1,9},{5,13},{9,1},{13,5},{2,10},{6,14},... | collective-permute-start | bytes 294920 | tf_op jit(solution)/shard_map/ppermute | solution.py:202
  87.2 3.8 %collective-permute-done.20 = bf16[192,256]{1,0:T(8,128)(2,1)S(1)} collective-permute-done((bf16[192,256]{1,0:T(8,128)(2,1)S(1)}, bf16[192,256]{1,0:T(8,128)(2,1)S(1)}, u32[]{:S(2)}, u32[]{:S(2)}) %collective-permute-start.20) | collective-permute-done | bytes 98336 | tf_op jit(solution)/shard_map/ppermute | solution.py:202
  91.1 3.0 %collective-permute-done.21 = bf16[192,1024]{1,0:T(8,128)(2,1)S(1)} collective-permute-done((bf16[192,1024]{1,0:T(8,128)(2,1)S(1)}, bf16[192,1024]{1,0:T(8,128)(2,1)S(1)}, u32[]{:S(2)}, u32[]{:S(2)}) %collective-permute-start.21) | collective-permute-done | bytes 393248 | tf_op jit(solution)/shard_map/ppermute | solution.py:211
  95.1 2.3 %shard_map.99 = (f32[2048,256]{1,0:T(8,128)S(1)}, f32[256,2048]{1,0:T(8,128)S(1)}) custom-call(s32[2]{0:T(128)S(1)} %pad_add_fusion.table, bf16[192,2048]{1,0:T(8,128)(2,1)S(1)} %fusion.17.value_ref.early, bf16[192,2048]{1,0:T(8,128)(2,1)S(1)} %fusion.16.late, bf16[192,256]{1,0:T(8,128)(2,1)S(1)} %get-tuple-element.96.small_early, ...), custom_call_target="tpu_custom_call" | custom-call | flops 402653184 | bytes 5767168 | tf_op jit(solution)/shard_map/pallas_call | solution.py:145
  97.5 3.3 %collective-permute-done.23.small_late = bf16[192,384]{1,0:T(8,128)(2,1)S(1)} collective-permute-done((bf16[192,384]{1,0:T(8,128)(2,1)S(1)}, bf16[192,384]{1,0:T(8,128)(2,1)S(1)}, u32[]{:S(2)}, u32[]{:S(2)}) %collective-permute-start.23) | collective-permute-done | bytes 147488 | tf_op jit(solution)/shard_map/ppermute | solution.py:211
  100.8 4.2 %shard_map.100 = (f32[2048,256]{1,0:T(8,128)}, f32[256,2048]{1,0:T(8,128)}) custom-call(s32[2]{0:T(128)S(1)} %pad_add_fusion.table, f32[1,2048]{1,0:T(1,128)S(1)} %copy-done.1, f32[2048,256]{1,0:T(8,128)S(1)} %get-tuple-element.71.down_sum, f32[256,2048]{1,0:T(8,128)S(1)} %get-tuple-element.72.up_sum, bf16[192,2048]{1,0:T(8,128)(2,1)S(1)} %collective-permute-done.8.early, ...), custom_call_target="tpu_custom_call" | custom-call | flops 402653184 | bytes 11534336 | tf_op jit(solution)/shard_map/pallas_call | solution.py:145
  (86 shorter events, 12.2 us)
Async XLA Ops:
  0.6 22.3 %copy-start = (bf16[1,2048,256]{2,1,0:T(8,128)(2,1)S(1)}, bf16[1,2048,256]{2,1,0:T(8,128)(2,1)}, u32[]{:S(2)}) copy-start(bf16[1,2048,256]{2,1,0:T(8,128)(2,1)} %param.12) | copy-start | bytes 3145732
  0.6 14.3 %collective-permute-start = (bf16[192,2048]{1,0:T(8,128)(2,1)}, bf16[192,2048]{1,0:T(8,128)(2,1)}, u32[]{:S(2)}, u32[]{:S(2)}) collective-permute-start(bf16[192,2048]{1,0:T(8,128)(2,1)} %param.9), channel_id=1, source_target_pairs={{0,6},{4,10},{8,14},{1,7},{5,11},{9,15},{16,22},{20,26},{24,30},{1... | collective-permute-start | bytes 2359304 | tf_op jit(solution)/shard_map/ppermute | solution.py:280
  6.1 14.0 %collective-permute-start.2 = (bf16[192,2048]{1,0:T(8,128)(2,1)}, bf16[192,2048]{1,0:T(8,128)(2,1)}, u32[]{:S(2)}, u32[]{:S(2)}) collective-permute-start(bf16[192,2048]{1,0:T(8,128)(2,1)} %param.9), channel_id=1, source_target_pairs={{6,2},{10,6},{14,10},{7,3},{11,7},{15,11},{22,18},{26,22},{30,26},... | collective-permute-start | bytes 2359304 | tf_op jit(solution)/shard_map/ppermute | solution.py:264
  9.1 5.2 %copy-start.6 = (f32[4]{0:T(128)S(1)}, f32[4]{0:T(128)}, u32[]{:S(2)}) copy-start(f32[4]{0:T(128)} %param.14) | copy-start | bytes 52
  16.4 5.8 %copy-start.3 = (bf16[192,2048]{1,0:T(8,128)(2,1)S(1)}, bf16[192,2048]{1,0:T(8,128)(2,1)}, u32[]{:S(2)}) copy-start(bf16[192,2048]{1,0:T(8,128)(2,1)} %param.8) | copy-start | bytes 2359300
  16.4 6.0 %copy-start.2 = (bf16[1,256,2048]{2,1,0:T(8,128)(2,1)S(1)}, bf16[1,256,2048]{2,1,0:T(8,128)(2,1)}, u32[]{:S(2)}) copy-start(bf16[1,256,2048]{2,1,0:T(8,128)(2,1)} %param.13) | copy-start | bytes 3145732
  16.4 14.0 %collective-permute-start.1 = (bf16[192,2048]{1,0:T(8,128)(2,1)S(1)}, bf16[192,2048]{1,0:T(8,128)(2,1)S(1)}, u32[]{:S(2)}, u32[]{:S(2)}) collective-permute-start(bf16[192,2048]{1,0:T(8,128)(2,1)S(1)} %add_convert_fusion.5), channel_id=1, source_target_pairs={{0,4},{6,10},{10,14},{1,5},{7,11},{11,15},{16,20},{22,26},{26,30},... | collective-permute-start | bytes 2359304 | tf_op jit(solution)/shard_map/ppermute | solution.py:264
  21.4 13.3 %collective-permute-start.3 = (bf16[192,2048]{1,0:T(8,128)(2,1)S(1)}, bf16[192,2048]{1,0:T(8,128)(2,1)S(1)}, u32[]{:S(2)}, u32[]{:S(2)}) collective-permute-start(bf16[192,2048]{1,0:T(8,128)(2,1)S(1)} %add_convert_fusion.4), channel_id=1, source_target_pairs={{12,8},{6,2},{10,6},{13,9},{7,3},{11,7},{28,24},{22,18},{26,22},{2... | collective-permute-start | bytes 2359304 | tf_op jit(solution)/shard_map/ppermute | solution.py:264
  28.8 7.0 %collective-permute-start.6 = (bf16[208,256]{1,0:T(8,128)(2,1)S(1)}, bf16[208,256]{1,0:T(8,128)(2,1)S(1)}, u32[]{:S(2)}, u32[]{:S(2)}) collective-permute-start(bf16[208,256]{1,0:T(8,128)(2,1)S(1)} %convert_element_type.139), channel_id=1, source_target_pairs={{0,4},{4,0},{8,12},{12,8},{1,5},{5,1},{9,13},{13,9},{2,6},{6,2},{1... | collective-permute-start | bytes 319496 | tf_op jit(solution)/shard_map/ppermute | solution.py:202
  28.8 31.3 %collective-permute-start.8 = (bf16[192,2048]{1,0:T(8,128)(2,1)S(1)}, bf16[192,2048]{1,0:T(8,128)(2,1)S(1)}, u32[]{:S(2)}, u32[]{:S(2)}) collective-permute-start(bf16[192,2048]{1,0:T(8,128)(2,1)S(1)} %fusion.17.value_ref.early), channel_id=1, source_target_pairs={{0,1},{1,0},{2,3},{3,2},{4,5},{5,4},{6,7},{7,6},{8,9},{9,8},{10,11... | collective-permute-start | bytes 2359304 | tf_op jit(solution)/shard_map/ppermute | solution.py:211
  30.8 14.8 %collective-permute-start.4 = (bf16[192,2048]{1,0:T(8,128)(2,1)S(1)}, bf16[192,2048]{1,0:T(8,128)(2,1)S(1)}, u32[]{:S(2)}, u32[]{:S(2)}) collective-permute-start(bf16[192,2048]{1,0:T(8,128)(2,1)S(1)} %add_convert_fusion.3), channel_id=1, source_target_pairs={{0,4},{4,8},{10,14},{1,5},{5,9},{11,15},{16,20},{20,24},{26,30},{1... | collective-permute-start | bytes 2359304 | tf_op jit(solution)/shard_map/ppermute | solution.py:264
  35.1 16.4 %collective-permute-start.5 = (bf16[192,2048]{1,0:T(8,128)(2,1)S(1)}, bf16[192,2048]{1,0:T(8,128)(2,1)S(1)}, u32[]{:S(2)}, u32[]{:S(2)}) collective-permute-start(bf16[192,2048]{1,0:T(8,128)(2,1)S(1)} %add_convert_fusion.2), channel_id=1, source_target_pairs={{8,4},{12,8},{6,2},{9,5},{13,9},{7,3},{24,20},{28,24},{22,18},{25,... | collective-permute-start | bytes 2359304 | tf_op jit(solution)/shard_map/ppermute | solution.py:264
  35.9 18.6 %collective-permute-start.7 = (bf16[208,256]{1,0:T(8,128)(2,1)S(1)}, bf16[208,256]{1,0:T(8,128)(2,1)S(1)}, u32[]{:S(2)}, u32[]{:S(2)}) collective-permute-start(bf16[208,256]{1,0:T(8,128)(2,1)S(1)} %convert_element_type.141), channel_id=1, source_target_pairs={{0,8},{4,12},{8,0},{12,4},{1,9},{5,13},{9,1},{13,5},{2,10},{6,14},... | collective-permute-start | bytes 319496 | tf_op jit(solution)/shard_map/ppermute | solution.py:202
  46.0 19.0 %collective-permute-start.9 = (bf16[192,2048]{1,0:T(8,128)(2,1)S(1)}, bf16[192,2048]{1,0:T(8,128)(2,1)S(1)}, u32[]{:S(2)}, u32[]{:S(2)}) collective-permute-start(bf16[192,2048]{1,0:T(8,128)(2,1)S(1)} %add_convert_fusion.1), channel_id=1, source_target_pairs={{0,4},{4,8},{8,12},{1,5},{5,9},{9,13},{16,20},{20,24},{24,28},{17,... | collective-permute-start | bytes 2359304 | tf_op jit(solution)/shard_map/ppermute | solution.py:264
  51.7 14.3 %collective-permute-start.10 = (bf16[192,2048]{1,0:T(8,128)(2,1)S(1)}, bf16[192,2048]{1,0:T(8,128)(2,1)S(1)}, u32[]{:S(2)}, u32[]{:S(2)}) collective-permute-start(bf16[192,2048]{1,0:T(8,128)(2,1)S(1)} %add_convert_fusion), channel_id=1, source_target_pairs={{4,0},{8,4},{12,8},{5,1},{9,5},{13,9},{20,16},{24,20},{28,24},{21,... | collective-permute-start | bytes 2359304 | tf_op jit(solution)/shard_map/ppermute | solution.py:264
  54.9 5.3 %copy-start.5 = (s32[192]{0:T(256)S(1)}, s32[192]{0:T(256)}, u32[]{:S(2)}) copy-start(s32[192]{0:T(256)} %param.15) | copy-start | bytes 2308
  60.1 1.2 %copy-start.1 = (f32[1,2048]{1,0:T(1,128)S(1)}, f32[1,2048]{1,0:T(1,128)}, u32[]{:S(2)}) copy-start(f32[1,2048]{1,0:T(1,128)} %gain_ref.1) | copy-start | bytes 24580
  60.3 4.7 %collective-permute-start.11 = (bf16[192,256]{1,0:T(8,128)(2,1)S(1)}, bf16[192,256]{1,0:T(8,128)(2,1)S(1)}, u32[]{:S(2)}, u32[]{:S(2)}) collective-permute-start(bf16[192,256]{1,0:T(8,128)(2,1)S(1)} %get-tuple-element.88), channel_id=1, source_target_pairs={{0,1},{1,0},{2,3},{3,2},{4,5},{5,4},{6,7},{7,6},{8,9},{9,8},{10,11... | collective-permute-start | bytes 294920 | tf_op jit(solution)/shard_map/ppermute | solution.py:211
  62.1 5.8 %collective-permute-start.12 = (bf16[192,2048]{1,0:T(8,128)(2,1)S(1)}, bf16[192,2048]{1,0:T(8,128)(2,1)S(1)}, u32[]{:S(2)}, u32[]{:S(2)}) collective-permute-start(bf16[192,2048]{1,0:T(8,128)(2,1)S(1)} %get-tuple-element.97), channel_id=1, source_target_pairs={{0,2},{2,0},{1,3},{3,1},{4,6},{6,4},{5,7},{7,5},{8,10},{10,8},{9,1... | collective-permute-start | bytes 2359304 | tf_op jit(solution)/shard_map/ppermute | solution.py:364
  67.1 11.7 %collective-permute-start.17 = (bf16[192,2048]{1,0:T(8,128)(2,1)S(1)}, bf16[192,2048]{1,0:T(8,128)(2,1)S(1)}, u32[]{:S(2)}, u32[]{:S(2)}) collective-permute-start(bf16[192,2048]{1,0:T(8,128)(2,1)S(1)} %broadcast_select_fusion.1), channel_id=1, source_target_pairs={{0,2},{2,0},{1,3},{3,1},{4,6},{6,4},{5,7},{7,5},{8,10},{10,8},{9,1... | collective-permute-start | bytes 2359304 | tf_op jit(solution)/shard_map/ppermute | solution.py:376
  67.2 11.7 %copy-start.4 = (bf16[192,2048]{1,0:T(8,128)(2,1)S(1)}, bf16[192,2048]{1,0:T(8,128)(2,1)}, u32[]{:S(2)}) copy-start(bf16[192,2048]{1,0:T(8,128)(2,1)} %param.9) | copy-start | bytes 2359300
  67.3 11.6 %collective-permute-start.16 = (bf16[192,1024]{1,0:T(8,128)(2,1)S(1)}, bf16[192,1024]{1,0:T(8,128)(2,1)S(1)}, u32[]{:S(2)}, u32[]{:S(2)}) collective-permute-start(bf16[192,1024]{1,0:T(8,128)(2,1)S(1)} %get-tuple-element.91), channel_id=1, source_target_pairs={{0,1},{1,0},{2,3},{3,2},{4,5},{5,4},{6,7},{7,6},{8,9},{9,8},{10,11... | collective-permute-start | bytes 1179656 | tf_op jit(solution)/shard_map/ppermute | solution.py:211
  68.3 4.1 %collective-permute-start.15 = (f32[2,192]{1,0:T(2,128)S(1)}, f32[2,192]{1,0:T(2,128)S(1)}, u32[]{:S(2)}, u32[]{:S(2)}) collective-permute-start(f32[2,192]{1,0:T(2,128)S(1)} %pad_maximum_fusion.1), channel_id=1, source_target_pairs={{0,12},{4,0},{8,4},{12,8},{1,13},{5,1},{9,5},{13,9},{2,14},{6,2},{... | collective-permute-start | bytes 4616 | tf_op jit(solution)/shard_map/ppermute | solution.py:387
  69.8 5.4 %collective-permute-start.13 = (f32[2,192]{1,0:T(2,128)S(1)}, f32[2,192]{1,0:T(2,128)S(1)}, u32[]{:S(2)}, u32[]{:S(2)}) collective-permute-start(f32[2,192]{1,0:T(2,128)S(1)} %pad_maximum_fusion.1), channel_id=1, source_target_pairs={{0,4},{4,8},{8,12},{12,0},{1,5},{5,9},{9,13},{13,1},{2,6},{6,10},{... | collective-permute-start | bytes 4616 | tf_op jit(solution)/shard_map/ppermute | solution.py:387
  70.6 4.6 %collective-permute-start.14 = (f32[2,192]{1,0:T(2,128)S(1)}, f32[2,192]{1,0:T(2,128)S(1)}, u32[]{:S(2)}, u32[]{:S(2)}) collective-permute-start(f32[2,192]{1,0:T(2,128)S(1)} %pad_maximum_fusion.1), channel_id=1, source_target_pairs={{0,8},{4,12},{8,0},{12,4},{1,9},{5,13},{9,1},{13,5},{2,10},{6,14},... | collective-permute-start | bytes 4616 | tf_op jit(solution)/shard_map/ppermute | solution.py:387
  80.4 4.7 %collective-permute-start.19 = (bf16[192,256]{1,0:T(8,128)(2,1)S(1)}, bf16[192,256]{1,0:T(8,128)(2,1)S(1)}, u32[]{:S(2)}, u32[]{:S(2)}) collective-permute-start(bf16[192,256]{1,0:T(8,128)(2,1)S(1)} %get-tuple-element.99), channel_id=1, source_target_pairs={{0,4},{4,0},{8,12},{12,8},{1,5},{5,1},{9,13},{13,9},{2,6},{6,2},{1... | collective-permute-start | bytes 294920 | tf_op jit(solution)/shard_map/ppermute | solution.py:202
  82.5 4.7 %collective-permute-start.18 = (f32[192]{0:T(256)S(1)}, f32[192]{0:T(256)S(1)}, u32[]{:S(2)}, u32[]{:S(2)}) collective-permute-start(f32[192]{0:T(256)S(1)} %bitcast.47), channel_id=1, source_target_pairs={{0,2},{2,0},{1,3},{3,1},{4,6},{6,4},{5,7},{7,5},{8,10},{10,8},{9,1... | collective-permute-start | bytes 2312 | tf_op jit(solution)/shard_map/ppermute | solution.py:408
  82.6 11.5 %collective-permute-start.21 = (bf16[192,1024]{1,0:T(8,128)(2,1)S(1)}, bf16[192,1024]{1,0:T(8,128)(2,1)S(1)}, u32[]{:S(2)}, u32[]{:S(2)}) collective-permute-start(bf16[192,1024]{1,0:T(8,128)(2,1)S(1)} %get-tuple-element.74), channel_id=1, source_target_pairs={{0,1},{1,0},{2,3},{3,2},{4,5},{5,4},{6,7},{7,6},{8,9},{9,8},{10,11... | collective-permute-start | bytes 1179656 | tf_op jit(solution)/shard_map/ppermute | solution.py:211
  85.1 5.8 %collective-permute-start.20 = (bf16[192,256]{1,0:T(8,128)(2,1)S(1)}, bf16[192,256]{1,0:T(8,128)(2,1)S(1)}, u32[]{:S(2)}, u32[]{:S(2)}) collective-permute-start(bf16[192,256]{1,0:T(8,128)(2,1)S(1)} %fusion.23), channel_id=1, source_target_pairs={{0,8},{4,12},{8,0},{12,4},{1,9},{5,13},{9,1},{13,5},{2,10},{6,14},... | collective-permute-start | bytes 294920 | tf_op jit(solution)/shard_map/ppermute | solution.py:202
  94.1 3.3 %collective-permute-start.22 = (bf16[192,2048]{1,0:T(8,128)(2,1)S(1)}, bf16[192,2048]{1,0:T(8,128)(2,1)S(1)}, u32[]{:S(2)}, u32[]{:S(2)}) collective-permute-start(bf16[192,2048]{1,0:T(8,128)(2,1)S(1)} %constant_dynamic-update-slice_fusion), channel_id=1, source_target_pairs={{0,2},{2,0},{1,3},{3,1},{4,6},{6,4},{5,7},{7,5},{8,10},{10,8},{9,1... | collective-permute-start | bytes 2359304 | tf_op jit(solution)/shard_map/ppermute | solution.py:439
  94.5 6.3 %collective-permute-start.23 = (bf16[192,384]{1,0:T(8,128)(2,1)S(1)}, bf16[192,384]{1,0:T(8,128)(2,1)S(1)}, u32[]{:S(2)}, u32[]{:S(2)}) collective-permute-start(bf16[192,384]{1,0:T(8,128)(2,1)S(1)} %pad_maximum_fusion), channel_id=1, source_target_pairs={{0,1},{1,0},{2,3},{3,2},{4,5},{5,4},{6,7},{7,6},{8,9},{9,8},{10,11... | collective-permute-start | bytes 442376 | tf_op jit(solution)/shard_map/ppermute | solution.py:211
